TPU v7x, 32 devices: a whole 2x2x4 slice. The times are simulated.
32 devices in a mesh: group: 2 (over x), row: 16 (over z, y, core).
Axes of the slice: x: 2, y: 2, z: 4, core: 2. Of those that a mesh axis runs over, the one named last changes fastest.
Arguments:
- voxels: bfloat16 [128, 4, 8, 768], P(('group', 'row')), parts along dimension 0, may hold values from -6 to 6
- dw_kernel: float32 [343, 768], replicated, may hold values from -0.3125 to 0.3125
- norm_gain: float32 [768], replicated, may hold values from 0.25 to 1.75
- norm_bias: float32 [768], replicated, may hold values from -3 to 3
- weight_in: bfloat16 [3072, 768], replicated, may hold values from -0.21875 to 0.21875
- weight_out: bfloat16 [3072, 768], replicated, may hold values from -0.109375 to 0.109375
- layer_scale: float32 [768], replicated, may hold values from 0.3 to 1
- cotangent: bfloat16 [128, 4, 8, 768], P(('group', 'row')), parts along dimension 0, may hold values from -6 to 6
Outputs:
- block_out: bfloat16 [128, 4, 8, 768], P(('group', 'row')), parts along dimension 0
- voxel_grad: bfloat16 [128, 4, 8, 768], P(('group', 'row')), parts along dimension 0
- kernel_grad: float32 [686, 768], P('group'), parts along dimension 0
- gain_grad: float32 [1536], P('group'), parts along dimension 0
- bias_grad: float32 [1536], P('group'), parts along dimension 0
- scale_grad: float32 [1536], P('group'), parts along dimension 0
- weight_in_grad: float32 [6144, 768], P(('group', 'row')), parts along dimension 0
- weight_out_grad: float32 [6144, 768], P(('group', 'row')), parts along dimension 0
There are 2 independent parts, one for each index of `group`. A program takes and returns all parts, laid end to end along the dimension named above; an argument that names none is the same for every part. Nothing has to cross between parts.
All inputs are finite; a program needn't handle non-finite values.
Results may differ from a plain program's by a relative error of at most 0.0064.
Values may be sent and summed in bfloat16 or wider, within the bound.
No kernel may reach another device: no remote copies, remote signals or barrier semaphores. Data moves between devices by JAX's collectives and lax.ppermute only.
A program may use at most 128 MiB of HBM per device.

v0:
```python
import jax
import jax.numpy as jnp
from jax import lax
from jax.sharding import PartitionSpec as P

KS = 7


root_half = 0.7071067811865476
inv_root_tau = 0.3989422804014327
norm_eps = 1e-06


def padded_2(cells, sides, width):
    for axis, dim in sides:
        count = lax.axis_size(axis)
        ends = count - 1
        head = lax.slice_in_dim(cells, 0, width, axis=dim)
        tail = lax.slice_in_dim(cells, cells.shape[dim] - width, cells.shape[dim], axis=dim)
        cells = jnp.concatenate(
            [
                lax.ppermute(tail, axis, [(i, (i + 1) % count) for i in range(ends)]),
                cells,
                lax.ppermute(head, axis, [((i + 1) % count, i) for i in range(ends)]),
            ],
            axis=dim,
        )
    return cells


def gelu_value(values):
    return 0.5 * values * (1.0 + lax.erf(values * root_half))


def gelu_slope(values):
    return (
        0.5 * (1.0 + lax.erf(values * root_half))
        + values * jnp.exp(-0.5 * values * values) * inv_root_tau
    )


def depthwise_apply(padded, kernel, window_shape, flipped):
    planes = window_shape[0]
    height = window_shape[1]
    breadth = window_shape[2]

    def advance(along_x, running):
        along_x = along_x.astype(jnp.int32)
        start_x = KS - 1 - along_x if flipped else along_x
        slab = lax.dynamic_slice_in_dim(padded, start_x, planes, 0).astype(jnp.float32)
        taps = lax.dynamic_slice_in_dim(kernel, along_x * (KS * KS), KS * KS, 0)
        for along_y in range(KS):
            for along_z in range(KS):
                start_y = KS - 1 - along_y if flipped else along_y
                start_z = KS - 1 - along_z if flipped else along_z
                window = slab[:, start_y : start_y + height, start_z : start_z + breadth, :]
                running = running + window * taps[along_y * KS + along_z]
        return running

    return lax.fori_loop(0, KS, advance, jnp.zeros(window_shape, jnp.float32))


def kernel_terms(padded, grads, window_shape):
    planes = window_shape[0]
    height = window_shape[1]
    breadth = window_shape[2]
    grads_wide = grads.astype(jnp.float32)

    def one_plane(along_x):
        slab = lax.dynamic_slice_in_dim(padded, along_x, planes, 0).astype(jnp.float32)
        rows_out = []
        for along_y in range(KS):
            for along_z in range(KS):
                window = slab[:, along_y : along_y + height, along_z : along_z + breadth, :]
                rows_out.append(jnp.sum(window * grads_wide, axis=(0, 1, 2)))
        return jnp.stack(rows_out)

    stacked = lax.map(one_plane, jnp.arange(KS, dtype=jnp.int32))
    return stacked.reshape(KS * KS * KS, grads.shape[3])


def side_pad(rimmed, margin):
    return jnp.pad(rimmed, ((0, 0), (margin, margin), (margin, margin), (0, 0)))


def contract_rows(left, right):
    return lax.dot_general(
        left, right, (((0,), (0,)), ((), ())), preferred_element_type=jnp.float32
    )


def on_device(
    voxels, dw_kernel, norm_gain, norm_bias, weight_in, weight_out, layer_scale, cotangent
):
    margin = KS // 2
    window_shape = voxels.shape
    channels = voxels.shape[3]
    rimmed = padded_2(voxels, (("row", 0),), margin)
    padded = side_pad(rimmed, margin)
    convolved = depthwise_apply(padded, dw_kernel, window_shape, False).reshape(-1, channels)
    average = jnp.mean(convolved, axis=-1, keepdims=True)
    centered = convolved - average
    variance = jnp.mean(centered * centered, axis=-1, keepdims=True)
    inverse_std = lax.rsqrt(variance + norm_eps)
    unit = centered * inverse_std
    normed = (unit * norm_gain + norm_bias).astype(jnp.bfloat16)
    hidden = jnp.dot(normed, weight_in.T, preferred_element_type=jnp.float32)
    activated = gelu_value(hidden).astype(jnp.bfloat16)
    mixed = jnp.dot(activated, weight_out, preferred_element_type=jnp.float32)
    block_out = (voxels.reshape(-1, channels).astype(jnp.float32) + layer_scale * mixed).astype(
        jnp.bfloat16
    )
    upstream = cotangent.reshape(-1, channels).astype(jnp.float32)
    scale_local = jnp.sum(upstream * mixed, axis=0)
    mixed_grad = (layer_scale * upstream).astype(jnp.bfloat16)
    activated_grad = jnp.dot(mixed_grad, weight_out.T, preferred_element_type=jnp.float32)
    hidden_grad = (activated_grad * gelu_slope(hidden)).astype(jnp.bfloat16)
    normed_grad = jnp.dot(hidden_grad, weight_in, preferred_element_type=jnp.float32)
    bias_local = jnp.sum(normed_grad, axis=0)
    gain_local = jnp.sum(normed_grad * unit, axis=0)
    scaled = normed_grad * norm_gain
    convolved_grad = inverse_std * (
        scaled
        - jnp.mean(scaled, axis=-1, keepdims=True)
        - unit * jnp.mean(scaled * unit, axis=-1, keepdims=True)
    )
    convolved_grad = convolved_grad.astype(jnp.bfloat16).reshape(window_shape)
    grad_rimmed = padded_2(convolved_grad, (("row", 0),), margin)
    back_conv = depthwise_apply(side_pad(grad_rimmed, margin), dw_kernel, window_shape, True)
    voxel_grad = (cotangent.astype(jnp.float32) + back_conv).astype(jnp.bfloat16)
    again_rimmed = padded_2(voxels, (("row", 0),), margin)
    source_padded = side_pad(again_rimmed, margin)
    kernel_local = kernel_terms(source_padded, convolved_grad, window_shape)
    kernel_grad, gain_grad, bias_grad, scale_grad = lax.psum(
        (kernel_local, gain_local, bias_local, scale_local), "row"
    )
    slices_act, slices_grad = (
        lax.all_to_all(activated, "row", split_axis=1, concat_axis=0, tiled=True),
        lax.all_to_all(hidden_grad, "row", split_axis=1, concat_axis=0, tiled=True),
    )
    weight_in_grad = contract_rows(slices_grad, lax.all_gather(normed, "row", axis=0, tiled=True))
    weight_out_grad = contract_rows(
        slices_act, lax.all_gather(mixed_grad, "row", axis=0, tiled=True)
    )
    return (
        block_out.reshape(window_shape),
        voxel_grad,
        kernel_grad,
        gain_grad,
        bias_grad,
        scale_grad,
        weight_in_grad,
        weight_out_grad,
    )


def solution(mesh):
    in_specs = (
        P(("group", "row"), None, None, None),
        P(),
        P(),
        P(),
        P(),
        P(),
        P(),
        P(("group", "row"), None, None, None),
    )
    out_specs = (
        P(("group", "row"), None, None, None),
        P(("group", "row"), None, None, None),
        P("group", None),
        P("group"),
        P("group"),
        P("group"),
        P(("group", "row"), None),
        P(("group", "row"), None),
    )
    return jax.shard_map(
        on_device, mesh=mesh, in_specs=in_specs, out_specs=out_specs, check_vma=False
    )
```

profile of v0, /device:TPU:1, one launch (start us, length us, event | category | flops | bytes accessed | tf_op | source)
XLA Modules:
  0.0 317.5 jit_solution(17583878613146733667)
XLA Ops:
  8.2 4.5 %collective-permute-start = (bf16[3,4,8,768]{3,2,1,0:T(8,128)(2,1)S(1)}, bf16[3,4,8,768]{3,2,1,0:T(8,128)(2,1)S(1)}, u32[]{:S(2)}, u32[]{:S(2)}) collective-permute-start(bf16[3,4,8,768]{3,2,1,0:T(8,128)(2,1)S(1)} %get-tuple-element.442), channel_id=1, source_target_pairs={{0,1},{1,2},{2,3},{3,4},{4,5},{5,6},{6,7},{7,8},{8,9},{9,10},{10,1... | collective-permute-start | bytes 442376 | tf_op jit(solution)/shard_map/ppermute | solution.py:22
  12.8 1.9 collective-permute-start.1
  14.8 4.4 %collective-permute-done.1 = bf16[3,4,8,768]{3,2,1,0:T(8,128)(2,1)S(1)} collective-permute-done((bf16[3,4,8,768]{3,2,1,0:T(8,128)(2,1)S(1)}, bf16[3,4,8,768]{3,2,1,0:T(8,128)(2,1)S(1)}, u32[]{:S(2)}, u32[]{:S(2)}) %collective-permute-start.1) | collective-permute-done | bytes 147488 | tf_op jit(solution)/shard_map/ppermute | solution.py:24
  19.2 2.6 select_maximum_fusion.2
  21.9 60.1 %while.41 = (s32[]{:T(128)}, f32[4,4,8,768]{3,2,1,0:T(8,128)S(1)}, bf16[10,10,14,768]{3,2,1,0:T(8,128)(2,1)}, f32[343,768]{1,0:T(8,128)}, s32[]{:T(128)}, /*inde...) while((s32[]{:T(128)}, f32[4,4,8,768]{3,2,1,0:T(8,128)S(1)}, ...), condition=%wide.region_1.2_spmd.clone, body=%wide.region_0.1_spmd.clone.sunk | while | flops 10162231 | bytes 23087380 | solution.py:60
  23.3 1.5 fusion.294
  27.6 2.8 fusion.296
  30.4 1.6 fusion.295
  32.0 1.5 fusion.294
  36.2 2.8 fusion.296
  40.6 1.5 fusion.294
  44.9 2.8 fusion.296
  47.8 1.5 fusion.295
  53.5 2.8 fusion.296
  57.8 1.5 fusion.294
  62.2 2.8 fusion.296
  65.0 1.5 fusion.295
  70.6 2.8 fusion.296
  79.1 2.8 fusion.296
  83.4 5.4 %multiply_convert_fusion = (bf16[128,3072]{1,0:T(8,128)(2,1)S(1)}, f32[128,3072]{1,0:T(8,128)}) fusion(bf16[128,768]{1,0:T(8,128)(2,1)} %add_convert_fusion, bf16[3072,768]{1,0:T(8,128)(2,1)} %param.18), kind=kOutput, calls=%fused_computation.513 | convolution fusion | flops 605945856 | bytes 7274496 | tf_op jit(solution)/shard_map/dot_general | solution.py:107
  88.8 1.5 fusion.263
  90.3 4.7 %fusion.248 = bf16[128,3072]{1,0:T(8,128)(2,1)S(1)} fusion(bf16[128,768]{1,0:T(8,128)(2,1)S(1)} %get-tuple-element.439, bf16[3072,768]{1,0:T(8,128)(2,1)} %param.19, f32[128,3072]{1,0:T(8,128)} %get-tuple-element.445), kind=kOutput, calls=%fused_computation.502 | convolution fusion | flops 607911936 | bytes 7274496 | tf_op jit(solution)/shard_map/dot_general | solution.py:116
  96.2 3.3 %multiply_reduce_fusion = (f32[768]{0:T(1024)S(1)}, f32[128]{0:T(128)S(1)}, f32[128]{0:T(128)S(1)}, f32[768]{0:T(1024)S(1)}, f32[128,768]{1,0:T(8,128)S(1)}) fusion(f32[4,4,8,768]{3,2,1,0:T(8,128)S(1)} %get-tuple-element.224, f32[128]{0:T(128)S(1)} %rsqrt.12, f32[128]{0:T(128)S(1)} %div.15, f32[768]{0:T(1024)S(1)} %copy-done.4, ...), kind=kOutput, calls=%fused_computation.531 | convolution fusion | flops 604862720 | bytes 6302720 | tf_op jit(solution)/shard_map/dot_general | solution.py:118
  100.5 1.9 collective-permute-start.2
  102.4 2.4 collective-permute-start.3
  104.8 6.8 %all-to-all-start = ((bf16[128,16,192]{0,2,1:T(8,128)(2,1)}), bf16[128,16,192]{0,2,1:T(8,128)(2,1)S(1)}, u32[]{:S(2)}, u32[]{:S(2)}) async-start(bf16[128,16,192]{0,2,1:T(8,128)(2,1)} %bitcast.9), calls=%async_computation | async-start | bytes 1572864 | tf_op jit(solution)/shard_map/all_to_all | solution.py:139
  112.4 56.0 %while.40 = (s32[]{:T(128)}, f32[7,49,768]{2,1,0:T(8,128)}, s32[7]{0:T(128)S(1)}, bf16[10,10,14,768]{3,2,1,0:T(8,128)(2,1)}, f32[4,4,8,768]{3,2,1,0:T(8,128)S(1)}, /*index=5*/s32[]{:T(128)}, s32[]{:T(128)}, s32[]{:T(128)}) while((s32[]{:T(128)}, f32[7,49,768]{2,1,0:T(8,128)}, s32[7]{0:T(128)S(1)}, bf16[10,10,14,768]{3,2,1,0:T(8,128)(2,1)}, ...), condition=%wide.region_58.59_spmd, body=%wide.region_8.58_spmd.sunk | while | flops 10026245 | bytes 24103560 | solution.py:78
  169.6 2.4 reshape.186
  172.0 57.8 %all-reduce.2 = (f32[768]{0:T(1024)}, f32[768]{0:T(1024)}, f32[768]{0:T(1024)}) all-reduce(f32[768]{0:T(1024)S(1)} %get-tuple-element.404, f32[768]{0:T(1024)S(1)} %get-tuple-element.407, f32[768]{0:T(1024)S(1)} %get-tuple-element.437), channel_id=1, replica_groups=mesh['group'=2,'row'=16] {'row'}, use_global_device_ids=true, to_apply=%region_61.62 | all-reduce | flops 2304 | bytes 18432 | tf_op jit(solution)/shard_map/psum | solution.py:134
  229.8 1.8 select_maximum_fusion
  231.6 9.0 %all-to-all-start.1 = ((bf16[128,16,192]{0,2,1:T(8,128)(2,1)}), bf16[128,16,192]{0,2,1:T(8,128)(2,1)}, u32[]{:S(2)}, u32[]{:S(2)}) async-start(bf16[128,16,192]{0,2,1:T(8,128)(2,1)} %bitcast.11), calls=%async_computation.1 | async-start | bytes 1572864 | tf_op jit(solution)/shard_map/all_to_all | solution.py:138
  240.5 60.2 %while.42 = (s32[]{:T(128)}, f32[4,4,8,768]{3,2,1,0:T(8,128)S(1)}, bf16[10,10,14,768]{3,2,1,0:T(8,128)(2,1)}, f32[343,768]{1,0:T(8,128)}, s32[]{:T(128)}, /*inde...) while((s32[]{:T(128)}, f32[4,4,8,768]{3,2,1,0:T(8,128)S(1)}, ...), condition=%wide.region_7.8_spmd.clone, body=%wide.region_6.7_spmd.clone.sunk | while | flops 10162235 | bytes 23087440 | solution.py:60
  242.0 1.5 fusion.298
  246.3 2.8 fusion.300
  249.2 1.6 fusion.299
  250.7 1.5 fusion.298
  255.0 2.8 fusion.300
  259.3 1.5 fusion.298
  263.7 2.8 fusion.300
  266.5 1.5 fusion.299
  272.2 2.8 fusion.300
  276.6 1.5 fusion.298
  281.0 2.8 fusion.300
  289.4 2.8 fusion.300
  297.9 2.8 fusion.300
  301.5 3.5 %fusion.257 = f32[192,768]{1,0:T(8,128)} fusion(bf16[2048,768]{1,0:T(8,128)(2,1)} %all-gather.3.cloned.1.call-done, bf16[128,16,192]{0,2,1:T(8,128)(2,1)S(1)} %all-to-all-done), kind=kOutput, calls=%fused_computation.518 | convolution fusion | flops 603979776 | bytes 4521984 | tf_op jit(solution)/shard_map/dot_general | solution.py:87
  305.0 3.7 %fusion.254 = f32[192,768]{1,0:T(8,128)} fusion(bf16[2048,768]{1,0:T(8,128)(2,1)} %all-gather.5.cloned.1.call-done, bf16[128,16,192]{0,2,1:T(8,128)(2,1)} %all-to-all-done.1), kind=kOutput, calls=%fused_computation.515 | convolution fusion | flops 603979776 | bytes 4521984 | tf_op jit(solution)/shard_map/dot_general | solution.py:87
  308.7 2.3 copy.50
  (482 shorter events, 106.5 us)
Async XLA Ops:
  7.2 294.3 %all-gather.3.cloned.1.call-start = ((), (), s32[]{:S(2)}) async-start(), calls=%async_computation.3 | async-start | bytes 3342336 | tf_op jit(solution)/shard_map/all_gather | solution.py:141
  8.2 6.6 %collective-permute-start = (bf16[3,4,8,768]{3,2,1,0:T(8,128)(2,1)S(1)}, bf16[3,4,8,768]{3,2,1,0:T(8,128)(2,1)S(1)}, u32[]{:S(2)}, u32[]{:S(2)}) collective-permute-start(bf16[3,4,8,768]{3,2,1,0:T(8,128)(2,1)S(1)} %get-tuple-element.442), channel_id=1, source_target_pairs={{0,1},{1,2},{2,3},{3,4},{4,5},{5,6},{6,7},{7,8},{8,9},{9,10},{10,1... | collective-permute-start | bytes 442376 | tf_op jit(solution)/shard_map/ppermute | solution.py:22
  12.8 6.5 %collective-permute-start.1 = (bf16[3,4,8,768]{3,2,1,0:T(8,128)(2,1)S(1)}, bf16[3,4,8,768]{3,2,1,0:T(8,128)(2,1)S(1)}, u32[]{:S(2)}, u32[]{:S(2)}) collective-permute-start(bf16[3,4,8,768]{3,2,1,0:T(8,128)(2,1)S(1)} %get-tuple-element.443), channel_id=1, source_target_pairs={{1,0},{2,1},{3,2},{4,3},{5,4},{6,5},{7,6},{8,7},{9,8},{10,9},{11,1... | collective-permute-start | bytes 442376 | tf_op jit(solution)/shard_map/ppermute | solution.py:24
  21.9 60.6 %copy-start.4 = (f32[768]{0:T(1024)S(1)}, f32[768]{0:T(1024)}, u32[]{:S(2)}) copy-start(f32[768]{0:T(1024)} %param.16) | copy-start | bytes 9220
  21.9 60.6 %copy-start.5 = (f32[768]{0:T(1024)S(1)}, f32[768]{0:T(1024)}, u32[]{:S(2)}) copy-start(f32[768]{0:T(1024)} %param.17) | copy-start | bytes 9220
  83.3 5.4 %copy-start = (bf16[3072,768]{1,0:T(8,128)(2,1)S(1)}, bf16[3072,768]{1,0:T(8,128)(2,1)}, u32[]{:S(2)}) copy-start(bf16[3072,768]{1,0:T(8,128)(2,1)} %param.19) | copy-start | bytes 14155780
  83.3 5.4 %copy-start.1 = (bf16[4,4,8,768]{3,2,1,0:T(8,128)(2,1)S(1)}, bf16[4,4,8,768]{3,2,1,0:T(8,128)(2,1)}, u32[]{:S(2)}) copy-start(bf16[4,4,8,768]{3,2,1,0:T(8,128)(2,1)} %param.14) | copy-start | bytes 589828
  83.4 5.4 %copy-start.3 = (bf16[4,4,8,768]{3,2,1,0:T(8,128)(2,1)S(1)}, bf16[4,4,8,768]{3,2,1,0:T(8,128)(2,1)}, u32[]{:S(2)}) copy-start(bf16[4,4,8,768]{3,2,1,0:T(8,128)(2,1)} %param.21) | copy-start | bytes 589828
  83.4 5.4 %copy-start.6 = (f32[768]{0:T(1024)S(1)}, f32[768]{0:T(1024)}, u32[]{:S(2)}) copy-start(f32[768]{0:T(1024)} %param.20) | copy-start | bytes 9220
  90.3 4.7 %copy-start.2 = (bf16[128,768]{1,0:T(8,128)(2,1)}, bf16[128,768]{1,0:T(8,128)(2,1)S(1)}, u32[]{:S(2)}) copy-start(bf16[128,768]{1,0:T(8,128)(2,1)S(1)} %get-tuple-element.439) | copy-start | bytes 589828
  100.5 129.3 %collective-permute-start.2 = (bf16[3,4,8,768]{3,2,1,0:T(8,128)(2,1)}, bf16[3,4,8,768]{3,2,1,0:T(8,128)(2,1)S(1)}, u32[]{:S(2)}, u32[]{:S(2)}) collective-permute-start(bf16[3,4,8,768]{3,2,1,0:T(8,128)(2,1)} %bitcast.6), channel_id=1, source_target_pairs={{0,1},{1,2},{2,3},{3,4},{4,5},{5,6},{6,7},{7,8},{8,9},{9,10},{10,1... | collective-permute-start | bytes 442376 | tf_op jit(solution)/shard_map/ppermute | solution.py:22
  102.4 127.4 %collective-permute-start.3 = (bf16[3,4,8,768]{3,2,1,0:T(8,128)(2,1)}, bf16[3,4,8,768]{3,2,1,0:T(8,128)(2,1)S(1)}, u32[]{:S(2)}, u32[]{:S(2)}) collective-permute-start(bf16[3,4,8,768]{3,2,1,0:T(8,128)(2,1)} %bitcast.8), channel_id=1, source_target_pairs={{1,0},{2,1},{3,2},{4,3},{5,4},{6,5},{7,6},{8,7},{9,8},{10,9},{11,1... | collective-permute-start | bytes 442376 | tf_op jit(solution)/shard_map/ppermute | solution.py:24
  104.8 126.8 %all-to-all-start = ((bf16[128,16,192]{0,2,1:T(8,128)(2,1)}), bf16[128,16,192]{0,2,1:T(8,128)(2,1)S(1)}, u32[]{:S(2)}, u32[]{:S(2)}) async-start(bf16[128,16,192]{0,2,1:T(8,128)(2,1)} %bitcast.9), calls=%async_computation | async-start | bytes 1572864 | tf_op jit(solution)/shard_map/all_to_all | solution.py:139
  111.6 193.3 %all-gather.5.cloned.1.call-start = ((), (), s32[]{:S(2)}) async-start(), calls=%async_computation.4 | async-start | bytes 3342336 | tf_op jit(solution)/shard_map/all_gather | solution.py:143
  112.4 196.3 %all-reduce.5.cloned.1.call-start = ((), (), s32[]{:S(2)}) async-start(), calls=%async_computation.2 | async-start | bytes 2113536 | tf_op jit(solution)/shard_map/psum | solution.py:134
  231.6 73.4 %all-to-all-start.1 = ((bf16[128,16,192]{0,2,1:T(8,128)(2,1)}), bf16[128,16,192]{0,2,1:T(8,128)(2,1)}, u32[]{:S(2)}, u32[]{:S(2)}) async-start(bf16[128,16,192]{0,2,1:T(8,128)(2,1)} %bitcast.11), calls=%async_computation.1 | async-start | bytes 1572864 | tf_op jit(solution)/shard_map/all_to_all | solution.py:138
Sparse Core Ops, SparseCore 0:
  83.4 57.7 all-gather.2
  143.5 44.4 all-gather.4
  192.0 94.8 all-reduce.4
where the time goes:
time: 324 us; the launch traced here: 318 us
  other arithmetic  93.2 us (29%)
  local copies, waits for them, and re-layouts  80.8 us (25%)
  blocking collectives  57.8 us (18%)
  starting transfers between devices  26.7 us (8%)
  matrix products  22.1 us (7%)
  loops' own time  17.7 us (5%)
  between operations  14 us (4%)
  waiting for transfers between devices  5.27 us (2%)
    slice x42, local copies, waits for them, and re-layouts, advance(): running = running + window * taps[along_y * KS + along_z]  59.3 us
    psum x1, blocking collectives, on_device(): lax.psum((kernel_local, gain_local, bias_local, scale_local), 'row')  57.8 us
    add x14, other arithmetic, advance(): running = running + window * taps[along_y * KS + along_z]  39.7 us
    convert_element_type x14, other arithmetic, advance(): lax.dynamic_slice_in_dim(padded, start_x, planes, 0).astype(jnp.float32)  20.2 us
    reduce_sum x21, other arithmetic, one_plane(): rows_out.append(jnp.sum(window * grads_wide, axis=(0, 1, 2)))  16.8 us
    another operation x1, loops' own time, kernel_terms(): stacked = lax.map(one_plane, jnp.arange(KS, dtype=jnp.int32))  16.5 us
    convert_element_type x7, other arithmetic, one_plane(): lax.dynamic_slice_in_dim(padded, along_x, planes, 0).astype(jnp.float32)  10.1 us
    all_to_all x1, starting transfers between devices, on_device(): lax.all_to_all(activated, 'row', split_axis=1, concat_axis=0, tiled=True)  8.97 us
  transfers between devices with their start and end apart: 9, of which 2 were waited for; matrix products, arithmetic and copies ran while one was open for 41% of the time, Pallas kernels for 0%

commit v1 on v0

v1 whole, which is shorter than its diff:
```python
import functools

import jax
import jax.numpy as jnp
from jax import lax
from jax.experimental import pallas as pl
from jax.experimental.pallas import tpu as pltpu
from jax.sharding import PartitionSpec as P

KS = 7
MARGIN = KS // 2
LANES = 128
SUB = 8
PAD = 3 * SUB
TAP_ROWS = KS * KS * KS

root_half = 0.7071067811865476
inv_root_tau = 0.3989422804014327
norm_eps = 1e-06

F32 = jnp.float32
BF16 = jnp.bfloat16


def split_source(v):
    terms = []
    for a, b in ((v[0] + v[2], v[1] + v[3]), (v[2], v[3]), (v[0], v[1])):
        terms += [a + b, b, a]
    return terms


def split_taps(t):
    terms = []
    for s in (
        (t[2], t[3], t[4]),
        (t[4] - t[2], t[5] - t[3], t[6] - t[4]),
        (t[0] - t[2], t[1] - t[3], t[2] - t[4]),
    ):
        terms += [s[1], s[2] - s[1], s[0] - s[1]]
    return terms


def split_grads(g):
    terms = []
    for a, b in ((g[0] + g[2], g[1] + g[3]), (g[0], g[1]), (g[2], g[3])):
        terms += [a + b, a, b]
    return terms


def join_outputs(m):
    pair = [(m[3 * k] + m[3 * k + 1], m[3 * k] + m[3 * k + 2]) for k in range(3)]
    return [
        pair[0][0] + pair[1][0],
        pair[0][1] + pair[1][1],
        pair[0][0] + pair[2][0],
        pair[0][1] + pair[2][1],
    ]


def join_taps(m):
    p, q, r = [
        (m[3 * k + 2], m[3 * k] - m[3 * k + 1] - m[3 * k + 2], m[3 * k + 1]) for k in range(3)
    ]
    return [
        r[0],
        r[1],
        p[0] - q[0] - r[0] + r[2],
        p[1] - q[1] - r[1],
        p[2] - q[2] - r[2] + q[0],
        q[1],
        q[2],
    ]


def tree_sum(terms):
    while len(terms) > 1:
        terms = [
            terms[k] + terms[k + 1] if k + 1 < len(terms) else terms[k]
            for k in range(0, len(terms), 2)
        ]
    return terms[0]


def stage_source(blocks, height, spread):
    row = height * SUB
    at = 0
    for block in blocks:
        for x in range(block.shape[0] // row):
            plane = block[x * row : (x + 1) * row, :].astype(F32)
            lines = [plane[y * SUB : (y + 1) * SUB, :] for y in range(height)]
            for j, term in enumerate(split_source(lines)):
                spread[j, at, SUB : 2 * SUB, :] = term
            at += 1


def clear_rims(spread):
    zeros = jnp.zeros(spread.shape[:2] + (SUB, LANES), F32)
    spread[:, :, :SUB, :] = zeros
    spread[:, :, 2 * SUB :, :] = zeros


def stage_taps(taps, flipped, split):
    for dx in range(KS):
        rows = []
        for dy in range(KS):
            first = dx * KS * KS + dy * KS
            if first + SUB <= TAP_ROWS:
                rows.append(taps[first : first + SUB, :])
            else:
                rows.append(pltpu.roll(taps[TAP_ROWS - SUB : TAP_ROWS, :], SUB - 1, 0))
        if flipped:
            rows = rows[::-1]
        for j, term in enumerate(split_taps(rows)):
            split[j, KS - 1 - dx if flipped else dx] = term


def convolve(spread, split, planes, flipped):
    terms = []
    for j in range(9):
        sums = [None] * planes
        for dz in range(KS):
            first = SUB - MARGIN + dz
            source = [
                spread[j, x, first : first + SUB, :] for x in range(planes + KS - 1)
            ]
            at = KS - 1 - dz if flipped else dz
            weights = [
                jnp.broadcast_to(split[j, dx, at : at + 1, :], (SUB, LANES)) for dx in range(KS)
            ]
            for x in range(planes):
                part = tree_sum([source[x + dx] * weights[dx] for dx in range(KS)])
                sums[x] = part if sums[x] is None else sums[x] + part
        terms.append(sums)
    return [join_outputs([terms[j][x] for j in range(9)]) for x in range(planes)]


def forward_kernel(
    planes, height, left, own, right, taps, gain, bias, normed, unit, inv, spread, split, conv
):
    step = pl.program_id(0)

    @pl.when(step == 0)
    def _():
        clear_rims(spread)

    stage_source((left, own, right), height, spread)
    stage_taps(taps, False, split)
    rows = convolve(spread, split, planes, False)
    for x in range(planes):
        for y in range(height):
            at = (x * height + y) * SUB
            conv[step, at : at + SUB, :] = rows[x][y]

    @pl.when(step == pl.num_programs(0) - 1)
    def _():
        tiles = conv.shape[0]
        channels = tiles * LANES
        parts = [conv[k] for k in range(tiles)]
        average = jnp.sum(tree_sum(parts), axis=1, keepdims=True) * (1.0 / channels)
        parts = [part - average for part in parts]
        variance = jnp.sum(
            tree_sum([part * part for part in parts]), axis=1, keepdims=True
        ) * (1.0 / channels)
        inverse = lax.rsqrt(variance + norm_eps)
        inv[...] = jnp.broadcast_to(inverse, inv.shape)
        for k in range(tiles):
            lanes = slice(k * LANES, (k + 1) * LANES)
            value = parts[k] * inverse
            unit[:, lanes] = value
            normed[:, lanes] = (value * gain[:, lanes] + bias[:, lanes]).astype(BF16)


def input_grad_kernel(planes, height, left, own, right, taps, cotangent, out, spread, split):
    @pl.when(pl.program_id(0) == 0)
    def _():
        clear_rims(spread)

    stage_source((left, own, right), height, spread)
    stage_taps(taps, True, split)
    rows = convolve(spread, split, planes, True)
    for x in range(planes):
        at = x * height * SUB
        whole = jnp.concatenate(rows[x], axis=0)
        upstream = cotangent[at : at + height * SUB, :].astype(F32)
        out[at : at + height * SUB, :] = (upstream + whole).astype(BF16)


def kernel_grad_kernel(
    planes, height, left, own, right, grads, small, out, spread, products, joined, flat
):
    @pl.when(pl.program_id(0) == 0)
    def _():
        clear_rims(spread)
        products[...] = jnp.zeros(products.shape, F32)
        flat[...] = jnp.zeros(flat.shape, F32)

    stage_source((left, own, right), height, spread)
    upstream = []
    for x in range(planes):
        plane = grads[x * height * SUB : (x + 1) * height * SUB, :].astype(F32)
        upstream.append(
            split_grads([plane[y * SUB : (y + 1) * SUB, :] for y in range(height)])
        )
    for j in range(9):
        for dz in range(KS):
            first = SUB - MARGIN + dz
            source = [
                spread[j, x, first : first + SUB, :] for x in range(planes + KS - 1)
            ]
            for dx in range(KS):
                products[j % 2, dx, dz * SUB : (dz + 1) * SUB, :] = tree_sum(
                    [source[x + dx] * upstream[x][j] for x in range(planes)]
                )
        for dx in range(KS):
            joined[j, dx] = tree_sum(
                [products[j % 2, dx, pl.ds(s, SUB, stride=SUB), :] for s in range(SUB)]
            )
    for dx in range(KS):
        for dy, tile in enumerate(join_taps([joined[j, dx] for j in range(9)])):
            first = dx * KS * KS + dy * KS
            flat[first : first + SUB, :] = tile
    flat[TAP_ROWS : TAP_ROWS + SUB, :] = small[...]
    out[...] = flat[...].astype(out.dtype)


def mlp_kernel(
    normed,
    mixed_grad,
    weight_in,
    weight_out,
    unit,
    inv,
    gain,
    scale,
    voxels,
    cotangent,
    act_out,
    hid_out,
    block_out,
    conv_grad,
    small,
    mixed,
    back,
):
    step = pl.program_id(0)
    hidden = lax.dot_general(
        normed[...], weight_in[...], (((1,), (1,)), ((), ())), preferred_element_type=F32
    )
    act_grad = lax.dot_general(
        mixed_grad[...], weight_out[...], (((1,), (1,)), ((), ())), preferred_element_type=F32
    )
    cover = 0.5 * (1.0 + lax.erf(hidden * root_half))
    activated = (hidden * cover).astype(BF16)
    slope = cover + hidden * jnp.exp(-0.5 * hidden * hidden) * inv_root_tau
    hidden_grad = (act_grad * slope).astype(BF16)
    act_out[...] = activated.T
    hid_out[...] = hidden_grad.T
    forward = jnp.dot(activated, weight_out[...], preferred_element_type=F32)
    backward = jnp.dot(hidden_grad, weight_in[...], preferred_element_type=F32)

    @pl.when(step == 0)
    def _():
        mixed[...] = forward
        back[...] = backward

    @pl.when(step > 0)
    def _():
        mixed[...] += forward
        back[...] += backward

    @pl.when(step == pl.num_programs(0) - 1)
    def _():
        channels = gain.shape[1]
        whole = mixed[...]
        block_out[...] = (voxels[...].astype(F32) + scale[...] * whole).astype(BF16)
        scale_local = jnp.sum(cotangent[...].astype(F32) * whole, axis=0, keepdims=True)
        grad = back[...]
        one = unit[...]
        bias_local = jnp.sum(grad, axis=0, keepdims=True)
        gain_local = jnp.sum(grad * one, axis=0, keepdims=True)
        small[...] = jnp.concatenate(
            [gain_local, bias_local, scale_local, jnp.zeros((SUB - 3, channels), F32)], axis=0
        )
        scaled = grad * gain[...]
        average = jnp.sum(scaled, axis=1, keepdims=True) * (1.0 / channels)
        slant = jnp.sum(scaled * one, axis=1, keepdims=True) * (1.0 / channels)
        conv_grad[...] = (inv[:, :1] * (scaled - average - one * slant)).astype(BF16)


def weight_grad_kernel(which, act, hid, mixed_grad, normed, out_grad, in_grad):
    del which
    tokens = act.shape[2]
    for lhs, rhs, out in ((act, mixed_grad, out_grad), (hid, normed, in_grad)):
        total = None
        for k in range(act.shape[0]):
            part = jnp.dot(
                lhs[k], rhs[k * tokens : (k + 1) * tokens, :], preferred_element_type=F32
            )
            total = part if total is None else total + part
        out[...] = total


def params(limit=48):
    return pltpu.CompilerParams(vmem_limit_bytes=limit * 1024 * 1024)


def lane_block(rows):
    return pl.BlockSpec((rows, LANES), lambda c: (0, c))


def whole_block(*shape):
    return pl.BlockSpec(shape, lambda *_: (0,) * len(shape))


def halo(cells, axis, width):
    count = lax.axis_size(axis)
    ends = count - 1
    tail = cells[cells.shape[0] - width :]
    head = cells[:width]
    return (
        lax.ppermute(tail, axis, [(i, i + 1) for i in range(ends)]),
        lax.ppermute(head, axis, [(i + 1, i) for i in range(ends)]),
    )


def conv_cost(rows, channels):
    return pl.CostEstimate(
        flops=rows * channels * TAP_ROWS * 2, bytes_accessed=4 * rows * channels * 4, transcendentals=0
    )


def on_device(
    voxels, dw_kernel, norm_gain, norm_bias, weight_in, weight_out, layer_scale, cotangent
):
    planes, height, breadth, channels = voxels.shape
    rows = planes * height * breadth
    width = MARGIN * height * breadth
    units = weight_in.shape[0]
    count = lax.axis_size("row")
    me = lax.axis_index("row")
    half = count // 2
    alike = [[2 * k + p for k in range(half)] for p in range(2)]
    swap = [(i, i ^ 1) for i in range(count)]
    tiles = channels // LANES

    own = voxels.reshape(rows, channels)
    upstream = cotangent.reshape(rows, channels)
    gain = norm_gain.reshape(1, channels)
    bias = norm_bias.reshape(1, channels)
    scale = layer_scale.reshape(1, channels)

    left, right = halo(own, "row", width)
    mixed_grad = (scale * upstream.astype(F32)).astype(BF16)
    mixed_all = lax.all_gather(
        mixed_grad, "row", axis=0, tiled=True, axis_index_groups=alike
    )

    spread = pltpu.VMEM((9, planes + KS - 1, PAD, LANES), F32)
    split = pltpu.VMEM((9, KS, SUB, LANES), F32)

    normed, unit, inv = pl.pallas_call(
        functools.partial(forward_kernel, planes, height),
        grid=(tiles,),
        in_specs=[
            lane_block(width),
            lane_block(rows),
            lane_block(width),
            lane_block(TAP_ROWS),
            whole_block(1, channels),
            whole_block(1, channels),
        ],
        out_specs=[
            whole_block(rows, channels),
            whole_block(rows, channels),
            whole_block(rows, LANES),
        ],
        out_shape=[
            jax.ShapeDtypeStruct((rows, channels), BF16),
            jax.ShapeDtypeStruct((rows, channels), F32),
            jax.ShapeDtypeStruct((rows, LANES), F32),
        ],
        scratch_shapes=[spread, split, pltpu.VMEM((tiles, rows, LANES), F32)],
        compiler_params=params(),
        cost_estimate=conv_cost(rows, channels),
        name="forward_conv",
    )(left, own, right, dw_kernel, gain, bias)

    normed_all = lax.all_gather(normed, "row", axis=0, tiled=True, axis_index_groups=alike)

    block = 512
    whole = whole_block(rows, channels)
    line = whole_block(1, channels)
    act, hid, block_out, conv_grad, small = pl.pallas_call(
        mlp_kernel,
        grid=(units // block,),
        in_specs=[
            whole,
            whole,
            pl.BlockSpec((block, channels), lambda f: (f, 0)),
            pl.BlockSpec((block, channels), lambda f: (f, 0)),
            whole,
            whole_block(rows, LANES),
            line,
            line,
            whole,
            whole,
        ],
        out_specs=[
            pl.BlockSpec((block, rows), lambda f: (f, 0)),
            pl.BlockSpec((block, rows), lambda f: (f, 0)),
            whole,
            whole,
            whole_block(SUB, channels),
        ],
        out_shape=[
            jax.ShapeDtypeStruct((units, rows), BF16),
            jax.ShapeDtypeStruct((units, rows), BF16),
            jax.ShapeDtypeStruct((rows, channels), BF16),
            jax.ShapeDtypeStruct((rows, channels), BF16),
            jax.ShapeDtypeStruct((SUB, channels), F32),
        ],
        scratch_shapes=[pltpu.VMEM((rows, channels), F32), pltpu.VMEM((rows, channels), F32)],
        compiler_params=params(),
        cost_estimate=pl.CostEstimate(
            flops=8 * rows * channels * units,
            bytes_accessed=4 * units * channels + 4 * units * rows,
            transcendentals=2 * rows * units,
        ),
        name="mlp_both_ways",
    )(
        normed,
        mixed_grad,
        weight_in,
        weight_out,
        unit,
        inv,
        gain,
        scale,
        own,
        upstream,
    )

    grad_left, grad_right = halo(conv_grad, "row", width)

    piece = -(-(TAP_ROWS + SUB) // count)
    piece += -piece % SUB if count <= 16 else 0
    padded = piece * count
    sums = pl.pallas_call(
        functools.partial(kernel_grad_kernel, planes, height),
        grid=(tiles,),
        in_specs=[
            lane_block(width),
            lane_block(rows),
            lane_block(width),
            lane_block(rows),
            lane_block(SUB),
        ],
        out_specs=lane_block(padded),
        out_shape=jax.ShapeDtypeStruct((padded, channels), BF16),
        scratch_shapes=[
            spread,
            pltpu.VMEM((2, KS, SUB * SUB, LANES), F32),
            pltpu.VMEM((9, KS, SUB, LANES), F32),
            pltpu.VMEM((padded, LANES), F32),
        ],
        compiler_params=params(),
        cost_estimate=conv_cost(rows, channels),
        name="kernel_grad_terms",
    )(left, own, right, conv_grad, small)

    scattered = lax.all_to_all(sums, "row", split_axis=0, concat_axis=0, tiled=True)
    act_all = lax.all_to_all(
        act.reshape(half, units // half, rows),
        "row",
        split_axis=0,
        concat_axis=0,
        tiled=True,
        axis_index_groups=alike,
    )
    hid_all = lax.all_to_all(
        hid.reshape(half, units // half, rows),
        "row",
        split_axis=0,
        concat_axis=0,
        tiled=True,
        axis_index_groups=alike,
    )

    voxel_grad = pl.pallas_call(
        functools.partial(input_grad_kernel, planes, height),
        grid=(tiles,),
        in_specs=[
            lane_block(width),
            lane_block(rows),
            lane_block(width),
            lane_block(TAP_ROWS),
            lane_block(rows),
        ],
        out_specs=lane_block(rows),
        out_shape=jax.ShapeDtypeStruct((rows, channels), BF16),
        scratch_shapes=[spread, split],
        compiler_params=params(),
        cost_estimate=conv_cost(rows, channels),
        name="input_grad_conv",
    )(grad_left, conv_grad, grad_right, dw_kernel, upstream)

    summed = jnp.sum(scattered.reshape(count, piece, channels).astype(F32), axis=0)
    gathered = lax.all_gather(summed.astype(BF16), "row", axis=0, tiled=True)
    totals = gathered.astype(F32)
    kernel_grad = totals[:TAP_ROWS]
    gain_grad = totals[TAP_ROWS]
    bias_grad = totals[TAP_ROWS + 1]
    scale_grad = totals[TAP_ROWS + 2]

    mine = units // count
    tokens = half * rows

    def weight_grads(which, name):
        return pl.pallas_call(
            weight_grad_kernel,
            grid_spec=pltpu.PrefetchScalarGridSpec(
                num_scalar_prefetch=1,
                grid=(1,),
                in_specs=[
                    pl.BlockSpec((half, mine, rows), lambda _, w: (0, w[0], 0)),
                    pl.BlockSpec((half, mine, rows), lambda _, w: (0, w[0], 0)),
                    whole_block(tokens, channels),
                    whole_block(tokens, channels),
                ],
                out_specs=[whole_block(mine, channels), whole_block(mine, channels)],
            ),
            out_shape=[
                jax.ShapeDtypeStruct((mine, channels), F32),
                jax.ShapeDtypeStruct((mine, channels), F32),
            ],
            compiler_params=params(),
            cost_estimate=pl.CostEstimate(
                flops=4 * tokens * channels * mine,
                bytes_accessed=4 * tokens * channels + 4 * mine * tokens,
                transcendentals=0,
            ),
            name=name,
        )(which.reshape(1), act_all, hid_all, mixed_all, normed_all)

    core = lax.rem(me, 2).astype(jnp.int32)
    sent = weight_grads(1 - core, "weight_grads_sent")
    got = [lax.ppermute(part, "row", swap) for part in sent]
    kept = weight_grads(core, "weight_grads_kept")
    weight_out_grad = kept[0] + got[0]
    weight_in_grad = kept[1] + got[1]

    return (
        block_out.reshape(voxels.shape),
        voxel_grad.reshape(voxels.shape),
        kernel_grad,
        gain_grad,
        bias_grad,
        scale_grad,
        weight_in_grad,
        weight_out_grad,
    )


def solution(mesh):
    in_specs = (
        P(("group", "row"), None, None, None),
        P(),
        P(),
        P(),
        P(),
        P(),
        P(),
        P(("group", "row"), None, None, None),
    )
    out_specs = (
        P(("group", "row"), None, None, None),
        P(("group", "row"), None, None, None),
        P("group", None),
        P("group"),
        P("group"),
        P("group"),
        P(("group", "row"), None),
        P(("group", "row"), None),
    )
    return jax.shard_map(
        on_device, mesh=mesh, in_specs=in_specs, out_specs=out_specs, check_vma=False
    )
```

time: 324 us -> 179 us (0.55); the launches traced: 318 us -> 177 us
  other arithmetic: 93.2 us -> 6.87 us
  local copies, waits for them, and re-layouts: 80.8 us -> 12.9 us
  waiting for transfers between devices: 5.27 us -> 68.3 us
  blocking collectives: 57.8 us -> 22.1 us
  Pallas kernels: 0 us -> 26.5 us
  matrix products: 22.1 us -> 0 us
  loops' own time: 17.7 us -> 0 us
    psum x1 -> x0, blocking collectives: 57.8 us -> none  [on_device(): lax.psum((kernel_local, gain_local, bias_local, scale_local), 'row')]
    slice x44 -> x4, local copies, waits for them, and re-layouts: 61 us -> 3.35 us  [the longest x2 1.69 us: halo(): head = cells[:width]]
    all_to_all x2 -> x3, waiting for transfers between devices: 0.01 us -> 48 us  [the longest x1 27.6 us: on_device(): lax.all_to_all(act.reshape(half, units // half, rows), 'row', split_axis=...]
    add x14 -> x2, other arithmetic: 39.7 us -> 3.9 us  [the longest x1 1.96 us: on_device(): weight_in_grad = kept[1] + got[1]]
    convert_element_type x25 -> x2, other arithmetic: 32 us -> 1.81 us  [the longest x1 1.73 us: on_device(): mixed_grad = (scale * upstream.astype(F32)).astype(BF16)]
    pallas_call x0 -> x6, Pallas kernels: none -> 26.5 us  [the longest x1 9.37 us: on_device(): pl.pallas_call(mlp_kernel, grid=(units // block,), in_specs=[whole, whole...]
    dot_general x6 -> x0, matrix products: 22.1 us -> none  [the longest x2 7.22 us: contract_rows(): lax.dot_general(left, right, (((0,), (0,)), ((), ())), preferred_element_...]
    all_gather x0 -> x1, blocking collectives: none -> 22.1 us  [on_device(): gathered = lax.all_gather(summed.astype(BF16), 'row', axis=0, tiled=True)]
  transfers between devices with their start and end apart: 9 -> 11, of which waited for: 2 -> 4; matrix products, arithmetic and copies ran while one was open for 41% -> 5% of each run, Pallas kernels for 0% -> 15%
where the time goes in v1:
time: 179 us; the launch traced here: 177 us
  waiting for transfers between devices  68.3 us (38%)
  starting transfers between devices  26.7 us (15%)
  Pallas kernels  26.5 us (15%)
  blocking collectives  22.1 us (12%)
  between operations  14.2 us (8%)
  local copies, waits for them, and re-layouts  12.9 us (7%)
  other arithmetic  6.87 us (4%)
    all_to_all x1, waiting for transfers between devices, on_device(): lax.all_to_all(act.reshape(half, units // half, rows), 'row', split_axis=...  27.6 us
    all_gather x1, blocking collectives, on_device(): gathered = lax.all_gather(summed.astype(BF16), 'row', axis=0, tiled=True)  22.1 us
    all_to_all x1, waiting for transfers between devices, on_device(): lax.all_to_all(hid.reshape(half, units // half, rows), 'row', split_axis=...  20.4 us
    all_gather x1, waiting for transfers between devices, on_device(): lax.all_gather(normed, 'row', axis=0, tiled=True, axis_index_groups=alike)  17.1 us
    pallas_call x1, Pallas kernels, on_device(): pl.pallas_call(mlp_kernel, grid=(units // block,), in_specs=[whole, whole...  9.37 us
    ppermute x2, starting transfers between devices, halo(): lax.ppermute(tail, axis, [(i, i + 1) for i in range(ends)])  8.07 us
    unnamed x26, local copies, waits for them, and re-layouts  7.45 us
    all_to_all x1, starting transfers between devices, on_device(): lax.all_to_all(act.reshape(half, units // half, rows), 'row', split_axis=...  5.42 us
  transfers between devices with their start and end apart: 11, of which 4 were waited for; matrix products, arithmetic and copies ran while one was open for 5% of the time, Pallas kernels for 15%

profile of v1, /device:TPU:1, one launch (start us, length us, event | category | flops | bytes accessed | tf_op | source)
XLA Modules:
  0.0 177.4 jit_solution(16856234088891863167)
XLA Ops:
  7.2 0.0 all-gather.3.cloned.1.call-start
  7.2 1.7 multiply_convert_fusion.mixed_grad
  9.0 0.0 all-gather.3.cloned.1.call-update
  9.0 1.0 fusion.1
  10.0 4.5 %collective-permute-start = (bf16[96,768]{1,0:T(8,128)(2,1)S(1)}, bf16[96,768]{1,0:T(8,128)(2,1)S(1)}, u32[]{:S(2)}, u32[]{:S(2)}) collective-permute-start(bf16[96,768]{1,0:T(8,128)(2,1)S(1)} %bitcast.21), channel_id=1, source_target_pairs={{0,1},{1,2},{2,3},{3,4},{4,5},{5,6},{6,7},{7,8},{8,9},{9,10},{10,1... | collective-permute-start | bytes 442376 | tf_op jit(solution)/shard_map/ppermute | solution.py:321
  14.5 1.9 %collective-permute-start.1 = (bf16[96,768]{1,0:T(8,128)(2,1)S(1)}, bf16[96,768]{1,0:T(8,128)(2,1)S(1)}, u32[]{:S(2)}, u32[]{:S(2)}) collective-permute-start(bf16[96,768]{1,0:T(8,128)(2,1)S(1)} %bitcast.20), channel_id=1, source_target_pairs={{1,0},{2,1},{3,2},{4,3},{5,4},{6,5},{7,6},{8,7},{9,8},{10,9},{11,1... | collective-permute-start | bytes 442376 | tf_op jit(solution)/shard_map/ppermute | solution.py:322
  16.5 0.7 reshape.60.scale
  17.2 0.7 reshape.57.gain
  17.8 0.7 reshape.58.bias
  18.5 2.5 %collective-permute-done.1.right = bf16[96,768]{1,0:T(8,128)(2,1)S(1)} collective-permute-done((bf16[96,768]{1,0:T(8,128)(2,1)S(1)}, bf16[96,768]{1,0:T(8,128)(2,1)S(1)}, u32[]{:S(2)}, u32[]{:S(2)}) %collective-permute-start.1) | collective-permute-done | bytes 147488 | tf_op jit(solution)/shard_map/ppermute | solution.py:322
  21.0 0.9 copy-done.5
  21.9 4.3 %forward_conv.1 = (bf16[128,768]{1,0:T(8,128)(2,1)}, f32[128,768]{1,0:T(8,128)S(1)}, f32[128,128]{1,0:T(8,128)S(1)}) custom-call(bf16[96,768]{1,0:T(8,128)(2,1)S(1)} %collective-permute-done.left, bf16[128,768]{1,0:T(8,128)(2,1)S(1)} %bitcast.12, bf16[96,768]{1,0:T(8,128)(2,1)S(1)} %collective-permute-done.1.right, f32[343,768]{1,0:T(8,128)S(1)} %copy-done.4, ...), custom_call_target="tpu_custom_call" | custom-call | flops 67436544 | bytes 1572864 | tf_op jit(solution)/shard_map/forward_conv/pallas_call | solution.py:361
  26.3 0.6 copy-done.11
  26.9 0.8 copy-done.12
  27.7 9.4 %mlp_both_ways.1 = (bf16[3072,128]{1,0:T(8,128)(2,1)}, bf16[3072,128]{1,0:T(8,128)(2,1)S(1)}, bf16[128,768]{1,0:T(8,128)(2,1)}, bf16[128,768]{1,0:T(8,128)(2,1)S(1)}, f32[8,768]{1,0:T(8,128)S(1)}) custom-call(bf16[128,768]{1,0:T(8,128)(2,1)} %get-tuple-element.20.normed, bf16[128,768]{1,0:T(8,128)(2,1)S(1)} %copy-done.9, bf16[3072,768]{1,0:T(8,128)(2,1)} %weight_in.1, ...), custom_call_target="tpu_custom_call" | custom-call | flops 2415919104 | bytes 11010048 | tf_op jit(solution)/shard_map/mlp_both_ways/pallas_call | solution.py:393
  37.1 0.9 copy-done.10
  38.0 5.4 %all-to-all-start.1 = ((bf16[8,384,128]{2,1,0:T(8,128)(2,1)}), bf16[8,384,128]{2,1,0:T(8,128)(2,1)S(1)}, u32[]{:S(2)}, u32[]{:S(2)}) async-start(bf16[8,384,128]{2,1,0:T(8,128)(2,1)} %bitcast.8), calls=%async_computation.1 | async-start | bytes 1572864 | tf_op jit(solution)/shard_map/all_to_all | solution.py:472
  43.4 0.0 all-gather.5.cloned.1.call-start
  43.5 0.7 all-gather.5.cloned.1.call-update
  44.2 27.6 %all-to-all-done.1.act = bf16[8,384,128]{2,1,0:T(8,128)(2,1)S(1)} async-done(((bf16[8,384,128]{2,1,0:T(8,128)(2,1)}), bf16[8,384,128]{2,1,0:T(8,128)(2,1)S(1)}, u32[]{:S(2)}, u32[]{:S(2)}) %all-to-all-start.1) | async-done | bytes 786464 | tf_op jit(solution)/shard_map/all_to_all | solution.py:472
  71.8 3.5 %all-to-all-start.2 = ((bf16[8,384,128]{2,1,0:T(8,128)(2,1)}), bf16[8,384,128]{2,1,0:T(8,128)(2,1)S(1)}, u32[]{:S(2)}, u32[]{:S(2)}) async-start(bf16[8,384,128]{2,1,0:T(8,128)(2,1)} %bitcast.18), calls=%async_computation.2 | async-start | bytes 1572864 | tf_op jit(solution)/shard_map/all_to_all | solution.py:480
  75.3 4.8 %kernel_grad_terms.1 = bf16[384,768]{1,0:T(8,128)(2,1)S(1)} custom-call(bf16[96,768]{1,0:T(8,128)(2,1)S(1)} %collective-permute-done.left, bf16[128,768]{1,0:T(8,128)(2,1)S(1)} %bitcast.14, bf16[96,768]{1,0:T(8,128)(2,1)S(1)} %collective-permute-done.1.right, bf16[128,768]{1,0:T(8,128)(2,1)S(1)} %get-tuple-element.24.own.grads, ...), custom_call_target="tpu_custom_call" | custom-call | flops 67436544 | bytes 1572864 | tf_op jit(solution)/shard_map/kernel_grad_terms/pallas_call | solution.py:448
  80.2 0.0 copy-start.7
  80.2 0.8 copy-done.7
  81.0 20.4 %all-to-all-done.2.hid = bf16[8,384,128]{2,1,0:T(8,128)(2,1)S(1)} async-done(((bf16[8,384,128]{2,1,0:T(8,128)(2,1)}), bf16[8,384,128]{2,1,0:T(8,128)(2,1)S(1)}, u32[]{:S(2)}, u32[]{:S(2)}) %all-to-all-start.2) | async-done | bytes 786464 | tf_op jit(solution)/shard_map/all_to_all | solution.py:480
  101.4 5.2 %all-to-all-start = ((bf16[16,24,768]{2,1,0:T(8,128)(2,1)}), bf16[16,24,768]{2,1,0:T(8,128)(2,1)}, u32[]{:S(2)}, u32[]{:S(2)}) async-start(bf16[16,24,768]{2,1,0:T(8,128)(2,1)} %bitcast.15), calls=%async_computation | async-start | bytes 1179648 | tf_op jit(solution)/shard_map/all_to_all | solution.py:471
  106.6 0.7 fusion
  107.3 3.5 %collective-permute-start.2 = (bf16[96,768]{1,0:T(8,128)(2,1)}, bf16[96,768]{1,0:T(8,128)(2,1)S(1)}, u32[]{:S(2)}, u32[]{:S(2)}) collective-permute-start(bf16[96,768]{1,0:T(8,128)(2,1)} %get-tuple-element.36), channel_id=1, source_target_pairs={{0,1},{1,2},{2,3},{3,4},{4,5},{5,6},{6,7},{7,8},{8,9},{9,10},{10,1... | collective-permute-start | bytes 442376 | tf_op jit(solution)/shard_map/ppermute | solution.py:321
  110.9 1.9 %collective-permute-start.3 = (bf16[96,768]{1,0:T(8,128)(2,1)S(1)}, bf16[96,768]{1,0:T(8,128)(2,1)S(1)}, u32[]{:S(2)}, u32[]{:S(2)}) collective-permute-start(bf16[96,768]{1,0:T(8,128)(2,1)S(1)} %get-tuple-element.35), channel_id=1, source_target_pairs={{1,0},{2,1},{3,2},{4,3},{5,4},{6,5},{7,6},{8,7},{9,8},{10,9},{11,1... | collective-permute-start | bytes 442376 | tf_op jit(solution)/shard_map/ppermute | solution.py:322
  112.8 0.0 all-gather.3.cloned.1.call-done.mixed_grad
  112.8 17.1 %all-gather.5.cloned.1.call-done.normed = bf16[1024,768]{1,0:T(8,128)(2,1)} async-done(((bf16[128,768]{1,0:T(8,128)(2,1)}), bf16[1024,768]{1,0:T(8,128)(2,1)}) %all-gather.5.cloned.1.call-update) | async-done | bytes 1572880 | tf_op jit(solution)/shard_map/all_gather | solution.py:388
  129.9 1.4 copy-done
  131.3 1.4 copy-done.2
  132.7 2.4 %weight_grads_sent.1 = (f32[192,768]{1,0:T(8,128)}, f32[192,768]{1,0:T(8,128)}) custom-call(s32[1]{0:T(128)} %bitcast.10.which, bf16[8,384,128]{2,1,0:T(8,128)(2,1)S(1)} %all-to-all-done.1.act, bf16[8,384,128]{2,1,0:T(8,128)(2,1)S(1)} %all-to-all-done.2.hid, bf16[1024,768]{1,0:T(8,128)(2,1)S(1)} %copy-done, bf16[1024,768]{1,0:T(8,128)(2,1)S(1)} %copy-done.2), custom_call_target="tpu_custom_call" | custom-call | flops 603979776 | bytes 3932160 | tf_op jit(solution)/shard_map/weight_grads_sent/pallas_call | solution.py:519
  135.1 0.5 collective-permute-start.5
  135.6 0.1 collective-permute-start.4
  135.6 0.0 collective-permute-done.3.right
  135.6 4.1 %input_grad_conv.1 = bf16[128,768]{1,0:T(8,128)(2,1)} custom-call(bf16[96,768]{1,0:T(8,128)(2,1)S(1)} %collective-permute-done.2.left, bf16[128,768]{1,0:T(8,128)(2,1)S(1)} %get-tuple-element.24.own.grads, bf16[96,768]{1,0:T(8,128)(2,1)S(1)} %collective-permute-done.3.right, f32[343,768]{1,0:T(8,128)S(1)} %copy-done.4, bf16[128,768]{1,0:T(8,128)(2,1)S(1)} %bitcast.17), custom_call_target="tpu_custom_call" | custom-call | flops 67436544 | bytes 1572864 | tf_op jit(solution)/shard_map/input_grad_conv/pallas_call | solution.py:489
  139.8 1.2 reduce_sum.12
  140.9 22.1 %all_gather.9 = bf16[384,768]{1,0:T(8,128)(2,1)S(1)} all-gather(bf16[24,768]{1,0:T(8,128)(2,1)S(1)} %reduce_sum.12), channel_id=1, replica_groups=mesh['group'=2,'row'=16] {'row'}, dimensions={0}, use_global_device_ids=true | all-gather | bytes 626688 | tf_op jit(solution)/shard_map/all_gather | solution.py:508
  163.0 0.1 convert_element_type.13
  163.1 1.0 slice.40
  164.1 0.6 slice_reduce_fusion
  164.8 0.0 copy-done.1
  164.8 0.5 copy-done.3
  165.3 1.4 weight_grads_kept.1
  166.7 1.9 %add.7 = f32[192,768]{1,0:T(8,128)} add(f32[192,768]{1,0:T(8,128)S(1)} %get-tuple-element.30, f32[192,768]{1,0:T(8,128)} %collective-permute-done.5) | non-fusion elementwise | flops 147456 | bytes 1769472 | tf_op jit(solution)/shard_map/add | solution.py:549
  168.6 2.0 %add.6 = f32[192,768]{1,0:T(8,128)} add(f32[192,768]{1,0:T(8,128)S(1)} %get-tuple-element.28, f32[192,768]{1,0:T(8,128)} %collective-permute-done.4) | non-fusion elementwise | flops 147456 | bytes 1769472 | tf_op jit(solution)/shard_map/add | solution.py:550
  (21 shorter events, 0.0 us)
Async XLA Ops:
  7.2 13.8 %copy-start.4 = (f32[343,768]{1,0:T(8,128)S(1)}, f32[343,768]{1,0:T(8,128)}, u32[]{:S(2)}) copy-start(f32[343,768]{1,0:T(8,128)} %taps.3) | copy-start | bytes 3161092
  7.2 105.6 %all-gather.3.cloned.1.call-start = ((), (), s32[]{:S(2)}) async-start(), calls=%async_computation.3 | async-start | bytes 1769472 | tf_op jit(solution)/shard_map/all_gather | solution.py:354
  10.0 8.5 %collective-permute-start = (bf16[96,768]{1,0:T(8,128)(2,1)S(1)}, bf16[96,768]{1,0:T(8,128)(2,1)S(1)}, u32[]{:S(2)}, u32[]{:S(2)}) collective-permute-start(bf16[96,768]{1,0:T(8,128)(2,1)S(1)} %bitcast.21), channel_id=1, source_target_pairs={{0,1},{1,2},{2,3},{3,4},{4,5},{5,6},{6,7},{7,8},{8,9},{9,10},{10,1... | collective-permute-start | bytes 442376 | tf_op jit(solution)/shard_map/ppermute | solution.py:321
  14.5 6.5 %collective-permute-start.1 = (bf16[96,768]{1,0:T(8,128)(2,1)S(1)}, bf16[96,768]{1,0:T(8,128)(2,1)S(1)}, u32[]{:S(2)}, u32[]{:S(2)}) collective-permute-start(bf16[96,768]{1,0:T(8,128)(2,1)S(1)} %bitcast.20), channel_id=1, source_target_pairs={{1,0},{2,1},{3,2},{4,3},{5,4},{6,5},{7,6},{8,7},{9,8},{10,9},{11,1... | collective-permute-start | bytes 442376 | tf_op jit(solution)/shard_map/ppermute | solution.py:322
  21.0 0.9 copy-start.5
  21.9 5.0 %copy-start.6 = (bf16[4,4,8,768]{3,2,1,0:T(8,128)(2,1)S(1)}, bf16[4,4,8,768]{3,2,1,0:T(8,128)(2,1)}, u32[]{:S(2)}) copy-start(bf16[4,4,8,768]{3,2,1,0:T(8,128)(2,1)} %param.8) | copy-start | bytes 589828
  21.9 5.0 %copy-start.8 = (bf16[4,4,8,768]{3,2,1,0:T(8,128)(2,1)S(1)}, bf16[4,4,8,768]{3,2,1,0:T(8,128)(2,1)}, u32[]{:S(2)}) copy-start(bf16[4,4,8,768]{3,2,1,0:T(8,128)(2,1)} %param.15) | copy-start | bytes 589828
  21.9 5.0 %copy-start.9 = (bf16[128,768]{1,0:T(8,128)(2,1)S(1)}, bf16[128,768]{1,0:T(8,128)(2,1)}, u32[]{:S(2)}) copy-start(bf16[128,768]{1,0:T(8,128)(2,1)} %multiply_convert_fusion.mixed_grad) | copy-start | bytes 589828
  26.3 0.6 copy-start.11
  26.9 0.8 copy-start.12
  37.1 0.9 copy-start.10
  38.0 33.8 %all-to-all-start.1 = ((bf16[8,384,128]{2,1,0:T(8,128)(2,1)}), bf16[8,384,128]{2,1,0:T(8,128)(2,1)S(1)}, u32[]{:S(2)}, u32[]{:S(2)}) async-start(bf16[8,384,128]{2,1,0:T(8,128)(2,1)} %bitcast.8), calls=%async_computation.1 | async-start | bytes 1572864 | tf_op jit(solution)/shard_map/all_to_all | solution.py:472
  43.4 86.5 %all-gather.5.cloned.1.call-start = ((), (), s32[]{:S(2)}) async-start(), calls=%async_computation.4 | async-start | bytes 1769472 | tf_op jit(solution)/shard_map/all_gather | solution.py:388
  71.8 29.7 %all-to-all-start.2 = ((bf16[8,384,128]{2,1,0:T(8,128)(2,1)}), bf16[8,384,128]{2,1,0:T(8,128)(2,1)S(1)}, u32[]{:S(2)}, u32[]{:S(2)}) async-start(bf16[8,384,128]{2,1,0:T(8,128)(2,1)} %bitcast.18), calls=%async_computation.2 | async-start | bytes 1572864 | tf_op jit(solution)/shard_map/all_to_all | solution.py:480
  80.2 0.8 copy-start.7
  101.4 38.4 %all-to-all-start = ((bf16[16,24,768]{2,1,0:T(8,128)(2,1)}), bf16[16,24,768]{2,1,0:T(8,128)(2,1)}, u32[]{:S(2)}, u32[]{:S(2)}) async-start(bf16[16,24,768]{2,1,0:T(8,128)(2,1)} %bitcast.15), calls=%async_computation | async-start | bytes 1179648 | tf_op jit(solution)/shard_map/all_to_all | solution.py:471
  107.3 28.3 %collective-permute-start.2 = (bf16[96,768]{1,0:T(8,128)(2,1)}, bf16[96,768]{1,0:T(8,128)(2,1)S(1)}, u32[]{:S(2)}, u32[]{:S(2)}) collective-permute-start(bf16[96,768]{1,0:T(8,128)(2,1)} %get-tuple-element.36), channel_id=1, source_target_pairs={{0,1},{1,2},{2,3},{3,4},{4,5},{5,6},{6,7},{7,8},{8,9},{9,10},{10,1... | collective-permute-start | bytes 442376 | tf_op jit(solution)/shard_map/ppermute | solution.py:321
  110.9 24.8 %collective-permute-start.3 = (bf16[96,768]{1,0:T(8,128)(2,1)S(1)}, bf16[96,768]{1,0:T(8,128)(2,1)S(1)}, u32[]{:S(2)}, u32[]{:S(2)}) collective-permute-start(bf16[96,768]{1,0:T(8,128)(2,1)S(1)} %get-tuple-element.35), channel_id=1, source_target_pairs={{1,0},{2,1},{3,2},{4,3},{5,4},{6,5},{7,6},{8,7},{9,8},{10,9},{11,1... | collective-permute-start | bytes 442376 | tf_op jit(solution)/shard_map/ppermute | solution.py:322
  129.9 1.4 copy-start
  131.3 1.4 copy-start.2
  135.1 31.6 %collective-permute-start.5 = (f32[192,768]{1,0:T(8,128)}, f32[192,768]{1,0:T(8,128)}, u32[]{:S(2)}, u32[]{:S(2)}) collective-permute-start(f32[192,768]{1,0:T(8,128)} %get-tuple-element.31), channel_id=1, source_target_pairs={{0,1},{1,0},{2,3},{3,2},{4,5},{5,4},{6,7},{7,6},{8,9},{9,8},{10,11... | collective-permute-start | bytes 1769480 | tf_op jit(solution)/shard_map/ppermute | solution.py:547
  135.6 33.1 %collective-permute-start.4 = (f32[192,768]{1,0:T(8,128)}, f32[192,768]{1,0:T(8,128)}, u32[]{:S(2)}, u32[]{:S(2)}) collective-permute-start(f32[192,768]{1,0:T(8,128)} %get-tuple-element.29), channel_id=1, source_target_pairs={{0,1},{1,0},{2,3},{3,2},{4,5},{5,4},{6,7},{7,6},{8,9},{9,8},{10,11... | collective-permute-start | bytes 1769480 | tf_op jit(solution)/shard_map/ppermute | solution.py:547
  163.0 1.8 %copy-start.1 = (bf16[1024,768]{1,0:T(8,128)(2,1)S(1)}, bf16[1024,768]{1,0:T(8,128)(2,1)}, u32[]{:S(2)}) copy-start(bf16[1024,768]{1,0:T(8,128)(2,1)} %all-gather.3.cloned.1.call-done.mixed_grad) | copy-start | bytes 4718596
  163.0 2.3 %copy-start.3 = (bf16[1024,768]{1,0:T(8,128)(2,1)S(1)}, bf16[1024,768]{1,0:T(8,128)(2,1)}, u32[]{:S(2)}) copy-start(bf16[1024,768]{1,0:T(8,128)(2,1)} %all-gather.5.cloned.1.call-done.normed) | copy-start | bytes 4718596
Sparse Core Ops, SparseCore 0:
  10.8 59.5 all-gather.2
  73.1 56.6 all-gather.4

commit v2 on v1

--- a/solution.py
+++ b/solution.py
@@ -81,16 +81,16 @@
     return terms[0]
 
 
-def stage_source(blocks, height, spread):
+def stage_source(left, own, right, planes, height, spread):
     row = height * SUB
-    at = 0
-    for block in blocks:
-        for x in range(block.shape[0] // row):
-            plane = block[x * row : (x + 1) * row, :].astype(F32)
-            lines = [plane[y * SUB : (y + 1) * SUB, :] for y in range(height)]
-            for j, term in enumerate(split_source(lines)):
-                spread[j, at, SUB : 2 * SUB, :] = term
-            at += 1
+    wanted = [(left, x) for x in range(planes - MARGIN, planes)]
+    wanted += [(own, x) for x in range(planes)]
+    wanted += [(right, x) for x in range(MARGIN)]
+    for at, (block, x) in enumerate(wanted):
+        plane = block[x * row : (x + 1) * row, :].astype(F32)
+        lines = [plane[y * SUB : (y + 1) * SUB, :] for y in range(height)]
+        for j, term in enumerate(split_source(lines)):
+            spread[j, at, SUB : 2 * SUB, :] = term
 
 
 def clear_rims(spread):
@@ -143,7 +143,7 @@
     def _():
         clear_rims(spread)
 
-    stage_source((left, own, right), height, spread)
+    stage_source(left, own, right, planes, height, spread)
     stage_taps(taps, False, split)
     rows = convolve(spread, split, planes, False)
     for x in range(planes):
@@ -167,7 +167,9 @@
             lanes = slice(k * LANES, (k + 1) * LANES)
             value = parts[k] * inverse
             unit[:, lanes] = value
-            normed[:, lanes] = (value * gain[:, lanes] + bias[:, lanes]).astype(BF16)
+            whole = (value * gain[:, lanes] + bias[:, lanes]).astype(BF16)
+            for copy in range(normed.shape[0]):
+                normed[copy, :, lanes] = whole
 
 
 def input_grad_kernel(planes, height, left, own, right, taps, cotangent, out, spread, split):
@@ -175,7 +177,7 @@
     def _():
         clear_rims(spread)
 
-    stage_source((left, own, right), height, spread)
+    stage_source(left, own, right, planes, height, spread)
     stage_taps(taps, True, split)
     rows = convolve(spread, split, planes, True)
     for x in range(planes):
@@ -186,15 +188,17 @@
 
 
 def kernel_grad_kernel(
-    planes, height, left, own, right, grads, small, out, spread, products, joined, flat
+    planes, height, which, left, own, right, grads, small, out, spread, products, joined, flat
 ):
+    del which
+
     @pl.when(pl.program_id(0) == 0)
     def _():
         clear_rims(spread)
         products[...] = jnp.zeros(products.shape, F32)
         flat[...] = jnp.zeros(flat.shape, F32)
 
-    stage_source((left, own, right), height, spread)
+    stage_source(left, own, right, planes, height, spread)
     upstream = []
     for x in range(planes):
         plane = grads[x * height * SUB : (x + 1) * height * SUB, :].astype(F32)
@@ -225,7 +229,6 @@
 
 def mlp_kernel(
     normed,
-    mixed_grad,
     weight_in,
     weight_out,
     unit,
@@ -234,27 +237,26 @@
     scale,
     voxels,
     cotangent,
-    act_out,
-    hid_out,
     block_out,
     conv_grad,
     small,
     mixed,
     back,
+    mixed_grad,
 ):
     step = pl.program_id(0)
+
+    @pl.when(step == 0)
+    def _():
+        mixed_grad[...] = (scale[...] * cotangent[...].astype(F32)).astype(BF16)
+
     hidden = lax.dot_general(
         normed[...], weight_in[...], (((1,), (1,)), ((), ())), preferred_element_type=F32
     )
     act_grad = lax.dot_general(
         mixed_grad[...], weight_out[...], (((1,), (1,)), ((), ())), preferred_element_type=F32
     )
-    cover = 0.5 * (1.0 + lax.erf(hidden * root_half))
-    activated = (hidden * cover).astype(BF16)
-    slope = cover + hidden * jnp.exp(-0.5 * hidden * hidden) * inv_root_tau
-    hidden_grad = (act_grad * slope).astype(BF16)
-    act_out[...] = activated.T
-    hid_out[...] = hidden_grad.T
+    activated, hidden_grad = slopes(hidden, act_grad)
     forward = jnp.dot(activated, weight_out[...], preferred_element_type=F32)
     backward = jnp.dot(hidden_grad, weight_in[...], preferred_element_type=F32)
 
@@ -287,17 +289,69 @@
         conv_grad[...] = (inv[:, :1] * (scaled - average - one * slant)).astype(BF16)
 
 
-def weight_grad_kernel(which, act, hid, mixed_grad, normed, out_grad, in_grad):
-    del which
-    tokens = act.shape[2]
-    for lhs, rhs, out in ((act, mixed_grad, out_grad), (hid, normed, in_grad)):
-        total = None
-        for k in range(act.shape[0]):
-            part = jnp.dot(
-                lhs[k], rhs[k * tokens : (k + 1) * tokens, :], preferred_element_type=F32
-            )
-            total = part if total is None else total + part
-        out[...] = total
+def slopes(hidden, act_grad):
+    cover = 0.5 * (1.0 + lax.erf(hidden * root_half))
+    activated = (hidden * cover).astype(BF16)
+    slope = cover + hidden * jnp.exp(-0.5 * hidden * hidden) * inv_root_tau
+    return activated, (act_grad * slope).astype(BF16)
+
+
+def weight_grad_terms(which, weight_in, weight_out, scale, cotangent, normed, aligned):
+    rows = cotangent.shape[1]
+    for k in range(cotangent.shape[0]):
+        upstream = cotangent[which[2 + k]].astype(F32)
+        aligned[k * rows : (k + 1) * rows, :] = (scale[...] * upstream).astype(BF16)
+    mixed_grad = aligned[...]
+    across = (((1,), (1,)), ((), ()))
+    hidden = lax.dot_general(weight_in[...], normed[...], across, preferred_element_type=F32)
+    act_grad = lax.dot_general(weight_out[...], mixed_grad, across, preferred_element_type=F32)
+    activated, hidden_grad = slopes(hidden, act_grad)
+    return (
+        jnp.dot(hidden_grad, normed[...], preferred_element_type=F32),
+        jnp.dot(activated, mixed_grad, preferred_element_type=F32),
+    )
+
+
+def first_terms_kernel(which, weight_in, weight_out, scale, cotangent, normed, out, aligned):
+    terms = weight_grad_terms(which, weight_in, weight_out, scale, cotangent, normed, aligned)
+    for k in range(2):
+        out[0, k] = terms[k]
+
+
+def sent_terms_kernel(
+    which, weight_in, weight_out, scale, cotangent, normed, before, out, aligned
+):
+    terms = weight_grad_terms(which, weight_in, weight_out, scale, cotangent, normed, aligned)
+    for k in range(2):
+        out[k] = before[0, k] + terms[k]
+
+
+def last_terms_kernel(
+    which, weight_in, weight_out, scale, cotangent, normed, before, got, in_grad, out_grad, aligned
+):
+    terms = weight_grad_terms(which, weight_in, weight_out, scale, cotangent, normed, aligned)
+    for k, out in enumerate((in_grad, out_grad)):
+        out[...] = before[0, k] + terms[k] + got[k]
+
+
+def spread_sum_kernel(parts, out):
+    total = tree_sum([parts[k].astype(F32) for k in range(parts.shape[0])]).astype(BF16)
+    for copy in range(out.shape[0]):
+        out[copy] = total
+
+
+def unpack_kernel(parts, out, small):
+    piece = parts.shape[1]
+    for k in range(-(-TAP_ROWS // piece)):
+        first = k * piece
+        length = min(piece, TAP_ROWS - first)
+        out[first : first + length, :] = parts[k].astype(F32)[:length, :]
+    k = TAP_ROWS // piece
+    first = TAP_ROWS - k * piece
+    rows = parts[k].astype(F32)
+    if first + SUB > piece:
+        rows = jnp.concatenate([rows, parts[k + 1].astype(F32)], axis=0)
+    small[...] = rows[first : first + SUB, :]
 
 
 def params(limit=48):
@@ -312,14 +366,11 @@
     return pl.BlockSpec(shape, lambda *_: (0,) * len(shape))
 
 
-def halo(cells, axis, width):
-    count = lax.axis_size(axis)
-    ends = count - 1
-    tail = cells[cells.shape[0] - width :]
-    head = cells[:width]
+def neighbours(cells):
+    ends = lax.axis_size("row") - 1
     return (
-        lax.ppermute(tail, axis, [(i, i + 1) for i in range(ends)]),
-        lax.ppermute(head, axis, [(i + 1, i) for i in range(ends)]),
+        lax.ppermute(cells, "row", [(i, i + 1) for i in range(ends)]),
+        lax.ppermute(cells, "row", [(i + 1, i) for i in range(ends)]),
     )
 
 
@@ -334,26 +385,35 @@
 ):
     planes, height, breadth, channels = voxels.shape
     rows = planes * height * breadth
-    width = MARGIN * height * breadth
     units = weight_in.shape[0]
     count = lax.axis_size("row")
     me = lax.axis_index("row")
     half = count // 2
+    quad = 4
+    line = count // quad
     alike = [[2 * k + p for k in range(half)] for p in range(2)]
-    swap = [(i, i ^ 1) for i in range(count)]
+    lines = [[quad * k + p for k in range(line)] for p in range(quad)]
+    other_core = [(i, i ^ 1) for i in range(count)]
+    other_side = [(i, i ^ 2) for i in range(count)]
     tiles = channels // LANES
+    half_tiles = tiles // 2
 
     own = voxels.reshape(rows, channels)
     upstream = cotangent.reshape(rows, channels)
     gain = norm_gain.reshape(1, channels)
     bias = norm_bias.reshape(1, channels)
     scale = layer_scale.reshape(1, channels)
-
-    left, right = halo(own, "row", width)
-    mixed_grad = (scale * upstream.astype(F32)).astype(BF16)
-    mixed_all = lax.all_gather(
-        mixed_grad, "row", axis=0, tiled=True, axis_index_groups=alike
-    )
+    core = lax.rem(me, 2).astype(jnp.int32)
+    mine = me.astype(jnp.int32)
+    theirs = mine + 1 - 2 * core
+
+    left, right = neighbours(own)
+    upstream_line = [upstream] + [
+        lax.ppermute(upstream, "row", [(i, (i + quad * k) % count) for i in range(count)])
+        for k in range(1, line)
+    ]
+    upstream_near = jnp.concatenate(upstream_line, axis=0).reshape(line, rows, channels)
+    upstream_far = lax.ppermute(upstream_near, "row", other_side)
 
     spread = pltpu.VMEM((9, planes + KS - 1, PAD, LANES), F32)
     split = pltpu.VMEM((9, KS, SUB, LANES), F32)
@@ -362,20 +422,20 @@
         functools.partial(forward_kernel, planes, height),
         grid=(tiles,),
         in_specs=[
-            lane_block(width),
             lane_block(rows),
-            lane_block(width),
+            lane_block(rows),
+            lane_block(rows),
             lane_block(TAP_ROWS),
             whole_block(1, channels),
             whole_block(1, channels),
         ],
         out_specs=[
-            whole_block(rows, channels),
+            whole_block(line, rows, channels),
             whole_block(rows, channels),
             whole_block(rows, LANES),
         ],
         out_shape=[
-            jax.ShapeDtypeStruct((rows, channels), BF16),
+            jax.ShapeDtypeStruct((line, rows, channels), BF16),
             jax.ShapeDtypeStruct((rows, channels), F32),
             jax.ShapeDtypeStruct((rows, LANES), F32),
         ],
@@ -385,114 +445,114 @@
         name="forward_conv",
     )(left, own, right, dw_kernel, gain, bias)
 
-    normed_all = lax.all_gather(normed, "row", axis=0, tiled=True, axis_index_groups=alike)
+    gathered = lax.all_to_all(
+        normed, "row", split_axis=0, concat_axis=0, tiled=True, axis_index_groups=lines
+    )
+    normed_near = gathered.reshape(line * rows, channels)
+    normed_far = lax.ppermute(normed_near, "row", other_side)
 
     block = 512
     whole = whole_block(rows, channels)
-    line = whole_block(1, channels)
-    act, hid, block_out, conv_grad, small = pl.pallas_call(
+    vector = whole_block(1, channels)
+    block_out, conv_grad, small = pl.pallas_call(
         mlp_kernel,
         grid=(units // block,),
         in_specs=[
-            whole,
-            whole,
+            pl.BlockSpec((None, rows, channels), lambda f: (0, 0, 0)),
             pl.BlockSpec((block, channels), lambda f: (f, 0)),
             pl.BlockSpec((block, channels), lambda f: (f, 0)),
             whole,
             whole_block(rows, LANES),
-            line,
-            line,
+            vector,
+            vector,
             whole,
             whole,
         ],
         out_specs=[
-            pl.BlockSpec((block, rows), lambda f: (f, 0)),
-            pl.BlockSpec((block, rows), lambda f: (f, 0)),
             whole,
             whole,
             whole_block(SUB, channels),
         ],
         out_shape=[
-            jax.ShapeDtypeStruct((units, rows), BF16),
-            jax.ShapeDtypeStruct((units, rows), BF16),
             jax.ShapeDtypeStruct((rows, channels), BF16),
             jax.ShapeDtypeStruct((rows, channels), BF16),
             jax.ShapeDtypeStruct((SUB, channels), F32),
         ],
-        scratch_shapes=[pltpu.VMEM((rows, channels), F32), pltpu.VMEM((rows, channels), F32)],
+        scratch_shapes=[
+            pltpu.VMEM((rows, channels), F32),
+            pltpu.VMEM((rows, channels), F32),
+            pltpu.VMEM((rows, channels), BF16),
+        ],
         compiler_params=params(),
         cost_estimate=pl.CostEstimate(
             flops=8 * rows * channels * units,
-            bytes_accessed=4 * units * channels + 4 * units * rows,
+            bytes_accessed=4 * units * channels,
             transcendentals=2 * rows * units,
         ),
         name="mlp_both_ways",
-    )(
-        normed,
-        mixed_grad,
-        weight_in,
-        weight_out,
-        unit,
-        inv,
-        gain,
-        scale,
-        own,
-        upstream,
-    )
-
-    grad_left, grad_right = halo(conv_grad, "row", width)
-
-    piece = -(-(TAP_ROWS + SUB) // count)
-    piece += -piece % SUB if count <= 16 else 0
-    padded = piece * count
-    sums = pl.pallas_call(
-        functools.partial(kernel_grad_kernel, planes, height),
-        grid=(tiles,),
-        in_specs=[
-            lane_block(width),
-            lane_block(rows),
-            lane_block(width),
-            lane_block(rows),
-            lane_block(SUB),
-        ],
-        out_specs=lane_block(padded),
-        out_shape=jax.ShapeDtypeStruct((padded, channels), BF16),
-        scratch_shapes=[
-            spread,
-            pltpu.VMEM((2, KS, SUB * SUB, LANES), F32),
-            pltpu.VMEM((9, KS, SUB, LANES), F32),
-            pltpu.VMEM((padded, LANES), F32),
-        ],
-        compiler_params=params(),
-        cost_estimate=conv_cost(rows, channels),
-        name="kernel_grad_terms",
-    )(left, own, right, conv_grad, small)
-
-    scattered = lax.all_to_all(sums, "row", split_axis=0, concat_axis=0, tiled=True)
-    act_all = lax.all_to_all(
-        act.reshape(half, units // half, rows),
+    )(normed, weight_in, weight_out, unit, inv, gain, scale, own, upstream)
+
+    grad_left, grad_right = neighbours(conv_grad)
+
+    piece = -(-(TAP_ROWS + SUB) // half)
+    piece += -piece % (2 * SUB)
+    padded = piece * half
+
+    def kernel_grad_half(which, name):
+        def at(block_rows):
+            return pl.BlockSpec((block_rows, LANES), lambda c, w: (0, w[0] * half_tiles + c))
+
+        return pl.pallas_call(
+            functools.partial(kernel_grad_kernel, planes, height),
+            grid_spec=pltpu.PrefetchScalarGridSpec(
+                num_scalar_prefetch=1,
+                grid=(half_tiles,),
+                in_specs=[at(rows), at(rows), at(rows), at(rows), at(SUB)],
+                out_specs=pl.BlockSpec((padded, LANES), lambda c, w: (0, c)),
+                scratch_shapes=[
+                    spread,
+                    pltpu.VMEM((2, KS, SUB * SUB, LANES), F32),
+                    pltpu.VMEM((9, KS, SUB, LANES), F32),
+                    pltpu.VMEM((padded, LANES), F32),
+                ],
+            ),
+            out_shape=jax.ShapeDtypeStruct((padded, half_tiles * LANES), BF16),
+            compiler_params=params(),
+            cost_estimate=conv_cost(rows, channels // 2),
+            name=name,
+        )(which.reshape(1), left, own, right, conv_grad, small)
+
+    for_other = kernel_grad_half(1 - core, "kernel_grad_sent")
+    from_other = lax.ppermute(for_other, "row", other_core)
+    for_self = kernel_grad_half(core, "kernel_grad_kept")
+    chip_sum = (for_self.astype(F32) + from_other.astype(F32)).astype(BF16)
+    wide = half_tiles * LANES
+    scattered = lax.all_to_all(
+        chip_sum.reshape(half, piece, wide),
         "row",
         split_axis=0,
         concat_axis=0,
         tiled=True,
         axis_index_groups=alike,
     )
-    hid_all = lax.all_to_all(
-        hid.reshape(half, units // half, rows),
-        "row",
-        split_axis=0,
-        concat_axis=0,
-        tiled=True,
-        axis_index_groups=alike,
-    )
+    copies = pl.pallas_call(
+        spread_sum_kernel,
+        in_specs=[whole_block(half, piece, wide)],
+        out_specs=whole_block(count, piece, wide),
+        out_shape=jax.ShapeDtypeStruct((count, piece, wide), BF16),
+        grid=(1,),
+        compiler_params=params(),
+        name="kernel_grad_sum",
+    )(scattered)
+    totals = lax.all_to_all(copies, "row", split_axis=0, concat_axis=0, tiled=True)
 
     voxel_grad = pl.pallas_call(
         functools.partial(input_grad_kernel, planes, height),
         grid=(tiles,),
         in_specs=[
-            lane_block(width),
             lane_block(rows),
-            lane_block(width),
+            lane_block(rows),
+            lane_block(rows),
             lane_block(TAP_ROWS),
             lane_block(rows),
         ],
@@ -504,58 +564,100 @@
         name="input_grad_conv",
     )(grad_left, conv_grad, grad_right, dw_kernel, upstream)
 
-    summed = jnp.sum(scattered.reshape(count, piece, channels).astype(F32), axis=0)
-    gathered = lax.all_gather(summed.astype(BF16), "row", axis=0, tiled=True)
-    totals = gathered.astype(F32)
-    kernel_grad = totals[:TAP_ROWS]
-    gain_grad = totals[TAP_ROWS]
-    bias_grad = totals[TAP_ROWS + 1]
-    scale_grad = totals[TAP_ROWS + 2]
-
-    mine = units // count
-    tokens = half * rows
-
-    def weight_grads(which, name):
-        return pl.pallas_call(
-            weight_grad_kernel,
-            grid_spec=pltpu.PrefetchScalarGridSpec(
-                num_scalar_prefetch=1,
-                grid=(1,),
-                in_specs=[
-                    pl.BlockSpec((half, mine, rows), lambda _, w: (0, w[0], 0)),
-                    pl.BlockSpec((half, mine, rows), lambda _, w: (0, w[0], 0)),
-                    whole_block(tokens, channels),
-                    whole_block(tokens, channels),
-                ],
-                out_specs=[whole_block(mine, channels), whole_block(mine, channels)],
-            ),
-            out_shape=[
-                jax.ShapeDtypeStruct((mine, channels), F32),
-                jax.ShapeDtypeStruct((mine, channels), F32),
+    kernel_grad, vectors = pl.pallas_call(
+        unpack_kernel,
+        grid=(2,),
+        in_specs=[pl.BlockSpec((half, None, piece, wide), lambda p: (0, p, 0, 0))],
+        out_specs=[
+            pl.BlockSpec((TAP_ROWS, wide), lambda p: (0, p)),
+            pl.BlockSpec((SUB, wide), lambda p: (0, p)),
+        ],
+        out_shape=[
+            jax.ShapeDtypeStruct((TAP_ROWS, channels), F32),
+            jax.ShapeDtypeStruct((SUB, channels), F32),
+        ],
+        compiler_params=params(),
+        name="kernel_grad_unpack",
+    )(totals.reshape(half, 2, piece, wide))
+
+    share = units // count
+    tokens = line * rows
+    terms_cost = pl.CostEstimate(
+        flops=8 * tokens * channels * share,
+        bytes_accessed=4 * tokens * channels + 4 * share * channels,
+        transcendentals=2 * tokens * share,
+    )
+    both = jax.ShapeDtypeStruct((2, share, channels), F32)
+    sets = [
+        whole_block(1, channels),
+        whole_block(line, rows, channels),
+        whole_block(tokens, channels),
+    ]
+    aligned = [pltpu.VMEM((tokens, channels), BF16)]
+    place = lax.rem(me // quad + line - jnp.arange(line, dtype=jnp.int32), line)
+    which = jnp.concatenate([theirs.reshape(1), mine.reshape(1), place.astype(jnp.int32)])
+
+    def chunk(at):
+        return pl.BlockSpec((share, channels), lambda s, w: (w[s + at], 0))
+
+    first = pl.pallas_call(
+        first_terms_kernel,
+        grid_spec=pltpu.PrefetchScalarGridSpec(
+            num_scalar_prefetch=1,
+            grid=(2,),
+            in_specs=[chunk(0), chunk(0)] + sets,
+            out_specs=pl.BlockSpec((1, 2, share, channels), lambda s, w: (s, 0, 0, 0)),
+            scratch_shapes=aligned,
+        ),
+        out_shape=jax.ShapeDtypeStruct((2, 2, share, channels), F32),
+        compiler_params=params(),
+        cost_estimate=terms_cost,
+        name="weight_grads_near",
+    )(which, weight_in, weight_out, scale, upstream_near, normed_near)
+    sent = pl.pallas_call(
+        sent_terms_kernel,
+        grid_spec=pltpu.PrefetchScalarGridSpec(
+            num_scalar_prefetch=1,
+            grid=(1,),
+            in_specs=[chunk(0), chunk(0)]
+            + sets
+            + [pl.BlockSpec((1, 2, share, channels), lambda s, w: (0, 0, 0, 0))],
+            out_specs=whole_block(2, share, channels),
+            scratch_shapes=aligned,
+        ),
+        out_shape=both,
+        compiler_params=params(),
+        cost_estimate=terms_cost,
+        name="weight_grads_sent",
+    )(which, weight_in, weight_out, scale, upstream_far, normed_far, first)
+    got = lax.ppermute(sent, "row", other_core)
+    weight_in_grad, weight_out_grad = pl.pallas_call(
+        last_terms_kernel,
+        grid_spec=pltpu.PrefetchScalarGridSpec(
+            num_scalar_prefetch=1,
+            grid=(1,),
+            in_specs=[chunk(1), chunk(1)]
+            + sets
+            + [
+                pl.BlockSpec((1, 2, share, channels), lambda s, w: (1, 0, 0, 0)),
+                whole_block(2, share, channels),
             ],
-            compiler_params=params(),
-            cost_estimate=pl.CostEstimate(
-                flops=4 * tokens * channels * mine,
-                bytes_accessed=4 * tokens * channels + 4 * mine * tokens,
-                transcendentals=0,
-            ),
-            name=name,
-        )(which.reshape(1), act_all, hid_all, mixed_all, normed_all)
-
-    core = lax.rem(me, 2).astype(jnp.int32)
-    sent = weight_grads(1 - core, "weight_grads_sent")
-    got = [lax.ppermute(part, "row", swap) for part in sent]
-    kept = weight_grads(core, "weight_grads_kept")
-    weight_out_grad = kept[0] + got[0]
-    weight_in_grad = kept[1] + got[1]
+            out_specs=[whole_block(share, channels), whole_block(share, channels)],
+            scratch_shapes=aligned,
+        ),
+        out_shape=[jax.ShapeDtypeStruct((share, channels), F32)] * 2,
+        compiler_params=params(),
+        cost_estimate=terms_cost,
+        name="weight_grads_kept",
+    )(which, weight_in, weight_out, scale, upstream_far, normed_far, first, got)
 
     return (
         block_out.reshape(voxels.shape),
         voxel_grad.reshape(voxels.shape),
         kernel_grad,
-        gain_grad,
-        bias_grad,
-        scale_grad,
+        vectors[0],
+        vectors[1],
+        vectors[2],
         weight_in_grad,
         weight_out_grad,
     )

time: 179 us -> 135 us (0.75)
  blocking collectives: 22.1 us -> 0 us
  waiting for transfers between devices: 68.3 us -> 53.2 us
  between operations: 14.2 us -> 0.79 us
  Pallas kernels: 26.5 us -> 38.6 us
  local copies, waits for them, and re-layouts: 12.9 us -> 4.19 us
  starting transfers between devices: 26.7 us -> 35.3 us
  other arithmetic: 6.87 us -> 1.83 us
    all_gather x1 -> x0, blocking collectives: 22.1 us -> none  [on_device(): gathered = lax.all_gather(summed.astype(BF16), 'row', axis=0, tiled=True)]
    ppermute x6 -> x11, waiting for transfers between devices: 2.47 us -> 23.7 us  [the longest x3 17 us: on_device(): lax.ppermute(upstream, 'row', [(i, (i + quad * k) % count) for i in range...]
    all_to_all x3, waiting for transfers between devices: 48 us -> 29.5 us  [the longest x1 29.5 us: on_device(): lax.all_to_all(chip_sum.reshape(half, piece, wide), 'row', split_axis=0,...]
    all_gather x2 -> x0, waiting for transfers between devices: 17.1 us -> none  [the longest x1 17.1 us: on_device(): lax.all_gather(normed, 'row', axis=0, tiled=True, axis_index_groups=alike)]
    pallas_call x4 -> x8, Pallas kernels: 18.1 us -> 29.8 us  [the longest x1 9.25 us: on_device(): pl.pallas_call(mlp_kernel, grid=(units // block,), in_specs=[pl.BlockSpec...]
    ppermute x6 -> x11, starting transfers between devices: 12.4 us -> 21.4 us  [the longest x2 7.91 us: neighbours(): lax.ppermute(cells, 'row', [(i, i + 1) for i in range(ends)])]
    unnamed x26 -> x12, local copies, waits for them, and re-layouts: 7.45 us -> 2.17 us
    add x2 -> x0, other arithmetic: 3.9 us -> none  [the longest x1 1.96 us: on_device(): weight_in_grad = kept[1] + got[1]]
  transfers between devices with their start and end apart: 11 -> 14, of which waited for: 4 -> 6; matrix products, arithmetic and copies ran while one was open for 5% -> 3% of each run, Pallas kernels for 15% -> 22%
where the time goes in v2:
time: 135 us; the launch traced here: 134 us
  waiting for transfers between devices  53.2 us (39%)
  Pallas kernels  38.6 us (29%)
  starting transfers between devices  35.3 us (26%)
  local copies, waits for them, and re-layouts  4.19 us (3%)
  other arithmetic  1.83 us (1%)
    all_to_all x1, waiting for transfers between devices, on_device(): lax.all_to_all(chip_sum.reshape(half, piece, wide), 'row', split_axis=0,...  29.5 us
    ppermute x3, waiting for transfers between devices, on_device(): lax.ppermute(upstream, 'row', [(i, (i + quad * k) % count) for i in range...  17 us
    pallas_call x1, Pallas kernels, on_device(): pl.pallas_call(mlp_kernel, grid=(units // block,), in_specs=[pl.BlockSpec...  9.25 us
    ppermute x2, starting transfers between devices, neighbours(): lax.ppermute(cells, 'row', [(i, i + 1) for i in range(ends)])  7.91 us
    all_to_all x1, starting transfers between devices, on_device(): lax.all_to_all(copies, 'row', split_axis=0, concat_axis=0, tiled=True)  6.27 us
    pallas_call x2, Pallas kernels, kernel_grad_half(): pl.pallas_call(functools.partial(kernel_grad_kernel, planes, height), gri...  5.14 us
    pallas_call x1, Pallas kernels, on_device(): pl.pallas_call(functools.partial(forward_kernel, planes, height), grid=(t...  4.59 us
    pallas_call x1, Pallas kernels, on_device(): pl.pallas_call(first_terms_kernel, grid_spec=pltpu.PrefetchScalarGridSpec...  4.39 us
  transfers between devices with their start and end apart: 14, of which 6 were waited for; matrix products, arithmetic and copies ran while one was open for 3% of the time, Pallas kernels for 22%

profile of v2, /device:TPU:1, one launch (start us, length us, event | category | flops | bytes accessed | tf_op | source)
XLA Modules:
  0.0 133.8 jit_solution(3939149033012546286)
XLA Ops:
  0.6 2.0 %collective-permute-start.1 = (bf16[128,768]{1,0:T(8,128)(2,1)}, bf16[128,768]{1,0:T(8,128)(2,1)S(1)}, u32[]{:S(2)}, u32[]{:S(2)}) collective-permute-start(bf16[128,768]{1,0:T(8,128)(2,1)} %bitcast.12), channel_id=1, source_target_pairs={{1,0},{2,1},{3,2},{4,3},{5,4},{6,5},{7,6},{8,7},{9,8},{10,9},{11,1... | collective-permute-start | bytes 589832 | tf_op jit(solution)/shard_map/ppermute | solution.py:373
  2.6 4.5 %collective-permute-start = (bf16[128,768]{1,0:T(8,128)(2,1)}, bf16[128,768]{1,0:T(8,128)(2,1)S(1)}, u32[]{:S(2)}, u32[]{:S(2)}) collective-permute-start(bf16[128,768]{1,0:T(8,128)(2,1)} %bitcast.13), channel_id=1, source_target_pairs={{0,1},{1,2},{2,3},{3,4},{4,5},{5,6},{6,7},{7,8},{8,9},{9,10},{10,1... | collective-permute-start | bytes 589832 | tf_op jit(solution)/shard_map/ppermute | solution.py:372
  7.1 0.7 reshape.62.gain
  7.8 0.7 reshape.63.bias
  8.5 0.2 collective-permute-done.1.right
  8.7 2.4 %collective-permute-done.left = bf16[128,768]{1,0:T(8,128)(2,1)S(1)} collective-permute-done((bf16[128,768]{1,0:T(8,128)(2,1)}, bf16[128,768]{1,0:T(8,128)(2,1)S(1)}, u32[]{:S(2)}, u32[]{:S(2)}) %collective-permute-start) | collective-permute-done | bytes 196640 | tf_op jit(solution)/shard_map/ppermute | solution.py:372
  11.1 1.2 copy-done
  12.3 0.9 copy-done.2
  13.3 4.6 %forward_conv.1 = (bf16[4,128,768]{2,1,0:T(8,128)(2,1)}, f32[128,768]{1,0:T(8,128)S(1)}, f32[128,128]{1,0:T(8,128)S(1)}) custom-call(bf16[128,768]{1,0:T(8,128)(2,1)S(1)} %collective-permute-done.left, bf16[128,768]{1,0:T(8,128)(2,1)S(1)} %bitcast.14, bf16[128,768]{1,0:T(8,128)(2,1)S(1)} %collective-permute-done.1.right, f32[343,768]{1,0:T(8,128)S(1)} %copy-done, ...), custom_call_target="tpu_custom_call" | custom-call | flops 67436544 | bytes 1572864 | tf_op jit(solution)/shard_map/forward_conv/pallas_call | solution.py:421
  17.9 4.2 %all-to-all-start.2 = ((bf16[4,128,768]{2,1,0:T(8,128)(2,1)}), bf16[4,128,768]{2,1,0:T(8,128)(2,1)}, u32[]{:S(2)}, u32[]{:S(2)}) async-start(bf16[4,128,768]{2,1,0:T(8,128)(2,1)} %get-tuple-element.18.normed), calls=%async_computation.2 | async-start | bytes 1572864 | tf_op jit(solution)/shard_map/all_to_all | solution.py:448
  22.1 0.0 copy-done.4
  22.1 3.2 %collective-permute-start.7 = (bf16[128,768]{1,0:T(8,128)(2,1)S(1)}, bf16[128,768]{1,0:T(8,128)(2,1)S(1)}, u32[]{:S(2)}, u32[]{:S(2)}) collective-permute-start(bf16[128,768]{1,0:T(8,128)(2,1)S(1)} %bitcast.18), channel_id=1, source_target_pairs={{0,12},{1,13},{2,14},{3,15},{4,0},{5,1},{6,2},{7,3},{8,4},{9,5},{1... | collective-permute-start | bytes 589832 | tf_op jit(solution)/shard_map/ppermute | solution.py:412
  25.3 0.0 collective-permute-start.6
  25.3 0.6 collective-permute-start.5
  25.9 9.2 %mlp_both_ways.1 = (bf16[128,768]{1,0:T(8,128)(2,1)}, bf16[128,768]{1,0:T(8,128)(2,1)S(1)}, f32[8,768]{1,0:T(8,128)S(1)}) custom-call(bf16[4,128,768]{2,1,0:T(8,128)(2,1)} %get-tuple-element.18.normed, bf16[3072,768]{1,0:T(8,128)(2,1)} %weight_in.7, bf16[3072,768]{1,0:T(8,128)(2,1)} %weight_out.7, f32[128,768]{1,0:T(8,128)S(1)} %get-tuple-element.19.unit, ...), custom_call_target="tpu_custom_call" | custom-call | flops 2415919104 | bytes 9437184 | tf_op jit(solution)/shard_map/mlp_both_ways/pallas_call | solution.py:457
  35.1 2.6 %kernel_grad_sent.1 = bf16[384,384]{1,0:T(8,128)(2,1)S(1)} custom-call(s32[1]{0:T(128)} %bitcast.5.which, bf16[128,768]{1,0:T(8,128)(2,1)S(1)} %collective-permute-done.left, bf16[128,768]{1,0:T(8,128)(2,1)S(1)} %bitcast.16, bf16[128,768]{1,0:T(8,128)(2,1)S(1)} %collective-permute-done.1.right, bf16[128,768]{1,0:T(8,128)(2,1)S(1)} %get-tuple-element.22.own.grads, ...), custom_call_target="tpu_custom_call" | custom-call | flops 33718272 | bytes 786432 | tf_op jit(solution)/shard_map/kernel_grad_sent/pallas_call | solution.py:505
  37.7 3.8 %collective-permute-start.4 = (bf16[384,384]{1,0:T(8,128)(2,1)S(1)}, bf16[384,384]{1,0:T(8,128)(2,1)S(1)}, u32[]{:S(2)}, u32[]{:S(2)}) collective-permute-start(bf16[384,384]{1,0:T(8,128)(2,1)S(1)} %kernel_grad_sent.1), channel_id=1, source_target_pairs={{0,1},{1,0},{2,3},{3,2},{4,5},{5,4},{6,7},{7,6},{8,9},{9,8},{10,11... | collective-permute-start | bytes 884744 | tf_op jit(solution)/shard_map/ppermute | solution.py:526
  41.5 0.0 collective-permute-done.7
  41.5 17.0 %collective-permute-done.6 = bf16[128,768]{1,0:T(8,128)(2,1)S(1)} collective-permute-done((bf16[128,768]{1,0:T(8,128)(2,1)S(1)}, bf16[128,768]{1,0:T(8,128)(2,1)S(1)}, u32[]{:S(2)}, u32[]{:S(2)}) %collective-permute-start.6) | collective-permute-done | bytes 196640 | tf_op jit(solution)/shard_map/ppermute | solution.py:412
  58.5 0.0 collective-permute-done.5
  58.5 1.0 pad_maximum_fusion
  59.4 1.0 collective-permute-start.8
  60.4 2.6 %kernel_grad_kept.1 = bf16[384,384]{1,0:T(8,128)(2,1)S(1)} custom-call(s32[1]{0:T(128)} %bitcast.4.which, bf16[128,768]{1,0:T(8,128)(2,1)S(1)} %collective-permute-done.left, bf16[128,768]{1,0:T(8,128)(2,1)S(1)} %bitcast.17, bf16[128,768]{1,0:T(8,128)(2,1)S(1)} %collective-permute-done.1.right, bf16[128,768]{1,0:T(8,128)(2,1)S(1)} %get-tuple-element.22.own.grads, ...), custom_call_target="tpu_custom_call" | custom-call | flops 33718272 | bytes 786432 | tf_op jit(solution)/shard_map/kernel_grad_kept/pallas_call | solution.py:505
  63.0 0.0 all-to-all-done.2
  63.0 0.5 collective-permute-start.9
  63.5 0.0 collective-permute-done.4
  63.5 0.8 add_convert_fusion
  64.3 3.4 %all-to-all-start = ((bf16[8,48,384]{2,1,0:T(8,128)(2,1)}), bf16[8,48,384]{2,1,0:T(8,128)(2,1)S(1)}, u32[]{:S(2)}, u32[]{:S(2)}) async-start(bf16[8,48,384]{2,1,0:T(8,128)(2,1)} %bitcast.6), calls=%async_computation | async-start | bytes 589824 | tf_op jit(solution)/shard_map/all_to_all | solution.py:530
  67.8 0.1 pad_add_fusion.which
  67.9 29.5 %all-to-all-done.parts = bf16[8,48,384]{2,1,0:T(8,128)(2,1)S(1)} async-done(((bf16[8,48,384]{2,1,0:T(8,128)(2,1)}), bf16[8,48,384]{2,1,0:T(8,128)(2,1)S(1)}, u32[]{:S(2)}, u32[]{:S(2)}) %all-to-all-start) | async-done | bytes 294944 | tf_op jit(solution)/shard_map/all_to_all | solution.py:530
  97.3 0.9 kernel_grad_sum.1
  98.2 6.3 %all-to-all-start.1 = ((bf16[16,48,384]{2,1,0:T(8,128)(2,1)}), bf16[16,48,384]{2,1,0:T(8,128)(2,1)}, u32[]{:S(2)}, u32[]{:S(2)}) async-start(bf16[16,48,384]{2,1,0:T(8,128)(2,1)} %kernel_grad_sum.1), calls=%async_computation.1 | async-start | bytes 1179648 | tf_op jit(solution)/shard_map/all_to_all | solution.py:547
  104.5 4.4 %weight_grads_near.1.before = f32[2,2,192,768]{3,2,1,0:T(8,128)S(1)} custom-call(s32[6]{0:T(128)S(1)} %pad_add_fusion.which, bf16[3072,768]{1,0:T(8,128)(2,1)} %weight_in.7, bf16[3072,768]{1,0:T(8,128)(2,1)} %weight_out.7, f32[1,768]{1,0:T(1,128)S(1)} %reshape.64.scale, bf16[4,128,768]{2,1,0:T(8,128)(2,1)} %bitcast.10.cotangent, bf16[512,768]{1,0:T(8,128)(2,1)} %bitcast.11.normed), custom_call_target="tpu_custom_call" | custom-call | flops 603979776 | bytes 2162688 | tf_op jit(solution)/shard_map/weight_grads_near/pallas_call | solution.py:603
  108.9 0.0 copy-start.1
  108.9 0.0 collective-permute-done.8.cotangent
  108.9 0.0 collective-permute-done.9.normed
  108.9 4.0 %weight_grads_sent.1 = f32[2,192,768]{2,1,0:T(8,128)} custom-call(s32[6]{0:T(128)S(1)} %pad_add_fusion.which, bf16[3072,768]{1,0:T(8,128)(2,1)} %weight_in.7, bf16[3072,768]{1,0:T(8,128)(2,1)} %weight_out.7, f32[1,768]{1,0:T(1,128)S(1)} %reshape.64.scale, bf16[4,128,768]{2,1,0:T(8,128)(2,1)S(1)} %collective-permute-done.8.cotangent, ...), custom_call_target="tpu_custom_call" | custom-call | flops 603979776 | bytes 2162688 | tf_op jit(solution)/shard_map/weight_grads_sent/pallas_call | solution.py:617
  112.9 0.3 collective-permute-start.10
  113.1 2.1 %collective-permute-start.3 = (bf16[128,768]{1,0:T(8,128)(2,1)S(1)}, bf16[128,768]{1,0:T(8,128)(2,1)S(1)}, u32[]{:S(2)}, u32[]{:S(2)}) collective-permute-start(bf16[128,768]{1,0:T(8,128)(2,1)S(1)} %get-tuple-element.22.own.grads), channel_id=1, source_target_pairs={{1,0},{2,1},{3,2},{4,3},{5,4},{6,5},{7,6},{8,7},{9,8},{10,9},{11,1... | collective-permute-start | bytes 589832 | tf_op jit(solution)/shard_map/ppermute | solution.py:373
  115.3 3.4 %collective-permute-start.2 = (bf16[128,768]{1,0:T(8,128)(2,1)S(1)}, bf16[128,768]{1,0:T(8,128)(2,1)S(1)}, u32[]{:S(2)}, u32[]{:S(2)}) collective-permute-start(bf16[128,768]{1,0:T(8,128)(2,1)S(1)} %get-tuple-element.22.own.grads), channel_id=1, source_target_pairs={{0,1},{1,2},{2,3},{3,4},{4,5},{5,6},{6,7},{7,8},{8,9},{9,10},{10,1... | collective-permute-start | bytes 589832 | tf_op jit(solution)/shard_map/ppermute | solution.py:372
  118.7 2.6 %collective-permute-done.3.right = bf16[128,768]{1,0:T(8,128)(2,1)S(1)} collective-permute-done((bf16[128,768]{1,0:T(8,128)(2,1)S(1)}, bf16[128,768]{1,0:T(8,128)(2,1)S(1)}, u32[]{:S(2)}, u32[]{:S(2)}) %collective-permute-start.3) | collective-permute-done | bytes 196640 | tf_op jit(solution)/shard_map/ppermute | solution.py:373
  121.3 1.6 %collective-permute-done.2.left = bf16[128,768]{1,0:T(8,128)(2,1)S(1)} collective-permute-done((bf16[128,768]{1,0:T(8,128)(2,1)S(1)}, bf16[128,768]{1,0:T(8,128)(2,1)S(1)}, u32[]{:S(2)}, u32[]{:S(2)}) %collective-permute-start.2) | collective-permute-done | bytes 196640 | tf_op jit(solution)/shard_map/ppermute | solution.py:372
  122.9 4.2 %input_grad_conv.1 = bf16[128,768]{1,0:T(8,128)(2,1)} custom-call(bf16[128,768]{1,0:T(8,128)(2,1)S(1)} %collective-permute-done.2.left, bf16[128,768]{1,0:T(8,128)(2,1)S(1)} %get-tuple-element.22.own.grads, bf16[128,768]{1,0:T(8,128)(2,1)S(1)} %collective-permute-done.3.right, f32[343,768]{1,0:T(8,128)S(1)} %copy-done.1, bf16[128,768]{1,0:T(8,128)(2,1)S(1)} %bitcast.23), custom_call_target="tpu_custom_call" | custom-call | flops 67436544 | bytes 1572864 | tf_op jit(solution)/shard_map/input_grad_conv/pallas_call | solution.py:549
  127.0 0.0 all-to-all-done.1
  127.0 2.0 %kernel_grad_unpack.1 = (f32[343,768]{1,0:T(8,128)}, f32[8,768]{1,0:T(8,128)S(1)}) custom-call(bf16[8,2,48,384]{3,2,1,0:T(8,128)(2,1)} %bitcast.7.parts), custom_call_target="tpu_custom_call" | custom-call | tf_op jit(solution)/shard_map/kernel_grad_unpack/pallas_call | solution.py:567
  129.0 0.6 slice_reduce_fusion
  129.6 0.0 collective-permute-done.10.got
  129.6 4.2 %weight_grads_kept.1 = (f32[192,768]{1,0:T(8,128)}, f32[192,768]{1,0:T(8,128)}) custom-call(s32[6]{0:T(128)S(1)} %pad_add_fusion.which, bf16[3072,768]{1,0:T(8,128)(2,1)} %weight_in.7, bf16[3072,768]{1,0:T(8,128)(2,1)} %weight_out.7, f32[1,768]{1,0:T(1,128)S(1)} %reshape.64.scale, bf16[4,128,768]{2,1,0:T(8,128)(2,1)S(1)} %collective-permute-done.8.cotangent, ...), custom_call_target="tpu_custom_call" | custom-call | flops 603979776 | bytes 2162688 | tf_op jit(solution)/shard_map/weight_grads_kept/pallas_call | solution.py:634
  (10 shorter events, 0.0 us)
Async XLA Ops:
  0.6 8.1 %collective-permute-start.1 = (bf16[128,768]{1,0:T(8,128)(2,1)}, bf16[128,768]{1,0:T(8,128)(2,1)S(1)}, u32[]{:S(2)}, u32[]{:S(2)}) collective-permute-start(bf16[128,768]{1,0:T(8,128)(2,1)} %bitcast.12), channel_id=1, source_target_pairs={{1,0},{2,1},{3,2},{4,3},{5,4},{6,5},{7,6},{8,7},{9,8},{10,9},{11,1... | collective-permute-start | bytes 589832 | tf_op jit(solution)/shard_map/ppermute | solution.py:373
  2.6 8.5 %collective-permute-start = (bf16[128,768]{1,0:T(8,128)(2,1)}, bf16[128,768]{1,0:T(8,128)(2,1)S(1)}, u32[]{:S(2)}, u32[]{:S(2)}) collective-permute-start(bf16[128,768]{1,0:T(8,128)(2,1)} %bitcast.13), channel_id=1, source_target_pairs={{0,1},{1,2},{2,3},{3,4},{4,5},{5,6},{6,7},{7,8},{8,9},{9,10},{10,1... | collective-permute-start | bytes 589832 | tf_op jit(solution)/shard_map/ppermute | solution.py:372
  7.8 18.1 %copy-start.5 = (f32[768]{0:T(1024)S(1)}, f32[768]{0:T(1024)}, u32[]{:S(2)}) copy-start(f32[768]{0:T(1024)} %param.14) | copy-start | bytes 9220
  11.1 1.2 copy-start
  12.3 0.9 copy-start.2
  13.3 8.8 %copy-start.4 = (bf16[4,4,8,768]{3,2,1,0:T(8,128)(2,1)S(1)}, bf16[4,4,8,768]{3,2,1,0:T(8,128)(2,1)}, u32[]{:S(2)}) copy-start(bf16[4,4,8,768]{3,2,1,0:T(8,128)(2,1)} %param.15) | copy-start | bytes 589828
  13.3 12.6 %copy-start.3 = (bf16[4,4,8,768]{3,2,1,0:T(8,128)(2,1)S(1)}, bf16[4,4,8,768]{3,2,1,0:T(8,128)(2,1)}, u32[]{:S(2)}) copy-start(bf16[4,4,8,768]{3,2,1,0:T(8,128)(2,1)} %param.8) | copy-start | bytes 589828
  17.9 45.1 %all-to-all-start.2 = ((bf16[4,128,768]{2,1,0:T(8,128)(2,1)}), bf16[4,128,768]{2,1,0:T(8,128)(2,1)}, u32[]{:S(2)}, u32[]{:S(2)}) async-start(bf16[4,128,768]{2,1,0:T(8,128)(2,1)} %get-tuple-element.18.normed), calls=%async_computation.2 | async-start | bytes 1572864 | tf_op jit(solution)/shard_map/all_to_all | solution.py:448
  22.1 19.4 %collective-permute-start.7 = (bf16[128,768]{1,0:T(8,128)(2,1)S(1)}, bf16[128,768]{1,0:T(8,128)(2,1)S(1)}, u32[]{:S(2)}, u32[]{:S(2)}) collective-permute-start(bf16[128,768]{1,0:T(8,128)(2,1)S(1)} %bitcast.18), channel_id=1, source_target_pairs={{0,12},{1,13},{2,14},{3,15},{4,0},{5,1},{6,2},{7,3},{8,4},{9,5},{1... | collective-permute-start | bytes 589832 | tf_op jit(solution)/shard_map/ppermute | solution.py:412
  25.3 33.2 %collective-permute-start.6 = (bf16[128,768]{1,0:T(8,128)(2,1)S(1)}, bf16[128,768]{1,0:T(8,128)(2,1)S(1)}, u32[]{:S(2)}, u32[]{:S(2)}) collective-permute-start(bf16[128,768]{1,0:T(8,128)(2,1)S(1)} %bitcast.19), channel_id=1, source_target_pairs={{0,8},{1,9},{2,10},{3,11},{4,12},{5,13},{6,14},{7,15},{8,0},{9,1},... | collective-permute-start | bytes 589832 | tf_op jit(solution)/shard_map/ppermute | solution.py:412
  25.3 33.2 %collective-permute-start.5 = (bf16[128,768]{1,0:T(8,128)(2,1)S(1)}, bf16[128,768]{1,0:T(8,128)(2,1)S(1)}, u32[]{:S(2)}, u32[]{:S(2)}) collective-permute-start(bf16[128,768]{1,0:T(8,128)(2,1)S(1)} %bitcast.20), channel_id=1, source_target_pairs={{0,4},{1,5},{2,6},{3,7},{4,8},{5,9},{6,10},{7,11},{8,12},{9,13},{1... | collective-permute-start | bytes 589832 | tf_op jit(solution)/shard_map/ppermute | solution.py:412
  37.7 25.8 %collective-permute-start.4 = (bf16[384,384]{1,0:T(8,128)(2,1)S(1)}, bf16[384,384]{1,0:T(8,128)(2,1)S(1)}, u32[]{:S(2)}, u32[]{:S(2)}) collective-permute-start(bf16[384,384]{1,0:T(8,128)(2,1)S(1)} %kernel_grad_sent.1), channel_id=1, source_target_pairs={{0,1},{1,0},{2,3},{3,2},{4,5},{5,4},{6,7},{7,6},{8,9},{9,8},{10,11... | collective-permute-start | bytes 884744 | tf_op jit(solution)/shard_map/ppermute | solution.py:526
  59.4 49.5 %collective-permute-start.8 = (bf16[4,128,768]{2,1,0:T(8,128)(2,1)}, bf16[4,128,768]{2,1,0:T(8,128)(2,1)S(1)}, u32[]{:S(2)}, u32[]{:S(2)}) collective-permute-start(bf16[4,128,768]{2,1,0:T(8,128)(2,1)} %bitcast.10.cotangent), channel_id=1, source_target_pairs={{0,2},{1,3},{2,0},{3,1},{4,6},{5,7},{6,4},{7,5},{8,10},{9,11},{10,... | collective-permute-start | bytes 2359304 | tf_op jit(solution)/shard_map/ppermute | solution.py:416
  63.0 45.9 %collective-permute-start.9 = (bf16[512,768]{1,0:T(8,128)(2,1)}, bf16[512,768]{1,0:T(8,128)(2,1)}, u32[]{:S(2)}, u32[]{:S(2)}) collective-permute-start(bf16[512,768]{1,0:T(8,128)(2,1)} %bitcast.11.normed), channel_id=1, source_target_pairs={{0,2},{1,3},{2,0},{3,1},{4,6},{5,7},{6,4},{7,5},{8,10},{9,11},{10,... | collective-permute-start | bytes 2359304 | tf_op jit(solution)/shard_map/ppermute | solution.py:452
  64.3 33.0 %all-to-all-start = ((bf16[8,48,384]{2,1,0:T(8,128)(2,1)}), bf16[8,48,384]{2,1,0:T(8,128)(2,1)S(1)}, u32[]{:S(2)}, u32[]{:S(2)}) async-start(bf16[8,48,384]{2,1,0:T(8,128)(2,1)} %bitcast.6), calls=%async_computation | async-start | bytes 589824 | tf_op jit(solution)/shard_map/all_to_all | solution.py:530
  98.2 28.8 %all-to-all-start.1 = ((bf16[16,48,384]{2,1,0:T(8,128)(2,1)}), bf16[16,48,384]{2,1,0:T(8,128)(2,1)}, u32[]{:S(2)}, u32[]{:S(2)}) async-start(bf16[16,48,384]{2,1,0:T(8,128)(2,1)} %kernel_grad_sum.1), calls=%async_computation.1 | async-start | bytes 1179648 | tf_op jit(solution)/shard_map/all_to_all | solution.py:547
  108.9 14.0 %copy-start.1 = (f32[343,768]{1,0:T(8,128)S(1)}, f32[343,768]{1,0:T(8,128)}, u32[]{:S(2)}) copy-start(f32[343,768]{1,0:T(8,128)} %taps.3) | copy-start | bytes 3161092
  112.9 16.7 %collective-permute-start.10 = (f32[2,192,768]{2,1,0:T(8,128)}, f32[2,192,768]{2,1,0:T(8,128)}, u32[]{:S(2)}, u32[]{:S(2)}) collective-permute-start(f32[2,192,768]{2,1,0:T(8,128)} %weight_grads_sent.1), channel_id=1, source_target_pairs={{0,1},{1,0},{2,3},{3,2},{4,5},{5,4},{6,7},{7,6},{8,9},{9,8},{10,11... | collective-permute-start | bytes 3538952 | tf_op jit(solution)/shard_map/ppermute | solution.py:633
  113.1 8.2 %collective-permute-start.3 = (bf16[128,768]{1,0:T(8,128)(2,1)S(1)}, bf16[128,768]{1,0:T(8,128)(2,1)S(1)}, u32[]{:S(2)}, u32[]{:S(2)}) collective-permute-start(bf16[128,768]{1,0:T(8,128)(2,1)S(1)} %get-tuple-element.22.own.grads), channel_id=1, source_target_pairs={{1,0},{2,1},{3,2},{4,3},{5,4},{6,5},{7,6},{8,7},{9,8},{10,9},{11,1... | collective-permute-start | bytes 589832 | tf_op jit(solution)/shard_map/ppermute | solution.py:373
  115.3 7.6 %collective-permute-start.2 = (bf16[128,768]{1,0:T(8,128)(2,1)S(1)}, bf16[128,768]{1,0:T(8,128)(2,1)S(1)}, u32[]{:S(2)}, u32[]{:S(2)}) collective-permute-start(bf16[128,768]{1,0:T(8,128)(2,1)S(1)} %get-tuple-element.22.own.grads), channel_id=1, source_target_pairs={{0,1},{1,2},{2,3},{3,4},{4,5},{5,6},{6,7},{7,8},{8,9},{9,10},{10,1... | collective-permute-start | bytes 589832 | tf_op jit(solution)/shard_map/ppermute | solution.py:372

commit v3 on v2

--- a/solution.py
+++ b/solution.py
@@ -188,10 +188,8 @@
 
 
 def kernel_grad_kernel(
-    planes, height, which, left, own, right, grads, small, out, spread, products, joined, flat
+    planes, height, left, own, right, grads, small, out, spread, products, joined, flat
 ):
-    del which
-
     @pl.when(pl.program_id(0) == 0)
     def _():
         clear_rims(spread)
@@ -296,42 +294,50 @@
     return activated, (act_grad * slope).astype(BF16)
 
 
-def weight_grad_terms(which, weight_in, weight_out, scale, cotangent, normed, aligned):
-    rows = cotangent.shape[1]
-    for k in range(cotangent.shape[0]):
-        upstream = cotangent[which[2 + k]].astype(F32)
-        aligned[k * rows : (k + 1) * rows, :] = (scale[...] * upstream).astype(BF16)
-    mixed_grad = aligned[...]
+def weight_grad_terms(which, weight_in, weight_out, scale, normed, cotangents, aligned):
+    rows = normed.shape[1]
+    line = len(cotangents)
+    mixed_grad = jnp.concatenate(
+        [(scale[...] * part[...].astype(F32)).astype(BF16) for part in cotangents], axis=0
+    )
+    for k in range(line):
+        aligned[k * rows : (k + 1) * rows, :] = normed[which[4 + k]]
     across = (((1,), (1,)), ((), ()))
-    hidden = lax.dot_general(weight_in[...], normed[...], across, preferred_element_type=F32)
+    hidden = lax.dot_general(weight_in[...], aligned[...], across, preferred_element_type=F32)
     act_grad = lax.dot_general(weight_out[...], mixed_grad, across, preferred_element_type=F32)
     activated, hidden_grad = slopes(hidden, act_grad)
     return (
-        jnp.dot(hidden_grad, normed[...], preferred_element_type=F32),
+        jnp.dot(hidden_grad, aligned[...], preferred_element_type=F32),
         jnp.dot(activated, mixed_grad, preferred_element_type=F32),
     )
 
 
-def first_terms_kernel(which, weight_in, weight_out, scale, cotangent, normed, out, aligned):
-    terms = weight_grad_terms(which, weight_in, weight_out, scale, cotangent, normed, aligned)
+def other_core_terms_kernel(which, weight_in, weight_out, scale, normed, *rest):
+    *cotangents, out, aligned = rest
+    terms = weight_grad_terms(which, weight_in, weight_out, scale, normed, cotangents, aligned)
     for k in range(2):
-        out[0, k] = terms[k]
-
-
-def sent_terms_kernel(
-    which, weight_in, weight_out, scale, cotangent, normed, before, out, aligned
-):
-    terms = weight_grad_terms(which, weight_in, weight_out, scale, cotangent, normed, aligned)
+        out[0, k] = terms[k].astype(BF16)
+
+
+def own_core_terms_kernel(which, weight_in, weight_out, scale, normed, got, *rest):
+    *cotangents, sent, kept, aligned = rest
+    terms = weight_grad_terms(which, weight_in, weight_out, scale, normed, cotangents, aligned)
+    step = pl.program_id(0)
     for k in range(2):
-        out[k] = before[0, k] + terms[k]
-
-
-def last_terms_kernel(
-    which, weight_in, weight_out, scale, cotangent, normed, before, got, in_grad, out_grad, aligned
-):
-    terms = weight_grad_terms(which, weight_in, weight_out, scale, cotangent, normed, aligned)
+        total = terms[k] + got[0, k].astype(F32)
+
+        @pl.when(step == 0)
+        def _():
+            sent[k] = total.astype(BF16)
+
+        @pl.when(step == 1)
+        def _():
+            kept[k] = total
+
+
+def last_sum_kernel(kept, got, in_grad, out_grad):
     for k, out in enumerate((in_grad, out_grad)):
-        out[...] = before[0, k] + terms[k] + got[k]
+        out[...] = kept[k] + got[k].astype(F32)
 
 
 def spread_sum_kernel(parts, out):
@@ -388,15 +394,12 @@
     units = weight_in.shape[0]
     count = lax.axis_size("row")
     me = lax.axis_index("row")
-    half = count // 2
     quad = 4
     line = count // quad
-    alike = [[2 * k + p for k in range(half)] for p in range(2)]
     lines = [[quad * k + p for k in range(line)] for p in range(quad)]
     other_core = [(i, i ^ 1) for i in range(count)]
     other_side = [(i, i ^ 2) for i in range(count)]
     tiles = channels // LANES
-    half_tiles = tiles // 2
 
     own = voxels.reshape(rows, channels)
     upstream = cotangent.reshape(rows, channels)
@@ -404,16 +407,11 @@
     bias = norm_bias.reshape(1, channels)
     scale = layer_scale.reshape(1, channels)
     core = lax.rem(me, 2).astype(jnp.int32)
-    mine = me.astype(jnp.int32)
-    theirs = mine + 1 - 2 * core
-
     left, right = neighbours(own)
     upstream_line = [upstream] + [
         lax.ppermute(upstream, "row", [(i, (i + quad * k) % count) for i in range(count)])
         for k in range(1, line)
     ]
-    upstream_near = jnp.concatenate(upstream_line, axis=0).reshape(line, rows, channels)
-    upstream_far = lax.ppermute(upstream_near, "row", other_side)
 
     spread = pltpu.VMEM((9, planes + KS - 1, PAD, LANES), F32)
     split = pltpu.VMEM((9, KS, SUB, LANES), F32)
@@ -448,8 +446,6 @@
     gathered = lax.all_to_all(
         normed, "row", split_axis=0, concat_axis=0, tiled=True, axis_index_groups=lines
     )
-    normed_near = gathered.reshape(line * rows, channels)
-    normed_far = lax.ppermute(normed_near, "row", other_side)
 
     block = 512
     whole = whole_block(rows, channels)
@@ -494,58 +490,120 @@
 
     grad_left, grad_right = neighbours(conv_grad)
 
-    piece = -(-(TAP_ROWS + SUB) // half)
-    piece += -piece % (2 * SUB)
-    padded = piece * half
-
-    def kernel_grad_half(which, name):
-        def at(block_rows):
-            return pl.BlockSpec((block_rows, LANES), lambda c, w: (0, w[0] * half_tiles + c))
-
-        return pl.pallas_call(
-            functools.partial(kernel_grad_kernel, planes, height),
-            grid_spec=pltpu.PrefetchScalarGridSpec(
-                num_scalar_prefetch=1,
-                grid=(half_tiles,),
-                in_specs=[at(rows), at(rows), at(rows), at(rows), at(SUB)],
-                out_specs=pl.BlockSpec((padded, LANES), lambda c, w: (0, c)),
-                scratch_shapes=[
-                    spread,
-                    pltpu.VMEM((2, KS, SUB * SUB, LANES), F32),
-                    pltpu.VMEM((9, KS, SUB, LANES), F32),
-                    pltpu.VMEM((padded, LANES), F32),
-                ],
-            ),
-            out_shape=jax.ShapeDtypeStruct((padded, half_tiles * LANES), BF16),
-            compiler_params=params(),
-            cost_estimate=conv_cost(rows, channels // 2),
-            name=name,
-        )(which.reshape(1), left, own, right, conv_grad, small)
-
-    for_other = kernel_grad_half(1 - core, "kernel_grad_sent")
+    piece = -(-(TAP_ROWS + SUB) // count)
+    piece += -piece % SUB
+    padded = piece * count
+    sums = pl.pallas_call(
+        functools.partial(kernel_grad_kernel, planes, height),
+        grid=(tiles,),
+        in_specs=[
+            lane_block(rows),
+            lane_block(rows),
+            lane_block(rows),
+            lane_block(rows),
+            lane_block(SUB),
+        ],
+        out_specs=lane_block(padded),
+        out_shape=jax.ShapeDtypeStruct((padded, channels), BF16),
+        scratch_shapes=[
+            spread,
+            pltpu.VMEM((2, KS, SUB * SUB, LANES), F32),
+            pltpu.VMEM((9, KS, SUB, LANES), F32),
+            pltpu.VMEM((padded, LANES), F32),
+        ],
+        compiler_params=params(),
+        cost_estimate=conv_cost(rows, channels),
+        name="kernel_grad_terms",
+    )(left, own, right, conv_grad, small)
+
+    share = units // count
+    tokens = line * rows
+    base = me // quad * quad
+    side = lax.rem(me, quad) // 2
+    place = lax.rem(me // quad + line - jnp.arange(line, dtype=jnp.int32), line)
+    which = jnp.concatenate(
+        [
+            jnp.stack(
+                [
+                    base + 1 - core,
+                    base + 3 - core,
+                    base + 2 - 2 * side + core,
+                    base + 2 * side + core,
+                ]
+            ).astype(jnp.int32),
+            place.astype(jnp.int32),
+        ]
+    )
+    terms_cost = pl.CostEstimate(
+        flops=16 * tokens * channels * share,
+        bytes_accessed=4 * tokens * channels + 8 * share * channels,
+        transcendentals=4 * tokens * share,
+    )
+    pair = (2, 2, share, channels)
+
+    def chunk(at):
+        return pl.BlockSpec((share, channels), lambda s, w: (w[s + at], 0))
+
+    sets = [whole_block(1, channels), whole_block(line, rows, channels)]
+    cotangents = [whole_block(rows, channels)] * line
+    aligned = [pltpu.VMEM((tokens, channels), BF16)]
+
+    which, sums = lax.optimization_barrier((which, sums))
+    for_other = pl.pallas_call(
+        other_core_terms_kernel,
+        grid_spec=pltpu.PrefetchScalarGridSpec(
+            num_scalar_prefetch=1,
+            grid=(2,),
+            in_specs=[chunk(0), chunk(0)] + sets + cotangents,
+            out_specs=pl.BlockSpec((1,) + pair[1:], lambda s, w: (s, 0, 0, 0)),
+            scratch_shapes=aligned,
+        ),
+        out_shape=jax.ShapeDtypeStruct(pair, BF16),
+        compiler_params=params(),
+        cost_estimate=terms_cost,
+        name="weight_grads_other_core",
+    )(which, weight_in, weight_out, scale, gathered, *upstream_line)
     from_other = lax.ppermute(for_other, "row", other_core)
-    for_self = kernel_grad_half(core, "kernel_grad_kept")
-    chip_sum = (for_self.astype(F32) + from_other.astype(F32)).astype(BF16)
-    wide = half_tiles * LANES
+
     scattered = lax.all_to_all(
-        chip_sum.reshape(half, piece, wide),
-        "row",
-        split_axis=0,
-        concat_axis=0,
-        tiled=True,
-        axis_index_groups=alike,
-    )
+        sums.reshape(count, piece, channels), "row", split_axis=0, concat_axis=0, tiled=True
+    )
+    scattered, for_other = lax.optimization_barrier((scattered, for_other))
     copies = pl.pallas_call(
         spread_sum_kernel,
-        in_specs=[whole_block(half, piece, wide)],
-        out_specs=whole_block(count, piece, wide),
-        out_shape=jax.ShapeDtypeStruct((count, piece, wide), BF16),
+        in_specs=[whole_block(count, piece, channels)],
+        out_specs=whole_block(count, piece, channels),
+        out_shape=jax.ShapeDtypeStruct((count, piece, channels), BF16),
         grid=(1,),
         compiler_params=params(),
         name="kernel_grad_sum",
     )(scattered)
     totals = lax.all_to_all(copies, "row", split_axis=0, concat_axis=0, tiled=True)
 
+    which, copies = lax.optimization_barrier((which, copies))
+    sent, kept = pl.pallas_call(
+        own_core_terms_kernel,
+        grid_spec=pltpu.PrefetchScalarGridSpec(
+            num_scalar_prefetch=1,
+            grid=(2,),
+            in_specs=[chunk(2), chunk(2)]
+            + sets
+            + [pl.BlockSpec((1,) + pair[1:], lambda s, w: ((w[s + 2] - w[0] // 4 * 4) // 2, 0, 0, 0))]
+            + cotangents,
+            out_specs=[whole_block(2, share, channels)] * 2,
+            scratch_shapes=aligned,
+        ),
+        out_shape=[
+            jax.ShapeDtypeStruct(pair[1:], BF16),
+            jax.ShapeDtypeStruct(pair[1:], F32),
+        ],
+        compiler_params=params(),
+        cost_estimate=terms_cost,
+        name="weight_grads_own_core",
+    )(which, weight_in, weight_out, scale, gathered, from_other, *upstream_line)
+    got = lax.ppermute(sent, "row", other_side)
+
+    conv_own, sent = lax.optimization_barrier((conv_grad, sent))
     voxel_grad = pl.pallas_call(
         functools.partial(input_grad_kernel, planes, height),
         grid=(tiles,),
@@ -562,94 +620,30 @@
         compiler_params=params(),
         cost_estimate=conv_cost(rows, channels),
         name="input_grad_conv",
-    )(grad_left, conv_grad, grad_right, dw_kernel, upstream)
+    )(grad_left, conv_own, grad_right, dw_kernel, upstream)
 
     kernel_grad, vectors = pl.pallas_call(
         unpack_kernel,
-        grid=(2,),
-        in_specs=[pl.BlockSpec((half, None, piece, wide), lambda p: (0, p, 0, 0))],
-        out_specs=[
-            pl.BlockSpec((TAP_ROWS, wide), lambda p: (0, p)),
-            pl.BlockSpec((SUB, wide), lambda p: (0, p)),
-        ],
+        grid=(1,),
+        in_specs=[whole_block(count, piece, channels)],
+        out_specs=[whole_block(TAP_ROWS, channels), whole_block(SUB, channels)],
         out_shape=[
             jax.ShapeDtypeStruct((TAP_ROWS, channels), F32),
             jax.ShapeDtypeStruct((SUB, channels), F32),
         ],
         compiler_params=params(),
         name="kernel_grad_unpack",
-    )(totals.reshape(half, 2, piece, wide))
-
-    share = units // count
-    tokens = line * rows
-    terms_cost = pl.CostEstimate(
-        flops=8 * tokens * channels * share,
-        bytes_accessed=4 * tokens * channels + 4 * share * channels,
-        transcendentals=2 * tokens * share,
-    )
-    both = jax.ShapeDtypeStruct((2, share, channels), F32)
-    sets = [
-        whole_block(1, channels),
-        whole_block(line, rows, channels),
-        whole_block(tokens, channels),
-    ]
-    aligned = [pltpu.VMEM((tokens, channels), BF16)]
-    place = lax.rem(me // quad + line - jnp.arange(line, dtype=jnp.int32), line)
-    which = jnp.concatenate([theirs.reshape(1), mine.reshape(1), place.astype(jnp.int32)])
-
-    def chunk(at):
-        return pl.BlockSpec((share, channels), lambda s, w: (w[s + at], 0))
-
-    first = pl.pallas_call(
-        first_terms_kernel,
-        grid_spec=pltpu.PrefetchScalarGridSpec(
-            num_scalar_prefetch=1,
-            grid=(2,),
-            in_specs=[chunk(0), chunk(0)] + sets,
-            out_specs=pl.BlockSpec((1, 2, share, channels), lambda s, w: (s, 0, 0, 0)),
-            scratch_shapes=aligned,
-        ),
-        out_shape=jax.ShapeDtypeStruct((2, 2, share, channels), F32),
-        compiler_params=params(),
-        cost_estimate=terms_cost,
-        name="weight_grads_near",
-    )(which, weight_in, weight_out, scale, upstream_near, normed_near)
-    sent = pl.pallas_call(
-        sent_terms_kernel,
-        grid_spec=pltpu.PrefetchScalarGridSpec(
-            num_scalar_prefetch=1,
-            grid=(1,),
-            in_specs=[chunk(0), chunk(0)]
-            + sets
-            + [pl.BlockSpec((1, 2, share, channels), lambda s, w: (0, 0, 0, 0))],
-            out_specs=whole_block(2, share, channels),
-            scratch_shapes=aligned,
-        ),
-        out_shape=both,
-        compiler_params=params(),
-        cost_estimate=terms_cost,
-        name="weight_grads_sent",
-    )(which, weight_in, weight_out, scale, upstream_far, normed_far, first)
-    got = lax.ppermute(sent, "row", other_core)
+    )(totals)
+
     weight_in_grad, weight_out_grad = pl.pallas_call(
-        last_terms_kernel,
-        grid_spec=pltpu.PrefetchScalarGridSpec(
-            num_scalar_prefetch=1,
-            grid=(1,),
-            in_specs=[chunk(1), chunk(1)]
-            + sets
-            + [
-                pl.BlockSpec((1, 2, share, channels), lambda s, w: (1, 0, 0, 0)),
-                whole_block(2, share, channels),
-            ],
-            out_specs=[whole_block(share, channels), whole_block(share, channels)],
-            scratch_shapes=aligned,
-        ),
+        last_sum_kernel,
+        grid=(1,),
+        in_specs=[whole_block(2, share, channels)] * 2,
+        out_specs=[whole_block(share, channels)] * 2,
         out_shape=[jax.ShapeDtypeStruct((share, channels), F32)] * 2,
         compiler_params=params(),
-        cost_estimate=terms_cost,
-        name="weight_grads_kept",
-    )(which, weight_in, weight_out, scale, upstream_far, normed_far, first, got)
+        name="weight_grads_sum",
+    )(kept, got)
 
     return (
         block_out.reshape(voxels.shape),

time: 135 us -> 125 us (0.926)
  waiting for transfers between devices: 53.2 us -> 46.5 us
  Pallas kernels: 38.6 us -> 36.7 us
  other arithmetic: 1.83 us -> 0.01 us
    all_to_all x1, waiting for transfers between devices: 29.5 us -> 0.01 us  [on_device(): lax.all_to_all(sums.reshape(count, piece, channels), 'row', split_axis=0,...]
    ppermute x3, waiting for transfers between devices: 17 us -> 24 us  [on_device(): lax.ppermute(upstream, 'row', [(i, (i + quad * k) % count) for i in range...]
    ppermute x2, waiting for transfers between devices: 3.93 us -> 10.4 us  [neighbours(): lax.ppermute(cells, 'row', [(i, i + 1) for i in range(ends)])]
    all_to_all x1, waiting for transfers between devices: 0.01 us -> 5.48 us  [on_device(): lax.all_to_all(normed, 'row', split_axis=0, concat_axis=0, tiled=True, ax...]
    all_to_all x1, waiting for transfers between devices: 0.01 us -> 2.78 us  [on_device(): lax.all_to_all(copies, 'row', split_axis=0, concat_axis=0, tiled=True)]
    ppermute x1, starting transfers between devices: 3.75 us -> 1.34 us  [on_device(): from_other = lax.ppermute(for_other, 'row', other_core)]
    pallas_call x7 -> x6, Pallas kernels: 20.6 us -> 18.8 us  [the longest x1 5.59 us: on_device(): pl.pallas_call(own_core_terms_kernel, grid_spec=pltpu.PrefetchScalarGridS...]
    unnamed x12 -> x16, local copies, waits for them, and re-layouts: 2.17 us -> 3.22 us
  transfers between devices with their start and end apart: 14 -> 12, of which waited for: 6 -> 6; matrix products, arithmetic and copies ran while one was open for 3% -> 2% of each run, Pallas kernels for 22% -> 25%
where the time goes in v3:
time: 125 us; the launch traced here: 124 us
  waiting for transfers between devices  46.5 us (37%)
  Pallas kernels  36.7 us (29%)
  starting transfers between devices  34.5 us (28%)
  local copies, waits for them, and re-layouts  5.31 us (4%)
    ppermute x3, waiting for transfers between devices, on_device(): lax.ppermute(upstream, 'row', [(i, (i + quad * k) % count) for i in range...  24 us
    ppermute x2, waiting for transfers between devices, neighbours(): lax.ppermute(cells, 'row', [(i, i + 1) for i in range(ends)])  10.4 us
    pallas_call x1, Pallas kernels, on_device(): pl.pallas_call(mlp_kernel, grid=(units // block,), in_specs=[pl.BlockSpec...  9.23 us
    all_to_all x1, starting transfers between devices, on_device(): lax.all_to_all(copies, 'row', split_axis=0, concat_axis=0, tiled=True)  7.4 us
    ppermute x2, starting transfers between devices, neighbours(): lax.ppermute(cells, 'row', [(i, i + 1) for i in range(ends)])  6.79 us
    pallas_call x1, Pallas kernels, on_device(): pl.pallas_call(own_core_terms_kernel, grid_spec=pltpu.PrefetchScalarGridS...  5.59 us
    all_to_all x1, waiting for transfers between devices, on_device(): lax.all_to_all(normed, 'row', split_axis=0, concat_axis=0, tiled=True, ax...  5.48 us
    pallas_call x1, Pallas kernels, on_device(): pl.pallas_call(functools.partial(kernel_grad_kernel, planes, height), gri...  5.41 us
  transfers between devices with their start and end apart: 12, of which 6 were waited for; matrix products, arithmetic and copies ran while one was open for 2% of the time, Pallas kernels for 25%

profile of v3, /device:TPU:1, one launch (start us, length us, event | category | flops | bytes accessed | tf_op | source)
XLA Modules:
  0.0 123.8 jit_solution(283615862025201199)
XLA Ops:
  0.6 4.5 %collective-permute-start = (bf16[128,768]{1,0:T(8,128)(2,1)}, bf16[128,768]{1,0:T(8,128)(2,1)S(1)}, u32[]{:S(2)}, u32[]{:S(2)}) collective-permute-start(bf16[128,768]{1,0:T(8,128)(2,1)} %bitcast.16), channel_id=1, source_target_pairs={{0,1},{1,2},{2,3},{3,4},{4,5},{5,6},{6,7},{7,8},{8,9},{9,10},{10,1... | collective-permute-start | bytes 589832 | tf_op jit(solution)/shard_map/ppermute | solution.py:378
  5.2 1.9 %collective-permute-start.1 = (bf16[128,768]{1,0:T(8,128)(2,1)}, bf16[128,768]{1,0:T(8,128)(2,1)S(1)}, u32[]{:S(2)}, u32[]{:S(2)}) collective-permute-start(bf16[128,768]{1,0:T(8,128)(2,1)} %bitcast.17), channel_id=1, source_target_pairs={{1,0},{2,1},{3,2},{4,3},{5,4},{6,5},{7,6},{8,7},{9,8},{10,9},{11,1... | collective-permute-start | bytes 589832 | tf_op jit(solution)/shard_map/ppermute | solution.py:379
  7.1 0.7 reshape.41.gain
  7.8 0.7 reshape.42.bias
  8.5 0.0 collective-permute-done.left
  8.5 3.9 %collective-permute-done.1.right = bf16[128,768]{1,0:T(8,128)(2,1)S(1)} collective-permute-done((bf16[128,768]{1,0:T(8,128)(2,1)}, bf16[128,768]{1,0:T(8,128)(2,1)S(1)}, u32[]{:S(2)}, u32[]{:S(2)}) %collective-permute-start.1) | collective-permute-done | bytes 196640 | tf_op jit(solution)/shard_map/ppermute | solution.py:379
  12.4 0.0 copy-start
  12.4 1.2 copy-done
  13.6 0.0 copy-start.3
  13.6 0.9 copy-done.3
  14.5 4.6 %forward_conv.1 = (bf16[4,128,768]{2,1,0:T(8,128)(2,1)}, f32[128,768]{1,0:T(8,128)S(1)}, f32[128,128]{1,0:T(8,128)S(1)}) custom-call(bf16[128,768]{1,0:T(8,128)(2,1)S(1)} %collective-permute-done.left, bf16[128,768]{1,0:T(8,128)(2,1)S(1)} %bitcast.18, bf16[128,768]{1,0:T(8,128)(2,1)S(1)} %collective-permute-done.1.right, f32[343,768]{1,0:T(8,128)S(1)} %copy-done, ...), custom_call_target="tpu_custom_call" | custom-call | flops 67436544 | bytes 1572864 | tf_op jit(solution)/shard_map/forward_conv/pallas_call | solution.py:419
  19.1 4.7 %all-to-all-start.1 = ((bf16[4,128,768]{2,1,0:T(8,128)(2,1)}), bf16[4,128,768]{2,1,0:T(8,128)(2,1)S(1)}, u32[]{:S(2)}, u32[]{:S(2)}) async-start(bf16[4,128,768]{2,1,0:T(8,128)(2,1)} %get-tuple-element.25.normed), calls=%async_computation.1 | async-start | bytes 1572864 | tf_op jit(solution)/shard_map/all_to_all | solution.py:446
  23.9 0.0 copy-done.7
  23.9 0.1 concatenate.3.which
  24.0 0.0 copy-done.2
  24.0 0.0 copy-done.4
  24.0 9.2 %mlp_both_ways.1 = (bf16[128,768]{1,0:T(8,128)(2,1)}, bf16[128,768]{1,0:T(8,128)(2,1)S(1)}, f32[8,768]{1,0:T(8,128)S(1)}) custom-call(bf16[4,128,768]{2,1,0:T(8,128)(2,1)} %get-tuple-element.25.normed, bf16[3072,768]{1,0:T(8,128)(2,1)} %weight_in.5, bf16[3072,768]{1,0:T(8,128)(2,1)} %weight_out.5, f32[128,768]{1,0:T(8,128)S(1)} %get-tuple-element.26.unit, ...), custom_call_target="tpu_custom_call" | custom-call | flops 2415919104 | bytes 9437184 | tf_op jit(solution)/shard_map/mlp_both_ways/pallas_call | solution.py:453
  33.2 5.4 %kernel_grad_terms.1 = bf16[384,768]{1,0:T(8,128)(2,1)} custom-call(bf16[128,768]{1,0:T(8,128)(2,1)S(1)} %collective-permute-done.left, bf16[128,768]{1,0:T(8,128)(2,1)S(1)} %bitcast.20, bf16[128,768]{1,0:T(8,128)(2,1)S(1)} %collective-permute-done.1.right, bf16[128,768]{1,0:T(8,128)(2,1)S(1)} %get-tuple-element.36.grads.own, ...), custom_call_target="tpu_custom_call" | custom-call | flops 67436544 | bytes 1572864 | tf_op jit(solution)/shard_map/kernel_grad_terms/pallas_call | solution.py:496
  38.7 5.5 %all-to-all-done.1.normed = bf16[4,128,768]{2,1,0:T(8,128)(2,1)S(1)} async-done(((bf16[4,128,768]{2,1,0:T(8,128)(2,1)}), bf16[4,128,768]{2,1,0:T(8,128)(2,1)S(1)}, u32[]{:S(2)}, u32[]{:S(2)}) %all-to-all-start.1) | async-done | bytes 786464 | tf_op jit(solution)/shard_map/all_to_all | solution.py:446
  44.1 4.2 %all-to-all-start = ((bf16[16,24,768]{2,1,0:T(8,128)(2,1)}), bf16[16,24,768]{2,1,0:T(8,128)(2,1)S(1)}, u32[]{:S(2)}, u32[]{:S(2)}) async-start(bf16[16,24,768]{2,1,0:T(8,128)(2,1)} %bitcast.7), calls=%async_computation | async-start | bytes 1179648 | tf_op jit(solution)/shard_map/all_to_all | solution.py:568
  48.3 1.4 %collective-permute-start.3 = (bf16[128,768]{1,0:T(8,128)(2,1)S(1)}, bf16[128,768]{1,0:T(8,128)(2,1)S(1)}, u32[]{:S(2)}, u32[]{:S(2)}) collective-permute-start(bf16[128,768]{1,0:T(8,128)(2,1)S(1)} %bitcast.10), channel_id=1, source_target_pairs={{0,4},{1,5},{2,6},{3,7},{4,8},{5,9},{6,10},{7,11},{8,12},{9,13},{1... | collective-permute-start | bytes 589832 | tf_op jit(solution)/shard_map/ppermute | solution.py:412
  49.7 2.1 %collective-permute-start.4 = (bf16[128,768]{1,0:T(8,128)(2,1)S(1)}, bf16[128,768]{1,0:T(8,128)(2,1)S(1)}, u32[]{:S(2)}, u32[]{:S(2)}) collective-permute-start(bf16[128,768]{1,0:T(8,128)(2,1)S(1)} %bitcast.11), channel_id=1, source_target_pairs={{0,8},{1,9},{2,10},{3,11},{4,12},{5,13},{6,14},{7,15},{8,0},{9,1},... | collective-permute-start | bytes 589832 | tf_op jit(solution)/shard_map/ppermute | solution.py:412
  51.8 1.2 collective-permute-start.5
  53.0 13.4 %collective-permute-done.3.rest_1_ = bf16[128,768]{1,0:T(8,128)(2,1)S(1)} collective-permute-done((bf16[128,768]{1,0:T(8,128)(2,1)S(1)}, bf16[128,768]{1,0:T(8,128)(2,1)S(1)}, u32[]{:S(2)}, u32[]{:S(2)}) %collective-permute-start.3) | collective-permute-done | bytes 196640 | tf_op jit(solution)/shard_map/ppermute | solution.py:412
  66.4 10.6 %collective-permute-done.4.rest_2_ = bf16[128,768]{1,0:T(8,128)(2,1)S(1)} collective-permute-done((bf16[128,768]{1,0:T(8,128)(2,1)S(1)}, bf16[128,768]{1,0:T(8,128)(2,1)S(1)}, u32[]{:S(2)}, u32[]{:S(2)}) %collective-permute-start.4) | collective-permute-done | bytes 196640 | tf_op jit(solution)/shard_map/ppermute | solution.py:412
  77.0 0.0 collective-permute-done.5.rest_3_
  77.0 4.7 %weight_grads_other_core.1 = bf16[2,2,192,768]{3,2,1,0:T(8,128)(2,1)} custom-call(s32[8]{0:T(128)S(1)} %concatenate.3.which, bf16[3072,768]{1,0:T(8,128)(2,1)} %weight_in.5, bf16[3072,768]{1,0:T(8,128)(2,1)} %weight_out.5, f32[1,768]{1,0:T(1,128)S(1)} %reshape.43.scale, bf16[4,128,768]{2,1,0:T(8,128)(2,1)S(1)} %all-to-all-done.1.normed, ...), custom_call_target="tpu_custom_call" | custom-call | flops 1207959552 | bytes 2752512 | tf_op jit(solution)/shard_map/weight_grads_other_core/pallas_call | solution.py:552
  81.7 1.3 %collective-permute-start.6 = (bf16[2,2,192,768]{3,2,1,0:T(8,128)(2,1)}, bf16[2,2,192,768]{3,2,1,0:T(8,128)(2,1)}, u32[]{:S(2)}, u32[]{:S(2)}) collective-permute-start(bf16[2,2,192,768]{3,2,1,0:T(8,128)(2,1)} %weight_grads_other_core.1), channel_id=1, source_target_pairs={{0,1},{1,0},{2,3},{3,2},{4,5},{5,4},{6,7},{7,6},{8,9},{9,8},{10,11... | collective-permute-start | bytes 3538952 | tf_op jit(solution)/shard_map/ppermute | solution.py:566
  83.0 0.0 all-to-all-done.parts
  83.0 0.9 kernel_grad_sum.1
  83.9 7.4 %all-to-all-start.2 = ((bf16[16,24,768]{2,1,0:T(8,128)(2,1)}), bf16[16,24,768]{2,1,0:T(8,128)(2,1)S(1)}, u32[]{:S(2)}, u32[]{:S(2)}) async-start(bf16[16,24,768]{2,1,0:T(8,128)(2,1)} %kernel_grad_sum.1), calls=%async_computation.2 | async-start | bytes 1179648 | tf_op jit(solution)/shard_map/all_to_all | solution.py:581
  91.3 0.0 collective-permute-done.6.got
  91.3 0.0 copy-start.1
  91.4 5.6 %weight_grads_own_core.1 = (bf16[2,192,768]{2,1,0:T(8,128)(2,1)}, f32[2,192,768]{2,1,0:T(8,128)S(1)}) custom-call(s32[8]{0:T(128)S(1)} %concatenate.3.which, bf16[3072,768]{1,0:T(8,128)(2,1)} %weight_in.5, bf16[3072,768]{1,0:T(8,128)(2,1)} %weight_out.5, f32[1,768]{1,0:T(1,128)S(1)} %reshape.43.scale, bf16[4,128,768]{2,1,0:T(8,128)(2,1)S(1)} %all-to-all-done.1.normed, ...), custom_call_target="tpu_custom_call" | custom-call | flops 1207959552 | bytes 2752512 | tf_op jit(solution)/shard_map/weight_grads_own_core/pallas_call | solution.py:584
  96.9 1.0 copy-done.5
  98.0 1.4 %collective-permute-start.8 = (bf16[2,192,768]{2,1,0:T(8,128)(2,1)}, bf16[2,192,768]{2,1,0:T(8,128)(2,1)S(1)}, u32[]{:S(2)}, u32[]{:S(2)}) collective-permute-start(bf16[2,192,768]{2,1,0:T(8,128)(2,1)} %get-tuple-element.35), channel_id=1, source_target_pairs={{0,2},{1,3},{2,0},{3,1},{4,6},{5,7},{6,4},{7,5},{8,10},{9,11},{10,... | collective-permute-start | bytes 1769480 | tf_op jit(solution)/shard_map/ppermute | solution.py:604
  99.4 2.2 %collective-permute-start.2 = (bf16[128,768]{1,0:T(8,128)(2,1)S(1)}, bf16[128,768]{1,0:T(8,128)(2,1)S(1)}, u32[]{:S(2)}, u32[]{:S(2)}) collective-permute-start(bf16[128,768]{1,0:T(8,128)(2,1)S(1)} %get-tuple-element.36.grads.own), channel_id=1, source_target_pairs={{0,1},{1,2},{2,3},{3,4},{4,5},{5,6},{6,7},{7,8},{8,9},{9,10},{10,1... | collective-permute-start | bytes 589832 | tf_op jit(solution)/shard_map/ppermute | solution.py:378
  101.6 2.1 %collective-permute-start.7 = (bf16[128,768]{1,0:T(8,128)(2,1)S(1)}, bf16[128,768]{1,0:T(8,128)(2,1)S(1)}, u32[]{:S(2)}, u32[]{:S(2)}) collective-permute-start(bf16[128,768]{1,0:T(8,128)(2,1)S(1)} %get-tuple-element.36.grads.own), channel_id=1, source_target_pairs={{1,0},{2,1},{3,2},{4,3},{5,4},{6,5},{7,6},{8,7},{9,8},{10,9},{11,1... | collective-permute-start | bytes 589832 | tf_op jit(solution)/shard_map/ppermute | solution.py:379
  103.7 2.8 %all-to-all-done.2.parts = bf16[16,24,768]{2,1,0:T(8,128)(2,1)S(1)} async-done(((bf16[16,24,768]{2,1,0:T(8,128)(2,1)}), bf16[16,24,768]{2,1,0:T(8,128)(2,1)S(1)}, u32[]{:S(2)}, u32[]{:S(2)}) %all-to-all-start.2) | async-done | bytes 589856 | tf_op jit(solution)/shard_map/all_to_all | solution.py:581
  106.5 1.0 kernel_grad_unpack.1
  107.5 0.6 slice_reduce_fusion
  108.2 10.4 %collective-permute-done.2.left = bf16[128,768]{1,0:T(8,128)(2,1)S(1)} collective-permute-done((bf16[128,768]{1,0:T(8,128)(2,1)S(1)}, bf16[128,768]{1,0:T(8,128)(2,1)S(1)}, u32[]{:S(2)}, u32[]{:S(2)}) %collective-permute-start.2) | collective-permute-done | bytes 196640 | tf_op jit(solution)/shard_map/ppermute | solution.py:378
  118.5 0.0 collective-permute-done.7.right
  118.5 0.0 copy-done.1
  118.5 4.2 %input_grad_conv.1 = bf16[128,768]{1,0:T(8,128)(2,1)} custom-call(bf16[128,768]{1,0:T(8,128)(2,1)S(1)} %collective-permute-done.2.left, bf16[128,768]{1,0:T(8,128)(2,1)S(1)} %get-tuple-element.36.grads.own, bf16[128,768]{1,0:T(8,128)(2,1)S(1)} %collective-permute-done.7.right, f32[343,768]{1,0:T(8,128)S(1)} %copy-done.1, bf16[128,768]{1,0:T(8,128)(2,1)S(1)} %bitcast.15), custom_call_target="tpu_custom_call" | custom-call | flops 67436544 | bytes 1572864 | tf_op jit(solution)/shard_map/input_grad_conv/pallas_call | solution.py:607
  122.7 0.0 collective-permute-done.8.got
  122.7 0.0 copy-done.6
  122.7 1.1 weight_grads_sum.1
  (7 shorter events, 0.0 us)
Async XLA Ops:
  0.6 7.9 %collective-permute-start = (bf16[128,768]{1,0:T(8,128)(2,1)}, bf16[128,768]{1,0:T(8,128)(2,1)S(1)}, u32[]{:S(2)}, u32[]{:S(2)}) collective-permute-start(bf16[128,768]{1,0:T(8,128)(2,1)} %bitcast.16), channel_id=1, source_target_pairs={{0,1},{1,2},{2,3},{3,4},{4,5},{5,6},{6,7},{7,8},{8,9},{9,10},{10,1... | collective-permute-start | bytes 589832 | tf_op jit(solution)/shard_map/ppermute | solution.py:378
  5.2 7.2 %collective-permute-start.1 = (bf16[128,768]{1,0:T(8,128)(2,1)}, bf16[128,768]{1,0:T(8,128)(2,1)S(1)}, u32[]{:S(2)}, u32[]{:S(2)}) collective-permute-start(bf16[128,768]{1,0:T(8,128)(2,1)} %bitcast.17), channel_id=1, source_target_pairs={{1,0},{2,1},{3,2},{4,3},{5,4},{6,5},{7,6},{8,7},{9,8},{10,9},{11,1... | collective-permute-start | bytes 589832 | tf_op jit(solution)/shard_map/ppermute | solution.py:379
  12.4 1.2 copy-start
  13.6 0.9 copy-start.3
  19.1 4.7 %copy-start.7 = (f32[768]{0:T(1024)S(1)}, f32[768]{0:T(1024)}, u32[]{:S(2)}) copy-start(f32[768]{0:T(1024)} %param.14) | copy-start | bytes 9220
  19.1 4.9 %copy-start.2 = (bf16[4,4,8,768]{3,2,1,0:T(8,128)(2,1)S(1)}, bf16[4,4,8,768]{3,2,1,0:T(8,128)(2,1)}, u32[]{:S(2)}) copy-start(bf16[4,4,8,768]{3,2,1,0:T(8,128)(2,1)} %param.15) | copy-start | bytes 589828
  19.1 4.9 %copy-start.4 = (bf16[4,4,8,768]{3,2,1,0:T(8,128)(2,1)S(1)}, bf16[4,4,8,768]{3,2,1,0:T(8,128)(2,1)}, u32[]{:S(2)}) copy-start(bf16[4,4,8,768]{3,2,1,0:T(8,128)(2,1)} %param.8) | copy-start | bytes 589828
  19.1 25.0 %all-to-all-start.1 = ((bf16[4,128,768]{2,1,0:T(8,128)(2,1)}), bf16[4,128,768]{2,1,0:T(8,128)(2,1)S(1)}, u32[]{:S(2)}, u32[]{:S(2)}) async-start(bf16[4,128,768]{2,1,0:T(8,128)(2,1)} %get-tuple-element.25.normed), calls=%async_computation.1 | async-start | bytes 1572864 | tf_op jit(solution)/shard_map/all_to_all | solution.py:446
  44.1 38.9 %all-to-all-start = ((bf16[16,24,768]{2,1,0:T(8,128)(2,1)}), bf16[16,24,768]{2,1,0:T(8,128)(2,1)S(1)}, u32[]{:S(2)}, u32[]{:S(2)}) async-start(bf16[16,24,768]{2,1,0:T(8,128)(2,1)} %bitcast.7), calls=%async_computation | async-start | bytes 1179648 | tf_op jit(solution)/shard_map/all_to_all | solution.py:568
  48.3 18.1 %collective-permute-start.3 = (bf16[128,768]{1,0:T(8,128)(2,1)S(1)}, bf16[128,768]{1,0:T(8,128)(2,1)S(1)}, u32[]{:S(2)}, u32[]{:S(2)}) collective-permute-start(bf16[128,768]{1,0:T(8,128)(2,1)S(1)} %bitcast.10), channel_id=1, source_target_pairs={{0,4},{1,5},{2,6},{3,7},{4,8},{5,9},{6,10},{7,11},{8,12},{9,13},{1... | collective-permute-start | bytes 589832 | tf_op jit(solution)/shard_map/ppermute | solution.py:412
  49.7 27.3 %collective-permute-start.4 = (bf16[128,768]{1,0:T(8,128)(2,1)S(1)}, bf16[128,768]{1,0:T(8,128)(2,1)S(1)}, u32[]{:S(2)}, u32[]{:S(2)}) collective-permute-start(bf16[128,768]{1,0:T(8,128)(2,1)S(1)} %bitcast.11), channel_id=1, source_target_pairs={{0,8},{1,9},{2,10},{3,11},{4,12},{5,13},{6,14},{7,15},{8,0},{9,1},... | collective-permute-start | bytes 589832 | tf_op jit(solution)/shard_map/ppermute | solution.py:412
  51.8 25.1 %collective-permute-start.5 = (bf16[128,768]{1,0:T(8,128)(2,1)S(1)}, bf16[128,768]{1,0:T(8,128)(2,1)S(1)}, u32[]{:S(2)}, u32[]{:S(2)}) collective-permute-start(bf16[128,768]{1,0:T(8,128)(2,1)S(1)} %bitcast.12), channel_id=1, source_target_pairs={{0,12},{1,13},{2,14},{3,15},{4,0},{5,1},{6,2},{7,3},{8,4},{9,5},{1... | collective-permute-start | bytes 589832 | tf_op jit(solution)/shard_map/ppermute | solution.py:412
  81.7 9.6 %collective-permute-start.6 = (bf16[2,2,192,768]{3,2,1,0:T(8,128)(2,1)}, bf16[2,2,192,768]{3,2,1,0:T(8,128)(2,1)}, u32[]{:S(2)}, u32[]{:S(2)}) collective-permute-start(bf16[2,2,192,768]{3,2,1,0:T(8,128)(2,1)} %weight_grads_other_core.1), channel_id=1, source_target_pairs={{0,1},{1,0},{2,3},{3,2},{4,5},{5,4},{6,7},{7,6},{8,9},{9,8},{10,11... | collective-permute-start | bytes 3538952 | tf_op jit(solution)/shard_map/ppermute | solution.py:566
  83.9 22.6 %all-to-all-start.2 = ((bf16[16,24,768]{2,1,0:T(8,128)(2,1)}), bf16[16,24,768]{2,1,0:T(8,128)(2,1)S(1)}, u32[]{:S(2)}, u32[]{:S(2)}) async-start(bf16[16,24,768]{2,1,0:T(8,128)(2,1)} %kernel_grad_sum.1), calls=%async_computation.2 | async-start | bytes 1179648 | tf_op jit(solution)/shard_map/all_to_all | solution.py:581
  91.3 27.2 %copy-start.1 = (f32[343,768]{1,0:T(8,128)S(1)}, f32[343,768]{1,0:T(8,128)}, u32[]{:S(2)}) copy-start(f32[343,768]{1,0:T(8,128)} %taps.3) | copy-start | bytes 3161092
  96.9 1.0 copy-start.5
  98.0 24.7 %collective-permute-start.8 = (bf16[2,192,768]{2,1,0:T(8,128)(2,1)}, bf16[2,192,768]{2,1,0:T(8,128)(2,1)S(1)}, u32[]{:S(2)}, u32[]{:S(2)}) collective-permute-start(bf16[2,192,768]{2,1,0:T(8,128)(2,1)} %get-tuple-element.35), channel_id=1, source_target_pairs={{0,2},{1,3},{2,0},{3,1},{4,6},{5,7},{6,4},{7,5},{8,10},{9,11},{10,... | collective-permute-start | bytes 1769480 | tf_op jit(solution)/shard_map/ppermute | solution.py:604
  99.4 19.2 %collective-permute-start.2 = (bf16[128,768]{1,0:T(8,128)(2,1)S(1)}, bf16[128,768]{1,0:T(8,128)(2,1)S(1)}, u32[]{:S(2)}, u32[]{:S(2)}) collective-permute-start(bf16[128,768]{1,0:T(8,128)(2,1)S(1)} %get-tuple-element.36.grads.own), channel_id=1, source_target_pairs={{0,1},{1,2},{2,3},{3,4},{4,5},{5,6},{6,7},{7,8},{8,9},{9,10},{10,1... | collective-permute-start | bytes 589832 | tf_op jit(solution)/shard_map/ppermute | solution.py:378
  101.6 16.9 %collective-permute-start.7 = (bf16[128,768]{1,0:T(8,128)(2,1)S(1)}, bf16[128,768]{1,0:T(8,128)(2,1)S(1)}, u32[]{:S(2)}, u32[]{:S(2)}) collective-permute-start(bf16[128,768]{1,0:T(8,128)(2,1)S(1)} %get-tuple-element.36.grads.own), channel_id=1, source_target_pairs={{1,0},{2,1},{3,2},{4,3},{5,4},{6,5},{7,6},{8,7},{9,8},{10,9},{11,1... | collective-permute-start | bytes 589832 | tf_op jit(solution)/shard_map/ppermute | solution.py:379
  107.5 15.2 %copy-start.6 = (f32[2,192,768]{2,1,0:T(8,128)S(1)}, f32[2,192,768]{2,1,0:T(8,128)}, u32[]{:S(2)}) copy-start(f32[2,192,768]{2,1,0:T(8,128)} %copy-done.5) | copy-start | bytes 3538948

commit v4 on v3

--- a/solution.py
+++ b/solution.py
@@ -81,11 +81,8 @@
     return terms[0]
 
 
-def stage_source(left, own, right, planes, height, spread):
+def stage_source(wanted, height, spread):
     row = height * SUB
-    wanted = [(left, x) for x in range(planes - MARGIN, planes)]
-    wanted += [(own, x) for x in range(planes)]
-    wanted += [(right, x) for x in range(MARGIN)]
     for at, (block, x) in enumerate(wanted):
         plane = block[x * row : (x + 1) * row, :].astype(F32)
         lines = [plane[y * SUB : (y + 1) * SUB, :] for y in range(height)]
@@ -93,13 +90,23 @@
             spread[j, at, SUB : 2 * SUB, :] = term
 
 
+def rim_planes(left, right, planes):
+    wanted = [(left, x) for x in range(planes - MARGIN, planes)]
+    return wanted + [(right, x) for x in range(MARGIN)]
+
+
+def all_planes(left, own, right, planes):
+    rim = rim_planes(left, right, planes)
+    return rim[:MARGIN] + [(own, x) for x in range(planes)] + rim[MARGIN:]
+
+
 def clear_rims(spread):
     zeros = jnp.zeros(spread.shape[:2] + (SUB, LANES), F32)
     spread[:, :, :SUB, :] = zeros
     spread[:, :, 2 * SUB :, :] = zeros
 
 
-def stage_taps(taps, flipped, split):
+def stage_taps(taps, split):
     for dx in range(KS):
         rows = []
         for dy in range(KS):
@@ -108,48 +115,66 @@
                 rows.append(taps[first : first + SUB, :])
             else:
                 rows.append(pltpu.roll(taps[TAP_ROWS - SUB : TAP_ROWS, :], SUB - 1, 0))
-        if flipped:
-            rows = rows[::-1]
         for j, term in enumerate(split_taps(rows)):
-            split[j, KS - 1 - dx if flipped else dx] = term
-
-
-def convolve(spread, split, planes, flipped):
+            split[j, dx] = term
+
+
+REVERSED = (0, 2, 1, 6, 8, 7, 3, 5, 4)
+
+
+def convolve(spread, split, planes, held, flipped):
     terms = []
     for j in range(9):
         sums = [None] * planes
         for dz in range(KS):
             first = SUB - MARGIN + dz
-            source = [
-                spread[j, x, first : first + SUB, :] for x in range(planes + KS - 1)
-            ]
-            at = KS - 1 - dz if flipped else dz
-            weights = [
-                jnp.broadcast_to(split[j, dx, at : at + 1, :], (SUB, LANES)) for dx in range(KS)
-            ]
+            source = {x: spread[j, at, first : first + SUB, :] for at, x in enumerate(held)}
+            weights = []
+            for dx in range(KS):
+                if flipped:
+                    tap = split[REVERSED[j], KS - 1 - dx, KS - 1 - dz : KS - dz, :]
+                else:
+                    tap = split[j, dx, dz : dz + 1, :]
+                weights.append(jnp.broadcast_to(tap, (SUB, LANES)))
             for x in range(planes):
-                part = tree_sum([source[x + dx] * weights[dx] for dx in range(KS)])
+                part = tree_sum(
+                    [source[x + dx] * weights[dx] for dx in range(KS) if x + dx in source]
+                )
                 sums[x] = part if sums[x] is None else sums[x] + part
         terms.append(sums)
     return [join_outputs([terms[j][x] for j in range(9)]) for x in range(planes)]
 
 
-def forward_kernel(
-    planes, height, left, own, right, taps, gain, bias, normed, unit, inv, spread, split, conv
-):
-    step = pl.program_id(0)
-
-    @pl.when(step == 0)
+def own_conv_kernel(planes, height, own, taps, out, split, spread):
+    @pl.when(pl.program_id(0) == 0)
     def _():
         clear_rims(spread)
 
-    stage_source(left, own, right, planes, height, spread)
-    stage_taps(taps, False, split)
-    rows = convolve(spread, split, planes, False)
+    stage_source([(own, x) for x in range(planes)], height, spread)
+    stage_taps(taps, split)
+    rows = convolve(spread, split, planes, range(MARGIN, MARGIN + planes), False)
     for x in range(planes):
         for y in range(height):
             at = (x * height + y) * SUB
-            conv[step, at : at + SUB, :] = rows[x][y]
+            out[at : at + SUB, :] = rows[x][y]
+
+
+def rim_conv_kernel(
+    planes, height, left, right, split, partial, gain, bias, normed, unit, inv, spread, conv
+):
+    step = pl.program_id(0)
+
+    @pl.when(step == 0)
+    def _():
+        clear_rims(spread)
+
+    stage_source(rim_planes(left, right, planes), height, spread)
+    held = list(range(MARGIN)) + list(range(MARGIN + planes, 2 * MARGIN + planes))
+    rows = convolve(spread, split, planes, held, False)
+    for x in range(planes):
+        for y in range(height):
+            at = (x * height + y) * SUB
+            conv[step, at : at + SUB, :] = rows[x][y] + partial[at : at + SUB, :]
 
     @pl.when(step == pl.num_programs(0) - 1)
     def _():
@@ -172,14 +197,13 @@
                 normed[copy, :, lanes] = whole
 
 
-def input_grad_kernel(planes, height, left, own, right, taps, cotangent, out, spread, split):
+def input_grad_kernel(planes, height, left, own, right, split, cotangent, out, spread):
     @pl.when(pl.program_id(0) == 0)
     def _():
         clear_rims(spread)
 
-    stage_source(left, own, right, planes, height, spread)
-    stage_taps(taps, True, split)
-    rows = convolve(spread, split, planes, True)
+    stage_source(all_planes(left, own, right, planes), height, spread)
+    rows = convolve(spread, split, planes, range(2 * MARGIN + planes), True)
     for x in range(planes):
         at = x * height * SUB
         whole = jnp.concatenate(rows[x], axis=0)
@@ -196,7 +220,7 @@
         products[...] = jnp.zeros(products.shape, F32)
         flat[...] = jnp.zeros(flat.shape, F32)
 
-    stage_source(left, own, right, planes, height, spread)
+    stage_source(all_planes(left, own, right, planes), height, spread)
     upstream = []
     for x in range(planes):
         plane = grads[x * height * SUB : (x + 1) * height * SUB, :].astype(F32)
@@ -408,22 +432,43 @@
     scale = layer_scale.reshape(1, channels)
     core = lax.rem(me, 2).astype(jnp.int32)
     left, right = neighbours(own)
-    upstream_line = [upstream] + [
-        lax.ppermute(upstream, "row", [(i, (i + quad * k) % count) for i in range(count)])
-        for k in range(1, line)
-    ]
-
-    spread = pltpu.VMEM((9, planes + KS - 1, PAD, LANES), F32)
-    split = pltpu.VMEM((9, KS, SUB, LANES), F32)
-
+
+    def next_in_line(cells):
+        return lax.ppermute(cells, "row", [(i, (i + quad) % count) for i in range(count)])
+
+    upstream_line = [upstream, next_in_line(upstream)]
+
+    def spread_of(held):
+        return pltpu.VMEM((9, held, PAD, LANES), F32)
+
+    split_block = pl.BlockSpec((None, 9, KS, SUB, LANES), lambda c: (c, 0, 0, 0, 0))
+    partial, split = pl.pallas_call(
+        functools.partial(own_conv_kernel, planes, height),
+        grid=(tiles,),
+        in_specs=[lane_block(rows), lane_block(TAP_ROWS)],
+        out_specs=[lane_block(rows), split_block],
+        out_shape=[
+            jax.ShapeDtypeStruct((rows, channels), F32),
+            jax.ShapeDtypeStruct((tiles, 9, KS, SUB, LANES), F32),
+        ],
+        scratch_shapes=[spread_of(planes)],
+        compiler_params=params(),
+        cost_estimate=conv_cost(rows, channels // 2),
+        name="own_conv",
+    )(own, dw_kernel)
+
+    left, right, partial, upstream_line[-1] = lax.optimization_barrier(
+        (left, right, partial, upstream_line[-1])
+    )
+    upstream_line.append(next_in_line(upstream_line[-1]))
     normed, unit, inv = pl.pallas_call(
-        functools.partial(forward_kernel, planes, height),
+        functools.partial(rim_conv_kernel, planes, height),
         grid=(tiles,),
         in_specs=[
             lane_block(rows),
             lane_block(rows),
-            lane_block(rows),
-            lane_block(TAP_ROWS),
+            split_block,
+            lane_block(rows),
             whole_block(1, channels),
             whole_block(1, channels),
         ],
@@ -437,15 +482,19 @@
             jax.ShapeDtypeStruct((rows, channels), F32),
             jax.ShapeDtypeStruct((rows, LANES), F32),
         ],
-        scratch_shapes=[spread, split, pltpu.VMEM((tiles, rows, LANES), F32)],
-        compiler_params=params(),
-        cost_estimate=conv_cost(rows, channels),
-        name="forward_conv",
-    )(left, own, right, dw_kernel, gain, bias)
+        scratch_shapes=[spread_of(2 * MARGIN), pltpu.VMEM((tiles, rows, LANES), F32)],
+        compiler_params=params(),
+        cost_estimate=conv_cost(rows, channels // 2),
+        name="rim_conv",
+    )(left, right, split, partial, gain, bias)
 
     gathered = lax.all_to_all(
         normed, "row", split_axis=0, concat_axis=0, tiled=True, axis_index_groups=lines
     )
+
+    unit, upstream_line[-1] = lax.optimization_barrier((unit, upstream_line[-1]))
+    for _ in range(3, line):
+        upstream_line.append(next_in_line(upstream_line[-1]))
 
     block = 512
     whole = whole_block(rows, channels)
@@ -490,6 +539,7 @@
 
     grad_left, grad_right = neighbours(conv_grad)
 
+    small, upstream_line[-1] = lax.optimization_barrier((small, upstream_line[-1]))
     piece = -(-(TAP_ROWS + SUB) // count)
     piece += -piece % SUB
     padded = piece * count
@@ -506,7 +556,7 @@
         out_specs=lane_block(padded),
         out_shape=jax.ShapeDtypeStruct((padded, channels), BF16),
         scratch_shapes=[
-            spread,
+            spread_of(2 * MARGIN + planes),
             pltpu.VMEM((2, KS, SUB * SUB, LANES), F32),
             pltpu.VMEM((9, KS, SUB, LANES), F32),
             pltpu.VMEM((padded, LANES), F32),
@@ -548,7 +598,9 @@
     cotangents = [whole_block(rows, channels)] * line
     aligned = [pltpu.VMEM((tokens, channels), BF16)]
 
-    which, sums = lax.optimization_barrier((which, sums))
+    which, sums, grad_left, grad_right = lax.optimization_barrier(
+        (which, sums, grad_left, grad_right)
+    )
     for_other = pl.pallas_call(
         other_core_terms_kernel,
         grid_spec=pltpu.PrefetchScalarGridSpec(
@@ -611,16 +663,16 @@
             lane_block(rows),
             lane_block(rows),
             lane_block(rows),
-            lane_block(TAP_ROWS),
+            split_block,
             lane_block(rows),
         ],
         out_specs=lane_block(rows),
         out_shape=jax.ShapeDtypeStruct((rows, channels), BF16),
-        scratch_shapes=[spread, split],
+        scratch_shapes=[spread_of(2 * MARGIN + planes)],
         compiler_params=params(),
         cost_estimate=conv_cost(rows, channels),
         name="input_grad_conv",
-    )(grad_left, conv_own, grad_right, dw_kernel, upstream)
+    )(grad_left, conv_own, grad_right, split, upstream)
 
     kernel_grad, vectors = pl.pallas_call(
         unpack_kernel,

time: 125 us -> 125 us (level)
  waiting for transfers between devices: 46.5 us -> 34.5 us
  local copies, waits for them, and re-layouts: 5.31 us -> 11.4 us
  starting transfers between devices: 34.5 us -> 38.4 us
  Pallas kernels: 36.7 us -> 38.4 us
    ppermute x2, waiting for transfers between devices: 10.4 us -> 0.01 us  [neighbours(): lax.ppermute(cells, 'row', [(i, i + 1) for i in range(ends)])]
    all_to_all x1, waiting for transfers between devices: 0.01 us -> 10.2 us  [on_device(): lax.all_to_all(sums.reshape(count, piece, channels), 'row', split_axis=0,...]
    ppermute x3, waiting for transfers between devices: 24 us -> 15.2 us  [next_in_line(): lax.ppermute(cells, 'row', [(i, (i + quad) % count) for i in range(count)])]
    ppermute x1, waiting for transfers between devices: 0.01 us -> 7.42 us  [on_device(): got = lax.ppermute(sent, 'row', other_side)]
    unnamed x16 -> x26, local copies, waits for them, and re-layouts: 3.22 us -> 9.31 us
    all_to_all x1, waiting for transfers between devices: 5.48 us -> 0.01 us  [on_device(): lax.all_to_all(normed, 'row', split_axis=0, concat_axis=0, tiled=True, ax...]
    ppermute x2, starting transfers between devices: 6.79 us -> 11.8 us  [neighbours(): lax.ppermute(cells, 'row', [(i, i + 1) for i in range(ends)])]
    ppermute x2, waiting for transfers between devices: 3.89 us -> 0.01 us  [neighbours(): lax.ppermute(cells, 'row', [(i + 1, i) for i in range(ends)])]
  transfers between devices with their start and end apart: 12 -> 12, of which waited for: 6 -> 4; matrix products, arithmetic and copies ran while one was open for 2% -> 2% of each run, Pallas kernels for 25% -> 27%
where the time goes in v4:
time: 125 us; the launch traced here: 123 us
  starting transfers between devices  38.4 us (31%)
  Pallas kernels  38.4 us (31%)
  waiting for transfers between devices  34.5 us (28%)
  local copies, waits for them, and re-layouts  11.4 us (9%)
    ppermute x3, waiting for transfers between devices, next_in_line(): lax.ppermute(cells, 'row', [(i, (i + quad) % count) for i in range(count)])  15.2 us
    ppermute x2, starting transfers between devices, neighbours(): lax.ppermute(cells, 'row', [(i, i + 1) for i in range(ends)])  11.8 us
    all_to_all x1, waiting for transfers between devices, on_device(): lax.all_to_all(sums.reshape(count, piece, channels), 'row', split_axis=0,...  10.2 us
    unnamed x26, local copies, waits for them, and re-layouts  9.31 us
    pallas_call x1, Pallas kernels, on_device(): pl.pallas_call(mlp_kernel, grid=(units // block,), in_specs=[pl.BlockSpec...  9.25 us
    ppermute x1, waiting for transfers between devices, on_device(): got = lax.ppermute(sent, 'row', other_side)  7.42 us
    ppermute x3, starting transfers between devices, next_in_line(): lax.ppermute(cells, 'row', [(i, (i + quad) % count) for i in range(count)])  7.25 us
    pallas_call x1, Pallas kernels, on_device(): pl.pallas_call(own_core_terms_kernel, grid_spec=pltpu.PrefetchScalarGridS...  5.79 us
  transfers between devices with their start and end apart: 12, of which 4 were waited for; matrix products, arithmetic and copies ran while one was open for 2% of the time, Pallas kernels for 27%

profile of v4, /device:TPU:1, one launch (start us, length us, event | category | flops | bytes accessed | tf_op | source)
XLA Modules:
  0.0 123.4 jit_solution(13214899489623561821)
XLA Ops:
  0.6 4.5 %collective-permute-start = (bf16[128,768]{1,0:T(8,128)(2,1)}, bf16[128,768]{1,0:T(8,128)(2,1)S(1)}, u32[]{:S(2)}, u32[]{:S(2)}) collective-permute-start(bf16[128,768]{1,0:T(8,128)(2,1)} %bitcast.15), channel_id=1, source_target_pairs={{0,1},{1,2},{2,3},{3,4},{4,5},{5,6},{6,7},{7,8},{8,9},{9,10},{10,1... | collective-permute-start | bytes 589832 | tf_op jit(solution)/shard_map/ppermute | solution.py:402
  5.2 1.9 %collective-permute-start.1 = (bf16[128,768]{1,0:T(8,128)(2,1)}, bf16[128,768]{1,0:T(8,128)(2,1)S(1)}, u32[]{:S(2)}, u32[]{:S(2)}) collective-permute-start(bf16[128,768]{1,0:T(8,128)(2,1)} %bitcast.16), channel_id=1, source_target_pairs={{1,0},{2,1},{3,2},{4,3},{5,4},{6,5},{7,6},{8,7},{9,8},{10,9},{11,1... | collective-permute-start | bytes 589832 | tf_op jit(solution)/shard_map/ppermute | solution.py:403
  7.1 1.3 %collective-permute-start.2 = (bf16[128,768]{1,0:T(8,128)(2,1)}, bf16[128,768]{1,0:T(8,128)(2,1)S(1)}, u32[]{:S(2)}, u32[]{:S(2)}) collective-permute-start(bf16[128,768]{1,0:T(8,128)(2,1)} %bitcast.9), channel_id=1, source_target_pairs={{0,4},{1,5},{2,6},{3,7},{4,8},{5,9},{6,10},{7,11},{8,12},{9,13},{1... | collective-permute-start | bytes 589832 | tf_op jit(solution)/shard_map/ppermute | solution.py:437
  8.5 0.7 reshape.42.gain
  9.1 0.7 reshape.43.bias
  9.8 0.9 copy-done.3
  10.8 1.2 copy-done.7
  12.0 2.2 %own_conv.1 = (f32[128,768]{1,0:T(8,128)S(1)}, f32[6,9,7,8,128]{4,3,2,1,0:T(8,128)S(1)}) custom-call(bf16[128,768]{1,0:T(8,128)(2,1)S(1)} %bitcast.17, f32[343,768]{1,0:T(8,128)S(1)} %copy-done.7), custom_call_target="tpu_custom_call" | custom-call | flops 33718272 | bytes 786432 | tf_op jit(solution)/shard_map/own_conv/pallas_call | solution.py:445
  14.2 0.0 collective-permute-done.left
  14.2 0.0 collective-permute-done.1.right
  14.2 0.0 collective-permute-done.2.rest_1_
  14.2 3.0 %rim_conv.1 = (bf16[4,128,768]{2,1,0:T(8,128)(2,1)}, f32[128,768]{1,0:T(8,128)S(1)}, f32[128,128]{1,0:T(8,128)S(1)}) custom-call(bf16[128,768]{1,0:T(8,128)(2,1)S(1)} %collective-permute-done.left, bf16[128,768]{1,0:T(8,128)(2,1)S(1)} %collective-permute-done.1.right, f32[6,9,7,8,128]{4,3,2,1,0:T(8,128)S(1)} %get-tuple-element.40.split, ...), custom_call_target="tpu_custom_call" | custom-call | flops 33718272 | bytes 786432 | tf_op jit(solution)/shard_map/rim_conv/pallas_call | solution.py:464
  17.2 0.7 copy-done.8
  17.9 0.6 copy-done.10
  18.5 3.7 %all-to-all-start.1 = ((bf16[4,128,768]{2,1,0:T(8,128)(2,1)}), bf16[4,128,768]{2,1,0:T(8,128)(2,1)S(1)}, u32[]{:S(2)}, u32[]{:S(2)}) async-start(bf16[4,128,768]{2,1,0:T(8,128)(2,1)} %get-tuple-element.42.normed), calls=%async_computation.1 | async-start | bytes 1572864 | tf_op jit(solution)/shard_map/all_to_all | solution.py:491
  22.2 1.5 %collective-permute-start.3 = (bf16[128,768]{1,0:T(8,128)(2,1)S(1)}, bf16[128,768]{1,0:T(8,128)(2,1)}, u32[]{:S(2)}, u32[]{:S(2)}) collective-permute-start(bf16[128,768]{1,0:T(8,128)(2,1)S(1)} %collective-permute-done.2.rest_1_), channel_id=1, source_target_pairs={{0,4},{1,5},{2,6},{3,7},{4,8},{5,9},{6,10},{7,11},{8,12},{9,13},{1... | collective-permute-start | bytes 589832 | tf_op jit(solution)/shard_map/ppermute | solution.py:437
  23.7 15.2 %collective-permute-done.3.rest_2_ = bf16[128,768]{1,0:T(8,128)(2,1)} collective-permute-done((bf16[128,768]{1,0:T(8,128)(2,1)S(1)}, bf16[128,768]{1,0:T(8,128)(2,1)}, u32[]{:S(2)}, u32[]{:S(2)}) %collective-permute-start.3) | collective-permute-done | bytes 196640 | tf_op jit(solution)/shard_map/ppermute | solution.py:437
  38.9 4.4 %collective-permute-start.4 = (bf16[128,768]{1,0:T(8,128)(2,1)}, bf16[128,768]{1,0:T(8,128)(2,1)}, u32[]{:S(2)}, u32[]{:S(2)}) collective-permute-start(bf16[128,768]{1,0:T(8,128)(2,1)} %collective-permute-done.3.rest_2_), channel_id=1, source_target_pairs={{0,4},{1,5},{2,6},{3,7},{4,8},{5,9},{6,10},{7,11},{8,12},{9,13},{1... | collective-permute-start | bytes 589832 | tf_op jit(solution)/shard_map/ppermute | solution.py:437
  43.3 1.0 copy-done.9
  44.3 0.8 copy-done.11
  45.2 9.2 %mlp_both_ways.1 = (bf16[128,768]{1,0:T(8,128)(2,1)}, bf16[128,768]{1,0:T(8,128)(2,1)S(1)}, f32[8,768]{1,0:T(8,128)S(1)}) custom-call(bf16[4,128,768]{2,1,0:T(8,128)(2,1)} %get-tuple-element.42.normed, bf16[3072,768]{1,0:T(8,128)(2,1)} %weight_in.5, bf16[3072,768]{1,0:T(8,128)(2,1)} %weight_out.5, f32[128,768]{1,0:T(8,128)S(1)} %copy-done.9, ...), custom_call_target="tpu_custom_call" | custom-call | flops 2415919104 | bytes 9437184 | tf_op jit(solution)/shard_map/mlp_both_ways/pallas_call | solution.py:502
  54.4 7.2 %collective-permute-start.5 = (bf16[128,768]{1,0:T(8,128)(2,1)S(1)}, bf16[128,768]{1,0:T(8,128)(2,1)}, u32[]{:S(2)}, u32[]{:S(2)}) collective-permute-start(bf16[128,768]{1,0:T(8,128)(2,1)S(1)} %get-tuple-element.59.grads.own), channel_id=1, source_target_pairs={{0,1},{1,2},{2,3},{3,4},{4,5},{5,6},{6,7},{7,8},{8,9},{9,10},{10,1... | collective-permute-start | bytes 589832 | tf_op jit(solution)/shard_map/ppermute | solution.py:402
  61.7 1.9 %collective-permute-start.6 = (bf16[128,768]{1,0:T(8,128)(2,1)S(1)}, bf16[128,768]{1,0:T(8,128)(2,1)}, u32[]{:S(2)}, u32[]{:S(2)}) collective-permute-start(bf16[128,768]{1,0:T(8,128)(2,1)S(1)} %get-tuple-element.59.grads.own), channel_id=1, source_target_pairs={{1,0},{2,1},{3,2},{4,3},{5,4},{6,5},{7,6},{8,7},{9,8},{10,9},{11,1... | collective-permute-start | bytes 589832 | tf_op jit(solution)/shard_map/ppermute | solution.py:403
  63.7 0.1 concatenate.3.which
  63.7 0.0 collective-permute-done.4.rest_3_
  63.7 4.8 %kernel_grad_terms.1 = bf16[384,768]{1,0:T(8,128)(2,1)S(1)} custom-call(bf16[128,768]{1,0:T(8,128)(2,1)S(1)} %collective-permute-done.left, bf16[128,768]{1,0:T(8,128)(2,1)S(1)} %bitcast.19, bf16[128,768]{1,0:T(8,128)(2,1)S(1)} %collective-permute-done.1.right, bf16[128,768]{1,0:T(8,128)(2,1)S(1)} %get-tuple-element.59.grads.own, ...), custom_call_target="tpu_custom_call" | custom-call | flops 67436544 | bytes 1572864 | tf_op jit(solution)/shard_map/kernel_grad_terms/pallas_call | solution.py:546
  68.6 0.0 copy-start.2
  68.6 0.8 copy-done.2
  69.4 0.0 collective-permute-done.5.left
  69.4 5.5 %all-to-all-start = ((bf16[16,24,768]{2,1,0:T(8,128)(2,1)}), bf16[16,24,768]{2,1,0:T(8,128)(2,1)S(1)}, u32[]{:S(2)}, u32[]{:S(2)}) async-start(bf16[16,24,768]{2,1,0:T(8,128)(2,1)} %bitcast.14), calls=%async_computation | async-start | bytes 1179648 | tf_op jit(solution)/shard_map/all_to_all | solution.py:620
  74.9 4.9 %weight_grads_other_core.1 = bf16[2,2,192,768]{3,2,1,0:T(8,128)(2,1)} custom-call(s32[8]{0:T(128)S(1)} %concatenate.3.which, bf16[3072,768]{1,0:T(8,128)(2,1)} %weight_in.5, bf16[3072,768]{1,0:T(8,128)(2,1)} %weight_out.5, f32[1,768]{1,0:T(1,128)S(1)} %reshape.44.scale, bf16[4,128,768]{2,1,0:T(8,128)(2,1)S(1)} %all-to-all-done.1.normed, ...), custom_call_target="tpu_custom_call" | custom-call | flops 1207959552 | bytes 2752512 | tf_op jit(solution)/shard_map/weight_grads_other_core/pallas_call | solution.py:604
  79.8 0.1 collective-permute-start.7
  79.9 10.2 %all-to-all-done.parts = bf16[16,24,768]{2,1,0:T(8,128)(2,1)S(1)} async-done(((bf16[16,24,768]{2,1,0:T(8,128)(2,1)}), bf16[16,24,768]{2,1,0:T(8,128)(2,1)S(1)}, u32[]{:S(2)}, u32[]{:S(2)}) %all-to-all-start) | async-done | bytes 589856 | tf_op jit(solution)/shard_map/all_to_all | solution.py:620
  90.0 0.1 kernel_grad_sum.1
  90.1 0.0 copy-start.1
  90.1 0.8 copy-done.1
  90.9 4.8 %all-to-all-start.2 = ((bf16[16,24,768]{2,1,0:T(8,128)(2,1)}), bf16[16,24,768]{2,1,0:T(8,128)(2,1)S(1)}, u32[]{:S(2)}, u32[]{:S(2)}) async-start(bf16[16,24,768]{2,1,0:T(8,128)(2,1)} %copy-done.1), calls=%async_computation.2 | async-start | bytes 1179648 | tf_op jit(solution)/shard_map/all_to_all | solution.py:633
  95.8 0.0 collective-permute-done.7.got
  95.8 5.8 %weight_grads_own_core.1 = (bf16[2,192,768]{2,1,0:T(8,128)(2,1)}, f32[2,192,768]{2,1,0:T(8,128)S(1)}) custom-call(s32[8]{0:T(128)S(1)} %concatenate.3.which, bf16[3072,768]{1,0:T(8,128)(2,1)} %weight_in.5, bf16[3072,768]{1,0:T(8,128)(2,1)} %weight_out.5, f32[1,768]{1,0:T(1,128)S(1)} %reshape.44.scale, bf16[4,128,768]{2,1,0:T(8,128)(2,1)S(1)} %all-to-all-done.1.normed, ...), custom_call_target="tpu_custom_call" | custom-call | flops 1207959552 | bytes 2752512 | tf_op jit(solution)/shard_map/weight_grads_own_core/pallas_call | solution.py:636
  101.6 1.1 copy-done.5
  102.6 1.4 %collective-permute-start.8 = (bf16[2,192,768]{2,1,0:T(8,128)(2,1)}, bf16[2,192,768]{2,1,0:T(8,128)(2,1)}, u32[]{:S(2)}, u32[]{:S(2)}) collective-permute-start(bf16[2,192,768]{2,1,0:T(8,128)(2,1)} %get-tuple-element.58), channel_id=1, source_target_pairs={{0,2},{1,3},{2,0},{3,1},{4,6},{5,7},{6,4},{7,5},{8,10},{9,11},{10,... | collective-permute-start | bytes 1769480 | tf_op jit(solution)/shard_map/ppermute | solution.py:656
  104.0 5.2 %input_grad_conv.1 = bf16[128,768]{1,0:T(8,128)(2,1)} custom-call(bf16[128,768]{1,0:T(8,128)(2,1)} %collective-permute-done.5.left, bf16[128,768]{1,0:T(8,128)(2,1)S(1)} %get-tuple-element.59.grads.own, bf16[128,768]{1,0:T(8,128)(2,1)} %collective-permute-done.6.right, f32[6,9,7,8,128]{4,3,2,1,0:T(8,128)S(1)} %get-tuple-element.40.split, ...), custom_call_target="tpu_custom_call" | custom-call | flops 67436544 | bytes 1572864 | tf_op jit(solution)/shard_map/input_grad_conv/pallas_call | solution.py:659
  109.2 1.7 %all-to-all-done.2.parts = bf16[16,24,768]{2,1,0:T(8,128)(2,1)S(1)} async-done(((bf16[16,24,768]{2,1,0:T(8,128)(2,1)}), bf16[16,24,768]{2,1,0:T(8,128)(2,1)S(1)}, u32[]{:S(2)}, u32[]{:S(2)}) %all-to-all-start.2) | async-done | bytes 589856 | tf_op jit(solution)/shard_map/all_to_all | solution.py:633
  110.9 1.0 kernel_grad_unpack.1
  112.0 0.6 slice_reduce_fusion
  112.6 7.4 %collective-permute-done.8.got = bf16[2,192,768]{2,1,0:T(8,128)(2,1)} collective-permute-done((bf16[2,192,768]{2,1,0:T(8,128)(2,1)}, bf16[2,192,768]{2,1,0:T(8,128)(2,1)}, u32[]{:S(2)}, u32[]{:S(2)}) %collective-permute-start.8) | collective-permute-done | bytes 589856 | tf_op jit(solution)/shard_map/ppermute | solution.py:656
  120.0 1.3 %copy-done.6 = f32[2,192,768]{2,1,0:T(8,128)S(1)} copy-done((f32[2,192,768]{2,1,0:T(8,128)S(1)}, f32[2,192,768]{2,1,0:T(8,128)}, u32[]{:S(2)}) %copy-start.6) | copy-done | bytes 1179672
  121.3 2.2 %weight_grads_sum.1 = (f32[192,768]{1,0:T(8,128)}, f32[192,768]{1,0:T(8,128)}) custom-call(f32[2,192,768]{2,1,0:T(8,128)S(1)} %copy-done.6, bf16[2,192,768]{2,1,0:T(8,128)(2,1)} %collective-permute-done.8.got), custom_call_target="tpu_custom_call" | custom-call | tf_op jit(solution)/shard_map/weight_grads_sum/pallas_call | solution.py:690
  (18 shorter events, 0.0 us)
Async XLA Ops:
  0.6 13.5 %collective-permute-start = (bf16[128,768]{1,0:T(8,128)(2,1)}, bf16[128,768]{1,0:T(8,128)(2,1)S(1)}, u32[]{:S(2)}, u32[]{:S(2)}) collective-permute-start(bf16[128,768]{1,0:T(8,128)(2,1)} %bitcast.15), channel_id=1, source_target_pairs={{0,1},{1,2},{2,3},{3,4},{4,5},{5,6},{6,7},{7,8},{8,9},{9,10},{10,1... | collective-permute-start | bytes 589832 | tf_op jit(solution)/shard_map/ppermute | solution.py:402
  5.2 9.0 %collective-permute-start.1 = (bf16[128,768]{1,0:T(8,128)(2,1)}, bf16[128,768]{1,0:T(8,128)(2,1)S(1)}, u32[]{:S(2)}, u32[]{:S(2)}) collective-permute-start(bf16[128,768]{1,0:T(8,128)(2,1)} %bitcast.16), channel_id=1, source_target_pairs={{1,0},{2,1},{3,2},{4,3},{5,4},{6,5},{7,6},{8,7},{9,8},{10,9},{11,1... | collective-permute-start | bytes 589832 | tf_op jit(solution)/shard_map/ppermute | solution.py:403
  7.1 7.1 %collective-permute-start.2 = (bf16[128,768]{1,0:T(8,128)(2,1)}, bf16[128,768]{1,0:T(8,128)(2,1)S(1)}, u32[]{:S(2)}, u32[]{:S(2)}) collective-permute-start(bf16[128,768]{1,0:T(8,128)(2,1)} %bitcast.9), channel_id=1, source_target_pairs={{0,4},{1,5},{2,6},{3,7},{4,8},{5,9},{6,10},{7,11},{8,12},{9,13},{1... | collective-permute-start | bytes 589832 | tf_op jit(solution)/shard_map/ppermute | solution.py:437
  9.8 0.9 copy-start.3
  10.8 1.2 copy-start.7
  17.2 0.7 copy-start.8
  17.9 0.6 copy-start.10
  18.5 5.2 %copy-start.12 = (f32[768]{0:T(1024)S(1)}, f32[768]{0:T(1024)}, u32[]{:S(2)}) copy-start(f32[768]{0:T(1024)} %param.14) | copy-start | bytes 9220
  18.5 24.8 %copy-start = (bf16[4,4,8,768]{3,2,1,0:T(8,128)(2,1)S(1)}, bf16[4,4,8,768]{3,2,1,0:T(8,128)(2,1)}, u32[]{:S(2)}) copy-start(bf16[4,4,8,768]{3,2,1,0:T(8,128)(2,1)} %param.15) | copy-start | bytes 589828
  18.5 24.8 %copy-start.4 = (bf16[4,4,8,768]{3,2,1,0:T(8,128)(2,1)S(1)}, bf16[4,4,8,768]{3,2,1,0:T(8,128)(2,1)}, u32[]{:S(2)}) copy-start(bf16[4,4,8,768]{3,2,1,0:T(8,128)(2,1)} %param.8) | copy-start | bytes 589828
  18.5 50.9 %all-to-all-start.1 = ((bf16[4,128,768]{2,1,0:T(8,128)(2,1)}), bf16[4,128,768]{2,1,0:T(8,128)(2,1)S(1)}, u32[]{:S(2)}, u32[]{:S(2)}) async-start(bf16[4,128,768]{2,1,0:T(8,128)(2,1)} %get-tuple-element.42.normed), calls=%async_computation.1 | async-start | bytes 1572864 | tf_op jit(solution)/shard_map/all_to_all | solution.py:491
  22.2 16.6 %collective-permute-start.3 = (bf16[128,768]{1,0:T(8,128)(2,1)S(1)}, bf16[128,768]{1,0:T(8,128)(2,1)}, u32[]{:S(2)}, u32[]{:S(2)}) collective-permute-start(bf16[128,768]{1,0:T(8,128)(2,1)S(1)} %collective-permute-done.2.rest_1_), channel_id=1, source_target_pairs={{0,4},{1,5},{2,6},{3,7},{4,8},{5,9},{6,10},{7,11},{8,12},{9,13},{1... | collective-permute-start | bytes 589832 | tf_op jit(solution)/shard_map/ppermute | solution.py:437
  38.9 24.9 %collective-permute-start.4 = (bf16[128,768]{1,0:T(8,128)(2,1)}, bf16[128,768]{1,0:T(8,128)(2,1)}, u32[]{:S(2)}, u32[]{:S(2)}) collective-permute-start(bf16[128,768]{1,0:T(8,128)(2,1)} %collective-permute-done.3.rest_2_), channel_id=1, source_target_pairs={{0,4},{1,5},{2,6},{3,7},{4,8},{5,9},{6,10},{7,11},{8,12},{9,13},{1... | collective-permute-start | bytes 589832 | tf_op jit(solution)/shard_map/ppermute | solution.py:437
  43.3 1.0 copy-start.9
  44.3 0.8 copy-start.11
  54.4 15.0 %collective-permute-start.5 = (bf16[128,768]{1,0:T(8,128)(2,1)S(1)}, bf16[128,768]{1,0:T(8,128)(2,1)}, u32[]{:S(2)}, u32[]{:S(2)}) collective-permute-start(bf16[128,768]{1,0:T(8,128)(2,1)S(1)} %get-tuple-element.59.grads.own), channel_id=1, source_target_pairs={{0,1},{1,2},{2,3},{3,4},{4,5},{5,6},{6,7},{7,8},{8,9},{9,10},{10,1... | collective-permute-start | bytes 589832 | tf_op jit(solution)/shard_map/ppermute | solution.py:402
  61.7 7.8 %collective-permute-start.6 = (bf16[128,768]{1,0:T(8,128)(2,1)S(1)}, bf16[128,768]{1,0:T(8,128)(2,1)}, u32[]{:S(2)}, u32[]{:S(2)}) collective-permute-start(bf16[128,768]{1,0:T(8,128)(2,1)S(1)} %get-tuple-element.59.grads.own), channel_id=1, source_target_pairs={{1,0},{2,1},{3,2},{4,3},{5,4},{6,5},{7,6},{8,7},{9,8},{10,9},{11,1... | collective-permute-start | bytes 589832 | tf_op jit(solution)/shard_map/ppermute | solution.py:403
  68.6 0.8 copy-start.2
  69.4 20.6 %all-to-all-start = ((bf16[16,24,768]{2,1,0:T(8,128)(2,1)}), bf16[16,24,768]{2,1,0:T(8,128)(2,1)S(1)}, u32[]{:S(2)}, u32[]{:S(2)}) async-start(bf16[16,24,768]{2,1,0:T(8,128)(2,1)} %bitcast.14), calls=%async_computation | async-start | bytes 1179648 | tf_op jit(solution)/shard_map/all_to_all | solution.py:620
  79.8 16.0 %collective-permute-start.7 = (bf16[2,2,192,768]{3,2,1,0:T(8,128)(2,1)}, bf16[2,2,192,768]{3,2,1,0:T(8,128)(2,1)}, u32[]{:S(2)}, u32[]{:S(2)}) collective-permute-start(bf16[2,2,192,768]{3,2,1,0:T(8,128)(2,1)} %weight_grads_other_core.1), channel_id=1, source_target_pairs={{0,1},{1,0},{2,3},{3,2},{4,5},{5,4},{6,7},{7,6},{8,9},{9,8},{10,11... | collective-permute-start | bytes 3538952 | tf_op jit(solution)/shard_map/ppermute | solution.py:618
  90.1 0.8 copy-start.1
  90.9 20.0 %all-to-all-start.2 = ((bf16[16,24,768]{2,1,0:T(8,128)(2,1)}), bf16[16,24,768]{2,1,0:T(8,128)(2,1)S(1)}, u32[]{:S(2)}, u32[]{:S(2)}) async-start(bf16[16,24,768]{2,1,0:T(8,128)(2,1)} %copy-done.1), calls=%async_computation.2 | async-start | bytes 1179648 | tf_op jit(solution)/shard_map/all_to_all | solution.py:633
  101.6 1.1 copy-start.5
  102.6 17.4 %collective-permute-start.8 = (bf16[2,192,768]{2,1,0:T(8,128)(2,1)}, bf16[2,192,768]{2,1,0:T(8,128)(2,1)}, u32[]{:S(2)}, u32[]{:S(2)}) collective-permute-start(bf16[2,192,768]{2,1,0:T(8,128)(2,1)} %get-tuple-element.58), channel_id=1, source_target_pairs={{0,2},{1,3},{2,0},{3,1},{4,6},{5,7},{6,4},{7,5},{8,10},{9,11},{10,... | collective-permute-start | bytes 1769480 | tf_op jit(solution)/shard_map/ppermute | solution.py:656
  120.0 1.3 %copy-start.6 = (f32[2,192,768]{2,1,0:T(8,128)S(1)}, f32[2,192,768]{2,1,0:T(8,128)}, u32[]{:S(2)}) copy-start(f32[2,192,768]{2,1,0:T(8,128)} %copy-done.5) | copy-start | bytes 3538948

commit v5 on v4

--- a/solution.py
+++ b/solution.py
@@ -98,6 +98,16 @@
 def all_planes(left, own, right, planes):
     rim = rim_planes(left, right, planes)
     return rim[:MARGIN] + [(own, x) for x in range(planes)] + rim[MARGIN:]
+
+
+def by_core(core, inner, outer, stage):
+    @pl.when(core[0] == 0)
+    def _():
+        stage(outer, inner)
+
+    @pl.when(core[0] != 0)
+    def _():
+        stage(inner, outer)
 
 
 def clear_rims(spread):
@@ -160,7 +170,7 @@
 
 
 def rim_conv_kernel(
-    planes, height, left, right, split, partial, gain, bias, normed, unit, inv, spread, conv
+    planes, height, core, inner, outer, split, partial, vectors, normed, unit, inv, spread, conv
 ):
     step = pl.program_id(0)
 
@@ -168,7 +178,10 @@
     def _():
         clear_rims(spread)
 
-    stage_source(rim_planes(left, right, planes), height, spread)
+    def stage(left, right):
+        stage_source(rim_planes(left, right, planes), height, spread)
+
+    by_core(core, inner, outer, stage)
     held = list(range(MARGIN)) + list(range(MARGIN + planes, 2 * MARGIN + planes))
     rows = convolve(spread, split, planes, held, False)
     for x in range(planes):
@@ -192,17 +205,20 @@
             lanes = slice(k * LANES, (k + 1) * LANES)
             value = parts[k] * inverse
             unit[:, lanes] = value
-            whole = (value * gain[:, lanes] + bias[:, lanes]).astype(BF16)
+            whole = (value * vectors[0:1, lanes] + vectors[1:2, lanes]).astype(BF16)
             for copy in range(normed.shape[0]):
                 normed[copy, :, lanes] = whole
 
 
-def input_grad_kernel(planes, height, left, own, right, split, cotangent, out, spread):
+def input_grad_kernel(planes, height, core, inner, own, outer, split, cotangent, out, spread):
     @pl.when(pl.program_id(0) == 0)
     def _():
         clear_rims(spread)
 
-    stage_source(all_planes(left, own, right, planes), height, spread)
+    def stage(left, right):
+        stage_source(all_planes(left, own, right, planes), height, spread)
+
+    by_core(core, inner, outer, stage)
     rows = convolve(spread, split, planes, range(2 * MARGIN + planes), True)
     for x in range(planes):
         at = x * height * SUB
@@ -212,7 +228,7 @@
 
 
 def kernel_grad_kernel(
-    planes, height, left, own, right, grads, small, out, spread, products, joined, flat
+    planes, height, core, inner, own, outer, grads, small, out, spread, products, joined, flat
 ):
     @pl.when(pl.program_id(0) == 0)
     def _():
@@ -220,7 +236,10 @@
         products[...] = jnp.zeros(products.shape, F32)
         flat[...] = jnp.zeros(flat.shape, F32)
 
-    stage_source(all_planes(left, own, right, planes), height, spread)
+    def stage(left, right):
+        stage_source(all_planes(left, own, right, planes), height, spread)
+
+    by_core(core, inner, outer, stage)
     upstream = []
     for x in range(planes):
         plane = grads[x * height * SUB : (x + 1) * height * SUB, :].astype(F32)
@@ -255,8 +274,7 @@
     weight_out,
     unit,
     inv,
-    gain,
-    scale,
+    vectors,
     voxels,
     cotangent,
     block_out,
@@ -267,10 +285,12 @@
     mixed_grad,
 ):
     step = pl.program_id(0)
+    gain = vectors[0:1, :]
+    scale = vectors[2:3, :]
 
     @pl.when(step == 0)
     def _():
-        mixed_grad[...] = (scale[...] * cotangent[...].astype(F32)).astype(BF16)
+        mixed_grad[...] = (scale * cotangent[...].astype(F32)).astype(BF16)
 
     hidden = lax.dot_general(
         normed[...], weight_in[...], (((1,), (1,)), ((), ())), preferred_element_type=F32
@@ -296,7 +316,7 @@
     def _():
         channels = gain.shape[1]
         whole = mixed[...]
-        block_out[...] = (voxels[...].astype(F32) + scale[...] * whole).astype(BF16)
+        block_out[...] = (voxels[...].astype(F32) + scale * whole).astype(BF16)
         scale_local = jnp.sum(cotangent[...].astype(F32) * whole, axis=0, keepdims=True)
         grad = back[...]
         one = unit[...]
@@ -305,7 +325,7 @@
         small[...] = jnp.concatenate(
             [gain_local, bias_local, scale_local, jnp.zeros((SUB - 3, channels), F32)], axis=0
         )
-        scaled = grad * gain[...]
+        scaled = grad * gain
         average = jnp.sum(scaled, axis=1, keepdims=True) * (1.0 / channels)
         slant = jnp.sum(scaled * one, axis=1, keepdims=True) * (1.0 / channels)
         conv_grad[...] = (inv[:, :1] * (scaled - average - one * slant)).astype(BF16)
@@ -318,11 +338,11 @@
     return activated, (act_grad * slope).astype(BF16)
 
 
-def weight_grad_terms(which, weight_in, weight_out, scale, normed, cotangents, aligned):
+def weight_grad_terms(which, weight_in, weight_out, vectors, normed, cotangents, aligned):
     rows = normed.shape[1]
     line = len(cotangents)
     mixed_grad = jnp.concatenate(
-        [(scale[...] * part[...].astype(F32)).astype(BF16) for part in cotangents], axis=0
+        [(vectors[2:3, :] * part[...].astype(F32)).astype(BF16) for part in cotangents], axis=0
     )
     for k in range(line):
         aligned[k * rows : (k + 1) * rows, :] = normed[which[4 + k]]
@@ -336,16 +356,16 @@
     )
 
 
-def other_core_terms_kernel(which, weight_in, weight_out, scale, normed, *rest):
+def other_core_terms_kernel(which, weight_in, weight_out, vectors, normed, *rest):
     *cotangents, out, aligned = rest
-    terms = weight_grad_terms(which, weight_in, weight_out, scale, normed, cotangents, aligned)
+    terms = weight_grad_terms(which, weight_in, weight_out, vectors, normed, cotangents, aligned)
     for k in range(2):
         out[0, k] = terms[k].astype(BF16)
 
 
-def own_core_terms_kernel(which, weight_in, weight_out, scale, normed, got, *rest):
+def own_core_terms_kernel(which, weight_in, weight_out, vectors, normed, got, *rest):
     *cotangents, sent, kept, aligned = rest
-    terms = weight_grad_terms(which, weight_in, weight_out, scale, normed, cotangents, aligned)
+    terms = weight_grad_terms(which, weight_in, weight_out, vectors, normed, cotangents, aligned)
     step = pl.program_id(0)
     for k in range(2):
         total = terms[k] + got[0, k].astype(F32)
@@ -384,23 +404,24 @@
     small[...] = rows[first : first + SUB, :]
 
 
-def params(limit=48):
+def params(limit=24):
     return pltpu.CompilerParams(vmem_limit_bytes=limit * 1024 * 1024)
 
 
 def lane_block(rows):
-    return pl.BlockSpec((rows, LANES), lambda c: (0, c))
+    return pl.BlockSpec((rows, LANES), lambda c, *_: (0, c))
 
 
 def whole_block(*shape):
     return pl.BlockSpec(shape, lambda *_: (0,) * len(shape))
 
 
-def neighbours(cells):
-    ends = lax.axis_size("row") - 1
+def rims(cells):
+    count = lax.axis_size("row")
+    between = [(i, i + 1) for i in range(1, count - 1, 2)]
     return (
-        lax.ppermute(cells, "row", [(i, i + 1) for i in range(ends)]),
-        lax.ppermute(cells, "row", [(i + 1, i) for i in range(ends)]),
+        lax.ppermute(cells, "row", [(i, i ^ 1) for i in range(count)]),
+        lax.ppermute(cells, "row", between + [(j, i) for i, j in between]),
     )
 
 
@@ -427,11 +448,11 @@
 
     own = voxels.reshape(rows, channels)
     upstream = cotangent.reshape(rows, channels)
-    gain = norm_gain.reshape(1, channels)
-    bias = norm_bias.reshape(1, channels)
-    scale = layer_scale.reshape(1, channels)
+    vectors = jnp.stack([norm_gain, norm_bias, layer_scale])
     core = lax.rem(me, 2).astype(jnp.int32)
-    left, right = neighbours(own)
+    parity = core.reshape(1)
+
+    inner, outer = rims(own)
 
     def next_in_line(cells):
         return lax.ppermute(cells, "row", [(i, (i + quad) % count) for i in range(count)])
@@ -441,7 +462,9 @@
     def spread_of(held):
         return pltpu.VMEM((9, held, PAD, LANES), F32)
 
-    split_block = pl.BlockSpec((None, 9, KS, SUB, LANES), lambda c: (c, 0, 0, 0, 0))
+    split_block = pl.BlockSpec((None, 9, KS, SUB, LANES), lambda c, *_: (c, 0, 0, 0, 0))
+    own, upstream_line[-1] = lax.optimization_barrier((own, upstream_line[-1]))
+    upstream_line.append(next_in_line(upstream_line[-1]))
     partial, split = pl.pallas_call(
         functools.partial(own_conv_kernel, planes, height),
         grid=(tiles,),
@@ -457,48 +480,45 @@
         name="own_conv",
     )(own, dw_kernel)
 
-    left, right, partial, upstream_line[-1] = lax.optimization_barrier(
-        (left, right, partial, upstream_line[-1])
-    )
-    upstream_line.append(next_in_line(upstream_line[-1]))
+    partial, upstream_line[-1] = lax.optimization_barrier((partial, upstream_line[-1]))
+    for _ in range(3, line):
+        upstream_line.append(next_in_line(upstream_line[-1]))
     normed, unit, inv = pl.pallas_call(
         functools.partial(rim_conv_kernel, planes, height),
-        grid=(tiles,),
-        in_specs=[
-            lane_block(rows),
-            lane_block(rows),
-            split_block,
-            lane_block(rows),
-            whole_block(1, channels),
-            whole_block(1, channels),
-        ],
-        out_specs=[
-            whole_block(line, rows, channels),
-            whole_block(rows, channels),
-            whole_block(rows, LANES),
-        ],
+        grid_spec=pltpu.PrefetchScalarGridSpec(
+            num_scalar_prefetch=1,
+            grid=(tiles,),
+            in_specs=[
+                lane_block(rows),
+                lane_block(rows),
+                split_block,
+                lane_block(rows),
+                whole_block(3, channels),
+            ],
+            out_specs=[
+                whole_block(line, rows, channels),
+                whole_block(rows, channels),
+                whole_block(rows, LANES),
+            ],
+            scratch_shapes=[spread_of(2 * MARGIN), pltpu.VMEM((tiles, rows, LANES), F32)],
+        ),
         out_shape=[
             jax.ShapeDtypeStruct((line, rows, channels), BF16),
             jax.ShapeDtypeStruct((rows, channels), F32),
             jax.ShapeDtypeStruct((rows, LANES), F32),
         ],
-        scratch_shapes=[spread_of(2 * MARGIN), pltpu.VMEM((tiles, rows, LANES), F32)],
         compiler_params=params(),
         cost_estimate=conv_cost(rows, channels // 2),
         name="rim_conv",
-    )(left, right, split, partial, gain, bias)
-
+    )(parity, inner, outer, split, partial, vectors)
+
+    copies_out, upstream_line[-1] = lax.optimization_barrier((normed, upstream_line[-1]))
     gathered = lax.all_to_all(
-        normed, "row", split_axis=0, concat_axis=0, tiled=True, axis_index_groups=lines
-    )
-
-    unit, upstream_line[-1] = lax.optimization_barrier((unit, upstream_line[-1]))
-    for _ in range(3, line):
-        upstream_line.append(next_in_line(upstream_line[-1]))
+        copies_out, "row", split_axis=0, concat_axis=0, tiled=True, axis_index_groups=lines
+    )
 
     block = 512
     whole = whole_block(rows, channels)
-    vector = whole_block(1, channels)
     block_out, conv_grad, small = pl.pallas_call(
         mlp_kernel,
         grid=(units // block,),
@@ -508,8 +528,7 @@
             pl.BlockSpec((block, channels), lambda f: (f, 0)),
             whole,
             whole_block(rows, LANES),
-            vector,
-            vector,
+            whole_block(3, channels),
             whole,
             whole,
         ],
@@ -535,36 +554,42 @@
             transcendentals=2 * rows * units,
         ),
         name="mlp_both_ways",
-    )(normed, weight_in, weight_out, unit, inv, gain, scale, own, upstream)
-
-    grad_left, grad_right = neighbours(conv_grad)
-
-    small, upstream_line[-1] = lax.optimization_barrier((small, upstream_line[-1]))
+    )(normed, weight_in, weight_out, unit, inv, vectors, own, upstream)
+
     piece = -(-(TAP_ROWS + SUB) // count)
     piece += -piece % SUB
     padded = piece * count
     sums = pl.pallas_call(
         functools.partial(kernel_grad_kernel, planes, height),
-        grid=(tiles,),
-        in_specs=[
-            lane_block(rows),
-            lane_block(rows),
-            lane_block(rows),
-            lane_block(rows),
-            lane_block(SUB),
-        ],
-        out_specs=lane_block(padded),
+        grid_spec=pltpu.PrefetchScalarGridSpec(
+            num_scalar_prefetch=1,
+            grid=(tiles,),
+            in_specs=[
+                lane_block(rows),
+                lane_block(rows),
+                lane_block(rows),
+                lane_block(rows),
+                lane_block(SUB),
+            ],
+            out_specs=lane_block(padded),
+            scratch_shapes=[
+                spread_of(2 * MARGIN + planes),
+                pltpu.VMEM((2, KS, SUB * SUB, LANES), F32),
+                pltpu.VMEM((9, KS, SUB, LANES), F32),
+                pltpu.VMEM((padded, LANES), F32),
+            ],
+        ),
         out_shape=jax.ShapeDtypeStruct((padded, channels), BF16),
-        scratch_shapes=[
-            spread_of(2 * MARGIN + planes),
-            pltpu.VMEM((2, KS, SUB * SUB, LANES), F32),
-            pltpu.VMEM((9, KS, SUB, LANES), F32),
-            pltpu.VMEM((padded, LANES), F32),
-        ],
         compiler_params=params(),
         cost_estimate=conv_cost(rows, channels),
         name="kernel_grad_terms",
-    )(left, own, right, conv_grad, small)
+    )(parity, inner, own, outer, conv_grad, small)
+    scattered = lax.all_to_all(
+        sums.reshape(count, piece, channels), "row", split_axis=0, concat_axis=0, tiled=True
+    )
+
+    conv_grad, sums = lax.optimization_barrier((conv_grad, sums))
+    grad_inner, grad_outer = rims(conv_grad)
 
     share = units // count
     tokens = line * rows
@@ -594,13 +619,11 @@
     def chunk(at):
         return pl.BlockSpec((share, channels), lambda s, w: (w[s + at], 0))
 
-    sets = [whole_block(1, channels), whole_block(line, rows, channels)]
+    sets = [whole_block(3, channels), whole_block(line, rows, channels)]
     cotangents = [whole_block(rows, channels)] * line
     aligned = [pltpu.VMEM((tokens, channels), BF16)]
 
-    which, sums, grad_left, grad_right = lax.optimization_barrier(
-        (which, sums, grad_left, grad_right)
-    )
+    which, sums = lax.optimization_barrier((which, sums))
     for_other = pl.pallas_call(
         other_core_terms_kernel,
         grid_spec=pltpu.PrefetchScalarGridSpec(
@@ -614,25 +637,9 @@
         compiler_params=params(),
         cost_estimate=terms_cost,
         name="weight_grads_other_core",
-    )(which, weight_in, weight_out, scale, gathered, *upstream_line)
+    )(which, weight_in, weight_out, vectors, gathered, *upstream_line)
     from_other = lax.ppermute(for_other, "row", other_core)
 
-    scattered = lax.all_to_all(
-        sums.reshape(count, piece, channels), "row", split_axis=0, concat_axis=0, tiled=True
-    )
-    scattered, for_other = lax.optimization_barrier((scattered, for_other))
-    copies = pl.pallas_call(
-        spread_sum_kernel,
-        in_specs=[whole_block(count, piece, channels)],
-        out_specs=whole_block(count, piece, channels),
-        out_shape=jax.ShapeDtypeStruct((count, piece, channels), BF16),
-        grid=(1,),
-        compiler_params=params(),
-        name="kernel_grad_sum",
-    )(scattered)
-    totals = lax.all_to_all(copies, "row", split_axis=0, concat_axis=0, tiled=True)
-
-    which, copies = lax.optimization_barrier((which, copies))
     sent, kept = pl.pallas_call(
         own_core_terms_kernel,
         grid_spec=pltpu.PrefetchScalarGridSpec(
@@ -652,29 +659,44 @@
         compiler_params=params(),
         cost_estimate=terms_cost,
         name="weight_grads_own_core",
-    )(which, weight_in, weight_out, scale, gathered, from_other, *upstream_line)
+    )(which, weight_in, weight_out, vectors, gathered, from_other, *upstream_line)
     got = lax.ppermute(sent, "row", other_side)
 
-    conv_own, sent = lax.optimization_barrier((conv_grad, sent))
+    scattered, sent = lax.optimization_barrier((scattered, sent))
+    copies = pl.pallas_call(
+        spread_sum_kernel,
+        in_specs=[whole_block(count, piece, channels)],
+        out_specs=whole_block(count, piece, channels),
+        out_shape=jax.ShapeDtypeStruct((count, piece, channels), BF16),
+        grid=(1,),
+        compiler_params=params(),
+        name="kernel_grad_sum",
+    )(scattered)
+    totals = lax.all_to_all(copies, "row", split_axis=0, concat_axis=0, tiled=True)
+
+    conv_own, copies = lax.optimization_barrier((conv_grad, copies))
     voxel_grad = pl.pallas_call(
         functools.partial(input_grad_kernel, planes, height),
-        grid=(tiles,),
-        in_specs=[
-            lane_block(rows),
-            lane_block(rows),
-            lane_block(rows),
-            split_block,
-            lane_block(rows),
-        ],
-        out_specs=lane_block(rows),
+        grid_spec=pltpu.PrefetchScalarGridSpec(
+            num_scalar_prefetch=1,
+            grid=(tiles,),
+            in_specs=[
+                lane_block(rows),
+                lane_block(rows),
+                lane_block(rows),
+                split_block,
+                lane_block(rows),
+            ],
+            out_specs=lane_block(rows),
+            scratch_shapes=[spread_of(2 * MARGIN + planes)],
+        ),
         out_shape=jax.ShapeDtypeStruct((rows, channels), BF16),
-        scratch_shapes=[spread_of(2 * MARGIN + planes)],
         compiler_params=params(),
         cost_estimate=conv_cost(rows, channels),
         name="input_grad_conv",
-    )(grad_left, conv_own, grad_right, split, upstream)
-
-    kernel_grad, vectors = pl.pallas_call(
+    )(parity, grad_inner, conv_own, grad_outer, split, upstream)
+
+    kernel_grad, vector_grads = pl.pallas_call(
         unpack_kernel,
         grid=(1,),
         in_specs=[whole_block(count, piece, channels)],
@@ -701,9 +723,9 @@
         block_out.reshape(voxels.shape),
         voxel_grad.reshape(voxels.shape),
         kernel_grad,
-        vectors[0],
-        vectors[1],
-        vectors[2],
+        vector_grads[0],
+        vector_grads[1],
+        vector_grads[2],
         weight_in_grad,
         weight_out_grad,
     )

time: 125 us -> 132 us (1.056)
  waiting for transfers between devices: 34.5 us -> 50.5 us
  starting transfers between devices: 38.4 us -> 24.7 us
  local copies, waits for them, and re-layouts: 11.4 us -> 17.3 us
  Pallas kernels: 38.4 us -> 36.7 us
    ppermute x4, waiting for transfers between devices: 0.01 us -> 19.9 us  [the longest x2 19.9 us: rims(): lax.ppermute(cells, 'row', between + [(j, i) for i, j in between])]
    all_to_all x1, waiting for transfers between devices: 0.01 us -> 19.4 us  [on_device(): lax.all_to_all(copies_out, 'row', split_axis=0, concat_axis=0, tiled=True...]
    ppermute x4, starting transfers between devices: 15.6 us -> 6.81 us  [the longest x2 4.94 us: rims(): lax.ppermute(cells, 'row', between + [(j, i) for i, j in between])]
    all_to_all x1, waiting for transfers between devices: 10.2 us -> 2.15 us  [on_device(): lax.all_to_all(sums.reshape(count, piece, channels), 'row', split_axis=0,...]
    ppermute x1, waiting for transfers between devices: 7.42 us -> 0.01 us  [on_device(): got = lax.ppermute(sent, 'row', other_side)]
    unnamed x26 -> x46, local copies, waits for them, and re-layouts: 9.31 us -> 16.6 us
    ppermute x3, waiting for transfers between devices: 15.2 us -> 9.06 us  [next_in_line(): lax.ppermute(cells, 'row', [(i, (i + quad) % count) for i in range(count)])]
    ppermute x3, starting transfers between devices: 7.25 us -> 3.24 us  [next_in_line(): lax.ppermute(cells, 'row', [(i, (i + quad) % count) for i in range(count)])]
  transfers between devices with their start and end apart: 12 -> 12, of which waited for: 4 -> 5; matrix products, arithmetic and copies ran while one was open for 2% -> 0% of each run, Pallas kernels for 27% -> 24%
where the time goes in v5:
time: 132 us; the launch traced here: 130 us
  waiting for transfers between devices  50.5 us (38%)
  Pallas kernels  36.7 us (28%)
  starting transfers between devices  24.7 us (19%)
  local copies, waits for them, and re-layouts  17.3 us (13%)
    ppermute x2, waiting for transfers between devices, rims(): lax.ppermute(cells, 'row', between + [(j, i) for i, j in between])  19.9 us
    all_to_all x1, waiting for transfers between devices, on_device(): lax.all_to_all(copies_out, 'row', split_axis=0, concat_axis=0, tiled=True...  19.4 us
    unnamed x46, local copies, waits for them, and re-layouts  16.6 us
    ppermute x3, waiting for transfers between devices, next_in_line(): lax.ppermute(cells, 'row', [(i, (i + quad) % count) for i in range(count)])  9.06 us
    pallas_call x1, Pallas kernels, on_device(): pl.pallas_call(mlp_kernel, grid=(units // block,), in_specs=[pl.BlockSpec...  7.9 us
    pallas_call x1, Pallas kernels, on_device(): pl.pallas_call(functools.partial(input_grad_kernel, planes, height), grid...  6.24 us
    pallas_call x1, Pallas kernels, on_device(): pl.pallas_call(functools.partial(kernel_grad_kernel, planes, height), gri...  5.46 us
    ppermute x2, starting transfers between devices, rims(): lax.ppermute(cells, 'row', between + [(j, i) for i, j in between])  4.94 us
  transfers between devices with their start and end apart: 12, of which 5 were waited for; matrix products, arithmetic and copies ran while one was open for 0% of the time, Pallas kernels for 24%

profile of v5, /device:TPU:1, one launch (start us, length us, event | category | flops | bytes accessed | tf_op | source)
XLA Modules:
  0.0 130.2 jit_solution(7003006380552619249)
XLA Ops:
  0.6 2.2 %collective-permute-start.2 = (bf16[128,768]{1,0:T(8,128)(2,1)}, bf16[128,768]{1,0:T(8,128)(2,1)S(1)}, u32[]{:S(2)}, u32[]{:S(2)}) collective-permute-start(bf16[128,768]{1,0:T(8,128)(2,1)} %bitcast.10), channel_id=1, source_target_pairs={{0,4},{1,5},{2,6},{3,7},{4,8},{5,9},{6,10},{7,11},{8,12},{9,13},{1... | collective-permute-start | bytes 589832 | tf_op jit(solution)/shard_map/ppermute | solution.py:458
  2.8 6.9 %collective-permute-done.2.rest_1_ = bf16[128,768]{1,0:T(8,128)(2,1)S(1)} collective-permute-done((bf16[128,768]{1,0:T(8,128)(2,1)}, bf16[128,768]{1,0:T(8,128)(2,1)S(1)}, u32[]{:S(2)}, u32[]{:S(2)}) %collective-permute-start.2) | collective-permute-done | bytes 196640 | tf_op jit(solution)/shard_map/ppermute | solution.py:458
  9.7 1.2 collective-permute-start
  10.9 3.0 %collective-permute-start.1 = (bf16[128,768]{1,0:T(8,128)(2,1)}, bf16[128,768]{1,0:T(8,128)(2,1)S(1)}, u32[]{:S(2)}, u32[]{:S(2)}) collective-permute-start(bf16[128,768]{1,0:T(8,128)(2,1)} %bitcast.16), channel_id=1, source_target_pairs={{1,2},{3,4},{5,6},{7,8},{9,10},{11,12},{13,14},{2,1},{4,3},{6,5},{... | collective-permute-start | bytes 589832 | tf_op jit(solution)/shard_map/ppermute | solution.py:424
  13.9 0.0 copy-start.6
  14.0 0.9 copy-done.6
  14.9 1.2 copy-done.10
  16.1 2.1 %own_conv.1 = (f32[128,768]{1,0:T(8,128)S(1)}, f32[6,9,7,8,128]{4,3,2,1,0:T(8,128)S(1)}) custom-call(bf16[128,768]{1,0:T(8,128)(2,1)S(1)} %bitcast.17, f32[343,768]{1,0:T(8,128)S(1)} %copy-done.10), custom_call_target="tpu_custom_call" | custom-call | flops 33718272 | bytes 786432 | tf_op jit(solution)/shard_map/own_conv/pallas_call | solution.py:468
  18.3 0.0 collective-permute-done.3.rest_2_
  18.3 0.0 copy-start.11
  18.3 1.1 collective-permute-start.5
  19.4 0.0 collective-permute-done.inner
  19.4 0.0 collective-permute-done.1.outer
  19.4 3.7 %rim_conv.1 = (bf16[4,128,768]{2,1,0:T(8,128)(2,1)}, f32[128,768]{1,0:T(8,128)S(1)}, f32[128,128]{1,0:T(8,128)S(1)}) custom-call(s32[1]{0:T(128)} %bitcast.core, bf16[128,768]{1,0:T(8,128)(2,1)S(1)} %collective-permute-done.inner, bf16[128,768]{1,0:T(8,128)(2,1)S(1)} %collective-permute-done.1.outer, f32[6,9,7,8,128]{4,3,2,1,0:T(8,128)S(1)} %get-tuple-element.32.split, ...), custom_call_target="tpu_custom_call" | custom-call | flops 33718272 | bytes 786432 | tf_op jit(solution)/shard_map/rim_conv/pallas_call | solution.py:486
  23.1 0.7 copy-done.15
  23.9 0.6 copy-done.17
  24.5 2.2 %collective-permute-done.5.rest_3_ = bf16[128,768]{1,0:T(8,128)(2,1)S(1)} collective-permute-done((bf16[128,768]{1,0:T(8,128)(2,1)S(1)}, bf16[128,768]{1,0:T(8,128)(2,1)S(1)}, u32[]{:S(2)}, u32[]{:S(2)}) %collective-permute-start.5) | collective-permute-done | bytes 196640 | tf_op jit(solution)/shard_map/ppermute | solution.py:458
  26.7 3.5 %all-to-all-start.1 = ((bf16[4,128,768]{2,1,0:T(8,128)(2,1)}), bf16[4,128,768]{2,1,0:T(8,128)(2,1)S(1)}, u32[]{:S(2)}, u32[]{:S(2)}) async-start(bf16[4,128,768]{2,1,0:T(8,128)(2,1)} %get-tuple-element.44.normed), calls=%async_computation.1 | async-start | bytes 1572864 | tf_op jit(solution)/shard_map/all_to_all | solution.py:516
  30.2 0.1 concatenate.3.which
  30.3 19.4 %all-to-all-done.1.normed = bf16[4,128,768]{2,1,0:T(8,128)(2,1)S(1)} async-done(((bf16[4,128,768]{2,1,0:T(8,128)(2,1)}), bf16[4,128,768]{2,1,0:T(8,128)(2,1)S(1)}, u32[]{:S(2)}, u32[]{:S(2)}) %all-to-all-start.1) | async-done | bytes 786464 | tf_op jit(solution)/shard_map/all_to_all | solution.py:516
  49.8 2.3 %copy-done = bf16[3072,768]{1,0:T(8,128)(2,1)S(1)} copy-done((bf16[3072,768]{1,0:T(8,128)(2,1)S(1)}, bf16[3072,768]{1,0:T(8,128)(2,1)}, u32[]{:S(2)}) %copy-start) | copy-done | bytes 4718616
  52.1 2.3 %copy-done.3 = bf16[3072,768]{1,0:T(8,128)(2,1)S(1)} copy-done((bf16[3072,768]{1,0:T(8,128)(2,1)S(1)}, bf16[3072,768]{1,0:T(8,128)(2,1)}, u32[]{:S(2)}) %copy-start.3) | copy-done | bytes 4718616
  54.5 3.6 %weight_grads_other_core.1 = bf16[2,2,192,768]{3,2,1,0:T(8,128)(2,1)} custom-call(s32[8]{0:T(128)S(1)} %concatenate.3.which, bf16[3072,768]{1,0:T(8,128)(2,1)S(1)} %copy-done, bf16[3072,768]{1,0:T(8,128)(2,1)S(1)} %copy-done.3, f32[3,768]{1,0:T(4,128)S(1)} %pad_maximum_fusion.vectors, bf16[4,128,768]{2,1,0:T(8,128)(2,1)S(1)} %all-to-all-done.1.normed, ...), custom_call_target="tpu_custom_call" | custom-call | flops 1207959552 | bytes 2752512 | tf_op jit(solution)/shard_map/weight_grads_other_core/pallas_call | solution.py:627
  58.1 1.5 %collective-permute-start.6 = (bf16[2,2,192,768]{3,2,1,0:T(8,128)(2,1)}, bf16[2,2,192,768]{3,2,1,0:T(8,128)(2,1)}, u32[]{:S(2)}, u32[]{:S(2)}) collective-permute-start(bf16[2,2,192,768]{3,2,1,0:T(8,128)(2,1)} %weight_grads_other_core.1), channel_id=1, source_target_pairs={{0,1},{1,0},{2,3},{3,2},{4,5},{5,4},{6,7},{7,6},{8,9},{9,8},{10,11... | collective-permute-start | bytes 3538952 | tf_op jit(solution)/shard_map/ppermute | solution.py:641
  59.6 7.9 %mlp_both_ways.1 = (bf16[128,768]{1,0:T(8,128)(2,1)}, bf16[128,768]{1,0:T(8,128)(2,1)S(1)}, f32[8,768]{1,0:T(8,128)S(1)}) custom-call(bf16[4,128,768]{2,1,0:T(8,128)(2,1)} %get-tuple-element.44.normed, bf16[3072,768]{1,0:T(8,128)(2,1)S(1)} %copy-done.1, bf16[3072,768]{1,0:T(8,128)(2,1)S(1)} %copy-done.3, f32[128,768]{1,0:T(8,128)S(1)} %copy-done.16, ...), custom_call_target="tpu_custom_call" | custom-call | flops 2415919104 | bytes 9437184 | tf_op jit(solution)/shard_map/mlp_both_ways/pallas_call | solution.py:522
  67.5 5.5 %kernel_grad_terms.1 = bf16[384,768]{1,0:T(8,128)(2,1)} custom-call(s32[1]{0:T(128)} %bitcast.core, bf16[128,768]{1,0:T(8,128)(2,1)S(1)} %collective-permute-done.inner, bf16[128,768]{1,0:T(8,128)(2,1)S(1)} %bitcast.19, bf16[128,768]{1,0:T(8,128)(2,1)S(1)} %collective-permute-done.1.outer, bf16[128,768]{1,0:T(8,128)(2,1)S(1)} %get-tuple-element.48.grads.own, ...), custom_call_target="tpu_custom_call" | custom-call | flops 67436544 | bytes 1572864 | tf_op jit(solution)/shard_map/kernel_grad_terms/pallas_call | solution.py:562
  72.9 3.5 %all-to-all-start = ((bf16[16,24,768]{2,1,0:T(8,128)(2,1)}), bf16[16,24,768]{2,1,0:T(8,128)(2,1)S(1)}, u32[]{:S(2)}, u32[]{:S(2)}) async-start(bf16[16,24,768]{2,1,0:T(8,128)(2,1)} %bitcast.4), calls=%async_computation | async-start | bytes 1179648 | tf_op jit(solution)/shard_map/all_to_all | solution.py:587
  76.4 0.0 collective-permute-done.6.got
  76.4 0.0 copy-start.2
  76.5 2.3 %copy-done.2 = bf16[3072,768]{1,0:T(8,128)(2,1)S(1)} copy-done((bf16[3072,768]{1,0:T(8,128)(2,1)S(1)}, bf16[3072,768]{1,0:T(8,128)(2,1)}, u32[]{:S(2)}) %copy-start.2) | copy-done | bytes 4718616
  78.8 2.3 %copy-done.4 = bf16[3072,768]{1,0:T(8,128)(2,1)S(1)} copy-done((bf16[3072,768]{1,0:T(8,128)(2,1)S(1)}, bf16[3072,768]{1,0:T(8,128)(2,1)}, u32[]{:S(2)}) %copy-start.4) | copy-done | bytes 4718616
  81.1 0.9 copy-done.12
  82.1 0.9 copy-done.14
  83.0 4.6 %weight_grads_own_core.1 = (bf16[2,192,768]{2,1,0:T(8,128)(2,1)S(1)}, f32[2,192,768]{2,1,0:T(8,128)S(1)}) custom-call(s32[8]{0:T(128)S(1)} %concatenate.3.which, bf16[3072,768]{1,0:T(8,128)(2,1)S(1)} %copy-done.2, bf16[3072,768]{1,0:T(8,128)(2,1)S(1)} %copy-done.4, f32[3,768]{1,0:T(4,128)S(1)} %pad_maximum_fusion.vectors, ...), custom_call_target="tpu_custom_call" | custom-call | flops 1207959552 | bytes 2752512 | tf_op jit(solution)/shard_map/weight_grads_own_core/pallas_call | solution.py:643
  87.6 1.0 copy-done.8
  88.6 0.8 copy-done.19
  89.4 2.2 %all-to-all-done.parts = bf16[16,24,768]{2,1,0:T(8,128)(2,1)S(1)} async-done(((bf16[16,24,768]{2,1,0:T(8,128)(2,1)}), bf16[16,24,768]{2,1,0:T(8,128)(2,1)S(1)}, u32[]{:S(2)}, u32[]{:S(2)}) %all-to-all-start) | async-done | bytes 589856 | tf_op jit(solution)/shard_map/all_to_all | solution.py:587
  91.6 0.9 kernel_grad_sum.1
  92.5 4.8 %all-to-all-start.2 = ((bf16[16,24,768]{2,1,0:T(8,128)(2,1)}), bf16[16,24,768]{2,1,0:T(8,128)(2,1)S(1)}, u32[]{:S(2)}, u32[]{:S(2)}) async-start(bf16[16,24,768]{2,1,0:T(8,128)(2,1)} %kernel_grad_sum.1), calls=%async_computation.2 | async-start | bytes 1179648 | tf_op jit(solution)/shard_map/all_to_all | solution.py:675
  97.2 1.5 %collective-permute-start.8 = (bf16[2,192,768]{2,1,0:T(8,128)(2,1)}, bf16[2,192,768]{2,1,0:T(8,128)(2,1)S(1)}, u32[]{:S(2)}, u32[]{:S(2)}) collective-permute-start(bf16[2,192,768]{2,1,0:T(8,128)(2,1)} %copy-done.19), channel_id=1, source_target_pairs={{0,2},{1,3},{2,0},{3,1},{4,6},{5,7},{6,4},{7,5},{8,10},{9,11},{10,... | collective-permute-start | bytes 1769480 | tf_op jit(solution)/shard_map/ppermute | solution.py:663
  98.7 0.6 collective-permute-start.4
  99.3 1.9 %collective-permute-start.7 = (bf16[128,768]{1,0:T(8,128)(2,1)S(1)}, bf16[128,768]{1,0:T(8,128)(2,1)S(1)}, u32[]{:S(2)}, u32[]{:S(2)}) collective-permute-start(bf16[128,768]{1,0:T(8,128)(2,1)S(1)} %get-tuple-element.48.grads.own), channel_id=1, source_target_pairs={{1,2},{3,4},{5,6},{7,8},{9,10},{11,12},{13,14},{2,1},{4,3},{6,5},{... | collective-permute-start | bytes 589832 | tf_op jit(solution)/shard_map/ppermute | solution.py:424
  101.3 19.9 %collective-permute-done.7.outer = bf16[128,768]{1,0:T(8,128)(2,1)S(1)} collective-permute-done((bf16[128,768]{1,0:T(8,128)(2,1)S(1)}, bf16[128,768]{1,0:T(8,128)(2,1)S(1)}, u32[]{:S(2)}, u32[]{:S(2)}) %collective-permute-start.7) | collective-permute-done | bytes 196640 | tf_op jit(solution)/shard_map/ppermute | solution.py:424
  121.1 6.2 %input_grad_conv.1 = bf16[128,768]{1,0:T(8,128)(2,1)} custom-call(s32[1]{0:T(128)} %bitcast.core, bf16[128,768]{1,0:T(8,128)(2,1)S(1)} %collective-permute-done.4.inner, bf16[128,768]{1,0:T(8,128)(2,1)S(1)} %get-tuple-element.48.grads.own, bf16[128,768]{1,0:T(8,128)(2,1)S(1)} %collective-permute-done.7.outer, ...), custom_call_target="tpu_custom_call" | custom-call | flops 67436544 | bytes 1572864 | tf_op jit(solution)/shard_map/input_grad_conv/pallas_call | solution.py:678
  127.4 0.0 collective-permute-done.8.got
  127.4 1.2 weight_grads_sum.1
  128.5 1.0 kernel_grad_unpack.1
  129.6 0.6 slice_reduce_fusion
  (39 shorter events, 0.1 us)
Async XLA Ops:
  0.6 9.0 %collective-permute-start.2 = (bf16[128,768]{1,0:T(8,128)(2,1)}, bf16[128,768]{1,0:T(8,128)(2,1)S(1)}, u32[]{:S(2)}, u32[]{:S(2)}) collective-permute-start(bf16[128,768]{1,0:T(8,128)(2,1)} %bitcast.10), channel_id=1, source_target_pairs={{0,4},{1,5},{2,6},{3,7},{4,8},{5,9},{6,10},{7,11},{8,12},{9,13},{1... | collective-permute-start | bytes 589832 | tf_op jit(solution)/shard_map/ppermute | solution.py:458
  9.7 8.6 %collective-permute-start.3 = (bf16[128,768]{1,0:T(8,128)(2,1)S(1)}, bf16[128,768]{1,0:T(8,128)(2,1)S(1)}, u32[]{:S(2)}, u32[]{:S(2)}) collective-permute-start(bf16[128,768]{1,0:T(8,128)(2,1)S(1)} %collective-permute-done.2.rest_1_), channel_id=1, source_target_pairs={{0,4},{1,5},{2,6},{3,7},{4,8},{5,9},{6,10},{7,11},{8,12},{9,13},{1... | collective-permute-start | bytes 589832 | tf_op jit(solution)/shard_map/ppermute | solution.py:458
  9.7 9.7 %collective-permute-start = (bf16[128,768]{1,0:T(8,128)(2,1)}, bf16[128,768]{1,0:T(8,128)(2,1)S(1)}, u32[]{:S(2)}, u32[]{:S(2)}) collective-permute-start(bf16[128,768]{1,0:T(8,128)(2,1)} %bitcast.15), channel_id=1, source_target_pairs={{0,1},{1,0},{2,3},{3,2},{4,5},{5,4},{6,7},{7,6},{8,9},{9,8},{10,11... | collective-permute-start | bytes 589832 | tf_op jit(solution)/shard_map/ppermute | solution.py:423
  10.9 8.5 %collective-permute-start.1 = (bf16[128,768]{1,0:T(8,128)(2,1)}, bf16[128,768]{1,0:T(8,128)(2,1)S(1)}, u32[]{:S(2)}, u32[]{:S(2)}) collective-permute-start(bf16[128,768]{1,0:T(8,128)(2,1)} %bitcast.16), channel_id=1, source_target_pairs={{1,2},{3,4},{5,6},{7,8},{9,10},{11,12},{13,14},{2,1},{4,3},{6,5},{... | collective-permute-start | bytes 589832 | tf_op jit(solution)/shard_map/ppermute | solution.py:424
  13.9 0.9 copy-start.6
  14.9 1.2 copy-start.10
  16.1 3.2 %copy-start.20 = (f32[768]{0:T(1024)S(1)}, f32[768]{0:T(1024)}, u32[]{:S(2)}) copy-start(f32[768]{0:T(1024)} %param.14) | copy-start | bytes 9220
  16.1 3.3 %copy-start.21 = (f32[768]{0:T(1024)S(1)}, f32[768]{0:T(1024)}, u32[]{:S(2)}) copy-start(f32[768]{0:T(1024)} %param.11) | copy-start | bytes 9220
  16.1 3.3 %copy-start.22 = (f32[768]{0:T(1024)S(1)}, f32[768]{0:T(1024)}, u32[]{:S(2)}) copy-start(f32[768]{0:T(1024)} %param.10) | copy-start | bytes 9220
  18.3 31.5 %copy-start.11 = (bf16[128,768]{1,0:T(8,128)(2,1)}, bf16[128,768]{1,0:T(8,128)(2,1)S(1)}, u32[]{:S(2)}) copy-start(bf16[128,768]{1,0:T(8,128)(2,1)S(1)} %collective-permute-done.3.rest_2_) | copy-start | bytes 589828
  18.3 8.4 %collective-permute-start.5 = (bf16[128,768]{1,0:T(8,128)(2,1)S(1)}, bf16[128,768]{1,0:T(8,128)(2,1)S(1)}, u32[]{:S(2)}, u32[]{:S(2)}) collective-permute-start(bf16[128,768]{1,0:T(8,128)(2,1)S(1)} %collective-permute-done.3.rest_2_), channel_id=1, source_target_pairs={{0,4},{1,5},{2,6},{3,7},{4,8},{5,9},{6,10},{7,11},{8,12},{9,13},{1... | collective-permute-start | bytes 589832 | tf_op jit(solution)/shard_map/ppermute | solution.py:458
  23.1 0.7 copy-start.15
  23.9 0.6 copy-start.17
  24.5 25.3 %copy-start.5 = (bf16[4,4,8,768]{3,2,1,0:T(8,128)(2,1)S(1)}, bf16[4,4,8,768]{3,2,1,0:T(8,128)(2,1)}, u32[]{:S(2)}) copy-start(bf16[4,4,8,768]{3,2,1,0:T(8,128)(2,1)} %param.15) | copy-start | bytes 589828
  26.7 31.4 %copy-start.13 = (bf16[128,768]{1,0:T(8,128)(2,1)}, bf16[128,768]{1,0:T(8,128)(2,1)S(1)}, u32[]{:S(2)}) copy-start(bf16[128,768]{1,0:T(8,128)(2,1)S(1)} %collective-permute-done.5.rest_3_) | copy-start | bytes 589828
  26.7 23.1 %all-to-all-start.1 = ((bf16[4,128,768]{2,1,0:T(8,128)(2,1)}), bf16[4,128,768]{2,1,0:T(8,128)(2,1)S(1)}, u32[]{:S(2)}, u32[]{:S(2)}) async-start(bf16[4,128,768]{2,1,0:T(8,128)(2,1)} %get-tuple-element.44.normed), calls=%async_computation.1 | async-start | bytes 1572864 | tf_op jit(solution)/shard_map/all_to_all | solution.py:516
  49.8 2.3 %copy-start = (bf16[3072,768]{1,0:T(8,128)(2,1)S(1)}, bf16[3072,768]{1,0:T(8,128)(2,1)}, u32[]{:S(2)}) copy-start(bf16[3072,768]{1,0:T(8,128)(2,1)} %weight_in.5) | copy-start | bytes 14155780
  52.1 2.3 %copy-start.3 = (bf16[3072,768]{1,0:T(8,128)(2,1)S(1)}, bf16[3072,768]{1,0:T(8,128)(2,1)}, u32[]{:S(2)}) copy-start(bf16[3072,768]{1,0:T(8,128)(2,1)} %weight_out.5) | copy-start | bytes 14155780
  54.5 5.1 %copy-start.1 = (bf16[3072,768]{1,0:T(8,128)(2,1)S(1)}, bf16[3072,768]{1,0:T(8,128)(2,1)}, u32[]{:S(2)}) copy-start(bf16[3072,768]{1,0:T(8,128)(2,1)} %weight_in.5) | copy-start | bytes 14155780
  54.5 5.1 %copy-start.7 = (bf16[4,4,8,768]{3,2,1,0:T(8,128)(2,1)S(1)}, bf16[4,4,8,768]{3,2,1,0:T(8,128)(2,1)}, u32[]{:S(2)}) copy-start(bf16[4,4,8,768]{3,2,1,0:T(8,128)(2,1)} %param.8) | copy-start | bytes 589828
  54.5 5.1 %copy-start.16 = (f32[128,768]{1,0:T(8,128)S(1)}, f32[128,768]{1,0:T(8,128)}, u32[]{:S(2)}) copy-start(f32[128,768]{1,0:T(8,128)} %copy-done.15) | copy-start | bytes 1179652
  54.5 5.1 %copy-start.18 = (f32[128,128]{1,0:T(8,128)S(1)}, f32[128,128]{1,0:T(8,128)}, u32[]{:S(2)}) copy-start(f32[128,128]{1,0:T(8,128)} %copy-done.17) | copy-start | bytes 196612
  58.1 18.3 %collective-permute-start.6 = (bf16[2,2,192,768]{3,2,1,0:T(8,128)(2,1)}, bf16[2,2,192,768]{3,2,1,0:T(8,128)(2,1)}, u32[]{:S(2)}, u32[]{:S(2)}) collective-permute-start(bf16[2,2,192,768]{3,2,1,0:T(8,128)(2,1)} %weight_grads_other_core.1), channel_id=1, source_target_pairs={{0,1},{1,0},{2,3},{3,2},{4,5},{5,4},{6,7},{7,6},{8,9},{9,8},{10,11... | collective-permute-start | bytes 3538952 | tf_op jit(solution)/shard_map/ppermute | solution.py:641
  72.9 18.6 %all-to-all-start = ((bf16[16,24,768]{2,1,0:T(8,128)(2,1)}), bf16[16,24,768]{2,1,0:T(8,128)(2,1)S(1)}, u32[]{:S(2)}, u32[]{:S(2)}) async-start(bf16[16,24,768]{2,1,0:T(8,128)(2,1)} %bitcast.4), calls=%async_computation | async-start | bytes 1179648 | tf_op jit(solution)/shard_map/all_to_all | solution.py:587
  76.4 2.3 %copy-start.2 = (bf16[3072,768]{1,0:T(8,128)(2,1)S(1)}, bf16[3072,768]{1,0:T(8,128)(2,1)}, u32[]{:S(2)}) copy-start(bf16[3072,768]{1,0:T(8,128)(2,1)} %weight_in.5) | copy-start | bytes 14155780
  78.8 2.3 %copy-start.4 = (bf16[3072,768]{1,0:T(8,128)(2,1)S(1)}, bf16[3072,768]{1,0:T(8,128)(2,1)}, u32[]{:S(2)}) copy-start(bf16[3072,768]{1,0:T(8,128)(2,1)} %weight_out.5) | copy-start | bytes 14155780
  81.1 0.9 copy-start.12
  82.1 0.9 copy-start.14
  87.6 1.0 copy-start.8
  88.6 0.8 copy-start.19
  92.5 36.1 %all-to-all-start.2 = ((bf16[16,24,768]{2,1,0:T(8,128)(2,1)}), bf16[16,24,768]{2,1,0:T(8,128)(2,1)S(1)}, u32[]{:S(2)}, u32[]{:S(2)}) async-start(bf16[16,24,768]{2,1,0:T(8,128)(2,1)} %kernel_grad_sum.1), calls=%async_computation.2 | async-start | bytes 1179648 | tf_op jit(solution)/shard_map/all_to_all | solution.py:675
  97.2 30.1 %copy-start.9 = (f32[2,192,768]{2,1,0:T(8,128)S(1)}, f32[2,192,768]{2,1,0:T(8,128)}, u32[]{:S(2)}) copy-start(f32[2,192,768]{2,1,0:T(8,128)} %copy-done.8) | copy-start | bytes 3538948
  97.2 30.1 %collective-permute-start.8 = (bf16[2,192,768]{2,1,0:T(8,128)(2,1)}, bf16[2,192,768]{2,1,0:T(8,128)(2,1)S(1)}, u32[]{:S(2)}, u32[]{:S(2)}) collective-permute-start(bf16[2,192,768]{2,1,0:T(8,128)(2,1)} %copy-done.19), channel_id=1, source_target_pairs={{0,2},{1,3},{2,0},{3,1},{4,6},{5,7},{6,4},{7,5},{8,10},{9,11},{10,... | collective-permute-start | bytes 1769480 | tf_op jit(solution)/shard_map/ppermute | solution.py:663
  98.7 2.6 %collective-permute-start.4 = (bf16[128,768]{1,0:T(8,128)(2,1)S(1)}, bf16[128,768]{1,0:T(8,128)(2,1)S(1)}, u32[]{:S(2)}, u32[]{:S(2)}) collective-permute-start(bf16[128,768]{1,0:T(8,128)(2,1)S(1)} %get-tuple-element.48.grads.own), channel_id=1, source_target_pairs={{0,1},{1,0},{2,3},{3,2},{4,5},{5,4},{6,7},{7,6},{8,9},{9,8},{10,11... | collective-permute-start | bytes 589832 | tf_op jit(solution)/shard_map/ppermute | solution.py:423
  99.3 21.8 %collective-permute-start.7 = (bf16[128,768]{1,0:T(8,128)(2,1)S(1)}, bf16[128,768]{1,0:T(8,128)(2,1)S(1)}, u32[]{:S(2)}, u32[]{:S(2)}) collective-permute-start(bf16[128,768]{1,0:T(8,128)(2,1)S(1)} %get-tuple-element.48.grads.own), channel_id=1, source_target_pairs={{1,2},{3,4},{5,6},{7,8},{9,10},{11,12},{13,14},{2,1},{4,3},{6,5},{... | collective-permute-start | bytes 589832 | tf_op jit(solution)/shard_map/ppermute | solution.py:424

commit v6 on v5

--- a/solution.py
+++ b/solution.py
@@ -17,6 +17,12 @@
 root_half = 0.7071067811865476
 inv_root_tau = 0.3989422804014327
 norm_eps = 1e-06
+erf_step = 0.3275911
+erf_terms = tuple(
+    0.5 * a for a in (0.254829592, -0.284496736, 1.421413741, -1.453152027, 1.061405429)
+)
+
+NO_COST = pl.CostEstimate(flops=0, bytes_accessed=0, transcendentals=0)
 
 F32 = jnp.float32
 BF16 = jnp.bfloat16
@@ -170,7 +176,7 @@
 
 
 def rim_conv_kernel(
-    planes, height, core, inner, outer, split, partial, vectors, normed, unit, inv, spread, conv
+    planes, height, core, inner, outer, split, partial, gain, bias, normed, unit, inv, spread, conv
 ):
     step = pl.program_id(0)
 
@@ -194,6 +200,8 @@
         tiles = conv.shape[0]
         channels = tiles * LANES
         parts = [conv[k] for k in range(tiles)]
+        gains = gain[...].reshape(1, channels)
+        biases = bias[...].reshape(1, channels)
         average = jnp.sum(tree_sum(parts), axis=1, keepdims=True) * (1.0 / channels)
         parts = [part - average for part in parts]
         variance = jnp.sum(
@@ -205,7 +213,7 @@
             lanes = slice(k * LANES, (k + 1) * LANES)
             value = parts[k] * inverse
             unit[:, lanes] = value
-            whole = (value * vectors[0:1, lanes] + vectors[1:2, lanes]).astype(BF16)
+            whole = (value * gains[:, lanes] + biases[:, lanes]).astype(BF16)
             for copy in range(normed.shape[0]):
                 normed[copy, :, lanes] = whole
 
@@ -274,7 +282,8 @@
     weight_out,
     unit,
     inv,
-    vectors,
+    norm_gain,
+    layer_scale,
     voxels,
     cotangent,
     block_out,
@@ -285,8 +294,8 @@
     mixed_grad,
 ):
     step = pl.program_id(0)
-    gain = vectors[0:1, :]
-    scale = vectors[2:3, :]
+    gain = norm_gain[...].reshape(1, -1)
+    scale = layer_scale[...].reshape(1, -1)
 
     @pl.when(step == 0)
     def _():
@@ -332,17 +341,26 @@
 
 
 def slopes(hidden, act_grad):
-    cover = 0.5 * (1.0 + lax.erf(hidden * root_half))
+    bell = jnp.exp(-0.5 * hidden * hidden)
+    below = 1.0 + (erf_step * root_half) * jnp.abs(hidden)
+    t = pl.reciprocal(below, approx=True)
+    t = t * (2.0 - below * t)
+    poly = erf_terms[-1]
+    for term in erf_terms[-2::-1]:
+        poly = poly * t + term
+    tail = poly * t * bell
+    cover = jnp.where(hidden < 0.0, tail, 1.0 - tail)
     activated = (hidden * cover).astype(BF16)
-    slope = cover + hidden * jnp.exp(-0.5 * hidden * hidden) * inv_root_tau
+    slope = cover + hidden * bell * inv_root_tau
     return activated, (act_grad * slope).astype(BF16)
 
 
-def weight_grad_terms(which, weight_in, weight_out, vectors, normed, cotangents, aligned):
+def weight_grad_terms(which, weight_in, weight_out, scale, normed, cotangents, aligned):
     rows = normed.shape[1]
     line = len(cotangents)
+    scales = scale[...].reshape(1, -1)
     mixed_grad = jnp.concatenate(
-        [(vectors[2:3, :] * part[...].astype(F32)).astype(BF16) for part in cotangents], axis=0
+        [(scales * part[...].astype(F32)).astype(BF16) for part in cotangents], axis=0
     )
     for k in range(line):
         aligned[k * rows : (k + 1) * rows, :] = normed[which[4 + k]]
@@ -356,16 +374,16 @@
     )
 
 
-def other_core_terms_kernel(which, weight_in, weight_out, vectors, normed, *rest):
+def other_core_terms_kernel(which, weight_in, weight_out, scale, normed, *rest):
     *cotangents, out, aligned = rest
-    terms = weight_grad_terms(which, weight_in, weight_out, vectors, normed, cotangents, aligned)
+    terms = weight_grad_terms(which, weight_in, weight_out, scale, normed, cotangents, aligned)
     for k in range(2):
         out[0, k] = terms[k].astype(BF16)
 
 
-def own_core_terms_kernel(which, weight_in, weight_out, vectors, normed, got, *rest):
+def own_core_terms_kernel(which, weight_in, weight_out, scale, normed, got, *rest):
     *cotangents, sent, kept, aligned = rest
-    terms = weight_grad_terms(which, weight_in, weight_out, vectors, normed, cotangents, aligned)
+    terms = weight_grad_terms(which, weight_in, weight_out, scale, normed, cotangents, aligned)
     step = pl.program_id(0)
     for k in range(2):
         total = terms[k] + got[0, k].astype(F32)
@@ -390,7 +408,7 @@
         out[copy] = total
 
 
-def unpack_kernel(parts, out, small):
+def unpack_kernel(parts, out, *small):
     piece = parts.shape[1]
     for k in range(-(-TAP_ROWS // piece)):
         first = k * piece
@@ -401,10 +419,11 @@
     rows = parts[k].astype(F32)
     if first + SUB > piece:
         rows = jnp.concatenate([rows, parts[k + 1].astype(F32)], axis=0)
-    small[...] = rows[first : first + SUB, :]
-
-
-def params(limit=24):
+    for k, line in enumerate(small):
+        line[...] = rows[first + k : first + k + 1, :].reshape(line.shape)
+
+
+def params(limit=48):
     return pltpu.CompilerParams(vmem_limit_bytes=limit * 1024 * 1024)
 
 
@@ -422,12 +441,6 @@
     return (
         lax.ppermute(cells, "row", [(i, i ^ 1) for i in range(count)]),
         lax.ppermute(cells, "row", between + [(j, i) for i, j in between]),
-    )
-
-
-def conv_cost(rows, channels):
-    return pl.CostEstimate(
-        flops=rows * channels * TAP_ROWS * 2, bytes_accessed=4 * rows * channels * 4, transcendentals=0
     )
 
 
@@ -448,23 +461,20 @@
 
     own = voxels.reshape(rows, channels)
     upstream = cotangent.reshape(rows, channels)
-    vectors = jnp.stack([norm_gain, norm_bias, layer_scale])
     core = lax.rem(me, 2).astype(jnp.int32)
     parity = core.reshape(1)
 
     inner, outer = rims(own)
 
-    def next_in_line(cells):
-        return lax.ppermute(cells, "row", [(i, (i + quad) % count) for i in range(count)])
-
-    upstream_line = [upstream, next_in_line(upstream)]
+    upstream_line = [upstream] + [
+        lax.ppermute(upstream, "row", [(i, (i + quad * k) % count) for i in range(count)])
+        for k in range(1, line)
+    ]
 
     def spread_of(held):
         return pltpu.VMEM((9, held, PAD, LANES), F32)
 
     split_block = pl.BlockSpec((None, 9, KS, SUB, LANES), lambda c, *_: (c, 0, 0, 0, 0))
-    own, upstream_line[-1] = lax.optimization_barrier((own, upstream_line[-1]))
-    upstream_line.append(next_in_line(upstream_line[-1]))
     partial, split = pl.pallas_call(
         functools.partial(own_conv_kernel, planes, height),
         grid=(tiles,),
@@ -476,13 +486,10 @@
         ],
         scratch_shapes=[spread_of(planes)],
         compiler_params=params(),
-        cost_estimate=conv_cost(rows, channels // 2),
+        cost_estimate=NO_COST,
         name="own_conv",
     )(own, dw_kernel)
 
-    partial, upstream_line[-1] = lax.optimization_barrier((partial, upstream_line[-1]))
-    for _ in range(3, line):
-        upstream_line.append(next_in_line(upstream_line[-1]))
     normed, unit, inv = pl.pallas_call(
         functools.partial(rim_conv_kernel, planes, height),
         grid_spec=pltpu.PrefetchScalarGridSpec(
@@ -493,7 +500,8 @@
                 lane_block(rows),
                 split_block,
                 lane_block(rows),
-                whole_block(3, channels),
+                whole_block(channels),
+                whole_block(channels),
             ],
             out_specs=[
                 whole_block(line, rows, channels),
@@ -508,13 +516,12 @@
             jax.ShapeDtypeStruct((rows, LANES), F32),
         ],
         compiler_params=params(),
-        cost_estimate=conv_cost(rows, channels // 2),
+        cost_estimate=NO_COST,
         name="rim_conv",
-    )(parity, inner, outer, split, partial, vectors)
-
-    copies_out, upstream_line[-1] = lax.optimization_barrier((normed, upstream_line[-1]))
+    )(parity, inner, outer, split, partial, norm_gain, norm_bias)
+
     gathered = lax.all_to_all(
-        copies_out, "row", split_axis=0, concat_axis=0, tiled=True, axis_index_groups=lines
+        normed, "row", split_axis=0, concat_axis=0, tiled=True, axis_index_groups=lines
     )
 
     block = 512
@@ -528,7 +535,8 @@
             pl.BlockSpec((block, channels), lambda f: (f, 0)),
             whole,
             whole_block(rows, LANES),
-            whole_block(3, channels),
+            whole_block(channels),
+            whole_block(channels),
             whole,
             whole,
         ],
@@ -548,13 +556,9 @@
             pltpu.VMEM((rows, channels), BF16),
         ],
         compiler_params=params(),
-        cost_estimate=pl.CostEstimate(
-            flops=8 * rows * channels * units,
-            bytes_accessed=4 * units * channels,
-            transcendentals=2 * rows * units,
-        ),
+        cost_estimate=NO_COST,
         name="mlp_both_ways",
-    )(normed, weight_in, weight_out, unit, inv, vectors, own, upstream)
+    )(normed, weight_in, weight_out, unit, inv, norm_gain, layer_scale, own, upstream)
 
     piece = -(-(TAP_ROWS + SUB) // count)
     piece += -piece % SUB
@@ -581,16 +585,9 @@
         ),
         out_shape=jax.ShapeDtypeStruct((padded, channels), BF16),
         compiler_params=params(),
-        cost_estimate=conv_cost(rows, channels),
+        cost_estimate=NO_COST,
         name="kernel_grad_terms",
     )(parity, inner, own, outer, conv_grad, small)
-    scattered = lax.all_to_all(
-        sums.reshape(count, piece, channels), "row", split_axis=0, concat_axis=0, tiled=True
-    )
-
-    conv_grad, sums = lax.optimization_barrier((conv_grad, sums))
-    grad_inner, grad_outer = rims(conv_grad)
-
     share = units // count
     tokens = line * rows
     base = me // quad * quad
@@ -609,21 +606,20 @@
             place.astype(jnp.int32),
         ]
     )
-    terms_cost = pl.CostEstimate(
-        flops=16 * tokens * channels * share,
-        bytes_accessed=4 * tokens * channels + 8 * share * channels,
-        transcendentals=4 * tokens * share,
-    )
     pair = (2, 2, share, channels)
 
     def chunk(at):
         return pl.BlockSpec((share, channels), lambda s, w: (w[s + at], 0))
 
-    sets = [whole_block(3, channels), whole_block(line, rows, channels)]
+    sets = [whole_block(channels), whole_block(line, rows, channels)]
     cotangents = [whole_block(rows, channels)] * line
     aligned = [pltpu.VMEM((tokens, channels), BF16)]
 
-    which, sums = lax.optimization_barrier((which, sums))
+    which, sums, conv_grad = lax.optimization_barrier((which, sums, conv_grad))
+    scattered = lax.all_to_all(
+        sums.reshape(count, piece, channels), "row", split_axis=0, concat_axis=0, tiled=True
+    )
+    grad_inner, grad_outer = rims(conv_grad)
     for_other = pl.pallas_call(
         other_core_terms_kernel,
         grid_spec=pltpu.PrefetchScalarGridSpec(
@@ -635,9 +631,9 @@
         ),
         out_shape=jax.ShapeDtypeStruct(pair, BF16),
         compiler_params=params(),
-        cost_estimate=terms_cost,
+        cost_estimate=NO_COST,
         name="weight_grads_other_core",
-    )(which, weight_in, weight_out, vectors, gathered, *upstream_line)
+    )(which, weight_in, weight_out, layer_scale, gathered, *upstream_line)
     from_other = lax.ppermute(for_other, "row", other_core)
 
     sent, kept = pl.pallas_call(
@@ -657,12 +653,12 @@
             jax.ShapeDtypeStruct(pair[1:], F32),
         ],
         compiler_params=params(),
-        cost_estimate=terms_cost,
+        cost_estimate=NO_COST,
         name="weight_grads_own_core",
-    )(which, weight_in, weight_out, vectors, gathered, from_other, *upstream_line)
+    )(which, weight_in, weight_out, layer_scale, gathered, from_other, *upstream_line)
     got = lax.ppermute(sent, "row", other_side)
 
-    scattered, sent = lax.optimization_barrier((scattered, sent))
+    scattered, kept = lax.optimization_barrier((scattered, kept))
     copies = pl.pallas_call(
         spread_sum_kernel,
         in_specs=[whole_block(count, piece, channels)],
@@ -670,11 +666,11 @@
         out_shape=jax.ShapeDtypeStruct((count, piece, channels), BF16),
         grid=(1,),
         compiler_params=params(),
+        cost_estimate=NO_COST,
         name="kernel_grad_sum",
     )(scattered)
+    conv_own, copies = lax.optimization_barrier((conv_grad, copies))
     totals = lax.all_to_all(copies, "row", split_axis=0, concat_axis=0, tiled=True)
-
-    conv_own, copies = lax.optimization_barrier((conv_grad, copies))
     voxel_grad = pl.pallas_call(
         functools.partial(input_grad_kernel, planes, height),
         grid_spec=pltpu.PrefetchScalarGridSpec(
@@ -692,20 +688,21 @@
         ),
         out_shape=jax.ShapeDtypeStruct((rows, channels), BF16),
         compiler_params=params(),
-        cost_estimate=conv_cost(rows, channels),
+        cost_estimate=NO_COST,
         name="input_grad_conv",
     )(parity, grad_inner, conv_own, grad_outer, split, upstream)
 
-    kernel_grad, vector_grads = pl.pallas_call(
+    kernel_grad, *vector_grads = pl.pallas_call(
         unpack_kernel,
         grid=(1,),
         in_specs=[whole_block(count, piece, channels)],
-        out_specs=[whole_block(TAP_ROWS, channels), whole_block(SUB, channels)],
+        out_specs=[whole_block(TAP_ROWS, channels)] + [whole_block(channels)] * 3,
         out_shape=[
             jax.ShapeDtypeStruct((TAP_ROWS, channels), F32),
-            jax.ShapeDtypeStruct((SUB, channels), F32),
-        ],
-        compiler_params=params(),
+        ]
+        + [jax.ShapeDtypeStruct((channels,), F32)] * 3,
+        compiler_params=params(),
+        cost_estimate=NO_COST,
         name="kernel_grad_unpack",
     )(totals)
 
@@ -716,6 +713,7 @@
         out_specs=[whole_block(share, channels)] * 2,
         out_shape=[jax.ShapeDtypeStruct((share, channels), F32)] * 2,
         compiler_params=params(),
+        cost_estimate=NO_COST,
         name="weight_grads_sum",
     )(kept, got)
 
@@ -723,9 +721,7 @@
         block_out.reshape(voxels.shape),
         voxel_grad.reshape(voxels.shape),
         kernel_grad,
-        vector_grads[0],
-        vector_grads[1],
-        vector_grads[2],
+        *vector_grads,
         weight_in_grad,
         weight_out_grad,
     )

time: 132 us -> 122 us (0.924)
  waiting for transfers between devices: 50.5 us -> 40.1 us
  local copies, waits for them, and re-layouts: 17.3 us -> 7.31 us
  starting transfers between devices: 24.7 us -> 31.2 us
  Pallas kernels: 36.7 us -> 40.6 us
    all_to_all x1, waiting for transfers between devices: 19.4 us -> 0.01 us  [on_device(): lax.all_to_all(normed, 'row', split_axis=0, concat_axis=0, tiled=True, ax...]
    unnamed x46 -> x28, local copies, waits for them, and re-layouts: 16.6 us -> 7.22 us
    all_to_all x1, waiting for transfers between devices: 2.15 us -> 7.9 us  [on_device(): lax.all_to_all(sums.reshape(count, piece, channels), 'row', split_axis=0,...]
    all_to_all x1, starting transfers between devices: 3.48 us -> 7.12 us  [on_device(): lax.all_to_all(sums.reshape(count, piece, channels), 'row', split_axis=0,...]
    ppermute x3, waiting for transfers between devices: 9.06 us -> 11.6 us  [on_device(): lax.ppermute(upstream, 'row', [(i, (i + quad * k) % count) for i in range...]
    all_to_all x1, starting transfers between devices: 3.5 us -> 5.91 us  [on_device(): lax.all_to_all(normed, 'row', split_axis=0, concat_axis=0, tiled=True, ax...]
    pallas_call x1, Pallas kernels: 3.64 us -> 5.22 us  [on_device(): pl.pallas_call(other_core_terms_kernel, grid_spec=pltpu.PrefetchScalarGri...]
    ppermute x3, starting transfers between devices: 3.24 us -> 4.73 us  [on_device(): lax.ppermute(upstream, 'row', [(i, (i + quad * k) % count) for i in range...]
  transfers between devices with their start and end apart: 12 -> 12, of which waited for: 5 -> 4; matrix products, arithmetic and copies ran while one was open for 0% -> 0% of each run, Pallas kernels for 24% -> 25%
where the time goes in v6:
time: 122 us; the launch traced here: 120 us
  Pallas kernels  40.6 us (33%)
  waiting for transfers between devices  40.1 us (33%)
  starting transfers between devices  31.2 us (26%)
  local copies, waits for them, and re-layouts  7.31 us (6%)
    ppermute x2, waiting for transfers between devices, rims(): lax.ppermute(cells, 'row', between + [(j, i) for i, j in between])  20.6 us
    ppermute x3, waiting for transfers between devices, on_device(): lax.ppermute(upstream, 'row', [(i, (i + quad * k) % count) for i in range...  11.6 us
    pallas_call x1, Pallas kernels, on_device(): pl.pallas_call(mlp_kernel, grid=(units // block,), in_specs=[pl.BlockSpec...  9.38 us
    all_to_all x1, waiting for transfers between devices, on_device(): lax.all_to_all(sums.reshape(count, piece, channels), 'row', split_axis=0,...  7.9 us
    unnamed x28, local copies, waits for them, and re-layouts  7.22 us
    all_to_all x1, starting transfers between devices, on_device(): lax.all_to_all(sums.reshape(count, piece, channels), 'row', split_axis=0,...  7.12 us
    ppermute x2, starting transfers between devices, rims(): lax.ppermute(cells, 'row', between + [(j, i) for i, j in between])  6.41 us
    pallas_call x1, Pallas kernels, on_device(): pl.pallas_call(functools.partial(input_grad_kernel, planes, height), grid...  6.24 us
  transfers between devices with their start and end apart: 12, of which 4 were waited for; matrix products, arithmetic and copies ran while one was open for 0% of the time, Pallas kernels for 25%

profile of v6, /device:TPU:1, one launch (start us, length us, event | category | flops | bytes accessed | tf_op | source)
XLA Modules:
  0.0 120.0 jit_solution(8498484467515669795)
XLA Ops:
  0.6 0.0 copy-start.11
  0.7 0.1 collective-permute-start
  0.8 4.5 %collective-permute-start.1 = (bf16[128,768]{1,0:T(8,128)(2,1)}, bf16[128,768]{1,0:T(8,128)(2,1)S(1)}, u32[]{:S(2)}, u32[]{:S(2)}) collective-permute-start(bf16[128,768]{1,0:T(8,128)(2,1)} %bitcast.18), channel_id=1, source_target_pairs={{1,2},{3,4},{5,6},{7,8},{9,10},{11,12},{13,14},{2,1},{4,3},{6,5},{... | collective-permute-start | bytes 589832 | tf_op jit(solution)/shard_map/ppermute | solution.py:443
  5.3 0.0 copy-start.1
  5.3 0.9 copy-done.1
  6.2 1.2 %copy-done.5 = f32[343,768]{1,0:T(8,128)S(1)} copy-done((f32[343,768]{1,0:T(8,128)S(1)}, f32[343,768]{1,0:T(8,128)}, u32[]{:S(2)}) %copy-start.5) | copy-done | bytes 1053720
  7.4 2.1 %own_conv.1 = (f32[128,768]{1,0:T(8,128)S(1)}, f32[6,9,7,8,128]{4,3,2,1,0:T(8,128)S(1)}) custom-call(bf16[128,768]{1,0:T(8,128)(2,1)S(1)} %bitcast.19, f32[343,768]{1,0:T(8,128)S(1)} %copy-done.5), custom_call_target="tpu_custom_call" | custom-call | tf_op jit(solution)/shard_map/own_conv/pallas_call | solution.py:478
  9.6 0.0 collective-permute-done.inner
  9.6 0.7 collective-permute-done.1.outer
  10.3 0.0 copy-done.11
  10.3 3.6 %rim_conv.1 = (bf16[4,128,768]{2,1,0:T(8,128)(2,1)}, f32[128,768]{1,0:T(8,128)S(1)}, f32[128,128]{1,0:T(8,128)S(1)}) custom-call(s32[1]{0:T(128)} %bitcast.core, bf16[128,768]{1,0:T(8,128)(2,1)S(1)} %collective-permute-done.inner, bf16[128,768]{1,0:T(8,128)(2,1)S(1)} %collective-permute-done.1.outer, f32[6,9,7,8,128]{4,3,2,1,0:T(8,128)S(1)} %get-tuple-element.31.split, ...), custom_call_target="tpu_custom_call" | custom-call | tf_op jit(solution)/shard_map/rim_conv/pallas_call | solution.py:493
  14.0 0.7 copy-done.6
  14.7 0.6 copy-done.8
  15.4 5.9 %all-to-all-start.1 = ((bf16[4,128,768]{2,1,0:T(8,128)(2,1)}), bf16[4,128,768]{2,1,0:T(8,128)(2,1)S(1)}, u32[]{:S(2)}, u32[]{:S(2)}) async-start(bf16[4,128,768]{2,1,0:T(8,128)(2,1)} %get-tuple-element.33.normed), calls=%async_computation.1 | async-start | bytes 1572864 | tf_op jit(solution)/shard_map/all_to_all | solution.py:523
  21.3 1.5 %collective-permute-start.3 = (bf16[128,768]{1,0:T(8,128)(2,1)S(1)}, bf16[128,768]{1,0:T(8,128)(2,1)S(1)}, u32[]{:S(2)}, u32[]{:S(2)}) collective-permute-start(bf16[128,768]{1,0:T(8,128)(2,1)S(1)} %bitcast.10), channel_id=1, source_target_pairs={{0,4},{1,5},{2,6},{3,7},{4,8},{5,9},{6,10},{7,11},{8,12},{9,13},{1... | collective-permute-start | bytes 589832 | tf_op jit(solution)/shard_map/ppermute | solution.py:470
  22.7 2.1 %collective-permute-start.4 = (bf16[128,768]{1,0:T(8,128)(2,1)S(1)}, bf16[128,768]{1,0:T(8,128)(2,1)}, u32[]{:S(2)}, u32[]{:S(2)}) collective-permute-start(bf16[128,768]{1,0:T(8,128)(2,1)S(1)} %bitcast.11), channel_id=1, source_target_pairs={{0,8},{1,9},{2,10},{3,11},{4,12},{5,13},{6,14},{7,15},{8,0},{9,1},... | collective-permute-start | bytes 589832 | tf_op jit(solution)/shard_map/ppermute | solution.py:470
  24.8 1.2 collective-permute-start.5
  26.0 0.1 concatenate.3.which
  26.1 0.0 copy-done.2
  26.1 1.0 copy-done.7
  27.1 0.8 copy-done.9
  27.9 9.4 %mlp_both_ways.1 = (bf16[128,768]{1,0:T(8,128)(2,1)}, bf16[128,768]{1,0:T(8,128)(2,1)S(1)}, f32[8,768]{1,0:T(8,128)S(1)}) custom-call(bf16[4,128,768]{2,1,0:T(8,128)(2,1)} %get-tuple-element.33.normed, bf16[3072,768]{1,0:T(8,128)(2,1)} %weight_in.5, bf16[3072,768]{1,0:T(8,128)(2,1)} %weight_out.5, f32[128,768]{1,0:T(8,128)S(1)} %copy-done.7, ...), custom_call_target="tpu_custom_call" | custom-call | tf_op jit(solution)/shard_map/mlp_both_ways/pallas_call | solution.py:529
  37.3 5.5 %kernel_grad_terms.1 = bf16[384,768]{1,0:T(8,128)(2,1)} custom-call(s32[1]{0:T(128)} %bitcast.core, bf16[128,768]{1,0:T(8,128)(2,1)S(1)} %collective-permute-done.inner, bf16[128,768]{1,0:T(8,128)(2,1)S(1)} %bitcast.21, bf16[128,768]{1,0:T(8,128)(2,1)S(1)} %collective-permute-done.1.outer, bf16[128,768]{1,0:T(8,128)(2,1)S(1)} %get-tuple-element.44.grads.own, ...), custom_call_target="tpu_custom_call" | custom-call | tf_op jit(solution)/shard_map/kernel_grad_terms/pallas_call | solution.py:566
  42.8 0.0 collective-permute-done.3.rest_1_
  42.8 11.6 %collective-permute-done.4.rest_2_ = bf16[128,768]{1,0:T(8,128)(2,1)} collective-permute-done((bf16[128,768]{1,0:T(8,128)(2,1)S(1)}, bf16[128,768]{1,0:T(8,128)(2,1)}, u32[]{:S(2)}, u32[]{:S(2)}) %collective-permute-start.4) | collective-permute-done | bytes 196640 | tf_op jit(solution)/shard_map/ppermute | solution.py:470
  54.4 0.0 collective-permute-done.5.rest_3_
  54.4 0.0 all-to-all-done.1.normed
  54.4 5.2 %weight_grads_other_core.1 = bf16[2,2,192,768]{3,2,1,0:T(8,128)(2,1)} custom-call(s32[8]{0:T(128)S(1)} %concatenate.3.which, bf16[3072,768]{1,0:T(8,128)(2,1)} %weight_in.5, bf16[3072,768]{1,0:T(8,128)(2,1)} %weight_out.5, f32[768]{0:T(1024)S(1)} %copy-done.10, bf16[4,128,768]{2,1,0:T(8,128)(2,1)S(1)} %all-to-all-done.1.normed, ...), custom_call_target="tpu_custom_call" | custom-call | tf_op jit(solution)/shard_map/weight_grads_other_core/pallas_call | solution.py:623
  59.6 0.0 collective-permute-start.6
  59.6 7.1 %all-to-all-start = ((bf16[16,24,768]{2,1,0:T(8,128)(2,1)}), bf16[16,24,768]{2,1,0:T(8,128)(2,1)S(1)}, u32[]{:S(2)}, u32[]{:S(2)}) async-start(bf16[16,24,768]{2,1,0:T(8,128)(2,1)} %bitcast.8), calls=%async_computation | async-start | bytes 1179648 | tf_op jit(solution)/shard_map/all_to_all | solution.py:619
  66.8 0.0 collective-permute-done.6.got
  66.8 5.4 %weight_grads_own_core.1 = (bf16[2,192,768]{2,1,0:T(8,128)(2,1)S(1)}, f32[2,192,768]{2,1,0:T(8,128)S(1)}) custom-call(s32[8]{0:T(128)S(1)} %concatenate.3.which, bf16[3072,768]{1,0:T(8,128)(2,1)} %weight_in.5, bf16[3072,768]{1,0:T(8,128)(2,1)} %weight_out.5, f32[768]{0:T(1024)S(1)} %copy-done.10, bf16[4,128,768]{2,1,0:T(8,128)(2,1)S(1)} %all-to-all-done.1.normed, ...), custom_call_target="tpu_custom_call" | custom-call | tf_op jit(solution)/shard_map/weight_grads_own_core/pallas_call | solution.py:639
  72.2 0.0 copy-start.3
  72.2 1.0 copy-done.3
  73.2 0.8 copy-done.13
  74.0 7.9 %all-to-all-done.parts = bf16[16,24,768]{2,1,0:T(8,128)(2,1)S(1)} async-done(((bf16[16,24,768]{2,1,0:T(8,128)(2,1)}), bf16[16,24,768]{2,1,0:T(8,128)(2,1)S(1)}, u32[]{:S(2)}, u32[]{:S(2)}) %all-to-all-start) | async-done | bytes 589856 | tf_op jit(solution)/shard_map/all_to_all | solution.py:619
  81.9 0.9 kernel_grad_sum.1
  82.8 4.8 %all-to-all-start.2 = ((bf16[16,24,768]{2,1,0:T(8,128)(2,1)}), bf16[16,24,768]{2,1,0:T(8,128)(2,1)S(1)}, u32[]{:S(2)}, u32[]{:S(2)}) async-start(bf16[16,24,768]{2,1,0:T(8,128)(2,1)} %kernel_grad_sum.1), calls=%async_computation.2 | async-start | bytes 1179648 | tf_op jit(solution)/shard_map/all_to_all | solution.py:673
  87.6 1.5 %collective-permute-start.8 = (bf16[2,192,768]{2,1,0:T(8,128)(2,1)}, bf16[2,192,768]{2,1,0:T(8,128)(2,1)S(1)}, u32[]{:S(2)}, u32[]{:S(2)}) collective-permute-start(bf16[2,192,768]{2,1,0:T(8,128)(2,1)} %copy-done.13), channel_id=1, source_target_pairs={{0,2},{1,3},{2,0},{3,1},{4,6},{5,7},{6,4},{7,5},{8,10},{9,11},{10,... | collective-permute-start | bytes 1769480 | tf_op jit(solution)/shard_map/ppermute | solution.py:659
  89.1 0.6 collective-permute-start.2
  89.7 1.9 %collective-permute-start.7 = (bf16[128,768]{1,0:T(8,128)(2,1)S(1)}, bf16[128,768]{1,0:T(8,128)(2,1)S(1)}, u32[]{:S(2)}, u32[]{:S(2)}) collective-permute-start(bf16[128,768]{1,0:T(8,128)(2,1)S(1)} %get-tuple-element.44.grads.own), channel_id=1, source_target_pairs={{1,2},{3,4},{5,6},{7,8},{9,10},{11,12},{13,14},{2,1},{4,3},{6,5},{... | collective-permute-start | bytes 589832 | tf_op jit(solution)/shard_map/ppermute | solution.py:443
  91.7 0.0 collective-permute-done.2.inner
  91.7 19.9 %collective-permute-done.7.outer = bf16[128,768]{1,0:T(8,128)(2,1)S(1)} collective-permute-done((bf16[128,768]{1,0:T(8,128)(2,1)S(1)}, bf16[128,768]{1,0:T(8,128)(2,1)S(1)}, u32[]{:S(2)}, u32[]{:S(2)}) %collective-permute-start.7) | collective-permute-done | bytes 196640 | tf_op jit(solution)/shard_map/ppermute | solution.py:443
  111.5 6.2 %input_grad_conv.1 = bf16[128,768]{1,0:T(8,128)(2,1)} custom-call(s32[1]{0:T(128)} %bitcast.core, bf16[128,768]{1,0:T(8,128)(2,1)S(1)} %collective-permute-done.2.inner, bf16[128,768]{1,0:T(8,128)(2,1)S(1)} %get-tuple-element.44.grads.own, bf16[128,768]{1,0:T(8,128)(2,1)S(1)} %collective-permute-done.7.outer, ...), custom_call_target="tpu_custom_call" | custom-call | tf_op jit(solution)/shard_map/input_grad_conv/pallas_call | solution.py:674
  117.8 0.0 collective-permute-done.8.got
  117.8 1.2 weight_grads_sum.1
  118.9 0.0 all-to-all-done.2.parts
  118.9 1.0 kernel_grad_unpack.1
  (16 shorter events, 0.0 us)
Async XLA Ops:
  0.6 9.7 %copy-start.11 = (f32[768]{0:T(1024)S(1)}, f32[768]{0:T(1024)}, u32[]{:S(2)}) copy-start(f32[768]{0:T(1024)} %norm_gain.1) | copy-start | bytes 9220
  0.6 9.7 %copy-start.12 = (f32[768]{0:T(1024)S(1)}, f32[768]{0:T(1024)}, u32[]{:S(2)}) copy-start(f32[768]{0:T(1024)} %bias.1) | copy-start | bytes 9220
  0.7 9.0 %collective-permute-start = (bf16[128,768]{1,0:T(8,128)(2,1)}, bf16[128,768]{1,0:T(8,128)(2,1)S(1)}, u32[]{:S(2)}, u32[]{:S(2)}) collective-permute-start(bf16[128,768]{1,0:T(8,128)(2,1)} %bitcast.17), channel_id=1, source_target_pairs={{0,1},{1,0},{2,3},{3,2},{4,5},{5,4},{6,7},{7,6},{8,9},{9,8},{10,11... | collective-permute-start | bytes 589832 | tf_op jit(solution)/shard_map/ppermute | solution.py:442
  0.8 9.6 %collective-permute-start.1 = (bf16[128,768]{1,0:T(8,128)(2,1)}, bf16[128,768]{1,0:T(8,128)(2,1)S(1)}, u32[]{:S(2)}, u32[]{:S(2)}) collective-permute-start(bf16[128,768]{1,0:T(8,128)(2,1)} %bitcast.18), channel_id=1, source_target_pairs={{1,2},{3,4},{5,6},{7,8},{9,10},{11,12},{13,14},{2,1},{4,3},{6,5},{... | collective-permute-start | bytes 589832 | tf_op jit(solution)/shard_map/ppermute | solution.py:443
  5.3 0.9 copy-start.1
  6.2 1.2 %copy-start.5 = (f32[343,768]{1,0:T(8,128)S(1)}, f32[343,768]{1,0:T(8,128)}, u32[]{:S(2)}) copy-start(f32[343,768]{1,0:T(8,128)} %taps.1) | copy-start | bytes 3161092
  14.0 0.7 copy-start.6
  14.7 0.6 copy-start.8
  15.4 5.9 %copy-start = (bf16[4,4,8,768]{3,2,1,0:T(8,128)(2,1)S(1)}, bf16[4,4,8,768]{3,2,1,0:T(8,128)(2,1)}, u32[]{:S(2)}) copy-start(bf16[4,4,8,768]{3,2,1,0:T(8,128)(2,1)} %param.15) | copy-start | bytes 589828
  15.4 10.7 %copy-start.2 = (bf16[4,4,8,768]{3,2,1,0:T(8,128)(2,1)S(1)}, bf16[4,4,8,768]{3,2,1,0:T(8,128)(2,1)}, u32[]{:S(2)}) copy-start(bf16[4,4,8,768]{3,2,1,0:T(8,128)(2,1)} %param.8) | copy-start | bytes 589828
  15.4 10.7 %copy-start.10 = (f32[768]{0:T(1024)S(1)}, f32[768]{0:T(1024)}, u32[]{:S(2)}) copy-start(f32[768]{0:T(1024)} %scale.3) | copy-start | bytes 9220
  15.4 39.0 %all-to-all-start.1 = ((bf16[4,128,768]{2,1,0:T(8,128)(2,1)}), bf16[4,128,768]{2,1,0:T(8,128)(2,1)S(1)}, u32[]{:S(2)}, u32[]{:S(2)}) async-start(bf16[4,128,768]{2,1,0:T(8,128)(2,1)} %get-tuple-element.33.normed), calls=%async_computation.1 | async-start | bytes 1572864 | tf_op jit(solution)/shard_map/all_to_all | solution.py:523
  21.3 21.5 %collective-permute-start.3 = (bf16[128,768]{1,0:T(8,128)(2,1)S(1)}, bf16[128,768]{1,0:T(8,128)(2,1)S(1)}, u32[]{:S(2)}, u32[]{:S(2)}) collective-permute-start(bf16[128,768]{1,0:T(8,128)(2,1)S(1)} %bitcast.10), channel_id=1, source_target_pairs={{0,4},{1,5},{2,6},{3,7},{4,8},{5,9},{6,10},{7,11},{8,12},{9,13},{1... | collective-permute-start | bytes 589832 | tf_op jit(solution)/shard_map/ppermute | solution.py:470
  22.7 31.6 %collective-permute-start.4 = (bf16[128,768]{1,0:T(8,128)(2,1)S(1)}, bf16[128,768]{1,0:T(8,128)(2,1)}, u32[]{:S(2)}, u32[]{:S(2)}) collective-permute-start(bf16[128,768]{1,0:T(8,128)(2,1)S(1)} %bitcast.11), channel_id=1, source_target_pairs={{0,8},{1,9},{2,10},{3,11},{4,12},{5,13},{6,14},{7,15},{8,0},{9,1},... | collective-permute-start | bytes 589832 | tf_op jit(solution)/shard_map/ppermute | solution.py:470
  24.8 29.6 %collective-permute-start.5 = (bf16[128,768]{1,0:T(8,128)(2,1)S(1)}, bf16[128,768]{1,0:T(8,128)(2,1)}, u32[]{:S(2)}, u32[]{:S(2)}) collective-permute-start(bf16[128,768]{1,0:T(8,128)(2,1)S(1)} %bitcast.12), channel_id=1, source_target_pairs={{0,12},{1,13},{2,14},{3,15},{4,0},{5,1},{6,2},{7,3},{8,4},{9,5},{1... | collective-permute-start | bytes 589832 | tf_op jit(solution)/shard_map/ppermute | solution.py:470
  26.1 1.0 copy-start.7
  27.1 0.8 copy-start.9
  59.6 7.1 %collective-permute-start.6 = (bf16[2,2,192,768]{3,2,1,0:T(8,128)(2,1)}, bf16[2,2,192,768]{3,2,1,0:T(8,128)(2,1)}, u32[]{:S(2)}, u32[]{:S(2)}) collective-permute-start(bf16[2,2,192,768]{3,2,1,0:T(8,128)(2,1)} %weight_grads_other_core.1), channel_id=1, source_target_pairs={{0,1},{1,0},{2,3},{3,2},{4,5},{5,4},{6,7},{7,6},{8,9},{9,8},{10,11... | collective-permute-start | bytes 3538952 | tf_op jit(solution)/shard_map/ppermute | solution.py:637
  59.6 22.3 %all-to-all-start = ((bf16[16,24,768]{2,1,0:T(8,128)(2,1)}), bf16[16,24,768]{2,1,0:T(8,128)(2,1)S(1)}, u32[]{:S(2)}, u32[]{:S(2)}) async-start(bf16[16,24,768]{2,1,0:T(8,128)(2,1)} %bitcast.8), calls=%async_computation | async-start | bytes 1179648 | tf_op jit(solution)/shard_map/all_to_all | solution.py:619
  72.2 1.0 copy-start.3
  73.2 0.8 copy-start.13
  82.8 36.1 %all-to-all-start.2 = ((bf16[16,24,768]{2,1,0:T(8,128)(2,1)}), bf16[16,24,768]{2,1,0:T(8,128)(2,1)S(1)}, u32[]{:S(2)}, u32[]{:S(2)}) async-start(bf16[16,24,768]{2,1,0:T(8,128)(2,1)} %kernel_grad_sum.1), calls=%async_computation.2 | async-start | bytes 1179648 | tf_op jit(solution)/shard_map/all_to_all | solution.py:673
  87.6 30.1 %copy-start.4 = (f32[2,192,768]{2,1,0:T(8,128)S(1)}, f32[2,192,768]{2,1,0:T(8,128)}, u32[]{:S(2)}) copy-start(f32[2,192,768]{2,1,0:T(8,128)} %copy-done.3) | copy-start | bytes 3538948
  87.6 30.1 %collective-permute-start.8 = (bf16[2,192,768]{2,1,0:T(8,128)(2,1)}, bf16[2,192,768]{2,1,0:T(8,128)(2,1)S(1)}, u32[]{:S(2)}, u32[]{:S(2)}) collective-permute-start(bf16[2,192,768]{2,1,0:T(8,128)(2,1)} %copy-done.13), channel_id=1, source_target_pairs={{0,2},{1,3},{2,0},{3,1},{4,6},{5,7},{6,4},{7,5},{8,10},{9,11},{10,... | collective-permute-start | bytes 1769480 | tf_op jit(solution)/shard_map/ppermute | solution.py:659
  89.1 2.6 %collective-permute-start.2 = (bf16[128,768]{1,0:T(8,128)(2,1)S(1)}, bf16[128,768]{1,0:T(8,128)(2,1)S(1)}, u32[]{:S(2)}, u32[]{:S(2)}) collective-permute-start(bf16[128,768]{1,0:T(8,128)(2,1)S(1)} %get-tuple-element.44.grads.own), channel_id=1, source_target_pairs={{0,1},{1,0},{2,3},{3,2},{4,5},{5,4},{6,7},{7,6},{8,9},{9,8},{10,11... | collective-permute-start | bytes 589832 | tf_op jit(solution)/shard_map/ppermute | solution.py:442
  89.7 21.8 %collective-permute-start.7 = (bf16[128,768]{1,0:T(8,128)(2,1)S(1)}, bf16[128,768]{1,0:T(8,128)(2,1)S(1)}, u32[]{:S(2)}, u32[]{:S(2)}) collective-permute-start(bf16[128,768]{1,0:T(8,128)(2,1)S(1)} %get-tuple-element.44.grads.own), channel_id=1, source_target_pairs={{1,2},{3,4},{5,6},{7,8},{9,10},{11,12},{13,14},{2,1},{4,3},{6,5},{... | collective-permute-start | bytes 589832 | tf_op jit(solution)/shard_map/ppermute | solution.py:443

commit v7 on v6

--- a/solution.py
+++ b/solution.py
@@ -176,7 +176,7 @@
 
 
 def rim_conv_kernel(
-    planes, height, core, inner, outer, split, partial, gain, bias, normed, unit, inv, spread, conv
+    planes, height, core, inner, outer, split, partial, gain, bias, normed, centered, spread, conv
 ):
     step = pl.program_id(0)
 
@@ -208,11 +208,10 @@
             tree_sum([part * part for part in parts]), axis=1, keepdims=True
         ) * (1.0 / channels)
         inverse = lax.rsqrt(variance + norm_eps)
-        inv[...] = jnp.broadcast_to(inverse, inv.shape)
         for k in range(tiles):
             lanes = slice(k * LANES, (k + 1) * LANES)
+            centered[:, lanes] = parts[k]
             value = parts[k] * inverse
-            unit[:, lanes] = value
             whole = (value * gains[:, lanes] + biases[:, lanes]).astype(BF16)
             for copy in range(normed.shape[0]):
                 normed[copy, :, lanes] = whole
@@ -236,7 +235,7 @@
 
 
 def kernel_grad_kernel(
-    planes, height, core, inner, own, outer, grads, small, out, spread, products, joined, flat
+    planes, height, which, inner, own, outer, grads, small, out, spread, products, joined, flat
 ):
     @pl.when(pl.program_id(0) == 0)
     def _():
@@ -247,7 +246,7 @@
     def stage(left, right):
         stage_source(all_planes(left, own, right, planes), height, spread)
 
-    by_core(core, inner, outer, stage)
+    by_core(which, inner, outer, stage)
     upstream = []
     for x in range(planes):
         plane = grads[x * height * SUB : (x + 1) * height * SUB, :].astype(F32)
@@ -280,8 +279,7 @@
     normed,
     weight_in,
     weight_out,
-    unit,
-    inv,
+    centered,
     norm_gain,
     layer_scale,
     voxels,
@@ -328,7 +326,10 @@
         block_out[...] = (voxels[...].astype(F32) + scale * whole).astype(BF16)
         scale_local = jnp.sum(cotangent[...].astype(F32) * whole, axis=0, keepdims=True)
         grad = back[...]
-        one = unit[...]
+        deviation = centered[...]
+        variance = jnp.sum(deviation * deviation, axis=1, keepdims=True) * (1.0 / channels)
+        inverse = lax.rsqrt(variance + norm_eps)
+        one = deviation * inverse
         bias_local = jnp.sum(grad, axis=0, keepdims=True)
         gain_local = jnp.sum(grad * one, axis=0, keepdims=True)
         small[...] = jnp.concatenate(
@@ -337,7 +338,7 @@
         scaled = grad * gain
         average = jnp.sum(scaled, axis=1, keepdims=True) * (1.0 / channels)
         slant = jnp.sum(scaled * one, axis=1, keepdims=True) * (1.0 / channels)
-        conv_grad[...] = (inv[:, :1] * (scaled - average - one * slant)).astype(BF16)
+        conv_grad[...] = (inverse * (scaled - average - one * slant)).astype(BF16)
 
 
 def slopes(hidden, act_grad):
@@ -408,19 +409,25 @@
         out[copy] = total
 
 
-def unpack_kernel(parts, out, *small):
-    piece = parts.shape[1]
-    for k in range(-(-TAP_ROWS // piece)):
-        first = k * piece
-        length = min(piece, TAP_ROWS - first)
-        out[first : first + length, :] = parts[k].astype(F32)[:length, :]
-    k = TAP_ROWS // piece
-    first = TAP_ROWS - k * piece
-    rows = parts[k].astype(F32)
-    if first + SUB > piece:
-        rows = jnp.concatenate([rows, parts[k + 1].astype(F32)], axis=0)
-    for k, line in enumerate(small):
-        line[...] = rows[first + k : first + k + 1, :].reshape(line.shape)
+def unpack_kernel(core, own, other, out, *small):
+    piece, wide = own.shape[1:]
+
+    def unpack(*halves):
+        last = []
+        for side, parts in enumerate(halves):
+            lanes = slice(side * wide, (side + 1) * wide)
+            for k in range(-(-TAP_ROWS // piece)):
+                first = k * piece
+                length = min(piece, TAP_ROWS - first)
+                out[first : first + length, lanes] = parts[k].astype(F32)[:length, :]
+            k = TAP_ROWS // piece
+            last.append(parts[k].astype(F32))
+        rows = jnp.concatenate(last, axis=1)
+        first = TAP_ROWS % piece
+        for k, line in enumerate(small):
+            line[...] = rows[first + k : first + k + 1, :].reshape(line.shape)
+
+    by_core(core, own, other, lambda outer, inner: unpack(inner, outer))
 
 
 def params(limit=48):
@@ -466,10 +473,10 @@
 
     inner, outer = rims(own)
 
-    upstream_line = [upstream] + [
-        lax.ppermute(upstream, "row", [(i, (i + quad * k) % count) for i in range(count)])
-        for k in range(1, line)
-    ]
+    def next_in_line(cells):
+        return lax.ppermute(cells, "row", [(i, (i + quad) % count) for i in range(count)])
+
+    upstream_line = [upstream, next_in_line(upstream)]
 
     def spread_of(held):
         return pltpu.VMEM((9, held, PAD, LANES), F32)
@@ -490,7 +497,9 @@
         name="own_conv",
     )(own, dw_kernel)
 
-    normed, unit, inv = pl.pallas_call(
+    partial, upstream_line[1] = lax.optimization_barrier((partial, upstream_line[1]))
+    upstream_line.append(next_in_line(upstream_line[1]))
+    normed, centered = pl.pallas_call(
         functools.partial(rim_conv_kernel, planes, height),
         grid_spec=pltpu.PrefetchScalarGridSpec(
             num_scalar_prefetch=1,
@@ -506,20 +515,21 @@
             out_specs=[
                 whole_block(line, rows, channels),
                 whole_block(rows, channels),
-                whole_block(rows, LANES),
             ],
             scratch_shapes=[spread_of(2 * MARGIN), pltpu.VMEM((tiles, rows, LANES), F32)],
         ),
         out_shape=[
             jax.ShapeDtypeStruct((line, rows, channels), BF16),
             jax.ShapeDtypeStruct((rows, channels), F32),
-            jax.ShapeDtypeStruct((rows, LANES), F32),
         ],
         compiler_params=params(),
         cost_estimate=NO_COST,
         name="rim_conv",
     )(parity, inner, outer, split, partial, norm_gain, norm_bias)
 
+    centered, upstream_line[2] = lax.optimization_barrier((centered, upstream_line[2]))
+    for _ in range(3, line):
+        upstream_line.append(next_in_line(upstream_line[-1]))
     gathered = lax.all_to_all(
         normed, "row", split_axis=0, concat_axis=0, tiled=True, axis_index_groups=lines
     )
@@ -534,7 +544,6 @@
             pl.BlockSpec((block, channels), lambda f: (f, 0)),
             pl.BlockSpec((block, channels), lambda f: (f, 0)),
             whole,
-            whole_block(rows, LANES),
             whole_block(channels),
             whole_block(channels),
             whole,
@@ -558,36 +567,48 @@
         compiler_params=params(),
         cost_estimate=NO_COST,
         name="mlp_both_ways",
-    )(normed, weight_in, weight_out, unit, inv, norm_gain, layer_scale, own, upstream)
-
-    piece = -(-(TAP_ROWS + SUB) // count)
-    piece += -piece % SUB
-    padded = piece * count
-    sums = pl.pallas_call(
-        functools.partial(kernel_grad_kernel, planes, height),
-        grid_spec=pltpu.PrefetchScalarGridSpec(
-            num_scalar_prefetch=1,
-            grid=(tiles,),
-            in_specs=[
-                lane_block(rows),
-                lane_block(rows),
-                lane_block(rows),
-                lane_block(rows),
-                lane_block(SUB),
-            ],
-            out_specs=lane_block(padded),
-            scratch_shapes=[
-                spread_of(2 * MARGIN + planes),
-                pltpu.VMEM((2, KS, SUB * SUB, LANES), F32),
-                pltpu.VMEM((9, KS, SUB, LANES), F32),
-                pltpu.VMEM((padded, LANES), F32),
-            ],
-        ),
-        out_shape=jax.ShapeDtypeStruct((padded, channels), BF16),
-        compiler_params=params(),
-        cost_estimate=NO_COST,
-        name="kernel_grad_terms",
-    )(parity, inner, own, outer, conv_grad, small)
+    )(normed, weight_in, weight_out, centered, norm_gain, layer_scale, own, upstream)
+
+    grad_inner, grad_outer = rims(conv_grad)
+
+    half = count // 2
+    alike = [[2 * k + p for k in range(half)] for p in range(2)]
+    half_tiles = tiles // 2
+    wide = half_tiles * LANES
+    piece = -(-(TAP_ROWS + SUB) // half)
+    piece += -piece % (2 * SUB)
+    padded = piece * half
+
+    def kernel_grad_half(side, name):
+        def at(block_rows):
+            return pl.BlockSpec((block_rows, LANES), lambda c, w: (0, w[1] * half_tiles + c))
+
+        return pl.pallas_call(
+            functools.partial(kernel_grad_kernel, planes, height),
+            grid_spec=pltpu.PrefetchScalarGridSpec(
+                num_scalar_prefetch=1,
+                grid=(half_tiles,),
+                in_specs=[at(rows), at(rows), at(rows), at(rows), at(SUB)],
+                out_specs=pl.BlockSpec((padded, LANES), lambda c, w: (0, c)),
+                scratch_shapes=[
+                    spread_of(2 * MARGIN + planes),
+                    pltpu.VMEM((2, KS, SUB * SUB, LANES), F32),
+                    pltpu.VMEM((9, KS, SUB, LANES), F32),
+                    pltpu.VMEM((padded, LANES), F32),
+                ],
+            ),
+            out_shape=jax.ShapeDtypeStruct((padded, wide), BF16),
+            compiler_params=params(),
+            cost_estimate=NO_COST,
+            name=name,
+        )(jnp.stack([core, side]), inner, own, outer, conv_grad, small)
+
+    half_sent = kernel_grad_half(1 - core, "kernel_grad_other_half")
+    half_got = lax.ppermute(half_sent, "row", other_core)
+    half_kept = kernel_grad_half(core, "kernel_grad_own_half")
+    half_got, grad_inner, grad_outer = lax.optimization_barrier((half_got, grad_inner, grad_outer))
+    sums = (half_kept.astype(F32) + half_got.astype(F32)).astype(BF16)
+
     share = units // count
     tokens = line * rows
     base = me // quad * quad
@@ -615,11 +636,15 @@
     cotangents = [whole_block(rows, channels)] * line
     aligned = [pltpu.VMEM((tokens, channels), BF16)]
 
-    which, sums, conv_grad = lax.optimization_barrier((which, sums, conv_grad))
+    which, sums = lax.optimization_barrier((which, sums))
     scattered = lax.all_to_all(
-        sums.reshape(count, piece, channels), "row", split_axis=0, concat_axis=0, tiled=True
-    )
-    grad_inner, grad_outer = rims(conv_grad)
+        sums.reshape(half, piece, wide),
+        "row",
+        split_axis=0,
+        concat_axis=0,
+        tiled=True,
+        axis_index_groups=alike,
+    )
     for_other = pl.pallas_call(
         other_core_terms_kernel,
         grid_spec=pltpu.PrefetchScalarGridSpec(
@@ -634,7 +659,23 @@
         cost_estimate=NO_COST,
         name="weight_grads_other_core",
     )(which, weight_in, weight_out, layer_scale, gathered, *upstream_line)
+    scattered, for_other = lax.optimization_barrier((scattered, for_other))
     from_other = lax.ppermute(for_other, "row", other_core)
+    copies = pl.pallas_call(
+        spread_sum_kernel,
+        in_specs=[whole_block(half, piece, wide)],
+        out_specs=whole_block(half, piece, wide),
+        out_shape=jax.ShapeDtypeStruct((half, piece, wide), BF16),
+        grid=(1,),
+        compiler_params=params(),
+        cost_estimate=NO_COST,
+        name="kernel_grad_sum",
+    )(scattered)
+    which, copies = lax.optimization_barrier((which, copies))
+    totals = lax.all_to_all(
+        copies, "row", split_axis=0, concat_axis=0, tiled=True, axis_index_groups=alike
+    )
+    other_totals = lax.ppermute(totals, "row", other_core)
 
     sent, kept = pl.pallas_call(
         own_core_terms_kernel,
@@ -658,19 +699,7 @@
     )(which, weight_in, weight_out, layer_scale, gathered, from_other, *upstream_line)
     got = lax.ppermute(sent, "row", other_side)
 
-    scattered, kept = lax.optimization_barrier((scattered, kept))
-    copies = pl.pallas_call(
-        spread_sum_kernel,
-        in_specs=[whole_block(count, piece, channels)],
-        out_specs=whole_block(count, piece, channels),
-        out_shape=jax.ShapeDtypeStruct((count, piece, channels), BF16),
-        grid=(1,),
-        compiler_params=params(),
-        cost_estimate=NO_COST,
-        name="kernel_grad_sum",
-    )(scattered)
-    conv_own, copies = lax.optimization_barrier((conv_grad, copies))
-    totals = lax.all_to_all(copies, "row", split_axis=0, concat_axis=0, tiled=True)
+    conv_own, kept = lax.optimization_barrier((conv_grad, kept))
     voxel_grad = pl.pallas_call(
         functools.partial(input_grad_kernel, planes, height),
         grid_spec=pltpu.PrefetchScalarGridSpec(
@@ -694,17 +723,18 @@
 
     kernel_grad, *vector_grads = pl.pallas_call(
         unpack_kernel,
-        grid=(1,),
-        in_specs=[whole_block(count, piece, channels)],
-        out_specs=[whole_block(TAP_ROWS, channels)] + [whole_block(channels)] * 3,
-        out_shape=[
-            jax.ShapeDtypeStruct((TAP_ROWS, channels), F32),
-        ]
+        grid_spec=pltpu.PrefetchScalarGridSpec(
+            num_scalar_prefetch=1,
+            grid=(1,),
+            in_specs=[whole_block(half, piece, wide)] * 2,
+            out_specs=[whole_block(TAP_ROWS, channels)] + [whole_block(channels)] * 3,
+        ),
+        out_shape=[jax.ShapeDtypeStruct((TAP_ROWS, channels), F32)]
         + [jax.ShapeDtypeStruct((channels,), F32)] * 3,
         compiler_params=params(),
         cost_estimate=NO_COST,
         name="kernel_grad_unpack",
-    )(totals)
+    )(parity, totals, other_totals)
 
     weight_in_grad, weight_out_grad = pl.pallas_call(
         last_sum_kernel,

time: 122 us -> 124 us (1.016)
  waiting for transfers between devices: 40.1 us -> 36.2 us
  other arithmetic: 0.01 us -> 1.92 us
  Pallas kernels: 40.6 us -> 42.3 us
  starting transfers between devices: 31.2 us -> 32.7 us
    ppermute x3 -> x5, waiting for transfers between devices: 11.6 us -> 31.2 us  [the longest x3 30 us: next_in_line(): lax.ppermute(cells, 'row', [(i, (i + quad) % count) for i in range(count)])]
    ppermute x2, waiting for transfers between devices: 20.6 us -> 1.34 us  [rims(): lax.ppermute(cells, 'row', between + [(j, i) for i, j in between])]
    all_to_all x2, waiting for transfers between devices: 7.91 us -> 0.25 us  [the longest x1 0.25 us: on_device(): lax.all_to_all(copies, 'row', split_axis=0, concat_axis=0, tiled=True, ax...]
    ppermute x1, waiting for transfers between devices: 0.01 us -> 3.45 us  [on_device(): got = lax.ppermute(sent, 'row', other_side)]
    ppermute x3 -> x5, starting transfers between devices: 4.73 us -> 7.3 us  [the longest x3 5.1 us: next_in_line(): lax.ppermute(cells, 'row', [(i, (i + quad) % count) for i in range(count)])]
    all_to_all x2, starting transfers between devices: 11.9 us -> 9.94 us  [the longest x1 6.52 us: on_device(): lax.all_to_all(sums.reshape(half, piece, wide), 'row', split_axis=0, conc...]
    ppermute x1, starting transfers between devices: 0.03 us -> 1.84 us  [on_device(): from_other = lax.ppermute(for_other, 'row', other_core)]
    convert_element_type x0 -> x1, other arithmetic: none -> 1.76 us  [on_device(): sums = (half_kept.astype(F32) + half_got.astype(F32)).astype(BF16)]
  transfers between devices with their start and end apart: 12 -> 14, of which waited for: 4 -> 6; matrix products, arithmetic and copies ran while one was open for 0% -> 2% of each run, Pallas kernels for 25% -> 31%
where the time goes in v7:
time: 124 us; the launch traced here: 122 us
  Pallas kernels  42.3 us (34%)
  waiting for transfers between devices  36.2 us (29%)
  starting transfers between devices  32.7 us (26%)
  local copies, waits for them, and re-layouts  8.37 us (7%)
  other arithmetic  1.92 us (2%)
    ppermute x3, waiting for transfers between devices, next_in_line(): lax.ppermute(cells, 'row', [(i, (i + quad) % count) for i in range(count)])  30 us
    pallas_call x1, Pallas kernels, on_device(): pl.pallas_call(mlp_kernel, grid=(units // block,), in_specs=[pl.BlockSpec...  9.41 us
    unnamed x32, local copies, waits for them, and re-layouts  8.29 us
    pallas_call x1, Pallas kernels, on_device(): pl.pallas_call(functools.partial(input_grad_kernel, planes, height), grid...  6.98 us
    pallas_call x2, Pallas kernels, kernel_grad_half(): pl.pallas_call(functools.partial(kernel_grad_kernel, planes, height), gri...  6.91 us
    all_to_all x1, starting transfers between devices, on_device(): lax.all_to_all(sums.reshape(half, piece, wide), 'row', split_axis=0, conc...  6.52 us
    pallas_call x1, Pallas kernels, on_device(): pl.pallas_call(own_core_terms_kernel, grid_spec=pltpu.PrefetchScalarGridS...  5.98 us
    ppermute x2, starting transfers between devices, rims(): lax.ppermute(cells, 'row', between + [(j, i) for i, j in between])  5.73 us
  transfers between devices with their start and end apart: 14, of which 6 were waited for; matrix products, arithmetic and copies ran while one was open for 2% of the time, Pallas kernels for 31%

profile of v7, /device:TPU:1, one launch (start us, length us, event | category | flops | bytes accessed | tf_op | source)
XLA Modules:
  0.0 122.4 jit_solution(2326592563902036950)
XLA Ops:
  0.7 2.2 %collective-permute-start.2 = (bf16[128,768]{1,0:T(8,128)(2,1)}, bf16[128,768]{1,0:T(8,128)(2,1)S(1)}, u32[]{:S(2)}, u32[]{:S(2)}) collective-permute-start(bf16[128,768]{1,0:T(8,128)(2,1)} %bitcast.17), channel_id=1, source_target_pairs={{0,4},{1,5},{2,6},{3,7},{4,8},{5,9},{6,10},{7,11},{8,12},{9,13},{1... | collective-permute-start | bytes 589832 | tf_op jit(solution)/shard_map/ppermute | solution.py:477
  2.8 1.0 collective-permute-start
  3.8 3.0 %collective-permute-start.1 = (bf16[128,768]{1,0:T(8,128)(2,1)}, bf16[128,768]{1,0:T(8,128)(2,1)S(1)}, u32[]{:S(2)}, u32[]{:S(2)}) collective-permute-start(bf16[128,768]{1,0:T(8,128)(2,1)} %bitcast.12), channel_id=1, source_target_pairs={{1,2},{3,4},{5,6},{7,8},{9,10},{11,12},{13,14},{2,1},{4,3},{6,5},{... | collective-permute-start | bytes 589832 | tf_op jit(solution)/shard_map/ppermute | solution.py:450
  6.8 0.0 copy-start
  6.8 0.9 copy-done
  7.8 1.2 %copy-done.6 = f32[343,768]{1,0:T(8,128)S(1)} copy-done((f32[343,768]{1,0:T(8,128)S(1)}, f32[343,768]{1,0:T(8,128)}, u32[]{:S(2)}) %copy-start.6) | copy-done | bytes 1053720
  9.0 2.1 %own_conv.1 = (f32[128,768]{1,0:T(8,128)S(1)}, f32[6,9,7,8,128]{4,3,2,1,0:T(8,128)S(1)}) custom-call(bf16[128,768]{1,0:T(8,128)(2,1)S(1)} %bitcast.13, f32[343,768]{1,0:T(8,128)S(1)} %copy-done.6), custom_call_target="tpu_custom_call" | custom-call | tf_op jit(solution)/shard_map/own_conv/pallas_call | solution.py:485
  11.2 0.0 collective-permute-done.inner
  11.2 0.0 collective-permute-done.1.outer
  11.2 3.7 %rim_conv.1 = (bf16[4,128,768]{2,1,0:T(8,128)(2,1)}, f32[128,768]{1,0:T(8,128)S(1)}) custom-call(s32[1]{0:T(128)} %bitcast.core, bf16[128,768]{1,0:T(8,128)(2,1)S(1)} %collective-permute-done.inner, bf16[128,768]{1,0:T(8,128)(2,1)S(1)} %collective-permute-done.1.outer, f32[6,9,7,8,128]{4,3,2,1,0:T(8,128)S(1)} %get-tuple-element.38.split, ...), custom_call_target="tpu_custom_call" | custom-call | tf_op jit(solution)/shard_map/rim_conv/pallas_call | solution.py:502
  14.9 0.7 copy-done.11
  15.6 5.6 %all-to-all-start.1 = ((bf16[4,128,768]{2,1,0:T(8,128)(2,1)}), bf16[4,128,768]{2,1,0:T(8,128)(2,1)S(1)}, u32[]{:S(2)}, u32[]{:S(2)}) async-start(bf16[4,128,768]{2,1,0:T(8,128)(2,1)} %get-tuple-element.41.normed), calls=%async_computation.1 | async-start | bytes 1572864 | tf_op jit(solution)/shard_map/all_to_all | solution.py:533
  21.2 1.5 %collective-permute-start.3 = (bf16[128,768]{1,0:T(8,128)(2,1)S(1)}, bf16[128,768]{1,0:T(8,128)(2,1)S(1)}, u32[]{:S(2)}, u32[]{:S(2)}) collective-permute-start(bf16[128,768]{1,0:T(8,128)(2,1)S(1)} %collective-permute-done.2.rest_1_), channel_id=1, source_target_pairs={{0,4},{1,5},{2,6},{3,7},{4,8},{5,9},{6,10},{7,11},{8,12},{9,13},{1... | collective-permute-start | bytes 589832 | tf_op jit(solution)/shard_map/ppermute | solution.py:477
  22.7 0.1 pad_add_fusion.which
  22.7 19.2 %collective-permute-done.3.rest_2_ = bf16[128,768]{1,0:T(8,128)(2,1)S(1)} collective-permute-done((bf16[128,768]{1,0:T(8,128)(2,1)S(1)}, bf16[128,768]{1,0:T(8,128)(2,1)S(1)}, u32[]{:S(2)}, u32[]{:S(2)}) %collective-permute-start.3) | collective-permute-done | bytes 196640 | tf_op jit(solution)/shard_map/ppermute | solution.py:477
  42.0 0.7 copy-done.7
  42.6 1.0 copy-done.12
  43.6 9.4 %mlp_both_ways.1 = (bf16[128,768]{1,0:T(8,128)(2,1)}, bf16[128,768]{1,0:T(8,128)(2,1)S(1)}, f32[8,768]{1,0:T(8,128)S(1)}) custom-call(bf16[4,128,768]{2,1,0:T(8,128)(2,1)} %get-tuple-element.41.normed, bf16[3072,768]{1,0:T(8,128)(2,1)} %weight_in.5, bf16[3072,768]{1,0:T(8,128)(2,1)} %weight_out.5, f32[128,768]{1,0:T(8,128)S(1)} %copy-done.12, ...), custom_call_target="tpu_custom_call" | custom-call | tf_op jit(solution)/shard_map/mlp_both_ways/pallas_call | solution.py:539
  53.0 3.8 %kernel_grad_other_half.1 = bf16[384,384]{1,0:T(8,128)(2,1)} custom-call(s32[2]{0:T(128)S(1)} %pad_add_fusion.which, bf16[128,768]{1,0:T(8,128)(2,1)S(1)} %collective-permute-done.inner, bf16[128,768]{1,0:T(8,128)(2,1)S(1)} %bitcast.15, bf16[128,768]{1,0:T(8,128)(2,1)S(1)} %collective-permute-done.1.outer, bf16[128,768]{1,0:T(8,128)(2,1)S(1)} %get-tuple-element.57.grads.own, ...), custom_call_target="tpu_custom_call" | custom-call | tf_op jit(solution)/shard_map/kernel_grad_other_half/pallas_call | solution.py:586
  56.8 1.3 %collective-permute-start.4 = (bf16[384,384]{1,0:T(8,128)(2,1)}, bf16[384,384]{1,0:T(8,128)(2,1)}, u32[]{:S(2)}, u32[]{:S(2)}) collective-permute-start(bf16[384,384]{1,0:T(8,128)(2,1)} %kernel_grad_other_half.1), channel_id=1, source_target_pairs={{0,1},{1,0},{2,3},{3,2},{4,5},{5,4},{6,7},{7,6},{8,9},{9,8},{10,11... | collective-permute-start | bytes 884744 | tf_op jit(solution)/shard_map/ppermute | solution.py:607
  58.1 2.7 %collective-permute-start.6 = (bf16[128,768]{1,0:T(8,128)(2,1)S(1)}, bf16[128,768]{1,0:T(8,128)(2,1)}, u32[]{:S(2)}, u32[]{:S(2)}) collective-permute-start(bf16[128,768]{1,0:T(8,128)(2,1)S(1)} %get-tuple-element.57.grads.own), channel_id=1, source_target_pairs={{1,2},{3,4},{5,6},{7,8},{9,10},{11,12},{13,14},{2,1},{4,3},{6,5},{... | collective-permute-start | bytes 589832 | tf_op jit(solution)/shard_map/ppermute | solution.py:450
  60.9 0.1 concatenate.3.which
  61.0 0.1 pad_add_fusion.1.which
  61.0 3.2 %kernel_grad_own_half.1 = bf16[384,384]{1,0:T(8,128)(2,1)S(1)} custom-call(s32[2]{0:T(128)S(1)} %pad_add_fusion.1.which, bf16[128,768]{1,0:T(8,128)(2,1)S(1)} %collective-permute-done.inner, bf16[128,768]{1,0:T(8,128)(2,1)S(1)} %bitcast.16, bf16[128,768]{1,0:T(8,128)(2,1)S(1)} %collective-permute-done.1.outer, ...), custom_call_target="tpu_custom_call" | custom-call | tf_op jit(solution)/shard_map/kernel_grad_own_half/pallas_call | solution.py:586
  64.2 0.0 copy-start.8
  64.2 1.3 %collective-permute-done.6.outer = bf16[128,768]{1,0:T(8,128)(2,1)} collective-permute-done((bf16[128,768]{1,0:T(8,128)(2,1)S(1)}, bf16[128,768]{1,0:T(8,128)(2,1)}, u32[]{:S(2)}, u32[]{:S(2)}) %collective-permute-start.6) | collective-permute-done | bytes 196640 | tf_op jit(solution)/shard_map/ppermute | solution.py:450
  65.6 1.8 %add_convert_fusion = bf16[384,384]{1,0:T(8,128)(2,1)} fusion(bf16[384,384]{1,0:T(8,128)(2,1)} %collective-permute-done.4, bf16[384,384]{1,0:T(8,128)(2,1)S(1)} %kernel_grad_own_half.1), kind=kLoop, calls=%fused_computation | loop fusion | flops 589824 | bytes 884736 | tf_op jit(solution)/shard_map/convert_element_type | solution.py:610
  67.3 6.5 %all-to-all-start = ((bf16[8,48,384]{2,1,0:T(8,128)(2,1)}), bf16[8,48,384]{2,1,0:T(8,128)(2,1)S(1)}, u32[]{:S(2)}, u32[]{:S(2)}) async-start(bf16[8,48,384]{2,1,0:T(8,128)(2,1)} %bitcast.22), calls=%async_computation | async-start | bytes 589824 | tf_op jit(solution)/shard_map/all_to_all | solution.py:640
  73.8 1.5 %collective-permute-start.7 = (bf16[128,768]{1,0:T(8,128)(2,1)S(1)}, bf16[128,768]{1,0:T(8,128)(2,1)S(1)}, u32[]{:S(2)}, u32[]{:S(2)}) collective-permute-start(bf16[128,768]{1,0:T(8,128)(2,1)S(1)} %copy-done.8), channel_id=1, source_target_pairs={{0,4},{1,5},{2,6},{3,7},{4,8},{5,9},{6,10},{7,11},{8,12},{9,13},{1... | collective-permute-start | bytes 589832 | tf_op jit(solution)/shard_map/ppermute | solution.py:477
  75.3 10.8 %collective-permute-done.7.rest_3_ = bf16[128,768]{1,0:T(8,128)(2,1)S(1)} collective-permute-done((bf16[128,768]{1,0:T(8,128)(2,1)S(1)}, bf16[128,768]{1,0:T(8,128)(2,1)S(1)}, u32[]{:S(2)}, u32[]{:S(2)}) %collective-permute-start.7) | collective-permute-done | bytes 196640 | tf_op jit(solution)/shard_map/ppermute | solution.py:477
  86.0 4.3 %weight_grads_other_core.1 = bf16[2,2,192,768]{3,2,1,0:T(8,128)(2,1)S(1)} custom-call(s32[8]{0:T(128)S(1)} %concatenate.3.which, bf16[3072,768]{1,0:T(8,128)(2,1)} %weight_in.5, bf16[3072,768]{1,0:T(8,128)(2,1)} %weight_out.5, f32[768]{0:T(1024)S(1)} %copy-done.13, bf16[4,128,768]{2,1,0:T(8,128)(2,1)S(1)} %all-to-all-done.1.normed, ...), custom_call_target="tpu_custom_call" | custom-call | tf_op jit(solution)/shard_map/weight_grads_other_core/pallas_call | solution.py:648
  90.4 1.0 copy-done.5
  91.4 0.7 copy-done.9
  92.1 1.8 %collective-permute-start.8 = (bf16[2,2,192,768]{3,2,1,0:T(8,128)(2,1)}, bf16[2,2,192,768]{3,2,1,0:T(8,128)(2,1)}, u32[]{:S(2)}, u32[]{:S(2)}) collective-permute-start(bf16[2,2,192,768]{3,2,1,0:T(8,128)(2,1)} %copy-done.5), channel_id=1, source_target_pairs={{0,1},{1,0},{2,3},{3,2},{4,5},{5,4},{6,7},{7,6},{8,9},{9,8},{10,11... | collective-permute-start | bytes 3538952 | tf_op jit(solution)/shard_map/ppermute | solution.py:663
  94.0 0.8 kernel_grad_sum.1
  94.7 3.4 %all-to-all-start.2 = ((bf16[8,48,384]{2,1,0:T(8,128)(2,1)}), bf16[8,48,384]{2,1,0:T(8,128)(2,1)S(1)}, u32[]{:S(2)}, u32[]{:S(2)}) async-start(bf16[8,48,384]{2,1,0:T(8,128)(2,1)} %kernel_grad_sum.1), calls=%async_computation.2 | async-start | bytes 589824 | tf_op jit(solution)/shard_map/all_to_all | solution.py:675
  98.2 0.0 copy-start.10
  98.2 0.9 copy-done.10
  99.1 6.0 %weight_grads_own_core.1 = (bf16[2,192,768]{2,1,0:T(8,128)(2,1)}, f32[2,192,768]{2,1,0:T(8,128)S(1)}) custom-call(s32[8]{0:T(128)S(1)} %concatenate.3.which, bf16[3072,768]{1,0:T(8,128)(2,1)} %weight_in.5, bf16[3072,768]{1,0:T(8,128)(2,1)} %weight_out.5, f32[768]{0:T(1024)S(1)} %copy-done.13, bf16[4,128,768]{2,1,0:T(8,128)(2,1)S(1)} %all-to-all-done.1.normed, ...), custom_call_target="tpu_custom_call" | custom-call | tf_op jit(solution)/shard_map/weight_grads_own_core/pallas_call | solution.py:680
  105.1 1.0 copy-done.3
  106.1 1.4 %collective-permute-start.10 = (bf16[2,192,768]{2,1,0:T(8,128)(2,1)}, bf16[2,192,768]{2,1,0:T(8,128)(2,1)S(1)}, u32[]{:S(2)}, u32[]{:S(2)}) collective-permute-start(bf16[2,192,768]{2,1,0:T(8,128)(2,1)} %get-tuple-element.65), channel_id=1, source_target_pairs={{0,2},{1,3},{2,0},{3,1},{4,6},{5,7},{6,4},{7,5},{8,10},{9,11},{10,... | collective-permute-start | bytes 1769480 | tf_op jit(solution)/shard_map/ppermute | solution.py:700
  107.5 0.2 all-to-all-done.2.own
  107.7 0.9 collective-permute-start.9
  108.6 1.2 collective-permute-done.9.other
  109.8 1.1 kernel_grad_unpack.1
  110.9 7.0 %input_grad_conv.1 = bf16[128,768]{1,0:T(8,128)(2,1)} custom-call(s32[1]{0:T(128)} %bitcast.core, bf16[128,768]{1,0:T(8,128)(2,1)} %collective-permute-done.5.inner, bf16[128,768]{1,0:T(8,128)(2,1)S(1)} %get-tuple-element.57.grads.own, bf16[128,768]{1,0:T(8,128)(2,1)} %collective-permute-done.6.outer, f32[6,9,7,8,128]{4,3,2,1,0:T(8,128)S(1)} %get-tuple-element.38.split, ...), custom_call_target="tpu_custom_call" | custom-call | tf_op jit(solution)/shard_map/input_grad_conv/pallas_call | solution.py:703
  117.8 3.5 %collective-permute-done.10.got = bf16[2,192,768]{2,1,0:T(8,128)(2,1)S(1)} collective-permute-done((bf16[2,192,768]{2,1,0:T(8,128)(2,1)}, bf16[2,192,768]{2,1,0:T(8,128)(2,1)S(1)}, u32[]{:S(2)}, u32[]{:S(2)}) %collective-permute-start.10) | collective-permute-done | bytes 589856 | tf_op jit(solution)/shard_map/ppermute | solution.py:700
  121.3 1.1 weight_grads_sum.1
  (28 shorter events, 0.1 us)
Async XLA Ops:
  0.6 10.5 %copy-start.14 = (f32[768]{0:T(1024)S(1)}, f32[768]{0:T(1024)}, u32[]{:S(2)}) copy-start(f32[768]{0:T(1024)} %norm_gain.1) | copy-start | bytes 9220
  0.6 10.5 %copy-start.15 = (f32[768]{0:T(1024)S(1)}, f32[768]{0:T(1024)}, u32[]{:S(2)}) copy-start(f32[768]{0:T(1024)} %bias.1) | copy-start | bytes 9220
  0.7 10.5 %collective-permute-start.2 = (bf16[128,768]{1,0:T(8,128)(2,1)}, bf16[128,768]{1,0:T(8,128)(2,1)S(1)}, u32[]{:S(2)}, u32[]{:S(2)}) collective-permute-start(bf16[128,768]{1,0:T(8,128)(2,1)} %bitcast.17), channel_id=1, source_target_pairs={{0,4},{1,5},{2,6},{3,7},{4,8},{5,9},{6,10},{7,11},{8,12},{9,13},{1... | collective-permute-start | bytes 589832 | tf_op jit(solution)/shard_map/ppermute | solution.py:477
  2.8 8.3 %collective-permute-start = (bf16[128,768]{1,0:T(8,128)(2,1)}, bf16[128,768]{1,0:T(8,128)(2,1)S(1)}, u32[]{:S(2)}, u32[]{:S(2)}) collective-permute-start(bf16[128,768]{1,0:T(8,128)(2,1)} %bitcast.11), channel_id=1, source_target_pairs={{0,1},{1,0},{2,3},{3,2},{4,5},{5,4},{6,7},{7,6},{8,9},{9,8},{10,11... | collective-permute-start | bytes 589832 | tf_op jit(solution)/shard_map/ppermute | solution.py:449
  3.8 7.4 %collective-permute-start.1 = (bf16[128,768]{1,0:T(8,128)(2,1)}, bf16[128,768]{1,0:T(8,128)(2,1)S(1)}, u32[]{:S(2)}, u32[]{:S(2)}) collective-permute-start(bf16[128,768]{1,0:T(8,128)(2,1)} %bitcast.12), channel_id=1, source_target_pairs={{1,2},{3,4},{5,6},{7,8},{9,10},{11,12},{13,14},{2,1},{4,3},{6,5},{... | collective-permute-start | bytes 589832 | tf_op jit(solution)/shard_map/ppermute | solution.py:450
  6.8 0.9 copy-start
  7.8 1.2 %copy-start.6 = (f32[343,768]{1,0:T(8,128)S(1)}, f32[343,768]{1,0:T(8,128)}, u32[]{:S(2)}) copy-start(f32[343,768]{1,0:T(8,128)} %taps.1) | copy-start | bytes 3161092
  14.9 0.7 copy-start.11
  15.6 27.0 %copy-start.1 = (bf16[4,4,8,768]{3,2,1,0:T(8,128)(2,1)S(1)}, bf16[4,4,8,768]{3,2,1,0:T(8,128)(2,1)}, u32[]{:S(2)}) copy-start(bf16[4,4,8,768]{3,2,1,0:T(8,128)(2,1)} %param.8) | copy-start | bytes 589828
  15.6 27.0 %copy-start.2 = (bf16[4,4,8,768]{3,2,1,0:T(8,128)(2,1)S(1)}, bf16[4,4,8,768]{3,2,1,0:T(8,128)(2,1)}, u32[]{:S(2)}) copy-start(bf16[4,4,8,768]{3,2,1,0:T(8,128)(2,1)} %param.15) | copy-start | bytes 589828
  15.6 27.0 %copy-start.13 = (f32[768]{0:T(1024)S(1)}, f32[768]{0:T(1024)}, u32[]{:S(2)}) copy-start(f32[768]{0:T(1024)} %scale.3) | copy-start | bytes 9220
  15.6 51.7 %all-to-all-start.1 = ((bf16[4,128,768]{2,1,0:T(8,128)(2,1)}), bf16[4,128,768]{2,1,0:T(8,128)(2,1)S(1)}, u32[]{:S(2)}, u32[]{:S(2)}) async-start(bf16[4,128,768]{2,1,0:T(8,128)(2,1)} %get-tuple-element.41.normed), calls=%async_computation.1 | async-start | bytes 1572864 | tf_op jit(solution)/shard_map/all_to_all | solution.py:533
  21.2 20.8 %collective-permute-start.3 = (bf16[128,768]{1,0:T(8,128)(2,1)S(1)}, bf16[128,768]{1,0:T(8,128)(2,1)S(1)}, u32[]{:S(2)}, u32[]{:S(2)}) collective-permute-start(bf16[128,768]{1,0:T(8,128)(2,1)S(1)} %collective-permute-done.2.rest_1_), channel_id=1, source_target_pairs={{0,4},{1,5},{2,6},{3,7},{4,8},{5,9},{6,10},{7,11},{8,12},{9,13},{1... | collective-permute-start | bytes 589832 | tf_op jit(solution)/shard_map/ppermute | solution.py:477
  42.0 0.7 copy-start.7
  42.6 1.0 copy-start.12
  56.8 8.8 %collective-permute-start.4 = (bf16[384,384]{1,0:T(8,128)(2,1)}, bf16[384,384]{1,0:T(8,128)(2,1)}, u32[]{:S(2)}, u32[]{:S(2)}) collective-permute-start(bf16[384,384]{1,0:T(8,128)(2,1)} %kernel_grad_other_half.1), channel_id=1, source_target_pairs={{0,1},{1,0},{2,3},{3,2},{4,5},{5,4},{6,7},{7,6},{8,9},{9,8},{10,11... | collective-permute-start | bytes 884744 | tf_op jit(solution)/shard_map/ppermute | solution.py:607
  58.1 6.1 %collective-permute-start.5 = (bf16[128,768]{1,0:T(8,128)(2,1)S(1)}, bf16[128,768]{1,0:T(8,128)(2,1)}, u32[]{:S(2)}, u32[]{:S(2)}) collective-permute-start(bf16[128,768]{1,0:T(8,128)(2,1)S(1)} %get-tuple-element.57.grads.own), channel_id=1, source_target_pairs={{0,1},{1,0},{2,3},{3,2},{4,5},{5,4},{6,7},{7,6},{8,9},{9,8},{10,11... | collective-permute-start | bytes 589832 | tf_op jit(solution)/shard_map/ppermute | solution.py:449
  58.1 7.4 %collective-permute-start.6 = (bf16[128,768]{1,0:T(8,128)(2,1)S(1)}, bf16[128,768]{1,0:T(8,128)(2,1)}, u32[]{:S(2)}, u32[]{:S(2)}) collective-permute-start(bf16[128,768]{1,0:T(8,128)(2,1)S(1)} %get-tuple-element.57.grads.own), channel_id=1, source_target_pairs={{1,2},{3,4},{5,6},{7,8},{9,10},{11,12},{13,14},{2,1},{4,3},{6,5},{... | collective-permute-start | bytes 589832 | tf_op jit(solution)/shard_map/ppermute | solution.py:450
  64.2 9.6 %copy-start.8 = (bf16[128,768]{1,0:T(8,128)(2,1)S(1)}, bf16[128,768]{1,0:T(8,128)(2,1)}, u32[]{:S(2)}) copy-start(bf16[128,768]{1,0:T(8,128)(2,1)} %copy-done.7) | copy-start | bytes 589828
  67.3 24.8 %all-to-all-start = ((bf16[8,48,384]{2,1,0:T(8,128)(2,1)}), bf16[8,48,384]{2,1,0:T(8,128)(2,1)S(1)}, u32[]{:S(2)}, u32[]{:S(2)}) async-start(bf16[8,48,384]{2,1,0:T(8,128)(2,1)} %bitcast.22), calls=%async_computation | async-start | bytes 589824 | tf_op jit(solution)/shard_map/all_to_all | solution.py:640
  73.8 12.2 %collective-permute-start.7 = (bf16[128,768]{1,0:T(8,128)(2,1)S(1)}, bf16[128,768]{1,0:T(8,128)(2,1)S(1)}, u32[]{:S(2)}, u32[]{:S(2)}) collective-permute-start(bf16[128,768]{1,0:T(8,128)(2,1)S(1)} %copy-done.8), channel_id=1, source_target_pairs={{0,4},{1,5},{2,6},{3,7},{4,8},{5,9},{6,10},{7,11},{8,12},{9,13},{1... | collective-permute-start | bytes 589832 | tf_op jit(solution)/shard_map/ppermute | solution.py:477
  90.4 1.1 copy-start.5
  91.4 0.7 copy-start.9
  92.1 6.0 %collective-permute-start.8 = (bf16[2,2,192,768]{3,2,1,0:T(8,128)(2,1)}, bf16[2,2,192,768]{3,2,1,0:T(8,128)(2,1)}, u32[]{:S(2)}, u32[]{:S(2)}) collective-permute-start(bf16[2,2,192,768]{3,2,1,0:T(8,128)(2,1)} %copy-done.5), channel_id=1, source_target_pairs={{0,1},{1,0},{2,3},{3,2},{4,5},{5,4},{6,7},{7,6},{8,9},{9,8},{10,11... | collective-permute-start | bytes 3538952 | tf_op jit(solution)/shard_map/ppermute | solution.py:663
  94.7 13.0 %all-to-all-start.2 = ((bf16[8,48,384]{2,1,0:T(8,128)(2,1)}), bf16[8,48,384]{2,1,0:T(8,128)(2,1)S(1)}, u32[]{:S(2)}, u32[]{:S(2)}) async-start(bf16[8,48,384]{2,1,0:T(8,128)(2,1)} %kernel_grad_sum.1), calls=%async_computation.2 | async-start | bytes 589824 | tf_op jit(solution)/shard_map/all_to_all | solution.py:675
  98.2 0.9 copy-start.10
  105.1 1.1 copy-start.3
  106.1 15.2 %collective-permute-start.10 = (bf16[2,192,768]{2,1,0:T(8,128)(2,1)}, bf16[2,192,768]{2,1,0:T(8,128)(2,1)S(1)}, u32[]{:S(2)}, u32[]{:S(2)}) collective-permute-start(bf16[2,192,768]{2,1,0:T(8,128)(2,1)} %get-tuple-element.65), channel_id=1, source_target_pairs={{0,2},{1,3},{2,0},{3,1},{4,6},{5,7},{6,4},{7,5},{8,10},{9,11},{10,... | collective-permute-start | bytes 1769480 | tf_op jit(solution)/shard_map/ppermute | solution.py:700
  107.7 2.1 %collective-permute-start.9 = (bf16[8,48,384]{2,1,0:T(8,128)(2,1)S(1)}, bf16[8,48,384]{2,1,0:T(8,128)(2,1)S(1)}, u32[]{:S(2)}, u32[]{:S(2)}) collective-permute-start(bf16[8,48,384]{2,1,0:T(8,128)(2,1)S(1)} %all-to-all-done.2.own), channel_id=1, source_target_pairs={{0,1},{1,0},{2,3},{3,2},{4,5},{5,4},{6,7},{7,6},{8,9},{9,8},{10,11... | collective-permute-start | bytes 884744 | tf_op jit(solution)/shard_map/ppermute | solution.py:678
  110.9 10.4 %copy-start.4 = (f32[2,192,768]{2,1,0:T(8,128)S(1)}, f32[2,192,768]{2,1,0:T(8,128)}, u32[]{:S(2)}) copy-start(f32[2,192,768]{2,1,0:T(8,128)} %copy-done.3) | copy-start | bytes 3538948

commit v8 on v7

--- a/solution.py
+++ b/solution.py
@@ -217,7 +217,9 @@
                 normed[copy, :, lanes] = whole
 
 
-def input_grad_kernel(planes, height, core, inner, own, outer, split, cotangent, out, spread):
+def input_grad_kernel(
+    planes, height, core, inner, own, outer, taps, cotangent, out, spread, split
+):
     @pl.when(pl.program_id(0) == 0)
     def _():
         clear_rims(spread)
@@ -226,6 +228,7 @@
         stage_source(all_planes(left, own, right, planes), height, spread)
 
     by_core(core, inner, outer, stage)
+    stage_taps(taps, split)
     rows = convolve(spread, split, planes, range(2 * MARGIN + planes), True)
     for x in range(planes):
         at = x * height * SUB
@@ -235,7 +238,7 @@
 
 
 def kernel_grad_kernel(
-    planes, height, which, inner, own, outer, grads, small, out, spread, products, joined, flat
+    planes, height, which, inner, own, outer, grads, small, sent, kept, spread, products, joined, flat
 ):
     @pl.when(pl.program_id(0) == 0)
     def _():
@@ -269,10 +272,19 @@
             )
     for dx in range(KS):
         for dy, tile in enumerate(join_taps([joined[j, dx] for j in range(9)])):
-            first = dx * KS * KS + dy * KS
-            flat[first : first + SUB, :] = tile
+            row = dx * KS * KS + dy * KS
+            flat[row : row + SUB, :] = tile
     flat[TAP_ROWS : TAP_ROWS + SUB, :] = small[...]
-    out[...] = flat[...].astype(out.dtype)
+    step = pl.program_id(0)
+    half = pl.num_programs(0) // 2
+
+    @pl.when(step < half)
+    def _():
+        sent[...] = flat[...].astype(BF16)
+
+    @pl.when(step >= half)
+    def _():
+        kept[...] = flat[...].astype(BF16)
 
 
 def mlp_kernel(
@@ -403,6 +415,10 @@
         out[...] = kept[k] + got[k].astype(F32)
 
 
+def chip_sum_kernel(kept, got, out):
+    out[...] = (kept[...].astype(F32) + got[...].astype(F32)).astype(BF16)
+
+
 def spread_sum_kernel(parts, out):
     total = tree_sum([parts[k].astype(F32) for k in range(parts.shape[0])]).astype(BF16)
     for copy in range(out.shape[0]):
@@ -473,10 +489,12 @@
 
     inner, outer = rims(own)
 
-    def next_in_line(cells):
-        return lax.ppermute(cells, "row", [(i, (i + quad) % count) for i in range(count)])
-
-    upstream_line = [upstream, next_in_line(upstream)]
+    def along_line(cells, steps):
+        return lax.ppermute(cells, "row", [(i, (i + quad * steps) % count) for i in range(count)])
+
+    upstream_line = [upstream] + [None] * (line - 1)
+    upstream_line[1] = along_line(upstream, 1)
+    upstream_line[-1] = along_line(upstream, -1)
 
     def spread_of(held):
         return pltpu.VMEM((9, held, PAD, LANES), F32)
@@ -497,8 +515,11 @@
         name="own_conv",
     )(own, dw_kernel)
 
-    partial, upstream_line[1] = lax.optimization_barrier((partial, upstream_line[1]))
-    upstream_line.append(next_in_line(upstream_line[1]))
+    partial, upstream_line[1], upstream_line[-1] = lax.optimization_barrier(
+        (partial, upstream_line[1], upstream_line[-1])
+    )
+    for k in range(2, line - 1):
+        upstream_line[k] = along_line(upstream_line[k - 1], 1)
     normed, centered = pl.pallas_call(
         functools.partial(rim_conv_kernel, planes, height),
         grid_spec=pltpu.PrefetchScalarGridSpec(
@@ -527,9 +548,9 @@
         name="rim_conv",
     )(parity, inner, outer, split, partial, norm_gain, norm_bias)
 
-    centered, upstream_line[2] = lax.optimization_barrier((centered, upstream_line[2]))
-    for _ in range(3, line):
-        upstream_line.append(next_in_line(upstream_line[-1]))
+    normed, centered, upstream_line[2] = lax.optimization_barrier(
+        (normed, centered, upstream_line[2])
+    )
     gathered = lax.all_to_all(
         normed, "row", split_axis=0, concat_axis=0, tiled=True, axis_index_groups=lines
     )
@@ -579,35 +600,34 @@
     piece += -piece % (2 * SUB)
     padded = piece * half
 
-    def kernel_grad_half(side, name):
-        def at(block_rows):
-            return pl.BlockSpec((block_rows, LANES), lambda c, w: (0, w[1] * half_tiles + c))
-
-        return pl.pallas_call(
-            functools.partial(kernel_grad_kernel, planes, height),
-            grid_spec=pltpu.PrefetchScalarGridSpec(
-                num_scalar_prefetch=1,
-                grid=(half_tiles,),
-                in_specs=[at(rows), at(rows), at(rows), at(rows), at(SUB)],
-                out_specs=pl.BlockSpec((padded, LANES), lambda c, w: (0, c)),
-                scratch_shapes=[
-                    spread_of(2 * MARGIN + planes),
-                    pltpu.VMEM((2, KS, SUB * SUB, LANES), F32),
-                    pltpu.VMEM((9, KS, SUB, LANES), F32),
-                    pltpu.VMEM((padded, LANES), F32),
-                ],
-            ),
-            out_shape=jax.ShapeDtypeStruct((padded, wide), BF16),
-            compiler_params=params(),
-            cost_estimate=NO_COST,
-            name=name,
-        )(jnp.stack([core, side]), inner, own, outer, conv_grad, small)
-
-    half_sent = kernel_grad_half(1 - core, "kernel_grad_other_half")
-    half_got = lax.ppermute(half_sent, "row", other_core)
-    half_kept = kernel_grad_half(core, "kernel_grad_own_half")
-    half_got, grad_inner, grad_outer = lax.optimization_barrier((half_got, grad_inner, grad_outer))
-    sums = (half_kept.astype(F32) + half_got.astype(F32)).astype(BF16)
+    def tile_of(block_rows):
+        def at(c, w):
+            return 0, (c + w[1] * half_tiles) % tiles
+
+        return pl.BlockSpec((block_rows, LANES), at)
+
+    half_sent, half_kept = pl.pallas_call(
+        functools.partial(kernel_grad_kernel, planes, height),
+        grid_spec=pltpu.PrefetchScalarGridSpec(
+            num_scalar_prefetch=1,
+            grid=(tiles,),
+            in_specs=[tile_of(rows), tile_of(rows), tile_of(rows), tile_of(rows), tile_of(SUB)],
+            out_specs=[
+                pl.BlockSpec((padded, LANES), lambda c, w: (0, jnp.minimum(c, half_tiles - 1))),
+                pl.BlockSpec((padded, LANES), lambda c, w: (0, jnp.maximum(c - half_tiles, 0))),
+            ],
+            scratch_shapes=[
+                spread_of(2 * MARGIN + planes),
+                pltpu.VMEM((2, KS, SUB * SUB, LANES), F32),
+                pltpu.VMEM((9, KS, SUB, LANES), F32),
+                pltpu.VMEM((padded, LANES), F32),
+            ],
+        ),
+        out_shape=[jax.ShapeDtypeStruct((padded, wide), BF16)] * 2,
+        compiler_params=params(),
+        cost_estimate=NO_COST,
+        name="kernel_grad_terms",
+    )(jnp.stack([core, 1 - core]), inner, own, outer, conv_grad, small)
 
     share = units // count
     tokens = line * rows
@@ -636,15 +656,10 @@
     cotangents = [whole_block(rows, channels)] * line
     aligned = [pltpu.VMEM((tokens, channels), BF16)]
 
-    which, sums = lax.optimization_barrier((which, sums))
-    scattered = lax.all_to_all(
-        sums.reshape(half, piece, wide),
-        "row",
-        split_axis=0,
-        concat_axis=0,
-        tiled=True,
-        axis_index_groups=alike,
-    )
+    which, half_sent, half_kept, grad_inner, grad_outer = lax.optimization_barrier(
+        (which, half_sent, half_kept, grad_inner, grad_outer)
+    )
+    half_got = lax.ppermute(half_sent, "row", other_core)
     for_other = pl.pallas_call(
         other_core_terms_kernel,
         grid_spec=pltpu.PrefetchScalarGridSpec(
@@ -659,24 +674,26 @@
         cost_estimate=NO_COST,
         name="weight_grads_other_core",
     )(which, weight_in, weight_out, layer_scale, gathered, *upstream_line)
-    scattered, for_other = lax.optimization_barrier((scattered, for_other))
+    half_kept, for_other = lax.optimization_barrier((half_kept, for_other))
     from_other = lax.ppermute(for_other, "row", other_core)
-    copies = pl.pallas_call(
-        spread_sum_kernel,
-        in_specs=[whole_block(half, piece, wide)],
-        out_specs=whole_block(half, piece, wide),
-        out_shape=jax.ShapeDtypeStruct((half, piece, wide), BF16),
+    sums = pl.pallas_call(
+        chip_sum_kernel,
+        in_specs=[whole_block(padded, wide)] * 2,
+        out_specs=whole_block(padded, wide),
+        out_shape=jax.ShapeDtypeStruct((padded, wide), BF16),
         grid=(1,),
         compiler_params=params(),
         cost_estimate=NO_COST,
-        name="kernel_grad_sum",
-    )(scattered)
-    which, copies = lax.optimization_barrier((which, copies))
-    totals = lax.all_to_all(
-        copies, "row", split_axis=0, concat_axis=0, tiled=True, axis_index_groups=alike
-    )
-    other_totals = lax.ppermute(totals, "row", other_core)
-
+        name="kernel_grad_chip_sum",
+    )(half_kept, half_got)
+    scattered = lax.all_to_all(
+        sums.reshape(half, piece, wide),
+        "row",
+        split_axis=0,
+        concat_axis=0,
+        tiled=True,
+        axis_index_groups=alike,
+    )
     sent, kept = pl.pallas_call(
         own_core_terms_kernel,
         grid_spec=pltpu.PrefetchScalarGridSpec(
@@ -699,7 +716,23 @@
     )(which, weight_in, weight_out, layer_scale, gathered, from_other, *upstream_line)
     got = lax.ppermute(sent, "row", other_side)
 
-    conv_own, kept = lax.optimization_barrier((conv_grad, kept))
+    scattered, kept = lax.optimization_barrier((scattered, kept))
+    copies = pl.pallas_call(
+        spread_sum_kernel,
+        in_specs=[whole_block(half, piece, wide)],
+        out_specs=whole_block(half, piece, wide),
+        out_shape=jax.ShapeDtypeStruct((half, piece, wide), BF16),
+        grid=(1,),
+        compiler_params=params(),
+        cost_estimate=NO_COST,
+        name="kernel_grad_sum",
+    )(scattered)
+    conv_own, copies = lax.optimization_barrier((conv_grad, copies))
+    totals = lax.all_to_all(
+        copies, "row", split_axis=0, concat_axis=0, tiled=True, axis_index_groups=alike
+    )
+    other_totals = lax.ppermute(totals, "row", other_core)
+
     voxel_grad = pl.pallas_call(
         functools.partial(input_grad_kernel, planes, height),
         grid_spec=pltpu.PrefetchScalarGridSpec(
@@ -709,17 +742,20 @@
                 lane_block(rows),
                 lane_block(rows),
                 lane_block(rows),
-                split_block,
+                lane_block(TAP_ROWS),
                 lane_block(rows),
             ],
             out_specs=lane_block(rows),
-            scratch_shapes=[spread_of(2 * MARGIN + planes)],
+            scratch_shapes=[
+                spread_of(2 * MARGIN + planes),
+                pltpu.VMEM((9, KS, SUB, LANES), F32),
+            ],
         ),
         out_shape=jax.ShapeDtypeStruct((rows, channels), BF16),
         compiler_params=params(),
         cost_estimate=NO_COST,
         name="input_grad_conv",
-    )(parity, grad_inner, conv_own, grad_outer, split, upstream)
+    )(parity, grad_inner, conv_own, grad_outer, dw_kernel, upstream)
 
     kernel_grad, *vector_grads = pl.pallas_call(
         unpack_kernel,

time: 124 us -> 97.7 us (0.79)
  the two profiles are of different devices: /device:TPU:1 before, /device:TPU:0 now
where the time goes in v8:
time: 97.7 us; the launch traced here: 97 us
  Pallas kernels  39.4 us (40%)
  starting transfers between devices  28.9 us (30%)
  waiting for transfers between devices  18.5 us (19%)
  local copies, waits for them, and re-layouts  9.3 us (10%)
    pallas_call x1, Pallas kernels, on_device(): pl.pallas_call(mlp_kernel, grid=(units // block,), in_specs=[pl.BlockSpec...  9.43 us
    unnamed x34, local copies, waits for them, and re-layouts  9.21 us
    all_to_all x1, waiting for transfers between devices, on_device(): lax.all_to_all(copies, 'row', split_axis=0, concat_axis=0, tiled=True, ax...  7.55 us
    ppermute x3, starting transfers between devices, along_line(): lax.ppermute(cells, 'row', [(i, (i + quad * steps) % count) for i in rang...  6.63 us
    pallas_call x1, Pallas kernels, on_device(): pl.pallas_call(functools.partial(kernel_grad_kernel, planes, height), gri...  6.17 us
    ppermute x2, starting transfers between devices, rims(): lax.ppermute(cells, 'row', [(i, i ^ 1) for i in range(count)])  5.99 us
    pallas_call x1, Pallas kernels, on_device(): pl.pallas_call(other_core_terms_kernel, grid_spec=pltpu.PrefetchScalarGri...  5.11 us
    all_to_all x1, starting transfers between devices, on_device(): lax.all_to_all(sums.reshape(half, piece, wide), 'row', split_axis=0, conc...  5.02 us
  transfers between devices with their start and end apart: 14, of which 6 were waited for; matrix products, arithmetic and copies ran while one was open for 0% of the time, Pallas kernels for 33%

profile of v8, /device:TPU:0, one launch (start us, length us, event | category | flops | bytes accessed | tf_op | source)
XLA Modules:
  0.0 97.0 jit_solution(14037161204364076024)
XLA Ops:
  0.6 5.1 %collective-permute-start.3 = (bf16[128,768]{1,0:T(8,128)(2,1)}, bf16[128,768]{1,0:T(8,128)(2,1)S(1)}, u32[]{:S(2)}, u32[]{:S(2)}) collective-permute-start(bf16[128,768]{1,0:T(8,128)(2,1)} %bitcast.11), channel_id=1, source_target_pairs={{0,12},{1,13},{2,14},{3,15},{4,0},{5,1},{6,2},{7,3},{8,4},{9,5},{1... | collective-permute-start | bytes 589832 | tf_op jit(solution)/shard_map/ppermute | solution.py:493
  5.7 0.0 collective-permute-start.2
  5.7 0.7 collective-permute-start.1
  6.4 2.9 %collective-permute-start = (bf16[128,768]{1,0:T(8,128)(2,1)}, bf16[128,768]{1,0:T(8,128)(2,1)S(1)}, u32[]{:S(2)}, u32[]{:S(2)}) collective-permute-start(bf16[128,768]{1,0:T(8,128)(2,1)} %bitcast.18), channel_id=1, source_target_pairs={{0,1},{1,0},{2,3},{3,2},{4,5},{5,4},{6,7},{7,6},{8,9},{9,8},{10,11... | collective-permute-start | bytes 589832 | tf_op jit(solution)/shard_map/ppermute | solution.py:465
  9.3 1.2 %copy-done = f32[343,768]{1,0:T(8,128)S(1)} copy-done((f32[343,768]{1,0:T(8,128)S(1)}, f32[343,768]{1,0:T(8,128)}, u32[]{:S(2)}) %copy-start) | copy-done | bytes 1053720
  10.6 0.9 copy-done.3
  11.5 2.1 %own_conv.1 = (f32[128,768]{1,0:T(8,128)S(1)}, f32[6,9,7,8,128]{4,3,2,1,0:T(8,128)S(1)}) custom-call(bf16[128,768]{1,0:T(8,128)(2,1)S(1)} %bitcast.19, f32[343,768]{1,0:T(8,128)S(1)} %copy-done), custom_call_target="tpu_custom_call" | custom-call | tf_op jit(solution)/shard_map/own_conv/pallas_call | solution.py:503
  13.7 1.6 %collective-permute-done.2.rest_1_ = bf16[128,768]{1,0:T(8,128)(2,1)S(1)} collective-permute-done((bf16[128,768]{1,0:T(8,128)(2,1)}, bf16[128,768]{1,0:T(8,128)(2,1)S(1)}, u32[]{:S(2)}, u32[]{:S(2)}) %collective-permute-start.2) | collective-permute-done | bytes 196640 | tf_op jit(solution)/shard_map/ppermute | solution.py:493
  15.3 1.5 %collective-permute-start.4 = (bf16[128,768]{1,0:T(8,128)(2,1)S(1)}, bf16[128,768]{1,0:T(8,128)(2,1)S(1)}, u32[]{:S(2)}, u32[]{:S(2)}) collective-permute-start(bf16[128,768]{1,0:T(8,128)(2,1)S(1)} %collective-permute-done.2.rest_1_), channel_id=1, source_target_pairs={{0,4},{1,5},{2,6},{3,7},{4,8},{5,9},{6,10},{7,11},{8,12},{9,13},{1... | collective-permute-start | bytes 589832 | tf_op jit(solution)/shard_map/ppermute | solution.py:493
  16.8 0.0 collective-permute-done.1.outer
  16.9 0.0 collective-permute-done.inner
  16.9 3.6 %rim_conv.1 = (bf16[4,128,768]{2,1,0:T(8,128)(2,1)}, f32[128,768]{1,0:T(8,128)S(1)}) custom-call(s32[1]{0:T(128)} %bitcast.core, bf16[128,768]{1,0:T(8,128)(2,1)S(1)} %collective-permute-done.inner, bf16[128,768]{1,0:T(8,128)(2,1)S(1)} %collective-permute-done.1.outer, f32[6,9,7,8,128]{4,3,2,1,0:T(8,128)S(1)} %get-tuple-element.42.split, ...), custom_call_target="tpu_custom_call" | custom-call | tf_op jit(solution)/shard_map/rim_conv/pallas_call | solution.py:523
  20.5 2.4 %collective-permute-done.4.rest_2_ = bf16[128,768]{1,0:T(8,128)(2,1)S(1)} collective-permute-done((bf16[128,768]{1,0:T(8,128)(2,1)S(1)}, bf16[128,768]{1,0:T(8,128)(2,1)S(1)}, u32[]{:S(2)}, u32[]{:S(2)}) %collective-permute-start.4) | collective-permute-done | bytes 196640 | tf_op jit(solution)/shard_map/ppermute | solution.py:493
  22.9 3.5 %all-to-all-start = ((bf16[4,128,768]{2,1,0:T(8,128)(2,1)}), bf16[4,128,768]{2,1,0:T(8,128)(2,1)S(1)}, u32[]{:S(2)}, u32[]{:S(2)}) async-start(bf16[4,128,768]{2,1,0:T(8,128)(2,1)} %get-tuple-element.48.normed), calls=%async_computation | async-start | bytes 1572864 | tf_op jit(solution)/shard_map/all_to_all | solution.py:554
  26.5 9.4 %mlp_both_ways.1 = (bf16[128,768]{1,0:T(8,128)(2,1)}, bf16[128,768]{1,0:T(8,128)(2,1)S(1)}, f32[8,768]{1,0:T(8,128)S(1)}) custom-call(bf16[4,128,768]{2,1,0:T(8,128)(2,1)} %get-tuple-element.48.normed, bf16[3072,768]{1,0:T(8,128)(2,1)} %weight_in.5, bf16[3072,768]{1,0:T(8,128)(2,1)} %weight_out.5, f32[128,768]{1,0:T(8,128)S(1)} %get-tuple-element.49.centered, ...), custom_call_target="tpu_custom_call" | custom-call | tf_op jit(solution)/shard_map/mlp_both_ways/pallas_call | solution.py:560
  35.9 0.7 collective-permute-start.6
  36.6 3.1 %collective-permute-start.5 = (bf16[128,768]{1,0:T(8,128)(2,1)S(1)}, bf16[128,768]{1,0:T(8,128)(2,1)S(1)}, u32[]{:S(2)}, u32[]{:S(2)}) collective-permute-start(bf16[128,768]{1,0:T(8,128)(2,1)S(1)} %get-tuple-element.65.grads.own), channel_id=1, source_target_pairs={{0,1},{1,0},{2,3},{3,2},{4,5},{5,4},{6,7},{7,6},{8,9},{9,8},{10,11... | collective-permute-start | bytes 589832 | tf_op jit(solution)/shard_map/ppermute | solution.py:465
  39.7 0.1 concatenate.3.which
  39.8 0.1 pad_add_fusion.which
  39.8 6.2 %kernel_grad_terms.1 = (bf16[384,384]{1,0:T(8,128)(2,1)S(1)}, bf16[384,384]{1,0:T(8,128)(2,1)S(1)}) custom-call(s32[2]{0:T(128)S(1)} %pad_add_fusion.which, bf16[128,768]{1,0:T(8,128)(2,1)S(1)} %collective-permute-done.inner, bf16[128,768]{1,0:T(8,128)(2,1)S(1)} %bitcast.21, bf16[128,768]{1,0:T(8,128)(2,1)S(1)} %collective-permute-done.1.outer, ...), custom_call_target="tpu_custom_call" | custom-call | tf_op jit(solution)/shard_map/kernel_grad_terms/pallas_call | solution.py:609
  46.0 0.0 copy-start.15
  46.0 0.7 copy-done.15
  46.7 0.0 collective-permute-done.6.outer
  46.7 0.7 copy-done.7
  47.4 0.7 copy-done.9
  48.1 0.0 all-to-all-done.normed
  48.1 5.1 %weight_grads_other_core.1 = bf16[2,2,192,768]{3,2,1,0:T(8,128)(2,1)} custom-call(s32[8]{0:T(128)S(1)} %concatenate.3.which, bf16[3072,768]{1,0:T(8,128)(2,1)} %weight_in.5, bf16[3072,768]{1,0:T(8,128)(2,1)} %weight_out.5, f32[768]{0:T(1024)S(1)} %copy-done.11, bf16[4,128,768]{2,1,0:T(8,128)(2,1)S(1)} %all-to-all-done.normed, bf16[128,768]{1,0:T(8,128)(2,1)S(1)} %bitcast.14, ...), custom_call_target="tpu_custom_call" | custom-call | tf_op jit(solution)/shard_map/weight_grads_other_core/pallas_call | solution.py:663
  53.2 0.0 collective-permute-start.8
  53.2 0.5 collective-permute-start.7
  53.7 2.4 %collective-permute-done.7.got = bf16[384,384]{1,0:T(8,128)(2,1)S(1)} collective-permute-done((bf16[384,384]{1,0:T(8,128)(2,1)S(1)}, bf16[384,384]{1,0:T(8,128)(2,1)S(1)}, u32[]{:S(2)}, u32[]{:S(2)}) %collective-permute-start.7) | collective-permute-done | bytes 294944 | tf_op jit(solution)/shard_map/ppermute | solution.py:662
  56.1 0.8 kernel_grad_chip_sum.1
  56.9 5.0 %all-to-all-start.1 = ((bf16[8,48,384]{2,1,0:T(8,128)(2,1)}), bf16[8,48,384]{2,1,0:T(8,128)(2,1)S(1)}, u32[]{:S(2)}, u32[]{:S(2)}) async-start(bf16[8,48,384]{2,1,0:T(8,128)(2,1)} %bitcast.9), calls=%async_computation.1 | async-start | bytes 589824 | tf_op jit(solution)/shard_map/all_to_all | solution.py:689
  62.0 1.0 %copy-done.5 = bf16[2,2,192,768]{3,2,1,0:T(8,128)(2,1)} copy-done((bf16[2,2,192,768]{3,2,1,0:T(8,128)(2,1)}, bf16[2,2,192,768]{3,2,1,0:T(8,128)(2,1)S(1)}, u32[]{:S(2)}) %copy-start.5) | copy-done | bytes 1179672
  63.0 1.3 %copy-done.6 = bf16[2,2,192,768]{3,2,1,0:T(8,128)(2,1)S(1)} copy-done((bf16[2,2,192,768]{3,2,1,0:T(8,128)(2,1)S(1)}, bf16[2,2,192,768]{3,2,1,0:T(8,128)(2,1)}, u32[]{:S(2)}) %copy-start.6) | copy-done | bytes 1179672
  64.3 4.9 %weight_grads_own_core.1 = (bf16[2,192,768]{2,1,0:T(8,128)(2,1)S(1)}, f32[2,192,768]{2,1,0:T(8,128)S(1)}) custom-call(s32[8]{0:T(128)S(1)} %concatenate.3.which, bf16[3072,768]{1,0:T(8,128)(2,1)} %weight_in.5, bf16[3072,768]{1,0:T(8,128)(2,1)} %weight_out.5, f32[768]{0:T(1024)S(1)} %copy-done.11, bf16[4,128,768]{2,1,0:T(8,128)(2,1)S(1)} %all-to-all-done.normed, ...), custom_call_target="tpu_custom_call" | custom-call | tf_op jit(solution)/shard_map/weight_grads_own_core/pallas_call | solution.py:697
  69.2 0.0 copy-start.14
  69.2 0.8 copy-done.14
  70.0 2.0 %all-to-all-done.1.parts = bf16[8,48,384]{2,1,0:T(8,128)(2,1)S(1)} async-done(((bf16[8,48,384]{2,1,0:T(8,128)(2,1)}), bf16[8,48,384]{2,1,0:T(8,128)(2,1)S(1)}, u32[]{:S(2)}, u32[]{:S(2)}) %all-to-all-start.1) | async-done | bytes 294944 | tf_op jit(solution)/shard_map/all_to_all | solution.py:689
  72.0 0.8 kernel_grad_sum.1
  72.8 4.0 %all-to-all-start.2 = ((bf16[8,48,384]{2,1,0:T(8,128)(2,1)}), bf16[8,48,384]{2,1,0:T(8,128)(2,1)S(1)}, u32[]{:S(2)}, u32[]{:S(2)}) async-start(bf16[8,48,384]{2,1,0:T(8,128)(2,1)} %kernel_grad_sum.1), calls=%async_computation.2 | async-start | bytes 589824 | tf_op jit(solution)/shard_map/all_to_all | solution.py:731
  76.7 2.0 %collective-permute-start.10 = (bf16[2,192,768]{2,1,0:T(8,128)(2,1)}, bf16[2,192,768]{2,1,0:T(8,128)(2,1)S(1)}, u32[]{:S(2)}, u32[]{:S(2)}) collective-permute-start(bf16[2,192,768]{2,1,0:T(8,128)(2,1)} %copy-done.14), channel_id=1, source_target_pairs={{0,2},{1,3},{2,0},{3,1},{4,6},{5,7},{6,4},{7,5},{8,10},{9,11},{10,... | collective-permute-start | bytes 1769480 | tf_op jit(solution)/shard_map/ppermute | solution.py:717
  78.8 7.6 %all-to-all-done.2.own = bf16[8,48,384]{2,1,0:T(8,128)(2,1)S(1)} async-done(((bf16[8,48,384]{2,1,0:T(8,128)(2,1)}), bf16[8,48,384]{2,1,0:T(8,128)(2,1)S(1)}, u32[]{:S(2)}, u32[]{:S(2)}) %all-to-all-start.2) | async-done | bytes 294944 | tf_op jit(solution)/shard_map/all_to_all | solution.py:731
  86.3 0.9 copy-done.8
  87.3 0.9 copy-done.10
  88.2 4.3 %input_grad_conv.1 = bf16[128,768]{1,0:T(8,128)(2,1)} custom-call(s32[1]{0:T(128)} %bitcast.core, bf16[128,768]{1,0:T(8,128)(2,1)S(1)} %copy-done.10, bf16[128,768]{1,0:T(8,128)(2,1)S(1)} %get-tuple-element.65.grads.own, bf16[128,768]{1,0:T(8,128)(2,1)S(1)} %copy-done.8, f32[343,768]{1,0:T(8,128)S(1)} %copy-done.1, bf16[128,768]{1,0:T(8,128)(2,1)S(1)} %bitcast.16), custom_call_target="tpu_custom_call" | custom-call | tf_op jit(solution)/shard_map/input_grad_conv/pallas_call | solution.py:736
  92.5 2.4 %collective-permute-done.10.got = bf16[2,192,768]{2,1,0:T(8,128)(2,1)S(1)} collective-permute-done((bf16[2,192,768]{2,1,0:T(8,128)(2,1)}, bf16[2,192,768]{2,1,0:T(8,128)(2,1)S(1)}, u32[]{:S(2)}, u32[]{:S(2)}) %collective-permute-start.10) | collective-permute-done | bytes 589856 | tf_op jit(solution)/shard_map/ppermute | solution.py:717
  94.9 1.1 %weight_grads_sum.1 = (f32[192,768]{1,0:T(8,128)}, f32[192,768]{1,0:T(8,128)}) custom-call(f32[2,192,768]{2,1,0:T(8,128)S(1)} %get-tuple-element.72.kept, bf16[2,192,768]{2,1,0:T(8,128)(2,1)S(1)} %collective-permute-done.10.got), custom_call_target="tpu_custom_call" | custom-call | tf_op jit(solution)/shard_map/weight_grads_sum/pallas_call | solution.py:775
  96.0 1.1 %kernel_grad_unpack.1 = (f32[343,768]{1,0:T(8,128)}, f32[768]{0:T(1024)}, f32[768]{0:T(1024)}, f32[768]{0:T(1024)}) custom-call(s32[1]{0:T(128)} %bitcast.core, bf16[8,48,384]{2,1,0:T(8,128)(2,1)S(1)} %all-to-all-done.2.own, bf16[8,48,384]{2,1,0:T(8,128)(2,1)S(1)} %collective-permute-done.9.other), custom_call_target="tpu_custom_call" | custom-call | tf_op jit(solution)/shard_map/kernel_grad_unpack/pallas_call | solution.py:760
  (28 shorter events, 0.1 us)
Async XLA Ops:
  0.6 13.0 %collective-permute-start.3 = (bf16[128,768]{1,0:T(8,128)(2,1)}, bf16[128,768]{1,0:T(8,128)(2,1)S(1)}, u32[]{:S(2)}, u32[]{:S(2)}) collective-permute-start(bf16[128,768]{1,0:T(8,128)(2,1)} %bitcast.11), channel_id=1, source_target_pairs={{0,12},{1,13},{2,14},{3,15},{4,0},{5,1},{6,2},{7,3},{8,4},{9,5},{1... | collective-permute-start | bytes 589832 | tf_op jit(solution)/shard_map/ppermute | solution.py:493
  5.7 9.6 %collective-permute-start.2 = (bf16[128,768]{1,0:T(8,128)(2,1)}, bf16[128,768]{1,0:T(8,128)(2,1)S(1)}, u32[]{:S(2)}, u32[]{:S(2)}) collective-permute-start(bf16[128,768]{1,0:T(8,128)(2,1)} %bitcast.12), channel_id=1, source_target_pairs={{0,4},{1,5},{2,6},{3,7},{4,8},{5,9},{6,10},{7,11},{8,12},{9,13},{1... | collective-permute-start | bytes 589832 | tf_op jit(solution)/shard_map/ppermute | solution.py:493
  5.7 11.1 %collective-permute-start.1 = (bf16[128,768]{1,0:T(8,128)(2,1)}, bf16[128,768]{1,0:T(8,128)(2,1)S(1)}, u32[]{:S(2)}, u32[]{:S(2)}) collective-permute-start(bf16[128,768]{1,0:T(8,128)(2,1)} %bitcast.17), channel_id=1, source_target_pairs={{1,2},{3,4},{5,6},{7,8},{9,10},{11,12},{13,14},{2,1},{4,3},{6,5},{... | collective-permute-start | bytes 589832 | tf_op jit(solution)/shard_map/ppermute | solution.py:466
  6.4 10.4 %collective-permute-start = (bf16[128,768]{1,0:T(8,128)(2,1)}, bf16[128,768]{1,0:T(8,128)(2,1)S(1)}, u32[]{:S(2)}, u32[]{:S(2)}) collective-permute-start(bf16[128,768]{1,0:T(8,128)(2,1)} %bitcast.18), channel_id=1, source_target_pairs={{0,1},{1,0},{2,3},{3,2},{4,5},{5,4},{6,7},{7,6},{8,9},{9,8},{10,11... | collective-permute-start | bytes 589832 | tf_op jit(solution)/shard_map/ppermute | solution.py:465
  9.3 1.2 %copy-start = (f32[343,768]{1,0:T(8,128)S(1)}, f32[343,768]{1,0:T(8,128)}, u32[]{:S(2)}) copy-start(f32[343,768]{1,0:T(8,128)} %taps.3) | copy-start | bytes 3161092
  10.6 0.9 copy-start.3
  11.5 5.4 %copy-start.12 = (f32[768]{0:T(1024)S(1)}, f32[768]{0:T(1024)}, u32[]{:S(2)}) copy-start(f32[768]{0:T(1024)} %norm_gain.1) | copy-start | bytes 9220
  11.5 5.4 %copy-start.13 = (f32[768]{0:T(1024)S(1)}, f32[768]{0:T(1024)}, u32[]{:S(2)}) copy-start(f32[768]{0:T(1024)} %bias.1) | copy-start | bytes 9220
  15.3 7.6 %collective-permute-start.4 = (bf16[128,768]{1,0:T(8,128)(2,1)S(1)}, bf16[128,768]{1,0:T(8,128)(2,1)S(1)}, u32[]{:S(2)}, u32[]{:S(2)}) collective-permute-start(bf16[128,768]{1,0:T(8,128)(2,1)S(1)} %collective-permute-done.2.rest_1_), channel_id=1, source_target_pairs={{0,4},{1,5},{2,6},{3,7},{4,8},{5,9},{6,10},{7,11},{8,12},{9,13},{1... | collective-permute-start | bytes 589832 | tf_op jit(solution)/shard_map/ppermute | solution.py:493
  20.5 6.0 %copy-start.2 = (bf16[4,4,8,768]{3,2,1,0:T(8,128)(2,1)S(1)}, bf16[4,4,8,768]{3,2,1,0:T(8,128)(2,1)}, u32[]{:S(2)}) copy-start(bf16[4,4,8,768]{3,2,1,0:T(8,128)(2,1)} %param.15) | copy-start | bytes 589828
  20.5 6.0 %copy-start.4 = (bf16[4,4,8,768]{3,2,1,0:T(8,128)(2,1)S(1)}, bf16[4,4,8,768]{3,2,1,0:T(8,128)(2,1)}, u32[]{:S(2)}) copy-start(bf16[4,4,8,768]{3,2,1,0:T(8,128)(2,1)} %param.8) | copy-start | bytes 589828
  20.5 6.0 %copy-start.11 = (f32[768]{0:T(1024)S(1)}, f32[768]{0:T(1024)}, u32[]{:S(2)}) copy-start(f32[768]{0:T(1024)} %scale.3) | copy-start | bytes 9220
  22.9 25.2 %all-to-all-start = ((bf16[4,128,768]{2,1,0:T(8,128)(2,1)}), bf16[4,128,768]{2,1,0:T(8,128)(2,1)S(1)}, u32[]{:S(2)}, u32[]{:S(2)}) async-start(bf16[4,128,768]{2,1,0:T(8,128)(2,1)} %get-tuple-element.48.normed), calls=%async_computation | async-start | bytes 1572864 | tf_op jit(solution)/shard_map/all_to_all | solution.py:554
  35.9 10.8 %collective-permute-start.6 = (bf16[128,768]{1,0:T(8,128)(2,1)S(1)}, bf16[128,768]{1,0:T(8,128)(2,1)S(1)}, u32[]{:S(2)}, u32[]{:S(2)}) collective-permute-start(bf16[128,768]{1,0:T(8,128)(2,1)S(1)} %get-tuple-element.65.grads.own), channel_id=1, source_target_pairs={{1,2},{3,4},{5,6},{7,8},{9,10},{11,12},{13,14},{2,1},{4,3},{6,5},{... | collective-permute-start | bytes 589832 | tf_op jit(solution)/shard_map/ppermute | solution.py:466
  36.6 10.8 %collective-permute-start.5 = (bf16[128,768]{1,0:T(8,128)(2,1)S(1)}, bf16[128,768]{1,0:T(8,128)(2,1)S(1)}, u32[]{:S(2)}, u32[]{:S(2)}) collective-permute-start(bf16[128,768]{1,0:T(8,128)(2,1)S(1)} %get-tuple-element.65.grads.own), channel_id=1, source_target_pairs={{0,1},{1,0},{2,3},{3,2},{4,5},{5,4},{6,7},{7,6},{8,9},{9,8},{10,11... | collective-permute-start | bytes 589832 | tf_op jit(solution)/shard_map/ppermute | solution.py:465
  46.0 0.7 copy-start.15
  46.7 0.7 copy-start.7
  47.4 0.7 copy-start.9
  48.1 5.1 %copy-start.16 = (bf16[384,384]{1,0:T(8,128)(2,1)S(1)}, bf16[384,384]{1,0:T(8,128)(2,1)}, u32[]{:S(2)}) copy-start(bf16[384,384]{1,0:T(8,128)(2,1)} %copy-done.15) | copy-start | bytes 884740
  53.2 8.7 %collective-permute-start.8 = (bf16[2,2,192,768]{3,2,1,0:T(8,128)(2,1)}, bf16[2,2,192,768]{3,2,1,0:T(8,128)(2,1)S(1)}, u32[]{:S(2)}, u32[]{:S(2)}) collective-permute-start(bf16[2,2,192,768]{3,2,1,0:T(8,128)(2,1)} %weight_grads_other_core.1), channel_id=1, source_target_pairs={{0,1},{1,0},{2,3},{3,2},{4,5},{5,4},{6,7},{7,6},{8,9},{9,8},{10,11... | collective-permute-start | bytes 3538952 | tf_op jit(solution)/shard_map/ppermute | solution.py:678
  53.2 2.9 %collective-permute-start.7 = (bf16[384,384]{1,0:T(8,128)(2,1)S(1)}, bf16[384,384]{1,0:T(8,128)(2,1)S(1)}, u32[]{:S(2)}, u32[]{:S(2)}) collective-permute-start(bf16[384,384]{1,0:T(8,128)(2,1)S(1)} %copy-done.16), channel_id=1, source_target_pairs={{0,1},{1,0},{2,3},{3,2},{4,5},{5,4},{6,7},{7,6},{8,9},{9,8},{10,11... | collective-permute-start | bytes 884744 | tf_op jit(solution)/shard_map/ppermute | solution.py:662
  56.9 15.1 %all-to-all-start.1 = ((bf16[8,48,384]{2,1,0:T(8,128)(2,1)}), bf16[8,48,384]{2,1,0:T(8,128)(2,1)S(1)}, u32[]{:S(2)}, u32[]{:S(2)}) async-start(bf16[8,48,384]{2,1,0:T(8,128)(2,1)} %bitcast.9), calls=%async_computation.1 | async-start | bytes 589824 | tf_op jit(solution)/shard_map/all_to_all | solution.py:689
  61.9 1.0 %copy-start.5 = (bf16[2,2,192,768]{3,2,1,0:T(8,128)(2,1)}, bf16[2,2,192,768]{3,2,1,0:T(8,128)(2,1)S(1)}, u32[]{:S(2)}) copy-start(bf16[2,2,192,768]{3,2,1,0:T(8,128)(2,1)S(1)} %collective-permute-done.8.got) | copy-start | bytes 3538948
  63.0 1.3 %copy-start.6 = (bf16[2,2,192,768]{3,2,1,0:T(8,128)(2,1)S(1)}, bf16[2,2,192,768]{3,2,1,0:T(8,128)(2,1)}, u32[]{:S(2)}) copy-start(bf16[2,2,192,768]{3,2,1,0:T(8,128)(2,1)} %copy-done.5) | copy-start | bytes 3538948
  69.2 0.8 copy-start.14
  70.0 16.3 %copy-start.1 = (f32[343,768]{1,0:T(8,128)S(1)}, f32[343,768]{1,0:T(8,128)}, u32[]{:S(2)}) copy-start(f32[343,768]{1,0:T(8,128)} %taps.3) | copy-start | bytes 3161092
  72.8 13.5 %all-to-all-start.2 = ((bf16[8,48,384]{2,1,0:T(8,128)(2,1)}), bf16[8,48,384]{2,1,0:T(8,128)(2,1)S(1)}, u32[]{:S(2)}, u32[]{:S(2)}) async-start(bf16[8,48,384]{2,1,0:T(8,128)(2,1)} %kernel_grad_sum.1), calls=%async_computation.2 | async-start | bytes 589824 | tf_op jit(solution)/shard_map/all_to_all | solution.py:731
  76.7 18.1 %collective-permute-start.10 = (bf16[2,192,768]{2,1,0:T(8,128)(2,1)}, bf16[2,192,768]{2,1,0:T(8,128)(2,1)S(1)}, u32[]{:S(2)}, u32[]{:S(2)}) collective-permute-start(bf16[2,192,768]{2,1,0:T(8,128)(2,1)} %copy-done.14), channel_id=1, source_target_pairs={{0,2},{1,3},{2,0},{3,1},{4,6},{5,7},{6,4},{7,5},{8,10},{9,11},{10,... | collective-permute-start | bytes 1769480 | tf_op jit(solution)/shard_map/ppermute | solution.py:717
  86.3 9.6 %collective-permute-start.9 = (bf16[8,48,384]{2,1,0:T(8,128)(2,1)S(1)}, bf16[8,48,384]{2,1,0:T(8,128)(2,1)S(1)}, u32[]{:S(2)}, u32[]{:S(2)}) collective-permute-start(bf16[8,48,384]{2,1,0:T(8,128)(2,1)S(1)} %all-to-all-done.2.own), channel_id=1, source_target_pairs={{0,1},{1,0},{2,3},{3,2},{4,5},{5,4},{6,7},{7,6},{8,9},{9,8},{10,11... | collective-permute-start | bytes 884744 | tf_op jit(solution)/shard_map/ppermute | solution.py:734
  86.3 0.9 copy-start.8
  87.3 0.9 copy-start.10

commit v9 on v8

--- a/solution.py
+++ b/solution.py
@@ -590,8 +590,6 @@
         name="mlp_both_ways",
     )(normed, weight_in, weight_out, centered, norm_gain, layer_scale, own, upstream)
 
-    grad_inner, grad_outer = rims(conv_grad)
-
     half = count // 2
     alike = [[2 * k + p for k in range(half)] for p in range(2)]
     half_tiles = tiles // 2
@@ -629,6 +627,20 @@
         name="kernel_grad_terms",
     )(jnp.stack([core, 1 - core]), inner, own, outer, conv_grad, small)
 
+    half_sent, conv_grad = lax.optimization_barrier((half_sent, conv_grad))
+    half_got = lax.ppermute(half_sent, "row", other_core)
+    grad_inner, grad_outer = rims(conv_grad)
+    sums = pl.pallas_call(
+        chip_sum_kernel,
+        in_specs=[whole_block(padded, wide)] * 2,
+        out_specs=whole_block(padded, wide),
+        out_shape=jax.ShapeDtypeStruct((padded, wide), BF16),
+        grid=(1,),
+        compiler_params=params(),
+        cost_estimate=NO_COST,
+        name="kernel_grad_chip_sum",
+    )(half_kept, half_got)
+
     share = units // count
     tokens = line * rows
     base = me // quad * quad
@@ -656,10 +668,15 @@
     cotangents = [whole_block(rows, channels)] * line
     aligned = [pltpu.VMEM((tokens, channels), BF16)]
 
-    which, half_sent, half_kept, grad_inner, grad_outer = lax.optimization_barrier(
-        (which, half_sent, half_kept, grad_inner, grad_outer)
-    )
-    half_got = lax.ppermute(half_sent, "row", other_core)
+    which, sums = lax.optimization_barrier((which, sums))
+    scattered = lax.all_to_all(
+        sums.reshape(half, piece, wide),
+        "row",
+        split_axis=0,
+        concat_axis=0,
+        tiled=True,
+        axis_index_groups=alike,
+    )
     for_other = pl.pallas_call(
         other_core_terms_kernel,
         grid_spec=pltpu.PrefetchScalarGridSpec(
@@ -674,26 +691,7 @@
         cost_estimate=NO_COST,
         name="weight_grads_other_core",
     )(which, weight_in, weight_out, layer_scale, gathered, *upstream_line)
-    half_kept, for_other = lax.optimization_barrier((half_kept, for_other))
     from_other = lax.ppermute(for_other, "row", other_core)
-    sums = pl.pallas_call(
-        chip_sum_kernel,
-        in_specs=[whole_block(padded, wide)] * 2,
-        out_specs=whole_block(padded, wide),
-        out_shape=jax.ShapeDtypeStruct((padded, wide), BF16),
-        grid=(1,),
-        compiler_params=params(),
-        cost_estimate=NO_COST,
-        name="kernel_grad_chip_sum",
-    )(half_kept, half_got)
-    scattered = lax.all_to_all(
-        sums.reshape(half, piece, wide),
-        "row",
-        split_axis=0,
-        concat_axis=0,
-        tiled=True,
-        axis_index_groups=alike,
-    )
     sent, kept = pl.pallas_call(
         own_core_terms_kernel,
         grid_spec=pltpu.PrefetchScalarGridSpec(
@@ -731,7 +729,6 @@
     totals = lax.all_to_all(
         copies, "row", split_axis=0, concat_axis=0, tiled=True, axis_index_groups=alike
     )
-    other_totals = lax.ppermute(totals, "row", other_core)
 
     voxel_grad = pl.pallas_call(
         functools.partial(input_grad_kernel, planes, height),
@@ -757,6 +754,8 @@
         name="input_grad_conv",
     )(parity, grad_inner, conv_own, grad_outer, dw_kernel, upstream)
 
+    totals, voxel_grad = lax.optimization_barrier((totals, voxel_grad))
+    other_totals = lax.ppermute(totals, "row", other_core)
     kernel_grad, *vector_grads = pl.pallas_call(
         unpack_kernel,
         grid_spec=pltpu.PrefetchScalarGridSpec(

time: 97.7 us -> 98.5 us (level)
  the two profiles are of different devices: /device:TPU:0 before, /device:TPU:1 now
where the time goes in v9:
time: 98.5 us; the launch traced here: 97.7 us
  Pallas kernels  39.4 us (40%)
  starting transfers between devices  31.5 us (32%)
  waiting for transfers between devices  20.6 us (21%)
  local copies, waits for them, and re-layouts  5.36 us (5%)
    ppermute x2, waiting for transfers between devices, rims(): lax.ppermute(cells, 'row', between + [(j, i) for i, j in between])  16.6 us
    pallas_call x1, Pallas kernels, on_device(): pl.pallas_call(mlp_kernel, grid=(units // block,), in_specs=[pl.BlockSpec...  9.41 us
    pallas_call x1, Pallas kernels, on_device(): pl.pallas_call(functools.partial(kernel_grad_kernel, planes, height), gri...  6.18 us
    ppermute x3, starting transfers between devices, along_line(): lax.ppermute(cells, 'row', [(i, (i + quad * steps) % count) for i in rang...  5.75 us
    unnamed x22, local copies, waits for them, and re-layouts  5.28 us
    pallas_call x1, Pallas kernels, on_device(): pl.pallas_call(other_core_terms_kernel, grid_spec=pltpu.PrefetchScalarGri...  5.11 us
    ppermute x2, starting transfers between devices, rims(): lax.ppermute(cells, 'row', between + [(j, i) for i, j in between])  5.09 us
    all_to_all x1, starting transfers between devices, on_device(): lax.all_to_all(copies, 'row', split_axis=0, concat_axis=0, tiled=True, ax...  4.99 us
  transfers between devices with their start and end apart: 14, of which 6 were waited for; matrix products, arithmetic and copies ran while one was open for 0% of the time, Pallas kernels for 33%

profile of v9, /device:TPU:1, one launch (start us, length us, event | category | flops | bytes accessed | tf_op | source)
XLA Modules:
  0.0 97.7 jit_solution(9697017065091447429)
XLA Ops:
  0.6 2.2 %collective-permute-start.2 = (bf16[128,768]{1,0:T(8,128)(2,1)}, bf16[128,768]{1,0:T(8,128)(2,1)S(1)}, u32[]{:S(2)}, u32[]{:S(2)}) collective-permute-start(bf16[128,768]{1,0:T(8,128)(2,1)} %bitcast.11), channel_id=1, source_target_pairs={{0,4},{1,5},{2,6},{3,7},{4,8},{5,9},{6,10},{7,11},{8,12},{9,13},{1... | collective-permute-start | bytes 589832 | tf_op jit(solution)/shard_map/ppermute | solution.py:493
  2.8 2.1 %collective-permute-start.3 = (bf16[128,768]{1,0:T(8,128)(2,1)}, bf16[128,768]{1,0:T(8,128)(2,1)S(1)}, u32[]{:S(2)}, u32[]{:S(2)}) collective-permute-start(bf16[128,768]{1,0:T(8,128)(2,1)} %bitcast.12), channel_id=1, source_target_pairs={{0,12},{1,13},{2,14},{3,15},{4,0},{5,1},{6,2},{7,3},{8,4},{9,5},{1... | collective-permute-start | bytes 589832 | tf_op jit(solution)/shard_map/ppermute | solution.py:493
  4.9 1.0 collective-permute-start
  5.9 3.2 %collective-permute-start.1 = (bf16[128,768]{1,0:T(8,128)(2,1)}, bf16[128,768]{1,0:T(8,128)(2,1)S(1)}, u32[]{:S(2)}, u32[]{:S(2)}) collective-permute-start(bf16[128,768]{1,0:T(8,128)(2,1)} %bitcast.18), channel_id=1, source_target_pairs={{1,2},{3,4},{5,6},{7,8},{9,10},{11,12},{13,14},{2,1},{4,3},{6,5},{... | collective-permute-start | bytes 589832 | tf_op jit(solution)/shard_map/ppermute | solution.py:466
  9.0 0.0 copy-start
  9.1 1.2 %copy-done = f32[343,768]{1,0:T(8,128)S(1)} copy-done((f32[343,768]{1,0:T(8,128)S(1)}, f32[343,768]{1,0:T(8,128)}, u32[]{:S(2)}) %copy-start) | copy-done | bytes 1053720
  10.3 0.9 copy-done.3
  11.2 2.1 %own_conv.1 = (f32[128,768]{1,0:T(8,128)S(1)}, f32[6,9,7,8,128]{4,3,2,1,0:T(8,128)S(1)}) custom-call(bf16[128,768]{1,0:T(8,128)(2,1)S(1)} %bitcast.19, f32[343,768]{1,0:T(8,128)S(1)} %copy-done), custom_call_target="tpu_custom_call" | custom-call | tf_op jit(solution)/shard_map/own_conv/pallas_call | solution.py:503
  13.4 0.0 collective-permute-done.2.rest_1_
  13.4 0.1 collective-permute-done.3.rest_3_
  13.4 1.5 %collective-permute-start.4 = (bf16[128,768]{1,0:T(8,128)(2,1)S(1)}, bf16[128,768]{1,0:T(8,128)(2,1)S(1)}, u32[]{:S(2)}, u32[]{:S(2)}) collective-permute-start(bf16[128,768]{1,0:T(8,128)(2,1)S(1)} %collective-permute-done.2.rest_1_), channel_id=1, source_target_pairs={{0,4},{1,5},{2,6},{3,7},{4,8},{5,9},{6,10},{7,11},{8,12},{9,13},{1... | collective-permute-start | bytes 589832 | tf_op jit(solution)/shard_map/ppermute | solution.py:493
  14.9 0.0 collective-permute-done.inner
  14.9 0.0 collective-permute-done.1.outer
  14.9 3.6 %rim_conv.1 = (bf16[4,128,768]{2,1,0:T(8,128)(2,1)}, f32[128,768]{1,0:T(8,128)S(1)}) custom-call(s32[1]{0:T(128)} %bitcast.core, bf16[128,768]{1,0:T(8,128)(2,1)S(1)} %collective-permute-done.inner, bf16[128,768]{1,0:T(8,128)(2,1)S(1)} %collective-permute-done.1.outer, f32[6,9,7,8,128]{4,3,2,1,0:T(8,128)S(1)} %get-tuple-element.41.split, ...), custom_call_target="tpu_custom_call" | custom-call | tf_op jit(solution)/shard_map/rim_conv/pallas_call | solution.py:523
  18.6 2.0 %collective-permute-done.4.rest_2_ = bf16[128,768]{1,0:T(8,128)(2,1)S(1)} collective-permute-done((bf16[128,768]{1,0:T(8,128)(2,1)S(1)}, bf16[128,768]{1,0:T(8,128)(2,1)S(1)}, u32[]{:S(2)}, u32[]{:S(2)}) %collective-permute-start.4) | collective-permute-done | bytes 196640 | tf_op jit(solution)/shard_map/ppermute | solution.py:493
  20.5 3.5 %all-to-all-start.1 = ((bf16[4,128,768]{2,1,0:T(8,128)(2,1)}), bf16[4,128,768]{2,1,0:T(8,128)(2,1)S(1)}, u32[]{:S(2)}, u32[]{:S(2)}) async-start(bf16[4,128,768]{2,1,0:T(8,128)(2,1)} %get-tuple-element.47.normed), calls=%async_computation.1 | async-start | bytes 1572864 | tf_op jit(solution)/shard_map/all_to_all | solution.py:554
  24.0 0.1 pad_add_fusion.which
  24.1 9.4 %mlp_both_ways.1 = (bf16[128,768]{1,0:T(8,128)(2,1)}, bf16[128,768]{1,0:T(8,128)(2,1)S(1)}, f32[8,768]{1,0:T(8,128)S(1)}) custom-call(bf16[4,128,768]{2,1,0:T(8,128)(2,1)} %get-tuple-element.47.normed, bf16[3072,768]{1,0:T(8,128)(2,1)} %weight_in.5, bf16[3072,768]{1,0:T(8,128)(2,1)} %weight_out.5, f32[128,768]{1,0:T(8,128)S(1)} %get-tuple-element.48.centered, ...), custom_call_target="tpu_custom_call" | custom-call | tf_op jit(solution)/shard_map/mlp_both_ways/pallas_call | solution.py:560
  33.5 6.2 %kernel_grad_terms.1 = (bf16[384,384]{1,0:T(8,128)(2,1)S(1)}, bf16[384,384]{1,0:T(8,128)(2,1)S(1)}) custom-call(s32[2]{0:T(128)S(1)} %pad_add_fusion.which, bf16[128,768]{1,0:T(8,128)(2,1)S(1)} %collective-permute-done.inner, bf16[128,768]{1,0:T(8,128)(2,1)S(1)} %bitcast.21, bf16[128,768]{1,0:T(8,128)(2,1)S(1)} %collective-permute-done.1.outer, ...), custom_call_target="tpu_custom_call" | custom-call | tf_op jit(solution)/shard_map/kernel_grad_terms/pallas_call | solution.py:607
  39.7 2.1 %collective-permute-start.5 = (bf16[384,384]{1,0:T(8,128)(2,1)S(1)}, bf16[384,384]{1,0:T(8,128)(2,1)S(1)}, u32[]{:S(2)}, u32[]{:S(2)}) collective-permute-start(bf16[384,384]{1,0:T(8,128)(2,1)S(1)} %get-tuple-element.55), channel_id=1, source_target_pairs={{0,1},{1,0},{2,3},{3,2},{4,5},{5,4},{6,7},{7,6},{8,9},{9,8},{10,11... | collective-permute-start | bytes 884744 | tf_op jit(solution)/shard_map/ppermute | solution.py:631
  41.8 0.1 concatenate.3.which
  41.9 1.1 %collective-permute-done.5.got = bf16[384,384]{1,0:T(8,128)(2,1)S(1)} collective-permute-done((bf16[384,384]{1,0:T(8,128)(2,1)S(1)}, bf16[384,384]{1,0:T(8,128)(2,1)S(1)}, u32[]{:S(2)}, u32[]{:S(2)}) %collective-permute-start.5) | collective-permute-done | bytes 294944 | tf_op jit(solution)/shard_map/ppermute | solution.py:631
  43.0 0.8 kernel_grad_chip_sum.1
  43.8 0.0 all-to-all-done.1.normed
  43.8 5.1 %weight_grads_other_core.1 = bf16[2,2,192,768]{3,2,1,0:T(8,128)(2,1)} custom-call(s32[8]{0:T(128)S(1)} %concatenate.3.which, bf16[3072,768]{1,0:T(8,128)(2,1)} %weight_in.5, bf16[3072,768]{1,0:T(8,128)(2,1)} %weight_out.5, f32[768]{0:T(1024)S(1)} %copy-done.7, bf16[4,128,768]{2,1,0:T(8,128)(2,1)S(1)} %all-to-all-done.1.normed, ...), custom_call_target="tpu_custom_call" | custom-call | tf_op jit(solution)/shard_map/weight_grads_other_core/pallas_call | solution.py:680
  48.9 1.3 %collective-permute-start.6 = (bf16[2,2,192,768]{3,2,1,0:T(8,128)(2,1)}, bf16[2,2,192,768]{3,2,1,0:T(8,128)(2,1)S(1)}, u32[]{:S(2)}, u32[]{:S(2)}) collective-permute-start(bf16[2,2,192,768]{3,2,1,0:T(8,128)(2,1)} %weight_grads_other_core.1), channel_id=1, source_target_pairs={{0,1},{1,0},{2,3},{3,2},{4,5},{5,4},{6,7},{7,6},{8,9},{9,8},{10,11... | collective-permute-start | bytes 3538952 | tf_op jit(solution)/shard_map/ppermute | solution.py:694
  50.2 4.8 %all-to-all-start = ((bf16[8,48,384]{2,1,0:T(8,128)(2,1)}), bf16[8,48,384]{2,1,0:T(8,128)(2,1)S(1)}, u32[]{:S(2)}, u32[]{:S(2)}) async-start(bf16[8,48,384]{2,1,0:T(8,128)(2,1)} %bitcast.9), calls=%async_computation | async-start | bytes 589824 | tf_op jit(solution)/shard_map/all_to_all | solution.py:672
  55.0 0.0 collective-permute-done.6.got
  55.0 1.0 %copy-done.5 = bf16[2,2,192,768]{3,2,1,0:T(8,128)(2,1)} copy-done((bf16[2,2,192,768]{3,2,1,0:T(8,128)(2,1)}, bf16[2,2,192,768]{3,2,1,0:T(8,128)(2,1)S(1)}, u32[]{:S(2)}) %copy-start.5) | copy-done | bytes 1179672
  56.1 1.3 %copy-done.6 = bf16[2,2,192,768]{3,2,1,0:T(8,128)(2,1)S(1)} copy-done((bf16[2,2,192,768]{3,2,1,0:T(8,128)(2,1)S(1)}, bf16[2,2,192,768]{3,2,1,0:T(8,128)(2,1)}, u32[]{:S(2)}) %copy-start.6) | copy-done | bytes 1179672
  57.3 4.9 %weight_grads_own_core.1 = (bf16[2,192,768]{2,1,0:T(8,128)(2,1)S(1)}, f32[2,192,768]{2,1,0:T(8,128)S(1)}) custom-call(s32[8]{0:T(128)S(1)} %concatenate.3.which, bf16[3072,768]{1,0:T(8,128)(2,1)} %weight_in.5, bf16[3072,768]{1,0:T(8,128)(2,1)} %weight_out.5, f32[768]{0:T(1024)S(1)} %copy-done.7, bf16[4,128,768]{2,1,0:T(8,128)(2,1)S(1)} %all-to-all-done.1.normed, ...), custom_call_target="tpu_custom_call" | custom-call | tf_op jit(solution)/shard_map/weight_grads_own_core/pallas_call | solution.py:695
  62.3 0.0 copy-start.10
  62.3 0.8 copy-done.10
  63.1 0.4 all-to-all-done.parts
  63.5 0.8 kernel_grad_sum.1
  64.3 5.0 %all-to-all-start.2 = ((bf16[8,48,384]{2,1,0:T(8,128)(2,1)}), bf16[8,48,384]{2,1,0:T(8,128)(2,1)S(1)}, u32[]{:S(2)}, u32[]{:S(2)}) async-start(bf16[8,48,384]{2,1,0:T(8,128)(2,1)} %kernel_grad_sum.1), calls=%async_computation.2 | async-start | bytes 589824 | tf_op jit(solution)/shard_map/all_to_all | solution.py:729
  69.3 1.5 %collective-permute-start.10 = (bf16[2,192,768]{2,1,0:T(8,128)(2,1)}, bf16[2,192,768]{2,1,0:T(8,128)(2,1)S(1)}, u32[]{:S(2)}, u32[]{:S(2)}) collective-permute-start(bf16[2,192,768]{2,1,0:T(8,128)(2,1)} %copy-done.10), channel_id=1, source_target_pairs={{0,2},{1,3},{2,0},{3,1},{4,6},{5,7},{6,4},{7,5},{8,10},{9,11},{10,... | collective-permute-start | bytes 1769480 | tf_op jit(solution)/shard_map/ppermute | solution.py:715
  70.7 1.6 %collective-permute-start.7 = (bf16[128,768]{1,0:T(8,128)(2,1)S(1)}, bf16[128,768]{1,0:T(8,128)(2,1)S(1)}, u32[]{:S(2)}, u32[]{:S(2)}) collective-permute-start(bf16[128,768]{1,0:T(8,128)(2,1)S(1)} %get-tuple-element.63.grads.own), channel_id=1, source_target_pairs={{0,1},{1,0},{2,3},{3,2},{4,5},{5,4},{6,7},{7,6},{8,9},{9,8},{10,11... | collective-permute-start | bytes 589832 | tf_op jit(solution)/shard_map/ppermute | solution.py:465
  72.3 1.9 %collective-permute-start.8 = (bf16[128,768]{1,0:T(8,128)(2,1)S(1)}, bf16[128,768]{1,0:T(8,128)(2,1)S(1)}, u32[]{:S(2)}, u32[]{:S(2)}) collective-permute-start(bf16[128,768]{1,0:T(8,128)(2,1)S(1)} %get-tuple-element.63.grads.own), channel_id=1, source_target_pairs={{1,2},{3,4},{5,6},{7,8},{9,10},{11,12},{13,14},{2,1},{4,3},{6,5},{... | collective-permute-start | bytes 589832 | tf_op jit(solution)/shard_map/ppermute | solution.py:466
  74.2 0.0 collective-permute-done.7.inner
  74.2 16.6 %collective-permute-done.8.outer = bf16[128,768]{1,0:T(8,128)(2,1)S(1)} collective-permute-done((bf16[128,768]{1,0:T(8,128)(2,1)S(1)}, bf16[128,768]{1,0:T(8,128)(2,1)S(1)}, u32[]{:S(2)}, u32[]{:S(2)}) %collective-permute-start.8) | collective-permute-done | bytes 196640 | tf_op jit(solution)/shard_map/ppermute | solution.py:466
  90.8 4.3 %input_grad_conv.1 = bf16[128,768]{1,0:T(8,128)(2,1)} custom-call(s32[1]{0:T(128)} %bitcast.core, bf16[128,768]{1,0:T(8,128)(2,1)S(1)} %collective-permute-done.7.inner, bf16[128,768]{1,0:T(8,128)(2,1)S(1)} %get-tuple-element.63.grads.own, bf16[128,768]{1,0:T(8,128)(2,1)S(1)} %collective-permute-done.8.outer, f32[343,768]{1,0:T(8,128)S(1)} %copy-done.1, ...), custom_call_target="tpu_custom_call" | custom-call | tf_op jit(solution)/shard_map/input_grad_conv/pallas_call | solution.py:733
  95.1 0.0 all-to-all-done.2.own
  95.1 0.0 collective-permute-start.9
  95.1 0.0 collective-permute-done.10.got
  95.1 1.1 %weight_grads_sum.1 = (f32[192,768]{1,0:T(8,128)}, f32[192,768]{1,0:T(8,128)}) custom-call(f32[2,192,768]{2,1,0:T(8,128)S(1)} %get-tuple-element.70.kept, bf16[2,192,768]{2,1,0:T(8,128)(2,1)S(1)} %collective-permute-done.10.got), custom_call_target="tpu_custom_call" | custom-call | tf_op jit(solution)/shard_map/weight_grads_sum/pallas_call | solution.py:774
  96.2 0.5 collective-permute-done.9.other
  96.7 1.1 %kernel_grad_unpack.1 = (f32[343,768]{1,0:T(8,128)}, f32[768]{0:T(1024)}, f32[768]{0:T(1024)}, f32[768]{0:T(1024)}) custom-call(s32[1]{0:T(128)} %bitcast.core, bf16[8,48,384]{2,1,0:T(8,128)(2,1)S(1)} %all-to-all-done.2.own, bf16[8,48,384]{2,1,0:T(8,128)(2,1)S(1)} %collective-permute-done.9.other), custom_call_target="tpu_custom_call" | custom-call | tf_op jit(solution)/shard_map/kernel_grad_unpack/pallas_call | solution.py:759
  (16 shorter events, 0.0 us)
Async XLA Ops:
  0.6 12.7 %collective-permute-start.2 = (bf16[128,768]{1,0:T(8,128)(2,1)}, bf16[128,768]{1,0:T(8,128)(2,1)S(1)}, u32[]{:S(2)}, u32[]{:S(2)}) collective-permute-start(bf16[128,768]{1,0:T(8,128)(2,1)} %bitcast.11), channel_id=1, source_target_pairs={{0,4},{1,5},{2,6},{3,7},{4,8},{5,9},{6,10},{7,11},{8,12},{9,13},{1... | collective-permute-start | bytes 589832 | tf_op jit(solution)/shard_map/ppermute | solution.py:493
  2.8 10.6 %collective-permute-start.3 = (bf16[128,768]{1,0:T(8,128)(2,1)}, bf16[128,768]{1,0:T(8,128)(2,1)S(1)}, u32[]{:S(2)}, u32[]{:S(2)}) collective-permute-start(bf16[128,768]{1,0:T(8,128)(2,1)} %bitcast.12), channel_id=1, source_target_pairs={{0,12},{1,13},{2,14},{3,15},{4,0},{5,1},{6,2},{7,3},{8,4},{9,5},{1... | collective-permute-start | bytes 589832 | tf_op jit(solution)/shard_map/ppermute | solution.py:493
  4.9 10.0 %collective-permute-start = (bf16[128,768]{1,0:T(8,128)(2,1)}, bf16[128,768]{1,0:T(8,128)(2,1)S(1)}, u32[]{:S(2)}, u32[]{:S(2)}) collective-permute-start(bf16[128,768]{1,0:T(8,128)(2,1)} %bitcast.17), channel_id=1, source_target_pairs={{0,1},{1,0},{2,3},{3,2},{4,5},{5,4},{6,7},{7,6},{8,9},{9,8},{10,11... | collective-permute-start | bytes 589832 | tf_op jit(solution)/shard_map/ppermute | solution.py:465
  5.9 9.1 %collective-permute-start.1 = (bf16[128,768]{1,0:T(8,128)(2,1)}, bf16[128,768]{1,0:T(8,128)(2,1)S(1)}, u32[]{:S(2)}, u32[]{:S(2)}) collective-permute-start(bf16[128,768]{1,0:T(8,128)(2,1)} %bitcast.18), channel_id=1, source_target_pairs={{1,2},{3,4},{5,6},{7,8},{9,10},{11,12},{13,14},{2,1},{4,3},{6,5},{... | collective-permute-start | bytes 589832 | tf_op jit(solution)/shard_map/ppermute | solution.py:466
  9.0 1.2 %copy-start = (f32[343,768]{1,0:T(8,128)S(1)}, f32[343,768]{1,0:T(8,128)}, u32[]{:S(2)}) copy-start(f32[343,768]{1,0:T(8,128)} %taps.3) | copy-start | bytes 3161092
  10.3 0.9 copy-start.3
  11.2 3.7 %copy-start.8 = (f32[768]{0:T(1024)S(1)}, f32[768]{0:T(1024)}, u32[]{:S(2)}) copy-start(f32[768]{0:T(1024)} %norm_gain.1) | copy-start | bytes 9220
  11.2 3.7 %copy-start.9 = (f32[768]{0:T(1024)S(1)}, f32[768]{0:T(1024)}, u32[]{:S(2)}) copy-start(f32[768]{0:T(1024)} %bias.1) | copy-start | bytes 9220
  13.4 7.1 %collective-permute-start.4 = (bf16[128,768]{1,0:T(8,128)(2,1)S(1)}, bf16[128,768]{1,0:T(8,128)(2,1)S(1)}, u32[]{:S(2)}, u32[]{:S(2)}) collective-permute-start(bf16[128,768]{1,0:T(8,128)(2,1)S(1)} %collective-permute-done.2.rest_1_), channel_id=1, source_target_pairs={{0,4},{1,5},{2,6},{3,7},{4,8},{5,9},{6,10},{7,11},{8,12},{9,13},{1... | collective-permute-start | bytes 589832 | tf_op jit(solution)/shard_map/ppermute | solution.py:493
  18.6 5.6 %copy-start.2 = (bf16[4,4,8,768]{3,2,1,0:T(8,128)(2,1)S(1)}, bf16[4,4,8,768]{3,2,1,0:T(8,128)(2,1)}, u32[]{:S(2)}) copy-start(bf16[4,4,8,768]{3,2,1,0:T(8,128)(2,1)} %param.15) | copy-start | bytes 589828
  18.6 5.6 %copy-start.4 = (bf16[4,4,8,768]{3,2,1,0:T(8,128)(2,1)S(1)}, bf16[4,4,8,768]{3,2,1,0:T(8,128)(2,1)}, u32[]{:S(2)}) copy-start(bf16[4,4,8,768]{3,2,1,0:T(8,128)(2,1)} %param.8) | copy-start | bytes 589828
  18.6 5.6 %copy-start.7 = (f32[768]{0:T(1024)S(1)}, f32[768]{0:T(1024)}, u32[]{:S(2)}) copy-start(f32[768]{0:T(1024)} %scale.3) | copy-start | bytes 9220
  20.5 23.3 %all-to-all-start.1 = ((bf16[4,128,768]{2,1,0:T(8,128)(2,1)}), bf16[4,128,768]{2,1,0:T(8,128)(2,1)S(1)}, u32[]{:S(2)}, u32[]{:S(2)}) async-start(bf16[4,128,768]{2,1,0:T(8,128)(2,1)} %get-tuple-element.47.normed), calls=%async_computation.1 | async-start | bytes 1572864 | tf_op jit(solution)/shard_map/all_to_all | solution.py:554
  39.7 3.3 %collective-permute-start.5 = (bf16[384,384]{1,0:T(8,128)(2,1)S(1)}, bf16[384,384]{1,0:T(8,128)(2,1)S(1)}, u32[]{:S(2)}, u32[]{:S(2)}) collective-permute-start(bf16[384,384]{1,0:T(8,128)(2,1)S(1)} %get-tuple-element.55), channel_id=1, source_target_pairs={{0,1},{1,0},{2,3},{3,2},{4,5},{5,4},{6,7},{7,6},{8,9},{9,8},{10,11... | collective-permute-start | bytes 884744 | tf_op jit(solution)/shard_map/ppermute | solution.py:631
  48.9 6.1 %collective-permute-start.6 = (bf16[2,2,192,768]{3,2,1,0:T(8,128)(2,1)}, bf16[2,2,192,768]{3,2,1,0:T(8,128)(2,1)S(1)}, u32[]{:S(2)}, u32[]{:S(2)}) collective-permute-start(bf16[2,2,192,768]{3,2,1,0:T(8,128)(2,1)} %weight_grads_other_core.1), channel_id=1, source_target_pairs={{0,1},{1,0},{2,3},{3,2},{4,5},{5,4},{6,7},{7,6},{8,9},{9,8},{10,11... | collective-permute-start | bytes 3538952 | tf_op jit(solution)/shard_map/ppermute | solution.py:694
  50.2 13.3 %all-to-all-start = ((bf16[8,48,384]{2,1,0:T(8,128)(2,1)}), bf16[8,48,384]{2,1,0:T(8,128)(2,1)S(1)}, u32[]{:S(2)}, u32[]{:S(2)}) async-start(bf16[8,48,384]{2,1,0:T(8,128)(2,1)} %bitcast.9), calls=%async_computation | async-start | bytes 589824 | tf_op jit(solution)/shard_map/all_to_all | solution.py:672
  55.0 1.0 %copy-start.5 = (bf16[2,2,192,768]{3,2,1,0:T(8,128)(2,1)}, bf16[2,2,192,768]{3,2,1,0:T(8,128)(2,1)S(1)}, u32[]{:S(2)}) copy-start(bf16[2,2,192,768]{3,2,1,0:T(8,128)(2,1)S(1)} %collective-permute-done.6.got) | copy-start | bytes 3538948
  56.1 1.3 %copy-start.6 = (bf16[2,2,192,768]{3,2,1,0:T(8,128)(2,1)S(1)}, bf16[2,2,192,768]{3,2,1,0:T(8,128)(2,1)}, u32[]{:S(2)}) copy-start(bf16[2,2,192,768]{3,2,1,0:T(8,128)(2,1)} %copy-done.5) | copy-start | bytes 3538948
  62.3 0.8 copy-start.10
  63.1 27.7 %copy-start.1 = (f32[343,768]{1,0:T(8,128)S(1)}, f32[343,768]{1,0:T(8,128)}, u32[]{:S(2)}) copy-start(f32[343,768]{1,0:T(8,128)} %taps.3) | copy-start | bytes 3161092
  64.3 30.8 %all-to-all-start.2 = ((bf16[8,48,384]{2,1,0:T(8,128)(2,1)}), bf16[8,48,384]{2,1,0:T(8,128)(2,1)S(1)}, u32[]{:S(2)}, u32[]{:S(2)}) async-start(bf16[8,48,384]{2,1,0:T(8,128)(2,1)} %kernel_grad_sum.1), calls=%async_computation.2 | async-start | bytes 589824 | tf_op jit(solution)/shard_map/all_to_all | solution.py:729
  69.3 25.8 %collective-permute-start.10 = (bf16[2,192,768]{2,1,0:T(8,128)(2,1)}, bf16[2,192,768]{2,1,0:T(8,128)(2,1)S(1)}, u32[]{:S(2)}, u32[]{:S(2)}) collective-permute-start(bf16[2,192,768]{2,1,0:T(8,128)(2,1)} %copy-done.10), channel_id=1, source_target_pairs={{0,2},{1,3},{2,0},{3,1},{4,6},{5,7},{6,4},{7,5},{8,10},{9,11},{10,... | collective-permute-start | bytes 1769480 | tf_op jit(solution)/shard_map/ppermute | solution.py:715
  70.7 3.5 %collective-permute-start.7 = (bf16[128,768]{1,0:T(8,128)(2,1)S(1)}, bf16[128,768]{1,0:T(8,128)(2,1)S(1)}, u32[]{:S(2)}, u32[]{:S(2)}) collective-permute-start(bf16[128,768]{1,0:T(8,128)(2,1)S(1)} %get-tuple-element.63.grads.own), channel_id=1, source_target_pairs={{0,1},{1,0},{2,3},{3,2},{4,5},{5,4},{6,7},{7,6},{8,9},{9,8},{10,11... | collective-permute-start | bytes 589832 | tf_op jit(solution)/shard_map/ppermute | solution.py:465
  72.3 18.5 %collective-permute-start.8 = (bf16[128,768]{1,0:T(8,128)(2,1)S(1)}, bf16[128,768]{1,0:T(8,128)(2,1)S(1)}, u32[]{:S(2)}, u32[]{:S(2)}) collective-permute-start(bf16[128,768]{1,0:T(8,128)(2,1)S(1)} %get-tuple-element.63.grads.own), channel_id=1, source_target_pairs={{1,2},{3,4},{5,6},{7,8},{9,10},{11,12},{13,14},{2,1},{4,3},{6,5},{... | collective-permute-start | bytes 589832 | tf_op jit(solution)/shard_map/ppermute | solution.py:466
  95.1 1.6 %collective-permute-start.9 = (bf16[8,48,384]{2,1,0:T(8,128)(2,1)S(1)}, bf16[8,48,384]{2,1,0:T(8,128)(2,1)S(1)}, u32[]{:S(2)}, u32[]{:S(2)}) collective-permute-start(bf16[8,48,384]{2,1,0:T(8,128)(2,1)S(1)} %all-to-all-done.2.own), channel_id=1, source_target_pairs={{0,1},{1,0},{2,3},{3,2},{4,5},{5,4},{6,7},{7,6},{8,9},{9,8},{10,11... | collective-permute-start | bytes 884744 | tf_op jit(solution)/shard_map/ppermute | solution.py:758

commit v10 on v9

--- a/solution.py
+++ b/solution.py
@@ -387,32 +387,30 @@
     )
 
 
-def other_core_terms_kernel(which, weight_in, weight_out, scale, normed, *rest):
-    *cotangents, out, aligned = rest
-    terms = weight_grad_terms(which, weight_in, weight_out, scale, normed, cotangents, aligned)
-    for k in range(2):
-        out[0, k] = terms[k].astype(BF16)
-
-
-def own_core_terms_kernel(which, weight_in, weight_out, scale, normed, got, *rest):
+def side_terms_kernel(which, weight_in, weight_out, scale, normed, *rest):
     *cotangents, sent, kept, aligned = rest
     terms = weight_grad_terms(which, weight_in, weight_out, scale, normed, cotangents, aligned)
     step = pl.program_id(0)
-    for k in range(2):
-        total = terms[k] + got[0, k].astype(F32)
-
-        @pl.when(step == 0)
-        def _():
-            sent[k] = total.astype(BF16)
-
-        @pl.when(step == 1)
-        def _():
-            kept[k] = total
-
-
-def last_sum_kernel(kept, got, in_grad, out_grad):
+
+    @pl.when(step == 0)
+    def _():
+        for k in range(2):
+            sent[k] = terms[k].astype(BF16)
+
+    @pl.when(step == 1)
+    def _():
+        for k in range(2):
+            kept[k] = terms[k]
+
+
+def far_sum_kernel(kept, got, in_grad, out_grad):
     for k, out in enumerate((in_grad, out_grad)):
-        out[...] = kept[k] + got[k].astype(F32)
+        out[...] = (kept[k] + got[k].astype(F32)).astype(BF16)
+
+
+def last_sum_kernel(kept, got, in_far, out_far, in_grad, out_grad):
+    for k, (far, out) in enumerate(((in_far, in_grad), (out_far, out_grad))):
+        out[...] = (kept[k] + got[k].astype(F32)) + far[...].astype(F32)
 
 
 def chip_sum_kernel(kept, got, out):
@@ -646,29 +644,44 @@
     base = me // quad * quad
     side = lax.rem(me, quad) // 2
     place = lax.rem(me // quad + line - jnp.arange(line, dtype=jnp.int32), line)
+    far = base + 2 * (1 - side)
+    near = base + 2 * side
     which = jnp.concatenate(
         [
-            jnp.stack(
-                [
-                    base + 1 - core,
-                    base + 3 - core,
-                    base + 2 - 2 * side + core,
-                    base + 2 * side + core,
-                ]
-            ).astype(jnp.int32),
+            jnp.stack([far + 1 - core, far + core, near + 1 - core, near + core]).astype(jnp.int32),
             place.astype(jnp.int32),
         ]
     )
-    pair = (2, 2, share, channels)
-
-    def chunk(at):
-        return pl.BlockSpec((share, channels), lambda s, w: (w[s + at], 0))
-
-    sets = [whole_block(channels), whole_block(line, rows, channels)]
-    cotangents = [whole_block(rows, channels)] * line
-    aligned = [pltpu.VMEM((tokens, channels), BF16)]
-
-    which, sums = lax.optimization_barrier((which, sums))
+    pair = (2, share, channels)
+
+    def side_terms(first, name):
+        chunk = pl.BlockSpec((share, channels), lambda s, w: (w[s + first], 0))
+        return pl.pallas_call(
+            side_terms_kernel,
+            grid_spec=pltpu.PrefetchScalarGridSpec(
+                num_scalar_prefetch=1,
+                grid=(2,),
+                in_specs=[
+                    chunk,
+                    chunk,
+                    whole_block(channels),
+                    whole_block(line, rows, channels),
+                ]
+                + [whole_block(rows, channels)] * line,
+                out_specs=[whole_block(*pair)] * 2,
+                scratch_shapes=[pltpu.VMEM((tokens, channels), BF16)],
+            ),
+            out_shape=[jax.ShapeDtypeStruct(pair, BF16), jax.ShapeDtypeStruct(pair, F32)],
+            compiler_params=params(),
+            cost_estimate=NO_COST,
+            name=name,
+        )(which, weight_in, weight_out, layer_scale, gathered, *upstream_line)
+
+    which, sums, grad_inner, grad_outer = lax.optimization_barrier(
+        (which, sums, grad_inner, grad_outer)
+    )
+    far_sent, far_kept = side_terms(0, "weight_grads_far_side")
+    far_got = lax.ppermute(far_sent, "row", other_core)
     scattered = lax.all_to_all(
         sums.reshape(half, piece, wide),
         "row",
@@ -677,42 +690,23 @@
         tiled=True,
         axis_index_groups=alike,
     )
-    for_other = pl.pallas_call(
-        other_core_terms_kernel,
-        grid_spec=pltpu.PrefetchScalarGridSpec(
-            num_scalar_prefetch=1,
-            grid=(2,),
-            in_specs=[chunk(0), chunk(0)] + sets + cotangents,
-            out_specs=pl.BlockSpec((1,) + pair[1:], lambda s, w: (s, 0, 0, 0)),
-            scratch_shapes=aligned,
-        ),
-        out_shape=jax.ShapeDtypeStruct(pair, BF16),
-        compiler_params=params(),
-        cost_estimate=NO_COST,
-        name="weight_grads_other_core",
-    )(which, weight_in, weight_out, layer_scale, gathered, *upstream_line)
-    from_other = lax.ppermute(for_other, "row", other_core)
-    sent, kept = pl.pallas_call(
-        own_core_terms_kernel,
-        grid_spec=pltpu.PrefetchScalarGridSpec(
-            num_scalar_prefetch=1,
-            grid=(2,),
-            in_specs=[chunk(2), chunk(2)]
-            + sets
-            + [pl.BlockSpec((1,) + pair[1:], lambda s, w: ((w[s + 2] - w[0] // 4 * 4) // 2, 0, 0, 0))]
-            + cotangents,
-            out_specs=[whole_block(2, share, channels)] * 2,
-            scratch_shapes=aligned,
-        ),
-        out_shape=[
-            jax.ShapeDtypeStruct(pair[1:], BF16),
-            jax.ShapeDtypeStruct(pair[1:], F32),
-        ],
-        compiler_params=params(),
-        cost_estimate=NO_COST,
-        name="weight_grads_own_core",
-    )(which, weight_in, weight_out, layer_scale, gathered, from_other, *upstream_line)
-    got = lax.ppermute(sent, "row", other_side)
+    in_sent, out_sent = pl.pallas_call(
+        far_sum_kernel,
+        grid=(1,),
+        in_specs=[whole_block(*pair)] * 2,
+        out_specs=[whole_block(*pair[1:])] * 2,
+        out_shape=[jax.ShapeDtypeStruct(pair[1:], BF16)] * 2,
+        compiler_params=params(),
+        cost_estimate=NO_COST,
+        name="weight_grads_far_sum",
+    )(far_kept, far_got)
+    in_far = lax.ppermute(in_sent, "row", other_side)
+
+    which, out_sent = lax.optimization_barrier((which, out_sent))
+    sent, kept = side_terms(2, "weight_grads_near_side")
+    sent, in_far = lax.optimization_barrier((sent, in_far))
+    got = lax.ppermute(sent, "row", other_core)
+    out_far = lax.ppermute(out_sent, "row", other_side)
 
     scattered, kept = lax.optimization_barrier((scattered, kept))
     copies = pl.pallas_call(
@@ -725,7 +719,7 @@
         cost_estimate=NO_COST,
         name="kernel_grad_sum",
     )(scattered)
-    conv_own, copies = lax.optimization_barrier((conv_grad, copies))
+    conv_own, copies, out_far = lax.optimization_barrier((conv_grad, copies, out_far))
     totals = lax.all_to_all(
         copies, "row", split_axis=0, concat_axis=0, tiled=True, axis_index_groups=alike
     )
@@ -774,13 +768,13 @@
     weight_in_grad, weight_out_grad = pl.pallas_call(
         last_sum_kernel,
         grid=(1,),
-        in_specs=[whole_block(2, share, channels)] * 2,
-        out_specs=[whole_block(share, channels)] * 2,
-        out_shape=[jax.ShapeDtypeStruct((share, channels), F32)] * 2,
+        in_specs=[whole_block(*pair)] * 2 + [whole_block(*pair[1:])] * 2,
+        out_specs=[whole_block(*pair[1:])] * 2,
+        out_shape=[jax.ShapeDtypeStruct(pair[1:], F32)] * 2,
         compiler_params=params(),
         cost_estimate=NO_COST,
         name="weight_grads_sum",
-    )(kept, got)
+    )(kept, got, in_far, out_far)
 
     return (
         block_out.reshape(voxels.shape),

time: 98.5 us -> 93.7 us (0.951)
  waiting for transfers between devices: 20.6 us -> 11.6 us
  Pallas kernels: 39.4 us -> 42 us
  starting transfers between devices: 31.5 us -> 32.9 us
    ppermute x2, waiting for transfers between devices: 16.6 us -> 3.76 us  [rims(): lax.ppermute(cells, 'row', between + [(j, i) for i, j in between])]
    ppermute x2 -> x4, waiting for transfers between devices: 0.01 us -> 5.79 us  [the longest x1 3.51 us: on_device(): out_far = lax.ppermute(out_sent, 'row', other_side)]
    pallas_call x3 -> x4, Pallas kernels: 11.1 us -> 13.8 us  [the longest x2 9.59 us: side_terms(): pl.pallas_call(side_terms_kernel, grid_spec=pltpu.PrefetchScalarGridSpec(...]
    ppermute x1, starting transfers between devices: 0.01 us -> 1.6 us  [on_device(): other_totals = lax.ppermute(totals, 'row', other_core)]
    ppermute x2, starting transfers between devices: 5.09 us -> 6.65 us  [rims(): lax.ppermute(cells, 'row', between + [(j, i) for i, j in between])]
    ppermute x2, starting transfers between devices: 2.51 us -> 1.03 us  [rims(): lax.ppermute(cells, 'row', [(i, i ^ 1) for i in range(count)])]
    all_to_all x1, starting transfers between devices: 4.84 us -> 6.18 us  [on_device(): lax.all_to_all(sums.reshape(half, piece, wide), 'row', split_axis=0, conc...]
    ppermute x1, waiting for transfers between devices: 1.11 us -> 0.01 us  [on_device(): half_got = lax.ppermute(half_sent, 'row', other_core)]
  transfers between devices with their start and end apart: 14 -> 16, of which waited for: 6 -> 5; matrix products, arithmetic and copies ran while one was open for 0% -> 0% of each run, Pallas kernels for 33% -> 38%
where the time goes in v10:
time: 93.7 us; the launch traced here: 93 us
  Pallas kernels  42 us (45%)
  starting transfers between devices  32.9 us (35%)
  waiting for transfers between devices  11.6 us (12%)
  local copies, waits for them, and re-layouts  5.6 us (6%)
    pallas_call x2, Pallas kernels, side_terms(): pl.pallas_call(side_terms_kernel, grid_spec=pltpu.PrefetchScalarGridSpec(...  9.59 us
    pallas_call x1, Pallas kernels, on_device(): pl.pallas_call(mlp_kernel, grid=(units // block,), in_specs=[pl.BlockSpec...  9.41 us
    ppermute x2, starting transfers between devices, rims(): lax.ppermute(cells, 'row', between + [(j, i) for i, j in between])  6.65 us
    all_to_all x1, starting transfers between devices, on_device(): lax.all_to_all(sums.reshape(half, piece, wide), 'row', split_axis=0, conc...  6.18 us
    pallas_call x1, Pallas kernels, on_device(): pl.pallas_call(functools.partial(kernel_grad_kernel, planes, height), gri...  6.18 us
    ppermute x3, starting transfers between devices, along_line(): lax.ppermute(cells, 'row', [(i, (i + quad * steps) % count) for i in rang...  5.75 us
    unnamed x26, local copies, waits for them, and re-layouts  5.51 us
    pallas_call x1, Pallas kernels, on_device(): pl.pallas_call(functools.partial(input_grad_kernel, planes, height), grid...  4.29 us
  transfers between devices with their start and end apart: 16, of which 5 were waited for; matrix products, arithmetic and copies ran while one was open for 0% of the time, Pallas kernels for 38%

profile of v10, /device:TPU:1, one launch (start us, length us, event | category | flops | bytes accessed | tf_op | source)
XLA Modules:
  0.0 93.0 jit_solution(947034646183082549)
XLA Ops:
  0.6 2.2 %collective-permute-start.2 = (bf16[128,768]{1,0:T(8,128)(2,1)}, bf16[128,768]{1,0:T(8,128)(2,1)S(1)}, u32[]{:S(2)}, u32[]{:S(2)}) collective-permute-start(bf16[128,768]{1,0:T(8,128)(2,1)} %bitcast.11), channel_id=1, source_target_pairs={{0,4},{1,5},{2,6},{3,7},{4,8},{5,9},{6,10},{7,11},{8,12},{9,13},{1... | collective-permute-start | bytes 589832 | tf_op jit(solution)/shard_map/ppermute | solution.py:491
  2.8 2.1 %collective-permute-start.3 = (bf16[128,768]{1,0:T(8,128)(2,1)}, bf16[128,768]{1,0:T(8,128)(2,1)S(1)}, u32[]{:S(2)}, u32[]{:S(2)}) collective-permute-start(bf16[128,768]{1,0:T(8,128)(2,1)} %bitcast.12), channel_id=1, source_target_pairs={{0,12},{1,13},{2,14},{3,15},{4,0},{5,1},{6,2},{7,3},{8,4},{9,5},{1... | collective-permute-start | bytes 589832 | tf_op jit(solution)/shard_map/ppermute | solution.py:491
  4.9 1.0 %collective-permute-start = (bf16[128,768]{1,0:T(8,128)(2,1)}, bf16[128,768]{1,0:T(8,128)(2,1)S(1)}, u32[]{:S(2)}, u32[]{:S(2)}) collective-permute-start(bf16[128,768]{1,0:T(8,128)(2,1)} %bitcast.17), channel_id=1, source_target_pairs={{0,1},{1,0},{2,3},{3,2},{4,5},{5,4},{6,7},{7,6},{8,9},{9,8},{10,11... | collective-permute-start | bytes 589832 | tf_op jit(solution)/shard_map/ppermute | solution.py:463
  5.9 3.2 %collective-permute-start.1 = (bf16[128,768]{1,0:T(8,128)(2,1)}, bf16[128,768]{1,0:T(8,128)(2,1)S(1)}, u32[]{:S(2)}, u32[]{:S(2)}) collective-permute-start(bf16[128,768]{1,0:T(8,128)(2,1)} %bitcast.18), channel_id=1, source_target_pairs={{1,2},{3,4},{5,6},{7,8},{9,10},{11,12},{13,14},{2,1},{4,3},{6,5},{... | collective-permute-start | bytes 589832 | tf_op jit(solution)/shard_map/ppermute | solution.py:464
  9.0 0.0 copy-start
  9.1 1.2 %copy-done = f32[343,768]{1,0:T(8,128)S(1)} copy-done((f32[343,768]{1,0:T(8,128)S(1)}, f32[343,768]{1,0:T(8,128)}, u32[]{:S(2)}) %copy-start) | copy-done | bytes 1053720
  10.3 0.9 copy-done.3
  11.2 2.1 %own_conv.1 = (f32[128,768]{1,0:T(8,128)S(1)}, f32[6,9,7,8,128]{4,3,2,1,0:T(8,128)S(1)}) custom-call(bf16[128,768]{1,0:T(8,128)(2,1)S(1)} %bitcast.19, f32[343,768]{1,0:T(8,128)S(1)} %copy-done), custom_call_target="tpu_custom_call" | custom-call | tf_op jit(solution)/shard_map/own_conv/pallas_call | solution.py:501
  13.4 0.0 collective-permute-done.2.rest_1_
  13.4 0.1 collective-permute-done.3.rest_3_
  13.4 1.5 %collective-permute-start.4 = (bf16[128,768]{1,0:T(8,128)(2,1)S(1)}, bf16[128,768]{1,0:T(8,128)(2,1)S(1)}, u32[]{:S(2)}, u32[]{:S(2)}) collective-permute-start(bf16[128,768]{1,0:T(8,128)(2,1)S(1)} %collective-permute-done.2.rest_1_), channel_id=1, source_target_pairs={{0,4},{1,5},{2,6},{3,7},{4,8},{5,9},{6,10},{7,11},{8,12},{9,13},{1... | collective-permute-start | bytes 589832 | tf_op jit(solution)/shard_map/ppermute | solution.py:491
  14.9 0.0 collective-permute-done.inner
  14.9 0.0 collective-permute-done.1.outer
  14.9 3.6 %rim_conv.1 = (bf16[4,128,768]{2,1,0:T(8,128)(2,1)}, f32[128,768]{1,0:T(8,128)S(1)}) custom-call(s32[1]{0:T(128)} %bitcast.core, bf16[128,768]{1,0:T(8,128)(2,1)S(1)} %collective-permute-done.inner, bf16[128,768]{1,0:T(8,128)(2,1)S(1)} %collective-permute-done.1.outer, f32[6,9,7,8,128]{4,3,2,1,0:T(8,128)S(1)} %get-tuple-element.52.split, ...), custom_call_target="tpu_custom_call" | custom-call | tf_op jit(solution)/shard_map/rim_conv/pallas_call | solution.py:521
  18.6 2.0 %collective-permute-done.4.rest_2_ = bf16[128,768]{1,0:T(8,128)(2,1)S(1)} collective-permute-done((bf16[128,768]{1,0:T(8,128)(2,1)S(1)}, bf16[128,768]{1,0:T(8,128)(2,1)S(1)}, u32[]{:S(2)}, u32[]{:S(2)}) %collective-permute-start.4) | collective-permute-done | bytes 196640 | tf_op jit(solution)/shard_map/ppermute | solution.py:491
  20.5 3.5 %all-to-all-start.1 = ((bf16[4,128,768]{2,1,0:T(8,128)(2,1)}), bf16[4,128,768]{2,1,0:T(8,128)(2,1)S(1)}, u32[]{:S(2)}, u32[]{:S(2)}) async-start(bf16[4,128,768]{2,1,0:T(8,128)(2,1)} %get-tuple-element.58.normed), calls=%async_computation.1 | async-start | bytes 1572864 | tf_op jit(solution)/shard_map/all_to_all | solution.py:552
  24.0 0.1 pad_add_fusion.which
  24.1 9.4 %mlp_both_ways.1 = (bf16[128,768]{1,0:T(8,128)(2,1)}, bf16[128,768]{1,0:T(8,128)(2,1)S(1)}, f32[8,768]{1,0:T(8,128)S(1)}) custom-call(bf16[4,128,768]{2,1,0:T(8,128)(2,1)} %get-tuple-element.58.normed, bf16[3072,768]{1,0:T(8,128)(2,1)} %weight_in.5, bf16[3072,768]{1,0:T(8,128)(2,1)} %weight_out.5, f32[128,768]{1,0:T(8,128)S(1)} %get-tuple-element.59.centered, ...), custom_call_target="tpu_custom_call" | custom-call | tf_op jit(solution)/shard_map/mlp_both_ways/pallas_call | solution.py:558
  33.5 6.2 %kernel_grad_terms.1 = (bf16[384,384]{1,0:T(8,128)(2,1)S(1)}, bf16[384,384]{1,0:T(8,128)(2,1)S(1)}) custom-call(s32[2]{0:T(128)S(1)} %pad_add_fusion.which, bf16[128,768]{1,0:T(8,128)(2,1)S(1)} %collective-permute-done.inner, bf16[128,768]{1,0:T(8,128)(2,1)S(1)} %bitcast.21, bf16[128,768]{1,0:T(8,128)(2,1)S(1)} %collective-permute-done.1.outer, ...), custom_call_target="tpu_custom_call" | custom-call | tf_op jit(solution)/shard_map/kernel_grad_terms/pallas_call | solution.py:605
  39.7 2.1 %collective-permute-start.5 = (bf16[384,384]{1,0:T(8,128)(2,1)S(1)}, bf16[384,384]{1,0:T(8,128)(2,1)S(1)}, u32[]{:S(2)}, u32[]{:S(2)}) collective-permute-start(bf16[384,384]{1,0:T(8,128)(2,1)S(1)} %get-tuple-element.66), channel_id=1, source_target_pairs={{0,1},{1,0},{2,3},{3,2},{4,5},{5,4},{6,7},{7,6},{8,9},{9,8},{10,11... | collective-permute-start | bytes 884744 | tf_op jit(solution)/shard_map/ppermute | solution.py:629
  41.8 0.1 collective-permute-start.6
  41.9 3.5 %collective-permute-start.7 = (bf16[128,768]{1,0:T(8,128)(2,1)S(1)}, bf16[128,768]{1,0:T(8,128)(2,1)S(1)}, u32[]{:S(2)}, u32[]{:S(2)}) collective-permute-start(bf16[128,768]{1,0:T(8,128)(2,1)S(1)} %get-tuple-element.80.grads.own), channel_id=1, source_target_pairs={{1,2},{3,4},{5,6},{7,8},{9,10},{11,12},{13,14},{2,1},{4,3},{6,5},{... | collective-permute-start | bytes 589832 | tf_op jit(solution)/shard_map/ppermute | solution.py:464
  45.4 0.1 concatenate.3.which
  45.5 0.8 kernel_grad_chip_sum.1
  46.3 3.8 %collective-permute-done.7.outer = bf16[128,768]{1,0:T(8,128)(2,1)S(1)} collective-permute-done((bf16[128,768]{1,0:T(8,128)(2,1)S(1)}, bf16[128,768]{1,0:T(8,128)(2,1)S(1)}, u32[]{:S(2)}, u32[]{:S(2)}) %collective-permute-start.7) | collective-permute-done | bytes 196640 | tf_op jit(solution)/shard_map/ppermute | solution.py:464
  50.1 0.7 copy-done.7
  50.7 0.0 all-to-all-done.1.normed
  50.7 5.2 %weight_grads_far_side.1 = (bf16[2,192,768]{2,1,0:T(8,128)(2,1)}, f32[2,192,768]{2,1,0:T(8,128)S(1)}) custom-call(s32[8]{0:T(128)S(1)} %concatenate.3.which, bf16[3072,768]{1,0:T(8,128)(2,1)} %weight_in.5, bf16[3072,768]{1,0:T(8,128)(2,1)} %weight_out.5, f32[768]{0:T(1024)S(1)} %copy-done.9, bf16[4,128,768]{2,1,0:T(8,128)(2,1)S(1)} %all-to-all-done.1.normed, ...), custom_call_target="tpu_custom_call" | custom-call | tf_op jit(solution)/shard_map/weight_grads_far_side/pallas_call | solution.py:659
  55.9 6.2 %all-to-all-start = ((bf16[8,48,384]{2,1,0:T(8,128)(2,1)}), bf16[8,48,384]{2,1,0:T(8,128)(2,1)S(1)}, u32[]{:S(2)}, u32[]{:S(2)}) async-start(bf16[8,48,384]{2,1,0:T(8,128)(2,1)} %bitcast.9), calls=%async_computation | async-start | bytes 589824 | tf_op jit(solution)/shard_map/all_to_all | solution.py:685
  62.1 2.0 %weight_grads_far_sum.1 = (bf16[192,768]{1,0:T(8,128)(2,1)}, bf16[192,768]{1,0:T(8,128)(2,1)}) custom-call(f32[2,192,768]{2,1,0:T(8,128)S(1)} %get-tuple-element.71.kept, bf16[2,192,768]{2,1,0:T(8,128)(2,1)} %collective-permute-done.8.got), custom_call_target="tpu_custom_call" | custom-call | tf_op jit(solution)/shard_map/weight_grads_far_sum/pallas_call | solution.py:693
  64.1 1.5 %collective-permute-start.9 = (bf16[192,768]{1,0:T(8,128)(2,1)}, bf16[192,768]{1,0:T(8,128)(2,1)}, u32[]{:S(2)}, u32[]{:S(2)}) collective-permute-start(bf16[192,768]{1,0:T(8,128)(2,1)} %get-tuple-element.77), channel_id=1, source_target_pairs={{0,2},{1,3},{2,0},{3,1},{4,6},{5,7},{6,4},{7,5},{8,10},{9,11},{10,... | collective-permute-start | bytes 884744 | tf_op jit(solution)/shard_map/ppermute | solution.py:709
  65.6 0.0 collective-permute-start.11
  65.6 4.4 %weight_grads_near_side.1 = (bf16[2,192,768]{2,1,0:T(8,128)(2,1)S(1)}, f32[2,192,768]{2,1,0:T(8,128)S(1)}) custom-call(s32[8]{0:T(128)S(1)} %concatenate.3.which, bf16[3072,768]{1,0:T(8,128)(2,1)} %weight_in.5, bf16[3072,768]{1,0:T(8,128)(2,1)} %weight_out.5, f32[768]{0:T(1024)S(1)} %copy-done.9, bf16[4,128,768]{2,1,0:T(8,128)(2,1)S(1)} %all-to-all-done.1.normed, ...), custom_call_target="tpu_custom_call" | custom-call | tf_op jit(solution)/shard_map/weight_grads_near_side/pallas_call | solution.py:659
  70.0 0.0 copy-start.12
  70.0 0.8 copy-done.12
  70.8 0.0 all-to-all-done.parts
  70.8 0.8 kernel_grad_sum.1
  71.6 3.5 %collective-permute-done.9.out_far = bf16[192,768]{1,0:T(8,128)(2,1)} collective-permute-done((bf16[192,768]{1,0:T(8,128)(2,1)}, bf16[192,768]{1,0:T(8,128)(2,1)}, u32[]{:S(2)}, u32[]{:S(2)}) %collective-permute-start.9) | collective-permute-done | bytes 294944 | tf_op jit(solution)/shard_map/ppermute | solution.py:709
  75.1 4.0 %all-to-all-start.2 = ((bf16[8,48,384]{2,1,0:T(8,128)(2,1)}), bf16[8,48,384]{2,1,0:T(8,128)(2,1)S(1)}, u32[]{:S(2)}, u32[]{:S(2)}) async-start(bf16[8,48,384]{2,1,0:T(8,128)(2,1)} %kernel_grad_sum.1), calls=%async_computation.2 | async-start | bytes 589824 | tf_op jit(solution)/shard_map/all_to_all | solution.py:723
  79.2 2.3 %collective-permute-done.11.in_far = bf16[192,768]{1,0:T(8,128)(2,1)} collective-permute-done((bf16[192,768]{1,0:T(8,128)(2,1)}, bf16[192,768]{1,0:T(8,128)(2,1)}, u32[]{:S(2)}, u32[]{:S(2)}) %collective-permute-start.11) | collective-permute-done | bytes 294944 | tf_op jit(solution)/shard_map/ppermute | solution.py:703
  81.4 0.6 collective-permute-start.12
  82.0 0.9 copy-done.6
  83.0 0.9 copy-done.8
  83.9 4.3 %input_grad_conv.1 = bf16[128,768]{1,0:T(8,128)(2,1)} custom-call(s32[1]{0:T(128)} %bitcast.core, bf16[128,768]{1,0:T(8,128)(2,1)S(1)} %copy-done.6, bf16[128,768]{1,0:T(8,128)(2,1)S(1)} %get-tuple-element.80.grads.own, bf16[128,768]{1,0:T(8,128)(2,1)S(1)} %copy-done.8, f32[343,768]{1,0:T(8,128)S(1)} %copy-done.1, bf16[128,768]{1,0:T(8,128)(2,1)S(1)} %bitcast.16), custom_call_target="tpu_custom_call" | custom-call | tf_op jit(solution)/shard_map/input_grad_conv/pallas_call | solution.py:727
  88.2 0.0 all-to-all-done.2.own
  88.2 1.6 %collective-permute-start.10 = (bf16[8,48,384]{2,1,0:T(8,128)(2,1)S(1)}, bf16[8,48,384]{2,1,0:T(8,128)(2,1)S(1)}, u32[]{:S(2)}, u32[]{:S(2)}) collective-permute-start(bf16[8,48,384]{2,1,0:T(8,128)(2,1)S(1)} %all-to-all-done.2.own), channel_id=1, source_target_pairs={{0,1},{1,0},{2,3},{3,2},{4,5},{5,4},{6,7},{7,6},{8,9},{9,8},{10,11... | collective-permute-start | bytes 884744 | tf_op jit(solution)/shard_map/ppermute | solution.py:752
  89.8 2.2 %weight_grads_sum.1 = (f32[192,768]{1,0:T(8,128)}, f32[192,768]{1,0:T(8,128)}) custom-call(f32[2,192,768]{2,1,0:T(8,128)S(1)} %get-tuple-element.88.kept, bf16[2,192,768]{2,1,0:T(8,128)(2,1)S(1)} %collective-permute-done.12.got, bf16[192,768]{1,0:T(8,128)(2,1)} %collective-permute-done.11.in_far, bf16[192,768]{1,0:T(8,128)(2,1)} %collective-permute-done.9.out_far), custom_call_target="tpu_custom_call" | custom-call | tf_op jit(solution)/shard_map/weight_grads_sum/pallas_call | solution.py:768
  92.0 1.1 %kernel_grad_unpack.1 = (f32[343,768]{1,0:T(8,128)}, f32[768]{0:T(1024)}, f32[768]{0:T(1024)}, f32[768]{0:T(1024)}) custom-call(s32[1]{0:T(128)} %bitcast.core, bf16[8,48,384]{2,1,0:T(8,128)(2,1)S(1)} %all-to-all-done.2.own, bf16[8,48,384]{2,1,0:T(8,128)(2,1)S(1)} %collective-permute-done.10.other), custom_call_target="tpu_custom_call" | custom-call | tf_op jit(solution)/shard_map/kernel_grad_unpack/pallas_call | solution.py:753
  (25 shorter events, 0.1 us)
Async XLA Ops:
  0.6 12.7 %collective-permute-start.2 = (bf16[128,768]{1,0:T(8,128)(2,1)}, bf16[128,768]{1,0:T(8,128)(2,1)S(1)}, u32[]{:S(2)}, u32[]{:S(2)}) collective-permute-start(bf16[128,768]{1,0:T(8,128)(2,1)} %bitcast.11), channel_id=1, source_target_pairs={{0,4},{1,5},{2,6},{3,7},{4,8},{5,9},{6,10},{7,11},{8,12},{9,13},{1... | collective-permute-start | bytes 589832 | tf_op jit(solution)/shard_map/ppermute | solution.py:491
  2.8 10.6 %collective-permute-start.3 = (bf16[128,768]{1,0:T(8,128)(2,1)}, bf16[128,768]{1,0:T(8,128)(2,1)S(1)}, u32[]{:S(2)}, u32[]{:S(2)}) collective-permute-start(bf16[128,768]{1,0:T(8,128)(2,1)} %bitcast.12), channel_id=1, source_target_pairs={{0,12},{1,13},{2,14},{3,15},{4,0},{5,1},{6,2},{7,3},{8,4},{9,5},{1... | collective-permute-start | bytes 589832 | tf_op jit(solution)/shard_map/ppermute | solution.py:491
  4.9 10.0 %collective-permute-start = (bf16[128,768]{1,0:T(8,128)(2,1)}, bf16[128,768]{1,0:T(8,128)(2,1)S(1)}, u32[]{:S(2)}, u32[]{:S(2)}) collective-permute-start(bf16[128,768]{1,0:T(8,128)(2,1)} %bitcast.17), channel_id=1, source_target_pairs={{0,1},{1,0},{2,3},{3,2},{4,5},{5,4},{6,7},{7,6},{8,9},{9,8},{10,11... | collective-permute-start | bytes 589832 | tf_op jit(solution)/shard_map/ppermute | solution.py:463
  5.9 9.1 %collective-permute-start.1 = (bf16[128,768]{1,0:T(8,128)(2,1)}, bf16[128,768]{1,0:T(8,128)(2,1)S(1)}, u32[]{:S(2)}, u32[]{:S(2)}) collective-permute-start(bf16[128,768]{1,0:T(8,128)(2,1)} %bitcast.18), channel_id=1, source_target_pairs={{1,2},{3,4},{5,6},{7,8},{9,10},{11,12},{13,14},{2,1},{4,3},{6,5},{... | collective-permute-start | bytes 589832 | tf_op jit(solution)/shard_map/ppermute | solution.py:464
  9.0 1.2 %copy-start = (f32[343,768]{1,0:T(8,128)S(1)}, f32[343,768]{1,0:T(8,128)}, u32[]{:S(2)}) copy-start(f32[343,768]{1,0:T(8,128)} %taps.3) | copy-start | bytes 3161092
  10.3 0.9 copy-start.3
  11.2 3.7 %copy-start.10 = (f32[768]{0:T(1024)S(1)}, f32[768]{0:T(1024)}, u32[]{:S(2)}) copy-start(f32[768]{0:T(1024)} %norm_gain.1) | copy-start | bytes 9220
  11.2 3.7 %copy-start.11 = (f32[768]{0:T(1024)S(1)}, f32[768]{0:T(1024)}, u32[]{:S(2)}) copy-start(f32[768]{0:T(1024)} %bias.1) | copy-start | bytes 9220
  13.4 7.1 %collective-permute-start.4 = (bf16[128,768]{1,0:T(8,128)(2,1)S(1)}, bf16[128,768]{1,0:T(8,128)(2,1)S(1)}, u32[]{:S(2)}, u32[]{:S(2)}) collective-permute-start(bf16[128,768]{1,0:T(8,128)(2,1)S(1)} %collective-permute-done.2.rest_1_), channel_id=1, source_target_pairs={{0,4},{1,5},{2,6},{3,7},{4,8},{5,9},{6,10},{7,11},{8,12},{9,13},{1... | collective-permute-start | bytes 589832 | tf_op jit(solution)/shard_map/ppermute | solution.py:491
  18.6 5.6 %copy-start.2 = (bf16[4,4,8,768]{3,2,1,0:T(8,128)(2,1)S(1)}, bf16[4,4,8,768]{3,2,1,0:T(8,128)(2,1)}, u32[]{:S(2)}) copy-start(bf16[4,4,8,768]{3,2,1,0:T(8,128)(2,1)} %param.15) | copy-start | bytes 589828
  18.6 5.6 %copy-start.4 = (bf16[4,4,8,768]{3,2,1,0:T(8,128)(2,1)S(1)}, bf16[4,4,8,768]{3,2,1,0:T(8,128)(2,1)}, u32[]{:S(2)}) copy-start(bf16[4,4,8,768]{3,2,1,0:T(8,128)(2,1)} %param.8) | copy-start | bytes 589828
  18.6 5.6 %copy-start.9 = (f32[768]{0:T(1024)S(1)}, f32[768]{0:T(1024)}, u32[]{:S(2)}) copy-start(f32[768]{0:T(1024)} %scale.3) | copy-start | bytes 9220
  20.5 30.2 %all-to-all-start.1 = ((bf16[4,128,768]{2,1,0:T(8,128)(2,1)}), bf16[4,128,768]{2,1,0:T(8,128)(2,1)S(1)}, u32[]{:S(2)}, u32[]{:S(2)}) async-start(bf16[4,128,768]{2,1,0:T(8,128)(2,1)} %get-tuple-element.58.normed), calls=%async_computation.1 | async-start | bytes 1572864 | tf_op jit(solution)/shard_map/all_to_all | solution.py:552
  39.7 5.8 %collective-permute-start.5 = (bf16[384,384]{1,0:T(8,128)(2,1)S(1)}, bf16[384,384]{1,0:T(8,128)(2,1)S(1)}, u32[]{:S(2)}, u32[]{:S(2)}) collective-permute-start(bf16[384,384]{1,0:T(8,128)(2,1)S(1)} %get-tuple-element.66), channel_id=1, source_target_pairs={{0,1},{1,0},{2,3},{3,2},{4,5},{5,4},{6,7},{7,6},{8,9},{9,8},{10,11... | collective-permute-start | bytes 884744 | tf_op jit(solution)/shard_map/ppermute | solution.py:629
  41.8 4.5 %collective-permute-start.6 = (bf16[128,768]{1,0:T(8,128)(2,1)S(1)}, bf16[128,768]{1,0:T(8,128)(2,1)S(1)}, u32[]{:S(2)}, u32[]{:S(2)}) collective-permute-start(bf16[128,768]{1,0:T(8,128)(2,1)S(1)} %get-tuple-element.80.grads.own), channel_id=1, source_target_pairs={{0,1},{1,0},{2,3},{3,2},{4,5},{5,4},{6,7},{7,6},{8,9},{9,8},{10,11... | collective-permute-start | bytes 589832 | tf_op jit(solution)/shard_map/ppermute | solution.py:463
  41.9 8.2 %collective-permute-start.7 = (bf16[128,768]{1,0:T(8,128)(2,1)S(1)}, bf16[128,768]{1,0:T(8,128)(2,1)S(1)}, u32[]{:S(2)}, u32[]{:S(2)}) collective-permute-start(bf16[128,768]{1,0:T(8,128)(2,1)S(1)} %get-tuple-element.80.grads.own), channel_id=1, source_target_pairs={{1,2},{3,4},{5,6},{7,8},{9,10},{11,12},{13,14},{2,1},{4,3},{6,5},{... | collective-permute-start | bytes 589832 | tf_op jit(solution)/shard_map/ppermute | solution.py:464
  46.3 9.6 %copy-start.5 = (bf16[128,768]{1,0:T(8,128)(2,1)}, bf16[128,768]{1,0:T(8,128)(2,1)S(1)}, u32[]{:S(2)}) copy-start(bf16[128,768]{1,0:T(8,128)(2,1)S(1)} %collective-permute-done.6.inner) | copy-start | bytes 589828
  50.1 0.7 copy-start.7
  55.9 6.2 %collective-permute-start.8 = (bf16[2,192,768]{2,1,0:T(8,128)(2,1)}, bf16[2,192,768]{2,1,0:T(8,128)(2,1)}, u32[]{:S(2)}, u32[]{:S(2)}) collective-permute-start(bf16[2,192,768]{2,1,0:T(8,128)(2,1)} %get-tuple-element.72), channel_id=1, source_target_pairs={{0,1},{1,0},{2,3},{3,2},{4,5},{5,4},{6,7},{7,6},{8,9},{9,8},{10,11... | collective-permute-start | bytes 1769480 | tf_op jit(solution)/shard_map/ppermute | solution.py:684
  55.9 14.9 %all-to-all-start = ((bf16[8,48,384]{2,1,0:T(8,128)(2,1)}), bf16[8,48,384]{2,1,0:T(8,128)(2,1)S(1)}, u32[]{:S(2)}, u32[]{:S(2)}) async-start(bf16[8,48,384]{2,1,0:T(8,128)(2,1)} %bitcast.9), calls=%async_computation | async-start | bytes 589824 | tf_op jit(solution)/shard_map/all_to_all | solution.py:685
  64.1 11.0 %collective-permute-start.9 = (bf16[192,768]{1,0:T(8,128)(2,1)}, bf16[192,768]{1,0:T(8,128)(2,1)}, u32[]{:S(2)}, u32[]{:S(2)}) collective-permute-start(bf16[192,768]{1,0:T(8,128)(2,1)} %get-tuple-element.77), channel_id=1, source_target_pairs={{0,2},{1,3},{2,0},{3,1},{4,6},{5,7},{6,4},{7,5},{8,10},{9,11},{10,... | collective-permute-start | bytes 884744 | tf_op jit(solution)/shard_map/ppermute | solution.py:709
  65.6 15.9 %collective-permute-start.11 = (bf16[192,768]{1,0:T(8,128)(2,1)}, bf16[192,768]{1,0:T(8,128)(2,1)}, u32[]{:S(2)}, u32[]{:S(2)}) collective-permute-start(bf16[192,768]{1,0:T(8,128)(2,1)} %get-tuple-element.90), channel_id=1, source_target_pairs={{0,2},{1,3},{2,0},{3,1},{4,6},{5,7},{6,4},{7,5},{8,10},{9,11},{10,... | collective-permute-start | bytes 884744 | tf_op jit(solution)/shard_map/ppermute | solution.py:703
  70.0 0.8 copy-start.12
  70.8 11.2 %copy-start.1 = (f32[343,768]{1,0:T(8,128)S(1)}, f32[343,768]{1,0:T(8,128)}, u32[]{:S(2)}) copy-start(f32[343,768]{1,0:T(8,128)} %taps.3) | copy-start | bytes 3161092
  75.1 13.1 %all-to-all-start.2 = ((bf16[8,48,384]{2,1,0:T(8,128)(2,1)}), bf16[8,48,384]{2,1,0:T(8,128)(2,1)S(1)}, u32[]{:S(2)}, u32[]{:S(2)}) async-start(bf16[8,48,384]{2,1,0:T(8,128)(2,1)} %kernel_grad_sum.1), calls=%async_computation.2 | async-start | bytes 589824 | tf_op jit(solution)/shard_map/all_to_all | solution.py:723
  81.4 8.4 %collective-permute-start.12 = (bf16[2,192,768]{2,1,0:T(8,128)(2,1)}, bf16[2,192,768]{2,1,0:T(8,128)(2,1)S(1)}, u32[]{:S(2)}, u32[]{:S(2)}) collective-permute-start(bf16[2,192,768]{2,1,0:T(8,128)(2,1)} %copy-done.12), channel_id=1, source_target_pairs={{0,1},{1,0},{2,3},{3,2},{4,5},{5,4},{6,7},{7,6},{8,9},{9,8},{10,11... | collective-permute-start | bytes 1769480 | tf_op jit(solution)/shard_map/ppermute | solution.py:708
  82.0 0.9 copy-start.6
  83.0 0.9 copy-start.8
  88.2 3.8 %collective-permute-start.10 = (bf16[8,48,384]{2,1,0:T(8,128)(2,1)S(1)}, bf16[8,48,384]{2,1,0:T(8,128)(2,1)S(1)}, u32[]{:S(2)}, u32[]{:S(2)}) collective-permute-start(bf16[8,48,384]{2,1,0:T(8,128)(2,1)S(1)} %all-to-all-done.2.own), channel_id=1, source_target_pairs={{0,1},{1,0},{2,3},{3,2},{4,5},{5,4},{6,7},{7,6},{8,9},{9,8},{10,11... | collective-permute-start | bytes 884744 | tf_op jit(solution)/shard_map/ppermute | solution.py:752

commit v11 on v10

--- a/solution.py
+++ b/solution.py
@@ -311,13 +311,12 @@
     def _():
         mixed_grad[...] = (scale * cotangent[...].astype(F32)).astype(BF16)
 
-    hidden = lax.dot_general(
-        normed[...], weight_in[...], (((1,), (1,)), ((), ())), preferred_element_type=F32
-    )
+    across = (((1,), (1,)), ((), ()))
+    hidden = lax.dot_general(weight_in[...], normed[...], across, preferred_element_type=F32)
     act_grad = lax.dot_general(
-        mixed_grad[...], weight_out[...], (((1,), (1,)), ((), ())), preferred_element_type=F32
-    )
-    activated, hidden_grad = slopes(hidden, act_grad)
+        weight_out[...], mixed_grad[...], across, preferred_element_type=F32
+    )
+    activated, hidden_grad = [part.T for part in slopes(hidden, act_grad)]
     forward = jnp.dot(activated, weight_out[...], preferred_element_type=F32)
     backward = jnp.dot(hidden_grad, weight_in[...], preferred_element_type=F32)
 
@@ -400,12 +399,12 @@
     @pl.when(step == 1)
     def _():
         for k in range(2):
-            kept[k] = terms[k]
+            kept[k] = terms[k].astype(kept.dtype)
 
 
 def far_sum_kernel(kept, got, in_grad, out_grad):
     for k, out in enumerate((in_grad, out_grad)):
-        out[...] = (kept[k] + got[k].astype(F32)).astype(BF16)
+        out[...] = (kept[k].astype(F32) + got[k].astype(F32)).astype(BF16)
 
 
 def last_sum_kernel(kept, got, in_far, out_far, in_grad, out_grad):
@@ -654,7 +653,7 @@
     )
     pair = (2, share, channels)
 
-    def side_terms(first, name):
+    def side_terms(first, kept_as, name):
         chunk = pl.BlockSpec((share, channels), lambda s, w: (w[s + first], 0))
         return pl.pallas_call(
             side_terms_kernel,
@@ -671,16 +670,17 @@
                 out_specs=[whole_block(*pair)] * 2,
                 scratch_shapes=[pltpu.VMEM((tokens, channels), BF16)],
             ),
-            out_shape=[jax.ShapeDtypeStruct(pair, BF16), jax.ShapeDtypeStruct(pair, F32)],
+            out_shape=[jax.ShapeDtypeStruct(pair, BF16), jax.ShapeDtypeStruct(pair, kept_as)],
             compiler_params=params(),
             cost_estimate=NO_COST,
             name=name,
         )(which, weight_in, weight_out, layer_scale, gathered, *upstream_line)
 
-    which, sums, grad_inner, grad_outer = lax.optimization_barrier(
-        (which, sums, grad_inner, grad_outer)
-    )
-    far_sent, far_kept = side_terms(0, "weight_grads_far_side")
+    which, sums = lax.optimization_barrier((which, sums))
+    far_sent, far_kept = side_terms(0, BF16, "weight_grads_far_side")
+    far_sent, conv_own, grad_inner, grad_outer = lax.optimization_barrier(
+        (far_sent, conv_grad, grad_inner, grad_outer)
+    )
     far_got = lax.ppermute(far_sent, "row", other_core)
     scattered = lax.all_to_all(
         sums.reshape(half, piece, wide),
@@ -690,40 +690,6 @@
         tiled=True,
         axis_index_groups=alike,
     )
-    in_sent, out_sent = pl.pallas_call(
-        far_sum_kernel,
-        grid=(1,),
-        in_specs=[whole_block(*pair)] * 2,
-        out_specs=[whole_block(*pair[1:])] * 2,
-        out_shape=[jax.ShapeDtypeStruct(pair[1:], BF16)] * 2,
-        compiler_params=params(),
-        cost_estimate=NO_COST,
-        name="weight_grads_far_sum",
-    )(far_kept, far_got)
-    in_far = lax.ppermute(in_sent, "row", other_side)
-
-    which, out_sent = lax.optimization_barrier((which, out_sent))
-    sent, kept = side_terms(2, "weight_grads_near_side")
-    sent, in_far = lax.optimization_barrier((sent, in_far))
-    got = lax.ppermute(sent, "row", other_core)
-    out_far = lax.ppermute(out_sent, "row", other_side)
-
-    scattered, kept = lax.optimization_barrier((scattered, kept))
-    copies = pl.pallas_call(
-        spread_sum_kernel,
-        in_specs=[whole_block(half, piece, wide)],
-        out_specs=whole_block(half, piece, wide),
-        out_shape=jax.ShapeDtypeStruct((half, piece, wide), BF16),
-        grid=(1,),
-        compiler_params=params(),
-        cost_estimate=NO_COST,
-        name="kernel_grad_sum",
-    )(scattered)
-    conv_own, copies, out_far = lax.optimization_barrier((conv_grad, copies, out_far))
-    totals = lax.all_to_all(
-        copies, "row", split_axis=0, concat_axis=0, tiled=True, axis_index_groups=alike
-    )
-
     voxel_grad = pl.pallas_call(
         functools.partial(input_grad_kernel, planes, height),
         grid_spec=pltpu.PrefetchScalarGridSpec(
@@ -748,7 +714,41 @@
         name="input_grad_conv",
     )(parity, grad_inner, conv_own, grad_outer, dw_kernel, upstream)
 
-    totals, voxel_grad = lax.optimization_barrier((totals, voxel_grad))
+    far_kept, voxel_grad = lax.optimization_barrier((far_kept, voxel_grad))
+    in_sent, out_sent = pl.pallas_call(
+        far_sum_kernel,
+        grid=(1,),
+        in_specs=[whole_block(*pair)] * 2,
+        out_specs=[whole_block(*pair[1:])] * 2,
+        out_shape=[jax.ShapeDtypeStruct(pair[1:], BF16)] * 2,
+        compiler_params=params(),
+        cost_estimate=NO_COST,
+        name="weight_grads_far_sum",
+    )(far_kept, far_got)
+    in_far = lax.ppermute(in_sent, "row", other_side)
+
+    scattered, voxel_grad = lax.optimization_barrier((scattered, voxel_grad))
+    copies = pl.pallas_call(
+        spread_sum_kernel,
+        in_specs=[whole_block(half, piece, wide)],
+        out_specs=whole_block(half, piece, wide),
+        out_shape=jax.ShapeDtypeStruct((half, piece, wide), BF16),
+        grid=(1,),
+        compiler_params=params(),
+        cost_estimate=NO_COST,
+        name="kernel_grad_sum",
+    )(scattered)
+    which, copies = lax.optimization_barrier((which, copies))
+    totals = lax.all_to_all(
+        copies, "row", split_axis=0, concat_axis=0, tiled=True, axis_index_groups=alike
+    )
+    which, out_sent = lax.optimization_barrier((which, out_sent))
+    sent, kept = side_terms(2, F32, "weight_grads_near_side")
+    sent, in_far = lax.optimization_barrier((sent, in_far))
+    got = lax.ppermute(sent, "row", other_core)
+    out_far = lax.ppermute(out_sent, "row", other_side)
+
+    totals, out_far = lax.optimization_barrier((totals, out_far))
     other_totals = lax.ppermute(totals, "row", other_core)
     kernel_grad, *vector_grads = pl.pallas_call(
         unpack_kernel,

time: 93.7 us -> 92 us (0.982)
  waiting for transfers between devices: 11.6 us -> 5.57 us
  Pallas kernels: 42 us -> 44.1 us
  local copies, waits for them, and re-layouts: 5.6 us -> 7.02 us
    ppermute x2, waiting for transfers between devices: 3.76 us -> 0.01 us  [rims(): lax.ppermute(cells, 'row', between + [(j, i) for i, j in between])]
    ppermute x1, waiting for transfers between devices: 2.27 us -> 0.01 us  [on_device(): in_far = lax.ppermute(in_sent, 'row', other_side)]
    ppermute x2, starting transfers between devices: 6.65 us -> 5.19 us  [rims(): lax.ppermute(cells, 'row', between + [(j, i) for i, j in between])]
    unnamed x26 -> x34, local copies, waits for them, and re-layouts: 5.51 us -> 6.93 us
    ppermute x1, starting transfers between devices: 0.03 us -> 1.45 us  [on_device(): in_far = lax.ppermute(in_sent, 'row', other_side)]
    ppermute x1, waiting for transfers between devices: 0.01 us -> 1.21 us  [on_device(): other_totals = lax.ppermute(totals, 'row', other_core)]
    ppermute x1, starting transfers between devices: 0.61 us -> 1.78 us  [on_device(): got = lax.ppermute(sent, 'row', other_core)]
    ppermute x3, starting transfers between devices: 5.75 us -> 4.61 us  [along_line(): lax.ppermute(cells, 'row', [(i, (i + quad * steps) % count) for i in rang...]
  transfers between devices with their start and end apart: 16 -> 16, of which waited for: 5 -> 3; matrix products, arithmetic and copies ran while one was open for 0% -> 0% of each run, Pallas kernels for 38% -> 46%
where the time goes in v11:
time: 92 us; the launch traced here: 90.5 us
  Pallas kernels  44.1 us (48%)
  starting transfers between devices  32.9 us (36%)
  local copies, waits for them, and re-layouts  7.02 us (8%)
  waiting for transfers between devices  5.57 us (6%)
    pallas_call x2, Pallas kernels, side_terms(): pl.pallas_call(side_terms_kernel, grid_spec=pltpu.PrefetchScalarGridSpec(...  10.4 us
    pallas_call x1, Pallas kernels, on_device(): pl.pallas_call(mlp_kernel, grid=(units // block,), in_specs=[pl.BlockSpec...  9.94 us
    unnamed x34, local copies, waits for them, and re-layouts  6.93 us
    pallas_call x1, Pallas kernels, on_device(): pl.pallas_call(functools.partial(kernel_grad_kernel, planes, height), gri...  6.18 us
    all_to_all x1, starting transfers between devices, on_device(): lax.all_to_all(sums.reshape(half, piece, wide), 'row', split_axis=0, conc...  5.71 us
    pallas_call x1, Pallas kernels, on_device(): pl.pallas_call(functools.partial(input_grad_kernel, planes, height), grid...  5.27 us
    ppermute x2, starting transfers between devices, rims(): lax.ppermute(cells, 'row', between + [(j, i) for i, j in between])  5.19 us
    ppermute x3, starting transfers between devices, along_line(): lax.ppermute(cells, 'row', [(i, (i + quad * steps) % count) for i in rang...  4.61 us
  transfers between devices with their start and end apart: 16, of which 3 were waited for; matrix products, arithmetic and copies ran while one was open for 0% of the time, Pallas kernels for 46%

profile of v11, /device:TPU:1, one launch (start us, length us, event | category | flops | bytes accessed | tf_op | source)
XLA Modules:
  0.0 90.5 jit_solution(15981597597633796782)
XLA Ops:
  0.6 2.2 %collective-permute-start.2 = (bf16[128,768]{1,0:T(8,128)(2,1)}, bf16[128,768]{1,0:T(8,128)(2,1)S(1)}, u32[]{:S(2)}, u32[]{:S(2)}) collective-permute-start(bf16[128,768]{1,0:T(8,128)(2,1)} %bitcast.11), channel_id=1, source_target_pairs={{0,4},{1,5},{2,6},{3,7},{4,8},{5,9},{6,10},{7,11},{8,12},{9,13},{1... | collective-permute-start | bytes 589832 | tf_op jit(solution)/shard_map/ppermute | solution.py:490
  2.8 2.1 %collective-permute-start.3 = (bf16[128,768]{1,0:T(8,128)(2,1)}, bf16[128,768]{1,0:T(8,128)(2,1)S(1)}, u32[]{:S(2)}, u32[]{:S(2)}) collective-permute-start(bf16[128,768]{1,0:T(8,128)(2,1)} %bitcast.12), channel_id=1, source_target_pairs={{0,12},{1,13},{2,14},{3,15},{4,0},{5,1},{6,2},{7,3},{8,4},{9,5},{1... | collective-permute-start | bytes 589832 | tf_op jit(solution)/shard_map/ppermute | solution.py:490
  4.9 1.0 %collective-permute-start = (bf16[128,768]{1,0:T(8,128)(2,1)}, bf16[128,768]{1,0:T(8,128)(2,1)S(1)}, u32[]{:S(2)}, u32[]{:S(2)}) collective-permute-start(bf16[128,768]{1,0:T(8,128)(2,1)} %bitcast.17), channel_id=1, source_target_pairs={{0,1},{1,0},{2,3},{3,2},{4,5},{5,4},{6,7},{7,6},{8,9},{9,8},{10,11... | collective-permute-start | bytes 589832 | tf_op jit(solution)/shard_map/ppermute | solution.py:462
  5.9 3.2 %collective-permute-start.1 = (bf16[128,768]{1,0:T(8,128)(2,1)}, bf16[128,768]{1,0:T(8,128)(2,1)S(1)}, u32[]{:S(2)}, u32[]{:S(2)}) collective-permute-start(bf16[128,768]{1,0:T(8,128)(2,1)} %bitcast.18), channel_id=1, source_target_pairs={{1,2},{3,4},{5,6},{7,8},{9,10},{11,12},{13,14},{2,1},{4,3},{6,5},{... | collective-permute-start | bytes 589832 | tf_op jit(solution)/shard_map/ppermute | solution.py:463
  9.0 0.0 copy-start
  9.1 1.2 %copy-done = f32[343,768]{1,0:T(8,128)S(1)} copy-done((f32[343,768]{1,0:T(8,128)S(1)}, f32[343,768]{1,0:T(8,128)}, u32[]{:S(2)}) %copy-start) | copy-done | bytes 1053720
  10.3 0.9 %copy-done.3 = bf16[4,4,8,768]{3,2,1,0:T(8,128)(2,1)S(1)} copy-done((bf16[4,4,8,768]{3,2,1,0:T(8,128)(2,1)S(1)}, bf16[4,4,8,768]{3,2,1,0:T(8,128)(2,1)}, u32[]{:S(2)}) %copy-start.3) | copy-done | bytes 196632
  11.2 2.2 %own_conv.1 = (f32[128,768]{1,0:T(8,128)S(1)}, f32[6,9,7,8,128]{4,3,2,1,0:T(8,128)S(1)}) custom-call(bf16[128,768]{1,0:T(8,128)(2,1)S(1)} %bitcast.19, f32[343,768]{1,0:T(8,128)S(1)} %copy-done), custom_call_target="tpu_custom_call" | custom-call | tf_op jit(solution)/shard_map/own_conv/pallas_call | solution.py:500
  13.4 1.2 %copy-done.5 = f32[6,9,7,8,128]{4,3,2,1,0:T(8,128)} copy-done((f32[6,9,7,8,128]{4,3,2,1,0:T(8,128)}, f32[6,9,7,8,128]{4,3,2,1,0:T(8,128)S(1)}, u32[]{:S(2)}) %copy-start.5) | copy-done | bytes 1548312
  14.6 0.3 collective-permute-start.4
  14.9 0.0 collective-permute-done.inner
  14.9 0.0 collective-permute-done.1.outer
  14.9 1.4 %copy-done.6 = f32[6,9,7,8,128]{4,3,2,1,0:T(8,128)S(1)} copy-done((f32[6,9,7,8,128]{4,3,2,1,0:T(8,128)S(1)}, f32[6,9,7,8,128]{4,3,2,1,0:T(8,128)}, u32[]{:S(2)}) %copy-start.6) | copy-done | bytes 1548312
  16.3 0.7 copy-done.14
  17.0 0.7 copy-done.15
  17.7 3.6 %rim_conv.1 = (bf16[4,128,768]{2,1,0:T(8,128)(2,1)}, f32[128,768]{1,0:T(8,128)S(1)}) custom-call(s32[1]{0:T(128)} %bitcast.core, bf16[128,768]{1,0:T(8,128)(2,1)S(1)} %collective-permute-done.inner, bf16[128,768]{1,0:T(8,128)(2,1)S(1)} %collective-permute-done.1.outer, f32[6,9,7,8,128]{4,3,2,1,0:T(8,128)S(1)} %copy-done.6, ...), custom_call_target="tpu_custom_call" | custom-call | tf_op jit(solution)/shard_map/rim_conv/pallas_call | solution.py:520
  21.3 1.7 %collective-permute-done.4.rest_2_ = bf16[128,768]{1,0:T(8,128)(2,1)S(1)} collective-permute-done((bf16[128,768]{1,0:T(8,128)(2,1)S(1)}, bf16[128,768]{1,0:T(8,128)(2,1)S(1)}, u32[]{:S(2)}, u32[]{:S(2)}) %collective-permute-start.4) | collective-permute-done | bytes 196640 | tf_op jit(solution)/shard_map/ppermute | solution.py:490
  23.0 3.5 %all-to-all-start.1 = ((bf16[4,128,768]{2,1,0:T(8,128)(2,1)}), bf16[4,128,768]{2,1,0:T(8,128)(2,1)S(1)}, u32[]{:S(2)}, u32[]{:S(2)}) async-start(bf16[4,128,768]{2,1,0:T(8,128)(2,1)} %get-tuple-element.61.normed), calls=%async_computation.1 | async-start | bytes 1572864 | tf_op jit(solution)/shard_map/all_to_all | solution.py:551
  26.5 0.1 pad_add_fusion.which
  26.6 9.9 %mlp_both_ways.1 = (bf16[128,768]{1,0:T(8,128)(2,1)}, bf16[128,768]{1,0:T(8,128)(2,1)S(1)}, f32[8,768]{1,0:T(8,128)S(1)}) custom-call(bf16[4,128,768]{2,1,0:T(8,128)(2,1)} %get-tuple-element.61.normed, bf16[3072,768]{1,0:T(8,128)(2,1)} %weight_in.5, bf16[3072,768]{1,0:T(8,128)(2,1)} %weight_out.5, f32[128,768]{1,0:T(8,128)S(1)} %get-tuple-element.62.centered, ...), custom_call_target="tpu_custom_call" | custom-call | tf_op jit(solution)/shard_map/mlp_both_ways/pallas_call | solution.py:557
  36.6 6.2 %kernel_grad_terms.1 = (bf16[384,384]{1,0:T(8,128)(2,1)S(1)}, bf16[384,384]{1,0:T(8,128)(2,1)S(1)}) custom-call(s32[2]{0:T(128)S(1)} %pad_add_fusion.which, bf16[128,768]{1,0:T(8,128)(2,1)S(1)} %collective-permute-done.inner, bf16[128,768]{1,0:T(8,128)(2,1)S(1)} %bitcast.21, bf16[128,768]{1,0:T(8,128)(2,1)S(1)} %collective-permute-done.1.outer, ...), custom_call_target="tpu_custom_call" | custom-call | tf_op jit(solution)/shard_map/kernel_grad_terms/pallas_call | solution.py:604
  42.8 1.1 %collective-permute-start.5 = (bf16[384,384]{1,0:T(8,128)(2,1)S(1)}, bf16[384,384]{1,0:T(8,128)(2,1)S(1)}, u32[]{:S(2)}, u32[]{:S(2)}) collective-permute-start(bf16[384,384]{1,0:T(8,128)(2,1)S(1)} %get-tuple-element.68), channel_id=1, source_target_pairs={{0,1},{1,0},{2,3},{3,2},{4,5},{5,4},{6,7},{7,6},{8,9},{9,8},{10,11... | collective-permute-start | bytes 884744 | tf_op jit(solution)/shard_map/ppermute | solution.py:628
  43.8 0.1 collective-permute-start.6
  43.9 2.0 %collective-permute-start.7 = (bf16[128,768]{1,0:T(8,128)(2,1)S(1)}, bf16[128,768]{1,0:T(8,128)(2,1)}, u32[]{:S(2)}, u32[]{:S(2)}) collective-permute-start(bf16[128,768]{1,0:T(8,128)(2,1)S(1)} %get-tuple-element.77.grads.own), channel_id=1, source_target_pairs={{1,2},{3,4},{5,6},{7,8},{9,10},{11,12},{13,14},{2,1},{4,3},{6,5},{... | collective-permute-start | bytes 589832 | tf_op jit(solution)/shard_map/ppermute | solution.py:463
  46.0 0.1 concatenate.3.which
  46.1 0.8 kernel_grad_chip_sum.1
  46.9 0.0 all-to-all-done.1.normed
  46.9 5.2 %weight_grads_far_side.1 = (bf16[2,192,768]{2,1,0:T(8,128)(2,1)}, bf16[2,192,768]{2,1,0:T(8,128)(2,1)S(1)}) custom-call(s32[8]{0:T(128)S(1)} %concatenate.3.which, bf16[3072,768]{1,0:T(8,128)(2,1)} %weight_in.5, bf16[3072,768]{1,0:T(8,128)(2,1)} %weight_out.5, f32[768]{0:T(1024)S(1)} %copy-done.13, bf16[4,128,768]{2,1,0:T(8,128)(2,1)S(1)} %all-to-all-done.1.normed, ...), custom_call_target="tpu_custom_call" | custom-call | tf_op jit(solution)/shard_map/weight_grads_far_side/pallas_call | solution.py:658
  52.1 0.8 copy-done.11
  52.9 0.0 collective-permute-done.6.inner
  52.9 0.0 collective-permute-done.7.outer
  52.9 0.7 collective-permute-start.8
  53.6 5.7 %all-to-all-start = ((bf16[8,48,384]{2,1,0:T(8,128)(2,1)}), bf16[8,48,384]{2,1,0:T(8,128)(2,1)S(1)}, u32[]{:S(2)}, u32[]{:S(2)}) async-start(bf16[8,48,384]{2,1,0:T(8,128)(2,1)} %bitcast.9), calls=%async_computation | async-start | bytes 589824 | tf_op jit(solution)/shard_map/all_to_all | solution.py:685
  59.3 5.3 %input_grad_conv.1 = bf16[128,768]{1,0:T(8,128)(2,1)} custom-call(s32[1]{0:T(128)} %bitcast.core, bf16[128,768]{1,0:T(8,128)(2,1)} %collective-permute-done.6.inner, bf16[128,768]{1,0:T(8,128)(2,1)S(1)} %get-tuple-element.77.grads.own, bf16[128,768]{1,0:T(8,128)(2,1)} %collective-permute-done.7.outer, f32[343,768]{1,0:T(8,128)S(1)} %copy-done.1, ...), custom_call_target="tpu_custom_call" | custom-call | tf_op jit(solution)/shard_map/input_grad_conv/pallas_call | solution.py:693
  64.6 0.0 collective-permute-done.8.got
  64.6 1.9 %weight_grads_far_sum.1 = (bf16[192,768]{1,0:T(8,128)(2,1)}, bf16[192,768]{1,0:T(8,128)(2,1)S(1)}) custom-call(bf16[2,192,768]{2,1,0:T(8,128)(2,1)S(1)} %copy-done.12, bf16[2,192,768]{2,1,0:T(8,128)(2,1)} %collective-permute-done.8.got), custom_call_target="tpu_custom_call" | custom-call | tf_op jit(solution)/shard_map/weight_grads_far_sum/pallas_call | solution.py:718
  66.5 1.4 %collective-permute-start.11 = (bf16[192,768]{1,0:T(8,128)(2,1)}, bf16[192,768]{1,0:T(8,128)(2,1)S(1)}, u32[]{:S(2)}, u32[]{:S(2)}) collective-permute-start(bf16[192,768]{1,0:T(8,128)(2,1)} %get-tuple-element.96), channel_id=1, source_target_pairs={{0,2},{1,3},{2,0},{3,1},{4,6},{5,7},{6,4},{7,5},{8,10},{9,11},{10,... | collective-permute-start | bytes 884744 | tf_op jit(solution)/shard_map/ppermute | solution.py:728
  68.0 0.8 kernel_grad_sum.1
  68.7 4.5 %all-to-all-start.2 = ((bf16[8,48,384]{2,1,0:T(8,128)(2,1)}), bf16[8,48,384]{2,1,0:T(8,128)(2,1)S(1)}, u32[]{:S(2)}, u32[]{:S(2)}) async-start(bf16[8,48,384]{2,1,0:T(8,128)(2,1)} %kernel_grad_sum.1), calls=%async_computation.2 | async-start | bytes 589824 | tf_op jit(solution)/shard_map/all_to_all | solution.py:742
  73.3 1.5 %collective-permute-start.9 = (bf16[192,768]{1,0:T(8,128)(2,1)}, bf16[192,768]{1,0:T(8,128)(2,1)}, u32[]{:S(2)}, u32[]{:S(2)}) collective-permute-start(bf16[192,768]{1,0:T(8,128)(2,1)} %copy-done.16), channel_id=1, source_target_pairs={{0,2},{1,3},{2,0},{3,1},{4,6},{5,7},{6,4},{7,5},{8,10},{9,11},{10,... | collective-permute-start | bytes 884744 | tf_op jit(solution)/shard_map/ppermute | solution.py:749
  74.7 5.2 %weight_grads_near_side.1 = (bf16[2,192,768]{2,1,0:T(8,128)(2,1)}, f32[2,192,768]{2,1,0:T(8,128)S(1)}) custom-call(s32[8]{0:T(128)S(1)} %concatenate.3.which, bf16[3072,768]{1,0:T(8,128)(2,1)} %weight_in.5, bf16[3072,768]{1,0:T(8,128)(2,1)} %weight_out.5, f32[768]{0:T(1024)S(1)} %copy-done.13, bf16[4,128,768]{2,1,0:T(8,128)(2,1)S(1)} %all-to-all-done.1.normed, ...), custom_call_target="tpu_custom_call" | custom-call | tf_op jit(solution)/shard_map/weight_grads_near_side/pallas_call | solution.py:658
  79.9 0.0 collective-permute-done.11.in_far
  79.9 1.8 %collective-permute-start.12 = (bf16[2,192,768]{2,1,0:T(8,128)(2,1)}, bf16[2,192,768]{2,1,0:T(8,128)(2,1)S(1)}, u32[]{:S(2)}, u32[]{:S(2)}) collective-permute-start(bf16[2,192,768]{2,1,0:T(8,128)(2,1)} %get-tuple-element.97), channel_id=1, source_target_pairs={{0,1},{1,0},{2,3},{3,2},{4,5},{5,4},{6,7},{7,6},{8,9},{9,8},{10,11... | collective-permute-start | bytes 1769480 | tf_op jit(solution)/shard_map/ppermute | solution.py:748
  81.7 2.6 %collective-permute-done.9.out_far = bf16[192,768]{1,0:T(8,128)(2,1)} collective-permute-done((bf16[192,768]{1,0:T(8,128)(2,1)}, bf16[192,768]{1,0:T(8,128)(2,1)}, u32[]{:S(2)}, u32[]{:S(2)}) %collective-permute-start.9) | collective-permute-done | bytes 294944 | tf_op jit(solution)/shard_map/ppermute | solution.py:749
  84.3 1.9 %collective-permute-start.10 = (bf16[8,48,384]{2,1,0:T(8,128)(2,1)S(1)}, bf16[8,48,384]{2,1,0:T(8,128)(2,1)S(1)}, u32[]{:S(2)}, u32[]{:S(2)}) collective-permute-start(bf16[8,48,384]{2,1,0:T(8,128)(2,1)S(1)} %all-to-all-done.2.own), channel_id=1, source_target_pairs={{0,1},{1,0},{2,3},{3,2},{4,5},{5,4},{6,7},{7,6},{8,9},{9,8},{10,11... | collective-permute-start | bytes 884744 | tf_op jit(solution)/shard_map/ppermute | solution.py:752
  86.2 1.2 %collective-permute-done.10.other = bf16[8,48,384]{2,1,0:T(8,128)(2,1)S(1)} collective-permute-done((bf16[8,48,384]{2,1,0:T(8,128)(2,1)S(1)}, bf16[8,48,384]{2,1,0:T(8,128)(2,1)S(1)}, u32[]{:S(2)}, u32[]{:S(2)}) %collective-permute-start.10) | collective-permute-done | bytes 294944 | tf_op jit(solution)/shard_map/ppermute | solution.py:752
  87.4 1.1 %kernel_grad_unpack.1 = (f32[343,768]{1,0:T(8,128)}, f32[768]{0:T(1024)}, f32[768]{0:T(1024)}, f32[768]{0:T(1024)}) custom-call(s32[1]{0:T(128)} %bitcast.core, bf16[8,48,384]{2,1,0:T(8,128)(2,1)S(1)} %all-to-all-done.2.own, bf16[8,48,384]{2,1,0:T(8,128)(2,1)S(1)} %collective-permute-done.10.other), custom_call_target="tpu_custom_call" | custom-call | tf_op jit(solution)/shard_map/kernel_grad_unpack/pallas_call | solution.py:753
  88.4 2.1 %weight_grads_sum.1 = (f32[192,768]{1,0:T(8,128)}, f32[192,768]{1,0:T(8,128)}) custom-call(f32[2,192,768]{2,1,0:T(8,128)S(1)} %get-tuple-element.94.kept, bf16[2,192,768]{2,1,0:T(8,128)(2,1)S(1)} %collective-permute-done.12.got, bf16[192,768]{1,0:T(8,128)(2,1)S(1)} %collective-permute-done.11.in_far, bf16[192,768]{1,0:T(8,128)(2,1)} %collective-permute-done.9.out_far), custom_call_target="tpu_custom_call" | custom-call | tf_op jit(solution)/shard_map/weight_grads_sum/pallas_call | solution.py:768
  (33 shorter events, 0.1 us)
Async XLA Ops:
  0.6 13.9 %collective-permute-start.2 = (bf16[128,768]{1,0:T(8,128)(2,1)}, bf16[128,768]{1,0:T(8,128)(2,1)S(1)}, u32[]{:S(2)}, u32[]{:S(2)}) collective-permute-start(bf16[128,768]{1,0:T(8,128)(2,1)} %bitcast.11), channel_id=1, source_target_pairs={{0,4},{1,5},{2,6},{3,7},{4,8},{5,9},{6,10},{7,11},{8,12},{9,13},{1... | collective-permute-start | bytes 589832 | tf_op jit(solution)/shard_map/ppermute | solution.py:490
  2.8 11.8 %collective-permute-start.3 = (bf16[128,768]{1,0:T(8,128)(2,1)}, bf16[128,768]{1,0:T(8,128)(2,1)S(1)}, u32[]{:S(2)}, u32[]{:S(2)}) collective-permute-start(bf16[128,768]{1,0:T(8,128)(2,1)} %bitcast.12), channel_id=1, source_target_pairs={{0,12},{1,13},{2,14},{3,15},{4,0},{5,1},{6,2},{7,3},{8,4},{9,5},{1... | collective-permute-start | bytes 589832 | tf_op jit(solution)/shard_map/ppermute | solution.py:490
  4.9 10.0 %collective-permute-start = (bf16[128,768]{1,0:T(8,128)(2,1)}, bf16[128,768]{1,0:T(8,128)(2,1)S(1)}, u32[]{:S(2)}, u32[]{:S(2)}) collective-permute-start(bf16[128,768]{1,0:T(8,128)(2,1)} %bitcast.17), channel_id=1, source_target_pairs={{0,1},{1,0},{2,3},{3,2},{4,5},{5,4},{6,7},{7,6},{8,9},{9,8},{10,11... | collective-permute-start | bytes 589832 | tf_op jit(solution)/shard_map/ppermute | solution.py:462
  5.9 9.1 %collective-permute-start.1 = (bf16[128,768]{1,0:T(8,128)(2,1)}, bf16[128,768]{1,0:T(8,128)(2,1)S(1)}, u32[]{:S(2)}, u32[]{:S(2)}) collective-permute-start(bf16[128,768]{1,0:T(8,128)(2,1)} %bitcast.18), channel_id=1, source_target_pairs={{1,2},{3,4},{5,6},{7,8},{9,10},{11,12},{13,14},{2,1},{4,3},{6,5},{... | collective-permute-start | bytes 589832 | tf_op jit(solution)/shard_map/ppermute | solution.py:463
  9.0 1.2 %copy-start = (f32[343,768]{1,0:T(8,128)S(1)}, f32[343,768]{1,0:T(8,128)}, u32[]{:S(2)}) copy-start(f32[343,768]{1,0:T(8,128)} %taps.3) | copy-start | bytes 3161092
  10.3 0.9 %copy-start.3 = (bf16[4,4,8,768]{3,2,1,0:T(8,128)(2,1)S(1)}, bf16[4,4,8,768]{3,2,1,0:T(8,128)(2,1)}, u32[]{:S(2)}) copy-start(bf16[4,4,8,768]{3,2,1,0:T(8,128)(2,1)} %param.8) | copy-start | bytes 589828
  13.4 1.2 %copy-start.5 = (f32[6,9,7,8,128]{4,3,2,1,0:T(8,128)}, f32[6,9,7,8,128]{4,3,2,1,0:T(8,128)S(1)}, u32[]{:S(2)}) copy-start(f32[6,9,7,8,128]{4,3,2,1,0:T(8,128)S(1)} %get-tuple-element.55.split) | copy-start | bytes 4644868
  14.6 32.3 %copy-start.7 = (bf16[128,768]{1,0:T(8,128)(2,1)}, bf16[128,768]{1,0:T(8,128)(2,1)S(1)}, u32[]{:S(2)}) copy-start(bf16[128,768]{1,0:T(8,128)(2,1)S(1)} %collective-permute-done.3.rest_3_) | copy-start | bytes 589828
  14.6 8.5 %collective-permute-start.4 = (bf16[128,768]{1,0:T(8,128)(2,1)S(1)}, bf16[128,768]{1,0:T(8,128)(2,1)S(1)}, u32[]{:S(2)}, u32[]{:S(2)}) collective-permute-start(bf16[128,768]{1,0:T(8,128)(2,1)S(1)} %collective-permute-done.2.rest_1_), channel_id=1, source_target_pairs={{0,4},{1,5},{2,6},{3,7},{4,8},{5,9},{6,10},{7,11},{8,12},{9,13},{1... | collective-permute-start | bytes 589832 | tf_op jit(solution)/shard_map/ppermute | solution.py:490
  14.9 1.4 %copy-start.6 = (f32[6,9,7,8,128]{4,3,2,1,0:T(8,128)S(1)}, f32[6,9,7,8,128]{4,3,2,1,0:T(8,128)}, u32[]{:S(2)}) copy-start(f32[6,9,7,8,128]{4,3,2,1,0:T(8,128)} %copy-done.5) | copy-start | bytes 4644868
  16.3 0.7 copy-start.14
  17.0 0.7 copy-start.15
  17.7 8.9 %copy-start.2 = (bf16[4,4,8,768]{3,2,1,0:T(8,128)(2,1)S(1)}, bf16[4,4,8,768]{3,2,1,0:T(8,128)(2,1)}, u32[]{:S(2)}) copy-start(bf16[4,4,8,768]{3,2,1,0:T(8,128)(2,1)} %param.15) | copy-start | bytes 589828
  17.7 8.9 %copy-start.4 = (bf16[4,4,8,768]{3,2,1,0:T(8,128)(2,1)S(1)}, bf16[4,4,8,768]{3,2,1,0:T(8,128)(2,1)}, u32[]{:S(2)}) copy-start(bf16[4,4,8,768]{3,2,1,0:T(8,128)(2,1)} %param.8) | copy-start | bytes 589828
  17.7 8.9 %copy-start.13 = (f32[768]{0:T(1024)S(1)}, f32[768]{0:T(1024)}, u32[]{:S(2)}) copy-start(f32[768]{0:T(1024)} %scale.3) | copy-start | bytes 9220
  23.0 23.9 %copy-start.9 = (bf16[128,768]{1,0:T(8,128)(2,1)}, bf16[128,768]{1,0:T(8,128)(2,1)S(1)}, u32[]{:S(2)}) copy-start(bf16[128,768]{1,0:T(8,128)(2,1)S(1)} %collective-permute-done.4.rest_2_) | copy-start | bytes 589828
  23.0 23.9 %all-to-all-start.1 = ((bf16[4,128,768]{2,1,0:T(8,128)(2,1)}), bf16[4,128,768]{2,1,0:T(8,128)(2,1)S(1)}, u32[]{:S(2)}, u32[]{:S(2)}) async-start(bf16[4,128,768]{2,1,0:T(8,128)(2,1)} %get-tuple-element.61.normed), calls=%async_computation.1 | async-start | bytes 1572864 | tf_op jit(solution)/shard_map/all_to_all | solution.py:551
  42.8 3.3 %collective-permute-start.5 = (bf16[384,384]{1,0:T(8,128)(2,1)S(1)}, bf16[384,384]{1,0:T(8,128)(2,1)S(1)}, u32[]{:S(2)}, u32[]{:S(2)}) collective-permute-start(bf16[384,384]{1,0:T(8,128)(2,1)S(1)} %get-tuple-element.68), channel_id=1, source_target_pairs={{0,1},{1,0},{2,3},{3,2},{4,5},{5,4},{6,7},{7,6},{8,9},{9,8},{10,11... | collective-permute-start | bytes 884744 | tf_op jit(solution)/shard_map/ppermute | solution.py:628
  43.8 9.1 %collective-permute-start.6 = (bf16[128,768]{1,0:T(8,128)(2,1)S(1)}, bf16[128,768]{1,0:T(8,128)(2,1)}, u32[]{:S(2)}, u32[]{:S(2)}) collective-permute-start(bf16[128,768]{1,0:T(8,128)(2,1)S(1)} %get-tuple-element.77.grads.own), channel_id=1, source_target_pairs={{0,1},{1,0},{2,3},{3,2},{4,5},{5,4},{6,7},{7,6},{8,9},{9,8},{10,11... | collective-permute-start | bytes 589832 | tf_op jit(solution)/shard_map/ppermute | solution.py:462
  43.9 9.0 %collective-permute-start.7 = (bf16[128,768]{1,0:T(8,128)(2,1)S(1)}, bf16[128,768]{1,0:T(8,128)(2,1)}, u32[]{:S(2)}, u32[]{:S(2)}) collective-permute-start(bf16[128,768]{1,0:T(8,128)(2,1)S(1)} %get-tuple-element.77.grads.own), channel_id=1, source_target_pairs={{1,2},{3,4},{5,6},{7,8},{9,10},{11,12},{13,14},{2,1},{4,3},{6,5},{... | collective-permute-start | bytes 589832 | tf_op jit(solution)/shard_map/ppermute | solution.py:463
  46.9 12.4 %copy-start.1 = (f32[343,768]{1,0:T(8,128)S(1)}, f32[343,768]{1,0:T(8,128)}, u32[]{:S(2)}) copy-start(f32[343,768]{1,0:T(8,128)} %taps.3) | copy-start | bytes 3161092
  52.1 0.8 copy-start.11
  52.9 11.7 %copy-start.12 = (bf16[2,192,768]{2,1,0:T(8,128)(2,1)S(1)}, bf16[2,192,768]{2,1,0:T(8,128)(2,1)}, u32[]{:S(2)}) copy-start(bf16[2,192,768]{2,1,0:T(8,128)(2,1)} %copy-done.11) | copy-start | bytes 1769476
  52.9 11.7 %collective-permute-start.8 = (bf16[2,192,768]{2,1,0:T(8,128)(2,1)}, bf16[2,192,768]{2,1,0:T(8,128)(2,1)}, u32[]{:S(2)}, u32[]{:S(2)}) collective-permute-start(bf16[2,192,768]{2,1,0:T(8,128)(2,1)} %get-tuple-element.85), channel_id=1, source_target_pairs={{0,1},{1,0},{2,3},{3,2},{4,5},{5,4},{6,7},{7,6},{8,9},{9,8},{10,11... | collective-permute-start | bytes 1769480 | tf_op jit(solution)/shard_map/ppermute | solution.py:684
  53.6 14.4 %all-to-all-start = ((bf16[8,48,384]{2,1,0:T(8,128)(2,1)}), bf16[8,48,384]{2,1,0:T(8,128)(2,1)S(1)}, u32[]{:S(2)}, u32[]{:S(2)}) async-start(bf16[8,48,384]{2,1,0:T(8,128)(2,1)} %bitcast.9), calls=%async_computation | async-start | bytes 589824 | tf_op jit(solution)/shard_map/all_to_all | solution.py:685
  64.6 10.1 %copy-start.8 = (bf16[128,768]{1,0:T(8,128)(2,1)S(1)}, bf16[128,768]{1,0:T(8,128)(2,1)}, u32[]{:S(2)}) copy-start(bf16[128,768]{1,0:T(8,128)(2,1)} %copy-done.7) | copy-start | bytes 589828
  64.6 10.1 %copy-start.10 = (bf16[128,768]{1,0:T(8,128)(2,1)S(1)}, bf16[128,768]{1,0:T(8,128)(2,1)}, u32[]{:S(2)}) copy-start(bf16[128,768]{1,0:T(8,128)(2,1)} %copy-done.9) | copy-start | bytes 589828
  66.5 2.2 %copy-start.16 = (bf16[192,768]{1,0:T(8,128)(2,1)}, bf16[192,768]{1,0:T(8,128)(2,1)S(1)}, u32[]{:S(2)}) copy-start(bf16[192,768]{1,0:T(8,128)(2,1)S(1)} %get-tuple-element.87) | copy-start | bytes 884740
  66.5 13.4 %collective-permute-start.11 = (bf16[192,768]{1,0:T(8,128)(2,1)}, bf16[192,768]{1,0:T(8,128)(2,1)S(1)}, u32[]{:S(2)}, u32[]{:S(2)}) collective-permute-start(bf16[192,768]{1,0:T(8,128)(2,1)} %get-tuple-element.96), channel_id=1, source_target_pairs={{0,2},{1,3},{2,0},{3,1},{4,6},{5,7},{6,4},{7,5},{8,10},{9,11},{10,... | collective-permute-start | bytes 884744 | tf_op jit(solution)/shard_map/ppermute | solution.py:728
  68.7 13.0 %all-to-all-start.2 = ((bf16[8,48,384]{2,1,0:T(8,128)(2,1)}), bf16[8,48,384]{2,1,0:T(8,128)(2,1)S(1)}, u32[]{:S(2)}, u32[]{:S(2)}) async-start(bf16[8,48,384]{2,1,0:T(8,128)(2,1)} %kernel_grad_sum.1), calls=%async_computation.2 | async-start | bytes 589824 | tf_op jit(solution)/shard_map/all_to_all | solution.py:742
  73.3 11.0 %collective-permute-start.9 = (bf16[192,768]{1,0:T(8,128)(2,1)}, bf16[192,768]{1,0:T(8,128)(2,1)}, u32[]{:S(2)}, u32[]{:S(2)}) collective-permute-start(bf16[192,768]{1,0:T(8,128)(2,1)} %copy-done.16), channel_id=1, source_target_pairs={{0,2},{1,3},{2,0},{3,1},{4,6},{5,7},{6,4},{7,5},{8,10},{9,11},{10,... | collective-permute-start | bytes 884744 | tf_op jit(solution)/shard_map/ppermute | solution.py:749
  79.9 8.5 %collective-permute-start.12 = (bf16[2,192,768]{2,1,0:T(8,128)(2,1)}, bf16[2,192,768]{2,1,0:T(8,128)(2,1)S(1)}, u32[]{:S(2)}, u32[]{:S(2)}) collective-permute-start(bf16[2,192,768]{2,1,0:T(8,128)(2,1)} %get-tuple-element.97), channel_id=1, source_target_pairs={{0,1},{1,0},{2,3},{3,2},{4,5},{5,4},{6,7},{7,6},{8,9},{9,8},{10,11... | collective-permute-start | bytes 1769480 | tf_op jit(solution)/shard_map/ppermute | solution.py:748
  84.3 3.1 %collective-permute-start.10 = (bf16[8,48,384]{2,1,0:T(8,128)(2,1)S(1)}, bf16[8,48,384]{2,1,0:T(8,128)(2,1)S(1)}, u32[]{:S(2)}, u32[]{:S(2)}) collective-permute-start(bf16[8,48,384]{2,1,0:T(8,128)(2,1)S(1)} %all-to-all-done.2.own), channel_id=1, source_target_pairs={{0,1},{1,0},{2,3},{3,2},{4,5},{5,4},{6,7},{7,6},{8,9},{9,8},{10,11... | collective-permute-start | bytes 884744 | tf_op jit(solution)/shard_map/ppermute | solution.py:752

commit v12 on v11

--- a/solution.py
+++ b/solution.py
@@ -288,21 +288,10 @@
 
 
 def mlp_kernel(
-    normed,
-    weight_in,
-    weight_out,
-    centered,
-    norm_gain,
-    layer_scale,
-    voxels,
-    cotangent,
-    block_out,
-    conv_grad,
-    small,
-    mixed,
-    back,
-    mixed_grad,
+    normed, weight_in, weight_out, centered, norm_gain, layer_scale, voxels, *rest
 ):
+    *cotangents, block_out, conv_grad, small, together, mixed, back, mixed_grad = rest
+    cotangent = cotangents[0]
     step = pl.program_id(0)
     gain = norm_gain[...].reshape(1, -1)
     scale = layer_scale[...].reshape(1, -1)
@@ -310,13 +299,15 @@
     @pl.when(step == 0)
     def _():
         mixed_grad[...] = (scale * cotangent[...].astype(F32)).astype(BF16)
+        for k, part in enumerate(cotangents):
+            together[k] = part[...]
 
     across = (((1,), (1,)), ((), ()))
-    hidden = lax.dot_general(weight_in[...], normed[...], across, preferred_element_type=F32)
+    hidden = lax.dot_general(normed[...], weight_in[...], across, preferred_element_type=F32)
     act_grad = lax.dot_general(
-        weight_out[...], mixed_grad[...], across, preferred_element_type=F32
-    )
-    activated, hidden_grad = [part.T for part in slopes(hidden, act_grad)]
+        mixed_grad[...], weight_out[...], across, preferred_element_type=F32
+    )
+    activated, hidden_grad = slopes(hidden, act_grad)
     forward = jnp.dot(activated, weight_out[...], preferred_element_type=F32)
     backward = jnp.dot(hidden_grad, weight_in[...], preferred_element_type=F32)
 
@@ -367,49 +358,54 @@
     return activated, (act_grad * slope).astype(BF16)
 
 
-def weight_grad_terms(which, weight_in, weight_out, scale, normed, cotangents, aligned):
-    rows = normed.shape[1]
-    line = len(cotangents)
+def weight_grad_terms(which, weight_in, weight_out, scale, sets, aligned, mixed_grad):
     scales = scale[...].reshape(1, -1)
-    mixed_grad = jnp.concatenate(
-        [(scales * part[...].astype(F32)).astype(BF16) for part in cotangents], axis=0
-    )
-    for k in range(line):
-        aligned[k * rows : (k + 1) * rows, :] = normed[which[4 + k]]
+    at = 0
+    for normed, cotangents in sets:
+        line, rows = normed.shape[:2]
+        for k in range(line):
+            aligned[at : at + rows, :] = normed[which[2 + k]]
+            upstream = cotangents[k].astype(F32)
+            mixed_grad[at : at + rows, :] = (scales * upstream).astype(BF16)
+            at += rows
     across = (((1,), (1,)), ((), ()))
     hidden = lax.dot_general(weight_in[...], aligned[...], across, preferred_element_type=F32)
-    act_grad = lax.dot_general(weight_out[...], mixed_grad, across, preferred_element_type=F32)
+    act_grad = lax.dot_general(weight_out[...], mixed_grad[...], across, preferred_element_type=F32)
     activated, hidden_grad = slopes(hidden, act_grad)
     return (
         jnp.dot(hidden_grad, aligned[...], preferred_element_type=F32),
-        jnp.dot(activated, mixed_grad, preferred_element_type=F32),
-    )
-
-
-def side_terms_kernel(which, weight_in, weight_out, scale, normed, *rest):
-    *cotangents, sent, kept, aligned = rest
-    terms = weight_grad_terms(which, weight_in, weight_out, scale, normed, cotangents, aligned)
-    step = pl.program_id(0)
-
-    @pl.when(step == 0)
-    def _():
-        for k in range(2):
-            sent[k] = terms[k].astype(BF16)
-
-    @pl.when(step == 1)
-    def _():
-        for k in range(2):
-            kept[k] = terms[k].astype(kept.dtype)
-
-
-def far_sum_kernel(kept, got, in_grad, out_grad):
+        jnp.dot(activated, mixed_grad[...], preferred_element_type=F32),
+    )
+
+
+def far_side_kernel(
+    which, weight_in, weight_out, scale, norm, cot, other_norm, other_cot, sent, aligned, mixed_grad
+):
+    sets = ((norm, cot), (other_norm, other_cot))
+    terms = weight_grad_terms(which, weight_in, weight_out, scale, sets, aligned, mixed_grad)
+    for k in range(2):
+        sent[k] = terms[k].astype(BF16)
+
+
+def near_side_kernel(
+    which,
+    weight_in,
+    weight_out,
+    scale,
+    norm,
+    cot,
+    other_norm,
+    other_cot,
+    got,
+    in_grad,
+    out_grad,
+    aligned,
+    mixed_grad,
+):
+    sets = ((norm, cot), (other_norm, other_cot))
+    terms = weight_grad_terms(which, weight_in, weight_out, scale, sets, aligned, mixed_grad)
     for k, out in enumerate((in_grad, out_grad)):
-        out[...] = (kept[k].astype(F32) + got[k].astype(F32)).astype(BF16)
-
-
-def last_sum_kernel(kept, got, in_far, out_far, in_grad, out_grad):
-    for k, (far, out) in enumerate(((in_far, in_grad), (out_far, out_grad))):
-        out[...] = (kept[k] + got[k].astype(F32)) + far[...].astype(F32)
+        out[...] = terms[k] + got[k].astype(F32)
 
 
 def chip_sum_kernel(kept, got, out):
@@ -443,7 +439,7 @@
     by_core(core, own, other, lambda outer, inner: unpack(inner, outer))
 
 
-def params(limit=48):
+def params(limit=16):
     return pltpu.CompilerParams(vmem_limit_bytes=limit * 1024 * 1024)
 
 
@@ -545,16 +541,14 @@
         name="rim_conv",
     )(parity, inner, outer, split, partial, norm_gain, norm_bias)
 
-    normed, centered, upstream_line[2] = lax.optimization_barrier(
-        (normed, centered, upstream_line[2])
-    )
+    normed, upstream_line[2] = lax.optimization_barrier((normed, upstream_line[2]))
     gathered = lax.all_to_all(
         normed, "row", split_axis=0, concat_axis=0, tiled=True, axis_index_groups=lines
     )
 
-    block = 512
+    block = 384
     whole = whole_block(rows, channels)
-    block_out, conv_grad, small = pl.pallas_call(
+    block_out, conv_grad, small, cotangents = pl.pallas_call(
         mlp_kernel,
         grid=(units // block,),
         in_specs=[
@@ -564,28 +558,29 @@
             whole,
             whole_block(channels),
             whole_block(channels),
-            whole,
-            whole,
-        ],
+        ]
+        + [whole] * (1 + line),
         out_specs=[
             whole,
             whole,
             whole_block(SUB, channels),
+            whole_block(line, rows, channels),
         ],
         out_shape=[
             jax.ShapeDtypeStruct((rows, channels), BF16),
             jax.ShapeDtypeStruct((rows, channels), BF16),
             jax.ShapeDtypeStruct((SUB, channels), F32),
+            jax.ShapeDtypeStruct((line, rows, channels), BF16),
         ],
         scratch_shapes=[
             pltpu.VMEM((rows, channels), F32),
             pltpu.VMEM((rows, channels), F32),
             pltpu.VMEM((rows, channels), BF16),
         ],
-        compiler_params=params(),
+        compiler_params=params(48),
         cost_estimate=NO_COST,
         name="mlp_both_ways",
-    )(normed, weight_in, weight_out, centered, norm_gain, layer_scale, own, upstream)
+    )(normed, weight_in, weight_out, centered, norm_gain, layer_scale, own, *upstream_line)
 
     half = count // 2
     alike = [[2 * k + p for k in range(half)] for p in range(2)]
@@ -646,42 +641,49 @@
     far = base + 2 * (1 - side)
     near = base + 2 * side
     which = jnp.concatenate(
-        [
-            jnp.stack([far + 1 - core, far + core, near + 1 - core, near + core]).astype(jnp.int32),
-            place.astype(jnp.int32),
-        ]
-    )
+        [jnp.stack([far + core, near + core]).astype(jnp.int32), place.astype(jnp.int32)]
+    )
+    other_gathered = lax.ppermute(gathered, "row", other_core)
+    other_cotangents = lax.ppermute(cotangents, "row", other_core)
     pair = (2, share, channels)
 
-    def side_terms(first, kept_as, name):
-        chunk = pl.BlockSpec((share, channels), lambda s, w: (w[s + first], 0))
+    def side_terms(kernel, number, more, outs, name):
+        chunk = pl.BlockSpec((share, channels), lambda _, w: (w[number], 0))
         return pl.pallas_call(
-            side_terms_kernel,
+            kernel,
             grid_spec=pltpu.PrefetchScalarGridSpec(
                 num_scalar_prefetch=1,
-                grid=(2,),
-                in_specs=[
-                    chunk,
-                    chunk,
-                    whole_block(channels),
-                    whole_block(line, rows, channels),
-                ]
-                + [whole_block(rows, channels)] * line,
-                out_specs=[whole_block(*pair)] * 2,
-                scratch_shapes=[pltpu.VMEM((tokens, channels), BF16)],
+                grid=(1,),
+                in_specs=[chunk, chunk, whole_block(channels)]
+                + [whole_block(line, rows, channels)] * 4
+                + [whole_block(*part.shape) for part in more],
+                out_specs=[whole_block(*out.shape) for out in outs],
+                scratch_shapes=[pltpu.VMEM((2 * tokens, channels), BF16)] * 2,
             ),
-            out_shape=[jax.ShapeDtypeStruct(pair, BF16), jax.ShapeDtypeStruct(pair, kept_as)],
-            compiler_params=params(),
+            out_shape=outs,
+            compiler_params=params(48),
             cost_estimate=NO_COST,
             name=name,
-        )(which, weight_in, weight_out, layer_scale, gathered, *upstream_line)
+        )(
+            which,
+            weight_in,
+            weight_out,
+            layer_scale,
+            gathered,
+            cotangents,
+            other_gathered,
+            other_cotangents,
+            *more,
+        )
 
     which, sums = lax.optimization_barrier((which, sums))
-    far_sent, far_kept = side_terms(0, BF16, "weight_grads_far_side")
-    far_sent, conv_own, grad_inner, grad_outer = lax.optimization_barrier(
-        (far_sent, conv_grad, grad_inner, grad_outer)
-    )
-    far_got = lax.ppermute(far_sent, "row", other_core)
+    (sent,) = side_terms(
+        far_side_kernel, 0, [], [jax.ShapeDtypeStruct(pair, BF16)], "weight_grads_far_side"
+    )
+    sent, conv_own, grad_inner, grad_outer = lax.optimization_barrier(
+        (sent, conv_grad, grad_inner, grad_outer)
+    )
+    got = lax.ppermute(sent, "row", other_side)
     scattered = lax.all_to_all(
         sums.reshape(half, piece, wide),
         "row",
@@ -714,19 +716,6 @@
         name="input_grad_conv",
     )(parity, grad_inner, conv_own, grad_outer, dw_kernel, upstream)
 
-    far_kept, voxel_grad = lax.optimization_barrier((far_kept, voxel_grad))
-    in_sent, out_sent = pl.pallas_call(
-        far_sum_kernel,
-        grid=(1,),
-        in_specs=[whole_block(*pair)] * 2,
-        out_specs=[whole_block(*pair[1:])] * 2,
-        out_shape=[jax.ShapeDtypeStruct(pair[1:], BF16)] * 2,
-        compiler_params=params(),
-        cost_estimate=NO_COST,
-        name="weight_grads_far_sum",
-    )(far_kept, far_got)
-    in_far = lax.ppermute(in_sent, "row", other_side)
-
     scattered, voxel_grad = lax.optimization_barrier((scattered, voxel_grad))
     copies = pl.pallas_call(
         spread_sum_kernel,
@@ -742,13 +731,14 @@
     totals = lax.all_to_all(
         copies, "row", split_axis=0, concat_axis=0, tiled=True, axis_index_groups=alike
     )
-    which, out_sent = lax.optimization_barrier((which, out_sent))
-    sent, kept = side_terms(2, F32, "weight_grads_near_side")
-    sent, in_far = lax.optimization_barrier((sent, in_far))
-    got = lax.ppermute(sent, "row", other_core)
-    out_far = lax.ppermute(out_sent, "row", other_side)
-
-    totals, out_far = lax.optimization_barrier((totals, out_far))
+    weight_in_grad, weight_out_grad = side_terms(
+        near_side_kernel,
+        1,
+        [got],
+        [jax.ShapeDtypeStruct(pair[1:], F32)] * 2,
+        "weight_grads_near_side",
+    )
+    totals, weight_in_grad = lax.optimization_barrier((totals, weight_in_grad))
     other_totals = lax.ppermute(totals, "row", other_core)
     kernel_grad, *vector_grads = pl.pallas_call(
         unpack_kernel,
@@ -765,17 +755,6 @@
         name="kernel_grad_unpack",
     )(parity, totals, other_totals)
 
-    weight_in_grad, weight_out_grad = pl.pallas_call(
-        last_sum_kernel,
-        grid=(1,),
-        in_specs=[whole_block(*pair)] * 2 + [whole_block(*pair[1:])] * 2,
-        out_specs=[whole_block(*pair[1:])] * 2,
-        out_shape=[jax.ShapeDtypeStruct(pair[1:], F32)] * 2,
-        compiler_params=params(),
-        cost_estimate=NO_COST,
-        name="weight_grads_sum",
-    )(kept, got, in_far, out_far)
-
     return (
         block_out.reshape(voxels.shape),
         voxel_grad.reshape(voxels.shape),

time: 92 us -> 104 us (1.13)
  local copies, waits for them, and re-layouts: 7.02 us -> 14.9 us
  waiting for transfers between devices: 5.57 us -> 13.3 us
  Pallas kernels: 44.1 us -> 39.8 us
    unnamed x34 -> x56, local copies, waits for them, and re-layouts: 6.93 us -> 14.9 us
    all_to_all x1, waiting for transfers between devices: 0.01 us -> 5.79 us  [on_device(): lax.all_to_all(normed, 'row', split_axis=0, concat_axis=0, tiled=True, ax...]
    pallas_call x4 -> x2, Pallas kernels: 14.3 us -> 9.51 us  [side_terms(): pl.pallas_call(kernel, grid_spec=pltpu.PrefetchScalarGridSpec(num_scalar_...]
    ppermute x2, starting transfers between devices: 5.19 us -> 8.06 us  [rims(): lax.ppermute(cells, 'row', between + [(j, i) for i, j in between])]
    all_to_all x1, starting transfers between devices: 5.71 us -> 3.49 us  [on_device(): lax.all_to_all(sums.reshape(half, piece, wide), 'row', split_axis=0, conc...]
    ppermute x1, waiting for transfers between devices: 0.01 us -> 1.83 us  [on_device(): half_got = lax.ppermute(half_sent, 'row', other_core)]
    ppermute x3, waiting for transfers between devices: 1.73 us -> 0.01 us  [along_line(): lax.ppermute(cells, 'row', [(i, (i + quad * steps) % count) for i in rang...]
    ppermute x1, starting transfers between devices: 1.86 us -> 3.14 us  [on_device(): other_totals = lax.ppermute(totals, 'row', other_core)]
  transfers between devices with their start and end apart: 16 -> 15, of which waited for: 3 -> 5; matrix products, arithmetic and copies ran while one was open for 0% -> 0% of each run, Pallas kernels for 46% -> 38%
where the time goes in v12:
time: 104 us; the launch traced here: 102 us
  Pallas kernels  39.8 us (38%)
  starting transfers between devices  33.5 us (32%)
  local copies, waits for them, and re-layouts  14.9 us (14%)
  waiting for transfers between devices  13.3 us (13%)
    unnamed x56, local copies, waits for them, and re-layouts  14.9 us
    pallas_call x1, Pallas kernels, on_device(): pl.pallas_call(mlp_kernel, grid=(units // block,), in_specs=[pl.BlockSpec...  10.6 us
    pallas_call x2, Pallas kernels, side_terms(): pl.pallas_call(kernel, grid_spec=pltpu.PrefetchScalarGridSpec(num_scalar_...  9.51 us
    ppermute x2, starting transfers between devices, rims(): lax.ppermute(cells, 'row', between + [(j, i) for i, j in between])  8.06 us
    pallas_call x1, Pallas kernels, on_device(): pl.pallas_call(functools.partial(kernel_grad_kernel, planes, height), gri...  6.73 us
    all_to_all x1, waiting for transfers between devices, on_device(): lax.all_to_all(normed, 'row', split_axis=0, concat_axis=0, tiled=True, ax...  5.79 us
    ppermute x3, starting transfers between devices, along_line(): lax.ppermute(cells, 'row', [(i, (i + quad * steps) % count) for i in rang...  4.92 us
    all_to_all x1, starting transfers between devices, on_device(): lax.all_to_all(copies, 'row', split_axis=0, concat_axis=0, tiled=True, ax...  4.63 us
  transfers between devices with their start and end apart: 15, of which 5 were waited for; matrix products, arithmetic and copies ran while one was open for 0% of the time, Pallas kernels for 38%

profile of v12, /device:TPU:1, one launch (start us, length us, event | category | flops | bytes accessed | tf_op | source)
XLA Modules:
  0.0 102.3 jit_solution(4848538620035014455)
XLA Ops:
  0.6 4.2 %collective-permute-start.3 = (bf16[128,768]{1,0:T(8,128)(2,1)}, bf16[128,768]{1,0:T(8,128)(2,1)S(1)}, u32[]{:S(2)}, u32[]{:S(2)}) collective-permute-start(bf16[128,768]{1,0:T(8,128)(2,1)} %bitcast.14), channel_id=1, source_target_pairs={{0,12},{1,13},{2,14},{3,15},{4,0},{5,1},{6,2},{7,3},{8,4},{9,5},{1... | collective-permute-start | bytes 589832 | tf_op jit(solution)/shard_map/ppermute | solution.py:486
  4.8 4.0 %collective-permute-start.1 = (bf16[128,768]{1,0:T(8,128)(2,1)}, bf16[128,768]{1,0:T(8,128)(2,1)S(1)}, u32[]{:S(2)}, u32[]{:S(2)}) collective-permute-start(bf16[128,768]{1,0:T(8,128)(2,1)} %bitcast.9), channel_id=1, source_target_pairs={{1,2},{3,4},{5,6},{7,8},{9,10},{11,12},{13,14},{2,1},{4,3},{6,5},{... | collective-permute-start | bytes 589832 | tf_op jit(solution)/shard_map/ppermute | solution.py:459
  8.8 0.1 collective-permute-start
  8.9 0.0 copy-start
  8.9 1.2 %copy-done = f32[343,768]{1,0:T(8,128)S(1)} copy-done((f32[343,768]{1,0:T(8,128)S(1)}, f32[343,768]{1,0:T(8,128)}, u32[]{:S(2)}) %copy-start) | copy-done | bytes 1053720
  10.1 0.9 copy-done.2
  11.1 2.1 %own_conv.1 = (f32[128,768]{1,0:T(8,128)S(1)}, f32[6,9,7,8,128]{4,3,2,1,0:T(8,128)S(1)}) custom-call(bf16[128,768]{1,0:T(8,128)(2,1)S(1)} %bitcast.11, f32[343,768]{1,0:T(8,128)S(1)} %copy-done), custom_call_target="tpu_custom_call" | custom-call | tf_op jit(solution)/shard_map/own_conv/pallas_call | solution.py:496
  13.2 0.7 copy-done.16
  14.0 0.7 copy-done.20
  14.7 0.7 collective-permute-start.4
  15.4 0.7 copy-done.9
  16.1 0.9 copy-done.10
  17.0 1.0 copy-done.17
  18.0 0.7 copy-done.25
  18.7 0.7 copy-done.27
  19.4 3.6 %rim_conv.1 = (bf16[4,128,768]{2,1,0:T(8,128)(2,1)}, f32[128,768]{1,0:T(8,128)S(1)}) custom-call(s32[1]{0:T(128)} %bitcast.core, bf16[128,768]{1,0:T(8,128)(2,1)S(1)} %copy-done.10, bf16[128,768]{1,0:T(8,128)(2,1)S(1)} %collective-permute-done.1.outer, f32[6,9,7,8,128]{4,3,2,1,0:T(8,128)S(1)} %get-tuple-element.43.split, f32[128,768]{1,0:T(8,128)S(1)} %copy-done.17, ...), custom_call_target="tpu_custom_call" | custom-call | tf_op jit(solution)/shard_map/rim_conv/pallas_call | solution.py:516
  23.0 0.7 copy-done.14
  23.8 4.5 %all-to-all-start.1 = ((bf16[4,128,768]{2,1,0:T(8,128)(2,1)}), bf16[4,128,768]{2,1,0:T(8,128)(2,1)S(1)}, u32[]{:S(2)}, u32[]{:S(2)}) async-start(bf16[4,128,768]{2,1,0:T(8,128)(2,1)} %get-tuple-element.48.normed), calls=%async_computation.1 | async-start | bytes 1572864 | tf_op jit(solution)/shard_map/all_to_all | solution.py:545
  28.3 0.9 copy-done.21
  29.3 10.6 %mlp_both_ways.1 = (bf16[128,768]{1,0:T(8,128)(2,1)}, bf16[128,768]{1,0:T(8,128)(2,1)S(1)}, f32[8,768]{1,0:T(8,128)S(1)}, bf16[4,128,768]{2,1,0:T(8,128)(2,1)S(1)}) custom-call(bf16[4,128,768]{2,1,0:T(8,128)(2,1)} %get-tuple-element.48.normed, bf16[3072,768]{1,0:T(8,128)(2,1)} %weight_in.5, bf16[3072,768]{1,0:T(8,128)(2,1)} %weight_out.5, ...), custom_call_target="tpu_custom_call" | custom-call | tf_op jit(solution)/shard_map/mlp_both_ways/pallas_call | solution.py:551
  39.9 0.6 copy-done.23
  40.5 1.6 %collective-permute-start.7 = (bf16[4,128,768]{2,1,0:T(8,128)(2,1)S(1)}, bf16[4,128,768]{2,1,0:T(8,128)(2,1)S(1)}, u32[]{:S(2)}, u32[]{:S(2)}) collective-permute-start(bf16[4,128,768]{2,1,0:T(8,128)(2,1)S(1)} %get-tuple-element.60.cot), channel_id=1, source_target_pairs={{0,1},{1,0},{2,3},{3,2},{4,5},{5,4},{6,7},{7,6},{8,9},{9,8},{10,11... | collective-permute-start | bytes 2359304 | tf_op jit(solution)/shard_map/ppermute | solution.py:647
  42.1 5.8 %all-to-all-done.1.norm = bf16[4,128,768]{2,1,0:T(8,128)(2,1)S(1)} async-done(((bf16[4,128,768]{2,1,0:T(8,128)(2,1)}), bf16[4,128,768]{2,1,0:T(8,128)(2,1)S(1)}, u32[]{:S(2)}, u32[]{:S(2)}) %all-to-all-start.1) | async-done | bytes 786464 | tf_op jit(solution)/shard_map/all_to_all | solution.py:545
  47.9 1.5 %collective-permute-start.6 = (bf16[4,128,768]{2,1,0:T(8,128)(2,1)S(1)}, bf16[4,128,768]{2,1,0:T(8,128)(2,1)S(1)}, u32[]{:S(2)}, u32[]{:S(2)}) collective-permute-start(bf16[4,128,768]{2,1,0:T(8,128)(2,1)S(1)} %all-to-all-done.1.norm), channel_id=1, source_target_pairs={{0,1},{1,0},{2,3},{3,2},{4,5},{5,4},{6,7},{7,6},{8,9},{9,8},{10,11... | collective-permute-start | bytes 2359304 | tf_op jit(solution)/shard_map/ppermute | solution.py:646
  49.4 0.1 pad_add_fusion.1.which
  49.4 0.9 copy-done.8
  50.4 0.9 copy-done.11
  51.3 0.7 copy-done.24
  52.0 6.7 %kernel_grad_terms.1 = (bf16[384,384]{1,0:T(8,128)(2,1)}, bf16[384,384]{1,0:T(8,128)(2,1)S(1)}) custom-call(s32[2]{0:T(128)S(1)} %pad_add_fusion.1.which, bf16[128,768]{1,0:T(8,128)(2,1)S(1)} %copy-done.11, bf16[128,768]{1,0:T(8,128)(2,1)S(1)} %bitcast.13, bf16[128,768]{1,0:T(8,128)(2,1)S(1)} %copy-done.8, bf16[128,768]{1,0:T(8,128)(2,1)S(1)} %get-tuple-element.63.grads.own, ...), custom_call_target="tpu_custom_call" | custom-call | tf_op jit(solution)/shard_map/kernel_grad_terms/pallas_call | solution.py:599
  58.8 0.7 copy-done.18
  59.5 0.1 pad_add_fusion.which
  59.6 1.8 %collective-permute-done.5.got = bf16[384,384]{1,0:T(8,128)(2,1)} collective-permute-done((bf16[384,384]{1,0:T(8,128)(2,1)}, bf16[384,384]{1,0:T(8,128)(2,1)}, u32[]{:S(2)}, u32[]{:S(2)}) %collective-permute-start.5) | collective-permute-done | bytes 294944 | tf_op jit(solution)/shard_map/ppermute | solution.py:623
  61.4 1.0 copy-done.19
  62.4 1.7 %kernel_grad_chip_sum.1 = bf16[384,384]{1,0:T(8,128)(2,1)} custom-call(bf16[384,384]{1,0:T(8,128)(2,1)S(1)} %copy-done.19, bf16[384,384]{1,0:T(8,128)(2,1)} %collective-permute-done.5.got), custom_call_target="tpu_custom_call" | custom-call | tf_op jit(solution)/shard_map/kernel_grad_chip_sum/pallas_call | solution.py:625
  64.1 3.5 %all-to-all-start = ((bf16[8,48,384]{2,1,0:T(8,128)(2,1)}), bf16[8,48,384]{2,1,0:T(8,128)(2,1)S(1)}, u32[]{:S(2)}, u32[]{:S(2)}) async-start(bf16[8,48,384]{2,1,0:T(8,128)(2,1)} %bitcast.7), calls=%async_computation | async-start | bytes 589824 | tf_op jit(solution)/shard_map/all_to_all | solution.py:687
  67.6 4.1 %collective-permute-start.9 = (bf16[128,768]{1,0:T(8,128)(2,1)}, bf16[128,768]{1,0:T(8,128)(2,1)S(1)}, u32[]{:S(2)}, u32[]{:S(2)}) collective-permute-start(bf16[128,768]{1,0:T(8,128)(2,1)} %copy-done.5), channel_id=1, source_target_pairs={{1,2},{3,4},{5,6},{7,8},{9,10},{11,12},{13,14},{2,1},{4,3},{6,5},{... | collective-permute-start | bytes 589832 | tf_op jit(solution)/shard_map/ppermute | solution.py:459
  71.7 0.1 collective-permute-start.8
  71.8 4.7 %weight_grads_far_side.1 = bf16[2,192,768]{2,1,0:T(8,128)(2,1)} custom-call(s32[6]{0:T(128)S(1)} %pad_add_fusion.which, bf16[3072,768]{1,0:T(8,128)(2,1)} %weight_in.5, bf16[3072,768]{1,0:T(8,128)(2,1)} %weight_out.5, f32[768]{0:T(1024)S(1)} %copy-done.22, bf16[4,128,768]{2,1,0:T(8,128)(2,1)S(1)} %all-to-all-done.1.norm, ...), custom_call_target="tpu_custom_call" | custom-call | tf_op jit(solution)/shard_map/weight_grads_far_side/pallas_call | solution.py:652
  76.5 1.1 %collective-permute-done.9.outer = bf16[128,768]{1,0:T(8,128)(2,1)S(1)} collective-permute-done((bf16[128,768]{1,0:T(8,128)(2,1)}, bf16[128,768]{1,0:T(8,128)(2,1)S(1)}, u32[]{:S(2)}, u32[]{:S(2)}) %collective-permute-start.9) | collective-permute-done | bytes 196640 | tf_op jit(solution)/shard_map/ppermute | solution.py:459
  77.6 1.5 %collective-permute-start.10 = (bf16[2,192,768]{2,1,0:T(8,128)(2,1)}, bf16[2,192,768]{2,1,0:T(8,128)(2,1)}, u32[]{:S(2)}, u32[]{:S(2)}) collective-permute-start(bf16[2,192,768]{2,1,0:T(8,128)(2,1)} %weight_grads_far_side.1), channel_id=1, source_target_pairs={{0,2},{1,3},{2,0},{3,1},{4,6},{5,7},{6,4},{7,5},{8,10},{9,11},{10,... | collective-permute-start | bytes 1769480 | tf_op jit(solution)/shard_map/ppermute | solution.py:686
  79.1 4.3 %input_grad_conv.1 = bf16[128,768]{1,0:T(8,128)(2,1)} custom-call(s32[1]{0:T(128)} %bitcast.core, bf16[128,768]{1,0:T(8,128)(2,1)S(1)} %collective-permute-done.8.inner, bf16[128,768]{1,0:T(8,128)(2,1)S(1)} %copy-done.6, bf16[128,768]{1,0:T(8,128)(2,1)S(1)} %collective-permute-done.9.outer, f32[343,768]{1,0:T(8,128)S(1)} %copy-done.1, ...), custom_call_target="tpu_custom_call" | custom-call | tf_op jit(solution)/shard_map/input_grad_conv/pallas_call | solution.py:695
  83.4 0.7 copy-done.4
  84.1 4.6 %all-to-all-start.2 = ((bf16[8,48,384]{2,1,0:T(8,128)(2,1)}), bf16[8,48,384]{2,1,0:T(8,128)(2,1)S(1)}, u32[]{:S(2)}, u32[]{:S(2)}) async-start(bf16[8,48,384]{2,1,0:T(8,128)(2,1)} %copy-done.4), calls=%async_computation.2 | async-start | bytes 589824 | tf_op jit(solution)/shard_map/all_to_all | solution.py:731
  88.8 3.3 %collective-permute-done.10.got = bf16[2,192,768]{2,1,0:T(8,128)(2,1)} collective-permute-done((bf16[2,192,768]{2,1,0:T(8,128)(2,1)}, bf16[2,192,768]{2,1,0:T(8,128)(2,1)}, u32[]{:S(2)}, u32[]{:S(2)}) %collective-permute-start.10) | collective-permute-done | bytes 589856 | tf_op jit(solution)/shard_map/ppermute | solution.py:686
  92.1 4.9 %weight_grads_near_side.1 = (f32[192,768]{1,0:T(8,128)}, f32[192,768]{1,0:T(8,128)}) custom-call(s32[6]{0:T(128)S(1)} %pad_add_fusion.which, bf16[3072,768]{1,0:T(8,128)(2,1)} %weight_in.5, bf16[3072,768]{1,0:T(8,128)(2,1)} %weight_out.5, f32[768]{0:T(1024)S(1)} %copy-done.22, bf16[4,128,768]{2,1,0:T(8,128)(2,1)S(1)} %all-to-all-done.1.norm, ...), custom_call_target="tpu_custom_call" | custom-call | tf_op jit(solution)/shard_map/weight_grads_near_side/pallas_call | solution.py:652
  96.9 3.1 %collective-permute-start.11 = (bf16[8,48,384]{2,1,0:T(8,128)(2,1)S(1)}, bf16[8,48,384]{2,1,0:T(8,128)(2,1)S(1)}, u32[]{:S(2)}, u32[]{:S(2)}) collective-permute-start(bf16[8,48,384]{2,1,0:T(8,128)(2,1)S(1)} %all-to-all-done.2.own), channel_id=1, source_target_pairs={{0,1},{1,0},{2,3},{3,2},{4,5},{5,4},{6,7},{7,6},{8,9},{9,8},{10,11... | collective-permute-start | bytes 884744 | tf_op jit(solution)/shard_map/ppermute | solution.py:742
  100.1 1.2 %collective-permute-done.11.other = bf16[8,48,384]{2,1,0:T(8,128)(2,1)S(1)} collective-permute-done((bf16[8,48,384]{2,1,0:T(8,128)(2,1)S(1)}, bf16[8,48,384]{2,1,0:T(8,128)(2,1)S(1)}, u32[]{:S(2)}, u32[]{:S(2)}) %collective-permute-start.11) | collective-permute-done | bytes 294944 | tf_op jit(solution)/shard_map/ppermute | solution.py:742
  101.3 1.1 %kernel_grad_unpack.1 = (f32[343,768]{1,0:T(8,128)}, f32[768]{0:T(1024)}, f32[768]{0:T(1024)}, f32[768]{0:T(1024)}) custom-call(s32[1]{0:T(128)} %bitcast.core, bf16[8,48,384]{2,1,0:T(8,128)(2,1)S(1)} %all-to-all-done.2.own, bf16[8,48,384]{2,1,0:T(8,128)(2,1)S(1)} %collective-permute-done.11.other), custom_call_target="tpu_custom_call" | custom-call | tf_op jit(solution)/shard_map/kernel_grad_unpack/pallas_call | solution.py:743
  (51 shorter events, 0.2 us)
Async XLA Ops:
  0.6 13.3 %collective-permute-start.3 = (bf16[128,768]{1,0:T(8,128)(2,1)}, bf16[128,768]{1,0:T(8,128)(2,1)S(1)}, u32[]{:S(2)}, u32[]{:S(2)}) collective-permute-start(bf16[128,768]{1,0:T(8,128)(2,1)} %bitcast.14), channel_id=1, source_target_pairs={{0,12},{1,13},{2,14},{3,15},{4,0},{5,1},{6,2},{7,3},{8,4},{9,5},{1... | collective-permute-start | bytes 589832 | tf_op jit(solution)/shard_map/ppermute | solution.py:486
  4.8 9.8 %collective-permute-start.2 = (bf16[128,768]{1,0:T(8,128)(2,1)}, bf16[128,768]{1,0:T(8,128)(2,1)}, u32[]{:S(2)}, u32[]{:S(2)}) collective-permute-start(bf16[128,768]{1,0:T(8,128)(2,1)} %bitcast.15), channel_id=1, source_target_pairs={{0,4},{1,5},{2,6},{3,7},{4,8},{5,9},{6,10},{7,11},{8,12},{9,13},{1... | collective-permute-start | bytes 589832 | tf_op jit(solution)/shard_map/ppermute | solution.py:486
  4.8 10.5 %collective-permute-start.1 = (bf16[128,768]{1,0:T(8,128)(2,1)}, bf16[128,768]{1,0:T(8,128)(2,1)S(1)}, u32[]{:S(2)}, u32[]{:S(2)}) collective-permute-start(bf16[128,768]{1,0:T(8,128)(2,1)} %bitcast.9), channel_id=1, source_target_pairs={{1,2},{3,4},{5,6},{7,8},{9,10},{11,12},{13,14},{2,1},{4,3},{6,5},{... | collective-permute-start | bytes 589832 | tf_op jit(solution)/shard_map/ppermute | solution.py:459
  8.8 6.6 %collective-permute-start = (bf16[128,768]{1,0:T(8,128)(2,1)}, bf16[128,768]{1,0:T(8,128)(2,1)S(1)}, u32[]{:S(2)}, u32[]{:S(2)}) collective-permute-start(bf16[128,768]{1,0:T(8,128)(2,1)} %bitcast.10), channel_id=1, source_target_pairs={{0,1},{1,0},{2,3},{3,2},{4,5},{5,4},{6,7},{7,6},{8,9},{9,8},{10,11... | collective-permute-start | bytes 589832 | tf_op jit(solution)/shard_map/ppermute | solution.py:458
  8.9 1.2 %copy-start = (f32[343,768]{1,0:T(8,128)S(1)}, f32[343,768]{1,0:T(8,128)}, u32[]{:S(2)}) copy-start(f32[343,768]{1,0:T(8,128)} %taps.3) | copy-start | bytes 3161092
  10.1 0.9 copy-start.2
  13.2 0.7 copy-start.16
  14.0 0.7 copy-start.20
  14.7 9.1 %collective-permute-start.4 = (bf16[128,768]{1,0:T(8,128)(2,1)}, bf16[128,768]{1,0:T(8,128)(2,1)}, u32[]{:S(2)}, u32[]{:S(2)}) collective-permute-start(bf16[128,768]{1,0:T(8,128)(2,1)} %collective-permute-done.2.rest_1_), channel_id=1, source_target_pairs={{0,4},{1,5},{2,6},{3,7},{4,8},{5,9},{6,10},{7,11},{8,12},{9,13},{1... | collective-permute-start | bytes 589832 | tf_op jit(solution)/shard_map/ppermute | solution.py:486
  15.4 8.4 %copy-start.7 = (bf16[128,768]{1,0:T(8,128)(2,1)}, bf16[128,768]{1,0:T(8,128)(2,1)S(1)}, u32[]{:S(2)}) copy-start(bf16[128,768]{1,0:T(8,128)(2,1)S(1)} %collective-permute-done.1.outer) | copy-start | bytes 589828
  15.4 0.7 copy-start.9
  16.1 0.9 copy-start.10
  17.0 1.0 copy-start.17
  18.0 0.7 copy-start.25
  18.7 0.7 copy-start.27
  19.4 8.9 %copy-start.3 = (bf16[4,4,8,768]{3,2,1,0:T(8,128)(2,1)S(1)}, bf16[4,4,8,768]{3,2,1,0:T(8,128)(2,1)}, u32[]{:S(2)}) copy-start(bf16[4,4,8,768]{3,2,1,0:T(8,128)(2,1)} %param.8) | copy-start | bytes 589828
  19.4 8.9 %copy-start.22 = (f32[768]{0:T(1024)S(1)}, f32[768]{0:T(1024)}, u32[]{:S(2)}) copy-start(f32[768]{0:T(1024)} %scale.3) | copy-start | bytes 9220
  19.4 8.9 %copy-start.26 = (f32[768]{0:T(1024)S(1)}, f32[768]{0:T(1024)}, u32[]{:S(2)}) copy-start(f32[768]{0:T(1024)} %norm_gain.1) | copy-start | bytes 9220
  23.0 0.7 copy-start.14
  23.8 4.5 %copy-start.12 = (bf16[4,4,8,768]{3,2,1,0:T(8,128)(2,1)S(1)}, bf16[4,4,8,768]{3,2,1,0:T(8,128)(2,1)}, u32[]{:S(2)}) copy-start(bf16[4,4,8,768]{3,2,1,0:T(8,128)(2,1)} %param.15) | copy-start | bytes 589828
  23.8 4.5 %copy-start.15 = (f32[128,768]{1,0:T(8,128)S(1)}, f32[128,768]{1,0:T(8,128)}, u32[]{:S(2)}) copy-start(f32[128,768]{1,0:T(8,128)} %copy-done.14) | copy-start | bytes 1179652
  23.8 24.1 %all-to-all-start.1 = ((bf16[4,128,768]{2,1,0:T(8,128)(2,1)}), bf16[4,128,768]{2,1,0:T(8,128)(2,1)S(1)}, u32[]{:S(2)}, u32[]{:S(2)}) async-start(bf16[4,128,768]{2,1,0:T(8,128)(2,1)} %get-tuple-element.48.normed), calls=%async_computation.1 | async-start | bytes 1572864 | tf_op jit(solution)/shard_map/all_to_all | solution.py:545
  28.3 0.9 copy-start.21
  39.9 0.6 copy-start.23
  40.5 23.6 %copy-start.5 = (bf16[128,768]{1,0:T(8,128)(2,1)}, bf16[128,768]{1,0:T(8,128)(2,1)S(1)}, u32[]{:S(2)}) copy-start(bf16[128,768]{1,0:T(8,128)(2,1)S(1)} %get-tuple-element.63.grads.own) | copy-start | bytes 589828
  40.5 31.3 %collective-permute-start.7 = (bf16[4,128,768]{2,1,0:T(8,128)(2,1)S(1)}, bf16[4,128,768]{2,1,0:T(8,128)(2,1)S(1)}, u32[]{:S(2)}, u32[]{:S(2)}) collective-permute-start(bf16[4,128,768]{2,1,0:T(8,128)(2,1)S(1)} %get-tuple-element.60.cot), channel_id=1, source_target_pairs={{0,1},{1,0},{2,3},{3,2},{4,5},{5,4},{6,7},{7,6},{8,9},{9,8},{10,11... | collective-permute-start | bytes 2359304 | tf_op jit(solution)/shard_map/ppermute | solution.py:647
  47.9 23.9 %collective-permute-start.6 = (bf16[4,128,768]{2,1,0:T(8,128)(2,1)S(1)}, bf16[4,128,768]{2,1,0:T(8,128)(2,1)S(1)}, u32[]{:S(2)}, u32[]{:S(2)}) collective-permute-start(bf16[4,128,768]{2,1,0:T(8,128)(2,1)S(1)} %all-to-all-done.1.norm), channel_id=1, source_target_pairs={{0,1},{1,0},{2,3},{3,2},{4,5},{5,4},{6,7},{7,6},{8,9},{9,8},{10,11... | collective-permute-start | bytes 2359304 | tf_op jit(solution)/shard_map/ppermute | solution.py:646
  49.4 0.9 copy-start.8
  50.4 0.9 copy-start.11
  51.3 0.7 copy-start.24
  58.8 0.7 copy-start.18
  59.5 1.9 %collective-permute-start.5 = (bf16[384,384]{1,0:T(8,128)(2,1)}, bf16[384,384]{1,0:T(8,128)(2,1)}, u32[]{:S(2)}, u32[]{:S(2)}) collective-permute-start(bf16[384,384]{1,0:T(8,128)(2,1)} %get-tuple-element.57), channel_id=1, source_target_pairs={{0,1},{1,0},{2,3},{3,2},{4,5},{5,4},{6,7},{7,6},{8,9},{9,8},{10,11... | collective-permute-start | bytes 884744 | tf_op jit(solution)/shard_map/ppermute | solution.py:623
  61.4 1.0 copy-start.19
  64.1 19.2 %all-to-all-start = ((bf16[8,48,384]{2,1,0:T(8,128)(2,1)}), bf16[8,48,384]{2,1,0:T(8,128)(2,1)S(1)}, u32[]{:S(2)}, u32[]{:S(2)}) async-start(bf16[8,48,384]{2,1,0:T(8,128)(2,1)} %bitcast.7), calls=%async_computation | async-start | bytes 589824 | tf_op jit(solution)/shard_map/all_to_all | solution.py:687
  67.6 11.4 %copy-start.1 = (f32[343,768]{1,0:T(8,128)S(1)}, f32[343,768]{1,0:T(8,128)}, u32[]{:S(2)}) copy-start(f32[343,768]{1,0:T(8,128)} %taps.3) | copy-start | bytes 3161092
  67.6 11.4 %copy-start.6 = (bf16[128,768]{1,0:T(8,128)(2,1)S(1)}, bf16[128,768]{1,0:T(8,128)(2,1)}, u32[]{:S(2)}) copy-start(bf16[128,768]{1,0:T(8,128)(2,1)} %copy-done.5) | copy-start | bytes 589828
  67.6 11.4 %copy-start.13 = (bf16[4,4,8,768]{3,2,1,0:T(8,128)(2,1)S(1)}, bf16[4,4,8,768]{3,2,1,0:T(8,128)(2,1)}, u32[]{:S(2)}) copy-start(bf16[4,4,8,768]{3,2,1,0:T(8,128)(2,1)} %param.15) | copy-start | bytes 589828
  67.6 9.9 %collective-permute-start.9 = (bf16[128,768]{1,0:T(8,128)(2,1)}, bf16[128,768]{1,0:T(8,128)(2,1)S(1)}, u32[]{:S(2)}, u32[]{:S(2)}) collective-permute-start(bf16[128,768]{1,0:T(8,128)(2,1)} %copy-done.5), channel_id=1, source_target_pairs={{1,2},{3,4},{5,6},{7,8},{9,10},{11,12},{13,14},{2,1},{4,3},{6,5},{... | collective-permute-start | bytes 589832 | tf_op jit(solution)/shard_map/ppermute | solution.py:459
  71.7 5.8 %collective-permute-start.8 = (bf16[128,768]{1,0:T(8,128)(2,1)}, bf16[128,768]{1,0:T(8,128)(2,1)S(1)}, u32[]{:S(2)}, u32[]{:S(2)}) collective-permute-start(bf16[128,768]{1,0:T(8,128)(2,1)} %copy-done.5), channel_id=1, source_target_pairs={{0,1},{1,0},{2,3},{3,2},{4,5},{5,4},{6,7},{7,6},{8,9},{9,8},{10,11... | collective-permute-start | bytes 589832 | tf_op jit(solution)/shard_map/ppermute | solution.py:458
  77.6 14.5 %collective-permute-start.10 = (bf16[2,192,768]{2,1,0:T(8,128)(2,1)}, bf16[2,192,768]{2,1,0:T(8,128)(2,1)}, u32[]{:S(2)}, u32[]{:S(2)}) collective-permute-start(bf16[2,192,768]{2,1,0:T(8,128)(2,1)} %weight_grads_far_side.1), channel_id=1, source_target_pairs={{0,2},{1,3},{2,0},{3,1},{4,6},{5,7},{6,4},{7,5},{8,10},{9,11},{10,... | collective-permute-start | bytes 1769480 | tf_op jit(solution)/shard_map/ppermute | solution.py:686
  83.4 0.7 copy-start.4
  84.1 12.8 %all-to-all-start.2 = ((bf16[8,48,384]{2,1,0:T(8,128)(2,1)}), bf16[8,48,384]{2,1,0:T(8,128)(2,1)S(1)}, u32[]{:S(2)}, u32[]{:S(2)}) async-start(bf16[8,48,384]{2,1,0:T(8,128)(2,1)} %copy-done.4), calls=%async_computation.2 | async-start | bytes 589824 | tf_op jit(solution)/shard_map/all_to_all | solution.py:731
  96.9 4.4 %collective-permute-start.11 = (bf16[8,48,384]{2,1,0:T(8,128)(2,1)S(1)}, bf16[8,48,384]{2,1,0:T(8,128)(2,1)S(1)}, u32[]{:S(2)}, u32[]{:S(2)}) collective-permute-start(bf16[8,48,384]{2,1,0:T(8,128)(2,1)S(1)} %all-to-all-done.2.own), channel_id=1, source_target_pairs={{0,1},{1,0},{2,3},{3,2},{4,5},{5,4},{6,7},{7,6},{8,9},{9,8},{10,11... | collective-permute-start | bytes 884744 | tf_op jit(solution)/shard_map/ppermute | solution.py:742

commit v13 on v12

--- a/solution.py
+++ b/solution.py
@@ -378,34 +378,19 @@
     )
 
 
-def far_side_kernel(
-    which, weight_in, weight_out, scale, norm, cot, other_norm, other_cot, sent, aligned, mixed_grad
+def one_side_kernel(
+    which, weight_in, weight_out, scale, norm, cot, other_norm, other_cot, *rest
 ):
+    *outs, aligned, mixed_grad = rest
     sets = ((norm, cot), (other_norm, other_cot))
     terms = weight_grad_terms(which, weight_in, weight_out, scale, sets, aligned, mixed_grad)
-    for k in range(2):
-        sent[k] = terms[k].astype(BF16)
-
-
-def near_side_kernel(
-    which,
-    weight_in,
-    weight_out,
-    scale,
-    norm,
-    cot,
-    other_norm,
-    other_cot,
-    got,
-    in_grad,
-    out_grad,
-    aligned,
-    mixed_grad,
-):
-    sets = ((norm, cot), (other_norm, other_cot))
-    terms = weight_grad_terms(which, weight_in, weight_out, scale, sets, aligned, mixed_grad)
-    for k, out in enumerate((in_grad, out_grad)):
-        out[...] = terms[k] + got[k].astype(F32)
+    for k, out in enumerate(outs):
+        out[...] = terms[k].astype(out.dtype)
+
+
+def last_sum_kernel(in_kept, out_kept, in_got, out_got, in_grad, out_grad):
+    in_grad[...] = in_kept[...] + in_got[...].astype(F32)
+    out_grad[...] = out_kept[...] + out_got[...].astype(F32)
 
 
 def chip_sum_kernel(kept, got, out):
@@ -439,7 +424,7 @@
     by_core(core, own, other, lambda outer, inner: unpack(inner, outer))
 
 
-def params(limit=16):
+def params(limit=44):
     return pltpu.CompilerParams(vmem_limit_bytes=limit * 1024 * 1024)
 
 
@@ -546,7 +531,7 @@
         normed, "row", split_axis=0, concat_axis=0, tiled=True, axis_index_groups=lines
     )
 
-    block = 384
+    block = 512
     whole = whole_block(rows, channels)
     block_out, conv_grad, small, cotangents = pl.pallas_call(
         mlp_kernel,
@@ -577,7 +562,7 @@
             pltpu.VMEM((rows, channels), F32),
             pltpu.VMEM((rows, channels), BF16),
         ],
-        compiler_params=params(48),
+        compiler_params=params(),
         cost_estimate=NO_COST,
         name="mlp_both_ways",
     )(normed, weight_in, weight_out, centered, norm_gain, layer_scale, own, *upstream_line)
@@ -619,7 +604,7 @@
         name="kernel_grad_terms",
     )(jnp.stack([core, 1 - core]), inner, own, outer, conv_grad, small)
 
-    half_sent, conv_grad = lax.optimization_barrier((half_sent, conv_grad))
+    half_sent, conv_grad, gathered = lax.optimization_barrier((half_sent, conv_grad, gathered))
     half_got = lax.ppermute(half_sent, "row", other_core)
     grad_inner, grad_outer = rims(conv_grad)
     sums = pl.pallas_call(
@@ -645,23 +630,22 @@
     )
     other_gathered = lax.ppermute(gathered, "row", other_core)
     other_cotangents = lax.ppermute(cotangents, "row", other_core)
-    pair = (2, share, channels)
-
-    def side_terms(kernel, number, more, outs, name):
+    single = (share, channels)
+
+    def side_terms(number, dtype, name):
         chunk = pl.BlockSpec((share, channels), lambda _, w: (w[number], 0))
         return pl.pallas_call(
-            kernel,
+            one_side_kernel,
             grid_spec=pltpu.PrefetchScalarGridSpec(
                 num_scalar_prefetch=1,
                 grid=(1,),
                 in_specs=[chunk, chunk, whole_block(channels)]
-                + [whole_block(line, rows, channels)] * 4
-                + [whole_block(*part.shape) for part in more],
-                out_specs=[whole_block(*out.shape) for out in outs],
+                + [whole_block(line, rows, channels)] * 4,
+                out_specs=[whole_block(*single)] * 2,
                 scratch_shapes=[pltpu.VMEM((2 * tokens, channels), BF16)] * 2,
             ),
-            out_shape=outs,
-            compiler_params=params(48),
+            out_shape=[jax.ShapeDtypeStruct(single, dtype)] * 2,
+            compiler_params=params(),
             cost_estimate=NO_COST,
             name=name,
         )(
@@ -673,17 +657,15 @@
             cotangents,
             other_gathered,
             other_cotangents,
-            *more,
         )
 
     which, sums = lax.optimization_barrier((which, sums))
-    (sent,) = side_terms(
-        far_side_kernel, 0, [], [jax.ShapeDtypeStruct(pair, BF16)], "weight_grads_far_side"
-    )
-    sent, conv_own, grad_inner, grad_outer = lax.optimization_barrier(
-        (sent, conv_grad, grad_inner, grad_outer)
-    )
-    got = lax.ppermute(sent, "row", other_side)
+    in_sent, out_sent = side_terms(0, BF16, "weight_grads_far_side")
+    in_sent, conv_own, grad_inner, grad_outer = lax.optimization_barrier(
+        (in_sent, conv_grad, grad_inner, grad_outer)
+    )
+    in_got = lax.ppermute(in_sent, "row", other_side)
+    out_got = lax.ppermute(out_sent, "row", other_side)
     scattered = lax.all_to_all(
         sums.reshape(half, piece, wide),
         "row",
@@ -731,14 +713,9 @@
     totals = lax.all_to_all(
         copies, "row", split_axis=0, concat_axis=0, tiled=True, axis_index_groups=alike
     )
-    weight_in_grad, weight_out_grad = side_terms(
-        near_side_kernel,
-        1,
-        [got],
-        [jax.ShapeDtypeStruct(pair[1:], F32)] * 2,
-        "weight_grads_near_side",
-    )
-    totals, weight_in_grad = lax.optimization_barrier((totals, weight_in_grad))
+    which, in_got = lax.optimization_barrier((which, in_got))
+    in_kept, out_kept = side_terms(1, F32, "weight_grads_near_side")
+    totals, in_kept = lax.optimization_barrier((totals, in_kept))
     other_totals = lax.ppermute(totals, "row", other_core)
     kernel_grad, *vector_grads = pl.pallas_call(
         unpack_kernel,
@@ -755,6 +732,17 @@
         name="kernel_grad_unpack",
     )(parity, totals, other_totals)
 
+    weight_in_grad, weight_out_grad = pl.pallas_call(
+        last_sum_kernel,
+        grid=(1,),
+        in_specs=[whole_block(*single)] * 4,
+        out_specs=[whole_block(*single)] * 2,
+        out_shape=[jax.ShapeDtypeStruct(single, F32)] * 2,
+        compiler_params=params(),
+        cost_estimate=NO_COST,
+        name="weight_grads_sum",
+    )(in_kept, out_kept, in_got, out_got)
+
     return (
         block_out.reshape(voxels.shape),
         voxel_grad.reshape(voxels.shape),

time: 104 us -> 104 us (level)
  local copies, waits for them, and re-layouts: 14.9 us -> 18.6 us
  Pallas kernels: 39.8 us -> 37.8 us
    ppermute x1 -> x2, waiting for transfers between devices: 3.32 us -> 9.63 us  [the longest x1 9.63 us: on_device(): in_got = lax.ppermute(in_sent, 'row', other_side)]
    all_to_all x1, waiting for transfers between devices: 5.79 us -> 0.92 us  [on_device(): lax.all_to_all(normed, 'row', split_axis=0, concat_axis=0, tiled=True, ax...]
    unnamed x56 -> x52, local copies, waits for them, and re-layouts: 14.9 us -> 18.6 us
    pallas_call x1, Pallas kernels: 10.6 us -> 8.67 us  [on_device(): pl.pallas_call(mlp_kernel, grid=(units // block,), in_specs=[pl.BlockSpec...]
    all_to_all x1, starting transfers between devices: 3.49 us -> 5.25 us  [on_device(): lax.all_to_all(sums.reshape(half, piece, wide), 'row', split_axis=0, conc...]
    pallas_call x1, Pallas kernels: 0.04 us -> 1.72 us  [on_device(): pl.pallas_call(spread_sum_kernel, in_specs=[whole_block(half, piece, wide...]
    pallas_call x1, Pallas kernels: 1.75 us -> 0.07 us  [on_device(): pl.pallas_call(chip_sum_kernel, in_specs=[whole_block(padded, wide)] * 2,...]
    ppermute x1, starting transfers between devices: 1.6 us -> 0.01 us  [on_device(): other_cotangents = lax.ppermute(cotangents, 'row', other_core)]
  transfers between devices with their start and end apart: 15 -> 16, of which waited for: 5 -> 5; matrix products, arithmetic and copies ran while one was open for 0% -> 0% of each run, Pallas kernels for 38% -> 34%
where the time goes in v13:
time: 104 us; the launch traced here: 103 us
  Pallas kernels  37.8 us (36%)
  starting transfers between devices  33.2 us (32%)
  local copies, waits for them, and re-layouts  18.6 us (18%)
  waiting for transfers between devices  12.3 us (12%)
    unnamed x52, local copies, waits for them, and re-layouts  18.6 us
    ppermute x1, waiting for transfers between devices, on_device(): in_got = lax.ppermute(in_sent, 'row', other_side)  9.63 us
    pallas_call x1, Pallas kernels, on_device(): pl.pallas_call(mlp_kernel, grid=(units // block,), in_specs=[pl.BlockSpec...  8.67 us
    ppermute x2, starting transfers between devices, rims(): lax.ppermute(cells, 'row', between + [(j, i) for i, j in between])  8.15 us
    pallas_call x2, Pallas kernels, side_terms(): pl.pallas_call(one_side_kernel, grid_spec=pltpu.PrefetchScalarGridSpec(nu...  7.97 us
    pallas_call x1, Pallas kernels, on_device(): pl.pallas_call(functools.partial(kernel_grad_kernel, planes, height), gri...  6.18 us
    ppermute x3, starting transfers between devices, along_line(): lax.ppermute(cells, 'row', [(i, (i + quad * steps) % count) for i in rang...  5.45 us
    all_to_all x1, starting transfers between devices, on_device(): lax.all_to_all(sums.reshape(half, piece, wide), 'row', split_axis=0, conc...  5.25 us
  transfers between devices with their start and end apart: 16, of which 5 were waited for; matrix products, arithmetic and copies ran while one was open for 0% of the time, Pallas kernels for 34%

profile of v13, /device:TPU:1, one launch (start us, length us, event | category | flops | bytes accessed | tf_op | source)
XLA Modules:
  0.0 103.0 jit_solution(5765614123092128085)
XLA Ops:
  0.6 4.2 %collective-permute-start.3 = (bf16[128,768]{1,0:T(8,128)(2,1)}, bf16[128,768]{1,0:T(8,128)(2,1)S(1)}, u32[]{:S(2)}, u32[]{:S(2)}) collective-permute-start(bf16[128,768]{1,0:T(8,128)(2,1)} %bitcast.15), channel_id=1, source_target_pairs={{0,12},{1,13},{2,14},{3,15},{4,0},{5,1},{6,2},{7,3},{8,4},{9,5},{1... | collective-permute-start | bytes 589832 | tf_op jit(solution)/shard_map/ppermute | solution.py:471
  4.8 4.0 %collective-permute-start.1 = (bf16[128,768]{1,0:T(8,128)(2,1)}, bf16[128,768]{1,0:T(8,128)(2,1)S(1)}, u32[]{:S(2)}, u32[]{:S(2)}) collective-permute-start(bf16[128,768]{1,0:T(8,128)(2,1)} %bitcast.9), channel_id=1, source_target_pairs={{1,2},{3,4},{5,6},{7,8},{9,10},{11,12},{13,14},{2,1},{4,3},{6,5},{... | collective-permute-start | bytes 589832 | tf_op jit(solution)/shard_map/ppermute | solution.py:444
  8.8 0.1 collective-permute-start
  8.9 1.2 %copy-done.3 = f32[343,768]{1,0:T(8,128)S(1)} copy-done((f32[343,768]{1,0:T(8,128)S(1)}, f32[343,768]{1,0:T(8,128)}, u32[]{:S(2)}) %copy-start.3) | copy-done | bytes 1053720
  10.1 0.9 copy-done.5
  11.1 2.1 %own_conv.1 = (f32[128,768]{1,0:T(8,128)S(1)}, f32[6,9,7,8,128]{4,3,2,1,0:T(8,128)S(1)}) custom-call(bf16[128,768]{1,0:T(8,128)(2,1)S(1)} %bitcast.11, f32[343,768]{1,0:T(8,128)S(1)} %copy-done.3), custom_call_target="tpu_custom_call" | custom-call | tf_op jit(solution)/shard_map/own_conv/pallas_call | solution.py:481
  13.2 0.7 copy-done.18
  14.0 1.2 %collective-permute-start.4 = (bf16[128,768]{1,0:T(8,128)(2,1)}, bf16[128,768]{1,0:T(8,128)(2,1)S(1)}, u32[]{:S(2)}, u32[]{:S(2)}) collective-permute-start(bf16[128,768]{1,0:T(8,128)(2,1)} %collective-permute-done.2.rest_1_), channel_id=1, source_target_pairs={{0,4},{1,5},{2,6},{3,7},{4,8},{5,9},{6,10},{7,11},{8,12},{9,13},{1... | collective-permute-start | bytes 589832 | tf_op jit(solution)/shard_map/ppermute | solution.py:471
  15.2 0.7 copy-done.21
  15.9 0.7 copy-done.23
  16.6 3.6 %rim_conv.1 = (bf16[4,128,768]{2,1,0:T(8,128)(2,1)}, f32[128,768]{1,0:T(8,128)S(1)}) custom-call(s32[1]{0:T(128)} %bitcast.core, bf16[128,768]{1,0:T(8,128)(2,1)S(1)} %collective-permute-done.inner, bf16[128,768]{1,0:T(8,128)(2,1)S(1)} %collective-permute-done.1.outer, f32[6,9,7,8,128]{4,3,2,1,0:T(8,128)S(1)} %get-tuple-element.50.split, ...), custom_call_target="tpu_custom_call" | custom-call | tf_op jit(solution)/shard_map/rim_conv/pallas_call | solution.py:501
  20.3 1.1 %collective-permute-done.4.rest_2_ = bf16[128,768]{1,0:T(8,128)(2,1)S(1)} collective-permute-done((bf16[128,768]{1,0:T(8,128)(2,1)}, bf16[128,768]{1,0:T(8,128)(2,1)S(1)}, u32[]{:S(2)}, u32[]{:S(2)}) %collective-permute-start.4) | collective-permute-done | bytes 196640 | tf_op jit(solution)/shard_map/ppermute | solution.py:471
  21.3 3.6 %all-to-all-start = ((bf16[4,128,768]{2,1,0:T(8,128)(2,1)}), bf16[4,128,768]{2,1,0:T(8,128)(2,1)S(1)}, u32[]{:S(2)}, u32[]{:S(2)}) async-start(bf16[4,128,768]{2,1,0:T(8,128)(2,1)} %get-tuple-element.55.normed), calls=%async_computation | async-start | bytes 1572864 | tf_op jit(solution)/shard_map/all_to_all | solution.py:530
  24.9 0.1 pad_add_fusion.1.which
  25.0 2.3 %copy-done = bf16[3072,768]{1,0:T(8,128)(2,1)S(1)} copy-done((bf16[3072,768]{1,0:T(8,128)(2,1)S(1)}, bf16[3072,768]{1,0:T(8,128)(2,1)}, u32[]{:S(2)}) %copy-start) | copy-done | bytes 4718616
  27.4 8.7 %mlp_both_ways.1 = (bf16[128,768]{1,0:T(8,128)(2,1)}, bf16[128,768]{1,0:T(8,128)(2,1)S(1)}, f32[8,768]{1,0:T(8,128)S(1)}, bf16[4,128,768]{2,1,0:T(8,128)(2,1)S(1)}) custom-call(bf16[4,128,768]{2,1,0:T(8,128)(2,1)} %get-tuple-element.55.normed, bf16[3072,768]{1,0:T(8,128)(2,1)S(1)} %copy-done, bf16[3072,768]{1,0:T(8,128)(2,1)} %weight_out.5, ...), custom_call_target="tpu_custom_call" | custom-call | tf_op jit(solution)/shard_map/mlp_both_ways/pallas_call | solution.py:536
  36.0 6.2 %kernel_grad_terms.1 = (bf16[384,384]{1,0:T(8,128)(2,1)S(1)}, bf16[384,384]{1,0:T(8,128)(2,1)S(1)}) custom-call(s32[2]{0:T(128)S(1)} %pad_add_fusion.1.which, bf16[128,768]{1,0:T(8,128)(2,1)S(1)} %collective-permute-done.inner, bf16[128,768]{1,0:T(8,128)(2,1)S(1)} %bitcast.13, bf16[128,768]{1,0:T(8,128)(2,1)S(1)} %collective-permute-done.1.outer, ...), custom_call_target="tpu_custom_call" | custom-call | tf_op jit(solution)/shard_map/kernel_grad_terms/pallas_call | solution.py:584
  42.2 0.7 copy-done.8
  42.9 0.7 copy-done.14
  43.6 0.9 all-to-all-done.norm
  44.5 1.5 %collective-permute-start.5 = (bf16[384,384]{1,0:T(8,128)(2,1)S(1)}, bf16[384,384]{1,0:T(8,128)(2,1)S(1)}, u32[]{:S(2)}, u32[]{:S(2)}) collective-permute-start(bf16[384,384]{1,0:T(8,128)(2,1)S(1)} %get-tuple-element.64), channel_id=1, source_target_pairs={{0,1},{1,0},{2,3},{3,2},{4,5},{5,4},{6,7},{7,6},{8,9},{9,8},{10,11... | collective-permute-start | bytes 884744 | tf_op jit(solution)/shard_map/ppermute | solution.py:608
  46.0 0.5 collective-permute-start.6
  46.5 0.1 pad_add_fusion.which
  46.6 0.6 collective-permute-done.5.got
  47.2 0.7 copy-done.16
  47.9 1.0 copy-done.15
  48.9 1.0 copy-done.17
  49.8 0.1 kernel_grad_chip_sum.1
  49.9 0.7 copy-done.7
  50.6 5.3 %all-to-all-start.1 = ((bf16[8,48,384]{2,1,0:T(8,128)(2,1)}), bf16[8,48,384]{2,1,0:T(8,128)(2,1)}, u32[]{:S(2)}, u32[]{:S(2)}) async-start(bf16[8,48,384]{2,1,0:T(8,128)(2,1)} %bitcast.14), calls=%async_computation.1 | async-start | bytes 589824 | tf_op jit(solution)/shard_map/all_to_all | solution.py:669
  55.9 4.2 %collective-permute-start.9 = (bf16[128,768]{1,0:T(8,128)(2,1)}, bf16[128,768]{1,0:T(8,128)(2,1)S(1)}, u32[]{:S(2)}, u32[]{:S(2)}) collective-permute-start(bf16[128,768]{1,0:T(8,128)(2,1)} %copy-done.8), channel_id=1, source_target_pairs={{1,2},{3,4},{5,6},{7,8},{9,10},{11,12},{13,14},{2,1},{4,3},{6,5},{... | collective-permute-start | bytes 589832 | tf_op jit(solution)/shard_map/ppermute | solution.py:444
  60.1 0.1 collective-permute-start.8
  60.2 2.3 %copy-done.1 = bf16[3072,768]{1,0:T(8,128)(2,1)S(1)} copy-done((bf16[3072,768]{1,0:T(8,128)(2,1)S(1)}, bf16[3072,768]{1,0:T(8,128)(2,1)}, u32[]{:S(2)}) %copy-start.1) | copy-done | bytes 4718616
  62.5 4.0 %weight_grads_far_side.1 = (bf16[192,768]{1,0:T(8,128)(2,1)S(1)}, bf16[192,768]{1,0:T(8,128)(2,1)S(1)}) custom-call(s32[6]{0:T(128)S(1)} %pad_add_fusion.which, bf16[3072,768]{1,0:T(8,128)(2,1)S(1)} %copy-done.1, bf16[3072,768]{1,0:T(8,128)(2,1)} %weight_out.5, f32[768]{0:T(1024)S(1)} %copy-done.20, bf16[4,128,768]{2,1,0:T(8,128)(2,1)S(1)} %all-to-all-done.norm, ...), custom_call_target="tpu_custom_call" | custom-call | tf_op jit(solution)/shard_map/weight_grads_far_side/pallas_call | solution.py:637
  66.5 0.7 copy-done.24
  67.2 0.1 copy-done.25
  67.3 4.3 %input_grad_conv.1 = bf16[128,768]{1,0:T(8,128)(2,1)} custom-call(s32[1]{0:T(128)} %bitcast.core, bf16[128,768]{1,0:T(8,128)(2,1)S(1)} %collective-permute-done.8.inner, bf16[128,768]{1,0:T(8,128)(2,1)S(1)} %copy-done.9, bf16[128,768]{1,0:T(8,128)(2,1)S(1)} %collective-permute-done.9.outer, f32[343,768]{1,0:T(8,128)S(1)} %copy-done.4, ...), custom_call_target="tpu_custom_call" | custom-call | tf_op jit(solution)/shard_map/input_grad_conv/pallas_call | solution.py:677
  71.6 1.7 %kernel_grad_sum.1 = bf16[8,48,384]{2,1,0:T(8,128)(2,1)} custom-call(bf16[8,48,384]{2,1,0:T(8,128)(2,1)} %all-to-all-done.1.parts), custom_call_target="tpu_custom_call" | custom-call | tf_op jit(solution)/shard_map/kernel_grad_sum/pallas_call | solution.py:702
  73.3 4.3 %all-to-all-start.2 = ((bf16[8,48,384]{2,1,0:T(8,128)(2,1)}), bf16[8,48,384]{2,1,0:T(8,128)(2,1)S(1)}, u32[]{:S(2)}, u32[]{:S(2)}) async-start(bf16[8,48,384]{2,1,0:T(8,128)(2,1)} %kernel_grad_sum.1), calls=%async_computation.2 | async-start | bytes 589824 | tf_op jit(solution)/shard_map/all_to_all | solution.py:713
  77.6 1.5 %collective-permute-start.10 = (bf16[192,768]{1,0:T(8,128)(2,1)}, bf16[192,768]{1,0:T(8,128)(2,1)S(1)}, u32[]{:S(2)}, u32[]{:S(2)}) collective-permute-start(bf16[192,768]{1,0:T(8,128)(2,1)} %copy-done.25), channel_id=1, source_target_pairs={{0,2},{1,3},{2,0},{3,1},{4,6},{5,7},{6,4},{7,5},{8,10},{9,11},{10,... | collective-permute-start | bytes 884744 | tf_op jit(solution)/shard_map/ppermute | solution.py:667
  79.1 9.6 %collective-permute-done.10.in_got = bf16[192,768]{1,0:T(8,128)(2,1)S(1)} collective-permute-done((bf16[192,768]{1,0:T(8,128)(2,1)}, bf16[192,768]{1,0:T(8,128)(2,1)S(1)}, u32[]{:S(2)}, u32[]{:S(2)}) %collective-permute-start.10) | collective-permute-done | bytes 294944 | tf_op jit(solution)/shard_map/ppermute | solution.py:667
  88.7 2.3 %copy-done.2 = bf16[3072,768]{1,0:T(8,128)(2,1)S(1)} copy-done((bf16[3072,768]{1,0:T(8,128)(2,1)S(1)}, bf16[3072,768]{1,0:T(8,128)(2,1)}, u32[]{:S(2)}) %copy-start.2) | copy-done | bytes 4718616
  91.1 4.0 %weight_grads_near_side.1 = (f32[192,768]{1,0:T(8,128)S(1)}, f32[192,768]{1,0:T(8,128)S(1)}) custom-call(s32[6]{0:T(128)S(1)} %pad_add_fusion.which, bf16[3072,768]{1,0:T(8,128)(2,1)S(1)} %copy-done.2, bf16[3072,768]{1,0:T(8,128)(2,1)} %weight_out.5, f32[768]{0:T(1024)S(1)} %copy-done.20, bf16[4,128,768]{2,1,0:T(8,128)(2,1)S(1)} %all-to-all-done.norm, ...), custom_call_target="tpu_custom_call" | custom-call | tf_op jit(solution)/shard_map/weight_grads_near_side/pallas_call | solution.py:637
  95.1 0.8 copy-done.12
  95.9 2.9 %collective-permute-start.11 = (bf16[8,48,384]{2,1,0:T(8,128)(2,1)S(1)}, bf16[8,48,384]{2,1,0:T(8,128)(2,1)S(1)}, u32[]{:S(2)}, u32[]{:S(2)}) collective-permute-start(bf16[8,48,384]{2,1,0:T(8,128)(2,1)S(1)} %all-to-all-done.2.own), channel_id=1, source_target_pairs={{0,1},{1,0},{2,3},{3,2},{4,5},{5,4},{6,7},{7,6},{8,9},{9,8},{10,11... | collective-permute-start | bytes 884744 | tf_op jit(solution)/shard_map/ppermute | solution.py:719
  98.8 1.1 %copy-done.13 = f32[192,768]{1,0:T(8,128)S(1)} copy-done((f32[192,768]{1,0:T(8,128)S(1)}, f32[192,768]{1,0:T(8,128)}, u32[]{:S(2)}) %copy-start.13) | copy-done | bytes 589848
  99.9 2.1 %weight_grads_sum.1 = (f32[192,768]{1,0:T(8,128)}, f32[192,768]{1,0:T(8,128)}) custom-call(f32[192,768]{1,0:T(8,128)S(1)} %get-tuple-element.86.in_kept, f32[192,768]{1,0:T(8,128)S(1)} %copy-done.13, bf16[192,768]{1,0:T(8,128)(2,1)S(1)} %collective-permute-done.10.in_got, bf16[192,768]{1,0:T(8,128)(2,1)} %collective-permute-done.12.out_got), custom_call_target="tpu_custom_call" | custom-call | tf_op jit(solution)/shard_map/weight_grads_sum/pallas_call | solution.py:735
  101.9 1.1 %kernel_grad_unpack.1 = (f32[343,768]{1,0:T(8,128)}, f32[768]{0:T(1024)}, f32[768]{0:T(1024)}, f32[768]{0:T(1024)}) custom-call(s32[1]{0:T(128)} %bitcast.core, bf16[8,48,384]{2,1,0:T(8,128)(2,1)S(1)} %all-to-all-done.2.own, bf16[8,48,384]{2,1,0:T(8,128)(2,1)S(1)} %collective-permute-done.11.other), custom_call_target="tpu_custom_call" | custom-call | tf_op jit(solution)/shard_map/kernel_grad_unpack/pallas_call | solution.py:720
  (50 shorter events, 0.2 us)
Async XLA Ops:
  0.6 12.6 %collective-permute-start.3 = (bf16[128,768]{1,0:T(8,128)(2,1)}, bf16[128,768]{1,0:T(8,128)(2,1)S(1)}, u32[]{:S(2)}, u32[]{:S(2)}) collective-permute-start(bf16[128,768]{1,0:T(8,128)(2,1)} %bitcast.15), channel_id=1, source_target_pairs={{0,12},{1,13},{2,14},{3,15},{4,0},{5,1},{6,2},{7,3},{8,4},{9,5},{1... | collective-permute-start | bytes 589832 | tf_op jit(solution)/shard_map/ppermute | solution.py:471
  4.8 9.1 %collective-permute-start.2 = (bf16[128,768]{1,0:T(8,128)(2,1)}, bf16[128,768]{1,0:T(8,128)(2,1)}, u32[]{:S(2)}, u32[]{:S(2)}) collective-permute-start(bf16[128,768]{1,0:T(8,128)(2,1)} %bitcast.16), channel_id=1, source_target_pairs={{0,4},{1,5},{2,6},{3,7},{4,8},{5,9},{6,10},{7,11},{8,12},{9,13},{1... | collective-permute-start | bytes 589832 | tf_op jit(solution)/shard_map/ppermute | solution.py:471
  4.8 10.4 %collective-permute-start.1 = (bf16[128,768]{1,0:T(8,128)(2,1)}, bf16[128,768]{1,0:T(8,128)(2,1)S(1)}, u32[]{:S(2)}, u32[]{:S(2)}) collective-permute-start(bf16[128,768]{1,0:T(8,128)(2,1)} %bitcast.9), channel_id=1, source_target_pairs={{1,2},{3,4},{5,6},{7,8},{9,10},{11,12},{13,14},{2,1},{4,3},{6,5},{... | collective-permute-start | bytes 589832 | tf_op jit(solution)/shard_map/ppermute | solution.py:444
  8.8 6.4 %collective-permute-start = (bf16[128,768]{1,0:T(8,128)(2,1)}, bf16[128,768]{1,0:T(8,128)(2,1)S(1)}, u32[]{:S(2)}, u32[]{:S(2)}) collective-permute-start(bf16[128,768]{1,0:T(8,128)(2,1)} %bitcast.10), channel_id=1, source_target_pairs={{0,1},{1,0},{2,3},{3,2},{4,5},{5,4},{6,7},{7,6},{8,9},{9,8},{10,11... | collective-permute-start | bytes 589832 | tf_op jit(solution)/shard_map/ppermute | solution.py:443
  8.9 1.2 %copy-start.3 = (f32[343,768]{1,0:T(8,128)S(1)}, f32[343,768]{1,0:T(8,128)}, u32[]{:S(2)}) copy-start(f32[343,768]{1,0:T(8,128)} %taps.3) | copy-start | bytes 3161092
  10.1 0.9 copy-start.5
  13.2 0.7 copy-start.18
  14.0 7.3 %collective-permute-start.4 = (bf16[128,768]{1,0:T(8,128)(2,1)}, bf16[128,768]{1,0:T(8,128)(2,1)S(1)}, u32[]{:S(2)}, u32[]{:S(2)}) collective-permute-start(bf16[128,768]{1,0:T(8,128)(2,1)} %collective-permute-done.2.rest_1_), channel_id=1, source_target_pairs={{0,4},{1,5},{2,6},{3,7},{4,8},{5,9},{6,10},{7,11},{8,12},{9,13},{1... | collective-permute-start | bytes 589832 | tf_op jit(solution)/shard_map/ppermute | solution.py:471
  15.2 0.7 copy-start.21
  15.9 0.7 copy-start.23
  16.6 8.4 %copy-start.6 = (bf16[4,4,8,768]{3,2,1,0:T(8,128)(2,1)S(1)}, bf16[4,4,8,768]{3,2,1,0:T(8,128)(2,1)}, u32[]{:S(2)}) copy-start(bf16[4,4,8,768]{3,2,1,0:T(8,128)(2,1)} %param.8) | copy-start | bytes 589828
  16.6 8.4 %copy-start.10 = (bf16[4,4,8,768]{3,2,1,0:T(8,128)(2,1)S(1)}, bf16[4,4,8,768]{3,2,1,0:T(8,128)(2,1)}, u32[]{:S(2)}) copy-start(bf16[4,4,8,768]{3,2,1,0:T(8,128)(2,1)} %param.15) | copy-start | bytes 589828
  16.6 8.4 %copy-start.19 = (bf16[128,768]{1,0:T(8,128)(2,1)S(1)}, bf16[128,768]{1,0:T(8,128)(2,1)}, u32[]{:S(2)}) copy-start(bf16[128,768]{1,0:T(8,128)(2,1)} %copy-done.18) | copy-start | bytes 589828
  16.6 8.4 %copy-start.20 = (f32[768]{0:T(1024)S(1)}, f32[768]{0:T(1024)}, u32[]{:S(2)}) copy-start(f32[768]{0:T(1024)} %scale.3) | copy-start | bytes 9220
  16.6 8.4 %copy-start.22 = (f32[768]{0:T(1024)S(1)}, f32[768]{0:T(1024)}, u32[]{:S(2)}) copy-start(f32[768]{0:T(1024)} %norm_gain.1) | copy-start | bytes 9220
  21.3 23.2 %all-to-all-start = ((bf16[4,128,768]{2,1,0:T(8,128)(2,1)}), bf16[4,128,768]{2,1,0:T(8,128)(2,1)S(1)}, u32[]{:S(2)}, u32[]{:S(2)}) async-start(bf16[4,128,768]{2,1,0:T(8,128)(2,1)} %get-tuple-element.55.normed), calls=%async_computation | async-start | bytes 1572864 | tf_op jit(solution)/shard_map/all_to_all | solution.py:530
  25.0 2.3 %copy-start = (bf16[3072,768]{1,0:T(8,128)(2,1)S(1)}, bf16[3072,768]{1,0:T(8,128)(2,1)}, u32[]{:S(2)}) copy-start(bf16[3072,768]{1,0:T(8,128)(2,1)} %weight_in.5) | copy-start | bytes 14155780
  42.2 0.7 copy-start.8
  42.9 0.7 copy-start.14
  44.5 2.7 %collective-permute-start.5 = (bf16[384,384]{1,0:T(8,128)(2,1)S(1)}, bf16[384,384]{1,0:T(8,128)(2,1)S(1)}, u32[]{:S(2)}, u32[]{:S(2)}) collective-permute-start(bf16[384,384]{1,0:T(8,128)(2,1)S(1)} %get-tuple-element.64), channel_id=1, source_target_pairs={{0,1},{1,0},{2,3},{3,2},{4,5},{5,4},{6,7},{7,6},{8,9},{9,8},{10,11... | collective-permute-start | bytes 884744 | tf_op jit(solution)/shard_map/ppermute | solution.py:608
  46.0 14.2 %collective-permute-start.7 = (bf16[4,128,768]{2,1,0:T(8,128)(2,1)S(1)}, bf16[4,128,768]{2,1,0:T(8,128)(2,1)S(1)}, u32[]{:S(2)}, u32[]{:S(2)}) collective-permute-start(bf16[4,128,768]{2,1,0:T(8,128)(2,1)S(1)} %get-tuple-element.68.cot), channel_id=1, source_target_pairs={{0,1},{1,0},{2,3},{3,2},{4,5},{5,4},{6,7},{7,6},{8,9},{9,8},{10,11... | collective-permute-start | bytes 2359304 | tf_op jit(solution)/shard_map/ppermute | solution.py:632
  46.0 14.2 %collective-permute-start.6 = (bf16[4,128,768]{2,1,0:T(8,128)(2,1)S(1)}, bf16[4,128,768]{2,1,0:T(8,128)(2,1)}, u32[]{:S(2)}, u32[]{:S(2)}) collective-permute-start(bf16[4,128,768]{2,1,0:T(8,128)(2,1)S(1)} %all-to-all-done.norm), channel_id=1, source_target_pairs={{0,1},{1,0},{2,3},{3,2},{4,5},{5,4},{6,7},{7,6},{8,9},{9,8},{10,11... | collective-permute-start | bytes 2359304 | tf_op jit(solution)/shard_map/ppermute | solution.py:631
  47.2 0.7 copy-start.16
  47.9 1.0 copy-start.15
  48.9 1.0 copy-start.17
  49.8 17.5 %copy-start.4 = (f32[343,768]{1,0:T(8,128)S(1)}, f32[343,768]{1,0:T(8,128)}, u32[]{:S(2)}) copy-start(f32[343,768]{1,0:T(8,128)} %taps.3) | copy-start | bytes 3161092
  49.9 0.7 copy-start.7
  50.6 21.0 %all-to-all-start.1 = ((bf16[8,48,384]{2,1,0:T(8,128)(2,1)}), bf16[8,48,384]{2,1,0:T(8,128)(2,1)}, u32[]{:S(2)}, u32[]{:S(2)}) async-start(bf16[8,48,384]{2,1,0:T(8,128)(2,1)} %bitcast.14), calls=%async_computation.1 | async-start | bytes 589824 | tf_op jit(solution)/shard_map/all_to_all | solution.py:669
  55.9 10.6 %collective-permute-start.9 = (bf16[128,768]{1,0:T(8,128)(2,1)}, bf16[128,768]{1,0:T(8,128)(2,1)S(1)}, u32[]{:S(2)}, u32[]{:S(2)}) collective-permute-start(bf16[128,768]{1,0:T(8,128)(2,1)} %copy-done.8), channel_id=1, source_target_pairs={{1,2},{3,4},{5,6},{7,8},{9,10},{11,12},{13,14},{2,1},{4,3},{6,5},{... | collective-permute-start | bytes 589832 | tf_op jit(solution)/shard_map/ppermute | solution.py:444
  60.1 6.5 %collective-permute-start.8 = (bf16[128,768]{1,0:T(8,128)(2,1)}, bf16[128,768]{1,0:T(8,128)(2,1)S(1)}, u32[]{:S(2)}, u32[]{:S(2)}) collective-permute-start(bf16[128,768]{1,0:T(8,128)(2,1)} %copy-done.8), channel_id=1, source_target_pairs={{0,1},{1,0},{2,3},{3,2},{4,5},{5,4},{6,7},{7,6},{8,9},{9,8},{10,11... | collective-permute-start | bytes 589832 | tf_op jit(solution)/shard_map/ppermute | solution.py:443
  60.2 2.3 %copy-start.1 = (bf16[3072,768]{1,0:T(8,128)(2,1)S(1)}, bf16[3072,768]{1,0:T(8,128)(2,1)}, u32[]{:S(2)}) copy-start(bf16[3072,768]{1,0:T(8,128)(2,1)} %weight_in.5) | copy-start | bytes 14155780
  62.5 4.8 %copy-start.9 = (bf16[128,768]{1,0:T(8,128)(2,1)S(1)}, bf16[128,768]{1,0:T(8,128)(2,1)}, u32[]{:S(2)}) copy-start(bf16[128,768]{1,0:T(8,128)(2,1)} %copy-done.8) | copy-start | bytes 589828
  62.5 4.8 %copy-start.11 = (bf16[4,4,8,768]{3,2,1,0:T(8,128)(2,1)S(1)}, bf16[4,4,8,768]{3,2,1,0:T(8,128)(2,1)}, u32[]{:S(2)}) copy-start(bf16[4,4,8,768]{3,2,1,0:T(8,128)(2,1)} %param.15) | copy-start | bytes 589828
  66.5 0.7 copy-start.24
  66.5 0.8 copy-start.25
  73.3 22.5 %all-to-all-start.2 = ((bf16[8,48,384]{2,1,0:T(8,128)(2,1)}), bf16[8,48,384]{2,1,0:T(8,128)(2,1)S(1)}, u32[]{:S(2)}, u32[]{:S(2)}) async-start(bf16[8,48,384]{2,1,0:T(8,128)(2,1)} %kernel_grad_sum.1), calls=%async_computation.2 | async-start | bytes 589824 | tf_op jit(solution)/shard_map/all_to_all | solution.py:713
  77.6 11.1 %collective-permute-start.10 = (bf16[192,768]{1,0:T(8,128)(2,1)}, bf16[192,768]{1,0:T(8,128)(2,1)S(1)}, u32[]{:S(2)}, u32[]{:S(2)}) collective-permute-start(bf16[192,768]{1,0:T(8,128)(2,1)} %copy-done.25), channel_id=1, source_target_pairs={{0,2},{1,3},{2,0},{3,1},{4,6},{5,7},{6,4},{7,5},{8,10},{9,11},{10,... | collective-permute-start | bytes 884744 | tf_op jit(solution)/shard_map/ppermute | solution.py:667
  79.1 19.7 %collective-permute-start.12 = (bf16[192,768]{1,0:T(8,128)(2,1)}, bf16[192,768]{1,0:T(8,128)(2,1)}, u32[]{:S(2)}, u32[]{:S(2)}) collective-permute-start(bf16[192,768]{1,0:T(8,128)(2,1)} %copy-done.24), channel_id=1, source_target_pairs={{0,2},{1,3},{2,0},{3,1},{4,6},{5,7},{6,4},{7,5},{8,10},{9,11},{10,... | collective-permute-start | bytes 884744 | tf_op jit(solution)/shard_map/ppermute | solution.py:668
  88.7 2.3 %copy-start.2 = (bf16[3072,768]{1,0:T(8,128)(2,1)S(1)}, bf16[3072,768]{1,0:T(8,128)(2,1)}, u32[]{:S(2)}) copy-start(bf16[3072,768]{1,0:T(8,128)(2,1)} %weight_in.5) | copy-start | bytes 14155780
  95.1 0.8 copy-start.12
  95.9 6.0 %collective-permute-start.11 = (bf16[8,48,384]{2,1,0:T(8,128)(2,1)S(1)}, bf16[8,48,384]{2,1,0:T(8,128)(2,1)S(1)}, u32[]{:S(2)}, u32[]{:S(2)}) collective-permute-start(bf16[8,48,384]{2,1,0:T(8,128)(2,1)S(1)} %all-to-all-done.2.own), channel_id=1, source_target_pairs={{0,1},{1,0},{2,3},{3,2},{4,5},{5,4},{6,7},{7,6},{8,9},{9,8},{10,11... | collective-permute-start | bytes 884744 | tf_op jit(solution)/shard_map/ppermute | solution.py:719
  98.8 1.1 %copy-start.13 = (f32[192,768]{1,0:T(8,128)S(1)}, f32[192,768]{1,0:T(8,128)}, u32[]{:S(2)}) copy-start(f32[192,768]{1,0:T(8,128)} %copy-done.12) | copy-start | bytes 1769476

commit v14 on v13

--- a/solution.py
+++ b/solution.py
@@ -218,7 +218,7 @@
 
 
 def input_grad_kernel(
-    planes, height, core, inner, own, outer, taps, cotangent, out, spread, split
+    planes, height, core, inner, own, outer, taps, cotangent, out, token, spread, split
 ):
     @pl.when(pl.program_id(0) == 0)
     def _():
@@ -229,6 +229,7 @@
 
     by_core(core, inner, outer, stage)
     stage_taps(taps, split)
+    token[...] = jnp.zeros(token.shape, F32)
     rows = convolve(spread, split, planes, range(2 * MARGIN + planes), True)
     for x in range(planes):
         at = x * height * SUB
@@ -238,8 +239,26 @@
 
 
 def kernel_grad_kernel(
-    planes, height, which, inner, own, outer, grads, small, sent, kept, spread, products, joined, flat
+    planes,
+    height,
+    which,
+    inner,
+    own,
+    outer,
+    grads,
+    small,
+    sent,
+    kept,
+    passed,
+    token,
+    spread,
+    products,
+    joined,
+    flat,
 ):
+    passed[...] = grads[...]
+    token[...] = jnp.zeros(token.shape, F32)
+
     @pl.when(pl.program_id(0) == 0)
     def _():
         clear_rims(spread)
@@ -381,11 +400,13 @@
 def one_side_kernel(
     which, weight_in, weight_out, scale, norm, cot, other_norm, other_cot, *rest
 ):
-    *outs, aligned, mixed_grad = rest
+    in_out, out_out, *token, aligned, mixed_grad = rest
     sets = ((norm, cot), (other_norm, other_cot))
     terms = weight_grad_terms(which, weight_in, weight_out, scale, sets, aligned, mixed_grad)
-    for k, out in enumerate(outs):
-        out[...] = terms[k].astype(out.dtype)
+    in_out[...] = terms[0].astype(in_out.dtype)
+    out_out[...] = terms[1].astype(out_out.dtype)
+    for line in token:
+        line[...] = jnp.zeros(line.shape, F32)
 
 
 def last_sum_kernel(in_kept, out_kept, in_got, out_got, in_grad, out_grad):
@@ -424,8 +445,19 @@
     by_core(core, own, other, lambda outer, inner: unpack(inner, outer))
 
 
-def params(limit=44):
+def params(limit=48):
     return pltpu.CompilerParams(vmem_limit_bytes=limit * 1024 * 1024)
+
+
+def follow(kernel, scalars, inputs, count):
+    def body(*refs):
+        head = refs[: scalars + inputs]
+        return kernel(*head, *refs[scalars + inputs + count :])
+
+    return body
+
+
+IN_PLACE = pl.BlockSpec(memory_space=pl.ANY)
 
 
 def lane_block(rows):
@@ -493,13 +525,10 @@
         name="own_conv",
     )(own, dw_kernel)
 
-    partial, upstream_line[1], upstream_line[-1] = lax.optimization_barrier(
-        (partial, upstream_line[1], upstream_line[-1])
-    )
     for k in range(2, line - 1):
         upstream_line[k] = along_line(upstream_line[k - 1], 1)
     normed, centered = pl.pallas_call(
-        functools.partial(rim_conv_kernel, planes, height),
+        follow(functools.partial(rim_conv_kernel, planes, height), 1, 6, 2),
         grid_spec=pltpu.PrefetchScalarGridSpec(
             num_scalar_prefetch=1,
             grid=(tiles,),
@@ -510,6 +539,8 @@
                 lane_block(rows),
                 whole_block(channels),
                 whole_block(channels),
+                IN_PLACE,
+                IN_PLACE,
             ],
             out_specs=[
                 whole_block(line, rows, channels),
@@ -524,7 +555,17 @@
         compiler_params=params(),
         cost_estimate=NO_COST,
         name="rim_conv",
-    )(parity, inner, outer, split, partial, norm_gain, norm_bias)
+    )(
+        parity,
+        inner,
+        outer,
+        split,
+        partial,
+        norm_gain,
+        norm_bias,
+        upstream_line[1],
+        upstream_line[-1],
+    )
 
     normed, upstream_line[2] = lax.optimization_barrier((normed, upstream_line[2]))
     gathered = lax.all_to_all(
@@ -581,7 +622,7 @@
 
         return pl.BlockSpec((block_rows, LANES), at)
 
-    half_sent, half_kept = pl.pallas_call(
+    half_sent, half_kept, conv_grad, token = pl.pallas_call(
         functools.partial(kernel_grad_kernel, planes, height),
         grid_spec=pltpu.PrefetchScalarGridSpec(
             num_scalar_prefetch=1,
@@ -590,6 +631,8 @@
             out_specs=[
                 pl.BlockSpec((padded, LANES), lambda c, w: (0, jnp.minimum(c, half_tiles - 1))),
                 pl.BlockSpec((padded, LANES), lambda c, w: (0, jnp.maximum(c - half_tiles, 0))),
+                tile_of(rows),
+                whole_block(SUB, LANES),
             ],
             scratch_shapes=[
                 spread_of(2 * MARGIN + planes),
@@ -598,25 +641,29 @@
                 pltpu.VMEM((padded, LANES), F32),
             ],
         ),
-        out_shape=[jax.ShapeDtypeStruct((padded, wide), BF16)] * 2,
+        out_shape=[jax.ShapeDtypeStruct((padded, wide), BF16)] * 2
+        + [
+            jax.ShapeDtypeStruct((rows, channels), BF16),
+            jax.ShapeDtypeStruct((SUB, LANES), F32),
+        ],
         compiler_params=params(),
         cost_estimate=NO_COST,
         name="kernel_grad_terms",
     )(jnp.stack([core, 1 - core]), inner, own, outer, conv_grad, small)
 
-    half_sent, conv_grad, gathered = lax.optimization_barrier((half_sent, conv_grad, gathered))
     half_got = lax.ppermute(half_sent, "row", other_core)
+    gathered, token = lax.optimization_barrier((gathered, token))
     grad_inner, grad_outer = rims(conv_grad)
     sums = pl.pallas_call(
-        chip_sum_kernel,
-        in_specs=[whole_block(padded, wide)] * 2,
+        follow(chip_sum_kernel, 0, 2, 1),
+        in_specs=[whole_block(padded, wide)] * 2 + [IN_PLACE],
         out_specs=whole_block(padded, wide),
         out_shape=jax.ShapeDtypeStruct((padded, wide), BF16),
         grid=(1,),
         compiler_params=params(),
         cost_estimate=NO_COST,
         name="kernel_grad_chip_sum",
-    )(half_kept, half_got)
+    )(half_kept, half_got, token)
 
     share = units // count
     tokens = line * rows
@@ -632,19 +679,21 @@
     other_cotangents = lax.ppermute(cotangents, "row", other_core)
     single = (share, channels)
 
-    def side_terms(number, dtype, name):
+    def side_terms(number, dtype, after, token, name):
         chunk = pl.BlockSpec((share, channels), lambda _, w: (w[number], 0))
         return pl.pallas_call(
-            one_side_kernel,
+            follow(one_side_kernel, 1, 7, 1),
             grid_spec=pltpu.PrefetchScalarGridSpec(
                 num_scalar_prefetch=1,
                 grid=(1,),
                 in_specs=[chunk, chunk, whole_block(channels)]
-                + [whole_block(line, rows, channels)] * 4,
-                out_specs=[whole_block(*single)] * 2,
+                + [whole_block(line, rows, channels)] * 4
+                + [IN_PLACE],
+                out_specs=[whole_block(*single)] * 2 + [whole_block(SUB, LANES)] * token,
                 scratch_shapes=[pltpu.VMEM((2 * tokens, channels), BF16)] * 2,
             ),
-            out_shape=[jax.ShapeDtypeStruct(single, dtype)] * 2,
+            out_shape=[jax.ShapeDtypeStruct(single, dtype)] * 2
+            + [jax.ShapeDtypeStruct((SUB, LANES), F32)] * token,
             compiler_params=params(),
             cost_estimate=NO_COST,
             name=name,
@@ -657,13 +706,10 @@
             cotangents,
             other_gathered,
             other_cotangents,
+            after,
         )
 
-    which, sums = lax.optimization_barrier((which, sums))
-    in_sent, out_sent = side_terms(0, BF16, "weight_grads_far_side")
-    in_sent, conv_own, grad_inner, grad_outer = lax.optimization_barrier(
-        (in_sent, conv_grad, grad_inner, grad_outer)
-    )
+    in_sent, out_sent = side_terms(0, BF16, sums, 0, "weight_grads_far_side")
     in_got = lax.ppermute(in_sent, "row", other_side)
     out_got = lax.ppermute(out_sent, "row", other_side)
     scattered = lax.all_to_all(
@@ -674,8 +720,8 @@
         tiled=True,
         axis_index_groups=alike,
     )
-    voxel_grad = pl.pallas_call(
-        functools.partial(input_grad_kernel, planes, height),
+    voxel_grad, token = pl.pallas_call(
+        follow(functools.partial(input_grad_kernel, planes, height), 1, 5, 1),
         grid_spec=pltpu.PrefetchScalarGridSpec(
             num_scalar_prefetch=1,
             grid=(tiles,),
@@ -685,44 +731,45 @@
                 lane_block(rows),
                 lane_block(TAP_ROWS),
                 lane_block(rows),
+                IN_PLACE,
             ],
-            out_specs=lane_block(rows),
+            out_specs=[lane_block(rows), whole_block(SUB, LANES)],
             scratch_shapes=[
                 spread_of(2 * MARGIN + planes),
                 pltpu.VMEM((9, KS, SUB, LANES), F32),
             ],
         ),
-        out_shape=jax.ShapeDtypeStruct((rows, channels), BF16),
+        out_shape=[
+            jax.ShapeDtypeStruct((rows, channels), BF16),
+            jax.ShapeDtypeStruct((SUB, LANES), F32),
+        ],
         compiler_params=params(),
         cost_estimate=NO_COST,
         name="input_grad_conv",
-    )(parity, grad_inner, conv_own, grad_outer, dw_kernel, upstream)
-
-    scattered, voxel_grad = lax.optimization_barrier((scattered, voxel_grad))
+    )(parity, grad_inner, conv_grad, grad_outer, dw_kernel, upstream, in_sent)
+
     copies = pl.pallas_call(
-        spread_sum_kernel,
-        in_specs=[whole_block(half, piece, wide)],
+        follow(spread_sum_kernel, 0, 1, 2),
+        in_specs=[whole_block(half, piece, wide), IN_PLACE, IN_PLACE],
         out_specs=whole_block(half, piece, wide),
         out_shape=jax.ShapeDtypeStruct((half, piece, wide), BF16),
         grid=(1,),
         compiler_params=params(),
         cost_estimate=NO_COST,
         name="kernel_grad_sum",
-    )(scattered)
-    which, copies = lax.optimization_barrier((which, copies))
+    )(scattered, token, in_got)
     totals = lax.all_to_all(
         copies, "row", split_axis=0, concat_axis=0, tiled=True, axis_index_groups=alike
     )
-    which, in_got = lax.optimization_barrier((which, in_got))
-    in_kept, out_kept = side_terms(1, F32, "weight_grads_near_side")
-    totals, in_kept = lax.optimization_barrier((totals, in_kept))
+    in_kept, out_kept, token = side_terms(1, F32, copies, 1, "weight_grads_near_side")
+    totals, token = lax.optimization_barrier((totals, token))
     other_totals = lax.ppermute(totals, "row", other_core)
     kernel_grad, *vector_grads = pl.pallas_call(
-        unpack_kernel,
+        follow(unpack_kernel, 1, 2, 1),
         grid_spec=pltpu.PrefetchScalarGridSpec(
             num_scalar_prefetch=1,
             grid=(1,),
-            in_specs=[whole_block(half, piece, wide)] * 2,
+            in_specs=[whole_block(half, piece, wide)] * 2 + [IN_PLACE],
             out_specs=[whole_block(TAP_ROWS, channels)] + [whole_block(channels)] * 3,
         ),
         out_shape=[jax.ShapeDtypeStruct((TAP_ROWS, channels), F32)]
@@ -730,7 +777,7 @@
         compiler_params=params(),
         cost_estimate=NO_COST,
         name="kernel_grad_unpack",
-    )(parity, totals, other_totals)
+    )(parity, totals, other_totals, token)
 
     weight_in_grad, weight_out_grad = pl.pallas_call(
         last_sum_kernel,

time: 104 us -> 102 us (0.981)
  the two profiles are of different devices: /device:TPU:1 before, /device:TPU:0 now
where the time goes in v14:
time: 102 us; the launch traced here: 101 us
  Pallas kernels  41.6 us (41%)
  starting transfers between devices  34.4 us (34%)
  waiting for transfers between devices  15.7 us (15%)
  local copies, waits for them, and re-layouts  8.69 us (9%)
    all_to_all x1, starting transfers between devices, on_device(): lax.all_to_all(copies, 'row', split_axis=0, concat_axis=0, tiled=True, ax...  10.2 us
    pallas_call x1, Pallas kernels, on_device(): pl.pallas_call(mlp_kernel, grid=(units // block,), in_specs=[pl.BlockSpec...  9.43 us
    unnamed x36, local copies, waits for them, and re-layouts  8.69 us
    pallas_call x2, Pallas kernels, side_terms(): pl.pallas_call(follow(one_side_kernel, 1, 7, 1), grid_spec=pltpu.Prefetch...  8.19 us
    pallas_call x1, Pallas kernels, on_device(): pl.pallas_call(functools.partial(kernel_grad_kernel, planes, height), gri...  6.34 us
    ppermute x3, starting transfers between devices, along_line(): lax.ppermute(cells, 'row', [(i, (i + quad * steps) % count) for i in rang...  5.68 us
    all_to_all x1, starting transfers between devices, on_device(): lax.all_to_all(sums.reshape(half, piece, wide), 'row', split_axis=0, conc...  4.75 us
    ppermute x2, starting transfers between devices, rims(): lax.ppermute(cells, 'row', [(i, i ^ 1) for i in range(count)])  4.37 us
  transfers between devices with their start and end apart: 16, of which 8 were waited for; matrix products, arithmetic and copies ran while one was open for 0% of the time, Pallas kernels for 37%

profile of v14, /device:TPU:0, one launch (start us, length us, event | category | flops | bytes accessed | tf_op | source)
XLA Modules:
  0.0 101.3 jit_solution(14533650786279586806)
XLA Ops:
  0.6 3.1 %collective-permute-start.2 = (bf16[128,768]{1,0:T(8,128)(2,1)}, bf16[128,768]{1,0:T(8,128)(2,1)S(1)}, u32[]{:S(2)}, u32[]{:S(2)}) collective-permute-start(bf16[128,768]{1,0:T(8,128)(2,1)} %bitcast.14), channel_id=1, source_target_pairs={{0,4},{1,5},{2,6},{3,7},{4,8},{5,9},{6,10},{7,11},{8,12},{9,13},{1... | collective-permute-start | bytes 589832 | tf_op jit(solution)/shard_map/ppermute | solution.py:503
  3.7 0.7 collective-permute-start.1
  4.4 2.9 %collective-permute-start = (bf16[128,768]{1,0:T(8,128)(2,1)}, bf16[128,768]{1,0:T(8,128)(2,1)S(1)}, u32[]{:S(2)}, u32[]{:S(2)}) collective-permute-start(bf16[128,768]{1,0:T(8,128)(2,1)} %bitcast.10), channel_id=1, source_target_pairs={{0,1},{1,0},{2,3},{3,2},{4,5},{5,4},{6,7},{7,6},{8,9},{9,8},{10,11... | collective-permute-start | bytes 589832 | tf_op jit(solution)/shard_map/ppermute | solution.py:475
  7.3 2.6 %collective-permute-start.3 = (bf16[128,768]{1,0:T(8,128)(2,1)}, bf16[128,768]{1,0:T(8,128)(2,1)S(1)}, u32[]{:S(2)}, u32[]{:S(2)}) collective-permute-start(bf16[128,768]{1,0:T(8,128)(2,1)} %bitcast.15), channel_id=1, source_target_pairs={{0,12},{1,13},{2,14},{3,15},{4,0},{5,1},{6,2},{7,3},{8,4},{9,5},{1... | collective-permute-start | bytes 589832 | tf_op jit(solution)/shard_map/ppermute | solution.py:503
  9.9 1.0 %collective-permute-done.2.refs_7_.rest_1_ = bf16[128,768]{1,0:T(8,128)(2,1)S(1)} collective-permute-done((bf16[128,768]{1,0:T(8,128)(2,1)}, bf16[128,768]{1,0:T(8,128)(2,1)S(1)}, u32[]{:S(2)}, u32[]{:S(2)}) %collective-permute-start.2) | collective-permute-done | bytes 196640 | tf_op jit(solution)/shard_map/ppermute | solution.py:503
  11.0 1.2 %copy-done = f32[343,768]{1,0:T(8,128)S(1)} copy-done((f32[343,768]{1,0:T(8,128)S(1)}, f32[343,768]{1,0:T(8,128)}, u32[]{:S(2)}) %copy-start) | copy-done | bytes 1053720
  12.2 0.9 copy-done.2
  13.1 2.2 %own_conv.1 = (f32[128,768]{1,0:T(8,128)S(1)}, f32[6,9,7,8,128]{4,3,2,1,0:T(8,128)S(1)}) custom-call(bf16[128,768]{1,0:T(8,128)(2,1)S(1)} %bitcast.11, f32[343,768]{1,0:T(8,128)S(1)} %copy-done), custom_call_target="tpu_custom_call" | custom-call | tf_op jit(solution)/shard_map/own_conv/pallas_call | solution.py:513
  15.3 0.0 collective-permute-done.refs_1_.inner
  15.3 2.7 %collective-permute-done.3.refs_8_.rest_3_ = bf16[128,768]{1,0:T(8,128)(2,1)S(1)} collective-permute-done((bf16[128,768]{1,0:T(8,128)(2,1)}, bf16[128,768]{1,0:T(8,128)(2,1)S(1)}, u32[]{:S(2)}, u32[]{:S(2)}) %collective-permute-start.3) | collective-permute-done | bytes 196640 | tf_op jit(solution)/shard_map/ppermute | solution.py:503
  17.9 0.7 copy-done.13
  18.6 0.7 copy-done.15
  19.3 3.6 %rim_conv.1 = (bf16[4,128,768]{2,1,0:T(8,128)(2,1)}, f32[128,768]{1,0:T(8,128)S(1)}) custom-call(s32[1]{0:T(128)} %bitcast.refs_0_, bf16[128,768]{1,0:T(8,128)(2,1)S(1)} %collective-permute-done.refs_1_.inner, bf16[128,768]{1,0:T(8,128)(2,1)S(1)} %collective-permute-done.1.refs_2_.outer, f32[6,9,7,8,128]{4,3,2,1,0:T(8,128)S(1)} %get-tuple-element.39.refs_3_, ...), custom_call_target="tpu_custom_call" | custom-call | tf_op jit(solution)/shard_map/rim_conv/pallas_call | solution.py:530
  23.0 0.0 collective-permute-done.4.rest_2_
  23.0 3.5 %all-to-all-start = ((bf16[4,128,768]{2,1,0:T(8,128)(2,1)}), bf16[4,128,768]{2,1,0:T(8,128)(2,1)S(1)}, u32[]{:S(2)}, u32[]{:S(2)}) async-start(bf16[4,128,768]{2,1,0:T(8,128)(2,1)} %get-tuple-element.42.normed), calls=%async_computation | async-start | bytes 1572864 | tf_op jit(solution)/shard_map/all_to_all | solution.py:571
  26.5 0.1 pad_add_fusion.which
  26.6 9.4 %mlp_both_ways.1 = (bf16[128,768]{1,0:T(8,128)(2,1)}, bf16[128,768]{1,0:T(8,128)(2,1)S(1)}, f32[8,768]{1,0:T(8,128)S(1)}, bf16[4,128,768]{2,1,0:T(8,128)(2,1)S(1)}) custom-call(bf16[4,128,768]{2,1,0:T(8,128)(2,1)} %get-tuple-element.42.normed, bf16[3072,768]{1,0:T(8,128)(2,1)} %refs_1_.3, bf16[3072,768]{1,0:T(8,128)(2,1)} %refs_2_.3, ...), custom_call_target="tpu_custom_call" | custom-call | tf_op jit(solution)/shard_map/mlp_both_ways/pallas_call | solution.py:577
  36.0 0.0 collective-permute-start.8
  36.0 6.3 %kernel_grad_terms.1 = (bf16[384,384]{1,0:T(8,128)(2,1)S(1)}, bf16[384,384]{1,0:T(8,128)(2,1)S(1)}, bf16[128,768]{1,0:T(8,128)(2,1)S(1)}, f32[8,128]{1,0:T(8,128)S(1)}) custom-call(s32[2]{0:T(128)S(1)} %pad_add_fusion.which, bf16[128,768]{1,0:T(8,128)(2,1)S(1)} %collective-permute-done.refs_1_.inner, bf16[128,768]{1,0:T(8,128)(2,1)S(1)} %bitcast.13, ...), custom_call_target="tpu_custom_call" | custom-call | tf_op jit(solution)/shard_map/kernel_grad_terms/pallas_call | solution.py:625
  42.3 0.0 copy-start.10
  42.3 0.7 copy-done.10
  43.0 0.7 copy-done.16
  43.7 1.7 %all-to-all-done.refs_4_ = bf16[4,128,768]{2,1,0:T(8,128)(2,1)S(1)} async-done(((bf16[4,128,768]{2,1,0:T(8,128)(2,1)}), bf16[4,128,768]{2,1,0:T(8,128)(2,1)S(1)}, u32[]{:S(2)}, u32[]{:S(2)}) %all-to-all-start) | async-done | bytes 786464 | tf_op jit(solution)/shard_map/all_to_all | solution.py:571
  45.4 0.5 collective-permute-start.9
  45.9 2.2 %collective-permute-done.9.refs_1_ = bf16[384,384]{1,0:T(8,128)(2,1)} collective-permute-done((bf16[384,384]{1,0:T(8,128)(2,1)}, bf16[384,384]{1,0:T(8,128)(2,1)}, u32[]{:S(2)}, u32[]{:S(2)}) %collective-permute-start.9) | collective-permute-done | bytes 294944 | tf_op jit(solution)/shard_map/ppermute | solution.py:654
  48.1 1.7 %kernel_grad_chip_sum.1.refs_8_ = bf16[384,384]{1,0:T(8,128)(2,1)} custom-call(bf16[384,384]{1,0:T(8,128)(2,1)S(1)} %get-tuple-element.52.refs_0_, bf16[384,384]{1,0:T(8,128)(2,1)} %collective-permute-done.9.refs_1_, f32[8,128]{1,0:T(8,128)S(1)} %get-tuple-element.54.refs_2_), custom_call_target="tpu_custom_call" | custom-call | tf_op jit(solution)/shard_map/kernel_grad_chip_sum/pallas_call | solution.py:657
  49.8 4.7 %all-to-all-start.1 = ((bf16[8,48,384]{2,1,0:T(8,128)(2,1)}), bf16[8,48,384]{2,1,0:T(8,128)(2,1)}, u32[]{:S(2)}, u32[]{:S(2)}) async-start(bf16[8,48,384]{2,1,0:T(8,128)(2,1)} %bitcast.8), calls=%async_computation.1 | async-start | bytes 589824 | tf_op jit(solution)/shard_map/all_to_all | solution.py:715
  54.6 0.1 pad_add_fusion.1.refs_0_
  54.7 4.4 %weight_grads_far_side.1 = (bf16[192,768]{1,0:T(8,128)(2,1)}, bf16[192,768]{1,0:T(8,128)(2,1)S(1)}) custom-call(s32[6]{0:T(128)S(1)} %pad_add_fusion.1.refs_0_, bf16[3072,768]{1,0:T(8,128)(2,1)} %refs_1_.3, bf16[3072,768]{1,0:T(8,128)(2,1)} %refs_2_.3, f32[768]{0:T(1024)S(1)} %copy-done.12, bf16[4,128,768]{2,1,0:T(8,128)(2,1)S(1)} %all-to-all-done.refs_4_, ...), custom_call_target="tpu_custom_call" | custom-call | tf_op jit(solution)/shard_map/weight_grads_far_side/pallas_call | solution.py:684
  59.1 2.0 %collective-permute-start.10 = (bf16[192,768]{1,0:T(8,128)(2,1)}, bf16[192,768]{1,0:T(8,128)(2,1)S(1)}, u32[]{:S(2)}, u32[]{:S(2)}) collective-permute-start(bf16[192,768]{1,0:T(8,128)(2,1)} %get-tuple-element.55.refs_6_), channel_id=1, source_target_pairs={{0,2},{1,3},{2,0},{3,1},{4,6},{5,7},{6,4},{7,5},{8,10},{9,11},{10,... | collective-permute-start | bytes 884744 | tf_op jit(solution)/shard_map/ppermute | solution.py:713
  61.1 0.7 collective-permute-start.6
  61.8 1.4 %collective-permute-start.5 = (bf16[128,768]{1,0:T(8,128)(2,1)S(1)}, bf16[128,768]{1,0:T(8,128)(2,1)S(1)}, u32[]{:S(2)}, u32[]{:S(2)}) collective-permute-start(bf16[128,768]{1,0:T(8,128)(2,1)S(1)} %copy-done.11), channel_id=1, source_target_pairs={{0,1},{1,0},{2,3},{3,2},{4,5},{5,4},{6,7},{7,6},{8,9},{9,8},{10,11... | collective-permute-start | bytes 589832 | tf_op jit(solution)/shard_map/ppermute | solution.py:475
  63.2 1.1 %collective-permute-done.5.refs_1_ = bf16[128,768]{1,0:T(8,128)(2,1)S(1)} collective-permute-done((bf16[128,768]{1,0:T(8,128)(2,1)S(1)}, bf16[128,768]{1,0:T(8,128)(2,1)S(1)}, u32[]{:S(2)}, u32[]{:S(2)}) %collective-permute-start.5) | collective-permute-done | bytes 196640 | tf_op jit(solution)/shard_map/ppermute | solution.py:475
  64.3 4.3 %input_grad_conv.1 = (bf16[128,768]{1,0:T(8,128)(2,1)}, f32[8,128]{1,0:T(8,128)S(1)}) custom-call(s32[1]{0:T(128)} %bitcast.refs_0_, bf16[128,768]{1,0:T(8,128)(2,1)S(1)} %collective-permute-done.5.refs_1_, bf16[128,768]{1,0:T(8,128)(2,1)S(1)} %copy-done.11, bf16[128,768]{1,0:T(8,128)(2,1)S(1)} %collective-permute-done.6.refs_3_, f32[343,768]{1,0:T(8,128)S(1)} %copy-done.1, ...), custom_call_target="tpu_custom_call" | custom-call | tf_op jit(solution)/shard_map/input_grad_conv/pallas_call | solution.py:723
  68.6 2.6 %collective-permute-done.10.refs_2_.in_got = bf16[192,768]{1,0:T(8,128)(2,1)S(1)} collective-permute-done((bf16[192,768]{1,0:T(8,128)(2,1)}, bf16[192,768]{1,0:T(8,128)(2,1)S(1)}, u32[]{:S(2)}, u32[]{:S(2)}) %collective-permute-start.10) | collective-permute-done | bytes 294944 | tf_op jit(solution)/shard_map/ppermute | solution.py:713
  71.2 1.7 %kernel_grad_sum.1.refs_8_ = bf16[8,48,384]{2,1,0:T(8,128)(2,1)} custom-call(bf16[8,48,384]{2,1,0:T(8,128)(2,1)} %all-to-all-done.1.refs_0_, f32[8,128]{1,0:T(8,128)S(1)} %get-tuple-element.57.refs_1_, bf16[192,768]{1,0:T(8,128)(2,1)S(1)} %collective-permute-done.10.refs_2_.in_got), custom_call_target="tpu_custom_call" | custom-call | tf_op jit(solution)/shard_map/kernel_grad_sum/pallas_call | solution.py:751
  72.9 10.2 %all-to-all-start.2 = ((bf16[8,48,384]{2,1,0:T(8,128)(2,1)}), bf16[8,48,384]{2,1,0:T(8,128)(2,1)}, u32[]{:S(2)}, u32[]{:S(2)}) async-start(bf16[8,48,384]{2,1,0:T(8,128)(2,1)} %kernel_grad_sum.1.refs_8_), calls=%async_computation.2 | async-start | bytes 589824 | tf_op jit(solution)/shard_map/all_to_all | solution.py:761
  83.1 2.0 %collective-permute-start.12 = (bf16[192,768]{1,0:T(8,128)(2,1)}, bf16[192,768]{1,0:T(8,128)(2,1)}, u32[]{:S(2)}, u32[]{:S(2)}) collective-permute-start(bf16[192,768]{1,0:T(8,128)(2,1)} %copy-done.17), channel_id=1, source_target_pairs={{0,2},{1,3},{2,0},{3,1},{4,6},{5,7},{6,4},{7,5},{8,10},{9,11},{10,... | collective-permute-start | bytes 884744 | tf_op jit(solution)/shard_map/ppermute | solution.py:714
  85.2 3.8 %weight_grads_near_side.1 = (f32[192,768]{1,0:T(8,128)S(1)}, f32[192,768]{1,0:T(8,128)S(1)}, f32[8,128]{1,0:T(8,128)S(1)}) custom-call(s32[6]{0:T(128)S(1)} %pad_add_fusion.1.refs_0_, bf16[3072,768]{1,0:T(8,128)(2,1)} %refs_1_.3, bf16[3072,768]{1,0:T(8,128)(2,1)} %refs_2_.3, f32[768]{0:T(1024)S(1)} %copy-done.12, ...), custom_call_target="tpu_custom_call" | custom-call | tf_op jit(solution)/shard_map/weight_grads_near_side/pallas_call | solution.py:684
  89.0 0.0 copy-start.6
  89.0 0.8 copy-done.6
  89.8 0.8 copy-done.8
  90.6 2.3 %all-to-all-done.2.refs_1_ = bf16[8,48,384]{2,1,0:T(8,128)(2,1)} async-done(((bf16[8,48,384]{2,1,0:T(8,128)(2,1)}), bf16[8,48,384]{2,1,0:T(8,128)(2,1)}, u32[]{:S(2)}, u32[]{:S(2)}) %all-to-all-start.2) | async-done | bytes 294944 | tf_op jit(solution)/shard_map/all_to_all | solution.py:761
  92.9 2.1 %collective-permute-done.12.out_got = bf16[192,768]{1,0:T(8,128)(2,1)} collective-permute-done((bf16[192,768]{1,0:T(8,128)(2,1)}, bf16[192,768]{1,0:T(8,128)(2,1)}, u32[]{:S(2)}, u32[]{:S(2)}) %collective-permute-start.12) | collective-permute-done | bytes 294944 | tf_op jit(solution)/shard_map/ppermute | solution.py:714
  95.1 1.1 %copy-done.7 = f32[192,768]{1,0:T(8,128)S(1)} copy-done((f32[192,768]{1,0:T(8,128)S(1)}, f32[192,768]{1,0:T(8,128)}, u32[]{:S(2)}) %copy-start.7) | copy-done | bytes 589848
  96.1 1.1 %copy-done.9 = f32[192,768]{1,0:T(8,128)S(1)} copy-done((f32[192,768]{1,0:T(8,128)S(1)}, f32[192,768]{1,0:T(8,128)}, u32[]{:S(2)}) %copy-start.9) | copy-done | bytes 589848
  97.2 2.1 %weight_grads_sum.1 = (f32[192,768]{1,0:T(8,128)}, f32[192,768]{1,0:T(8,128)}) custom-call(f32[192,768]{1,0:T(8,128)S(1)} %copy-done.7, f32[192,768]{1,0:T(8,128)S(1)} %copy-done.9, bf16[192,768]{1,0:T(8,128)(2,1)S(1)} %collective-permute-done.10.refs_2_.in_got, bf16[192,768]{1,0:T(8,128)(2,1)} %collective-permute-done.12.out_got), custom_call_target="tpu_custom_call" | custom-call | tf_op jit(solution)/shard_map/weight_grads_sum/pallas_call | solution.py:782
  99.3 2.0 %kernel_grad_unpack.1 = (f32[343,768]{1,0:T(8,128)}, f32[768]{0:T(1024)}, f32[768]{0:T(1024)}, f32[768]{0:T(1024)}) custom-call(s32[1]{0:T(128)} %bitcast.refs_0_, bf16[8,48,384]{2,1,0:T(8,128)(2,1)} %all-to-all-done.2.refs_1_, bf16[8,48,384]{2,1,0:T(8,128)(2,1)S(1)} %collective-permute-done.11.refs_2_, f32[8,128]{1,0:T(8,128)S(1)} %get-tuple-element.60.refs_3_), custom_call_target="tpu_custom_call" | custom-call | tf_op jit(solution)/shard_map/kernel_grad_unpack/pallas_call | solution.py:767
  (34 shorter events, 0.1 us)
Async XLA Ops:
  0.6 10.3 %collective-permute-start.2 = (bf16[128,768]{1,0:T(8,128)(2,1)}, bf16[128,768]{1,0:T(8,128)(2,1)S(1)}, u32[]{:S(2)}, u32[]{:S(2)}) collective-permute-start(bf16[128,768]{1,0:T(8,128)(2,1)} %bitcast.14), channel_id=1, source_target_pairs={{0,4},{1,5},{2,6},{3,7},{4,8},{5,9},{6,10},{7,11},{8,12},{9,13},{1... | collective-permute-start | bytes 589832 | tf_op jit(solution)/shard_map/ppermute | solution.py:503
  3.7 11.6 %collective-permute-start.1 = (bf16[128,768]{1,0:T(8,128)(2,1)}, bf16[128,768]{1,0:T(8,128)(2,1)S(1)}, u32[]{:S(2)}, u32[]{:S(2)}) collective-permute-start(bf16[128,768]{1,0:T(8,128)(2,1)} %bitcast.9), channel_id=1, source_target_pairs={{1,2},{3,4},{5,6},{7,8},{9,10},{11,12},{13,14},{2,1},{4,3},{6,5},{... | collective-permute-start | bytes 589832 | tf_op jit(solution)/shard_map/ppermute | solution.py:476
  4.4 10.9 %collective-permute-start = (bf16[128,768]{1,0:T(8,128)(2,1)}, bf16[128,768]{1,0:T(8,128)(2,1)S(1)}, u32[]{:S(2)}, u32[]{:S(2)}) collective-permute-start(bf16[128,768]{1,0:T(8,128)(2,1)} %bitcast.10), channel_id=1, source_target_pairs={{0,1},{1,0},{2,3},{3,2},{4,5},{5,4},{6,7},{7,6},{8,9},{9,8},{10,11... | collective-permute-start | bytes 589832 | tf_op jit(solution)/shard_map/ppermute | solution.py:475
  7.3 10.6 %collective-permute-start.3 = (bf16[128,768]{1,0:T(8,128)(2,1)}, bf16[128,768]{1,0:T(8,128)(2,1)S(1)}, u32[]{:S(2)}, u32[]{:S(2)}) collective-permute-start(bf16[128,768]{1,0:T(8,128)(2,1)} %bitcast.15), channel_id=1, source_target_pairs={{0,12},{1,13},{2,14},{3,15},{4,0},{5,1},{6,2},{7,3},{8,4},{9,5},{1... | collective-permute-start | bytes 589832 | tf_op jit(solution)/shard_map/ppermute | solution.py:503
  10.9 12.0 %collective-permute-start.4 = (bf16[128,768]{1,0:T(8,128)(2,1)S(1)}, bf16[128,768]{1,0:T(8,128)(2,1)S(1)}, u32[]{:S(2)}, u32[]{:S(2)}) collective-permute-start(bf16[128,768]{1,0:T(8,128)(2,1)S(1)} %collective-permute-done.2.refs_7_.rest_1_), channel_id=1, source_target_pairs={{0,4},{1,5},{2,6},{3,7},{4,8},{5,9},{6,10},{7,11},{8,12},{9,13},{1... | collective-permute-start | bytes 589832 | tf_op jit(solution)/shard_map/ppermute | solution.py:503
  10.9 1.2 %copy-start = (f32[343,768]{1,0:T(8,128)S(1)}, f32[343,768]{1,0:T(8,128)}, u32[]{:S(2)}) copy-start(f32[343,768]{1,0:T(8,128)} %refs_4_.1) | copy-start | bytes 3161092
  12.2 0.9 copy-start.2
  17.9 0.7 copy-start.13
  18.6 0.7 copy-start.15
  19.3 7.2 %copy-start.3 = (bf16[4,4,8,768]{3,2,1,0:T(8,128)(2,1)S(1)}, bf16[4,4,8,768]{3,2,1,0:T(8,128)(2,1)}, u32[]{:S(2)}) copy-start(bf16[4,4,8,768]{3,2,1,0:T(8,128)(2,1)} %param.8) | copy-start | bytes 589828
  19.3 7.2 %copy-start.4 = (bf16[4,4,8,768]{3,2,1,0:T(8,128)(2,1)S(1)}, bf16[4,4,8,768]{3,2,1,0:T(8,128)(2,1)}, u32[]{:S(2)}) copy-start(bf16[4,4,8,768]{3,2,1,0:T(8,128)(2,1)} %param.15) | copy-start | bytes 589828
  19.3 7.2 %copy-start.12 = (f32[768]{0:T(1024)S(1)}, f32[768]{0:T(1024)}, u32[]{:S(2)}) copy-start(f32[768]{0:T(1024)} %refs_3_.3) | copy-start | bytes 9220
  19.3 7.2 %copy-start.14 = (f32[768]{0:T(1024)S(1)}, f32[768]{0:T(1024)}, u32[]{:S(2)}) copy-start(f32[768]{0:T(1024)} %norm_gain.1) | copy-start | bytes 9220
  23.0 22.5 %all-to-all-start = ((bf16[4,128,768]{2,1,0:T(8,128)(2,1)}), bf16[4,128,768]{2,1,0:T(8,128)(2,1)S(1)}, u32[]{:S(2)}, u32[]{:S(2)}) async-start(bf16[4,128,768]{2,1,0:T(8,128)(2,1)} %get-tuple-element.42.normed), calls=%async_computation | async-start | bytes 1572864 | tf_op jit(solution)/shard_map/all_to_all | solution.py:571
  36.0 18.7 %collective-permute-start.8 = (bf16[4,128,768]{2,1,0:T(8,128)(2,1)S(1)}, bf16[4,128,768]{2,1,0:T(8,128)(2,1)S(1)}, u32[]{:S(2)}, u32[]{:S(2)}) collective-permute-start(bf16[4,128,768]{2,1,0:T(8,128)(2,1)S(1)} %get-tuple-element.51.refs_5_), channel_id=1, source_target_pairs={{0,1},{1,0},{2,3},{3,2},{4,5},{5,4},{6,7},{7,6},{8,9},{9,8},{10,11... | collective-permute-start | bytes 2359304 | tf_op jit(solution)/shard_map/ppermute | solution.py:679
  42.3 0.7 copy-start.10
  43.0 0.7 copy-start.16
  45.4 9.3 %collective-permute-start.7 = (bf16[4,128,768]{2,1,0:T(8,128)(2,1)S(1)}, bf16[4,128,768]{2,1,0:T(8,128)(2,1)S(1)}, u32[]{:S(2)}, u32[]{:S(2)}) collective-permute-start(bf16[4,128,768]{2,1,0:T(8,128)(2,1)S(1)} %all-to-all-done.refs_4_), channel_id=1, source_target_pairs={{0,1},{1,0},{2,3},{3,2},{4,5},{5,4},{6,7},{7,6},{8,9},{9,8},{10,11... | collective-permute-start | bytes 2359304 | tf_op jit(solution)/shard_map/ppermute | solution.py:678
  45.4 2.7 %collective-permute-start.9 = (bf16[384,384]{1,0:T(8,128)(2,1)}, bf16[384,384]{1,0:T(8,128)(2,1)}, u32[]{:S(2)}, u32[]{:S(2)}) collective-permute-start(bf16[384,384]{1,0:T(8,128)(2,1)} %copy-done.16), channel_id=1, source_target_pairs={{0,1},{1,0},{2,3},{3,2},{4,5},{5,4},{6,7},{7,6},{8,9},{9,8},{10,11... | collective-permute-start | bytes 884744 | tf_op jit(solution)/shard_map/ppermute | solution.py:654
  49.8 18.7 %all-to-all-start.1 = ((bf16[8,48,384]{2,1,0:T(8,128)(2,1)}), bf16[8,48,384]{2,1,0:T(8,128)(2,1)}, u32[]{:S(2)}, u32[]{:S(2)}) async-start(bf16[8,48,384]{2,1,0:T(8,128)(2,1)} %bitcast.8), calls=%async_computation.1 | async-start | bytes 589824 | tf_op jit(solution)/shard_map/all_to_all | solution.py:715
  54.7 6.4 %copy-start.11 = (bf16[128,768]{1,0:T(8,128)(2,1)S(1)}, bf16[128,768]{1,0:T(8,128)(2,1)}, u32[]{:S(2)}) copy-start(bf16[128,768]{1,0:T(8,128)(2,1)} %copy-done.10) | copy-start | bytes 589828
  54.7 9.6 %copy-start.1 = (f32[343,768]{1,0:T(8,128)S(1)}, f32[343,768]{1,0:T(8,128)}, u32[]{:S(2)}) copy-start(f32[343,768]{1,0:T(8,128)} %refs_4_.1) | copy-start | bytes 3161092
  54.7 9.6 %copy-start.5 = (bf16[4,4,8,768]{3,2,1,0:T(8,128)(2,1)S(1)}, bf16[4,4,8,768]{3,2,1,0:T(8,128)(2,1)}, u32[]{:S(2)}) copy-start(bf16[4,4,8,768]{3,2,1,0:T(8,128)(2,1)} %param.15) | copy-start | bytes 589828
  59.1 5.2 %copy-start.17 = (bf16[192,768]{1,0:T(8,128)(2,1)}, bf16[192,768]{1,0:T(8,128)(2,1)S(1)}, u32[]{:S(2)}) copy-start(bf16[192,768]{1,0:T(8,128)(2,1)S(1)} %get-tuple-element.67) | copy-start | bytes 884740
  59.1 12.2 %collective-permute-start.10 = (bf16[192,768]{1,0:T(8,128)(2,1)}, bf16[192,768]{1,0:T(8,128)(2,1)S(1)}, u32[]{:S(2)}, u32[]{:S(2)}) collective-permute-start(bf16[192,768]{1,0:T(8,128)(2,1)} %get-tuple-element.55.refs_6_), channel_id=1, source_target_pairs={{0,2},{1,3},{2,0},{3,1},{4,6},{5,7},{6,4},{7,5},{8,10},{9,11},{10,... | collective-permute-start | bytes 884744 | tf_op jit(solution)/shard_map/ppermute | solution.py:713
  61.1 2.1 %collective-permute-start.6 = (bf16[128,768]{1,0:T(8,128)(2,1)S(1)}, bf16[128,768]{1,0:T(8,128)(2,1)S(1)}, u32[]{:S(2)}, u32[]{:S(2)}) collective-permute-start(bf16[128,768]{1,0:T(8,128)(2,1)S(1)} %copy-done.11), channel_id=1, source_target_pairs={{1,2},{3,4},{5,6},{7,8},{9,10},{11,12},{13,14},{2,1},{4,3},{6,5},{... | collective-permute-start | bytes 589832 | tf_op jit(solution)/shard_map/ppermute | solution.py:476
  61.8 2.5 %collective-permute-start.5 = (bf16[128,768]{1,0:T(8,128)(2,1)S(1)}, bf16[128,768]{1,0:T(8,128)(2,1)S(1)}, u32[]{:S(2)}, u32[]{:S(2)}) collective-permute-start(bf16[128,768]{1,0:T(8,128)(2,1)S(1)} %copy-done.11), channel_id=1, source_target_pairs={{0,1},{1,0},{2,3},{3,2},{4,5},{5,4},{6,7},{7,6},{8,9},{9,8},{10,11... | collective-permute-start | bytes 589832 | tf_op jit(solution)/shard_map/ppermute | solution.py:475
  72.9 20.0 %all-to-all-start.2 = ((bf16[8,48,384]{2,1,0:T(8,128)(2,1)}), bf16[8,48,384]{2,1,0:T(8,128)(2,1)}, u32[]{:S(2)}, u32[]{:S(2)}) async-start(bf16[8,48,384]{2,1,0:T(8,128)(2,1)} %kernel_grad_sum.1.refs_8_), calls=%async_computation.2 | async-start | bytes 589824 | tf_op jit(solution)/shard_map/all_to_all | solution.py:761
  83.1 11.9 %collective-permute-start.12 = (bf16[192,768]{1,0:T(8,128)(2,1)}, bf16[192,768]{1,0:T(8,128)(2,1)}, u32[]{:S(2)}, u32[]{:S(2)}) collective-permute-start(bf16[192,768]{1,0:T(8,128)(2,1)} %copy-done.17), channel_id=1, source_target_pairs={{0,2},{1,3},{2,0},{3,1},{4,6},{5,7},{6,4},{7,5},{8,10},{9,11},{10,... | collective-permute-start | bytes 884744 | tf_op jit(solution)/shard_map/ppermute | solution.py:714
  89.0 0.8 copy-start.6
  89.8 0.8 copy-start.8
  92.9 6.3 %collective-permute-start.11 = (bf16[8,48,384]{2,1,0:T(8,128)(2,1)}, bf16[8,48,384]{2,1,0:T(8,128)(2,1)S(1)}, u32[]{:S(2)}, u32[]{:S(2)}) collective-permute-start(bf16[8,48,384]{2,1,0:T(8,128)(2,1)} %all-to-all-done.2.refs_1_), channel_id=1, source_target_pairs={{0,1},{1,0},{2,3},{3,2},{4,5},{5,4},{6,7},{7,6},{8,9},{9,8},{10,11... | collective-permute-start | bytes 884744 | tf_op jit(solution)/shard_map/ppermute | solution.py:766
  95.1 1.1 %copy-start.7 = (f32[192,768]{1,0:T(8,128)S(1)}, f32[192,768]{1,0:T(8,128)}, u32[]{:S(2)}) copy-start(f32[192,768]{1,0:T(8,128)} %copy-done.6) | copy-start | bytes 1769476
  96.1 1.1 %copy-start.9 = (f32[192,768]{1,0:T(8,128)S(1)}, f32[192,768]{1,0:T(8,128)}, u32[]{:S(2)}) copy-start(f32[192,768]{1,0:T(8,128)} %copy-done.8) | copy-start | bytes 1769476

commit v15 on v14

--- a/solution.py
+++ b/solution.py
@@ -397,21 +397,34 @@
     )
 
 
-def one_side_kernel(
-    which, weight_in, weight_out, scale, norm, cot, other_norm, other_cot, *rest
+def far_side_kernel(
+    which, weight_in, weight_out, scale, norm, cot, other_norm, other_cot, sent, aligned, mixed_grad
 ):
-    in_out, out_out, *token, aligned, mixed_grad = rest
     sets = ((norm, cot), (other_norm, other_cot))
     terms = weight_grad_terms(which, weight_in, weight_out, scale, sets, aligned, mixed_grad)
-    in_out[...] = terms[0].astype(in_out.dtype)
-    out_out[...] = terms[1].astype(out_out.dtype)
-    for line in token:
-        line[...] = jnp.zeros(line.shape, F32)
-
-
-def last_sum_kernel(in_kept, out_kept, in_got, out_got, in_grad, out_grad):
-    in_grad[...] = in_kept[...] + in_got[...].astype(F32)
-    out_grad[...] = out_kept[...] + out_got[...].astype(F32)
+    for k in range(2):
+        sent[k] = terms[k].astype(BF16)
+
+
+def near_side_kernel(
+    which,
+    weight_in,
+    weight_out,
+    scale,
+    norm,
+    cot,
+    other_norm,
+    other_cot,
+    got,
+    in_grad,
+    out_grad,
+    aligned,
+    mixed_grad,
+):
+    sets = ((norm, cot), (other_norm, other_cot))
+    terms = weight_grad_terms(which, weight_in, weight_out, scale, sets, aligned, mixed_grad)
+    for k, out in enumerate((in_grad, out_grad)):
+        out[...] = terms[k] + got[k].astype(F32)
 
 
 def chip_sum_kernel(kept, got, out):
@@ -677,23 +690,22 @@
     )
     other_gathered = lax.ppermute(gathered, "row", other_core)
     other_cotangents = lax.ppermute(cotangents, "row", other_core)
-    single = (share, channels)
-
-    def side_terms(number, dtype, after, token, name):
+
+    def side_terms(kernel, number, more, after, outs, name):
         chunk = pl.BlockSpec((share, channels), lambda _, w: (w[number], 0))
         return pl.pallas_call(
-            follow(one_side_kernel, 1, 7, 1),
+            follow(kernel, 1, 7 + len(more), len(after)),
             grid_spec=pltpu.PrefetchScalarGridSpec(
                 num_scalar_prefetch=1,
                 grid=(1,),
                 in_specs=[chunk, chunk, whole_block(channels)]
                 + [whole_block(line, rows, channels)] * 4
-                + [IN_PLACE],
-                out_specs=[whole_block(*single)] * 2 + [whole_block(SUB, LANES)] * token,
+                + [whole_block(*part.shape) for part in more]
+                + [IN_PLACE] * len(after),
+                out_specs=[whole_block(*out.shape) for out in outs],
                 scratch_shapes=[pltpu.VMEM((2 * tokens, channels), BF16)] * 2,
             ),
-            out_shape=[jax.ShapeDtypeStruct(single, dtype)] * 2
-            + [jax.ShapeDtypeStruct((SUB, LANES), F32)] * token,
+            out_shape=outs,
             compiler_params=params(),
             cost_estimate=NO_COST,
             name=name,
@@ -706,12 +718,16 @@
             cotangents,
             other_gathered,
             other_cotangents,
-            after,
+            *more,
+            *after,
         )
 
-    in_sent, out_sent = side_terms(0, BF16, sums, 0, "weight_grads_far_side")
-    in_got = lax.ppermute(in_sent, "row", other_side)
-    out_got = lax.ppermute(out_sent, "row", other_side)
+    pair = jax.ShapeDtypeStruct((2, share, channels), BF16)
+    single = jax.ShapeDtypeStruct((share, channels), F32)
+    (sent,) = side_terms(
+        far_side_kernel, 0, [], [sums, grad_inner, grad_outer], [pair], "weight_grads_far_side"
+    )
+    got = lax.ppermute(sent, "row", other_side)
     scattered = lax.all_to_all(
         sums.reshape(half, piece, wide),
         "row",
@@ -746,30 +762,32 @@
         compiler_params=params(),
         cost_estimate=NO_COST,
         name="input_grad_conv",
-    )(parity, grad_inner, conv_grad, grad_outer, dw_kernel, upstream, in_sent)
+    )(parity, grad_inner, conv_grad, grad_outer, dw_kernel, upstream, sent)
 
     copies = pl.pallas_call(
-        follow(spread_sum_kernel, 0, 1, 2),
-        in_specs=[whole_block(half, piece, wide), IN_PLACE, IN_PLACE],
+        follow(spread_sum_kernel, 0, 1, 1),
+        in_specs=[whole_block(half, piece, wide), IN_PLACE],
         out_specs=whole_block(half, piece, wide),
         out_shape=jax.ShapeDtypeStruct((half, piece, wide), BF16),
         grid=(1,),
         compiler_params=params(),
         cost_estimate=NO_COST,
         name="kernel_grad_sum",
-    )(scattered, token, in_got)
+    )(scattered, token)
     totals = lax.all_to_all(
         copies, "row", split_axis=0, concat_axis=0, tiled=True, axis_index_groups=alike
     )
-    in_kept, out_kept, token = side_terms(1, F32, copies, 1, "weight_grads_near_side")
-    totals, token = lax.optimization_barrier((totals, token))
+    weight_in_grad, weight_out_grad = side_terms(
+        near_side_kernel, 1, [got], [copies], [single, single], "weight_grads_near_side"
+    )
+    totals, weight_in_grad = lax.optimization_barrier((totals, weight_in_grad))
     other_totals = lax.ppermute(totals, "row", other_core)
     kernel_grad, *vector_grads = pl.pallas_call(
-        follow(unpack_kernel, 1, 2, 1),
+        unpack_kernel,
         grid_spec=pltpu.PrefetchScalarGridSpec(
             num_scalar_prefetch=1,
             grid=(1,),
-            in_specs=[whole_block(half, piece, wide)] * 2 + [IN_PLACE],
+            in_specs=[whole_block(half, piece, wide)] * 2,
             out_specs=[whole_block(TAP_ROWS, channels)] + [whole_block(channels)] * 3,
         ),
         out_shape=[jax.ShapeDtypeStruct((TAP_ROWS, channels), F32)]
@@ -777,18 +795,7 @@
         compiler_params=params(),
         cost_estimate=NO_COST,
         name="kernel_grad_unpack",
-    )(parity, totals, other_totals, token)
-
-    weight_in_grad, weight_out_grad = pl.pallas_call(
-        last_sum_kernel,
-        grid=(1,),
-        in_specs=[whole_block(*single)] * 4,
-        out_specs=[whole_block(*single)] * 2,
-        out_shape=[jax.ShapeDtypeStruct(single, F32)] * 2,
-        compiler_params=params(),
-        cost_estimate=NO_COST,
-        name="weight_grads_sum",
-    )(in_kept, out_kept, in_got, out_got)
+    )(parity, totals, other_totals)
 
     return (
         block_out.reshape(voxels.shape),

time: 102 us -> 94.8 us (0.929)
  the two profiles are of different devices: /device:TPU:0 before, /device:TPU:19 now
where the time goes in v15:
time: 94.8 us; the launch traced here: 94.1 us
  Pallas kernels  38 us (40%)
  starting transfers between devices  32.1 us (34%)
  waiting for transfers between devices  18.2 us (19%)
  local copies, waits for them, and re-layouts  4.93 us (5%)
    pallas_call x2, Pallas kernels, side_terms(): pl.pallas_call(follow(kernel, 1, 7 + len(more), len(after)), grid_spec=pl...  9.52 us
    pallas_call x1, Pallas kernels, on_device(): pl.pallas_call(mlp_kernel, grid=(units // block,), in_specs=[pl.BlockSpec...  9.45 us
    ppermute x2, waiting for transfers between devices, rims(): lax.ppermute(cells, 'row', between + [(j, i) for i, j in between])  7.62 us
    ppermute x1, waiting for transfers between devices, on_device(): got = lax.ppermute(sent, 'row', other_side)  6.49 us
    pallas_call x1, Pallas kernels, on_device(): pl.pallas_call(functools.partial(kernel_grad_kernel, planes, height), gri...  6.35 us
    ppermute x2, starting transfers between devices, rims(): lax.ppermute(cells, 'row', between + [(j, i) for i, j in between])  5.99 us
    unnamed x26, local copies, waits for them, and re-layouts  4.93 us
    all_to_all x1, starting transfers between devices, on_device(): lax.all_to_all(copies, 'row', split_axis=0, concat_axis=0, tiled=True, ax...  4.82 us
  transfers between devices with their start and end apart: 15, of which 7 were waited for; matrix products, arithmetic and copies ran while one was open for 0% of the time, Pallas kernels for 39%

profile of v15, /device:TPU:19, one launch (start us, length us, event | category | flops | bytes accessed | tf_op | source)
XLA Modules:
  0.0 94.1 jit_solution(1201344493183000867)
XLA Ops:
  0.6 1.3 %collective-permute-start.2 = (bf16[128,768]{1,0:T(8,128)(2,1)}, bf16[128,768]{1,0:T(8,128)(2,1)S(1)}, u32[]{:S(2)}, u32[]{:S(2)}) collective-permute-start(bf16[128,768]{1,0:T(8,128)(2,1)} %bitcast.14), channel_id=1, source_target_pairs={{0,4},{1,5},{2,6},{3,7},{4,8},{5,9},{6,10},{7,11},{8,12},{9,13},{1... | collective-permute-start | bytes 589832 | tf_op jit(solution)/shard_map/ppermute | solution.py:516
  2.0 1.0 %collective-permute-start = (bf16[128,768]{1,0:T(8,128)(2,1)}, bf16[128,768]{1,0:T(8,128)(2,1)S(1)}, u32[]{:S(2)}, u32[]{:S(2)}) collective-permute-start(bf16[128,768]{1,0:T(8,128)(2,1)} %bitcast.9), channel_id=1, source_target_pairs={{0,1},{1,0},{2,3},{3,2},{4,5},{5,4},{6,7},{7,6},{8,9},{9,8},{10,11... | collective-permute-start | bytes 589832 | tf_op jit(solution)/shard_map/ppermute | solution.py:488
  2.9 3.0 %collective-permute-start.1 = (bf16[128,768]{1,0:T(8,128)(2,1)}, bf16[128,768]{1,0:T(8,128)(2,1)S(1)}, u32[]{:S(2)}, u32[]{:S(2)}) collective-permute-start(bf16[128,768]{1,0:T(8,128)(2,1)} %bitcast.10), channel_id=1, source_target_pairs={{1,2},{3,4},{5,6},{7,8},{9,10},{11,12},{13,14},{2,1},{4,3},{6,5},{... | collective-permute-start | bytes 589832 | tf_op jit(solution)/shard_map/ppermute | solution.py:489
  6.0 0.2 collective-permute-start.3
  6.2 0.5 collective-permute-done.2.refs_7_.rest_1_
  6.7 1.3 %collective-permute-start.4 = (bf16[128,768]{1,0:T(8,128)(2,1)S(1)}, bf16[128,768]{1,0:T(8,128)(2,1)S(1)}, u32[]{:S(2)}, u32[]{:S(2)}) collective-permute-start(bf16[128,768]{1,0:T(8,128)(2,1)S(1)} %collective-permute-done.2.refs_7_.rest_1_), channel_id=1, source_target_pairs={{0,4},{1,5},{2,6},{3,7},{4,8},{5,9},{6,10},{7,11},{8,12},{9,13},{1... | collective-permute-start | bytes 589832 | tf_op jit(solution)/shard_map/ppermute | solution.py:516
  8.0 1.2 %copy-done = f32[343,768]{1,0:T(8,128)S(1)} copy-done((f32[343,768]{1,0:T(8,128)S(1)}, f32[343,768]{1,0:T(8,128)}, u32[]{:S(2)}) %copy-start) | copy-done | bytes 1053720
  9.2 0.9 copy-done.2
  10.1 2.2 %own_conv.1 = (f32[128,768]{1,0:T(8,128)S(1)}, f32[6,9,7,8,128]{4,3,2,1,0:T(8,128)S(1)}) custom-call(bf16[128,768]{1,0:T(8,128)(2,1)S(1)} %bitcast.11, f32[343,768]{1,0:T(8,128)S(1)} %copy-done), custom_call_target="tpu_custom_call" | custom-call | tf_op jit(solution)/shard_map/own_conv/pallas_call | solution.py:526
  12.3 0.0 collective-permute-done.refs_1_.inner
  12.3 0.2 collective-permute-done.1.refs_2_.outer
  12.5 0.3 collective-permute-done.3.refs_8_.rest_3_
  12.8 0.7 copy-done.9
  13.5 0.7 copy-done.11
  14.2 3.6 %rim_conv.1 = (bf16[4,128,768]{2,1,0:T(8,128)(2,1)}, f32[128,768]{1,0:T(8,128)S(1)}) custom-call(s32[1]{0:T(128)} %bitcast.refs_0_.core, bf16[128,768]{1,0:T(8,128)(2,1)S(1)} %collective-permute-done.refs_1_.inner, bf16[128,768]{1,0:T(8,128)(2,1)S(1)} %collective-permute-done.1.refs_2_.outer, f32[6,9,7,8,128]{4,3,2,1,0:T(8,128)S(1)} %get-tuple-element.34.refs_3_, ...), custom_call_target="tpu_custom_call" | custom-call | tf_op jit(solution)/shard_map/rim_conv/pallas_call | solution.py:543
  17.8 0.0 collective-permute-done.4.rest_2_
  17.8 4.7 %all-to-all-start = ((bf16[4,128,768]{2,1,0:T(8,128)(2,1)}), bf16[4,128,768]{2,1,0:T(8,128)(2,1)S(1)}, u32[]{:S(2)}, u32[]{:S(2)}) async-start(bf16[4,128,768]{2,1,0:T(8,128)(2,1)} %get-tuple-element.37.normed), calls=%async_computation | async-start | bytes 1572864 | tf_op jit(solution)/shard_map/all_to_all | solution.py:584
  22.6 0.1 pad_add_fusion.which
  22.6 9.5 %mlp_both_ways.1 = (bf16[128,768]{1,0:T(8,128)(2,1)}, bf16[128,768]{1,0:T(8,128)(2,1)S(1)}, f32[8,768]{1,0:T(8,128)S(1)}, bf16[4,128,768]{2,1,0:T(8,128)(2,1)S(1)}) custom-call(bf16[4,128,768]{2,1,0:T(8,128)(2,1)} %get-tuple-element.37.normed, bf16[3072,768]{1,0:T(8,128)(2,1)} %refs_1_.3, bf16[3072,768]{1,0:T(8,128)(2,1)} %refs_2_.3, ...), custom_call_target="tpu_custom_call" | custom-call | tf_op jit(solution)/shard_map/mlp_both_ways/pallas_call | solution.py:590
  32.1 4.4 %collective-permute-start.8 = (bf16[4,128,768]{2,1,0:T(8,128)(2,1)S(1)}, bf16[4,128,768]{2,1,0:T(8,128)(2,1)S(1)}, u32[]{:S(2)}, u32[]{:S(2)}) collective-permute-start(bf16[4,128,768]{2,1,0:T(8,128)(2,1)S(1)} %get-tuple-element.46.refs_5_), channel_id=1, source_target_pairs={{0,1},{1,0},{2,3},{3,2},{4,5},{5,4},{6,7},{7,6},{8,9},{9,8},{10,11... | collective-permute-start | bytes 2359304 | tf_op jit(solution)/shard_map/ppermute | solution.py:692
  36.5 6.4 %kernel_grad_terms.1 = (bf16[384,384]{1,0:T(8,128)(2,1)S(1)}, bf16[384,384]{1,0:T(8,128)(2,1)S(1)}, bf16[128,768]{1,0:T(8,128)(2,1)S(1)}, f32[8,128]{1,0:T(8,128)S(1)}) custom-call(s32[2]{0:T(128)S(1)} %pad_add_fusion.which, bf16[128,768]{1,0:T(8,128)(2,1)S(1)} %collective-permute-done.refs_1_.inner, bf16[128,768]{1,0:T(8,128)(2,1)S(1)} %bitcast.13, ...), custom_call_target="tpu_custom_call" | custom-call | tf_op jit(solution)/shard_map/kernel_grad_terms/pallas_call | solution.py:638
  42.9 0.0 copy-start.12
  42.9 0.7 copy-done.12
  43.6 0.0 all-to-all-done.refs_4_
  43.6 0.7 copy-done.6
  44.3 0.0 collective-permute-start.7
  44.3 0.5 collective-permute-start.9
  44.8 2.0 %collective-permute-done.9.refs_1_ = bf16[384,384]{1,0:T(8,128)(2,1)S(1)} collective-permute-done((bf16[384,384]{1,0:T(8,128)(2,1)}, bf16[384,384]{1,0:T(8,128)(2,1)S(1)}, u32[]{:S(2)}, u32[]{:S(2)}) %collective-permute-start.9) | collective-permute-done | bytes 294944 | tf_op jit(solution)/shard_map/ppermute | solution.py:667
  46.8 0.8 kernel_grad_chip_sum.1.refs_8_
  47.6 4.5 %all-to-all-start.1 = ((bf16[8,48,384]{2,1,0:T(8,128)(2,1)}), bf16[8,48,384]{2,1,0:T(8,128)(2,1)S(1)}, u32[]{:S(2)}, u32[]{:S(2)}) async-start(bf16[8,48,384]{2,1,0:T(8,128)(2,1)} %bitcast.8), calls=%async_computation.1 | async-start | bytes 589824 | tf_op jit(solution)/shard_map/all_to_all | solution.py:731
  52.1 0.9 collective-permute-start.5
  53.1 3.0 %collective-permute-start.6 = (bf16[128,768]{1,0:T(8,128)(2,1)}, bf16[128,768]{1,0:T(8,128)(2,1)S(1)}, u32[]{:S(2)}, u32[]{:S(2)}) collective-permute-start(bf16[128,768]{1,0:T(8,128)(2,1)} %copy-done.6), channel_id=1, source_target_pairs={{1,2},{3,4},{5,6},{7,8},{9,10},{11,12},{13,14},{2,1},{4,3},{6,5},{... | collective-permute-start | bytes 589832 | tf_op jit(solution)/shard_map/ppermute | solution.py:489
  56.1 0.1 pad_add_fusion.1.refs_0_
  56.1 0.0 collective-permute-done.5.refs_9_.refs_1_
  56.2 7.4 %collective-permute-done.6.refs_10_.refs_3_ = bf16[128,768]{1,0:T(8,128)(2,1)S(1)} collective-permute-done((bf16[128,768]{1,0:T(8,128)(2,1)}, bf16[128,768]{1,0:T(8,128)(2,1)S(1)}, u32[]{:S(2)}, u32[]{:S(2)}) %collective-permute-start.6) | collective-permute-done | bytes 196640 | tf_op jit(solution)/shard_map/ppermute | solution.py:489
  63.6 0.0 collective-permute-done.8.refs_7_
  63.6 0.0 collective-permute-done.7.refs_6_
  63.6 4.7 %weight_grads_far_side.1.refs_6_ = bf16[2,192,768]{2,1,0:T(8,128)(2,1)} custom-call(s32[6]{0:T(128)S(1)} %pad_add_fusion.1.refs_0_, bf16[3072,768]{1,0:T(8,128)(2,1)} %refs_1_.3, bf16[3072,768]{1,0:T(8,128)(2,1)} %refs_2_.3, f32[768]{0:T(1024)S(1)} %copy-done.8, bf16[4,128,768]{2,1,0:T(8,128)(2,1)S(1)} %all-to-all-done.refs_4_, ...), custom_call_target="tpu_custom_call" | custom-call | tf_op jit(solution)/shard_map/weight_grads_far_side/pallas_call | solution.py:696
  68.2 0.0 collective-permute-start.10
  68.2 4.3 %input_grad_conv.1 = (bf16[128,768]{1,0:T(8,128)(2,1)}, f32[8,128]{1,0:T(8,128)S(1)}) custom-call(s32[1]{0:T(128)} %bitcast.refs_0_.core, bf16[128,768]{1,0:T(8,128)(2,1)S(1)} %collective-permute-done.5.refs_9_.refs_1_, bf16[128,768]{1,0:T(8,128)(2,1)S(1)} %copy-done.7, bf16[128,768]{1,0:T(8,128)(2,1)S(1)} %collective-permute-done.6.refs_10_.refs_3_, ...), custom_call_target="tpu_custom_call" | custom-call | tf_op jit(solution)/shard_map/input_grad_conv/pallas_call | solution.py:739
  72.6 0.0 all-to-all-done.1.refs_0_
  72.6 0.8 kernel_grad_sum.1.refs_9_
  73.3 4.8 %all-to-all-start.2 = ((bf16[8,48,384]{2,1,0:T(8,128)(2,1)}), bf16[8,48,384]{2,1,0:T(8,128)(2,1)S(1)}, u32[]{:S(2)}, u32[]{:S(2)}) async-start(bf16[8,48,384]{2,1,0:T(8,128)(2,1)} %kernel_grad_sum.1.refs_9_), calls=%async_computation.2 | async-start | bytes 589824 | tf_op jit(solution)/shard_map/all_to_all | solution.py:777
  78.1 6.5 %collective-permute-done.10.refs_8_ = bf16[2,192,768]{2,1,0:T(8,128)(2,1)} collective-permute-done((bf16[2,192,768]{2,1,0:T(8,128)(2,1)}, bf16[2,192,768]{2,1,0:T(8,128)(2,1)}, u32[]{:S(2)}, u32[]{:S(2)}) %collective-permute-start.10) | collective-permute-done | bytes 589856 | tf_op jit(solution)/shard_map/ppermute | solution.py:730
  84.6 4.9 %weight_grads_near_side.1 = (f32[192,768]{1,0:T(8,128)}, f32[192,768]{1,0:T(8,128)}) custom-call(s32[6]{0:T(128)S(1)} %pad_add_fusion.1.refs_0_, bf16[3072,768]{1,0:T(8,128)(2,1)} %refs_1_.3, bf16[3072,768]{1,0:T(8,128)(2,1)} %refs_2_.3, f32[768]{0:T(1024)S(1)} %copy-done.8, bf16[4,128,768]{2,1,0:T(8,128)(2,1)S(1)} %all-to-all-done.refs_4_, ...), custom_call_target="tpu_custom_call" | custom-call | tf_op jit(solution)/shard_map/weight_grads_near_side/pallas_call | solution.py:696
  89.5 2.4 %collective-permute-start.11 = (bf16[8,48,384]{2,1,0:T(8,128)(2,1)S(1)}, bf16[8,48,384]{2,1,0:T(8,128)(2,1)S(1)}, u32[]{:S(2)}, u32[]{:S(2)}) collective-permute-start(bf16[8,48,384]{2,1,0:T(8,128)(2,1)S(1)} %all-to-all-done.2.own), channel_id=1, source_target_pairs={{0,1},{1,0},{2,3},{3,2},{4,5},{5,4},{6,7},{7,6},{8,9},{9,8},{10,11... | collective-permute-start | bytes 884744 | tf_op jit(solution)/shard_map/ppermute | solution.py:784
  91.9 1.2 %collective-permute-done.11.other = bf16[8,48,384]{2,1,0:T(8,128)(2,1)S(1)} collective-permute-done((bf16[8,48,384]{2,1,0:T(8,128)(2,1)S(1)}, bf16[8,48,384]{2,1,0:T(8,128)(2,1)S(1)}, u32[]{:S(2)}, u32[]{:S(2)}) %collective-permute-start.11) | collective-permute-done | bytes 294944 | tf_op jit(solution)/shard_map/ppermute | solution.py:784
  93.1 1.1 %kernel_grad_unpack.1 = (f32[343,768]{1,0:T(8,128)}, f32[768]{0:T(1024)}, f32[768]{0:T(1024)}, f32[768]{0:T(1024)}) custom-call(s32[1]{0:T(128)} %bitcast.refs_0_.core, bf16[8,48,384]{2,1,0:T(8,128)(2,1)S(1)} %all-to-all-done.2.own, bf16[8,48,384]{2,1,0:T(8,128)(2,1)S(1)} %collective-permute-done.11.other), custom_call_target="tpu_custom_call" | custom-call | tf_op jit(solution)/shard_map/kernel_grad_unpack/pallas_call | solution.py:785
  (21 shorter events, 0.0 us)
Async XLA Ops:
  0.6 6.0 %collective-permute-start.2 = (bf16[128,768]{1,0:T(8,128)(2,1)}, bf16[128,768]{1,0:T(8,128)(2,1)S(1)}, u32[]{:S(2)}, u32[]{:S(2)}) collective-permute-start(bf16[128,768]{1,0:T(8,128)(2,1)} %bitcast.14), channel_id=1, source_target_pairs={{0,4},{1,5},{2,6},{3,7},{4,8},{5,9},{6,10},{7,11},{8,12},{9,13},{1... | collective-permute-start | bytes 589832 | tf_op jit(solution)/shard_map/ppermute | solution.py:516
  2.0 10.3 %collective-permute-start = (bf16[128,768]{1,0:T(8,128)(2,1)}, bf16[128,768]{1,0:T(8,128)(2,1)S(1)}, u32[]{:S(2)}, u32[]{:S(2)}) collective-permute-start(bf16[128,768]{1,0:T(8,128)(2,1)} %bitcast.9), channel_id=1, source_target_pairs={{0,1},{1,0},{2,3},{3,2},{4,5},{5,4},{6,7},{7,6},{8,9},{9,8},{10,11... | collective-permute-start | bytes 589832 | tf_op jit(solution)/shard_map/ppermute | solution.py:488
  2.9 9.6 %collective-permute-start.1 = (bf16[128,768]{1,0:T(8,128)(2,1)}, bf16[128,768]{1,0:T(8,128)(2,1)S(1)}, u32[]{:S(2)}, u32[]{:S(2)}) collective-permute-start(bf16[128,768]{1,0:T(8,128)(2,1)} %bitcast.10), channel_id=1, source_target_pairs={{1,2},{3,4},{5,6},{7,8},{9,10},{11,12},{13,14},{2,1},{4,3},{6,5},{... | collective-permute-start | bytes 589832 | tf_op jit(solution)/shard_map/ppermute | solution.py:489
  6.0 6.9 %collective-permute-start.3 = (bf16[128,768]{1,0:T(8,128)(2,1)}, bf16[128,768]{1,0:T(8,128)(2,1)S(1)}, u32[]{:S(2)}, u32[]{:S(2)}) collective-permute-start(bf16[128,768]{1,0:T(8,128)(2,1)} %bitcast.15), channel_id=1, source_target_pairs={{0,12},{1,13},{2,14},{3,15},{4,0},{5,1},{6,2},{7,3},{8,4},{9,5},{1... | collective-permute-start | bytes 589832 | tf_op jit(solution)/shard_map/ppermute | solution.py:516
  6.7 11.2 %collective-permute-start.4 = (bf16[128,768]{1,0:T(8,128)(2,1)S(1)}, bf16[128,768]{1,0:T(8,128)(2,1)S(1)}, u32[]{:S(2)}, u32[]{:S(2)}) collective-permute-start(bf16[128,768]{1,0:T(8,128)(2,1)S(1)} %collective-permute-done.2.refs_7_.rest_1_), channel_id=1, source_target_pairs={{0,4},{1,5},{2,6},{3,7},{4,8},{5,9},{6,10},{7,11},{8,12},{9,13},{1... | collective-permute-start | bytes 589832 | tf_op jit(solution)/shard_map/ppermute | solution.py:516
  8.0 1.2 %copy-start = (f32[343,768]{1,0:T(8,128)S(1)}, f32[343,768]{1,0:T(8,128)}, u32[]{:S(2)}) copy-start(f32[343,768]{1,0:T(8,128)} %refs_4_.1) | copy-start | bytes 3161092
  9.2 0.9 copy-start.2
  12.8 0.7 copy-start.9
  13.5 0.7 copy-start.11
  14.2 8.4 %copy-start.3 = (bf16[4,4,8,768]{3,2,1,0:T(8,128)(2,1)S(1)}, bf16[4,4,8,768]{3,2,1,0:T(8,128)(2,1)}, u32[]{:S(2)}) copy-start(bf16[4,4,8,768]{3,2,1,0:T(8,128)(2,1)} %param.8) | copy-start | bytes 589828
  14.2 8.4 %copy-start.4 = (bf16[4,4,8,768]{3,2,1,0:T(8,128)(2,1)S(1)}, bf16[4,4,8,768]{3,2,1,0:T(8,128)(2,1)}, u32[]{:S(2)}) copy-start(bf16[4,4,8,768]{3,2,1,0:T(8,128)(2,1)} %param.15) | copy-start | bytes 589828
  14.2 8.4 %copy-start.8 = (f32[768]{0:T(1024)S(1)}, f32[768]{0:T(1024)}, u32[]{:S(2)}) copy-start(f32[768]{0:T(1024)} %refs_3_.3) | copy-start | bytes 9220
  14.2 8.4 %copy-start.10 = (f32[768]{0:T(1024)S(1)}, f32[768]{0:T(1024)}, u32[]{:S(2)}) copy-start(f32[768]{0:T(1024)} %norm_gain.1) | copy-start | bytes 9220
  17.8 25.8 %all-to-all-start = ((bf16[4,128,768]{2,1,0:T(8,128)(2,1)}), bf16[4,128,768]{2,1,0:T(8,128)(2,1)S(1)}, u32[]{:S(2)}, u32[]{:S(2)}) async-start(bf16[4,128,768]{2,1,0:T(8,128)(2,1)} %get-tuple-element.37.normed), calls=%async_computation | async-start | bytes 1572864 | tf_op jit(solution)/shard_map/all_to_all | solution.py:584
  32.1 31.5 %collective-permute-start.8 = (bf16[4,128,768]{2,1,0:T(8,128)(2,1)S(1)}, bf16[4,128,768]{2,1,0:T(8,128)(2,1)S(1)}, u32[]{:S(2)}, u32[]{:S(2)}) collective-permute-start(bf16[4,128,768]{2,1,0:T(8,128)(2,1)S(1)} %get-tuple-element.46.refs_5_), channel_id=1, source_target_pairs={{0,1},{1,0},{2,3},{3,2},{4,5},{5,4},{6,7},{7,6},{8,9},{9,8},{10,11... | collective-permute-start | bytes 2359304 | tf_op jit(solution)/shard_map/ppermute | solution.py:692
  42.9 0.7 copy-start.12
  43.6 0.7 copy-start.6
  44.3 19.3 %collective-permute-start.7 = (bf16[4,128,768]{2,1,0:T(8,128)(2,1)S(1)}, bf16[4,128,768]{2,1,0:T(8,128)(2,1)S(1)}, u32[]{:S(2)}, u32[]{:S(2)}) collective-permute-start(bf16[4,128,768]{2,1,0:T(8,128)(2,1)S(1)} %all-to-all-done.refs_4_), channel_id=1, source_target_pairs={{0,1},{1,0},{2,3},{3,2},{4,5},{5,4},{6,7},{7,6},{8,9},{9,8},{10,11... | collective-permute-start | bytes 2359304 | tf_op jit(solution)/shard_map/ppermute | solution.py:691
  44.3 2.5 %collective-permute-start.9 = (bf16[384,384]{1,0:T(8,128)(2,1)}, bf16[384,384]{1,0:T(8,128)(2,1)S(1)}, u32[]{:S(2)}, u32[]{:S(2)}) collective-permute-start(bf16[384,384]{1,0:T(8,128)(2,1)} %copy-done.12), channel_id=1, source_target_pairs={{0,1},{1,0},{2,3},{3,2},{4,5},{5,4},{6,7},{7,6},{8,9},{9,8},{10,11... | collective-permute-start | bytes 884744 | tf_op jit(solution)/shard_map/ppermute | solution.py:667
  47.6 25.0 %all-to-all-start.1 = ((bf16[8,48,384]{2,1,0:T(8,128)(2,1)}), bf16[8,48,384]{2,1,0:T(8,128)(2,1)S(1)}, u32[]{:S(2)}, u32[]{:S(2)}) async-start(bf16[8,48,384]{2,1,0:T(8,128)(2,1)} %bitcast.8), calls=%async_computation.1 | async-start | bytes 589824 | tf_op jit(solution)/shard_map/all_to_all | solution.py:731
  52.1 4.0 %collective-permute-start.5 = (bf16[128,768]{1,0:T(8,128)(2,1)}, bf16[128,768]{1,0:T(8,128)(2,1)S(1)}, u32[]{:S(2)}, u32[]{:S(2)}) collective-permute-start(bf16[128,768]{1,0:T(8,128)(2,1)} %copy-done.6), channel_id=1, source_target_pairs={{0,1},{1,0},{2,3},{3,2},{4,5},{5,4},{6,7},{7,6},{8,9},{9,8},{10,11... | collective-permute-start | bytes 589832 | tf_op jit(solution)/shard_map/ppermute | solution.py:488
  53.1 10.5 %collective-permute-start.6 = (bf16[128,768]{1,0:T(8,128)(2,1)}, bf16[128,768]{1,0:T(8,128)(2,1)S(1)}, u32[]{:S(2)}, u32[]{:S(2)}) collective-permute-start(bf16[128,768]{1,0:T(8,128)(2,1)} %copy-done.6), channel_id=1, source_target_pairs={{1,2},{3,4},{5,6},{7,8},{9,10},{11,12},{13,14},{2,1},{4,3},{6,5},{... | collective-permute-start | bytes 589832 | tf_op jit(solution)/shard_map/ppermute | solution.py:489
  56.1 12.1 %copy-start.1 = (f32[343,768]{1,0:T(8,128)S(1)}, f32[343,768]{1,0:T(8,128)}, u32[]{:S(2)}) copy-start(f32[343,768]{1,0:T(8,128)} %refs_4_.1) | copy-start | bytes 3161092
  56.1 12.1 %copy-start.5 = (bf16[4,4,8,768]{3,2,1,0:T(8,128)(2,1)S(1)}, bf16[4,4,8,768]{3,2,1,0:T(8,128)(2,1)}, u32[]{:S(2)}) copy-start(bf16[4,4,8,768]{3,2,1,0:T(8,128)(2,1)} %param.15) | copy-start | bytes 589828
  56.1 12.1 %copy-start.7 = (bf16[128,768]{1,0:T(8,128)(2,1)S(1)}, bf16[128,768]{1,0:T(8,128)(2,1)}, u32[]{:S(2)}) copy-start(bf16[128,768]{1,0:T(8,128)(2,1)} %copy-done.6) | copy-start | bytes 589828
  68.2 16.4 %collective-permute-start.10 = (bf16[2,192,768]{2,1,0:T(8,128)(2,1)}, bf16[2,192,768]{2,1,0:T(8,128)(2,1)}, u32[]{:S(2)}, u32[]{:S(2)}) collective-permute-start(bf16[2,192,768]{2,1,0:T(8,128)(2,1)} %weight_grads_far_side.1.refs_6_), channel_id=1, source_target_pairs={{0,2},{1,3},{2,0},{3,1},{4,6},{5,7},{6,4},{7,5},{8,10},{9,11},{10,... | collective-permute-start | bytes 1769480 | tf_op jit(solution)/shard_map/ppermute | solution.py:730
  73.3 16.2 %all-to-all-start.2 = ((bf16[8,48,384]{2,1,0:T(8,128)(2,1)}), bf16[8,48,384]{2,1,0:T(8,128)(2,1)S(1)}, u32[]{:S(2)}, u32[]{:S(2)}) async-start(bf16[8,48,384]{2,1,0:T(8,128)(2,1)} %kernel_grad_sum.1.refs_9_), calls=%async_computation.2 | async-start | bytes 589824 | tf_op jit(solution)/shard_map/all_to_all | solution.py:777
  89.5 3.6 %collective-permute-start.11 = (bf16[8,48,384]{2,1,0:T(8,128)(2,1)S(1)}, bf16[8,48,384]{2,1,0:T(8,128)(2,1)S(1)}, u32[]{:S(2)}, u32[]{:S(2)}) collective-permute-start(bf16[8,48,384]{2,1,0:T(8,128)(2,1)S(1)} %all-to-all-done.2.own), channel_id=1, source_target_pairs={{0,1},{1,0},{2,3},{3,2},{4,5},{5,4},{6,7},{7,6},{8,9},{9,8},{10,11... | collective-permute-start | bytes 884744 | tf_op jit(solution)/shard_map/ppermute | solution.py:784

commit v16 on v15

--- a/solution.py
+++ b/solution.py
@@ -250,14 +250,12 @@
     sent,
     kept,
     passed,
-    token,
     spread,
     products,
     joined,
     flat,
 ):
     passed[...] = grads[...]
-    token[...] = jnp.zeros(token.shape, F32)
 
     @pl.when(pl.program_id(0) == 0)
     def _():
@@ -427,7 +425,8 @@
         out[...] = terms[k] + got[k].astype(F32)
 
 
-def chip_sum_kernel(kept, got, out):
+def chip_sum_kernel(kept, got, out, token):
+    token[...] = jnp.zeros(token.shape, F32)
     out[...] = (kept[...].astype(F32) + got[...].astype(F32)).astype(BF16)
 
 
@@ -635,7 +634,7 @@
 
         return pl.BlockSpec((block_rows, LANES), at)
 
-    half_sent, half_kept, conv_grad, token = pl.pallas_call(
+    half_sent, half_kept, conv_grad = pl.pallas_call(
         functools.partial(kernel_grad_kernel, planes, height),
         grid_spec=pltpu.PrefetchScalarGridSpec(
             num_scalar_prefetch=1,
@@ -645,7 +644,6 @@
                 pl.BlockSpec((padded, LANES), lambda c, w: (0, jnp.minimum(c, half_tiles - 1))),
                 pl.BlockSpec((padded, LANES), lambda c, w: (0, jnp.maximum(c - half_tiles, 0))),
                 tile_of(rows),
-                whole_block(SUB, LANES),
             ],
             scratch_shapes=[
                 spread_of(2 * MARGIN + planes),
@@ -657,7 +655,6 @@
         out_shape=[jax.ShapeDtypeStruct((padded, wide), BF16)] * 2
         + [
             jax.ShapeDtypeStruct((rows, channels), BF16),
-            jax.ShapeDtypeStruct((SUB, LANES), F32),
         ],
         compiler_params=params(),
         cost_estimate=NO_COST,
@@ -665,18 +662,21 @@
     )(jnp.stack([core, 1 - core]), inner, own, outer, conv_grad, small)
 
     half_got = lax.ppermute(half_sent, "row", other_core)
-    gathered, token = lax.optimization_barrier((gathered, token))
     grad_inner, grad_outer = rims(conv_grad)
-    sums = pl.pallas_call(
-        follow(chip_sum_kernel, 0, 2, 1),
-        in_specs=[whole_block(padded, wide)] * 2 + [IN_PLACE],
-        out_specs=whole_block(padded, wide),
-        out_shape=jax.ShapeDtypeStruct((padded, wide), BF16),
+    sums, token = pl.pallas_call(
+        follow(chip_sum_kernel, 0, 2, 2),
+        in_specs=[whole_block(padded, wide)] * 2 + [IN_PLACE] * 2,
+        out_specs=[whole_block(padded, wide), whole_block(SUB, LANES)],
+        out_shape=[
+            jax.ShapeDtypeStruct((padded, wide), BF16),
+            jax.ShapeDtypeStruct((SUB, LANES), F32),
+        ],
         grid=(1,),
         compiler_params=params(),
         cost_estimate=NO_COST,
         name="kernel_grad_chip_sum",
-    )(half_kept, half_got, token)
+    )(half_kept, half_got, grad_inner, grad_outer)
+    gathered, token = lax.optimization_barrier((gathered, token))
 
     share = units // count
     tokens = line * rows
@@ -725,7 +725,7 @@
     pair = jax.ShapeDtypeStruct((2, share, channels), BF16)
     single = jax.ShapeDtypeStruct((share, channels), F32)
     (sent,) = side_terms(
-        far_side_kernel, 0, [], [sums, grad_inner, grad_outer], [pair], "weight_grads_far_side"
+        far_side_kernel, 0, [], [sums, token], [pair], "weight_grads_far_side"
     )
     got = lax.ppermute(sent, "row", other_side)
     scattered = lax.all_to_all(

time: 94.8 us -> 90.5 us (0.955)
  the two profiles are of different devices: /device:TPU:19 before, /device:TPU:1 now
where the time goes in v16:
time: 90.5 us; the launch traced here: 89.5 us
  Pallas kernels  38 us (42%)
  starting transfers between devices  32.5 us (36%)
  waiting for transfers between devices  12.5 us (14%)
  local copies, waits for them, and re-layouts  5.58 us (6%)
    pallas_call x2, Pallas kernels, side_terms(): pl.pallas_call(follow(kernel, 1, 7 + len(more), len(after)), grid_spec=pl...  9.52 us
    pallas_call x1, Pallas kernels, on_device(): pl.pallas_call(mlp_kernel, grid=(units // block,), in_specs=[pl.BlockSpec...  9.45 us
    all_to_all x1, starting transfers between devices, on_device(): lax.all_to_all(sums.reshape(half, piece, wide), 'row', split_axis=0, conc...  6.89 us
    pallas_call x1, Pallas kernels, on_device(): pl.pallas_call(functools.partial(kernel_grad_kernel, planes, height), gri...  6.35 us
    unnamed x32, local copies, waits for them, and re-layouts  5.58 us
    ppermute x1, waiting for transfers between devices, on_device(): got = lax.ppermute(sent, 'row', other_side)  5.43 us
    ppermute x2, starting transfers between devices, rims(): lax.ppermute(cells, 'row', between + [(j, i) for i, j in between])  4.93 us
    ppermute x2, waiting for transfers between devices, rims(): lax.ppermute(cells, 'row', between + [(j, i) for i, j in between])  4.37 us
  transfers between devices with their start and end apart: 15, of which 6 were waited for; matrix products, arithmetic and copies ran while one was open for 0% of the time, Pallas kernels for 41%

profile of v16, /device:TPU:1, one launch (start us, length us, event | category | flops | bytes accessed | tf_op | source)
XLA Modules:
  0.0 89.5 jit_solution(1997413021623309679)
XLA Ops:
  0.6 2.2 %collective-permute-start.2 = (bf16[128,768]{1,0:T(8,128)(2,1)}, bf16[128,768]{1,0:T(8,128)(2,1)S(1)}, u32[]{:S(2)}, u32[]{:S(2)}) collective-permute-start(bf16[128,768]{1,0:T(8,128)(2,1)} %bitcast.14), channel_id=1, source_target_pairs={{0,4},{1,5},{2,6},{3,7},{4,8},{5,9},{6,10},{7,11},{8,12},{9,13},{1... | collective-permute-start | bytes 589832 | tf_op jit(solution)/shard_map/ppermute | solution.py:515
  2.8 1.0 %collective-permute-start = (bf16[128,768]{1,0:T(8,128)(2,1)}, bf16[128,768]{1,0:T(8,128)(2,1)S(1)}, u32[]{:S(2)}, u32[]{:S(2)}) collective-permute-start(bf16[128,768]{1,0:T(8,128)(2,1)} %bitcast.9), channel_id=1, source_target_pairs={{0,1},{1,0},{2,3},{3,2},{4,5},{5,4},{6,7},{7,6},{8,9},{9,8},{10,11... | collective-permute-start | bytes 589832 | tf_op jit(solution)/shard_map/ppermute | solution.py:487
  3.8 3.0 %collective-permute-start.1 = (bf16[128,768]{1,0:T(8,128)(2,1)}, bf16[128,768]{1,0:T(8,128)(2,1)S(1)}, u32[]{:S(2)}, u32[]{:S(2)}) collective-permute-start(bf16[128,768]{1,0:T(8,128)(2,1)} %bitcast.10), channel_id=1, source_target_pairs={{1,2},{3,4},{5,6},{7,8},{9,10},{11,12},{13,14},{2,1},{4,3},{6,5},{... | collective-permute-start | bytes 589832 | tf_op jit(solution)/shard_map/ppermute | solution.py:488
  6.8 2.0 %collective-permute-start.3 = (bf16[128,768]{1,0:T(8,128)(2,1)}, bf16[128,768]{1,0:T(8,128)(2,1)S(1)}, u32[]{:S(2)}, u32[]{:S(2)}) collective-permute-start(bf16[128,768]{1,0:T(8,128)(2,1)} %bitcast.15), channel_id=1, source_target_pairs={{0,12},{1,13},{2,14},{3,15},{4,0},{5,1},{6,2},{7,3},{8,4},{9,5},{1... | collective-permute-start | bytes 589832 | tf_op jit(solution)/shard_map/ppermute | solution.py:515
  8.8 0.9 collective-permute-done.2.refs_7_.rest_1_
  9.7 0.0 collective-permute-start.4
  9.7 1.2 %copy-done = f32[343,768]{1,0:T(8,128)S(1)} copy-done((f32[343,768]{1,0:T(8,128)S(1)}, f32[343,768]{1,0:T(8,128)}, u32[]{:S(2)}) %copy-start) | copy-done | bytes 1053720
  10.9 0.9 %copy-done.2 = bf16[4,4,8,768]{3,2,1,0:T(8,128)(2,1)S(1)} copy-done((bf16[4,4,8,768]{3,2,1,0:T(8,128)(2,1)S(1)}, bf16[4,4,8,768]{3,2,1,0:T(8,128)(2,1)}, u32[]{:S(2)}) %copy-start.2) | copy-done | bytes 196632
  11.8 2.2 %own_conv.1 = (f32[128,768]{1,0:T(8,128)S(1)}, f32[6,9,7,8,128]{4,3,2,1,0:T(8,128)S(1)}) custom-call(bf16[128,768]{1,0:T(8,128)(2,1)S(1)} %bitcast.11, f32[343,768]{1,0:T(8,128)S(1)} %copy-done), custom_call_target="tpu_custom_call" | custom-call | tf_op jit(solution)/shard_map/own_conv/pallas_call | solution.py:525
  14.0 0.0 collective-permute-done.refs_1_.inner
  14.0 0.0 collective-permute-done.1.refs_2_.outer
  14.0 0.4 collective-permute-done.3.refs_8_.rest_3_
  14.4 0.7 copy-done.13
  15.1 0.7 copy-done.15
  15.8 3.6 %rim_conv.1 = (bf16[4,128,768]{2,1,0:T(8,128)(2,1)}, f32[128,768]{1,0:T(8,128)S(1)}) custom-call(s32[1]{0:T(128)} %bitcast.refs_0_.core, bf16[128,768]{1,0:T(8,128)(2,1)S(1)} %collective-permute-done.refs_1_.inner, bf16[128,768]{1,0:T(8,128)(2,1)S(1)} %collective-permute-done.1.refs_2_.outer, f32[6,9,7,8,128]{4,3,2,1,0:T(8,128)S(1)} %get-tuple-element.35.refs_3_, ...), custom_call_target="tpu_custom_call" | custom-call | tf_op jit(solution)/shard_map/rim_conv/pallas_call | solution.py:542
  19.4 0.2 collective-permute-done.4.rest_2_
  19.6 4.0 %all-to-all-start = ((bf16[4,128,768]{2,1,0:T(8,128)(2,1)}), bf16[4,128,768]{2,1,0:T(8,128)(2,1)S(1)}, u32[]{:S(2)}, u32[]{:S(2)}) async-start(bf16[4,128,768]{2,1,0:T(8,128)(2,1)} %get-tuple-element.38.normed), calls=%async_computation | async-start | bytes 1572864 | tf_op jit(solution)/shard_map/all_to_all | solution.py:583
  23.6 0.1 pad_add_fusion.which
  23.7 9.5 %mlp_both_ways.1 = (bf16[128,768]{1,0:T(8,128)(2,1)}, bf16[128,768]{1,0:T(8,128)(2,1)S(1)}, f32[8,768]{1,0:T(8,128)S(1)}, bf16[4,128,768]{2,1,0:T(8,128)(2,1)S(1)}) custom-call(bf16[4,128,768]{2,1,0:T(8,128)(2,1)} %get-tuple-element.38.normed, bf16[3072,768]{1,0:T(8,128)(2,1)} %refs_1_.3, bf16[3072,768]{1,0:T(8,128)(2,1)} %refs_2_.3, ...), custom_call_target="tpu_custom_call" | custom-call | tf_op jit(solution)/shard_map/mlp_both_ways/pallas_call | solution.py:589
  33.1 6.4 %kernel_grad_terms.1 = (bf16[384,384]{1,0:T(8,128)(2,1)S(1)}, bf16[384,384]{1,0:T(8,128)(2,1)S(1)}, bf16[128,768]{1,0:T(8,128)(2,1)S(1)}) custom-call(s32[2]{0:T(128)S(1)} %pad_add_fusion.which, bf16[128,768]{1,0:T(8,128)(2,1)S(1)} %collective-permute-done.refs_1_.inner, bf16[128,768]{1,0:T(8,128)(2,1)S(1)} %bitcast.13, ...), custom_call_target="tpu_custom_call" | custom-call | tf_op jit(solution)/shard_map/kernel_grad_terms/pallas_call | solution.py:637
  39.5 4.0 %collective-permute-start.7 = (bf16[384,384]{1,0:T(8,128)(2,1)S(1)}, bf16[384,384]{1,0:T(8,128)(2,1)S(1)}, u32[]{:S(2)}, u32[]{:S(2)}) collective-permute-start(bf16[384,384]{1,0:T(8,128)(2,1)S(1)} %get-tuple-element.46), channel_id=1, source_target_pairs={{0,1},{1,0},{2,3},{3,2},{4,5},{5,4},{6,7},{7,6},{8,9},{9,8},{10,11... | collective-permute-start | bytes 884744 | tf_op jit(solution)/shard_map/ppermute | solution.py:664
  43.4 0.1 collective-permute-start.5
  43.5 1.9 %collective-permute-start.6 = (bf16[128,768]{1,0:T(8,128)(2,1)S(1)}, bf16[128,768]{1,0:T(8,128)(2,1)S(1)}, u32[]{:S(2)}, u32[]{:S(2)}) collective-permute-start(bf16[128,768]{1,0:T(8,128)(2,1)S(1)} %get-tuple-element.44.refs_2_), channel_id=1, source_target_pairs={{1,2},{3,4},{5,6},{7,8},{9,10},{11,12},{13,14},{2,1},{4,3},{6,5},{... | collective-permute-start | bytes 589832 | tf_op jit(solution)/shard_map/ppermute | solution.py:488
  45.4 0.7 copy-done.10
  46.1 0.0 collective-permute-start.9
  46.1 0.0 collective-permute-done.5.refs_2_.refs_1_
  46.1 4.4 %collective-permute-done.6.refs_3_ = bf16[128,768]{1,0:T(8,128)(2,1)S(1)} collective-permute-done((bf16[128,768]{1,0:T(8,128)(2,1)S(1)}, bf16[128,768]{1,0:T(8,128)(2,1)S(1)}, u32[]{:S(2)}, u32[]{:S(2)}) %collective-permute-start.6) | collective-permute-done | bytes 196640 | tf_op jit(solution)/shard_map/ppermute | solution.py:488
  50.5 0.0 collective-permute-done.7.refs_1_
  50.5 0.8 kernel_grad_chip_sum.1
  51.3 0.7 copy-done.4
  52.0 0.7 copy-done.6
  52.6 0.0 all-to-all-done.refs_4_
  52.6 0.0 collective-permute-start.8
  52.6 6.9 %all-to-all-start.1 = ((bf16[8,48,384]{2,1,0:T(8,128)(2,1)}), bf16[8,48,384]{2,1,0:T(8,128)(2,1)S(1)}, u32[]{:S(2)}, u32[]{:S(2)}) async-start(bf16[8,48,384]{2,1,0:T(8,128)(2,1)} %bitcast.8), calls=%async_computation.1 | async-start | bytes 589824 | tf_op jit(solution)/shard_map/all_to_all | solution.py:731
  59.5 0.1 pad_add_fusion.1.refs_0_
  59.6 0.0 collective-permute-done.9.refs_7_
  59.6 0.0 collective-permute-done.8.refs_6_
  59.7 4.7 %weight_grads_far_side.1.refs_6_ = bf16[2,192,768]{2,1,0:T(8,128)(2,1)} custom-call(s32[6]{0:T(128)S(1)} %pad_add_fusion.1.refs_0_, bf16[3072,768]{1,0:T(8,128)(2,1)} %refs_1_.3, bf16[3072,768]{1,0:T(8,128)(2,1)} %refs_2_.3, f32[768]{0:T(1024)S(1)} %copy-done.12, bf16[4,128,768]{2,1,0:T(8,128)(2,1)S(1)} %all-to-all-done.refs_4_, ...), custom_call_target="tpu_custom_call" | custom-call | tf_op jit(solution)/shard_map/weight_grads_far_side/pallas_call | solution.py:696
  64.3 1.5 %collective-permute-start.10 = (bf16[2,192,768]{2,1,0:T(8,128)(2,1)}, bf16[2,192,768]{2,1,0:T(8,128)(2,1)}, u32[]{:S(2)}, u32[]{:S(2)}) collective-permute-start(bf16[2,192,768]{2,1,0:T(8,128)(2,1)} %weight_grads_far_side.1.refs_6_), channel_id=1, source_target_pairs={{0,2},{1,3},{2,0},{3,1},{4,6},{5,7},{6,4},{7,5},{8,10},{9,11},{10,... | collective-permute-start | bytes 1769480 | tf_op jit(solution)/shard_map/ppermute | solution.py:730
  65.8 4.3 %input_grad_conv.1 = (bf16[128,768]{1,0:T(8,128)(2,1)}, f32[8,128]{1,0:T(8,128)S(1)}) custom-call(s32[1]{0:T(128)} %bitcast.refs_0_.core, bf16[128,768]{1,0:T(8,128)(2,1)S(1)} %copy-done.5, bf16[128,768]{1,0:T(8,128)(2,1)S(1)} %copy-done.11, bf16[128,768]{1,0:T(8,128)(2,1)S(1)} %copy-done.7, f32[343,768]{1,0:T(8,128)S(1)} %copy-done.1, ...), custom_call_target="tpu_custom_call" | custom-call | tf_op jit(solution)/shard_map/input_grad_conv/pallas_call | solution.py:739
  70.1 0.8 kernel_grad_sum.1.refs_9_
  70.9 4.3 %all-to-all-start.2 = ((bf16[8,48,384]{2,1,0:T(8,128)(2,1)}), bf16[8,48,384]{2,1,0:T(8,128)(2,1)S(1)}, u32[]{:S(2)}, u32[]{:S(2)}) async-start(bf16[8,48,384]{2,1,0:T(8,128)(2,1)} %kernel_grad_sum.1.refs_9_), calls=%async_computation.2 | async-start | bytes 589824 | tf_op jit(solution)/shard_map/all_to_all | solution.py:777
  75.1 5.4 %collective-permute-done.10.refs_8_ = bf16[2,192,768]{2,1,0:T(8,128)(2,1)} collective-permute-done((bf16[2,192,768]{2,1,0:T(8,128)(2,1)}, bf16[2,192,768]{2,1,0:T(8,128)(2,1)}, u32[]{:S(2)}, u32[]{:S(2)}) %collective-permute-start.10) | collective-permute-done | bytes 589856 | tf_op jit(solution)/shard_map/ppermute | solution.py:730
  80.6 4.9 %weight_grads_near_side.1 = (f32[192,768]{1,0:T(8,128)}, f32[192,768]{1,0:T(8,128)}) custom-call(s32[6]{0:T(128)S(1)} %pad_add_fusion.1.refs_0_, bf16[3072,768]{1,0:T(8,128)(2,1)} %refs_1_.3, bf16[3072,768]{1,0:T(8,128)(2,1)} %refs_2_.3, f32[768]{0:T(1024)S(1)} %copy-done.12, bf16[4,128,768]{2,1,0:T(8,128)(2,1)S(1)} %all-to-all-done.refs_4_, ...), custom_call_target="tpu_custom_call" | custom-call | tf_op jit(solution)/shard_map/weight_grads_near_side/pallas_call | solution.py:696
  85.4 0.0 all-to-all-done.2.own
  85.4 1.8 %collective-permute-start.11 = (bf16[8,48,384]{2,1,0:T(8,128)(2,1)S(1)}, bf16[8,48,384]{2,1,0:T(8,128)(2,1)S(1)}, u32[]{:S(2)}, u32[]{:S(2)}) collective-permute-start(bf16[8,48,384]{2,1,0:T(8,128)(2,1)S(1)} %all-to-all-done.2.own), channel_id=1, source_target_pairs={{0,1},{1,0},{2,3},{3,2},{4,5},{5,4},{6,7},{7,6},{8,9},{9,8},{10,11... | collective-permute-start | bytes 884744 | tf_op jit(solution)/shard_map/ppermute | solution.py:784
  87.3 1.2 %collective-permute-done.11.other = bf16[8,48,384]{2,1,0:T(8,128)(2,1)S(1)} collective-permute-done((bf16[8,48,384]{2,1,0:T(8,128)(2,1)S(1)}, bf16[8,48,384]{2,1,0:T(8,128)(2,1)S(1)}, u32[]{:S(2)}, u32[]{:S(2)}) %collective-permute-start.11) | collective-permute-done | bytes 294944 | tf_op jit(solution)/shard_map/ppermute | solution.py:784
  88.5 1.1 %kernel_grad_unpack.1 = (f32[343,768]{1,0:T(8,128)}, f32[768]{0:T(1024)}, f32[768]{0:T(1024)}, f32[768]{0:T(1024)}) custom-call(s32[1]{0:T(128)} %bitcast.refs_0_.core, bf16[8,48,384]{2,1,0:T(8,128)(2,1)S(1)} %all-to-all-done.2.own, bf16[8,48,384]{2,1,0:T(8,128)(2,1)S(1)} %collective-permute-done.11.other), custom_call_target="tpu_custom_call" | custom-call | tf_op jit(solution)/shard_map/kernel_grad_unpack/pallas_call | solution.py:785
  (27 shorter events, 0.1 us)
Async XLA Ops:
  0.6 9.0 %collective-permute-start.2 = (bf16[128,768]{1,0:T(8,128)(2,1)}, bf16[128,768]{1,0:T(8,128)(2,1)S(1)}, u32[]{:S(2)}, u32[]{:S(2)}) collective-permute-start(bf16[128,768]{1,0:T(8,128)(2,1)} %bitcast.14), channel_id=1, source_target_pairs={{0,4},{1,5},{2,6},{3,7},{4,8},{5,9},{6,10},{7,11},{8,12},{9,13},{1... | collective-permute-start | bytes 589832 | tf_op jit(solution)/shard_map/ppermute | solution.py:515
  2.8 11.2 %collective-permute-start = (bf16[128,768]{1,0:T(8,128)(2,1)}, bf16[128,768]{1,0:T(8,128)(2,1)S(1)}, u32[]{:S(2)}, u32[]{:S(2)}) collective-permute-start(bf16[128,768]{1,0:T(8,128)(2,1)} %bitcast.9), channel_id=1, source_target_pairs={{0,1},{1,0},{2,3},{3,2},{4,5},{5,4},{6,7},{7,6},{8,9},{9,8},{10,11... | collective-permute-start | bytes 589832 | tf_op jit(solution)/shard_map/ppermute | solution.py:487
  3.8 10.2 %collective-permute-start.1 = (bf16[128,768]{1,0:T(8,128)(2,1)}, bf16[128,768]{1,0:T(8,128)(2,1)S(1)}, u32[]{:S(2)}, u32[]{:S(2)}) collective-permute-start(bf16[128,768]{1,0:T(8,128)(2,1)} %bitcast.10), channel_id=1, source_target_pairs={{1,2},{3,4},{5,6},{7,8},{9,10},{11,12},{13,14},{2,1},{4,3},{6,5},{... | collective-permute-start | bytes 589832 | tf_op jit(solution)/shard_map/ppermute | solution.py:488
  6.8 7.6 %collective-permute-start.3 = (bf16[128,768]{1,0:T(8,128)(2,1)}, bf16[128,768]{1,0:T(8,128)(2,1)S(1)}, u32[]{:S(2)}, u32[]{:S(2)}) collective-permute-start(bf16[128,768]{1,0:T(8,128)(2,1)} %bitcast.15), channel_id=1, source_target_pairs={{0,12},{1,13},{2,14},{3,15},{4,0},{5,1},{6,2},{7,3},{8,4},{9,5},{1... | collective-permute-start | bytes 589832 | tf_op jit(solution)/shard_map/ppermute | solution.py:515
  9.7 9.9 %collective-permute-start.4 = (bf16[128,768]{1,0:T(8,128)(2,1)S(1)}, bf16[128,768]{1,0:T(8,128)(2,1)S(1)}, u32[]{:S(2)}, u32[]{:S(2)}) collective-permute-start(bf16[128,768]{1,0:T(8,128)(2,1)S(1)} %collective-permute-done.2.refs_7_.rest_1_), channel_id=1, source_target_pairs={{0,4},{1,5},{2,6},{3,7},{4,8},{5,9},{6,10},{7,11},{8,12},{9,13},{1... | collective-permute-start | bytes 589832 | tf_op jit(solution)/shard_map/ppermute | solution.py:515
  9.7 1.2 %copy-start = (f32[343,768]{1,0:T(8,128)S(1)}, f32[343,768]{1,0:T(8,128)}, u32[]{:S(2)}) copy-start(f32[343,768]{1,0:T(8,128)} %refs_4_.1) | copy-start | bytes 3161092
  10.9 0.9 %copy-start.2 = (bf16[4,4,8,768]{3,2,1,0:T(8,128)(2,1)S(1)}, bf16[4,4,8,768]{3,2,1,0:T(8,128)(2,1)}, u32[]{:S(2)}) copy-start(bf16[4,4,8,768]{3,2,1,0:T(8,128)(2,1)} %param.8) | copy-start | bytes 589828
  14.4 0.7 copy-start.13
  15.1 0.7 copy-start.15
  15.8 7.9 %copy-start.3 = (bf16[4,4,8,768]{3,2,1,0:T(8,128)(2,1)S(1)}, bf16[4,4,8,768]{3,2,1,0:T(8,128)(2,1)}, u32[]{:S(2)}) copy-start(bf16[4,4,8,768]{3,2,1,0:T(8,128)(2,1)} %param.8) | copy-start | bytes 589828
  15.8 7.9 %copy-start.8 = (bf16[4,4,8,768]{3,2,1,0:T(8,128)(2,1)S(1)}, bf16[4,4,8,768]{3,2,1,0:T(8,128)(2,1)}, u32[]{:S(2)}) copy-start(bf16[4,4,8,768]{3,2,1,0:T(8,128)(2,1)} %param.15) | copy-start | bytes 589828
  15.8 7.9 %copy-start.12 = (f32[768]{0:T(1024)S(1)}, f32[768]{0:T(1024)}, u32[]{:S(2)}) copy-start(f32[768]{0:T(1024)} %refs_3_.3) | copy-start | bytes 9220
  15.8 7.9 %copy-start.14 = (f32[768]{0:T(1024)S(1)}, f32[768]{0:T(1024)}, u32[]{:S(2)}) copy-start(f32[768]{0:T(1024)} %norm_gain.1) | copy-start | bytes 9220
  19.6 33.0 %all-to-all-start = ((bf16[4,128,768]{2,1,0:T(8,128)(2,1)}), bf16[4,128,768]{2,1,0:T(8,128)(2,1)S(1)}, u32[]{:S(2)}, u32[]{:S(2)}) async-start(bf16[4,128,768]{2,1,0:T(8,128)(2,1)} %get-tuple-element.38.normed), calls=%async_computation | async-start | bytes 1572864 | tf_op jit(solution)/shard_map/all_to_all | solution.py:583
  39.5 11.0 %collective-permute-start.7 = (bf16[384,384]{1,0:T(8,128)(2,1)S(1)}, bf16[384,384]{1,0:T(8,128)(2,1)S(1)}, u32[]{:S(2)}, u32[]{:S(2)}) collective-permute-start(bf16[384,384]{1,0:T(8,128)(2,1)S(1)} %get-tuple-element.46), channel_id=1, source_target_pairs={{0,1},{1,0},{2,3},{3,2},{4,5},{5,4},{6,7},{7,6},{8,9},{9,8},{10,11... | collective-permute-start | bytes 884744 | tf_op jit(solution)/shard_map/ppermute | solution.py:664
  43.4 2.7 %collective-permute-start.5 = (bf16[128,768]{1,0:T(8,128)(2,1)S(1)}, bf16[128,768]{1,0:T(8,128)(2,1)S(1)}, u32[]{:S(2)}, u32[]{:S(2)}) collective-permute-start(bf16[128,768]{1,0:T(8,128)(2,1)S(1)} %get-tuple-element.44.refs_2_), channel_id=1, source_target_pairs={{0,1},{1,0},{2,3},{3,2},{4,5},{5,4},{6,7},{7,6},{8,9},{9,8},{10,11... | collective-permute-start | bytes 589832 | tf_op jit(solution)/shard_map/ppermute | solution.py:487
  43.5 7.0 %collective-permute-start.6 = (bf16[128,768]{1,0:T(8,128)(2,1)S(1)}, bf16[128,768]{1,0:T(8,128)(2,1)S(1)}, u32[]{:S(2)}, u32[]{:S(2)}) collective-permute-start(bf16[128,768]{1,0:T(8,128)(2,1)S(1)} %get-tuple-element.44.refs_2_), channel_id=1, source_target_pairs={{1,2},{3,4},{5,6},{7,8},{9,10},{11,12},{13,14},{2,1},{4,3},{6,5},{... | collective-permute-start | bytes 589832 | tf_op jit(solution)/shard_map/ppermute | solution.py:488
  45.4 0.7 copy-start.10
  46.1 13.5 %collective-permute-start.9 = (bf16[4,128,768]{2,1,0:T(8,128)(2,1)S(1)}, bf16[4,128,768]{2,1,0:T(8,128)(2,1)S(1)}, u32[]{:S(2)}, u32[]{:S(2)}) collective-permute-start(bf16[4,128,768]{2,1,0:T(8,128)(2,1)S(1)} %get-tuple-element.49.refs_5_), channel_id=1, source_target_pairs={{0,1},{1,0},{2,3},{3,2},{4,5},{5,4},{6,7},{7,6},{8,9},{9,8},{10,11... | collective-permute-start | bytes 2359304 | tf_op jit(solution)/shard_map/ppermute | solution.py:692
  51.3 0.7 copy-start.4
  52.0 0.7 copy-start.6
  52.6 7.0 %collective-permute-start.8 = (bf16[4,128,768]{2,1,0:T(8,128)(2,1)S(1)}, bf16[4,128,768]{2,1,0:T(8,128)(2,1)S(1)}, u32[]{:S(2)}, u32[]{:S(2)}) collective-permute-start(bf16[4,128,768]{2,1,0:T(8,128)(2,1)S(1)} %all-to-all-done.refs_4_), channel_id=1, source_target_pairs={{0,1},{1,0},{2,3},{3,2},{4,5},{5,4},{6,7},{7,6},{8,9},{9,8},{10,11... | collective-permute-start | bytes 2359304 | tf_op jit(solution)/shard_map/ppermute | solution.py:691
  52.6 17.5 %all-to-all-start.1 = ((bf16[8,48,384]{2,1,0:T(8,128)(2,1)}), bf16[8,48,384]{2,1,0:T(8,128)(2,1)S(1)}, u32[]{:S(2)}, u32[]{:S(2)}) async-start(bf16[8,48,384]{2,1,0:T(8,128)(2,1)} %bitcast.8), calls=%async_computation.1 | async-start | bytes 589824 | tf_op jit(solution)/shard_map/all_to_all | solution.py:731
  59.6 6.2 %copy-start.1 = (f32[343,768]{1,0:T(8,128)S(1)}, f32[343,768]{1,0:T(8,128)}, u32[]{:S(2)}) copy-start(f32[343,768]{1,0:T(8,128)} %refs_4_.1) | copy-start | bytes 3161092
  59.6 6.2 %copy-start.5 = (bf16[128,768]{1,0:T(8,128)(2,1)S(1)}, bf16[128,768]{1,0:T(8,128)(2,1)}, u32[]{:S(2)}) copy-start(bf16[128,768]{1,0:T(8,128)(2,1)} %copy-done.4) | copy-start | bytes 589828
  59.6 6.2 %copy-start.7 = (bf16[128,768]{1,0:T(8,128)(2,1)S(1)}, bf16[128,768]{1,0:T(8,128)(2,1)}, u32[]{:S(2)}) copy-start(bf16[128,768]{1,0:T(8,128)(2,1)} %copy-done.6) | copy-start | bytes 589828
  59.6 6.2 %copy-start.9 = (bf16[4,4,8,768]{3,2,1,0:T(8,128)(2,1)S(1)}, bf16[4,4,8,768]{3,2,1,0:T(8,128)(2,1)}, u32[]{:S(2)}) copy-start(bf16[4,4,8,768]{3,2,1,0:T(8,128)(2,1)} %param.15) | copy-start | bytes 589828
  59.6 6.2 %copy-start.11 = (bf16[128,768]{1,0:T(8,128)(2,1)S(1)}, bf16[128,768]{1,0:T(8,128)(2,1)}, u32[]{:S(2)}) copy-start(bf16[128,768]{1,0:T(8,128)(2,1)} %copy-done.10) | copy-start | bytes 589828
  64.3 16.2 %collective-permute-start.10 = (bf16[2,192,768]{2,1,0:T(8,128)(2,1)}, bf16[2,192,768]{2,1,0:T(8,128)(2,1)}, u32[]{:S(2)}, u32[]{:S(2)}) collective-permute-start(bf16[2,192,768]{2,1,0:T(8,128)(2,1)} %weight_grads_far_side.1.refs_6_), channel_id=1, source_target_pairs={{0,2},{1,3},{2,0},{3,1},{4,6},{5,7},{6,4},{7,5},{8,10},{9,11},{10,... | collective-permute-start | bytes 1769480 | tf_op jit(solution)/shard_map/ppermute | solution.py:730
  70.9 14.6 %all-to-all-start.2 = ((bf16[8,48,384]{2,1,0:T(8,128)(2,1)}), bf16[8,48,384]{2,1,0:T(8,128)(2,1)S(1)}, u32[]{:S(2)}, u32[]{:S(2)}) async-start(bf16[8,48,384]{2,1,0:T(8,128)(2,1)} %kernel_grad_sum.1.refs_9_), calls=%async_computation.2 | async-start | bytes 589824 | tf_op jit(solution)/shard_map/all_to_all | solution.py:777
  85.4 3.0 %collective-permute-start.11 = (bf16[8,48,384]{2,1,0:T(8,128)(2,1)S(1)}, bf16[8,48,384]{2,1,0:T(8,128)(2,1)S(1)}, u32[]{:S(2)}, u32[]{:S(2)}) collective-permute-start(bf16[8,48,384]{2,1,0:T(8,128)(2,1)S(1)} %all-to-all-done.2.own), channel_id=1, source_target_pairs={{0,1},{1,0},{2,3},{3,2},{4,5},{5,4},{6,7},{7,6},{8,9},{9,8},{10,11... | collective-permute-start | bytes 884744 | tf_op jit(solution)/shard_map/ppermute | solution.py:784

commit v17 on v16

--- a/solution.py
+++ b/solution.py
@@ -161,9 +161,11 @@
     return [join_outputs([terms[j][x] for j in range(9)]) for x in range(planes)]
 
 
-def own_conv_kernel(planes, height, own, taps, out, split, spread):
+def own_conv_kernel(planes, height, own, taps, gain, bias, out, split, vectors, spread):
     @pl.when(pl.program_id(0) == 0)
     def _():
+        for k, line in enumerate((gain, bias)):
+            vectors[k : k + 1, :] = line[...].reshape(1, -1)
         clear_rims(spread)
 
     stage_source([(own, x) for x in range(planes)], height, spread)
@@ -176,7 +178,7 @@
 
 
 def rim_conv_kernel(
-    planes, height, core, inner, outer, split, partial, gain, bias, normed, centered, spread, conv
+    planes, height, core, inner, outer, split, partial, vectors, normed, centered, spread, conv
 ):
     step = pl.program_id(0)
 
@@ -200,8 +202,8 @@
         tiles = conv.shape[0]
         channels = tiles * LANES
         parts = [conv[k] for k in range(tiles)]
-        gains = gain[...].reshape(1, channels)
-        biases = bias[...].reshape(1, channels)
+        gains = vectors[0:1, :]
+        biases = vectors[1:2, :]
         average = jnp.sum(tree_sum(parts), axis=1, keepdims=True) * (1.0 / channels)
         parts = [part - average for part in parts]
         variance = jnp.sum(
@@ -213,8 +215,7 @@
             centered[:, lanes] = parts[k]
             value = parts[k] * inverse
             whole = (value * gains[:, lanes] + biases[:, lanes]).astype(BF16)
-            for copy in range(normed.shape[0]):
-                normed[copy, :, lanes] = whole
+            normed[:, lanes] = whole
 
 
 def input_grad_kernel(
@@ -375,13 +376,13 @@
     return activated, (act_grad * slope).astype(BF16)
 
 
-def weight_grad_terms(which, weight_in, weight_out, scale, sets, aligned, mixed_grad):
+def weight_grad_terms(weight_in, weight_out, scale, sets, aligned, mixed_grad):
     scales = scale[...].reshape(1, -1)
     at = 0
     for normed, cotangents in sets:
         line, rows = normed.shape[:2]
         for k in range(line):
-            aligned[at : at + rows, :] = normed[which[2 + k]]
+            aligned[at : at + rows, :] = normed[k]
             upstream = cotangents[k].astype(F32)
             mixed_grad[at : at + rows, :] = (scales * upstream).astype(BF16)
             at += rows
@@ -399,7 +400,7 @@
     which, weight_in, weight_out, scale, norm, cot, other_norm, other_cot, sent, aligned, mixed_grad
 ):
     sets = ((norm, cot), (other_norm, other_cot))
-    terms = weight_grad_terms(which, weight_in, weight_out, scale, sets, aligned, mixed_grad)
+    terms = weight_grad_terms(weight_in, weight_out, scale, sets, aligned, mixed_grad)
     for k in range(2):
         sent[k] = terms[k].astype(BF16)
 
@@ -420,13 +421,15 @@
     mixed_grad,
 ):
     sets = ((norm, cot), (other_norm, other_cot))
-    terms = weight_grad_terms(which, weight_in, weight_out, scale, sets, aligned, mixed_grad)
+    terms = weight_grad_terms(weight_in, weight_out, scale, sets, aligned, mixed_grad)
     for k, out in enumerate((in_grad, out_grad)):
         out[...] = terms[k] + got[k].astype(F32)
 
 
-def chip_sum_kernel(kept, got, out, token):
-    token[...] = jnp.zeros(token.shape, F32)
+def chip_sum_kernel(kept, got, *rest):
+    *blocks, out, together = rest
+    for k, block in enumerate(blocks):
+        together[k] = block[...]
     out[...] = (kept[...].astype(F32) + got[...].astype(F32)).astype(BF16)
 
 
@@ -499,7 +502,6 @@
     me = lax.axis_index("row")
     quad = 4
     line = count // quad
-    lines = [[quad * k + p for k in range(line)] for p in range(quad)]
     other_core = [(i, i ^ 1) for i in range(count)]
     other_side = [(i, i ^ 2) for i in range(count)]
     tiles = channels // LANES
@@ -522,25 +524,26 @@
         return pltpu.VMEM((9, held, PAD, LANES), F32)
 
     split_block = pl.BlockSpec((None, 9, KS, SUB, LANES), lambda c, *_: (c, 0, 0, 0, 0))
-    partial, split = pl.pallas_call(
+    partial, split, vectors = pl.pallas_call(
         functools.partial(own_conv_kernel, planes, height),
         grid=(tiles,),
-        in_specs=[lane_block(rows), lane_block(TAP_ROWS)],
-        out_specs=[lane_block(rows), split_block],
+        in_specs=[lane_block(rows), lane_block(TAP_ROWS)] + [whole_block(channels)] * 2,
+        out_specs=[lane_block(rows), split_block, whole_block(SUB, channels)],
         out_shape=[
             jax.ShapeDtypeStruct((rows, channels), F32),
             jax.ShapeDtypeStruct((tiles, 9, KS, SUB, LANES), F32),
+            jax.ShapeDtypeStruct((SUB, channels), F32),
         ],
         scratch_shapes=[spread_of(planes)],
         compiler_params=params(),
         cost_estimate=NO_COST,
         name="own_conv",
-    )(own, dw_kernel)
+    )(own, dw_kernel, norm_gain, norm_bias)
 
     for k in range(2, line - 1):
         upstream_line[k] = along_line(upstream_line[k - 1], 1)
     normed, centered = pl.pallas_call(
-        follow(functools.partial(rim_conv_kernel, planes, height), 1, 6, 2),
+        follow(functools.partial(rim_conv_kernel, planes, height), 1, 5, 2),
         grid_spec=pltpu.PrefetchScalarGridSpec(
             num_scalar_prefetch=1,
             grid=(tiles,),
@@ -549,19 +552,18 @@
                 lane_block(rows),
                 split_block,
                 lane_block(rows),
-                whole_block(channels),
-                whole_block(channels),
+                whole_block(SUB, channels),
                 IN_PLACE,
                 IN_PLACE,
             ],
             out_specs=[
-                whole_block(line, rows, channels),
+                whole_block(rows, channels),
                 whole_block(rows, channels),
             ],
             scratch_shapes=[spread_of(2 * MARGIN), pltpu.VMEM((tiles, rows, LANES), F32)],
         ),
         out_shape=[
-            jax.ShapeDtypeStruct((line, rows, channels), BF16),
+            jax.ShapeDtypeStruct((rows, channels), BF16),
             jax.ShapeDtypeStruct((rows, channels), F32),
         ],
         compiler_params=params(),
@@ -573,16 +575,15 @@
         outer,
         split,
         partial,
-        norm_gain,
-        norm_bias,
+        vectors,
         upstream_line[1],
         upstream_line[-1],
     )
 
     normed, upstream_line[2] = lax.optimization_barrier((normed, upstream_line[2]))
-    gathered = lax.all_to_all(
-        normed, "row", split_axis=0, concat_axis=0, tiled=True, axis_index_groups=lines
-    )
+    norm_line = [normed] + [None] * (line - 1)
+    norm_line[1] = along_line(normed, 1)
+    norm_line[-1] = along_line(normed, -1)
 
     block = 512
     whole = whole_block(rows, channels)
@@ -590,7 +591,7 @@
         mlp_kernel,
         grid=(units // block,),
         in_specs=[
-            pl.BlockSpec((None, rows, channels), lambda f: (0, 0, 0)),
+            whole,
             pl.BlockSpec((block, channels), lambda f: (f, 0)),
             pl.BlockSpec((block, channels), lambda f: (f, 0)),
             whole,
@@ -620,6 +621,12 @@
         name="mlp_both_ways",
     )(normed, weight_in, weight_out, centered, norm_gain, layer_scale, own, *upstream_line)
 
+    small, norm_line[1], norm_line[-1] = lax.optimization_barrier(
+        (small, norm_line[1], norm_line[-1])
+    )
+    for k in range(2, line - 1):
+        norm_line[k] = along_line(norm_line[k - 1], 1)
+
     half = count // 2
     alike = [[2 * k + p for k in range(half)] for p in range(2)]
     half_tiles = tiles // 2
@@ -662,32 +669,29 @@
     )(jnp.stack([core, 1 - core]), inner, own, outer, conv_grad, small)
 
     half_got = lax.ppermute(half_sent, "row", other_core)
+    conv_grad, norm_line[2] = lax.optimization_barrier((conv_grad, norm_line[2]))
     grad_inner, grad_outer = rims(conv_grad)
-    sums, token = pl.pallas_call(
-        follow(chip_sum_kernel, 0, 2, 2),
-        in_specs=[whole_block(padded, wide)] * 2 + [IN_PLACE] * 2,
-        out_specs=[whole_block(padded, wide), whole_block(SUB, LANES)],
+    sums, gathered = pl.pallas_call(
+        follow(chip_sum_kernel, 0, 2 + line, 2),
+        in_specs=[whole_block(padded, wide)] * 2 + [whole] * line + [IN_PLACE] * 2,
+        out_specs=[whole_block(padded, wide), whole_block(line, rows, channels)],
         out_shape=[
             jax.ShapeDtypeStruct((padded, wide), BF16),
-            jax.ShapeDtypeStruct((SUB, LANES), F32),
+            jax.ShapeDtypeStruct((line, rows, channels), BF16),
         ],
         grid=(1,),
         compiler_params=params(),
         cost_estimate=NO_COST,
         name="kernel_grad_chip_sum",
-    )(half_kept, half_got, grad_inner, grad_outer)
-    gathered, token = lax.optimization_barrier((gathered, token))
+    )(half_kept, half_got, *norm_line, grad_inner, grad_outer)
 
     share = units // count
     tokens = line * rows
     base = me // quad * quad
     side = lax.rem(me, quad) // 2
-    place = lax.rem(me // quad + line - jnp.arange(line, dtype=jnp.int32), line)
     far = base + 2 * (1 - side)
     near = base + 2 * side
-    which = jnp.concatenate(
-        [jnp.stack([far + core, near + core]).astype(jnp.int32), place.astype(jnp.int32)]
-    )
+    which = jnp.stack([far + core, near + core]).astype(jnp.int32)
     other_gathered = lax.ppermute(gathered, "row", other_core)
     other_cotangents = lax.ppermute(cotangents, "row", other_core)
 
@@ -725,7 +729,7 @@
     pair = jax.ShapeDtypeStruct((2, share, channels), BF16)
     single = jax.ShapeDtypeStruct((share, channels), F32)
     (sent,) = side_terms(
-        far_side_kernel, 0, [], [sums, token], [pair], "weight_grads_far_side"
+        far_side_kernel, 0, [], [sums], [pair], "weight_grads_far_side"
     )
     got = lax.ppermute(sent, "row", other_side)
     scattered = lax.all_to_all(

time: 90.5 us -> 88.4 us (0.977)
  local copies, waits for them, and re-layouts: 5.58 us -> 3.59 us
  waiting for transfers between devices: 12.5 us -> 14 us
    all_to_all x1 -> x0, starting transfers between devices: 3.97 us -> none  [on_device(): lax.all_to_all(normed, 'row', split_axis=0, concat_axis=0, tiled=True, ax...]
    ppermute x3 -> x6, starting transfers between devices: 4.2 us -> 7.52 us  [along_line(): lax.ppermute(cells, 'row', [(i, (i + quad * steps) % count) for i in rang...]
    unnamed x32, local copies, waits for them, and re-layouts: 5.58 us -> 3.59 us
    pallas_call x1, Pallas kernels: 3.62 us -> 2.7 us  [on_device(): pl.pallas_call(follow(functools.partial(rim_conv_kernel, planes, height),...]
    ppermute x3 -> x6, waiting for transfers between devices: 1.43 us -> 2.3 us  [along_line(): lax.ppermute(cells, 'row', [(i, (i + quad * steps) % count) for i in rang...]
  transfers between devices with their start and end apart: 15 -> 17, of which waited for: 6 -> 5; matrix products, arithmetic and copies ran while one was open for 0% -> 0% of each run, Pallas kernels for 41% -> 41%
where the time goes in v17:
time: 88.4 us; the launch traced here: 87.4 us
  Pallas kernels  37.1 us (42%)
  starting transfers between devices  31.8 us (36%)
  waiting for transfers between devices  14 us (16%)
  local copies, waits for them, and re-layouts  3.59 us (4%)
    pallas_call x2, Pallas kernels, side_terms(): pl.pallas_call(follow(kernel, 1, 7 + len(more), len(after)), grid_spec=pl...  9.51 us
    pallas_call x1, Pallas kernels, on_device(): pl.pallas_call(mlp_kernel, grid=(units // block,), in_specs=[whole, pl.Bl...  9.43 us
    ppermute x6, starting transfers between devices, along_line(): lax.ppermute(cells, 'row', [(i, (i + quad * steps) % count) for i in rang...  7.52 us
    pallas_call x1, Pallas kernels, on_device(): pl.pallas_call(functools.partial(kernel_grad_kernel, planes, height), gri...  6.35 us
    all_to_all x1, starting transfers between devices, on_device(): lax.all_to_all(sums.reshape(half, piece, wide), 'row', split_axis=0, conc...  6.06 us
    ppermute x1, waiting for transfers between devices, on_device(): got = lax.ppermute(sent, 'row', other_side)  5.5 us
    ppermute x2, waiting for transfers between devices, rims(): lax.ppermute(cells, 'row', between + [(j, i) for i, j in between])  4.95 us
    ppermute x2, starting transfers between devices, rims(): lax.ppermute(cells, 'row', between + [(j, i) for i, j in between])  4.93 us
  transfers between devices with their start and end apart: 17, of which 5 were waited for; matrix products, arithmetic and copies ran while one was open for 0% of the time, Pallas kernels for 41%

profile of v17, /device:TPU:1, one launch (start us, length us, event | category | flops | bytes accessed | tf_op | source)
XLA Modules:
  0.0 87.4 jit_solution(1804659063557365190)
XLA Ops:
  0.6 2.2 %collective-permute-start.2 = (bf16[128,768]{1,0:T(8,128)(2,1)}, bf16[128,768]{1,0:T(8,128)(2,1)S(1)}, u32[]{:S(2)}, u32[]{:S(2)}) collective-permute-start(bf16[128,768]{1,0:T(8,128)(2,1)} %bitcast.14), channel_id=1, source_target_pairs={{0,4},{1,5},{2,6},{3,7},{4,8},{5,9},{6,10},{7,11},{8,12},{9,13},{1... | collective-permute-start | bytes 589832 | tf_op jit(solution)/shard_map/ppermute | solution.py:517
  2.8 1.0 %collective-permute-start = (bf16[128,768]{1,0:T(8,128)(2,1)}, bf16[128,768]{1,0:T(8,128)(2,1)S(1)}, u32[]{:S(2)}, u32[]{:S(2)}) collective-permute-start(bf16[128,768]{1,0:T(8,128)(2,1)} %bitcast.9), channel_id=1, source_target_pairs={{0,1},{1,0},{2,3},{3,2},{4,5},{5,4},{6,7},{7,6},{8,9},{9,8},{10,11... | collective-permute-start | bytes 589832 | tf_op jit(solution)/shard_map/ppermute | solution.py:490
  3.8 3.0 %collective-permute-start.1 = (bf16[128,768]{1,0:T(8,128)(2,1)}, bf16[128,768]{1,0:T(8,128)(2,1)S(1)}, u32[]{:S(2)}, u32[]{:S(2)}) collective-permute-start(bf16[128,768]{1,0:T(8,128)(2,1)} %bitcast.10), channel_id=1, source_target_pairs={{1,2},{3,4},{5,6},{7,8},{9,10},{11,12},{13,14},{2,1},{4,3},{6,5},{... | collective-permute-start | bytes 589832 | tf_op jit(solution)/shard_map/ppermute | solution.py:491
  6.8 2.0 %collective-permute-start.3 = (bf16[128,768]{1,0:T(8,128)(2,1)}, bf16[128,768]{1,0:T(8,128)(2,1)S(1)}, u32[]{:S(2)}, u32[]{:S(2)}) collective-permute-start(bf16[128,768]{1,0:T(8,128)(2,1)} %bitcast.15), channel_id=1, source_target_pairs={{0,12},{1,13},{2,14},{3,15},{4,0},{5,1},{6,2},{7,3},{8,4},{9,5},{1... | collective-permute-start | bytes 589832 | tf_op jit(solution)/shard_map/ppermute | solution.py:517
  8.8 0.9 collective-permute-done.2.refs_6_.rest_1_
  9.7 0.0 collective-permute-start.4
  9.7 1.2 %copy-done = f32[343,768]{1,0:T(8,128)S(1)} copy-done((f32[343,768]{1,0:T(8,128)S(1)}, f32[343,768]{1,0:T(8,128)}, u32[]{:S(2)}) %copy-start) | copy-done | bytes 1053720
  10.9 0.9 %copy-done.2 = bf16[4,4,8,768]{3,2,1,0:T(8,128)(2,1)S(1)} copy-done((bf16[4,4,8,768]{3,2,1,0:T(8,128)(2,1)S(1)}, bf16[4,4,8,768]{3,2,1,0:T(8,128)(2,1)}, u32[]{:S(2)}) %copy-start.2) | copy-done | bytes 196632
  11.8 0.7 copy-done.13
  12.5 0.7 copy-done.15
  13.2 2.2 %own_conv.1 = (f32[128,768]{1,0:T(8,128)S(1)}, f32[6,9,7,8,128]{4,3,2,1,0:T(8,128)S(1)}, f32[8,768]{1,0:T(8,128)S(1)}) custom-call(bf16[128,768]{1,0:T(8,128)(2,1)S(1)} %bitcast.11, f32[343,768]{1,0:T(8,128)S(1)} %copy-done, f32[768]{0:T(1024)S(1)} %copy-done.13, f32[768]{0:T(1024)S(1)} %copy-done.15), custom_call_target="tpu_custom_call" | custom-call | tf_op jit(solution)/shard_map/own_conv/pallas_call | solution.py:527
  15.4 0.0 copy-start.3
  15.4 0.0 copy-start.8
  15.4 0.0 copy-start.12
  15.4 0.0 copy-start.14
  15.4 0.0 collective-permute-done.refs_1_.inner
  15.4 0.0 collective-permute-done.1.refs_2_.outer
  15.5 2.7 %rim_conv.1 = (bf16[128,768]{1,0:T(8,128)(2,1)S(1)}, f32[128,768]{1,0:T(8,128)S(1)}) custom-call(s32[1]{0:T(128)} %bitcast.refs_0_.core, bf16[128,768]{1,0:T(8,128)(2,1)S(1)} %collective-permute-done.refs_1_.inner, bf16[128,768]{1,0:T(8,128)(2,1)S(1)} %collective-permute-done.1.refs_2_.outer, f32[6,9,7,8,128]{4,3,2,1,0:T(8,128)S(1)} %get-tuple-element.39.refs_3_, ...), custom_call_target="tpu_custom_call" | custom-call | tf_op jit(solution)/shard_map/rim_conv/pallas_call | solution.py:545
  18.2 1.4 %collective-permute-done.4.rest_2_ = bf16[128,768]{1,0:T(8,128)(2,1)S(1)} collective-permute-done((bf16[128,768]{1,0:T(8,128)(2,1)S(1)}, bf16[128,768]{1,0:T(8,128)(2,1)S(1)}, u32[]{:S(2)}, u32[]{:S(2)}) %collective-permute-start.4) | collective-permute-done | bytes 196640 | tf_op jit(solution)/shard_map/ppermute | solution.py:517
  19.6 0.0 collective-permute-start.5
  19.6 3.3 %collective-permute-start.6 = (bf16[128,768]{1,0:T(8,128)(2,1)S(1)}, bf16[128,768]{1,0:T(8,128)(2,1)S(1)}, u32[]{:S(2)}, u32[]{:S(2)}) collective-permute-start(bf16[128,768]{1,0:T(8,128)(2,1)S(1)} %get-tuple-element.43.normed.refs_2_), channel_id=1, source_target_pairs={{0,12},{1,13},{2,14},{3,15},{4,0},{5,1},{6,2},{7,3},{8,4},{9,5},{1... | collective-permute-start | bytes 589832 | tf_op jit(solution)/shard_map/ppermute | solution.py:517
  22.9 9.4 %mlp_both_ways.1 = (bf16[128,768]{1,0:T(8,128)(2,1)}, bf16[128,768]{1,0:T(8,128)(2,1)S(1)}, f32[8,768]{1,0:T(8,128)S(1)}, bf16[4,128,768]{2,1,0:T(8,128)(2,1)S(1)}) custom-call(bf16[128,768]{1,0:T(8,128)(2,1)S(1)} %get-tuple-element.43.normed.refs_2_, bf16[3072,768]{1,0:T(8,128)(2,1)} %refs_1_.3, bf16[3072,768]{1,0:T(8,128)(2,1)} %refs_2_.3, ...), custom_call_target="tpu_custom_call" | custom-call | tf_op jit(solution)/shard_map/mlp_both_ways/pallas_call | solution.py:590
  32.3 0.0 collective-permute-done.5.refs_3_
  32.3 0.0 collective-permute-done.6.refs_5_
  32.3 0.1 collective-permute-start.7
  32.4 0.1 pad_add_fusion.which
  32.5 6.4 %kernel_grad_terms.1 = (bf16[384,384]{1,0:T(8,128)(2,1)S(1)}, bf16[384,384]{1,0:T(8,128)(2,1)S(1)}, bf16[128,768]{1,0:T(8,128)(2,1)S(1)}) custom-call(s32[2]{0:T(128)S(1)} %pad_add_fusion.which, bf16[128,768]{1,0:T(8,128)(2,1)S(1)} %collective-permute-done.refs_1_.inner, bf16[128,768]{1,0:T(8,128)(2,1)S(1)} %bitcast.13, ...), custom_call_target="tpu_custom_call" | custom-call | tf_op jit(solution)/shard_map/kernel_grad_terms/pallas_call | solution.py:644
  38.8 0.0 copy-start.10
  38.8 3.7 %collective-permute-start.10 = (bf16[384,384]{1,0:T(8,128)(2,1)S(1)}, bf16[384,384]{1,0:T(8,128)(2,1)S(1)}, u32[]{:S(2)}, u32[]{:S(2)}) collective-permute-start(bf16[384,384]{1,0:T(8,128)(2,1)S(1)} %get-tuple-element.54), channel_id=1, source_target_pairs={{0,1},{1,0},{2,3},{3,2},{4,5},{5,4},{6,7},{7,6},{8,9},{9,8},{10,11... | collective-permute-start | bytes 884744 | tf_op jit(solution)/shard_map/ppermute | solution.py:671
  42.6 0.9 %collective-permute-start.8 = (bf16[128,768]{1,0:T(8,128)(2,1)S(1)}, bf16[128,768]{1,0:T(8,128)(2,1)S(1)}, u32[]{:S(2)}, u32[]{:S(2)}) collective-permute-start(bf16[128,768]{1,0:T(8,128)(2,1)S(1)} %get-tuple-element.52.refs_2_), channel_id=1, source_target_pairs={{0,1},{1,0},{2,3},{3,2},{4,5},{5,4},{6,7},{7,6},{8,9},{9,8},{10,11... | collective-permute-start | bytes 589832 | tf_op jit(solution)/shard_map/ppermute | solution.py:490
  43.5 1.9 %collective-permute-start.9 = (bf16[128,768]{1,0:T(8,128)(2,1)S(1)}, bf16[128,768]{1,0:T(8,128)(2,1)S(1)}, u32[]{:S(2)}, u32[]{:S(2)}) collective-permute-start(bf16[128,768]{1,0:T(8,128)(2,1)S(1)} %get-tuple-element.52.refs_2_), channel_id=1, source_target_pairs={{1,2},{3,4},{5,6},{7,8},{9,10},{11,12},{13,14},{2,1},{4,3},{6,5},{... | collective-permute-start | bytes 589832 | tf_op jit(solution)/shard_map/ppermute | solution.py:491
  45.4 0.1 collective-permute-start.12
  45.5 0.0 copy-start.4
  45.6 4.9 %collective-permute-done.9.refs_7_.refs_3_ = bf16[128,768]{1,0:T(8,128)(2,1)S(1)} collective-permute-done((bf16[128,768]{1,0:T(8,128)(2,1)S(1)}, bf16[128,768]{1,0:T(8,128)(2,1)S(1)}, u32[]{:S(2)}, u32[]{:S(2)}) %collective-permute-start.9) | collective-permute-done | bytes 196640 | tf_op jit(solution)/shard_map/ppermute | solution.py:491
  50.5 0.8 kernel_grad_chip_sum.1
  51.3 6.1 %all-to-all-start = ((bf16[8,48,384]{2,1,0:T(8,128)(2,1)}), bf16[8,48,384]{2,1,0:T(8,128)(2,1)S(1)}, u32[]{:S(2)}, u32[]{:S(2)}) async-start(bf16[8,48,384]{2,1,0:T(8,128)(2,1)} %bitcast.8), calls=%async_computation | async-start | bytes 589824 | tf_op jit(solution)/shard_map/all_to_all | solution.py:735
  57.4 0.1 pad_add_fusion.1.refs_0_
  57.5 0.0 copy-start.11
  57.5 4.7 %weight_grads_far_side.1.refs_6_ = bf16[2,192,768]{2,1,0:T(8,128)(2,1)} custom-call(s32[2]{0:T(128)S(1)} %pad_add_fusion.1.refs_0_, bf16[3072,768]{1,0:T(8,128)(2,1)} %refs_1_.3, bf16[3072,768]{1,0:T(8,128)(2,1)} %refs_2_.3, f32[768]{0:T(1024)S(1)} %copy-done.12, bf16[4,128,768]{2,1,0:T(8,128)(2,1)S(1)} %get-tuple-element.57.refs_4_, ...), custom_call_target="tpu_custom_call" | custom-call | tf_op jit(solution)/shard_map/weight_grads_far_side/pallas_call | solution.py:700
  62.2 1.5 %collective-permute-start.13 = (bf16[2,192,768]{2,1,0:T(8,128)(2,1)}, bf16[2,192,768]{2,1,0:T(8,128)(2,1)}, u32[]{:S(2)}, u32[]{:S(2)}) collective-permute-start(bf16[2,192,768]{2,1,0:T(8,128)(2,1)} %weight_grads_far_side.1.refs_6_), channel_id=1, source_target_pairs={{0,2},{1,3},{2,0},{3,1},{4,6},{5,7},{6,4},{7,5},{8,10},{9,11},{10,... | collective-permute-start | bytes 1769480 | tf_op jit(solution)/shard_map/ppermute | solution.py:734
  63.7 4.3 %input_grad_conv.1 = (bf16[128,768]{1,0:T(8,128)(2,1)}, f32[8,128]{1,0:T(8,128)S(1)}) custom-call(s32[1]{0:T(128)} %bitcast.refs_0_.core, bf16[128,768]{1,0:T(8,128)(2,1)S(1)} %copy-done.5, bf16[128,768]{1,0:T(8,128)(2,1)S(1)} %copy-done.11, bf16[128,768]{1,0:T(8,128)(2,1)S(1)} %copy-done.7, f32[343,768]{1,0:T(8,128)S(1)} %copy-done.1, ...), custom_call_target="tpu_custom_call" | custom-call | tf_op jit(solution)/shard_map/input_grad_conv/pallas_call | solution.py:743
  68.0 0.8 kernel_grad_sum.1.refs_9_
  68.7 4.3 %all-to-all-start.1 = ((bf16[8,48,384]{2,1,0:T(8,128)(2,1)}), bf16[8,48,384]{2,1,0:T(8,128)(2,1)S(1)}, u32[]{:S(2)}, u32[]{:S(2)}) async-start(bf16[8,48,384]{2,1,0:T(8,128)(2,1)} %kernel_grad_sum.1.refs_9_), calls=%async_computation.1 | async-start | bytes 589824 | tf_op jit(solution)/shard_map/all_to_all | solution.py:781
  73.0 5.5 %collective-permute-done.13.refs_8_ = bf16[2,192,768]{2,1,0:T(8,128)(2,1)} collective-permute-done((bf16[2,192,768]{2,1,0:T(8,128)(2,1)}, bf16[2,192,768]{2,1,0:T(8,128)(2,1)}, u32[]{:S(2)}, u32[]{:S(2)}) %collective-permute-start.13) | collective-permute-done | bytes 589856 | tf_op jit(solution)/shard_map/ppermute | solution.py:734
  78.5 4.9 %weight_grads_near_side.1 = (f32[192,768]{1,0:T(8,128)}, f32[192,768]{1,0:T(8,128)}) custom-call(s32[2]{0:T(128)S(1)} %pad_add_fusion.1.refs_0_, bf16[3072,768]{1,0:T(8,128)(2,1)} %refs_1_.3, bf16[3072,768]{1,0:T(8,128)(2,1)} %refs_2_.3, f32[768]{0:T(1024)S(1)} %copy-done.12, bf16[4,128,768]{2,1,0:T(8,128)(2,1)S(1)} %get-tuple-element.57.refs_4_, ...), custom_call_target="tpu_custom_call" | custom-call | tf_op jit(solution)/shard_map/weight_grads_near_side/pallas_call | solution.py:700
  83.4 1.8 %collective-permute-start.14 = (bf16[8,48,384]{2,1,0:T(8,128)(2,1)S(1)}, bf16[8,48,384]{2,1,0:T(8,128)(2,1)S(1)}, u32[]{:S(2)}, u32[]{:S(2)}) collective-permute-start(bf16[8,48,384]{2,1,0:T(8,128)(2,1)S(1)} %all-to-all-done.1.own), channel_id=1, source_target_pairs={{0,1},{1,0},{2,3},{3,2},{4,5},{5,4},{6,7},{7,6},{8,9},{9,8},{10,11... | collective-permute-start | bytes 884744 | tf_op jit(solution)/shard_map/ppermute | solution.py:788
  85.2 1.2 %collective-permute-done.14.other = bf16[8,48,384]{2,1,0:T(8,128)(2,1)S(1)} collective-permute-done((bf16[8,48,384]{2,1,0:T(8,128)(2,1)S(1)}, bf16[8,48,384]{2,1,0:T(8,128)(2,1)S(1)}, u32[]{:S(2)}, u32[]{:S(2)}) %collective-permute-start.14) | collective-permute-done | bytes 294944 | tf_op jit(solution)/shard_map/ppermute | solution.py:788
  86.4 1.1 %kernel_grad_unpack.1 = (f32[343,768]{1,0:T(8,128)}, f32[768]{0:T(1024)}, f32[768]{0:T(1024)}, f32[768]{0:T(1024)}) custom-call(s32[1]{0:T(128)} %bitcast.refs_0_.core, bf16[8,48,384]{2,1,0:T(8,128)(2,1)S(1)} %all-to-all-done.1.own, bf16[8,48,384]{2,1,0:T(8,128)(2,1)S(1)} %collective-permute-done.14.other), custom_call_target="tpu_custom_call" | custom-call | tf_op jit(solution)/shard_map/kernel_grad_unpack/pallas_call | solution.py:789
  (30 shorter events, 0.1 us)
Async XLA Ops:
  0.6 9.0 %collective-permute-start.2 = (bf16[128,768]{1,0:T(8,128)(2,1)}, bf16[128,768]{1,0:T(8,128)(2,1)S(1)}, u32[]{:S(2)}, u32[]{:S(2)}) collective-permute-start(bf16[128,768]{1,0:T(8,128)(2,1)} %bitcast.14), channel_id=1, source_target_pairs={{0,4},{1,5},{2,6},{3,7},{4,8},{5,9},{6,10},{7,11},{8,12},{9,13},{1... | collective-permute-start | bytes 589832 | tf_op jit(solution)/shard_map/ppermute | solution.py:517
  2.8 12.6 %collective-permute-start = (bf16[128,768]{1,0:T(8,128)(2,1)}, bf16[128,768]{1,0:T(8,128)(2,1)S(1)}, u32[]{:S(2)}, u32[]{:S(2)}) collective-permute-start(bf16[128,768]{1,0:T(8,128)(2,1)} %bitcast.9), channel_id=1, source_target_pairs={{0,1},{1,0},{2,3},{3,2},{4,5},{5,4},{6,7},{7,6},{8,9},{9,8},{10,11... | collective-permute-start | bytes 589832 | tf_op jit(solution)/shard_map/ppermute | solution.py:490
  3.8 11.7 %collective-permute-start.1 = (bf16[128,768]{1,0:T(8,128)(2,1)}, bf16[128,768]{1,0:T(8,128)(2,1)S(1)}, u32[]{:S(2)}, u32[]{:S(2)}) collective-permute-start(bf16[128,768]{1,0:T(8,128)(2,1)} %bitcast.10), channel_id=1, source_target_pairs={{1,2},{3,4},{5,6},{7,8},{9,10},{11,12},{13,14},{2,1},{4,3},{6,5},{... | collective-permute-start | bytes 589832 | tf_op jit(solution)/shard_map/ppermute | solution.py:491
  6.8 8.6 %collective-permute-start.3 = (bf16[128,768]{1,0:T(8,128)(2,1)}, bf16[128,768]{1,0:T(8,128)(2,1)S(1)}, u32[]{:S(2)}, u32[]{:S(2)}) collective-permute-start(bf16[128,768]{1,0:T(8,128)(2,1)} %bitcast.15), channel_id=1, source_target_pairs={{0,12},{1,13},{2,14},{3,15},{4,0},{5,1},{6,2},{7,3},{8,4},{9,5},{1... | collective-permute-start | bytes 589832 | tf_op jit(solution)/shard_map/ppermute | solution.py:517
  9.7 9.9 %collective-permute-start.4 = (bf16[128,768]{1,0:T(8,128)(2,1)S(1)}, bf16[128,768]{1,0:T(8,128)(2,1)S(1)}, u32[]{:S(2)}, u32[]{:S(2)}) collective-permute-start(bf16[128,768]{1,0:T(8,128)(2,1)S(1)} %collective-permute-done.2.refs_6_.rest_1_), channel_id=1, source_target_pairs={{0,4},{1,5},{2,6},{3,7},{4,8},{5,9},{6,10},{7,11},{8,12},{9,13},{1... | collective-permute-start | bytes 589832 | tf_op jit(solution)/shard_map/ppermute | solution.py:517
  9.7 1.2 %copy-start = (f32[343,768]{1,0:T(8,128)S(1)}, f32[343,768]{1,0:T(8,128)}, u32[]{:S(2)}) copy-start(f32[343,768]{1,0:T(8,128)} %refs_4_.1) | copy-start | bytes 3161092
  10.9 0.9 %copy-start.2 = (bf16[4,4,8,768]{3,2,1,0:T(8,128)(2,1)S(1)}, bf16[4,4,8,768]{3,2,1,0:T(8,128)(2,1)}, u32[]{:S(2)}) copy-start(bf16[4,4,8,768]{3,2,1,0:T(8,128)(2,1)} %param.8) | copy-start | bytes 589828
  11.8 0.7 copy-start.13
  12.5 0.7 copy-start.15
  15.4 7.5 %copy-start.3 = (bf16[4,4,8,768]{3,2,1,0:T(8,128)(2,1)S(1)}, bf16[4,4,8,768]{3,2,1,0:T(8,128)(2,1)}, u32[]{:S(2)}) copy-start(bf16[4,4,8,768]{3,2,1,0:T(8,128)(2,1)} %param.8) | copy-start | bytes 589828
  15.4 7.5 %copy-start.8 = (bf16[4,4,8,768]{3,2,1,0:T(8,128)(2,1)S(1)}, bf16[4,4,8,768]{3,2,1,0:T(8,128)(2,1)}, u32[]{:S(2)}) copy-start(bf16[4,4,8,768]{3,2,1,0:T(8,128)(2,1)} %param.15) | copy-start | bytes 589828
  15.4 7.5 %copy-start.12 = (f32[768]{0:T(1024)S(1)}, f32[768]{0:T(1024)}, u32[]{:S(2)}) copy-start(f32[768]{0:T(1024)} %refs_3_.3) | copy-start | bytes 9220
  15.4 7.5 %copy-start.14 = (f32[768]{0:T(1024)S(1)}, f32[768]{0:T(1024)}, u32[]{:S(2)}) copy-start(f32[768]{0:T(1024)} %norm_gain.1) | copy-start | bytes 9220
  19.6 12.7 %collective-permute-start.5 = (bf16[128,768]{1,0:T(8,128)(2,1)S(1)}, bf16[128,768]{1,0:T(8,128)(2,1)S(1)}, u32[]{:S(2)}, u32[]{:S(2)}) collective-permute-start(bf16[128,768]{1,0:T(8,128)(2,1)S(1)} %get-tuple-element.43.normed.refs_2_), channel_id=1, source_target_pairs={{0,4},{1,5},{2,6},{3,7},{4,8},{5,9},{6,10},{7,11},{8,12},{9,13},{1... | collective-permute-start | bytes 589832 | tf_op jit(solution)/shard_map/ppermute | solution.py:517
  19.6 12.7 %collective-permute-start.6 = (bf16[128,768]{1,0:T(8,128)(2,1)S(1)}, bf16[128,768]{1,0:T(8,128)(2,1)S(1)}, u32[]{:S(2)}, u32[]{:S(2)}) collective-permute-start(bf16[128,768]{1,0:T(8,128)(2,1)S(1)} %get-tuple-element.43.normed.refs_2_), channel_id=1, source_target_pairs={{0,12},{1,13},{2,14},{3,15},{4,0},{5,1},{6,2},{7,3},{8,4},{9,5},{1... | collective-permute-start | bytes 589832 | tf_op jit(solution)/shard_map/ppermute | solution.py:517
  32.3 10.3 %collective-permute-start.7 = (bf16[128,768]{1,0:T(8,128)(2,1)S(1)}, bf16[128,768]{1,0:T(8,128)(2,1)S(1)}, u32[]{:S(2)}, u32[]{:S(2)}) collective-permute-start(bf16[128,768]{1,0:T(8,128)(2,1)S(1)} %collective-permute-done.5.refs_3_), channel_id=1, source_target_pairs={{0,4},{1,5},{2,6},{3,7},{4,8},{5,9},{6,10},{7,11},{8,12},{9,13},{1... | collective-permute-start | bytes 589832 | tf_op jit(solution)/shard_map/ppermute | solution.py:517
  38.8 12.5 %copy-start.10 = (bf16[128,768]{1,0:T(8,128)(2,1)}, bf16[128,768]{1,0:T(8,128)(2,1)S(1)}, u32[]{:S(2)}) copy-start(bf16[128,768]{1,0:T(8,128)(2,1)S(1)} %get-tuple-element.52.refs_2_) | copy-start | bytes 589828
  38.8 6.7 %collective-permute-start.10 = (bf16[384,384]{1,0:T(8,128)(2,1)S(1)}, bf16[384,384]{1,0:T(8,128)(2,1)S(1)}, u32[]{:S(2)}, u32[]{:S(2)}) collective-permute-start(bf16[384,384]{1,0:T(8,128)(2,1)S(1)} %get-tuple-element.54), channel_id=1, source_target_pairs={{0,1},{1,0},{2,3},{3,2},{4,5},{5,4},{6,7},{7,6},{8,9},{9,8},{10,11... | collective-permute-start | bytes 884744 | tf_op jit(solution)/shard_map/ppermute | solution.py:671
  42.6 3.0 %collective-permute-start.8 = (bf16[128,768]{1,0:T(8,128)(2,1)S(1)}, bf16[128,768]{1,0:T(8,128)(2,1)S(1)}, u32[]{:S(2)}, u32[]{:S(2)}) collective-permute-start(bf16[128,768]{1,0:T(8,128)(2,1)S(1)} %get-tuple-element.52.refs_2_), channel_id=1, source_target_pairs={{0,1},{1,0},{2,3},{3,2},{4,5},{5,4},{6,7},{7,6},{8,9},{9,8},{10,11... | collective-permute-start | bytes 589832 | tf_op jit(solution)/shard_map/ppermute | solution.py:490
  43.5 7.0 %collective-permute-start.9 = (bf16[128,768]{1,0:T(8,128)(2,1)S(1)}, bf16[128,768]{1,0:T(8,128)(2,1)S(1)}, u32[]{:S(2)}, u32[]{:S(2)}) collective-permute-start(bf16[128,768]{1,0:T(8,128)(2,1)S(1)} %get-tuple-element.52.refs_2_), channel_id=1, source_target_pairs={{1,2},{3,4},{5,6},{7,8},{9,10},{11,12},{13,14},{2,1},{4,3},{6,5},{... | collective-permute-start | bytes 589832 | tf_op jit(solution)/shard_map/ppermute | solution.py:491
  45.4 12.1 %collective-permute-start.12 = (bf16[4,128,768]{2,1,0:T(8,128)(2,1)S(1)}, bf16[4,128,768]{2,1,0:T(8,128)(2,1)S(1)}, u32[]{:S(2)}, u32[]{:S(2)}) collective-permute-start(bf16[4,128,768]{2,1,0:T(8,128)(2,1)S(1)} %get-tuple-element.58.refs_5_), channel_id=1, source_target_pairs={{0,1},{1,0},{2,3},{3,2},{4,5},{5,4},{6,7},{7,6},{8,9},{9,8},{10,11... | collective-permute-start | bytes 2359304 | tf_op jit(solution)/shard_map/ppermute | solution.py:696
  45.5 5.8 %copy-start.4 = (bf16[128,768]{1,0:T(8,128)(2,1)}, bf16[128,768]{1,0:T(8,128)(2,1)S(1)}, u32[]{:S(2)}) copy-start(bf16[128,768]{1,0:T(8,128)(2,1)S(1)} %collective-permute-done.8.refs_6_.refs_1_) | copy-start | bytes 589828
  50.5 0.8 copy-start.6
  51.3 6.2 %collective-permute-start.11 = (bf16[4,128,768]{2,1,0:T(8,128)(2,1)S(1)}, bf16[4,128,768]{2,1,0:T(8,128)(2,1)S(1)}, u32[]{:S(2)}, u32[]{:S(2)}) collective-permute-start(bf16[4,128,768]{2,1,0:T(8,128)(2,1)S(1)} %get-tuple-element.57.refs_4_), channel_id=1, source_target_pairs={{0,1},{1,0},{2,3},{3,2},{4,5},{5,4},{6,7},{7,6},{8,9},{9,8},{10,11... | collective-permute-start | bytes 2359304 | tf_op jit(solution)/shard_map/ppermute | solution.py:695
  51.3 16.6 %all-to-all-start = ((bf16[8,48,384]{2,1,0:T(8,128)(2,1)}), bf16[8,48,384]{2,1,0:T(8,128)(2,1)S(1)}, u32[]{:S(2)}, u32[]{:S(2)}) async-start(bf16[8,48,384]{2,1,0:T(8,128)(2,1)} %bitcast.8), calls=%async_computation | async-start | bytes 589824 | tf_op jit(solution)/shard_map/all_to_all | solution.py:735
  57.5 6.2 %copy-start.1 = (f32[343,768]{1,0:T(8,128)S(1)}, f32[343,768]{1,0:T(8,128)}, u32[]{:S(2)}) copy-start(f32[343,768]{1,0:T(8,128)} %refs_4_.1) | copy-start | bytes 3161092
  57.5 6.2 %copy-start.5 = (bf16[128,768]{1,0:T(8,128)(2,1)S(1)}, bf16[128,768]{1,0:T(8,128)(2,1)}, u32[]{:S(2)}) copy-start(bf16[128,768]{1,0:T(8,128)(2,1)} %copy-done.4) | copy-start | bytes 589828
  57.5 6.2 %copy-start.7 = (bf16[128,768]{1,0:T(8,128)(2,1)S(1)}, bf16[128,768]{1,0:T(8,128)(2,1)}, u32[]{:S(2)}) copy-start(bf16[128,768]{1,0:T(8,128)(2,1)} %copy-done.6) | copy-start | bytes 589828
  57.5 6.2 %copy-start.9 = (bf16[4,4,8,768]{3,2,1,0:T(8,128)(2,1)S(1)}, bf16[4,4,8,768]{3,2,1,0:T(8,128)(2,1)}, u32[]{:S(2)}) copy-start(bf16[4,4,8,768]{3,2,1,0:T(8,128)(2,1)} %param.15) | copy-start | bytes 589828
  57.5 6.2 %copy-start.11 = (bf16[128,768]{1,0:T(8,128)(2,1)S(1)}, bf16[128,768]{1,0:T(8,128)(2,1)}, u32[]{:S(2)}) copy-start(bf16[128,768]{1,0:T(8,128)(2,1)} %copy-done.10) | copy-start | bytes 589828
  62.2 16.3 %collective-permute-start.13 = (bf16[2,192,768]{2,1,0:T(8,128)(2,1)}, bf16[2,192,768]{2,1,0:T(8,128)(2,1)}, u32[]{:S(2)}, u32[]{:S(2)}) collective-permute-start(bf16[2,192,768]{2,1,0:T(8,128)(2,1)} %weight_grads_far_side.1.refs_6_), channel_id=1, source_target_pairs={{0,2},{1,3},{2,0},{3,1},{4,6},{5,7},{6,4},{7,5},{8,10},{9,11},{10,... | collective-permute-start | bytes 1769480 | tf_op jit(solution)/shard_map/ppermute | solution.py:734
  68.7 14.6 %all-to-all-start.1 = ((bf16[8,48,384]{2,1,0:T(8,128)(2,1)}), bf16[8,48,384]{2,1,0:T(8,128)(2,1)S(1)}, u32[]{:S(2)}, u32[]{:S(2)}) async-start(bf16[8,48,384]{2,1,0:T(8,128)(2,1)} %kernel_grad_sum.1.refs_9_), calls=%async_computation.1 | async-start | bytes 589824 | tf_op jit(solution)/shard_map/all_to_all | solution.py:781
  83.4 3.0 %collective-permute-start.14 = (bf16[8,48,384]{2,1,0:T(8,128)(2,1)S(1)}, bf16[8,48,384]{2,1,0:T(8,128)(2,1)S(1)}, u32[]{:S(2)}, u32[]{:S(2)}) collective-permute-start(bf16[8,48,384]{2,1,0:T(8,128)(2,1)S(1)} %all-to-all-done.1.own), channel_id=1, source_target_pairs={{0,1},{1,0},{2,3},{3,2},{4,5},{5,4},{6,7},{7,6},{8,9},{9,8},{10,11... | collective-permute-start | bytes 884744 | tf_op jit(solution)/shard_map/ppermute | solution.py:788

commit v18 on v17

--- a/solution.py
+++ b/solution.py
@@ -250,14 +250,11 @@
     small,
     sent,
     kept,
-    passed,
     spread,
     products,
     joined,
     flat,
 ):
-    passed[...] = grads[...]
-
     @pl.when(pl.program_id(0) == 0)
     def _():
         clear_rims(spread)
@@ -627,6 +624,8 @@
     for k in range(2, line - 1):
         norm_line[k] = along_line(norm_line[k - 1], 1)
 
+    grad_inner, grad_outer = rims(conv_grad)
+
     half = count // 2
     alike = [[2 * k + p for k in range(half)] for p in range(2)]
     half_tiles = tiles // 2
@@ -641,7 +640,7 @@
 
         return pl.BlockSpec((block_rows, LANES), at)
 
-    half_sent, half_kept, conv_grad = pl.pallas_call(
+    half_sent, half_kept = pl.pallas_call(
         functools.partial(kernel_grad_kernel, planes, height),
         grid_spec=pltpu.PrefetchScalarGridSpec(
             num_scalar_prefetch=1,
@@ -650,7 +649,6 @@
             out_specs=[
                 pl.BlockSpec((padded, LANES), lambda c, w: (0, jnp.minimum(c, half_tiles - 1))),
                 pl.BlockSpec((padded, LANES), lambda c, w: (0, jnp.maximum(c - half_tiles, 0))),
-                tile_of(rows),
             ],
             scratch_shapes=[
                 spread_of(2 * MARGIN + planes),
@@ -659,21 +657,19 @@
                 pltpu.VMEM((padded, LANES), F32),
             ],
         ),
-        out_shape=[jax.ShapeDtypeStruct((padded, wide), BF16)] * 2
-        + [
-            jax.ShapeDtypeStruct((rows, channels), BF16),
-        ],
+        out_shape=[jax.ShapeDtypeStruct((padded, wide), BF16)] * 2,
         compiler_params=params(),
         cost_estimate=NO_COST,
         name="kernel_grad_terms",
     )(jnp.stack([core, 1 - core]), inner, own, outer, conv_grad, small)
 
+    half_sent, norm_line[2], grad_inner, grad_outer = lax.optimization_barrier(
+        (half_sent, norm_line[2], grad_inner, grad_outer)
+    )
     half_got = lax.ppermute(half_sent, "row", other_core)
-    conv_grad, norm_line[2] = lax.optimization_barrier((conv_grad, norm_line[2]))
-    grad_inner, grad_outer = rims(conv_grad)
     sums, gathered = pl.pallas_call(
-        follow(chip_sum_kernel, 0, 2 + line, 2),
-        in_specs=[whole_block(padded, wide)] * 2 + [whole] * line + [IN_PLACE] * 2,
+        chip_sum_kernel,
+        in_specs=[whole_block(padded, wide)] * 2 + [whole] * line,
         out_specs=[whole_block(padded, wide), whole_block(line, rows, channels)],
         out_shape=[
             jax.ShapeDtypeStruct((padded, wide), BF16),
@@ -683,7 +679,7 @@
         compiler_params=params(),
         cost_estimate=NO_COST,
         name="kernel_grad_chip_sum",
-    )(half_kept, half_got, *norm_line, grad_inner, grad_outer)
+    )(half_kept, half_got, *norm_line)
 
     share = units // count
     tokens = line * rows

time: 88.4 us -> 85.9 us (0.972)
  waiting for transfers between devices: 14 us -> 10.8 us
  local copies, waits for them, and re-layouts: 3.59 us -> 4.93 us
    ppermute x2, waiting for transfers between devices: 4.95 us -> 0.01 us  [rims(): lax.ppermute(cells, 'row', between + [(j, i) for i, j in between])]
    ppermute x1, starting transfers between devices: 3.74 us -> 0.21 us  [on_device(): half_got = lax.ppermute(half_sent, 'row', other_core)]
    ppermute x2, starting transfers between devices: 1.9 us -> 4.64 us  [rims(): lax.ppermute(cells, 'row', [(i, i ^ 1) for i in range(count)])]
    unnamed x32, local copies, waits for them, and re-layouts: 3.59 us -> 4.93 us
    ppermute x1, waiting for transfers between devices: 0.01 us -> 1.07 us  [on_device(): half_got = lax.ppermute(half_sent, 'row', other_core)]
  transfers between devices with their start and end apart: 17 -> 17, of which waited for: 5 -> 6; matrix products, arithmetic and copies ran while one was open for 0% -> 0% of each run, Pallas kernels for 41% -> 42%
where the time goes in v18:
time: 85.9 us; the launch traced here: 84.9 us
  Pallas kernels  36.9 us (43%)
  starting transfers between devices  31.3 us (36%)
  waiting for transfers between devices  10.8 us (13%)
  local copies, waits for them, and re-layouts  4.93 us (6%)
    pallas_call x2, Pallas kernels, side_terms(): pl.pallas_call(follow(kernel, 1, 7 + len(more), len(after)), grid_spec=pl...  9.51 us
    pallas_call x1, Pallas kernels, on_device(): pl.pallas_call(mlp_kernel, grid=(units // block,), in_specs=[whole, pl.Bl...  9.43 us
    ppermute x6, starting transfers between devices, along_line(): lax.ppermute(cells, 'row', [(i, (i + quad * steps) % count) for i in rang...  7.52 us
    pallas_call x1, Pallas kernels, on_device(): pl.pallas_call(functools.partial(kernel_grad_kernel, planes, height), gri...  6.18 us
    ppermute x1, waiting for transfers between devices, on_device(): got = lax.ppermute(sent, 'row', other_side)  5.84 us
    all_to_all x1, starting transfers between devices, on_device(): lax.all_to_all(sums.reshape(half, piece, wide), 'row', split_axis=0, conc...  5.79 us
    ppermute x2, starting transfers between devices, rims(): lax.ppermute(cells, 'row', between + [(j, i) for i, j in between])  4.93 us
    unnamed x32, local copies, waits for them, and re-layouts  4.93 us
  transfers between devices with their start and end apart: 17, of which 6 were waited for; matrix products, arithmetic and copies ran while one was open for 0% of the time, Pallas kernels for 42%

profile of v18, /device:TPU:1, one launch (start us, length us, event | category | flops | bytes accessed | tf_op | source)
XLA Modules:
  0.0 84.9 jit_solution(11346862915456151674)
XLA Ops:
  0.6 2.2 %collective-permute-start.2 = (bf16[128,768]{1,0:T(8,128)(2,1)}, bf16[128,768]{1,0:T(8,128)(2,1)S(1)}, u32[]{:S(2)}, u32[]{:S(2)}) collective-permute-start(bf16[128,768]{1,0:T(8,128)(2,1)} %bitcast.14), channel_id=1, source_target_pairs={{0,4},{1,5},{2,6},{3,7},{4,8},{5,9},{6,10},{7,11},{8,12},{9,13},{1... | collective-permute-start | bytes 589832 | tf_op jit(solution)/shard_map/ppermute | solution.py:514
  2.8 1.0 %collective-permute-start = (bf16[128,768]{1,0:T(8,128)(2,1)}, bf16[128,768]{1,0:T(8,128)(2,1)S(1)}, u32[]{:S(2)}, u32[]{:S(2)}) collective-permute-start(bf16[128,768]{1,0:T(8,128)(2,1)} %bitcast.9), channel_id=1, source_target_pairs={{0,1},{1,0},{2,3},{3,2},{4,5},{5,4},{6,7},{7,6},{8,9},{9,8},{10,11... | collective-permute-start | bytes 589832 | tf_op jit(solution)/shard_map/ppermute | solution.py:487
  3.8 3.0 %collective-permute-start.1 = (bf16[128,768]{1,0:T(8,128)(2,1)}, bf16[128,768]{1,0:T(8,128)(2,1)S(1)}, u32[]{:S(2)}, u32[]{:S(2)}) collective-permute-start(bf16[128,768]{1,0:T(8,128)(2,1)} %bitcast.10), channel_id=1, source_target_pairs={{1,2},{3,4},{5,6},{7,8},{9,10},{11,12},{13,14},{2,1},{4,3},{6,5},{... | collective-permute-start | bytes 589832 | tf_op jit(solution)/shard_map/ppermute | solution.py:488
  6.8 2.0 %collective-permute-start.3 = (bf16[128,768]{1,0:T(8,128)(2,1)}, bf16[128,768]{1,0:T(8,128)(2,1)S(1)}, u32[]{:S(2)}, u32[]{:S(2)}) collective-permute-start(bf16[128,768]{1,0:T(8,128)(2,1)} %bitcast.15), channel_id=1, source_target_pairs={{0,12},{1,13},{2,14},{3,15},{4,0},{5,1},{6,2},{7,3},{8,4},{9,5},{1... | collective-permute-start | bytes 589832 | tf_op jit(solution)/shard_map/ppermute | solution.py:514
  8.8 0.9 %collective-permute-done.2.refs_6_.rest_1_ = bf16[128,768]{1,0:T(8,128)(2,1)S(1)} collective-permute-done((bf16[128,768]{1,0:T(8,128)(2,1)}, bf16[128,768]{1,0:T(8,128)(2,1)S(1)}, u32[]{:S(2)}, u32[]{:S(2)}) %collective-permute-start.2) | collective-permute-done | bytes 196640 | tf_op jit(solution)/shard_map/ppermute | solution.py:514
  9.7 0.0 collective-permute-start.4
  9.7 1.2 %copy-done = f32[343,768]{1,0:T(8,128)S(1)} copy-done((f32[343,768]{1,0:T(8,128)S(1)}, f32[343,768]{1,0:T(8,128)}, u32[]{:S(2)}) %copy-start) | copy-done | bytes 1053720
  10.9 0.9 %copy-done.2 = bf16[4,4,8,768]{3,2,1,0:T(8,128)(2,1)S(1)} copy-done((bf16[4,4,8,768]{3,2,1,0:T(8,128)(2,1)S(1)}, bf16[4,4,8,768]{3,2,1,0:T(8,128)(2,1)}, u32[]{:S(2)}) %copy-start.2) | copy-done | bytes 196632
  11.8 0.7 copy-done.13
  12.5 0.7 copy-done.15
  13.2 2.2 %own_conv.1 = (f32[128,768]{1,0:T(8,128)S(1)}, f32[6,9,7,8,128]{4,3,2,1,0:T(8,128)S(1)}, f32[8,768]{1,0:T(8,128)S(1)}) custom-call(bf16[128,768]{1,0:T(8,128)(2,1)S(1)} %bitcast.11, f32[343,768]{1,0:T(8,128)S(1)} %copy-done, f32[768]{0:T(1024)S(1)} %copy-done.13, f32[768]{0:T(1024)S(1)} %copy-done.15), custom_call_target="tpu_custom_call" | custom-call | tf_op jit(solution)/shard_map/own_conv/pallas_call | solution.py:524
  15.4 0.0 copy-start.3
  15.4 0.0 copy-start.6
  15.4 0.0 copy-start.12
  15.4 0.0 copy-start.14
  15.4 0.0 collective-permute-done.1.refs_2_.outer
  15.4 0.0 collective-permute-done.3.refs_7_.rest_3_
  15.5 2.7 %rim_conv.1 = (bf16[128,768]{1,0:T(8,128)(2,1)S(1)}, f32[128,768]{1,0:T(8,128)S(1)}) custom-call(s32[1]{0:T(128)} %bitcast.refs_0_.core, bf16[128,768]{1,0:T(8,128)(2,1)S(1)} %collective-permute-done.refs_1_.inner, bf16[128,768]{1,0:T(8,128)(2,1)S(1)} %collective-permute-done.1.refs_2_.outer, f32[6,9,7,8,128]{4,3,2,1,0:T(8,128)S(1)} %get-tuple-element.40.refs_3_, ...), custom_call_target="tpu_custom_call" | custom-call | tf_op jit(solution)/shard_map/rim_conv/pallas_call | solution.py:542
  18.2 1.4 %collective-permute-done.4.rest_2_ = bf16[128,768]{1,0:T(8,128)(2,1)S(1)} collective-permute-done((bf16[128,768]{1,0:T(8,128)(2,1)S(1)}, bf16[128,768]{1,0:T(8,128)(2,1)S(1)}, u32[]{:S(2)}, u32[]{:S(2)}) %collective-permute-start.4) | collective-permute-done | bytes 196640 | tf_op jit(solution)/shard_map/ppermute | solution.py:514
  19.6 0.0 collective-permute-start.5
  19.6 3.3 %collective-permute-start.6 = (bf16[128,768]{1,0:T(8,128)(2,1)S(1)}, bf16[128,768]{1,0:T(8,128)(2,1)S(1)}, u32[]{:S(2)}, u32[]{:S(2)}) collective-permute-start(bf16[128,768]{1,0:T(8,128)(2,1)S(1)} %get-tuple-element.44.normed.rest_0_), channel_id=1, source_target_pairs={{0,12},{1,13},{2,14},{3,15},{4,0},{5,1},{6,2},{7,3},{8,4},{9,5},{1... | collective-permute-start | bytes 589832 | tf_op jit(solution)/shard_map/ppermute | solution.py:514
  22.9 9.4 %mlp_both_ways.1 = (bf16[128,768]{1,0:T(8,128)(2,1)}, bf16[128,768]{1,0:T(8,128)(2,1)S(1)}, f32[8,768]{1,0:T(8,128)S(1)}, bf16[4,128,768]{2,1,0:T(8,128)(2,1)S(1)}) custom-call(bf16[128,768]{1,0:T(8,128)(2,1)S(1)} %get-tuple-element.44.normed.rest_0_, bf16[3072,768]{1,0:T(8,128)(2,1)} %refs_1_.3, bf16[3072,768]{1,0:T(8,128)(2,1)} %refs_2_.3, ...), custom_call_target="tpu_custom_call" | custom-call | tf_op jit(solution)/shard_map/mlp_both_ways/pallas_call | solution.py:587
  32.3 3.7 %collective-permute-start.8 = (bf16[128,768]{1,0:T(8,128)(2,1)S(1)}, bf16[128,768]{1,0:T(8,128)(2,1)S(1)}, u32[]{:S(2)}, u32[]{:S(2)}) collective-permute-start(bf16[128,768]{1,0:T(8,128)(2,1)S(1)} %get-tuple-element.48.grads.refs_2_), channel_id=1, source_target_pairs={{0,1},{1,0},{2,3},{3,2},{4,5},{5,4},{6,7},{7,6},{8,9},{9,8},{10,11... | collective-permute-start | bytes 589832 | tf_op jit(solution)/shard_map/ppermute | solution.py:487
  36.0 1.9 %collective-permute-start.9 = (bf16[128,768]{1,0:T(8,128)(2,1)S(1)}, bf16[128,768]{1,0:T(8,128)(2,1)S(1)}, u32[]{:S(2)}, u32[]{:S(2)}) collective-permute-start(bf16[128,768]{1,0:T(8,128)(2,1)S(1)} %get-tuple-element.48.grads.refs_2_), channel_id=1, source_target_pairs={{1,2},{3,4},{5,6},{7,8},{9,10},{11,12},{13,14},{2,1},{4,3},{6,5},{... | collective-permute-start | bytes 589832 | tf_op jit(solution)/shard_map/ppermute | solution.py:488
  37.9 0.1 collective-permute-start.7
  38.0 0.1 pad_add_fusion.which
  38.1 6.2 %kernel_grad_terms.1 = (bf16[384,384]{1,0:T(8,128)(2,1)S(1)}, bf16[384,384]{1,0:T(8,128)(2,1)S(1)}) custom-call(s32[2]{0:T(128)S(1)} %pad_add_fusion.which, bf16[128,768]{1,0:T(8,128)(2,1)S(1)} %collective-permute-done.refs_1_.inner, bf16[128,768]{1,0:T(8,128)(2,1)S(1)} %bitcast.13, bf16[128,768]{1,0:T(8,128)(2,1)S(1)} %collective-permute-done.1.refs_2_.outer, ...), custom_call_target="tpu_custom_call" | custom-call | tf_op jit(solution)/shard_map/kernel_grad_terms/pallas_call | solution.py:643
  44.3 0.0 copy-start.8
  44.3 0.7 copy-done.8
  45.0 0.7 copy-done.10
  45.7 0.4 collective-permute-done.7.rest_2_
  46.0 0.2 collective-permute-start.10
  46.2 0.3 collective-permute-start.12
  46.5 1.1 %collective-permute-done.10.got = bf16[384,384]{1,0:T(8,128)(2,1)S(1)} collective-permute-done((bf16[384,384]{1,0:T(8,128)(2,1)S(1)}, bf16[384,384]{1,0:T(8,128)(2,1)S(1)}, u32[]{:S(2)}, u32[]{:S(2)}) %collective-permute-start.10) | collective-permute-done | bytes 294944 | tf_op jit(solution)/shard_map/ppermute | solution.py:669
  47.6 0.8 kernel_grad_chip_sum.1
  48.4 0.2 collective-permute-start.11
  48.6 5.8 %all-to-all-start = ((bf16[8,48,384]{2,1,0:T(8,128)(2,1)}), bf16[8,48,384]{2,1,0:T(8,128)(2,1)S(1)}, u32[]{:S(2)}, u32[]{:S(2)}) async-start(bf16[8,48,384]{2,1,0:T(8,128)(2,1)} %bitcast.8), calls=%async_computation | async-start | bytes 589824 | tf_op jit(solution)/shard_map/all_to_all | solution.py:731
  54.4 0.1 pad_add_fusion.1.refs_0_
  54.5 4.7 %weight_grads_far_side.1.refs_6_ = bf16[2,192,768]{2,1,0:T(8,128)(2,1)} custom-call(s32[2]{0:T(128)S(1)} %pad_add_fusion.1.refs_0_, bf16[3072,768]{1,0:T(8,128)(2,1)} %refs_1_.3, bf16[3072,768]{1,0:T(8,128)(2,1)} %refs_2_.3, f32[768]{0:T(1024)S(1)} %copy-done.12, bf16[4,128,768]{2,1,0:T(8,128)(2,1)S(1)} %get-tuple-element.59.refs_4_, ...), custom_call_target="tpu_custom_call" | custom-call | tf_op jit(solution)/shard_map/weight_grads_far_side/pallas_call | solution.py:696
  59.2 1.5 %collective-permute-start.13 = (bf16[2,192,768]{2,1,0:T(8,128)(2,1)}, bf16[2,192,768]{2,1,0:T(8,128)(2,1)}, u32[]{:S(2)}, u32[]{:S(2)}) collective-permute-start(bf16[2,192,768]{2,1,0:T(8,128)(2,1)} %weight_grads_far_side.1.refs_6_), channel_id=1, source_target_pairs={{0,2},{1,3},{2,0},{3,1},{4,6},{5,7},{6,4},{7,5},{8,10},{9,11},{10,... | collective-permute-start | bytes 1769480 | tf_op jit(solution)/shard_map/ppermute | solution.py:730
  60.7 4.3 %input_grad_conv.1 = (bf16[128,768]{1,0:T(8,128)(2,1)}, f32[8,128]{1,0:T(8,128)S(1)}) custom-call(s32[1]{0:T(128)} %bitcast.refs_0_.core, bf16[128,768]{1,0:T(8,128)(2,1)S(1)} %copy-done.9, bf16[128,768]{1,0:T(8,128)(2,1)S(1)} %copy-done.5, bf16[128,768]{1,0:T(8,128)(2,1)S(1)} %copy-done.11, f32[343,768]{1,0:T(8,128)S(1)} %copy-done.1, ...), custom_call_target="tpu_custom_call" | custom-call | tf_op jit(solution)/shard_map/input_grad_conv/pallas_call | solution.py:739
  65.0 0.8 kernel_grad_sum.1.refs_9_
  65.8 4.3 %all-to-all-start.1 = ((bf16[8,48,384]{2,1,0:T(8,128)(2,1)}), bf16[8,48,384]{2,1,0:T(8,128)(2,1)S(1)}, u32[]{:S(2)}, u32[]{:S(2)}) async-start(bf16[8,48,384]{2,1,0:T(8,128)(2,1)} %kernel_grad_sum.1.refs_9_), calls=%async_computation.1 | async-start | bytes 589824 | tf_op jit(solution)/shard_map/all_to_all | solution.py:777
  70.0 5.8 %collective-permute-done.13.refs_8_ = bf16[2,192,768]{2,1,0:T(8,128)(2,1)} collective-permute-done((bf16[2,192,768]{2,1,0:T(8,128)(2,1)}, bf16[2,192,768]{2,1,0:T(8,128)(2,1)}, u32[]{:S(2)}, u32[]{:S(2)}) %collective-permute-start.13) | collective-permute-done | bytes 589856 | tf_op jit(solution)/shard_map/ppermute | solution.py:730
  75.9 4.9 %weight_grads_near_side.1 = (f32[192,768]{1,0:T(8,128)}, f32[192,768]{1,0:T(8,128)}) custom-call(s32[2]{0:T(128)S(1)} %pad_add_fusion.1.refs_0_, bf16[3072,768]{1,0:T(8,128)(2,1)} %refs_1_.3, bf16[3072,768]{1,0:T(8,128)(2,1)} %refs_2_.3, f32[768]{0:T(1024)S(1)} %copy-done.12, bf16[4,128,768]{2,1,0:T(8,128)(2,1)S(1)} %get-tuple-element.59.refs_4_, ...), custom_call_target="tpu_custom_call" | custom-call | tf_op jit(solution)/shard_map/weight_grads_near_side/pallas_call | solution.py:696
  80.7 1.9 %collective-permute-start.14 = (bf16[8,48,384]{2,1,0:T(8,128)(2,1)S(1)}, bf16[8,48,384]{2,1,0:T(8,128)(2,1)S(1)}, u32[]{:S(2)}, u32[]{:S(2)}) collective-permute-start(bf16[8,48,384]{2,1,0:T(8,128)(2,1)S(1)} %all-to-all-done.1.own), channel_id=1, source_target_pairs={{0,1},{1,0},{2,3},{3,2},{4,5},{5,4},{6,7},{7,6},{8,9},{9,8},{10,11... | collective-permute-start | bytes 884744 | tf_op jit(solution)/shard_map/ppermute | solution.py:784
  82.7 1.2 %collective-permute-done.14.other = bf16[8,48,384]{2,1,0:T(8,128)(2,1)S(1)} collective-permute-done((bf16[8,48,384]{2,1,0:T(8,128)(2,1)S(1)}, bf16[8,48,384]{2,1,0:T(8,128)(2,1)S(1)}, u32[]{:S(2)}, u32[]{:S(2)}) %collective-permute-start.14) | collective-permute-done | bytes 294944 | tf_op jit(solution)/shard_map/ppermute | solution.py:784
  83.9 1.1 %kernel_grad_unpack.1 = (f32[343,768]{1,0:T(8,128)}, f32[768]{0:T(1024)}, f32[768]{0:T(1024)}, f32[768]{0:T(1024)}) custom-call(s32[1]{0:T(128)} %bitcast.refs_0_.core, bf16[8,48,384]{2,1,0:T(8,128)(2,1)S(1)} %all-to-all-done.1.own, bf16[8,48,384]{2,1,0:T(8,128)(2,1)S(1)} %collective-permute-done.14.other), custom_call_target="tpu_custom_call" | custom-call | tf_op jit(solution)/shard_map/kernel_grad_unpack/pallas_call | solution.py:785
  (30 shorter events, 0.1 us)
Async XLA Ops:
  0.6 9.0 %collective-permute-start.2 = (bf16[128,768]{1,0:T(8,128)(2,1)}, bf16[128,768]{1,0:T(8,128)(2,1)S(1)}, u32[]{:S(2)}, u32[]{:S(2)}) collective-permute-start(bf16[128,768]{1,0:T(8,128)(2,1)} %bitcast.14), channel_id=1, source_target_pairs={{0,4},{1,5},{2,6},{3,7},{4,8},{5,9},{6,10},{7,11},{8,12},{9,13},{1... | collective-permute-start | bytes 589832 | tf_op jit(solution)/shard_map/ppermute | solution.py:514
  2.8 12.6 %collective-permute-start = (bf16[128,768]{1,0:T(8,128)(2,1)}, bf16[128,768]{1,0:T(8,128)(2,1)S(1)}, u32[]{:S(2)}, u32[]{:S(2)}) collective-permute-start(bf16[128,768]{1,0:T(8,128)(2,1)} %bitcast.9), channel_id=1, source_target_pairs={{0,1},{1,0},{2,3},{3,2},{4,5},{5,4},{6,7},{7,6},{8,9},{9,8},{10,11... | collective-permute-start | bytes 589832 | tf_op jit(solution)/shard_map/ppermute | solution.py:487
  3.8 11.7 %collective-permute-start.1 = (bf16[128,768]{1,0:T(8,128)(2,1)}, bf16[128,768]{1,0:T(8,128)(2,1)S(1)}, u32[]{:S(2)}, u32[]{:S(2)}) collective-permute-start(bf16[128,768]{1,0:T(8,128)(2,1)} %bitcast.10), channel_id=1, source_target_pairs={{1,2},{3,4},{5,6},{7,8},{9,10},{11,12},{13,14},{2,1},{4,3},{6,5},{... | collective-permute-start | bytes 589832 | tf_op jit(solution)/shard_map/ppermute | solution.py:488
  6.8 8.6 %collective-permute-start.3 = (bf16[128,768]{1,0:T(8,128)(2,1)}, bf16[128,768]{1,0:T(8,128)(2,1)S(1)}, u32[]{:S(2)}, u32[]{:S(2)}) collective-permute-start(bf16[128,768]{1,0:T(8,128)(2,1)} %bitcast.15), channel_id=1, source_target_pairs={{0,12},{1,13},{2,14},{3,15},{4,0},{5,1},{6,2},{7,3},{8,4},{9,5},{1... | collective-permute-start | bytes 589832 | tf_op jit(solution)/shard_map/ppermute | solution.py:514
  9.7 9.9 %collective-permute-start.4 = (bf16[128,768]{1,0:T(8,128)(2,1)S(1)}, bf16[128,768]{1,0:T(8,128)(2,1)S(1)}, u32[]{:S(2)}, u32[]{:S(2)}) collective-permute-start(bf16[128,768]{1,0:T(8,128)(2,1)S(1)} %collective-permute-done.2.refs_6_.rest_1_), channel_id=1, source_target_pairs={{0,4},{1,5},{2,6},{3,7},{4,8},{5,9},{6,10},{7,11},{8,12},{9,13},{1... | collective-permute-start | bytes 589832 | tf_op jit(solution)/shard_map/ppermute | solution.py:514
  9.7 1.2 %copy-start = (f32[343,768]{1,0:T(8,128)S(1)}, f32[343,768]{1,0:T(8,128)}, u32[]{:S(2)}) copy-start(f32[343,768]{1,0:T(8,128)} %refs_4_.1) | copy-start | bytes 3161092
  10.9 0.9 %copy-start.2 = (bf16[4,4,8,768]{3,2,1,0:T(8,128)(2,1)S(1)}, bf16[4,4,8,768]{3,2,1,0:T(8,128)(2,1)}, u32[]{:S(2)}) copy-start(bf16[4,4,8,768]{3,2,1,0:T(8,128)(2,1)} %param.8) | copy-start | bytes 589828
  11.8 0.7 copy-start.13
  12.5 0.7 copy-start.15
  15.4 7.5 %copy-start.3 = (bf16[4,4,8,768]{3,2,1,0:T(8,128)(2,1)S(1)}, bf16[4,4,8,768]{3,2,1,0:T(8,128)(2,1)}, u32[]{:S(2)}) copy-start(bf16[4,4,8,768]{3,2,1,0:T(8,128)(2,1)} %param.8) | copy-start | bytes 589828
  15.4 7.5 %copy-start.6 = (bf16[4,4,8,768]{3,2,1,0:T(8,128)(2,1)S(1)}, bf16[4,4,8,768]{3,2,1,0:T(8,128)(2,1)}, u32[]{:S(2)}) copy-start(bf16[4,4,8,768]{3,2,1,0:T(8,128)(2,1)} %param.15) | copy-start | bytes 589828
  15.4 7.5 %copy-start.12 = (f32[768]{0:T(1024)S(1)}, f32[768]{0:T(1024)}, u32[]{:S(2)}) copy-start(f32[768]{0:T(1024)} %refs_3_.3) | copy-start | bytes 9220
  15.4 7.5 %copy-start.14 = (f32[768]{0:T(1024)S(1)}, f32[768]{0:T(1024)}, u32[]{:S(2)}) copy-start(f32[768]{0:T(1024)} %norm_gain.1) | copy-start | bytes 9220
  19.6 18.3 %collective-permute-start.5 = (bf16[128,768]{1,0:T(8,128)(2,1)S(1)}, bf16[128,768]{1,0:T(8,128)(2,1)S(1)}, u32[]{:S(2)}, u32[]{:S(2)}) collective-permute-start(bf16[128,768]{1,0:T(8,128)(2,1)S(1)} %get-tuple-element.44.normed.rest_0_), channel_id=1, source_target_pairs={{0,4},{1,5},{2,6},{3,7},{4,8},{5,9},{6,10},{7,11},{8,12},{9,13},{1... | collective-permute-start | bytes 589832 | tf_op jit(solution)/shard_map/ppermute | solution.py:514
  19.6 18.3 %collective-permute-start.6 = (bf16[128,768]{1,0:T(8,128)(2,1)S(1)}, bf16[128,768]{1,0:T(8,128)(2,1)S(1)}, u32[]{:S(2)}, u32[]{:S(2)}) collective-permute-start(bf16[128,768]{1,0:T(8,128)(2,1)S(1)} %get-tuple-element.44.normed.rest_0_), channel_id=1, source_target_pairs={{0,12},{1,13},{2,14},{3,15},{4,0},{5,1},{6,2},{7,3},{8,4},{9,5},{1... | collective-permute-start | bytes 589832 | tf_op jit(solution)/shard_map/ppermute | solution.py:514
  32.3 15.3 %copy-start.4 = (bf16[128,768]{1,0:T(8,128)(2,1)}, bf16[128,768]{1,0:T(8,128)(2,1)S(1)}, u32[]{:S(2)}) copy-start(bf16[128,768]{1,0:T(8,128)(2,1)S(1)} %get-tuple-element.48.grads.refs_2_) | copy-start | bytes 589828
  32.3 12.0 %collective-permute-start.8 = (bf16[128,768]{1,0:T(8,128)(2,1)S(1)}, bf16[128,768]{1,0:T(8,128)(2,1)S(1)}, u32[]{:S(2)}, u32[]{:S(2)}) collective-permute-start(bf16[128,768]{1,0:T(8,128)(2,1)S(1)} %get-tuple-element.48.grads.refs_2_), channel_id=1, source_target_pairs={{0,1},{1,0},{2,3},{3,2},{4,5},{5,4},{6,7},{7,6},{8,9},{9,8},{10,11... | collective-permute-start | bytes 589832 | tf_op jit(solution)/shard_map/ppermute | solution.py:487
  36.0 9.0 %collective-permute-start.9 = (bf16[128,768]{1,0:T(8,128)(2,1)S(1)}, bf16[128,768]{1,0:T(8,128)(2,1)S(1)}, u32[]{:S(2)}, u32[]{:S(2)}) collective-permute-start(bf16[128,768]{1,0:T(8,128)(2,1)S(1)} %get-tuple-element.48.grads.refs_2_), channel_id=1, source_target_pairs={{1,2},{3,4},{5,6},{7,8},{9,10},{11,12},{13,14},{2,1},{4,3},{6,5},{... | collective-permute-start | bytes 589832 | tf_op jit(solution)/shard_map/ppermute | solution.py:488
  37.9 8.1 %collective-permute-start.7 = (bf16[128,768]{1,0:T(8,128)(2,1)S(1)}, bf16[128,768]{1,0:T(8,128)(2,1)S(1)}, u32[]{:S(2)}, u32[]{:S(2)}) collective-permute-start(bf16[128,768]{1,0:T(8,128)(2,1)S(1)} %collective-permute-done.5.rest_1_), channel_id=1, source_target_pairs={{0,4},{1,5},{2,6},{3,7},{4,8},{5,9},{6,10},{7,11},{8,12},{9,13},{1... | collective-permute-start | bytes 589832 | tf_op jit(solution)/shard_map/ppermute | solution.py:514
  44.3 0.7 copy-start.8
  45.0 0.7 copy-start.10
  46.0 1.6 %collective-permute-start.10 = (bf16[384,384]{1,0:T(8,128)(2,1)S(1)}, bf16[384,384]{1,0:T(8,128)(2,1)S(1)}, u32[]{:S(2)}, u32[]{:S(2)}) collective-permute-start(bf16[384,384]{1,0:T(8,128)(2,1)S(1)} %get-tuple-element.56), channel_id=1, source_target_pairs={{0,1},{1,0},{2,3},{3,2},{4,5},{5,4},{6,7},{7,6},{8,9},{9,8},{10,11... | collective-permute-start | bytes 884744 | tf_op jit(solution)/shard_map/ppermute | solution.py:669
  46.2 8.3 %collective-permute-start.12 = (bf16[4,128,768]{2,1,0:T(8,128)(2,1)S(1)}, bf16[4,128,768]{2,1,0:T(8,128)(2,1)S(1)}, u32[]{:S(2)}, u32[]{:S(2)}) collective-permute-start(bf16[4,128,768]{2,1,0:T(8,128)(2,1)S(1)} %get-tuple-element.60.refs_5_), channel_id=1, source_target_pairs={{0,1},{1,0},{2,3},{3,2},{4,5},{5,4},{6,7},{7,6},{8,9},{9,8},{10,11... | collective-permute-start | bytes 2359304 | tf_op jit(solution)/shard_map/ppermute | solution.py:692
  48.4 6.1 %collective-permute-start.11 = (bf16[4,128,768]{2,1,0:T(8,128)(2,1)S(1)}, bf16[4,128,768]{2,1,0:T(8,128)(2,1)S(1)}, u32[]{:S(2)}, u32[]{:S(2)}) collective-permute-start(bf16[4,128,768]{2,1,0:T(8,128)(2,1)S(1)} %get-tuple-element.59.refs_4_), channel_id=1, source_target_pairs={{0,1},{1,0},{2,3},{3,2},{4,5},{5,4},{6,7},{7,6},{8,9},{9,8},{10,11... | collective-permute-start | bytes 2359304 | tf_op jit(solution)/shard_map/ppermute | solution.py:691
  48.6 16.4 %all-to-all-start = ((bf16[8,48,384]{2,1,0:T(8,128)(2,1)}), bf16[8,48,384]{2,1,0:T(8,128)(2,1)S(1)}, u32[]{:S(2)}, u32[]{:S(2)}) async-start(bf16[8,48,384]{2,1,0:T(8,128)(2,1)} %bitcast.8), calls=%async_computation | async-start | bytes 589824 | tf_op jit(solution)/shard_map/all_to_all | solution.py:731
  54.5 6.2 %copy-start.1 = (f32[343,768]{1,0:T(8,128)S(1)}, f32[343,768]{1,0:T(8,128)}, u32[]{:S(2)}) copy-start(f32[343,768]{1,0:T(8,128)} %refs_4_.1) | copy-start | bytes 3161092
  54.5 6.2 %copy-start.5 = (bf16[128,768]{1,0:T(8,128)(2,1)S(1)}, bf16[128,768]{1,0:T(8,128)(2,1)}, u32[]{:S(2)}) copy-start(bf16[128,768]{1,0:T(8,128)(2,1)} %copy-done.4) | copy-start | bytes 589828
  54.5 6.2 %copy-start.7 = (bf16[4,4,8,768]{3,2,1,0:T(8,128)(2,1)S(1)}, bf16[4,4,8,768]{3,2,1,0:T(8,128)(2,1)}, u32[]{:S(2)}) copy-start(bf16[4,4,8,768]{3,2,1,0:T(8,128)(2,1)} %param.15) | copy-start | bytes 589828
  54.5 6.2 %copy-start.9 = (bf16[128,768]{1,0:T(8,128)(2,1)S(1)}, bf16[128,768]{1,0:T(8,128)(2,1)}, u32[]{:S(2)}) copy-start(bf16[128,768]{1,0:T(8,128)(2,1)} %copy-done.8) | copy-start | bytes 589828
  54.5 6.2 %copy-start.11 = (bf16[128,768]{1,0:T(8,128)(2,1)S(1)}, bf16[128,768]{1,0:T(8,128)(2,1)}, u32[]{:S(2)}) copy-start(bf16[128,768]{1,0:T(8,128)(2,1)} %copy-done.10) | copy-start | bytes 589828
  59.2 16.7 %collective-permute-start.13 = (bf16[2,192,768]{2,1,0:T(8,128)(2,1)}, bf16[2,192,768]{2,1,0:T(8,128)(2,1)}, u32[]{:S(2)}, u32[]{:S(2)}) collective-permute-start(bf16[2,192,768]{2,1,0:T(8,128)(2,1)} %weight_grads_far_side.1.refs_6_), channel_id=1, source_target_pairs={{0,2},{1,3},{2,0},{3,1},{4,6},{5,7},{6,4},{7,5},{8,10},{9,11},{10,... | collective-permute-start | bytes 1769480 | tf_op jit(solution)/shard_map/ppermute | solution.py:730
  65.8 15.0 %all-to-all-start.1 = ((bf16[8,48,384]{2,1,0:T(8,128)(2,1)}), bf16[8,48,384]{2,1,0:T(8,128)(2,1)S(1)}, u32[]{:S(2)}, u32[]{:S(2)}) async-start(bf16[8,48,384]{2,1,0:T(8,128)(2,1)} %kernel_grad_sum.1.refs_9_), calls=%async_computation.1 | async-start | bytes 589824 | tf_op jit(solution)/shard_map/all_to_all | solution.py:777
  80.7 3.2 %collective-permute-start.14 = (bf16[8,48,384]{2,1,0:T(8,128)(2,1)S(1)}, bf16[8,48,384]{2,1,0:T(8,128)(2,1)S(1)}, u32[]{:S(2)}, u32[]{:S(2)}) collective-permute-start(bf16[8,48,384]{2,1,0:T(8,128)(2,1)S(1)} %all-to-all-done.1.own), channel_id=1, source_target_pairs={{0,1},{1,0},{2,3},{3,2},{4,5},{5,4},{6,7},{7,6},{8,9},{9,8},{10,11... | collective-permute-start | bytes 884744 | tf_op jit(solution)/shard_map/ppermute | solution.py:784

commit v19 on v18

--- a/solution.py
+++ b/solution.py
@@ -582,7 +582,7 @@
     norm_line[1] = along_line(normed, 1)
     norm_line[-1] = along_line(normed, -1)
 
-    block = 512
+    block = 1024
     whole = whole_block(rows, channels)
     block_out, conv_grad, small, cotangents = pl.pallas_call(
         mlp_kernel,
@@ -699,7 +699,7 @@
                 num_scalar_prefetch=1,
                 grid=(1,),
                 in_specs=[chunk, chunk, whole_block(channels)]
-                + [whole_block(line, rows, channels)] * 4
+                + [pl.BlockSpec(memory_space=pltpu.VMEM)] * 4
                 + [whole_block(*part.shape) for part in more]
                 + [IN_PLACE] * len(after),
                 out_specs=[whole_block(*out.shape) for out in outs],

time: 85.9 us -> 84.6 us (0.985)
  Pallas kernels: 36.9 us -> 35.8 us
    pallas_call x1, Pallas kernels: 9.43 us -> 8.29 us  [on_device(): pl.pallas_call(mlp_kernel, grid=(units // block,), in_specs=[whole, pl.Bl...]
  transfers between devices with their start and end apart: 17 -> 17, of which waited for: 6 -> 6; matrix products, arithmetic and copies ran while one was open for 0% -> 0% of each run, Pallas kernels for 42% -> 41%
where the time goes in v19:
time: 84.6 us; the launch traced here: 83.8 us
  Pallas kernels  35.8 us (42%)
  starting transfers between devices  31.3 us (37%)
  waiting for transfers between devices  10.8 us (13%)
  local copies, waits for them, and re-layouts  4.93 us (6%)
    pallas_call x2, Pallas kernels, side_terms(): pl.pallas_call(follow(kernel, 1, 7 + len(more), len(after)), grid_spec=pl...  9.51 us
    pallas_call x1, Pallas kernels, on_device(): pl.pallas_call(mlp_kernel, grid=(units // block,), in_specs=[whole, pl.Bl...  8.29 us
    ppermute x6, starting transfers between devices, along_line(): lax.ppermute(cells, 'row', [(i, (i + quad * steps) % count) for i in rang...  7.52 us
    pallas_call x1, Pallas kernels, on_device(): pl.pallas_call(functools.partial(kernel_grad_kernel, planes, height), gri...  6.18 us
    ppermute x1, waiting for transfers between devices, on_device(): got = lax.ppermute(sent, 'row', other_side)  5.85 us
    all_to_all x1, starting transfers between devices, on_device(): lax.all_to_all(sums.reshape(half, piece, wide), 'row', split_axis=0, conc...  5.81 us
    ppermute x2, starting transfers between devices, rims(): lax.ppermute(cells, 'row', between + [(j, i) for i, j in between])  4.93 us
    unnamed x32, local copies, waits for them, and re-layouts  4.93 us
  transfers between devices with their start and end apart: 17, of which 6 were waited for; matrix products, arithmetic and copies ran while one was open for 0% of the time, Pallas kernels for 41%

profile of v19, /device:TPU:1, one launch (start us, length us, event | category | flops | bytes accessed | tf_op | source)
XLA Modules:
  0.0 83.8 jit_solution(17062082501379040774)
XLA Ops:
  0.6 2.2 %collective-permute-start.2 = (bf16[128,768]{1,0:T(8,128)(2,1)}, bf16[128,768]{1,0:T(8,128)(2,1)S(1)}, u32[]{:S(2)}, u32[]{:S(2)}) collective-permute-start(bf16[128,768]{1,0:T(8,128)(2,1)} %bitcast.14), channel_id=1, source_target_pairs={{0,4},{1,5},{2,6},{3,7},{4,8},{5,9},{6,10},{7,11},{8,12},{9,13},{1... | collective-permute-start | bytes 589832 | tf_op jit(solution)/shard_map/ppermute | solution.py:514
  2.8 1.0 %collective-permute-start = (bf16[128,768]{1,0:T(8,128)(2,1)}, bf16[128,768]{1,0:T(8,128)(2,1)S(1)}, u32[]{:S(2)}, u32[]{:S(2)}) collective-permute-start(bf16[128,768]{1,0:T(8,128)(2,1)} %bitcast.9), channel_id=1, source_target_pairs={{0,1},{1,0},{2,3},{3,2},{4,5},{5,4},{6,7},{7,6},{8,9},{9,8},{10,11... | collective-permute-start | bytes 589832 | tf_op jit(solution)/shard_map/ppermute | solution.py:487
  3.8 3.0 %collective-permute-start.1 = (bf16[128,768]{1,0:T(8,128)(2,1)}, bf16[128,768]{1,0:T(8,128)(2,1)S(1)}, u32[]{:S(2)}, u32[]{:S(2)}) collective-permute-start(bf16[128,768]{1,0:T(8,128)(2,1)} %bitcast.10), channel_id=1, source_target_pairs={{1,2},{3,4},{5,6},{7,8},{9,10},{11,12},{13,14},{2,1},{4,3},{6,5},{... | collective-permute-start | bytes 589832 | tf_op jit(solution)/shard_map/ppermute | solution.py:488
  6.8 2.0 %collective-permute-start.3 = (bf16[128,768]{1,0:T(8,128)(2,1)}, bf16[128,768]{1,0:T(8,128)(2,1)S(1)}, u32[]{:S(2)}, u32[]{:S(2)}) collective-permute-start(bf16[128,768]{1,0:T(8,128)(2,1)} %bitcast.15), channel_id=1, source_target_pairs={{0,12},{1,13},{2,14},{3,15},{4,0},{5,1},{6,2},{7,3},{8,4},{9,5},{1... | collective-permute-start | bytes 589832 | tf_op jit(solution)/shard_map/ppermute | solution.py:514
  8.8 0.9 %collective-permute-done.2.refs_6_.rest_1_ = bf16[128,768]{1,0:T(8,128)(2,1)S(1)} collective-permute-done((bf16[128,768]{1,0:T(8,128)(2,1)}, bf16[128,768]{1,0:T(8,128)(2,1)S(1)}, u32[]{:S(2)}, u32[]{:S(2)}) %collective-permute-start.2) | collective-permute-done | bytes 196640 | tf_op jit(solution)/shard_map/ppermute | solution.py:514
  9.7 0.0 collective-permute-start.4
  9.7 1.2 %copy-done = f32[343,768]{1,0:T(8,128)S(1)} copy-done((f32[343,768]{1,0:T(8,128)S(1)}, f32[343,768]{1,0:T(8,128)}, u32[]{:S(2)}) %copy-start) | copy-done | bytes 1053720
  10.9 0.9 %copy-done.2 = bf16[4,4,8,768]{3,2,1,0:T(8,128)(2,1)S(1)} copy-done((bf16[4,4,8,768]{3,2,1,0:T(8,128)(2,1)S(1)}, bf16[4,4,8,768]{3,2,1,0:T(8,128)(2,1)}, u32[]{:S(2)}) %copy-start.2) | copy-done | bytes 196632
  11.8 0.7 copy-done.13
  12.5 0.7 copy-done.15
  13.2 2.2 %own_conv.1 = (f32[128,768]{1,0:T(8,128)S(1)}, f32[6,9,7,8,128]{4,3,2,1,0:T(8,128)S(1)}, f32[8,768]{1,0:T(8,128)S(1)}) custom-call(bf16[128,768]{1,0:T(8,128)(2,1)S(1)} %bitcast.11, f32[343,768]{1,0:T(8,128)S(1)} %copy-done, f32[768]{0:T(1024)S(1)} %copy-done.13, f32[768]{0:T(1024)S(1)} %copy-done.15), custom_call_target="tpu_custom_call" | custom-call | tf_op jit(solution)/shard_map/own_conv/pallas_call | solution.py:524
  15.4 0.0 copy-start.3
  15.4 0.0 copy-start.6
  15.4 0.0 copy-start.12
  15.4 0.0 copy-start.14
  15.4 0.0 collective-permute-done.1.refs_2_.outer
  15.4 0.0 collective-permute-done.3.refs_7_.rest_3_
  15.5 2.7 %rim_conv.1 = (bf16[128,768]{1,0:T(8,128)(2,1)S(1)}, f32[128,768]{1,0:T(8,128)S(1)}) custom-call(s32[1]{0:T(128)} %bitcast.refs_0_.core, bf16[128,768]{1,0:T(8,128)(2,1)S(1)} %collective-permute-done.refs_1_.inner, bf16[128,768]{1,0:T(8,128)(2,1)S(1)} %collective-permute-done.1.refs_2_.outer, f32[6,9,7,8,128]{4,3,2,1,0:T(8,128)S(1)} %get-tuple-element.40.refs_3_, ...), custom_call_target="tpu_custom_call" | custom-call | tf_op jit(solution)/shard_map/rim_conv/pallas_call | solution.py:542
  18.2 1.4 %collective-permute-done.4.rest_2_ = bf16[128,768]{1,0:T(8,128)(2,1)S(1)} collective-permute-done((bf16[128,768]{1,0:T(8,128)(2,1)S(1)}, bf16[128,768]{1,0:T(8,128)(2,1)S(1)}, u32[]{:S(2)}, u32[]{:S(2)}) %collective-permute-start.4) | collective-permute-done | bytes 196640 | tf_op jit(solution)/shard_map/ppermute | solution.py:514
  19.6 0.0 collective-permute-start.5
  19.6 3.3 %collective-permute-start.6 = (bf16[128,768]{1,0:T(8,128)(2,1)S(1)}, bf16[128,768]{1,0:T(8,128)(2,1)S(1)}, u32[]{:S(2)}, u32[]{:S(2)}) collective-permute-start(bf16[128,768]{1,0:T(8,128)(2,1)S(1)} %get-tuple-element.44.normed.rest_0_), channel_id=1, source_target_pairs={{0,12},{1,13},{2,14},{3,15},{4,0},{5,1},{6,2},{7,3},{8,4},{9,5},{1... | collective-permute-start | bytes 589832 | tf_op jit(solution)/shard_map/ppermute | solution.py:514
  22.9 8.3 %mlp_both_ways.1 = (bf16[128,768]{1,0:T(8,128)(2,1)}, bf16[128,768]{1,0:T(8,128)(2,1)S(1)}, f32[8,768]{1,0:T(8,128)S(1)}, bf16[4,128,768]{2,1,0:T(8,128)(2,1)S(1)}) custom-call(bf16[128,768]{1,0:T(8,128)(2,1)S(1)} %get-tuple-element.44.normed.rest_0_, bf16[3072,768]{1,0:T(8,128)(2,1)} %refs_1_.3, bf16[3072,768]{1,0:T(8,128)(2,1)} %refs_2_.3, ...), custom_call_target="tpu_custom_call" | custom-call | tf_op jit(solution)/shard_map/mlp_both_ways/pallas_call | solution.py:587
  31.2 3.7 %collective-permute-start.8 = (bf16[128,768]{1,0:T(8,128)(2,1)S(1)}, bf16[128,768]{1,0:T(8,128)(2,1)S(1)}, u32[]{:S(2)}, u32[]{:S(2)}) collective-permute-start(bf16[128,768]{1,0:T(8,128)(2,1)S(1)} %get-tuple-element.48.grads.refs_2_), channel_id=1, source_target_pairs={{0,1},{1,0},{2,3},{3,2},{4,5},{5,4},{6,7},{7,6},{8,9},{9,8},{10,11... | collective-permute-start | bytes 589832 | tf_op jit(solution)/shard_map/ppermute | solution.py:487
  34.9 1.9 %collective-permute-start.9 = (bf16[128,768]{1,0:T(8,128)(2,1)S(1)}, bf16[128,768]{1,0:T(8,128)(2,1)S(1)}, u32[]{:S(2)}, u32[]{:S(2)}) collective-permute-start(bf16[128,768]{1,0:T(8,128)(2,1)S(1)} %get-tuple-element.48.grads.refs_2_), channel_id=1, source_target_pairs={{1,2},{3,4},{5,6},{7,8},{9,10},{11,12},{13,14},{2,1},{4,3},{6,5},{... | collective-permute-start | bytes 589832 | tf_op jit(solution)/shard_map/ppermute | solution.py:488
  36.8 0.1 collective-permute-start.7
  36.9 0.1 pad_add_fusion.which
  37.0 6.2 %kernel_grad_terms.1 = (bf16[384,384]{1,0:T(8,128)(2,1)S(1)}, bf16[384,384]{1,0:T(8,128)(2,1)S(1)}) custom-call(s32[2]{0:T(128)S(1)} %pad_add_fusion.which, bf16[128,768]{1,0:T(8,128)(2,1)S(1)} %collective-permute-done.refs_1_.inner, bf16[128,768]{1,0:T(8,128)(2,1)S(1)} %bitcast.13, bf16[128,768]{1,0:T(8,128)(2,1)S(1)} %collective-permute-done.1.refs_2_.outer, ...), custom_call_target="tpu_custom_call" | custom-call | tf_op jit(solution)/shard_map/kernel_grad_terms/pallas_call | solution.py:643
  43.2 0.0 copy-start.8
  43.2 0.7 copy-done.8
  43.8 0.7 copy-done.10
  44.5 0.3 collective-permute-done.7.rest_2_
  44.9 0.2 collective-permute-start.10
  45.1 0.3 collective-permute-start.12
  45.4 1.1 %collective-permute-done.10.got = bf16[384,384]{1,0:T(8,128)(2,1)S(1)} collective-permute-done((bf16[384,384]{1,0:T(8,128)(2,1)S(1)}, bf16[384,384]{1,0:T(8,128)(2,1)S(1)}, u32[]{:S(2)}, u32[]{:S(2)}) %collective-permute-start.10) | collective-permute-done | bytes 294944 | tf_op jit(solution)/shard_map/ppermute | solution.py:669
  46.5 0.8 kernel_grad_chip_sum.1
  47.3 0.2 collective-permute-start.11
  47.5 5.8 %all-to-all-start = ((bf16[8,48,384]{2,1,0:T(8,128)(2,1)}), bf16[8,48,384]{2,1,0:T(8,128)(2,1)S(1)}, u32[]{:S(2)}, u32[]{:S(2)}) async-start(bf16[8,48,384]{2,1,0:T(8,128)(2,1)} %bitcast.8), calls=%async_computation | async-start | bytes 589824 | tf_op jit(solution)/shard_map/all_to_all | solution.py:731
  53.3 0.1 pad_add_fusion.1.refs_0_
  53.4 4.7 %weight_grads_far_side.1.refs_6_ = bf16[2,192,768]{2,1,0:T(8,128)(2,1)} custom-call(s32[2]{0:T(128)S(1)} %pad_add_fusion.1.refs_0_, bf16[3072,768]{1,0:T(8,128)(2,1)} %refs_1_.3, bf16[3072,768]{1,0:T(8,128)(2,1)} %refs_2_.3, f32[768]{0:T(1024)S(1)} %copy-done.12, bf16[4,128,768]{2,1,0:T(8,128)(2,1)S(1)} %get-tuple-element.59.refs_4_, ...), custom_call_target="tpu_custom_call" | custom-call | tf_op jit(solution)/shard_map/weight_grads_far_side/pallas_call | solution.py:696
  58.1 1.5 %collective-permute-start.13 = (bf16[2,192,768]{2,1,0:T(8,128)(2,1)}, bf16[2,192,768]{2,1,0:T(8,128)(2,1)}, u32[]{:S(2)}, u32[]{:S(2)}) collective-permute-start(bf16[2,192,768]{2,1,0:T(8,128)(2,1)} %weight_grads_far_side.1.refs_6_), channel_id=1, source_target_pairs={{0,2},{1,3},{2,0},{3,1},{4,6},{5,7},{6,4},{7,5},{8,10},{9,11},{10,... | collective-permute-start | bytes 1769480 | tf_op jit(solution)/shard_map/ppermute | solution.py:730
  59.6 4.3 %input_grad_conv.1 = (bf16[128,768]{1,0:T(8,128)(2,1)}, f32[8,128]{1,0:T(8,128)S(1)}) custom-call(s32[1]{0:T(128)} %bitcast.refs_0_.core, bf16[128,768]{1,0:T(8,128)(2,1)S(1)} %copy-done.9, bf16[128,768]{1,0:T(8,128)(2,1)S(1)} %copy-done.5, bf16[128,768]{1,0:T(8,128)(2,1)S(1)} %copy-done.11, f32[343,768]{1,0:T(8,128)S(1)} %copy-done.1, ...), custom_call_target="tpu_custom_call" | custom-call | tf_op jit(solution)/shard_map/input_grad_conv/pallas_call | solution.py:739
  63.9 0.8 kernel_grad_sum.1.refs_9_
  64.6 4.3 %all-to-all-start.1 = ((bf16[8,48,384]{2,1,0:T(8,128)(2,1)}), bf16[8,48,384]{2,1,0:T(8,128)(2,1)S(1)}, u32[]{:S(2)}, u32[]{:S(2)}) async-start(bf16[8,48,384]{2,1,0:T(8,128)(2,1)} %kernel_grad_sum.1.refs_9_), calls=%async_computation.1 | async-start | bytes 589824 | tf_op jit(solution)/shard_map/all_to_all | solution.py:777
  68.9 5.8 %collective-permute-done.13.refs_8_ = bf16[2,192,768]{2,1,0:T(8,128)(2,1)} collective-permute-done((bf16[2,192,768]{2,1,0:T(8,128)(2,1)}, bf16[2,192,768]{2,1,0:T(8,128)(2,1)}, u32[]{:S(2)}, u32[]{:S(2)}) %collective-permute-start.13) | collective-permute-done | bytes 589856 | tf_op jit(solution)/shard_map/ppermute | solution.py:730
  74.7 4.9 %weight_grads_near_side.1 = (f32[192,768]{1,0:T(8,128)}, f32[192,768]{1,0:T(8,128)}) custom-call(s32[2]{0:T(128)S(1)} %pad_add_fusion.1.refs_0_, bf16[3072,768]{1,0:T(8,128)(2,1)} %refs_1_.3, bf16[3072,768]{1,0:T(8,128)(2,1)} %refs_2_.3, f32[768]{0:T(1024)S(1)} %copy-done.12, bf16[4,128,768]{2,1,0:T(8,128)(2,1)S(1)} %get-tuple-element.59.refs_4_, ...), custom_call_target="tpu_custom_call" | custom-call | tf_op jit(solution)/shard_map/weight_grads_near_side/pallas_call | solution.py:696
  79.6 1.9 %collective-permute-start.14 = (bf16[8,48,384]{2,1,0:T(8,128)(2,1)S(1)}, bf16[8,48,384]{2,1,0:T(8,128)(2,1)S(1)}, u32[]{:S(2)}, u32[]{:S(2)}) collective-permute-start(bf16[8,48,384]{2,1,0:T(8,128)(2,1)S(1)} %all-to-all-done.1.own), channel_id=1, source_target_pairs={{0,1},{1,0},{2,3},{3,2},{4,5},{5,4},{6,7},{7,6},{8,9},{9,8},{10,11... | collective-permute-start | bytes 884744 | tf_op jit(solution)/shard_map/ppermute | solution.py:784
  81.5 1.2 %collective-permute-done.14.other = bf16[8,48,384]{2,1,0:T(8,128)(2,1)S(1)} collective-permute-done((bf16[8,48,384]{2,1,0:T(8,128)(2,1)S(1)}, bf16[8,48,384]{2,1,0:T(8,128)(2,1)S(1)}, u32[]{:S(2)}, u32[]{:S(2)}) %collective-permute-start.14) | collective-permute-done | bytes 294944 | tf_op jit(solution)/shard_map/ppermute | solution.py:784
  82.7 1.1 %kernel_grad_unpack.1 = (f32[343,768]{1,0:T(8,128)}, f32[768]{0:T(1024)}, f32[768]{0:T(1024)}, f32[768]{0:T(1024)}) custom-call(s32[1]{0:T(128)} %bitcast.refs_0_.core, bf16[8,48,384]{2,1,0:T(8,128)(2,1)S(1)} %all-to-all-done.1.own, bf16[8,48,384]{2,1,0:T(8,128)(2,1)S(1)} %collective-permute-done.14.other), custom_call_target="tpu_custom_call" | custom-call | tf_op jit(solution)/shard_map/kernel_grad_unpack/pallas_call | solution.py:785
  (30 shorter events, 0.1 us)
Async XLA Ops:
  0.6 9.0 %collective-permute-start.2 = (bf16[128,768]{1,0:T(8,128)(2,1)}, bf16[128,768]{1,0:T(8,128)(2,1)S(1)}, u32[]{:S(2)}, u32[]{:S(2)}) collective-permute-start(bf16[128,768]{1,0:T(8,128)(2,1)} %bitcast.14), channel_id=1, source_target_pairs={{0,4},{1,5},{2,6},{3,7},{4,8},{5,9},{6,10},{7,11},{8,12},{9,13},{1... | collective-permute-start | bytes 589832 | tf_op jit(solution)/shard_map/ppermute | solution.py:514
  2.8 12.6 %collective-permute-start = (bf16[128,768]{1,0:T(8,128)(2,1)}, bf16[128,768]{1,0:T(8,128)(2,1)S(1)}, u32[]{:S(2)}, u32[]{:S(2)}) collective-permute-start(bf16[128,768]{1,0:T(8,128)(2,1)} %bitcast.9), channel_id=1, source_target_pairs={{0,1},{1,0},{2,3},{3,2},{4,5},{5,4},{6,7},{7,6},{8,9},{9,8},{10,11... | collective-permute-start | bytes 589832 | tf_op jit(solution)/shard_map/ppermute | solution.py:487
  3.8 11.7 %collective-permute-start.1 = (bf16[128,768]{1,0:T(8,128)(2,1)}, bf16[128,768]{1,0:T(8,128)(2,1)S(1)}, u32[]{:S(2)}, u32[]{:S(2)}) collective-permute-start(bf16[128,768]{1,0:T(8,128)(2,1)} %bitcast.10), channel_id=1, source_target_pairs={{1,2},{3,4},{5,6},{7,8},{9,10},{11,12},{13,14},{2,1},{4,3},{6,5},{... | collective-permute-start | bytes 589832 | tf_op jit(solution)/shard_map/ppermute | solution.py:488
  6.8 8.6 %collective-permute-start.3 = (bf16[128,768]{1,0:T(8,128)(2,1)}, bf16[128,768]{1,0:T(8,128)(2,1)S(1)}, u32[]{:S(2)}, u32[]{:S(2)}) collective-permute-start(bf16[128,768]{1,0:T(8,128)(2,1)} %bitcast.15), channel_id=1, source_target_pairs={{0,12},{1,13},{2,14},{3,15},{4,0},{5,1},{6,2},{7,3},{8,4},{9,5},{1... | collective-permute-start | bytes 589832 | tf_op jit(solution)/shard_map/ppermute | solution.py:514
  9.7 9.9 %collective-permute-start.4 = (bf16[128,768]{1,0:T(8,128)(2,1)S(1)}, bf16[128,768]{1,0:T(8,128)(2,1)S(1)}, u32[]{:S(2)}, u32[]{:S(2)}) collective-permute-start(bf16[128,768]{1,0:T(8,128)(2,1)S(1)} %collective-permute-done.2.refs_6_.rest_1_), channel_id=1, source_target_pairs={{0,4},{1,5},{2,6},{3,7},{4,8},{5,9},{6,10},{7,11},{8,12},{9,13},{1... | collective-permute-start | bytes 589832 | tf_op jit(solution)/shard_map/ppermute | solution.py:514
  9.7 1.2 %copy-start = (f32[343,768]{1,0:T(8,128)S(1)}, f32[343,768]{1,0:T(8,128)}, u32[]{:S(2)}) copy-start(f32[343,768]{1,0:T(8,128)} %refs_4_.1) | copy-start | bytes 3161092
  10.9 0.9 %copy-start.2 = (bf16[4,4,8,768]{3,2,1,0:T(8,128)(2,1)S(1)}, bf16[4,4,8,768]{3,2,1,0:T(8,128)(2,1)}, u32[]{:S(2)}) copy-start(bf16[4,4,8,768]{3,2,1,0:T(8,128)(2,1)} %param.8) | copy-start | bytes 589828
  11.8 0.7 copy-start.13
  12.5 0.7 copy-start.15
  15.4 7.5 %copy-start.3 = (bf16[4,4,8,768]{3,2,1,0:T(8,128)(2,1)S(1)}, bf16[4,4,8,768]{3,2,1,0:T(8,128)(2,1)}, u32[]{:S(2)}) copy-start(bf16[4,4,8,768]{3,2,1,0:T(8,128)(2,1)} %param.8) | copy-start | bytes 589828
  15.4 7.5 %copy-start.6 = (bf16[4,4,8,768]{3,2,1,0:T(8,128)(2,1)S(1)}, bf16[4,4,8,768]{3,2,1,0:T(8,128)(2,1)}, u32[]{:S(2)}) copy-start(bf16[4,4,8,768]{3,2,1,0:T(8,128)(2,1)} %param.15) | copy-start | bytes 589828
  15.4 7.5 %copy-start.12 = (f32[768]{0:T(1024)S(1)}, f32[768]{0:T(1024)}, u32[]{:S(2)}) copy-start(f32[768]{0:T(1024)} %refs_3_.3) | copy-start | bytes 9220
  15.4 7.5 %copy-start.14 = (f32[768]{0:T(1024)S(1)}, f32[768]{0:T(1024)}, u32[]{:S(2)}) copy-start(f32[768]{0:T(1024)} %norm_gain.1) | copy-start | bytes 9220
  19.6 17.2 %collective-permute-start.5 = (bf16[128,768]{1,0:T(8,128)(2,1)S(1)}, bf16[128,768]{1,0:T(8,128)(2,1)S(1)}, u32[]{:S(2)}, u32[]{:S(2)}) collective-permute-start(bf16[128,768]{1,0:T(8,128)(2,1)S(1)} %get-tuple-element.44.normed.rest_0_), channel_id=1, source_target_pairs={{0,4},{1,5},{2,6},{3,7},{4,8},{5,9},{6,10},{7,11},{8,12},{9,13},{1... | collective-permute-start | bytes 589832 | tf_op jit(solution)/shard_map/ppermute | solution.py:514
  19.6 17.2 %collective-permute-start.6 = (bf16[128,768]{1,0:T(8,128)(2,1)S(1)}, bf16[128,768]{1,0:T(8,128)(2,1)S(1)}, u32[]{:S(2)}, u32[]{:S(2)}) collective-permute-start(bf16[128,768]{1,0:T(8,128)(2,1)S(1)} %get-tuple-element.44.normed.rest_0_), channel_id=1, source_target_pairs={{0,12},{1,13},{2,14},{3,15},{4,0},{5,1},{6,2},{7,3},{8,4},{9,5},{1... | collective-permute-start | bytes 589832 | tf_op jit(solution)/shard_map/ppermute | solution.py:514
  31.2 15.3 %copy-start.4 = (bf16[128,768]{1,0:T(8,128)(2,1)}, bf16[128,768]{1,0:T(8,128)(2,1)S(1)}, u32[]{:S(2)}) copy-start(bf16[128,768]{1,0:T(8,128)(2,1)S(1)} %get-tuple-element.48.grads.refs_2_) | copy-start | bytes 589828
  31.2 12.0 %collective-permute-start.8 = (bf16[128,768]{1,0:T(8,128)(2,1)S(1)}, bf16[128,768]{1,0:T(8,128)(2,1)S(1)}, u32[]{:S(2)}, u32[]{:S(2)}) collective-permute-start(bf16[128,768]{1,0:T(8,128)(2,1)S(1)} %get-tuple-element.48.grads.refs_2_), channel_id=1, source_target_pairs={{0,1},{1,0},{2,3},{3,2},{4,5},{5,4},{6,7},{7,6},{8,9},{9,8},{10,11... | collective-permute-start | bytes 589832 | tf_op jit(solution)/shard_map/ppermute | solution.py:487
  34.9 9.0 %collective-permute-start.9 = (bf16[128,768]{1,0:T(8,128)(2,1)S(1)}, bf16[128,768]{1,0:T(8,128)(2,1)S(1)}, u32[]{:S(2)}, u32[]{:S(2)}) collective-permute-start(bf16[128,768]{1,0:T(8,128)(2,1)S(1)} %get-tuple-element.48.grads.refs_2_), channel_id=1, source_target_pairs={{1,2},{3,4},{5,6},{7,8},{9,10},{11,12},{13,14},{2,1},{4,3},{6,5},{... | collective-permute-start | bytes 589832 | tf_op jit(solution)/shard_map/ppermute | solution.py:488
  36.8 8.1 %collective-permute-start.7 = (bf16[128,768]{1,0:T(8,128)(2,1)S(1)}, bf16[128,768]{1,0:T(8,128)(2,1)S(1)}, u32[]{:S(2)}, u32[]{:S(2)}) collective-permute-start(bf16[128,768]{1,0:T(8,128)(2,1)S(1)} %collective-permute-done.5.rest_1_), channel_id=1, source_target_pairs={{0,4},{1,5},{2,6},{3,7},{4,8},{5,9},{6,10},{7,11},{8,12},{9,13},{1... | collective-permute-start | bytes 589832 | tf_op jit(solution)/shard_map/ppermute | solution.py:514
  43.2 0.7 copy-start.8
  43.8 0.7 copy-start.10
  44.9 1.6 %collective-permute-start.10 = (bf16[384,384]{1,0:T(8,128)(2,1)S(1)}, bf16[384,384]{1,0:T(8,128)(2,1)S(1)}, u32[]{:S(2)}, u32[]{:S(2)}) collective-permute-start(bf16[384,384]{1,0:T(8,128)(2,1)S(1)} %get-tuple-element.56), channel_id=1, source_target_pairs={{0,1},{1,0},{2,3},{3,2},{4,5},{5,4},{6,7},{7,6},{8,9},{9,8},{10,11... | collective-permute-start | bytes 884744 | tf_op jit(solution)/shard_map/ppermute | solution.py:669
  45.1 8.3 %collective-permute-start.12 = (bf16[4,128,768]{2,1,0:T(8,128)(2,1)S(1)}, bf16[4,128,768]{2,1,0:T(8,128)(2,1)S(1)}, u32[]{:S(2)}, u32[]{:S(2)}) collective-permute-start(bf16[4,128,768]{2,1,0:T(8,128)(2,1)S(1)} %get-tuple-element.60.refs_5_), channel_id=1, source_target_pairs={{0,1},{1,0},{2,3},{3,2},{4,5},{5,4},{6,7},{7,6},{8,9},{9,8},{10,11... | collective-permute-start | bytes 2359304 | tf_op jit(solution)/shard_map/ppermute | solution.py:692
  47.3 6.1 %collective-permute-start.11 = (bf16[4,128,768]{2,1,0:T(8,128)(2,1)S(1)}, bf16[4,128,768]{2,1,0:T(8,128)(2,1)S(1)}, u32[]{:S(2)}, u32[]{:S(2)}) collective-permute-start(bf16[4,128,768]{2,1,0:T(8,128)(2,1)S(1)} %get-tuple-element.59.refs_4_), channel_id=1, source_target_pairs={{0,1},{1,0},{2,3},{3,2},{4,5},{5,4},{6,7},{7,6},{8,9},{9,8},{10,11... | collective-permute-start | bytes 2359304 | tf_op jit(solution)/shard_map/ppermute | solution.py:691
  47.5 16.4 %all-to-all-start = ((bf16[8,48,384]{2,1,0:T(8,128)(2,1)}), bf16[8,48,384]{2,1,0:T(8,128)(2,1)S(1)}, u32[]{:S(2)}, u32[]{:S(2)}) async-start(bf16[8,48,384]{2,1,0:T(8,128)(2,1)} %bitcast.8), calls=%async_computation | async-start | bytes 589824 | tf_op jit(solution)/shard_map/all_to_all | solution.py:731
  53.4 6.2 %copy-start.1 = (f32[343,768]{1,0:T(8,128)S(1)}, f32[343,768]{1,0:T(8,128)}, u32[]{:S(2)}) copy-start(f32[343,768]{1,0:T(8,128)} %refs_4_.1) | copy-start | bytes 3161092
  53.4 6.2 %copy-start.5 = (bf16[128,768]{1,0:T(8,128)(2,1)S(1)}, bf16[128,768]{1,0:T(8,128)(2,1)}, u32[]{:S(2)}) copy-start(bf16[128,768]{1,0:T(8,128)(2,1)} %copy-done.4) | copy-start | bytes 589828
  53.4 6.2 %copy-start.7 = (bf16[4,4,8,768]{3,2,1,0:T(8,128)(2,1)S(1)}, bf16[4,4,8,768]{3,2,1,0:T(8,128)(2,1)}, u32[]{:S(2)}) copy-start(bf16[4,4,8,768]{3,2,1,0:T(8,128)(2,1)} %param.15) | copy-start | bytes 589828
  53.4 6.2 %copy-start.9 = (bf16[128,768]{1,0:T(8,128)(2,1)S(1)}, bf16[128,768]{1,0:T(8,128)(2,1)}, u32[]{:S(2)}) copy-start(bf16[128,768]{1,0:T(8,128)(2,1)} %copy-done.8) | copy-start | bytes 589828
  53.4 6.2 %copy-start.11 = (bf16[128,768]{1,0:T(8,128)(2,1)S(1)}, bf16[128,768]{1,0:T(8,128)(2,1)}, u32[]{:S(2)}) copy-start(bf16[128,768]{1,0:T(8,128)(2,1)} %copy-done.10) | copy-start | bytes 589828
  58.1 16.7 %collective-permute-start.13 = (bf16[2,192,768]{2,1,0:T(8,128)(2,1)}, bf16[2,192,768]{2,1,0:T(8,128)(2,1)}, u32[]{:S(2)}, u32[]{:S(2)}) collective-permute-start(bf16[2,192,768]{2,1,0:T(8,128)(2,1)} %weight_grads_far_side.1.refs_6_), channel_id=1, source_target_pairs={{0,2},{1,3},{2,0},{3,1},{4,6},{5,7},{6,4},{7,5},{8,10},{9,11},{10,... | collective-permute-start | bytes 1769480 | tf_op jit(solution)/shard_map/ppermute | solution.py:730
  64.6 15.0 %all-to-all-start.1 = ((bf16[8,48,384]{2,1,0:T(8,128)(2,1)}), bf16[8,48,384]{2,1,0:T(8,128)(2,1)S(1)}, u32[]{:S(2)}, u32[]{:S(2)}) async-start(bf16[8,48,384]{2,1,0:T(8,128)(2,1)} %kernel_grad_sum.1.refs_9_), calls=%async_computation.1 | async-start | bytes 589824 | tf_op jit(solution)/shard_map/all_to_all | solution.py:777
  79.6 3.2 %collective-permute-start.14 = (bf16[8,48,384]{2,1,0:T(8,128)(2,1)S(1)}, bf16[8,48,384]{2,1,0:T(8,128)(2,1)S(1)}, u32[]{:S(2)}, u32[]{:S(2)}) collective-permute-start(bf16[8,48,384]{2,1,0:T(8,128)(2,1)S(1)} %all-to-all-done.1.own), channel_id=1, source_target_pairs={{0,1},{1,0},{2,3},{3,2},{4,5},{5,4},{6,7},{7,6},{8,9},{9,8},{10,11... | collective-permute-start | bytes 884744 | tf_op jit(solution)/shard_map/ppermute | solution.py:784

commit v20 on v19

--- a/solution.py
+++ b/solution.py
@@ -373,54 +373,36 @@
     return activated, (act_grad * slope).astype(BF16)
 
 
-def weight_grad_terms(weight_in, weight_out, scale, sets, aligned, mixed_grad):
+def weight_grad_terms(weight_in, weight_out, scale, sets):
     scales = scale[...].reshape(1, -1)
-    at = 0
-    for normed, cotangents in sets:
-        line, rows = normed.shape[:2]
-        for k in range(line):
-            aligned[at : at + rows, :] = normed[k]
-            upstream = cotangents[k].astype(F32)
-            mixed_grad[at : at + rows, :] = (scales * upstream).astype(BF16)
-            at += rows
     across = (((1,), (1,)), ((), ()))
-    hidden = lax.dot_general(weight_in[...], aligned[...], across, preferred_element_type=F32)
-    act_grad = lax.dot_general(weight_out[...], mixed_grad[...], across, preferred_element_type=F32)
-    activated, hidden_grad = slopes(hidden, act_grad)
-    return (
-        jnp.dot(hidden_grad, aligned[...], preferred_element_type=F32),
-        jnp.dot(activated, mixed_grad[...], preferred_element_type=F32),
-    )
-
-
-def far_side_kernel(
-    which, weight_in, weight_out, scale, norm, cot, other_norm, other_cot, sent, aligned, mixed_grad
+    in_terms, out_terms = [], []
+    for norm, cot in sets:
+        channels = norm.shape[2]
+        normed = norm[...].reshape(-1, channels)
+        upstream = cot[...].reshape(-1, channels).astype(F32)
+        mixed_grad = (scales * upstream).astype(BF16)
+        hidden = lax.dot_general(weight_in[...], normed, across, preferred_element_type=F32)
+        act_grad = lax.dot_general(weight_out[...], mixed_grad, across, preferred_element_type=F32)
+        activated, hidden_grad = slopes(hidden, act_grad)
+        in_terms.append(jnp.dot(hidden_grad, normed, preferred_element_type=F32))
+        out_terms.append(jnp.dot(activated, mixed_grad, preferred_element_type=F32))
+    return tree_sum(in_terms), tree_sum(out_terms)
+
+
+def one_side_kernel(
+    which, weight_in, weight_out, scale, norm, cot, other_norm, other_cot, out
 ):
+    del which
     sets = ((norm, cot), (other_norm, other_cot))
-    terms = weight_grad_terms(weight_in, weight_out, scale, sets, aligned, mixed_grad)
+    terms = weight_grad_terms(weight_in, weight_out, scale, sets)
     for k in range(2):
-        sent[k] = terms[k].astype(BF16)
-
-
-def near_side_kernel(
-    which,
-    weight_in,
-    weight_out,
-    scale,
-    norm,
-    cot,
-    other_norm,
-    other_cot,
-    got,
-    in_grad,
-    out_grad,
-    aligned,
-    mixed_grad,
-):
-    sets = ((norm, cot), (other_norm, other_cot))
-    terms = weight_grad_terms(weight_in, weight_out, scale, sets, aligned, mixed_grad)
+        out[k] = terms[k].astype(out.dtype)
+
+
+def last_sum_kernel(kept, got, in_grad, out_grad):
     for k, out in enumerate((in_grad, out_grad)):
-        out[...] = terms[k] + got[k].astype(F32)
+        out[...] = kept[k] + got[k].astype(F32)
 
 
 def chip_sum_kernel(kept, got, *rest):
@@ -691,21 +673,19 @@
     other_gathered = lax.ppermute(gathered, "row", other_core)
     other_cotangents = lax.ppermute(cotangents, "row", other_core)
 
-    def side_terms(kernel, number, more, after, outs, name):
+    def side_terms(number, dtype, after, name):
         chunk = pl.BlockSpec((share, channels), lambda _, w: (w[number], 0))
         return pl.pallas_call(
-            follow(kernel, 1, 7 + len(more), len(after)),
+            follow(one_side_kernel, 1, 7, 1),
             grid_spec=pltpu.PrefetchScalarGridSpec(
                 num_scalar_prefetch=1,
                 grid=(1,),
                 in_specs=[chunk, chunk, whole_block(channels)]
                 + [pl.BlockSpec(memory_space=pltpu.VMEM)] * 4
-                + [whole_block(*part.shape) for part in more]
-                + [IN_PLACE] * len(after),
-                out_specs=[whole_block(*out.shape) for out in outs],
-                scratch_shapes=[pltpu.VMEM((2 * tokens, channels), BF16)] * 2,
+                + [IN_PLACE],
+                out_specs=whole_block(2, share, channels),
             ),
-            out_shape=outs,
+            out_shape=jax.ShapeDtypeStruct((2, share, channels), dtype),
             compiler_params=params(),
             cost_estimate=NO_COST,
             name=name,
@@ -718,15 +698,10 @@
             cotangents,
             other_gathered,
             other_cotangents,
-            *more,
-            *after,
+            after,
         )
 
-    pair = jax.ShapeDtypeStruct((2, share, channels), BF16)
-    single = jax.ShapeDtypeStruct((share, channels), F32)
-    (sent,) = side_terms(
-        far_side_kernel, 0, [], [sums], [pair], "weight_grads_far_side"
-    )
+    sent = side_terms(0, BF16, sums, "weight_grads_far_side")
     got = lax.ppermute(sent, "row", other_side)
     scattered = lax.all_to_all(
         sums.reshape(half, piece, wide),
@@ -777,10 +752,8 @@
     totals = lax.all_to_all(
         copies, "row", split_axis=0, concat_axis=0, tiled=True, axis_index_groups=alike
     )
-    weight_in_grad, weight_out_grad = side_terms(
-        near_side_kernel, 1, [got], [copies], [single, single], "weight_grads_near_side"
-    )
-    totals, weight_in_grad = lax.optimization_barrier((totals, weight_in_grad))
+    kept = side_terms(1, F32, copies, "weight_grads_near_side")
+    totals, kept = lax.optimization_barrier((totals, kept))
     other_totals = lax.ppermute(totals, "row", other_core)
     kernel_grad, *vector_grads = pl.pallas_call(
         unpack_kernel,
@@ -797,6 +770,17 @@
         name="kernel_grad_unpack",
     )(parity, totals, other_totals)
 
+    weight_in_grad, weight_out_grad = pl.pallas_call(
+        last_sum_kernel,
+        grid=(1,),
+        in_specs=[whole_block(2, share, channels)] * 2,
+        out_specs=[whole_block(share, channels)] * 2,
+        out_shape=[jax.ShapeDtypeStruct((share, channels), F32)] * 2,
+        compiler_params=params(),
+        cost_estimate=NO_COST,
+        name="weight_grads_sum",
+    )(kept, got)
+
     return (
         block_out.reshape(voxels.shape),
         voxel_grad.reshape(voxels.shape),

time: 84.6 us -> 90.6 us (1.071)
  the two profiles are of different devices: /device:TPU:1 before, /device:TPU:0 now
where the time goes in v20:
time: 90.6 us; the launch traced here: 89.9 us
  Pallas kernels  37.1 us (41%)
  starting transfers between devices  26.9 us (30%)
  waiting for transfers between devices  18 us (20%)
  local copies, waits for them, and re-layouts  6.87 us (8%)
    ppermute x6, starting transfers between devices, along_line(): lax.ppermute(cells, 'row', [(i, (i + quad * steps) % count) for i in rang...  9.39 us
    ppermute x1, waiting for transfers between devices, on_device(): got = lax.ppermute(sent, 'row', other_side)  8.58 us
    pallas_call x1, Pallas kernels, on_device(): pl.pallas_call(mlp_kernel, grid=(units // block,), in_specs=[whole, pl.Bl...  8.31 us
    pallas_call x2, Pallas kernels, side_terms(): pl.pallas_call(follow(one_side_kernel, 1, 7, 1), grid_spec=pltpu.Prefetch...  7.7 us
    unnamed x36, local copies, waits for them, and re-layouts  6.87 us
    pallas_call x1, Pallas kernels, on_device(): pl.pallas_call(functools.partial(kernel_grad_kernel, planes, height), gri...  6.17 us
    ppermute x2, starting transfers between devices, rims(): lax.ppermute(cells, 'row', [(i, i ^ 1) for i in range(count)])  5.11 us
    all_to_all x1, starting transfers between devices, on_device(): lax.all_to_all(copies, 'row', split_axis=0, concat_axis=0, tiled=True, ax...  4.94 us
  transfers between devices with their start and end apart: 17, of which 8 were waited for; matrix products, arithmetic and copies ran while one was open for 0% of the time, Pallas kernels for 38%

profile of v20, /device:TPU:0, one launch (start us, length us, event | category | flops | bytes accessed | tf_op | source)
XLA Modules:
  0.0 89.9 jit_solution(8259087528122001573)
XLA Ops:
  0.6 3.1 %collective-permute-start.2 = (bf16[128,768]{1,0:T(8,128)(2,1)}, bf16[128,768]{1,0:T(8,128)(2,1)S(1)}, u32[]{:S(2)}, u32[]{:S(2)}) collective-permute-start(bf16[128,768]{1,0:T(8,128)(2,1)} %bitcast.14), channel_id=1, source_target_pairs={{0,4},{1,5},{2,6},{3,7},{4,8},{5,9},{6,10},{7,11},{8,12},{9,13},{1... | collective-permute-start | bytes 589832 | tf_op jit(solution)/shard_map/ppermute | solution.py:496
  3.7 0.7 collective-permute-start.1
  4.4 2.9 %collective-permute-start = (bf16[128,768]{1,0:T(8,128)(2,1)}, bf16[128,768]{1,0:T(8,128)(2,1)S(1)}, u32[]{:S(2)}, u32[]{:S(2)}) collective-permute-start(bf16[128,768]{1,0:T(8,128)(2,1)} %bitcast.10), channel_id=1, source_target_pairs={{0,1},{1,0},{2,3},{3,2},{4,5},{5,4},{6,7},{7,6},{8,9},{9,8},{10,11... | collective-permute-start | bytes 589832 | tf_op jit(solution)/shard_map/ppermute | solution.py:469
  7.3 2.6 %collective-permute-start.3 = (bf16[128,768]{1,0:T(8,128)(2,1)}, bf16[128,768]{1,0:T(8,128)(2,1)S(1)}, u32[]{:S(2)}, u32[]{:S(2)}) collective-permute-start(bf16[128,768]{1,0:T(8,128)(2,1)} %bitcast.15), channel_id=1, source_target_pairs={{0,12},{1,13},{2,14},{3,15},{4,0},{5,1},{6,2},{7,3},{8,4},{9,5},{1... | collective-permute-start | bytes 589832 | tf_op jit(solution)/shard_map/ppermute | solution.py:496
  9.9 1.0 %collective-permute-done.2.refs_6_.rest_1_ = bf16[128,768]{1,0:T(8,128)(2,1)S(1)} collective-permute-done((bf16[128,768]{1,0:T(8,128)(2,1)}, bf16[128,768]{1,0:T(8,128)(2,1)S(1)}, u32[]{:S(2)}, u32[]{:S(2)}) %collective-permute-start.2) | collective-permute-done | bytes 196640 | tf_op jit(solution)/shard_map/ppermute | solution.py:496
  11.0 1.2 %copy-done = f32[343,768]{1,0:T(8,128)S(1)} copy-done((f32[343,768]{1,0:T(8,128)S(1)}, f32[343,768]{1,0:T(8,128)}, u32[]{:S(2)}) %copy-start) | copy-done | bytes 1053720
  12.2 0.9 %copy-done.5 = bf16[4,4,8,768]{3,2,1,0:T(8,128)(2,1)S(1)} copy-done((bf16[4,4,8,768]{3,2,1,0:T(8,128)(2,1)S(1)}, bf16[4,4,8,768]{3,2,1,0:T(8,128)(2,1)}, u32[]{:S(2)}) %copy-start.5) | copy-done | bytes 196632
  13.1 0.7 copy-done.16
  13.8 0.7 copy-done.17
  14.5 2.1 %own_conv.1 = (f32[128,768]{1,0:T(8,128)S(1)}, f32[6,9,7,8,128]{4,3,2,1,0:T(8,128)S(1)}, f32[8,768]{1,0:T(8,128)S(1)}) custom-call(bf16[128,768]{1,0:T(8,128)(2,1)S(1)} %bitcast.11, f32[343,768]{1,0:T(8,128)S(1)} %copy-done, f32[768]{0:T(1024)S(1)} %copy-done.16, f32[768]{0:T(1024)S(1)} %copy-done.17), custom_call_target="tpu_custom_call" | custom-call | tf_op jit(solution)/shard_map/own_conv/pallas_call | solution.py:506
  16.6 0.0 copy-start.6
  16.7 0.0 copy-start.9
  16.7 0.0 copy-start.15
  16.7 1.3 %collective-permute-done.3.refs_7_.rest_3_ = bf16[128,768]{1,0:T(8,128)(2,1)S(1)} collective-permute-done((bf16[128,768]{1,0:T(8,128)(2,1)}, bf16[128,768]{1,0:T(8,128)(2,1)S(1)}, u32[]{:S(2)}, u32[]{:S(2)}) %collective-permute-start.3) | collective-permute-done | bytes 196640 | tf_op jit(solution)/shard_map/ppermute | solution.py:496
  17.9 2.7 %rim_conv.1 = (bf16[128,768]{1,0:T(8,128)(2,1)S(1)}, f32[128,768]{1,0:T(8,128)S(1)}) custom-call(s32[1]{0:T(128)} %bitcast.refs_0_.core, bf16[128,768]{1,0:T(8,128)(2,1)S(1)} %collective-permute-done.refs_1_.inner, bf16[128,768]{1,0:T(8,128)(2,1)S(1)} %collective-permute-done.1.refs_2_.outer, f32[6,9,7,8,128]{4,3,2,1,0:T(8,128)S(1)} %get-tuple-element.40.refs_3_, ...), custom_call_target="tpu_custom_call" | custom-call | tf_op jit(solution)/shard_map/rim_conv/pallas_call | solution.py:524
  20.7 1.4 %collective-permute-done.4.rest_2_ = bf16[128,768]{1,0:T(8,128)(2,1)S(1)} collective-permute-done((bf16[128,768]{1,0:T(8,128)(2,1)S(1)}, bf16[128,768]{1,0:T(8,128)(2,1)S(1)}, u32[]{:S(2)}, u32[]{:S(2)}) %collective-permute-start.4) | collective-permute-done | bytes 196640 | tf_op jit(solution)/shard_map/ppermute | solution.py:496
  22.0 1.3 %collective-permute-start.6 = (bf16[128,768]{1,0:T(8,128)(2,1)S(1)}, bf16[128,768]{1,0:T(8,128)(2,1)S(1)}, u32[]{:S(2)}, u32[]{:S(2)}) collective-permute-start(bf16[128,768]{1,0:T(8,128)(2,1)S(1)} %get-tuple-element.44.normed.rest_0_), channel_id=1, source_target_pairs={{0,12},{1,13},{2,14},{3,15},{4,0},{5,1},{6,2},{7,3},{8,4},{9,5},{1... | collective-permute-start | bytes 589832 | tf_op jit(solution)/shard_map/ppermute | solution.py:496
  23.3 0.8 collective-permute-start.5
  24.1 8.3 %mlp_both_ways.1 = (bf16[128,768]{1,0:T(8,128)(2,1)}, bf16[128,768]{1,0:T(8,128)(2,1)S(1)}, f32[8,768]{1,0:T(8,128)S(1)}, bf16[4,128,768]{2,1,0:T(8,128)(2,1)S(1)}) custom-call(bf16[128,768]{1,0:T(8,128)(2,1)S(1)} %get-tuple-element.44.normed.rest_0_, bf16[3072,768]{1,0:T(8,128)(2,1)} %refs_1_.3, bf16[3072,768]{1,0:T(8,128)(2,1)} %refs_2_.3, ...), custom_call_target="tpu_custom_call" | custom-call | tf_op jit(solution)/shard_map/mlp_both_ways/pallas_call | solution.py:569
  32.4 0.7 collective-permute-start.9
  33.1 2.2 %collective-permute-start.8 = (bf16[128,768]{1,0:T(8,128)(2,1)S(1)}, bf16[128,768]{1,0:T(8,128)(2,1)S(1)}, u32[]{:S(2)}, u32[]{:S(2)}) collective-permute-start(bf16[128,768]{1,0:T(8,128)(2,1)S(1)} %get-tuple-element.48.grads.refs_2_), channel_id=1, source_target_pairs={{0,1},{1,0},{2,3},{3,2},{4,5},{5,4},{6,7},{7,6},{8,9},{9,8},{10,11... | collective-permute-start | bytes 589832 | tf_op jit(solution)/shard_map/ppermute | solution.py:469
  35.2 1.7 %collective-permute-start.7 = (bf16[128,768]{1,0:T(8,128)(2,1)S(1)}, bf16[128,768]{1,0:T(8,128)(2,1)S(1)}, u32[]{:S(2)}, u32[]{:S(2)}) collective-permute-start(bf16[128,768]{1,0:T(8,128)(2,1)S(1)} %collective-permute-done.5.rest_1_), channel_id=1, source_target_pairs={{0,4},{1,5},{2,6},{3,7},{4,8},{5,9},{6,10},{7,11},{8,12},{9,13},{1... | collective-permute-start | bytes 589832 | tf_op jit(solution)/shard_map/ppermute | solution.py:496
  36.9 0.1 pad_add_fusion.which
  37.0 6.2 %kernel_grad_terms.1 = (bf16[384,384]{1,0:T(8,128)(2,1)S(1)}, bf16[384,384]{1,0:T(8,128)(2,1)S(1)}) custom-call(s32[2]{0:T(128)S(1)} %pad_add_fusion.which, bf16[128,768]{1,0:T(8,128)(2,1)S(1)} %collective-permute-done.refs_1_.inner, bf16[128,768]{1,0:T(8,128)(2,1)S(1)} %bitcast.13, bf16[128,768]{1,0:T(8,128)(2,1)S(1)} %collective-permute-done.1.refs_2_.outer, ...), custom_call_target="tpu_custom_call" | custom-call | tf_op jit(solution)/shard_map/kernel_grad_terms/pallas_call | solution.py:625
  43.2 0.7 copy-done.11
  43.9 0.7 copy-done.13
  44.5 0.7 collective-permute-done.7.rest_2_
  45.3 0.5 collective-permute-start.12
  45.8 1.1 %collective-permute-done.10.got = bf16[384,384]{1,0:T(8,128)(2,1)S(1)} collective-permute-done((bf16[384,384]{1,0:T(8,128)(2,1)S(1)}, bf16[384,384]{1,0:T(8,128)(2,1)S(1)}, u32[]{:S(2)}, u32[]{:S(2)}) %collective-permute-start.10) | collective-permute-done | bytes 294944 | tf_op jit(solution)/shard_map/ppermute | solution.py:651
  46.8 0.8 kernel_grad_chip_sum.1
  47.6 0.1 collective-permute-start.11
  47.8 3.4 %all-to-all-start = ((bf16[8,48,384]{2,1,0:T(8,128)(2,1)}), bf16[8,48,384]{2,1,0:T(8,128)(2,1)S(1)}, u32[]{:S(2)}, u32[]{:S(2)}) async-start(bf16[8,48,384]{2,1,0:T(8,128)(2,1)} %bitcast.8), calls=%async_computation | async-start | bytes 589824 | tf_op jit(solution)/shard_map/all_to_all | solution.py:706
  51.3 0.1 pad_add_fusion.1.refs_0_
  51.3 0.0 copy-start.14
  51.4 0.0 copy-start.2
  51.4 4.0 %weight_grads_far_side.1.refs_6_ = bf16[2,192,768]{2,1,0:T(8,128)(2,1)S(1)} custom-call(s32[2]{0:T(128)S(1)} %pad_add_fusion.1.refs_0_, bf16[3072,768]{1,0:T(8,128)(2,1)} %refs_1_.3, bf16[3072,768]{1,0:T(8,128)(2,1)} %refs_2_.3, f32[768]{0:T(1024)S(1)} %copy-done.15, bf16[4,128,768]{2,1,0:T(8,128)(2,1)S(1)} %get-tuple-element.59.refs_4_, ...), custom_call_target="tpu_custom_call" | custom-call | tf_op jit(solution)/shard_map/weight_grads_far_side/pallas_call | solution.py:678
  55.4 4.3 %input_grad_conv.1 = (bf16[128,768]{1,0:T(8,128)(2,1)}, f32[8,128]{1,0:T(8,128)S(1)}) custom-call(s32[1]{0:T(128)} %bitcast.refs_0_.core, bf16[128,768]{1,0:T(8,128)(2,1)S(1)} %copy-done.14, bf16[128,768]{1,0:T(8,128)(2,1)S(1)} %copy-done.8, bf16[128,768]{1,0:T(8,128)(2,1)S(1)} %copy-done.12, f32[343,768]{1,0:T(8,128)S(1)} %copy-done.1, ...), custom_call_target="tpu_custom_call" | custom-call | tf_op jit(solution)/shard_map/input_grad_conv/pallas_call | solution.py:714
  59.7 0.8 copy-done.4
  60.6 1.0 %all-to-all-done.refs_0_ = bf16[8,48,384]{2,1,0:T(8,128)(2,1)S(1)} async-done(((bf16[8,48,384]{2,1,0:T(8,128)(2,1)}), bf16[8,48,384]{2,1,0:T(8,128)(2,1)S(1)}, u32[]{:S(2)}, u32[]{:S(2)}) %all-to-all-start) | async-done | bytes 294944 | tf_op jit(solution)/shard_map/all_to_all | solution.py:706
  61.5 0.8 kernel_grad_sum.1.refs_8_
  62.3 4.9 %all-to-all-start.1 = ((bf16[8,48,384]{2,1,0:T(8,128)(2,1)}), bf16[8,48,384]{2,1,0:T(8,128)(2,1)}, u32[]{:S(2)}, u32[]{:S(2)}) async-start(bf16[8,48,384]{2,1,0:T(8,128)(2,1)} %kernel_grad_sum.1.refs_8_), calls=%async_computation.1 | async-start | bytes 589824 | tf_op jit(solution)/shard_map/all_to_all | solution.py:752
  67.2 2.0 %collective-permute-start.14 = (bf16[2,192,768]{2,1,0:T(8,128)(2,1)}, bf16[2,192,768]{2,1,0:T(8,128)(2,1)}, u32[]{:S(2)}, u32[]{:S(2)}) collective-permute-start(bf16[2,192,768]{2,1,0:T(8,128)(2,1)} %copy-done.4), channel_id=1, source_target_pairs={{0,2},{1,3},{2,0},{3,1},{4,6},{5,7},{6,4},{7,5},{8,10},{9,11},{10,... | collective-permute-start | bytes 1769480 | tf_op jit(solution)/shard_map/ppermute | solution.py:705
  69.2 1.1 %copy-done.3 = bf16[4,128,768]{2,1,0:T(8,128)(2,1)S(1)} copy-done((bf16[4,128,768]{2,1,0:T(8,128)(2,1)S(1)}, bf16[4,128,768]{2,1,0:T(8,128)(2,1)}, u32[]{:S(2)}) %copy-start.3) | copy-done | bytes 786456
  70.4 3.7 %weight_grads_near_side.1.kept = f32[2,192,768]{2,1,0:T(8,128)S(1)} custom-call(s32[2]{0:T(128)S(1)} %pad_add_fusion.1.refs_0_, bf16[3072,768]{1,0:T(8,128)(2,1)} %refs_1_.3, bf16[3072,768]{1,0:T(8,128)(2,1)} %refs_2_.3, f32[768]{0:T(1024)S(1)} %copy-done.15, bf16[4,128,768]{2,1,0:T(8,128)(2,1)S(1)} %get-tuple-element.59.refs_4_, ...), custom_call_target="tpu_custom_call" | custom-call | tf_op jit(solution)/shard_map/weight_grads_near_side/pallas_call | solution.py:678
  74.1 3.0 %all-to-all-done.1.own = bf16[8,48,384]{2,1,0:T(8,128)(2,1)} async-done(((bf16[8,48,384]{2,1,0:T(8,128)(2,1)}), bf16[8,48,384]{2,1,0:T(8,128)(2,1)}, u32[]{:S(2)}, u32[]{:S(2)}) %all-to-all-start.1) | async-done | bytes 294944 | tf_op jit(solution)/shard_map/all_to_all | solution.py:752
  77.1 8.6 %collective-permute-done.14.got = bf16[2,192,768]{2,1,0:T(8,128)(2,1)} collective-permute-done((bf16[2,192,768]{2,1,0:T(8,128)(2,1)}, bf16[2,192,768]{2,1,0:T(8,128)(2,1)}, u32[]{:S(2)}, u32[]{:S(2)}) %collective-permute-start.14) | collective-permute-done | bytes 589856 | tf_op jit(solution)/shard_map/ppermute | solution.py:705
  85.7 2.2 %weight_grads_sum.1 = (f32[192,768]{1,0:T(8,128)}, f32[192,768]{1,0:T(8,128)}) custom-call(f32[2,192,768]{2,1,0:T(8,128)S(1)} %weight_grads_near_side.1.kept, bf16[2,192,768]{2,1,0:T(8,128)(2,1)} %collective-permute-done.14.got), custom_call_target="tpu_custom_call" | custom-call | tf_op jit(solution)/shard_map/weight_grads_sum/pallas_call | solution.py:773
  87.9 2.0 %kernel_grad_unpack.1 = (f32[343,768]{1,0:T(8,128)}, f32[768]{0:T(1024)}, f32[768]{0:T(1024)}, f32[768]{0:T(1024)}) custom-call(s32[1]{0:T(128)} %bitcast.refs_0_.core, bf16[8,48,384]{2,1,0:T(8,128)(2,1)} %all-to-all-done.1.own, bf16[8,48,384]{2,1,0:T(8,128)(2,1)S(1)} %collective-permute-done.13.other), custom_call_target="tpu_custom_call" | custom-call | tf_op jit(solution)/shard_map/kernel_grad_unpack/pallas_call | solution.py:758
  (35 shorter events, 0.1 us)
Async XLA Ops:
  0.6 10.3 %collective-permute-start.2 = (bf16[128,768]{1,0:T(8,128)(2,1)}, bf16[128,768]{1,0:T(8,128)(2,1)S(1)}, u32[]{:S(2)}, u32[]{:S(2)}) collective-permute-start(bf16[128,768]{1,0:T(8,128)(2,1)} %bitcast.14), channel_id=1, source_target_pairs={{0,4},{1,5},{2,6},{3,7},{4,8},{5,9},{6,10},{7,11},{8,12},{9,13},{1... | collective-permute-start | bytes 589832 | tf_op jit(solution)/shard_map/ppermute | solution.py:496
  3.7 13.0 %collective-permute-start.1 = (bf16[128,768]{1,0:T(8,128)(2,1)}, bf16[128,768]{1,0:T(8,128)(2,1)S(1)}, u32[]{:S(2)}, u32[]{:S(2)}) collective-permute-start(bf16[128,768]{1,0:T(8,128)(2,1)} %bitcast.9), channel_id=1, source_target_pairs={{1,2},{3,4},{5,6},{7,8},{9,10},{11,12},{13,14},{2,1},{4,3},{6,5},{... | collective-permute-start | bytes 589832 | tf_op jit(solution)/shard_map/ppermute | solution.py:470
  4.4 12.3 %collective-permute-start = (bf16[128,768]{1,0:T(8,128)(2,1)}, bf16[128,768]{1,0:T(8,128)(2,1)S(1)}, u32[]{:S(2)}, u32[]{:S(2)}) collective-permute-start(bf16[128,768]{1,0:T(8,128)(2,1)} %bitcast.10), channel_id=1, source_target_pairs={{0,1},{1,0},{2,3},{3,2},{4,5},{5,4},{6,7},{7,6},{8,9},{9,8},{10,11... | collective-permute-start | bytes 589832 | tf_op jit(solution)/shard_map/ppermute | solution.py:469
  7.3 10.6 %collective-permute-start.3 = (bf16[128,768]{1,0:T(8,128)(2,1)}, bf16[128,768]{1,0:T(8,128)(2,1)S(1)}, u32[]{:S(2)}, u32[]{:S(2)}) collective-permute-start(bf16[128,768]{1,0:T(8,128)(2,1)} %bitcast.15), channel_id=1, source_target_pairs={{0,12},{1,13},{2,14},{3,15},{4,0},{5,1},{6,2},{7,3},{8,4},{9,5},{1... | collective-permute-start | bytes 589832 | tf_op jit(solution)/shard_map/ppermute | solution.py:496
  10.9 11.1 %collective-permute-start.4 = (bf16[128,768]{1,0:T(8,128)(2,1)S(1)}, bf16[128,768]{1,0:T(8,128)(2,1)S(1)}, u32[]{:S(2)}, u32[]{:S(2)}) collective-permute-start(bf16[128,768]{1,0:T(8,128)(2,1)S(1)} %collective-permute-done.2.refs_6_.rest_1_), channel_id=1, source_target_pairs={{0,4},{1,5},{2,6},{3,7},{4,8},{5,9},{6,10},{7,11},{8,12},{9,13},{1... | collective-permute-start | bytes 589832 | tf_op jit(solution)/shard_map/ppermute | solution.py:496
  11.0 1.2 %copy-start = (f32[343,768]{1,0:T(8,128)S(1)}, f32[343,768]{1,0:T(8,128)}, u32[]{:S(2)}) copy-start(f32[343,768]{1,0:T(8,128)} %refs_4_.1) | copy-start | bytes 3161092
  12.2 0.9 %copy-start.5 = (bf16[4,4,8,768]{3,2,1,0:T(8,128)(2,1)S(1)}, bf16[4,4,8,768]{3,2,1,0:T(8,128)(2,1)}, u32[]{:S(2)}) copy-start(bf16[4,4,8,768]{3,2,1,0:T(8,128)(2,1)} %param.8) | copy-start | bytes 589828
  13.1 0.7 copy-start.16
  13.8 0.7 copy-start.17
  16.6 7.4 %copy-start.6 = (bf16[4,4,8,768]{3,2,1,0:T(8,128)(2,1)S(1)}, bf16[4,4,8,768]{3,2,1,0:T(8,128)(2,1)}, u32[]{:S(2)}) copy-start(bf16[4,4,8,768]{3,2,1,0:T(8,128)(2,1)} %param.8) | copy-start | bytes 589828
  16.7 7.4 %copy-start.9 = (bf16[4,4,8,768]{3,2,1,0:T(8,128)(2,1)S(1)}, bf16[4,4,8,768]{3,2,1,0:T(8,128)(2,1)}, u32[]{:S(2)}) copy-start(bf16[4,4,8,768]{3,2,1,0:T(8,128)(2,1)} %param.15) | copy-start | bytes 589828
  16.7 7.4 %copy-start.15 = (f32[768]{0:T(1024)S(1)}, f32[768]{0:T(1024)}, u32[]{:S(2)}) copy-start(f32[768]{0:T(1024)} %refs_3_.3) | copy-start | bytes 9220
  22.0 13.2 %collective-permute-start.6 = (bf16[128,768]{1,0:T(8,128)(2,1)S(1)}, bf16[128,768]{1,0:T(8,128)(2,1)S(1)}, u32[]{:S(2)}, u32[]{:S(2)}) collective-permute-start(bf16[128,768]{1,0:T(8,128)(2,1)S(1)} %get-tuple-element.44.normed.rest_0_), channel_id=1, source_target_pairs={{0,12},{1,13},{2,14},{3,15},{4,0},{5,1},{6,2},{7,3},{8,4},{9,5},{1... | collective-permute-start | bytes 589832 | tf_op jit(solution)/shard_map/ppermute | solution.py:496
  23.3 11.9 %collective-permute-start.5 = (bf16[128,768]{1,0:T(8,128)(2,1)S(1)}, bf16[128,768]{1,0:T(8,128)(2,1)S(1)}, u32[]{:S(2)}, u32[]{:S(2)}) collective-permute-start(bf16[128,768]{1,0:T(8,128)(2,1)S(1)} %get-tuple-element.44.normed.rest_0_), channel_id=1, source_target_pairs={{0,4},{1,5},{2,6},{3,7},{4,8},{5,9},{6,10},{7,11},{8,12},{9,13},{1... | collective-permute-start | bytes 589832 | tf_op jit(solution)/shard_map/ppermute | solution.py:496
  32.4 14.4 %copy-start.7 = (bf16[128,768]{1,0:T(8,128)(2,1)}, bf16[128,768]{1,0:T(8,128)(2,1)S(1)}, u32[]{:S(2)}) copy-start(bf16[128,768]{1,0:T(8,128)(2,1)S(1)} %get-tuple-element.48.grads.refs_2_) | copy-start | bytes 589828
  32.4 10.8 %collective-permute-start.9 = (bf16[128,768]{1,0:T(8,128)(2,1)S(1)}, bf16[128,768]{1,0:T(8,128)(2,1)S(1)}, u32[]{:S(2)}, u32[]{:S(2)}) collective-permute-start(bf16[128,768]{1,0:T(8,128)(2,1)S(1)} %get-tuple-element.48.grads.refs_2_), channel_id=1, source_target_pairs={{1,2},{3,4},{5,6},{7,8},{9,10},{11,12},{13,14},{2,1},{4,3},{6,5},{... | collective-permute-start | bytes 589832 | tf_op jit(solution)/shard_map/ppermute | solution.py:470
  33.1 10.8 %collective-permute-start.8 = (bf16[128,768]{1,0:T(8,128)(2,1)S(1)}, bf16[128,768]{1,0:T(8,128)(2,1)S(1)}, u32[]{:S(2)}, u32[]{:S(2)}) collective-permute-start(bf16[128,768]{1,0:T(8,128)(2,1)S(1)} %get-tuple-element.48.grads.refs_2_), channel_id=1, source_target_pairs={{0,1},{1,0},{2,3},{3,2},{4,5},{5,4},{6,7},{7,6},{8,9},{9,8},{10,11... | collective-permute-start | bytes 589832 | tf_op jit(solution)/shard_map/ppermute | solution.py:469
  35.2 10.0 %collective-permute-start.7 = (bf16[128,768]{1,0:T(8,128)(2,1)S(1)}, bf16[128,768]{1,0:T(8,128)(2,1)S(1)}, u32[]{:S(2)}, u32[]{:S(2)}) collective-permute-start(bf16[128,768]{1,0:T(8,128)(2,1)S(1)} %collective-permute-done.5.rest_1_), channel_id=1, source_target_pairs={{0,4},{1,5},{2,6},{3,7},{4,8},{5,9},{6,10},{7,11},{8,12},{9,13},{1... | collective-permute-start | bytes 589832 | tf_op jit(solution)/shard_map/ppermute | solution.py:496
  43.2 0.7 copy-start.11
  43.9 0.7 copy-start.13
  45.2 1.6 %collective-permute-start.10 = (bf16[384,384]{1,0:T(8,128)(2,1)S(1)}, bf16[384,384]{1,0:T(8,128)(2,1)S(1)}, u32[]{:S(2)}, u32[]{:S(2)}) collective-permute-start(bf16[384,384]{1,0:T(8,128)(2,1)S(1)} %get-tuple-element.56), channel_id=1, source_target_pairs={{0,1},{1,0},{2,3},{3,2},{4,5},{5,4},{6,7},{7,6},{8,9},{9,8},{10,11... | collective-permute-start | bytes 884744 | tf_op jit(solution)/shard_map/ppermute | solution.py:651
  45.3 6.1 %collective-permute-start.12 = (bf16[4,128,768]{2,1,0:T(8,128)(2,1)S(1)}, bf16[4,128,768]{2,1,0:T(8,128)(2,1)S(1)}, u32[]{:S(2)}, u32[]{:S(2)}) collective-permute-start(bf16[4,128,768]{2,1,0:T(8,128)(2,1)S(1)} %get-tuple-element.60.refs_5_), channel_id=1, source_target_pairs={{0,1},{1,0},{2,3},{3,2},{4,5},{5,4},{6,7},{7,6},{8,9},{9,8},{10,11... | collective-permute-start | bytes 2359304 | tf_op jit(solution)/shard_map/ppermute | solution.py:674
  47.6 3.7 %collective-permute-start.11 = (bf16[4,128,768]{2,1,0:T(8,128)(2,1)S(1)}, bf16[4,128,768]{2,1,0:T(8,128)(2,1)S(1)}, u32[]{:S(2)}, u32[]{:S(2)}) collective-permute-start(bf16[4,128,768]{2,1,0:T(8,128)(2,1)S(1)} %get-tuple-element.59.refs_4_), channel_id=1, source_target_pairs={{0,1},{1,0},{2,3},{3,2},{4,5},{5,4},{6,7},{7,6},{8,9},{9,8},{10,11... | collective-permute-start | bytes 2359304 | tf_op jit(solution)/shard_map/ppermute | solution.py:673
  47.8 13.7 %all-to-all-start = ((bf16[8,48,384]{2,1,0:T(8,128)(2,1)}), bf16[8,48,384]{2,1,0:T(8,128)(2,1)S(1)}, u32[]{:S(2)}, u32[]{:S(2)}) async-start(bf16[8,48,384]{2,1,0:T(8,128)(2,1)} %bitcast.8), calls=%async_computation | async-start | bytes 589824 | tf_op jit(solution)/shard_map/all_to_all | solution.py:706
  51.3 4.0 %copy-start.1 = (f32[343,768]{1,0:T(8,128)S(1)}, f32[343,768]{1,0:T(8,128)}, u32[]{:S(2)}) copy-start(f32[343,768]{1,0:T(8,128)} %refs_4_.1) | copy-start | bytes 3161092
  51.3 4.1 %copy-start.8 = (bf16[128,768]{1,0:T(8,128)(2,1)S(1)}, bf16[128,768]{1,0:T(8,128)(2,1)}, u32[]{:S(2)}) copy-start(bf16[128,768]{1,0:T(8,128)(2,1)} %copy-done.7) | copy-start | bytes 589828
  51.3 4.1 %copy-start.10 = (bf16[4,4,8,768]{3,2,1,0:T(8,128)(2,1)S(1)}, bf16[4,4,8,768]{3,2,1,0:T(8,128)(2,1)}, u32[]{:S(2)}) copy-start(bf16[4,4,8,768]{3,2,1,0:T(8,128)(2,1)} %param.15) | copy-start | bytes 589828
  51.3 4.1 %copy-start.12 = (bf16[128,768]{1,0:T(8,128)(2,1)S(1)}, bf16[128,768]{1,0:T(8,128)(2,1)}, u32[]{:S(2)}) copy-start(bf16[128,768]{1,0:T(8,128)(2,1)} %copy-done.11) | copy-start | bytes 589828
  51.3 4.1 %copy-start.14 = (bf16[128,768]{1,0:T(8,128)(2,1)S(1)}, bf16[128,768]{1,0:T(8,128)(2,1)}, u32[]{:S(2)}) copy-start(bf16[128,768]{1,0:T(8,128)(2,1)} %copy-done.13) | copy-start | bytes 589828
  51.4 4.0 %copy-start.2 = (bf16[4,128,768]{2,1,0:T(8,128)(2,1)}, bf16[4,128,768]{2,1,0:T(8,128)(2,1)S(1)}, u32[]{:S(2)}) copy-start(bf16[4,128,768]{2,1,0:T(8,128)(2,1)S(1)} %collective-permute-done.11.refs_6_) | copy-start | bytes 2359300
  59.7 0.8 copy-start.4
  62.3 14.9 %all-to-all-start.1 = ((bf16[8,48,384]{2,1,0:T(8,128)(2,1)}), bf16[8,48,384]{2,1,0:T(8,128)(2,1)}, u32[]{:S(2)}, u32[]{:S(2)}) async-start(bf16[8,48,384]{2,1,0:T(8,128)(2,1)} %kernel_grad_sum.1.refs_8_), calls=%async_computation.1 | async-start | bytes 589824 | tf_op jit(solution)/shard_map/all_to_all | solution.py:752
  67.2 18.5 %collective-permute-start.14 = (bf16[2,192,768]{2,1,0:T(8,128)(2,1)}, bf16[2,192,768]{2,1,0:T(8,128)(2,1)}, u32[]{:S(2)}, u32[]{:S(2)}) collective-permute-start(bf16[2,192,768]{2,1,0:T(8,128)(2,1)} %copy-done.4), channel_id=1, source_target_pairs={{0,2},{1,3},{2,0},{3,1},{4,6},{5,7},{6,4},{7,5},{8,10},{9,11},{10,... | collective-permute-start | bytes 1769480 | tf_op jit(solution)/shard_map/ppermute | solution.py:705
  69.2 1.1 %copy-start.3 = (bf16[4,128,768]{2,1,0:T(8,128)(2,1)S(1)}, bf16[4,128,768]{2,1,0:T(8,128)(2,1)}, u32[]{:S(2)}) copy-start(bf16[4,128,768]{2,1,0:T(8,128)(2,1)} %copy-done.2) | copy-start | bytes 2359300
  77.1 10.8 %collective-permute-start.13 = (bf16[8,48,384]{2,1,0:T(8,128)(2,1)}, bf16[8,48,384]{2,1,0:T(8,128)(2,1)S(1)}, u32[]{:S(2)}, u32[]{:S(2)}) collective-permute-start(bf16[8,48,384]{2,1,0:T(8,128)(2,1)} %all-to-all-done.1.own), channel_id=1, source_target_pairs={{0,1},{1,0},{2,3},{3,2},{4,5},{5,4},{6,7},{7,6},{8,9},{9,8},{10,11... | collective-permute-start | bytes 884744 | tf_op jit(solution)/shard_map/ppermute | solution.py:757

commit v21 on v20

--- a/solution.py
+++ b/solution.py
@@ -390,19 +390,22 @@
     return tree_sum(in_terms), tree_sum(out_terms)
 
 
-def one_side_kernel(
-    which, weight_in, weight_out, scale, norm, cot, other_norm, other_cot, out
+def far_side_kernel(which, weight_in, weight_out, scale, norm, cot, other_norm, other_cot, sent):
+    del which
+    sets = ((norm, cot), (other_norm, other_cot))
+    terms = weight_grad_terms(weight_in, weight_out, scale, sets)
+    for k in range(2):
+        sent[k] = terms[k].astype(BF16)
+
+
+def near_side_kernel(
+    which, weight_in, weight_out, scale, norm, cot, other_norm, other_cot, got, in_grad, out_grad
 ):
     del which
     sets = ((norm, cot), (other_norm, other_cot))
     terms = weight_grad_terms(weight_in, weight_out, scale, sets)
-    for k in range(2):
-        out[k] = terms[k].astype(out.dtype)
-
-
-def last_sum_kernel(kept, got, in_grad, out_grad):
     for k, out in enumerate((in_grad, out_grad)):
-        out[...] = kept[k] + got[k].astype(F32)
+        out[...] = terms[k] + got[k].astype(F32)
 
 
 def chip_sum_kernel(kept, got, *rest):
@@ -673,19 +676,20 @@
     other_gathered = lax.ppermute(gathered, "row", other_core)
     other_cotangents = lax.ppermute(cotangents, "row", other_core)
 
-    def side_terms(number, dtype, after, name):
+    def side_terms(kernel, number, more, after, outs, name):
         chunk = pl.BlockSpec((share, channels), lambda _, w: (w[number], 0))
         return pl.pallas_call(
-            follow(one_side_kernel, 1, 7, 1),
+            follow(kernel, 1, 7 + len(more), 1),
             grid_spec=pltpu.PrefetchScalarGridSpec(
                 num_scalar_prefetch=1,
                 grid=(1,),
                 in_specs=[chunk, chunk, whole_block(channels)]
                 + [pl.BlockSpec(memory_space=pltpu.VMEM)] * 4
+                + [whole_block(*part.shape) for part in more]
                 + [IN_PLACE],
-                out_specs=whole_block(2, share, channels),
+                out_specs=[whole_block(*out.shape) for out in outs],
             ),
-            out_shape=jax.ShapeDtypeStruct((2, share, channels), dtype),
+            out_shape=outs,
             compiler_params=params(),
             cost_estimate=NO_COST,
             name=name,
@@ -698,10 +702,13 @@
             cotangents,
             other_gathered,
             other_cotangents,
+            *more,
             after,
         )
 
-    sent = side_terms(0, BF16, sums, "weight_grads_far_side")
+    pair = jax.ShapeDtypeStruct((2, share, channels), BF16)
+    single = jax.ShapeDtypeStruct((share, channels), F32)
+    (sent,) = side_terms(far_side_kernel, 0, [], sums, [pair], "weight_grads_far_side")
     got = lax.ppermute(sent, "row", other_side)
     scattered = lax.all_to_all(
         sums.reshape(half, piece, wide),
@@ -752,8 +759,10 @@
     totals = lax.all_to_all(
         copies, "row", split_axis=0, concat_axis=0, tiled=True, axis_index_groups=alike
     )
-    kept = side_terms(1, F32, copies, "weight_grads_near_side")
-    totals, kept = lax.optimization_barrier((totals, kept))
+    weight_in_grad, weight_out_grad = side_terms(
+        near_side_kernel, 1, [got], copies, [single, single], "weight_grads_near_side"
+    )
+    totals, weight_in_grad = lax.optimization_barrier((totals, weight_in_grad))
     other_totals = lax.ppermute(totals, "row", other_core)
     kernel_grad, *vector_grads = pl.pallas_call(
         unpack_kernel,
@@ -770,17 +779,6 @@
         name="kernel_grad_unpack",
     )(parity, totals, other_totals)
 
-    weight_in_grad, weight_out_grad = pl.pallas_call(
-        last_sum_kernel,
-        grid=(1,),
-        in_specs=[whole_block(2, share, channels)] * 2,
-        out_specs=[whole_block(share, channels)] * 2,
-        out_shape=[jax.ShapeDtypeStruct((share, channels), F32)] * 2,
-        compiler_params=params(),
-        cost_estimate=NO_COST,
-        name="weight_grads_sum",
-    )(kept, got)
-
     return (
         block_out.reshape(voxels.shape),
         voxel_grad.reshape(voxels.shape),

time: 90.6 us -> 84.5 us (0.933)
  the two profiles are of different devices: /device:TPU:0 before, /device:TPU:1 now
where the time goes in v21:
time: 84.5 us; the launch traced here: 83.7 us
  Pallas kernels  35.7 us (42%)
  starting transfers between devices  31.4 us (37%)
  waiting for transfers between devices  10.7 us (13%)
  local copies, waits for them, and re-layouts  4.93 us (6%)
    pallas_call x2, Pallas kernels, side_terms(): pl.pallas_call(follow(kernel, 1, 7 + len(more), 1), grid_spec=pltpu.Prefe...  9.4 us
    pallas_call x1, Pallas kernels, on_device(): pl.pallas_call(mlp_kernel, grid=(units // block,), in_specs=[whole, pl.Bl...  8.29 us
    ppermute x6, starting transfers between devices, along_line(): lax.ppermute(cells, 'row', [(i, (i + quad * steps) % count) for i in rang...  7.52 us
    pallas_call x1, Pallas kernels, on_device(): pl.pallas_call(functools.partial(kernel_grad_kernel, planes, height), gri...  6.18 us
    all_to_all x1, starting transfers between devices, on_device(): lax.all_to_all(sums.reshape(half, piece, wide), 'row', split_axis=0, conc...  5.81 us
    ppermute x1, waiting for transfers between devices, on_device(): got = lax.ppermute(sent, 'row', other_side)  5.79 us
    ppermute x2, starting transfers between devices, rims(): lax.ppermute(cells, 'row', between + [(j, i) for i, j in between])  4.93 us
    unnamed x32, local copies, waits for them, and re-layouts  4.93 us
  transfers between devices with their start and end apart: 17, of which 6 were waited for; matrix products, arithmetic and copies ran while one was open for 0% of the time, Pallas kernels for 41%

profile of v21, /device:TPU:1, one launch (start us, length us, event | category | flops | bytes accessed | tf_op | source)
XLA Modules:
  0.0 83.7 jit_solution(3418357491089480105)
XLA Ops:
  0.6 2.2 %collective-permute-start.2 = (bf16[128,768]{1,0:T(8,128)(2,1)}, bf16[128,768]{1,0:T(8,128)(2,1)S(1)}, u32[]{:S(2)}, u32[]{:S(2)}) collective-permute-start(bf16[128,768]{1,0:T(8,128)(2,1)} %bitcast.14), channel_id=1, source_target_pairs={{0,4},{1,5},{2,6},{3,7},{4,8},{5,9},{6,10},{7,11},{8,12},{9,13},{1... | collective-permute-start | bytes 589832 | tf_op jit(solution)/shard_map/ppermute | solution.py:499
  2.8 1.0 %collective-permute-start = (bf16[128,768]{1,0:T(8,128)(2,1)}, bf16[128,768]{1,0:T(8,128)(2,1)S(1)}, u32[]{:S(2)}, u32[]{:S(2)}) collective-permute-start(bf16[128,768]{1,0:T(8,128)(2,1)} %bitcast.9), channel_id=1, source_target_pairs={{0,1},{1,0},{2,3},{3,2},{4,5},{5,4},{6,7},{7,6},{8,9},{9,8},{10,11... | collective-permute-start | bytes 589832 | tf_op jit(solution)/shard_map/ppermute | solution.py:472
  3.8 3.0 %collective-permute-start.1 = (bf16[128,768]{1,0:T(8,128)(2,1)}, bf16[128,768]{1,0:T(8,128)(2,1)S(1)}, u32[]{:S(2)}, u32[]{:S(2)}) collective-permute-start(bf16[128,768]{1,0:T(8,128)(2,1)} %bitcast.10), channel_id=1, source_target_pairs={{1,2},{3,4},{5,6},{7,8},{9,10},{11,12},{13,14},{2,1},{4,3},{6,5},{... | collective-permute-start | bytes 589832 | tf_op jit(solution)/shard_map/ppermute | solution.py:473
  6.8 2.0 %collective-permute-start.3 = (bf16[128,768]{1,0:T(8,128)(2,1)}, bf16[128,768]{1,0:T(8,128)(2,1)S(1)}, u32[]{:S(2)}, u32[]{:S(2)}) collective-permute-start(bf16[128,768]{1,0:T(8,128)(2,1)} %bitcast.15), channel_id=1, source_target_pairs={{0,12},{1,13},{2,14},{3,15},{4,0},{5,1},{6,2},{7,3},{8,4},{9,5},{1... | collective-permute-start | bytes 589832 | tf_op jit(solution)/shard_map/ppermute | solution.py:499
  8.8 0.9 %collective-permute-done.2.refs_6_.rest_1_ = bf16[128,768]{1,0:T(8,128)(2,1)S(1)} collective-permute-done((bf16[128,768]{1,0:T(8,128)(2,1)}, bf16[128,768]{1,0:T(8,128)(2,1)S(1)}, u32[]{:S(2)}, u32[]{:S(2)}) %collective-permute-start.2) | collective-permute-done | bytes 196640 | tf_op jit(solution)/shard_map/ppermute | solution.py:499
  9.7 0.0 collective-permute-start.4
  9.7 1.2 %copy-done = f32[343,768]{1,0:T(8,128)S(1)} copy-done((f32[343,768]{1,0:T(8,128)S(1)}, f32[343,768]{1,0:T(8,128)}, u32[]{:S(2)}) %copy-start) | copy-done | bytes 1053720
  10.9 0.9 %copy-done.2 = bf16[4,4,8,768]{3,2,1,0:T(8,128)(2,1)S(1)} copy-done((bf16[4,4,8,768]{3,2,1,0:T(8,128)(2,1)S(1)}, bf16[4,4,8,768]{3,2,1,0:T(8,128)(2,1)}, u32[]{:S(2)}) %copy-start.2) | copy-done | bytes 196632
  11.8 0.7 copy-done.13
  12.5 0.7 copy-done.15
  13.2 2.2 %own_conv.1 = (f32[128,768]{1,0:T(8,128)S(1)}, f32[6,9,7,8,128]{4,3,2,1,0:T(8,128)S(1)}, f32[8,768]{1,0:T(8,128)S(1)}) custom-call(bf16[128,768]{1,0:T(8,128)(2,1)S(1)} %bitcast.11, f32[343,768]{1,0:T(8,128)S(1)} %copy-done, f32[768]{0:T(1024)S(1)} %copy-done.13, f32[768]{0:T(1024)S(1)} %copy-done.15), custom_call_target="tpu_custom_call" | custom-call | tf_op jit(solution)/shard_map/own_conv/pallas_call | solution.py:509
  15.4 0.0 copy-start.3
  15.4 0.0 copy-start.6
  15.4 0.0 copy-start.12
  15.4 0.0 copy-start.14
  15.4 0.0 collective-permute-done.1.refs_2_.outer
  15.4 0.0 collective-permute-done.3.refs_7_.rest_3_
  15.5 2.7 %rim_conv.1 = (bf16[128,768]{1,0:T(8,128)(2,1)S(1)}, f32[128,768]{1,0:T(8,128)S(1)}) custom-call(s32[1]{0:T(128)} %bitcast.refs_0_.core, bf16[128,768]{1,0:T(8,128)(2,1)S(1)} %collective-permute-done.refs_1_.inner, bf16[128,768]{1,0:T(8,128)(2,1)S(1)} %collective-permute-done.1.refs_2_.outer, f32[6,9,7,8,128]{4,3,2,1,0:T(8,128)S(1)} %get-tuple-element.40.refs_3_, ...), custom_call_target="tpu_custom_call" | custom-call | tf_op jit(solution)/shard_map/rim_conv/pallas_call | solution.py:527
  18.2 1.4 %collective-permute-done.4.rest_2_ = bf16[128,768]{1,0:T(8,128)(2,1)S(1)} collective-permute-done((bf16[128,768]{1,0:T(8,128)(2,1)S(1)}, bf16[128,768]{1,0:T(8,128)(2,1)S(1)}, u32[]{:S(2)}, u32[]{:S(2)}) %collective-permute-start.4) | collective-permute-done | bytes 196640 | tf_op jit(solution)/shard_map/ppermute | solution.py:499
  19.6 0.0 collective-permute-start.5
  19.6 3.3 %collective-permute-start.6 = (bf16[128,768]{1,0:T(8,128)(2,1)S(1)}, bf16[128,768]{1,0:T(8,128)(2,1)S(1)}, u32[]{:S(2)}, u32[]{:S(2)}) collective-permute-start(bf16[128,768]{1,0:T(8,128)(2,1)S(1)} %get-tuple-element.44.normed.rest_0_), channel_id=1, source_target_pairs={{0,12},{1,13},{2,14},{3,15},{4,0},{5,1},{6,2},{7,3},{8,4},{9,5},{1... | collective-permute-start | bytes 589832 | tf_op jit(solution)/shard_map/ppermute | solution.py:499
  22.9 8.3 %mlp_both_ways.1 = (bf16[128,768]{1,0:T(8,128)(2,1)}, bf16[128,768]{1,0:T(8,128)(2,1)S(1)}, f32[8,768]{1,0:T(8,128)S(1)}, bf16[4,128,768]{2,1,0:T(8,128)(2,1)S(1)}) custom-call(bf16[128,768]{1,0:T(8,128)(2,1)S(1)} %get-tuple-element.44.normed.rest_0_, bf16[3072,768]{1,0:T(8,128)(2,1)} %refs_1_.3, bf16[3072,768]{1,0:T(8,128)(2,1)} %refs_2_.3, ...), custom_call_target="tpu_custom_call" | custom-call | tf_op jit(solution)/shard_map/mlp_both_ways/pallas_call | solution.py:572
  31.2 3.7 %collective-permute-start.8 = (bf16[128,768]{1,0:T(8,128)(2,1)S(1)}, bf16[128,768]{1,0:T(8,128)(2,1)S(1)}, u32[]{:S(2)}, u32[]{:S(2)}) collective-permute-start(bf16[128,768]{1,0:T(8,128)(2,1)S(1)} %get-tuple-element.48.grads.refs_2_), channel_id=1, source_target_pairs={{0,1},{1,0},{2,3},{3,2},{4,5},{5,4},{6,7},{7,6},{8,9},{9,8},{10,11... | collective-permute-start | bytes 589832 | tf_op jit(solution)/shard_map/ppermute | solution.py:472
  34.9 1.9 %collective-permute-start.9 = (bf16[128,768]{1,0:T(8,128)(2,1)S(1)}, bf16[128,768]{1,0:T(8,128)(2,1)S(1)}, u32[]{:S(2)}, u32[]{:S(2)}) collective-permute-start(bf16[128,768]{1,0:T(8,128)(2,1)S(1)} %get-tuple-element.48.grads.refs_2_), channel_id=1, source_target_pairs={{1,2},{3,4},{5,6},{7,8},{9,10},{11,12},{13,14},{2,1},{4,3},{6,5},{... | collective-permute-start | bytes 589832 | tf_op jit(solution)/shard_map/ppermute | solution.py:473
  36.8 0.1 collective-permute-start.7
  36.9 0.1 pad_add_fusion.which
  37.0 6.2 %kernel_grad_terms.1 = (bf16[384,384]{1,0:T(8,128)(2,1)S(1)}, bf16[384,384]{1,0:T(8,128)(2,1)S(1)}) custom-call(s32[2]{0:T(128)S(1)} %pad_add_fusion.which, bf16[128,768]{1,0:T(8,128)(2,1)S(1)} %collective-permute-done.refs_1_.inner, bf16[128,768]{1,0:T(8,128)(2,1)S(1)} %bitcast.13, bf16[128,768]{1,0:T(8,128)(2,1)S(1)} %collective-permute-done.1.refs_2_.outer, ...), custom_call_target="tpu_custom_call" | custom-call | tf_op jit(solution)/shard_map/kernel_grad_terms/pallas_call | solution.py:628
  43.2 0.0 copy-start.8
  43.2 0.7 copy-done.8
  43.8 0.7 copy-done.10
  44.5 0.3 collective-permute-done.7.rest_2_
  44.9 0.2 collective-permute-start.10
  45.1 0.3 collective-permute-start.12
  45.4 1.1 %collective-permute-done.10.got = bf16[384,384]{1,0:T(8,128)(2,1)S(1)} collective-permute-done((bf16[384,384]{1,0:T(8,128)(2,1)S(1)}, bf16[384,384]{1,0:T(8,128)(2,1)S(1)}, u32[]{:S(2)}, u32[]{:S(2)}) %collective-permute-start.10) | collective-permute-done | bytes 294944 | tf_op jit(solution)/shard_map/ppermute | solution.py:654
  46.5 0.8 kernel_grad_chip_sum.1
  47.3 0.2 collective-permute-start.11
  47.5 5.8 %all-to-all-start = ((bf16[8,48,384]{2,1,0:T(8,128)(2,1)}), bf16[8,48,384]{2,1,0:T(8,128)(2,1)S(1)}, u32[]{:S(2)}, u32[]{:S(2)}) async-start(bf16[8,48,384]{2,1,0:T(8,128)(2,1)} %bitcast.8), calls=%async_computation | async-start | bytes 589824 | tf_op jit(solution)/shard_map/all_to_all | solution.py:713
  53.3 0.1 pad_add_fusion.1.refs_0_
  53.4 4.6 %weight_grads_far_side.1.refs_6_ = bf16[2,192,768]{2,1,0:T(8,128)(2,1)} custom-call(s32[2]{0:T(128)S(1)} %pad_add_fusion.1.refs_0_, bf16[3072,768]{1,0:T(8,128)(2,1)} %refs_1_.3, bf16[3072,768]{1,0:T(8,128)(2,1)} %refs_2_.3, f32[768]{0:T(1024)S(1)} %copy-done.12, bf16[4,128,768]{2,1,0:T(8,128)(2,1)S(1)} %get-tuple-element.59.refs_4_, ...), custom_call_target="tpu_custom_call" | custom-call | tf_op jit(solution)/shard_map/weight_grads_far_side/pallas_call | solution.py:681
  58.0 1.5 %collective-permute-start.13 = (bf16[2,192,768]{2,1,0:T(8,128)(2,1)}, bf16[2,192,768]{2,1,0:T(8,128)(2,1)}, u32[]{:S(2)}, u32[]{:S(2)}) collective-permute-start(bf16[2,192,768]{2,1,0:T(8,128)(2,1)} %weight_grads_far_side.1.refs_6_), channel_id=1, source_target_pairs={{0,2},{1,3},{2,0},{3,1},{4,6},{5,7},{6,4},{7,5},{8,10},{9,11},{10,... | collective-permute-start | bytes 1769480 | tf_op jit(solution)/shard_map/ppermute | solution.py:712
  59.5 4.3 %input_grad_conv.1 = (bf16[128,768]{1,0:T(8,128)(2,1)}, f32[8,128]{1,0:T(8,128)S(1)}) custom-call(s32[1]{0:T(128)} %bitcast.refs_0_.core, bf16[128,768]{1,0:T(8,128)(2,1)S(1)} %copy-done.9, bf16[128,768]{1,0:T(8,128)(2,1)S(1)} %copy-done.5, bf16[128,768]{1,0:T(8,128)(2,1)S(1)} %copy-done.11, f32[343,768]{1,0:T(8,128)S(1)} %copy-done.1, ...), custom_call_target="tpu_custom_call" | custom-call | tf_op jit(solution)/shard_map/input_grad_conv/pallas_call | solution.py:721
  63.8 0.8 kernel_grad_sum.1.refs_9_
  64.5 4.3 %all-to-all-start.1 = ((bf16[8,48,384]{2,1,0:T(8,128)(2,1)}), bf16[8,48,384]{2,1,0:T(8,128)(2,1)S(1)}, u32[]{:S(2)}, u32[]{:S(2)}) async-start(bf16[8,48,384]{2,1,0:T(8,128)(2,1)} %kernel_grad_sum.1.refs_9_), calls=%async_computation.1 | async-start | bytes 589824 | tf_op jit(solution)/shard_map/all_to_all | solution.py:759
  68.8 5.8 %collective-permute-done.13.refs_8_ = bf16[2,192,768]{2,1,0:T(8,128)(2,1)} collective-permute-done((bf16[2,192,768]{2,1,0:T(8,128)(2,1)}, bf16[2,192,768]{2,1,0:T(8,128)(2,1)}, u32[]{:S(2)}, u32[]{:S(2)}) %collective-permute-start.13) | collective-permute-done | bytes 589856 | tf_op jit(solution)/shard_map/ppermute | solution.py:712
  74.6 4.8 %weight_grads_near_side.1 = (f32[192,768]{1,0:T(8,128)}, f32[192,768]{1,0:T(8,128)}) custom-call(s32[2]{0:T(128)S(1)} %pad_add_fusion.1.refs_0_, bf16[3072,768]{1,0:T(8,128)(2,1)} %refs_1_.3, bf16[3072,768]{1,0:T(8,128)(2,1)} %refs_2_.3, f32[768]{0:T(1024)S(1)} %copy-done.12, bf16[4,128,768]{2,1,0:T(8,128)(2,1)S(1)} %get-tuple-element.59.refs_4_, ...), custom_call_target="tpu_custom_call" | custom-call | tf_op jit(solution)/shard_map/weight_grads_near_side/pallas_call | solution.py:681
  79.4 2.0 %collective-permute-start.14 = (bf16[8,48,384]{2,1,0:T(8,128)(2,1)S(1)}, bf16[8,48,384]{2,1,0:T(8,128)(2,1)S(1)}, u32[]{:S(2)}, u32[]{:S(2)}) collective-permute-start(bf16[8,48,384]{2,1,0:T(8,128)(2,1)S(1)} %all-to-all-done.1.own), channel_id=1, source_target_pairs={{0,1},{1,0},{2,3},{3,2},{4,5},{5,4},{6,7},{7,6},{8,9},{9,8},{10,11... | collective-permute-start | bytes 884744 | tf_op jit(solution)/shard_map/ppermute | solution.py:766
  81.4 1.2 %collective-permute-done.14.other = bf16[8,48,384]{2,1,0:T(8,128)(2,1)S(1)} collective-permute-done((bf16[8,48,384]{2,1,0:T(8,128)(2,1)S(1)}, bf16[8,48,384]{2,1,0:T(8,128)(2,1)S(1)}, u32[]{:S(2)}, u32[]{:S(2)}) %collective-permute-start.14) | collective-permute-done | bytes 294944 | tf_op jit(solution)/shard_map/ppermute | solution.py:766
  82.6 1.1 %kernel_grad_unpack.1 = (f32[343,768]{1,0:T(8,128)}, f32[768]{0:T(1024)}, f32[768]{0:T(1024)}, f32[768]{0:T(1024)}) custom-call(s32[1]{0:T(128)} %bitcast.refs_0_.core, bf16[8,48,384]{2,1,0:T(8,128)(2,1)S(1)} %all-to-all-done.1.own, bf16[8,48,384]{2,1,0:T(8,128)(2,1)S(1)} %collective-permute-done.14.other), custom_call_target="tpu_custom_call" | custom-call | tf_op jit(solution)/shard_map/kernel_grad_unpack/pallas_call | solution.py:767
  (30 shorter events, 0.1 us)
Async XLA Ops:
  0.6 9.0 %collective-permute-start.2 = (bf16[128,768]{1,0:T(8,128)(2,1)}, bf16[128,768]{1,0:T(8,128)(2,1)S(1)}, u32[]{:S(2)}, u32[]{:S(2)}) collective-permute-start(bf16[128,768]{1,0:T(8,128)(2,1)} %bitcast.14), channel_id=1, source_target_pairs={{0,4},{1,5},{2,6},{3,7},{4,8},{5,9},{6,10},{7,11},{8,12},{9,13},{1... | collective-permute-start | bytes 589832 | tf_op jit(solution)/shard_map/ppermute | solution.py:499
  2.8 12.6 %collective-permute-start = (bf16[128,768]{1,0:T(8,128)(2,1)}, bf16[128,768]{1,0:T(8,128)(2,1)S(1)}, u32[]{:S(2)}, u32[]{:S(2)}) collective-permute-start(bf16[128,768]{1,0:T(8,128)(2,1)} %bitcast.9), channel_id=1, source_target_pairs={{0,1},{1,0},{2,3},{3,2},{4,5},{5,4},{6,7},{7,6},{8,9},{9,8},{10,11... | collective-permute-start | bytes 589832 | tf_op jit(solution)/shard_map/ppermute | solution.py:472
  3.8 11.7 %collective-permute-start.1 = (bf16[128,768]{1,0:T(8,128)(2,1)}, bf16[128,768]{1,0:T(8,128)(2,1)S(1)}, u32[]{:S(2)}, u32[]{:S(2)}) collective-permute-start(bf16[128,768]{1,0:T(8,128)(2,1)} %bitcast.10), channel_id=1, source_target_pairs={{1,2},{3,4},{5,6},{7,8},{9,10},{11,12},{13,14},{2,1},{4,3},{6,5},{... | collective-permute-start | bytes 589832 | tf_op jit(solution)/shard_map/ppermute | solution.py:473
  6.8 8.6 %collective-permute-start.3 = (bf16[128,768]{1,0:T(8,128)(2,1)}, bf16[128,768]{1,0:T(8,128)(2,1)S(1)}, u32[]{:S(2)}, u32[]{:S(2)}) collective-permute-start(bf16[128,768]{1,0:T(8,128)(2,1)} %bitcast.15), channel_id=1, source_target_pairs={{0,12},{1,13},{2,14},{3,15},{4,0},{5,1},{6,2},{7,3},{8,4},{9,5},{1... | collective-permute-start | bytes 589832 | tf_op jit(solution)/shard_map/ppermute | solution.py:499
  9.7 9.9 %collective-permute-start.4 = (bf16[128,768]{1,0:T(8,128)(2,1)S(1)}, bf16[128,768]{1,0:T(8,128)(2,1)S(1)}, u32[]{:S(2)}, u32[]{:S(2)}) collective-permute-start(bf16[128,768]{1,0:T(8,128)(2,1)S(1)} %collective-permute-done.2.refs_6_.rest_1_), channel_id=1, source_target_pairs={{0,4},{1,5},{2,6},{3,7},{4,8},{5,9},{6,10},{7,11},{8,12},{9,13},{1... | collective-permute-start | bytes 589832 | tf_op jit(solution)/shard_map/ppermute | solution.py:499
  9.7 1.2 %copy-start = (f32[343,768]{1,0:T(8,128)S(1)}, f32[343,768]{1,0:T(8,128)}, u32[]{:S(2)}) copy-start(f32[343,768]{1,0:T(8,128)} %refs_4_.1) | copy-start | bytes 3161092
  10.9 0.9 %copy-start.2 = (bf16[4,4,8,768]{3,2,1,0:T(8,128)(2,1)S(1)}, bf16[4,4,8,768]{3,2,1,0:T(8,128)(2,1)}, u32[]{:S(2)}) copy-start(bf16[4,4,8,768]{3,2,1,0:T(8,128)(2,1)} %param.8) | copy-start | bytes 589828
  11.8 0.7 copy-start.13
  12.5 0.7 copy-start.15
  15.4 7.5 %copy-start.3 = (bf16[4,4,8,768]{3,2,1,0:T(8,128)(2,1)S(1)}, bf16[4,4,8,768]{3,2,1,0:T(8,128)(2,1)}, u32[]{:S(2)}) copy-start(bf16[4,4,8,768]{3,2,1,0:T(8,128)(2,1)} %param.8) | copy-start | bytes 589828
  15.4 7.5 %copy-start.6 = (bf16[4,4,8,768]{3,2,1,0:T(8,128)(2,1)S(1)}, bf16[4,4,8,768]{3,2,1,0:T(8,128)(2,1)}, u32[]{:S(2)}) copy-start(bf16[4,4,8,768]{3,2,1,0:T(8,128)(2,1)} %param.15) | copy-start | bytes 589828
  15.4 7.5 %copy-start.12 = (f32[768]{0:T(1024)S(1)}, f32[768]{0:T(1024)}, u32[]{:S(2)}) copy-start(f32[768]{0:T(1024)} %refs_3_.3) | copy-start | bytes 9220
  15.4 7.5 %copy-start.14 = (f32[768]{0:T(1024)S(1)}, f32[768]{0:T(1024)}, u32[]{:S(2)}) copy-start(f32[768]{0:T(1024)} %norm_gain.1) | copy-start | bytes 9220
  19.6 17.2 %collective-permute-start.5 = (bf16[128,768]{1,0:T(8,128)(2,1)S(1)}, bf16[128,768]{1,0:T(8,128)(2,1)S(1)}, u32[]{:S(2)}, u32[]{:S(2)}) collective-permute-start(bf16[128,768]{1,0:T(8,128)(2,1)S(1)} %get-tuple-element.44.normed.rest_0_), channel_id=1, source_target_pairs={{0,4},{1,5},{2,6},{3,7},{4,8},{5,9},{6,10},{7,11},{8,12},{9,13},{1... | collective-permute-start | bytes 589832 | tf_op jit(solution)/shard_map/ppermute | solution.py:499
  19.6 17.2 %collective-permute-start.6 = (bf16[128,768]{1,0:T(8,128)(2,1)S(1)}, bf16[128,768]{1,0:T(8,128)(2,1)S(1)}, u32[]{:S(2)}, u32[]{:S(2)}) collective-permute-start(bf16[128,768]{1,0:T(8,128)(2,1)S(1)} %get-tuple-element.44.normed.rest_0_), channel_id=1, source_target_pairs={{0,12},{1,13},{2,14},{3,15},{4,0},{5,1},{6,2},{7,3},{8,4},{9,5},{1... | collective-permute-start | bytes 589832 | tf_op jit(solution)/shard_map/ppermute | solution.py:499
  31.2 15.3 %copy-start.4 = (bf16[128,768]{1,0:T(8,128)(2,1)}, bf16[128,768]{1,0:T(8,128)(2,1)S(1)}, u32[]{:S(2)}) copy-start(bf16[128,768]{1,0:T(8,128)(2,1)S(1)} %get-tuple-element.48.grads.refs_2_) | copy-start | bytes 589828
  31.2 12.0 %collective-permute-start.8 = (bf16[128,768]{1,0:T(8,128)(2,1)S(1)}, bf16[128,768]{1,0:T(8,128)(2,1)S(1)}, u32[]{:S(2)}, u32[]{:S(2)}) collective-permute-start(bf16[128,768]{1,0:T(8,128)(2,1)S(1)} %get-tuple-element.48.grads.refs_2_), channel_id=1, source_target_pairs={{0,1},{1,0},{2,3},{3,2},{4,5},{5,4},{6,7},{7,6},{8,9},{9,8},{10,11... | collective-permute-start | bytes 589832 | tf_op jit(solution)/shard_map/ppermute | solution.py:472
  34.9 9.0 %collective-permute-start.9 = (bf16[128,768]{1,0:T(8,128)(2,1)S(1)}, bf16[128,768]{1,0:T(8,128)(2,1)S(1)}, u32[]{:S(2)}, u32[]{:S(2)}) collective-permute-start(bf16[128,768]{1,0:T(8,128)(2,1)S(1)} %get-tuple-element.48.grads.refs_2_), channel_id=1, source_target_pairs={{1,2},{3,4},{5,6},{7,8},{9,10},{11,12},{13,14},{2,1},{4,3},{6,5},{... | collective-permute-start | bytes 589832 | tf_op jit(solution)/shard_map/ppermute | solution.py:473
  36.8 8.1 %collective-permute-start.7 = (bf16[128,768]{1,0:T(8,128)(2,1)S(1)}, bf16[128,768]{1,0:T(8,128)(2,1)S(1)}, u32[]{:S(2)}, u32[]{:S(2)}) collective-permute-start(bf16[128,768]{1,0:T(8,128)(2,1)S(1)} %collective-permute-done.5.rest_1_), channel_id=1, source_target_pairs={{0,4},{1,5},{2,6},{3,7},{4,8},{5,9},{6,10},{7,11},{8,12},{9,13},{1... | collective-permute-start | bytes 589832 | tf_op jit(solution)/shard_map/ppermute | solution.py:499
  43.2 0.7 copy-start.8
  43.8 0.7 copy-start.10
  44.9 1.6 %collective-permute-start.10 = (bf16[384,384]{1,0:T(8,128)(2,1)S(1)}, bf16[384,384]{1,0:T(8,128)(2,1)S(1)}, u32[]{:S(2)}, u32[]{:S(2)}) collective-permute-start(bf16[384,384]{1,0:T(8,128)(2,1)S(1)} %get-tuple-element.56), channel_id=1, source_target_pairs={{0,1},{1,0},{2,3},{3,2},{4,5},{5,4},{6,7},{7,6},{8,9},{9,8},{10,11... | collective-permute-start | bytes 884744 | tf_op jit(solution)/shard_map/ppermute | solution.py:654
  45.1 8.3 %collective-permute-start.12 = (bf16[4,128,768]{2,1,0:T(8,128)(2,1)S(1)}, bf16[4,128,768]{2,1,0:T(8,128)(2,1)S(1)}, u32[]{:S(2)}, u32[]{:S(2)}) collective-permute-start(bf16[4,128,768]{2,1,0:T(8,128)(2,1)S(1)} %get-tuple-element.60.refs_5_), channel_id=1, source_target_pairs={{0,1},{1,0},{2,3},{3,2},{4,5},{5,4},{6,7},{7,6},{8,9},{9,8},{10,11... | collective-permute-start | bytes 2359304 | tf_op jit(solution)/shard_map/ppermute | solution.py:677
  47.3 6.1 %collective-permute-start.11 = (bf16[4,128,768]{2,1,0:T(8,128)(2,1)S(1)}, bf16[4,128,768]{2,1,0:T(8,128)(2,1)S(1)}, u32[]{:S(2)}, u32[]{:S(2)}) collective-permute-start(bf16[4,128,768]{2,1,0:T(8,128)(2,1)S(1)} %get-tuple-element.59.refs_4_), channel_id=1, source_target_pairs={{0,1},{1,0},{2,3},{3,2},{4,5},{5,4},{6,7},{7,6},{8,9},{9,8},{10,11... | collective-permute-start | bytes 2359304 | tf_op jit(solution)/shard_map/ppermute | solution.py:676
  47.5 16.3 %all-to-all-start = ((bf16[8,48,384]{2,1,0:T(8,128)(2,1)}), bf16[8,48,384]{2,1,0:T(8,128)(2,1)S(1)}, u32[]{:S(2)}, u32[]{:S(2)}) async-start(bf16[8,48,384]{2,1,0:T(8,128)(2,1)} %bitcast.8), calls=%async_computation | async-start | bytes 589824 | tf_op jit(solution)/shard_map/all_to_all | solution.py:713
  53.4 6.1 %copy-start.1 = (f32[343,768]{1,0:T(8,128)S(1)}, f32[343,768]{1,0:T(8,128)}, u32[]{:S(2)}) copy-start(f32[343,768]{1,0:T(8,128)} %refs_4_.1) | copy-start | bytes 3161092
  53.4 6.1 %copy-start.5 = (bf16[128,768]{1,0:T(8,128)(2,1)S(1)}, bf16[128,768]{1,0:T(8,128)(2,1)}, u32[]{:S(2)}) copy-start(bf16[128,768]{1,0:T(8,128)(2,1)} %copy-done.4) | copy-start | bytes 589828
  53.4 6.1 %copy-start.7 = (bf16[4,4,8,768]{3,2,1,0:T(8,128)(2,1)S(1)}, bf16[4,4,8,768]{3,2,1,0:T(8,128)(2,1)}, u32[]{:S(2)}) copy-start(bf16[4,4,8,768]{3,2,1,0:T(8,128)(2,1)} %param.15) | copy-start | bytes 589828
  53.4 6.1 %copy-start.9 = (bf16[128,768]{1,0:T(8,128)(2,1)S(1)}, bf16[128,768]{1,0:T(8,128)(2,1)}, u32[]{:S(2)}) copy-start(bf16[128,768]{1,0:T(8,128)(2,1)} %copy-done.8) | copy-start | bytes 589828
  53.4 6.1 %copy-start.11 = (bf16[128,768]{1,0:T(8,128)(2,1)S(1)}, bf16[128,768]{1,0:T(8,128)(2,1)}, u32[]{:S(2)}) copy-start(bf16[128,768]{1,0:T(8,128)(2,1)} %copy-done.10) | copy-start | bytes 589828
  58.0 16.6 %collective-permute-start.13 = (bf16[2,192,768]{2,1,0:T(8,128)(2,1)}, bf16[2,192,768]{2,1,0:T(8,128)(2,1)}, u32[]{:S(2)}, u32[]{:S(2)}) collective-permute-start(bf16[2,192,768]{2,1,0:T(8,128)(2,1)} %weight_grads_far_side.1.refs_6_), channel_id=1, source_target_pairs={{0,2},{1,3},{2,0},{3,1},{4,6},{5,7},{6,4},{7,5},{8,10},{9,11},{10,... | collective-permute-start | bytes 1769480 | tf_op jit(solution)/shard_map/ppermute | solution.py:712
  64.5 14.9 %all-to-all-start.1 = ((bf16[8,48,384]{2,1,0:T(8,128)(2,1)}), bf16[8,48,384]{2,1,0:T(8,128)(2,1)S(1)}, u32[]{:S(2)}, u32[]{:S(2)}) async-start(bf16[8,48,384]{2,1,0:T(8,128)(2,1)} %kernel_grad_sum.1.refs_9_), calls=%async_computation.1 | async-start | bytes 589824 | tf_op jit(solution)/shard_map/all_to_all | solution.py:759
  79.4 3.2 %collective-permute-start.14 = (bf16[8,48,384]{2,1,0:T(8,128)(2,1)S(1)}, bf16[8,48,384]{2,1,0:T(8,128)(2,1)S(1)}, u32[]{:S(2)}, u32[]{:S(2)}) collective-permute-start(bf16[8,48,384]{2,1,0:T(8,128)(2,1)S(1)} %all-to-all-done.1.own), channel_id=1, source_target_pairs={{0,1},{1,0},{2,3},{3,2},{4,5},{5,4},{6,7},{7,6},{8,9},{9,8},{10,11... | collective-permute-start | bytes 884744 | tf_op jit(solution)/shard_map/ppermute | solution.py:766

commit v22 on v21

--- a/solution.py
+++ b/solution.py
@@ -17,10 +17,6 @@
 root_half = 0.7071067811865476
 inv_root_tau = 0.3989422804014327
 norm_eps = 1e-06
-erf_step = 0.3275911
-erf_terms = tuple(
-    0.5 * a for a in (0.254829592, -0.284496736, 1.421413741, -1.453152027, 1.061405429)
-)
 
 NO_COST = pl.CostEstimate(flops=0, bytes_accessed=0, transcendentals=0)
 
@@ -359,17 +355,9 @@
 
 
 def slopes(hidden, act_grad):
-    bell = jnp.exp(-0.5 * hidden * hidden)
-    below = 1.0 + (erf_step * root_half) * jnp.abs(hidden)
-    t = pl.reciprocal(below, approx=True)
-    t = t * (2.0 - below * t)
-    poly = erf_terms[-1]
-    for term in erf_terms[-2::-1]:
-        poly = poly * t + term
-    tail = poly * t * bell
-    cover = jnp.where(hidden < 0.0, tail, 1.0 - tail)
+    cover = 0.5 * (1.0 + lax.erf(hidden * root_half))
     activated = (hidden * cover).astype(BF16)
-    slope = cover + hidden * bell * inv_root_tau
+    slope = cover + hidden * jnp.exp(-0.5 * hidden * hidden) * inv_root_tau
     return activated, (act_grad * slope).astype(BF16)
 
 

time: 84.5 us -> 84.5 us (level)
  no operation moved by 1% of the time
where the time goes in v22:
time: 84.5 us; the launch traced here: 83.6 us
  Pallas kernels  35.2 us (42%)
  starting transfers between devices  31.7 us (38%)
  waiting for transfers between devices  10.8 us (13%)
  local copies, waits for them, and re-layouts  4.93 us (6%)
    pallas_call x2, Pallas kernels, side_terms(): pl.pallas_call(follow(kernel, 1, 7 + len(more), 1), grid_spec=pltpu.Prefe...  9.03 us
    pallas_call x1, Pallas kernels, on_device(): pl.pallas_call(mlp_kernel, grid=(units // block,), in_specs=[whole, pl.Bl...  8.2 us
    ppermute x6, starting transfers between devices, along_line(): lax.ppermute(cells, 'row', [(i, (i + quad * steps) % count) for i in rang...  7.52 us
    pallas_call x1, Pallas kernels, on_device(): pl.pallas_call(functools.partial(kernel_grad_kernel, planes, height), gri...  6.18 us
    ppermute x1, waiting for transfers between devices, on_device(): got = lax.ppermute(sent, 'row', other_side)  5.85 us
    all_to_all x1, starting transfers between devices, on_device(): lax.all_to_all(sums.reshape(half, piece, wide), 'row', split_axis=0, conc...  5.81 us
    ppermute x2, starting transfers between devices, rims(): lax.ppermute(cells, 'row', between + [(j, i) for i, j in between])  4.93 us
    unnamed x32, local copies, waits for them, and re-layouts  4.93 us
  transfers between devices with their start and end apart: 17, of which 6 were waited for; matrix products, arithmetic and copies ran while one was open for 0% of the time, Pallas kernels for 41%

profile of v22, /device:TPU:1, one launch (start us, length us, event | category | flops | bytes accessed | tf_op | source)
XLA Modules:
  0.0 83.6 jit_solution(9754137445471698061)
XLA Ops:
  0.6 2.2 %collective-permute-start.2 = (bf16[128,768]{1,0:T(8,128)(2,1)}, bf16[128,768]{1,0:T(8,128)(2,1)S(1)}, u32[]{:S(2)}, u32[]{:S(2)}) collective-permute-start(bf16[128,768]{1,0:T(8,128)(2,1)} %bitcast.14), channel_id=1, source_target_pairs={{0,4},{1,5},{2,6},{3,7},{4,8},{5,9},{6,10},{7,11},{8,12},{9,13},{1... | collective-permute-start | bytes 589832 | tf_op jit(solution)/shard_map/ppermute | solution.py:487
  2.8 1.0 %collective-permute-start = (bf16[128,768]{1,0:T(8,128)(2,1)}, bf16[128,768]{1,0:T(8,128)(2,1)S(1)}, u32[]{:S(2)}, u32[]{:S(2)}) collective-permute-start(bf16[128,768]{1,0:T(8,128)(2,1)} %bitcast.9), channel_id=1, source_target_pairs={{0,1},{1,0},{2,3},{3,2},{4,5},{5,4},{6,7},{7,6},{8,9},{9,8},{10,11... | collective-permute-start | bytes 589832 | tf_op jit(solution)/shard_map/ppermute | solution.py:460
  3.8 3.0 %collective-permute-start.1 = (bf16[128,768]{1,0:T(8,128)(2,1)}, bf16[128,768]{1,0:T(8,128)(2,1)S(1)}, u32[]{:S(2)}, u32[]{:S(2)}) collective-permute-start(bf16[128,768]{1,0:T(8,128)(2,1)} %bitcast.10), channel_id=1, source_target_pairs={{1,2},{3,4},{5,6},{7,8},{9,10},{11,12},{13,14},{2,1},{4,3},{6,5},{... | collective-permute-start | bytes 589832 | tf_op jit(solution)/shard_map/ppermute | solution.py:461
  6.8 2.0 %collective-permute-start.3 = (bf16[128,768]{1,0:T(8,128)(2,1)}, bf16[128,768]{1,0:T(8,128)(2,1)S(1)}, u32[]{:S(2)}, u32[]{:S(2)}) collective-permute-start(bf16[128,768]{1,0:T(8,128)(2,1)} %bitcast.15), channel_id=1, source_target_pairs={{0,12},{1,13},{2,14},{3,15},{4,0},{5,1},{6,2},{7,3},{8,4},{9,5},{1... | collective-permute-start | bytes 589832 | tf_op jit(solution)/shard_map/ppermute | solution.py:487
  8.8 0.9 %collective-permute-done.2.refs_6_.rest_1_ = bf16[128,768]{1,0:T(8,128)(2,1)S(1)} collective-permute-done((bf16[128,768]{1,0:T(8,128)(2,1)}, bf16[128,768]{1,0:T(8,128)(2,1)S(1)}, u32[]{:S(2)}, u32[]{:S(2)}) %collective-permute-start.2) | collective-permute-done | bytes 196640 | tf_op jit(solution)/shard_map/ppermute | solution.py:487
  9.7 1.2 %copy-done = f32[343,768]{1,0:T(8,128)S(1)} copy-done((f32[343,768]{1,0:T(8,128)S(1)}, f32[343,768]{1,0:T(8,128)}, u32[]{:S(2)}) %copy-start) | copy-done | bytes 1053720
  10.9 0.9 %copy-done.2 = bf16[4,4,8,768]{3,2,1,0:T(8,128)(2,1)S(1)} copy-done((bf16[4,4,8,768]{3,2,1,0:T(8,128)(2,1)S(1)}, bf16[4,4,8,768]{3,2,1,0:T(8,128)(2,1)}, u32[]{:S(2)}) %copy-start.2) | copy-done | bytes 196632
  11.8 0.7 copy-done.13
  12.5 0.7 copy-done.15
  13.2 2.2 %own_conv.1 = (f32[128,768]{1,0:T(8,128)S(1)}, f32[6,9,7,8,128]{4,3,2,1,0:T(8,128)S(1)}, f32[8,768]{1,0:T(8,128)S(1)}) custom-call(bf16[128,768]{1,0:T(8,128)(2,1)S(1)} %bitcast.11, f32[343,768]{1,0:T(8,128)S(1)} %copy-done, f32[768]{0:T(1024)S(1)} %copy-done.13, f32[768]{0:T(1024)S(1)} %copy-done.15), custom_call_target="tpu_custom_call" | custom-call | tf_op jit(solution)/shard_map/own_conv/pallas_call | solution.py:497
  15.4 0.0 copy-start.3
  15.4 0.0 copy-start.6
  15.4 0.0 copy-start.12
  15.4 0.0 copy-start.14
  15.4 0.0 collective-permute-done.refs_1_.inner
  15.4 0.0 collective-permute-done.1.refs_2_.outer
  15.5 2.7 %rim_conv.1 = (bf16[128,768]{1,0:T(8,128)(2,1)S(1)}, f32[128,768]{1,0:T(8,128)S(1)}) custom-call(s32[1]{0:T(128)} %bitcast.refs_0_.core, bf16[128,768]{1,0:T(8,128)(2,1)S(1)} %collective-permute-done.refs_1_.inner, bf16[128,768]{1,0:T(8,128)(2,1)S(1)} %collective-permute-done.1.refs_2_.outer, f32[6,9,7,8,128]{4,3,2,1,0:T(8,128)S(1)} %get-tuple-element.40.refs_3_, ...), custom_call_target="tpu_custom_call" | custom-call | tf_op jit(solution)/shard_map/rim_conv/pallas_call | solution.py:515
  18.2 1.4 %collective-permute-done.4.rest_2_ = bf16[128,768]{1,0:T(8,128)(2,1)S(1)} collective-permute-done((bf16[128,768]{1,0:T(8,128)(2,1)S(1)}, bf16[128,768]{1,0:T(8,128)(2,1)S(1)}, u32[]{:S(2)}, u32[]{:S(2)}) %collective-permute-start.4) | collective-permute-done | bytes 196640 | tf_op jit(solution)/shard_map/ppermute | solution.py:487
  19.6 3.3 %collective-permute-start.6 = (bf16[128,768]{1,0:T(8,128)(2,1)S(1)}, bf16[128,768]{1,0:T(8,128)(2,1)S(1)}, u32[]{:S(2)}, u32[]{:S(2)}) collective-permute-start(bf16[128,768]{1,0:T(8,128)(2,1)S(1)} %get-tuple-element.44.normed.rest_0_), channel_id=1, source_target_pairs={{0,12},{1,13},{2,14},{3,15},{4,0},{5,1},{6,2},{7,3},{8,4},{9,5},{1... | collective-permute-start | bytes 589832 | tf_op jit(solution)/shard_map/ppermute | solution.py:487
  22.9 8.2 %mlp_both_ways.1 = (bf16[128,768]{1,0:T(8,128)(2,1)}, bf16[128,768]{1,0:T(8,128)(2,1)S(1)}, f32[8,768]{1,0:T(8,128)S(1)}, bf16[4,128,768]{2,1,0:T(8,128)(2,1)S(1)}) custom-call(bf16[128,768]{1,0:T(8,128)(2,1)S(1)} %get-tuple-element.44.normed.rest_0_, bf16[3072,768]{1,0:T(8,128)(2,1)} %refs_1_.3, bf16[3072,768]{1,0:T(8,128)(2,1)} %refs_2_.3, ...), custom_call_target="tpu_custom_call" | custom-call | tf_op jit(solution)/shard_map/mlp_both_ways/pallas_call | solution.py:560
  31.1 3.7 %collective-permute-start.8 = (bf16[128,768]{1,0:T(8,128)(2,1)S(1)}, bf16[128,768]{1,0:T(8,128)(2,1)S(1)}, u32[]{:S(2)}, u32[]{:S(2)}) collective-permute-start(bf16[128,768]{1,0:T(8,128)(2,1)S(1)} %get-tuple-element.48.grads.refs_2_), channel_id=1, source_target_pairs={{0,1},{1,0},{2,3},{3,2},{4,5},{5,4},{6,7},{7,6},{8,9},{9,8},{10,11... | collective-permute-start | bytes 589832 | tf_op jit(solution)/shard_map/ppermute | solution.py:460
  34.8 1.9 %collective-permute-start.9 = (bf16[128,768]{1,0:T(8,128)(2,1)S(1)}, bf16[128,768]{1,0:T(8,128)(2,1)S(1)}, u32[]{:S(2)}, u32[]{:S(2)}) collective-permute-start(bf16[128,768]{1,0:T(8,128)(2,1)S(1)} %get-tuple-element.48.grads.refs_2_), channel_id=1, source_target_pairs={{1,2},{3,4},{5,6},{7,8},{9,10},{11,12},{13,14},{2,1},{4,3},{6,5},{... | collective-permute-start | bytes 589832 | tf_op jit(solution)/shard_map/ppermute | solution.py:461
  36.7 0.0 collective-permute-done.6.rest_3_
  36.7 0.1 collective-permute-start.7
  36.8 0.1 pad_add_fusion.which
  36.9 6.2 %kernel_grad_terms.1 = (bf16[384,384]{1,0:T(8,128)(2,1)S(1)}, bf16[384,384]{1,0:T(8,128)(2,1)S(1)}) custom-call(s32[2]{0:T(128)S(1)} %pad_add_fusion.which, bf16[128,768]{1,0:T(8,128)(2,1)S(1)} %collective-permute-done.refs_1_.inner, bf16[128,768]{1,0:T(8,128)(2,1)S(1)} %bitcast.13, bf16[128,768]{1,0:T(8,128)(2,1)S(1)} %collective-permute-done.1.refs_2_.outer, ...), custom_call_target="tpu_custom_call" | custom-call | tf_op jit(solution)/shard_map/kernel_grad_terms/pallas_call | solution.py:616
  43.0 0.0 collective-permute-done.8.refs_1_
  43.1 0.0 copy-start.8
  43.1 0.7 copy-done.8
  43.7 0.7 copy-done.10
  44.4 0.3 collective-permute-done.7.rest_2_
  44.8 0.2 collective-permute-start.10
  45.0 0.3 collective-permute-start.12
  45.3 1.1 %collective-permute-done.10.got = bf16[384,384]{1,0:T(8,128)(2,1)S(1)} collective-permute-done((bf16[384,384]{1,0:T(8,128)(2,1)S(1)}, bf16[384,384]{1,0:T(8,128)(2,1)S(1)}, u32[]{:S(2)}, u32[]{:S(2)}) %collective-permute-start.10) | collective-permute-done | bytes 294944 | tf_op jit(solution)/shard_map/ppermute | solution.py:642
  46.4 0.8 kernel_grad_chip_sum.1
  47.2 0.2 collective-permute-start.11
  47.4 5.8 %all-to-all-start = ((bf16[8,48,384]{2,1,0:T(8,128)(2,1)}), bf16[8,48,384]{2,1,0:T(8,128)(2,1)S(1)}, u32[]{:S(2)}, u32[]{:S(2)}) async-start(bf16[8,48,384]{2,1,0:T(8,128)(2,1)} %bitcast.8), calls=%async_computation | async-start | bytes 589824 | tf_op jit(solution)/shard_map/all_to_all | solution.py:701
  53.2 0.1 pad_add_fusion.1.refs_0_
  53.3 4.4 %weight_grads_far_side.1.refs_6_ = bf16[2,192,768]{2,1,0:T(8,128)(2,1)} custom-call(s32[2]{0:T(128)S(1)} %pad_add_fusion.1.refs_0_, bf16[3072,768]{1,0:T(8,128)(2,1)} %refs_1_.3, bf16[3072,768]{1,0:T(8,128)(2,1)} %refs_2_.3, f32[768]{0:T(1024)S(1)} %copy-done.12, bf16[4,128,768]{2,1,0:T(8,128)(2,1)S(1)} %get-tuple-element.59.refs_4_, ...), custom_call_target="tpu_custom_call" | custom-call | tf_op jit(solution)/shard_map/weight_grads_far_side/pallas_call | solution.py:669
  57.7 1.5 %collective-permute-start.13 = (bf16[2,192,768]{2,1,0:T(8,128)(2,1)}, bf16[2,192,768]{2,1,0:T(8,128)(2,1)}, u32[]{:S(2)}, u32[]{:S(2)}) collective-permute-start(bf16[2,192,768]{2,1,0:T(8,128)(2,1)} %weight_grads_far_side.1.refs_6_), channel_id=1, source_target_pairs={{0,2},{1,3},{2,0},{3,1},{4,6},{5,7},{6,4},{7,5},{8,10},{9,11},{10,... | collective-permute-start | bytes 1769480 | tf_op jit(solution)/shard_map/ppermute | solution.py:700
  59.2 4.3 %input_grad_conv.1 = (bf16[128,768]{1,0:T(8,128)(2,1)}, f32[8,128]{1,0:T(8,128)S(1)}) custom-call(s32[1]{0:T(128)} %bitcast.refs_0_.core, bf16[128,768]{1,0:T(8,128)(2,1)S(1)} %copy-done.9, bf16[128,768]{1,0:T(8,128)(2,1)S(1)} %copy-done.5, bf16[128,768]{1,0:T(8,128)(2,1)S(1)} %copy-done.11, f32[343,768]{1,0:T(8,128)S(1)} %copy-done.1, ...), custom_call_target="tpu_custom_call" | custom-call | tf_op jit(solution)/shard_map/input_grad_conv/pallas_call | solution.py:709
  63.5 0.8 kernel_grad_sum.1.refs_9_
  64.2 4.3 %all-to-all-start.1 = ((bf16[8,48,384]{2,1,0:T(8,128)(2,1)}), bf16[8,48,384]{2,1,0:T(8,128)(2,1)S(1)}, u32[]{:S(2)}, u32[]{:S(2)}) async-start(bf16[8,48,384]{2,1,0:T(8,128)(2,1)} %kernel_grad_sum.1.refs_9_), calls=%async_computation.1 | async-start | bytes 589824 | tf_op jit(solution)/shard_map/all_to_all | solution.py:747
  68.5 5.9 %collective-permute-done.13.refs_8_ = bf16[2,192,768]{2,1,0:T(8,128)(2,1)} collective-permute-done((bf16[2,192,768]{2,1,0:T(8,128)(2,1)}, bf16[2,192,768]{2,1,0:T(8,128)(2,1)}, u32[]{:S(2)}, u32[]{:S(2)}) %collective-permute-start.13) | collective-permute-done | bytes 589856 | tf_op jit(solution)/shard_map/ppermute | solution.py:700
  74.4 4.7 %weight_grads_near_side.1 = (f32[192,768]{1,0:T(8,128)}, f32[192,768]{1,0:T(8,128)}) custom-call(s32[2]{0:T(128)S(1)} %pad_add_fusion.1.refs_0_, bf16[3072,768]{1,0:T(8,128)(2,1)} %refs_1_.3, bf16[3072,768]{1,0:T(8,128)(2,1)} %refs_2_.3, f32[768]{0:T(1024)S(1)} %copy-done.12, bf16[4,128,768]{2,1,0:T(8,128)(2,1)S(1)} %get-tuple-element.59.refs_4_, ...), custom_call_target="tpu_custom_call" | custom-call | tf_op jit(solution)/shard_map/weight_grads_near_side/pallas_call | solution.py:669
  79.0 2.4 %collective-permute-start.14 = (bf16[8,48,384]{2,1,0:T(8,128)(2,1)S(1)}, bf16[8,48,384]{2,1,0:T(8,128)(2,1)S(1)}, u32[]{:S(2)}, u32[]{:S(2)}) collective-permute-start(bf16[8,48,384]{2,1,0:T(8,128)(2,1)S(1)} %all-to-all-done.1.own), channel_id=1, source_target_pairs={{0,1},{1,0},{2,3},{3,2},{4,5},{5,4},{6,7},{7,6},{8,9},{9,8},{10,11... | collective-permute-start | bytes 884744 | tf_op jit(solution)/shard_map/ppermute | solution.py:754
  81.4 1.2 %collective-permute-done.14.other = bf16[8,48,384]{2,1,0:T(8,128)(2,1)S(1)} collective-permute-done((bf16[8,48,384]{2,1,0:T(8,128)(2,1)S(1)}, bf16[8,48,384]{2,1,0:T(8,128)(2,1)S(1)}, u32[]{:S(2)}, u32[]{:S(2)}) %collective-permute-start.14) | collective-permute-done | bytes 294944 | tf_op jit(solution)/shard_map/ppermute | solution.py:754
  82.6 1.1 %kernel_grad_unpack.1 = (f32[343,768]{1,0:T(8,128)}, f32[768]{0:T(1024)}, f32[768]{0:T(1024)}, f32[768]{0:T(1024)}) custom-call(s32[1]{0:T(128)} %bitcast.refs_0_.core, bf16[8,48,384]{2,1,0:T(8,128)(2,1)S(1)} %all-to-all-done.1.own, bf16[8,48,384]{2,1,0:T(8,128)(2,1)S(1)} %collective-permute-done.14.other), custom_call_target="tpu_custom_call" | custom-call | tf_op jit(solution)/shard_map/kernel_grad_unpack/pallas_call | solution.py:755
  (30 shorter events, 0.1 us)
Async XLA Ops:
  0.6 9.0 %collective-permute-start.2 = (bf16[128,768]{1,0:T(8,128)(2,1)}, bf16[128,768]{1,0:T(8,128)(2,1)S(1)}, u32[]{:S(2)}, u32[]{:S(2)}) collective-permute-start(bf16[128,768]{1,0:T(8,128)(2,1)} %bitcast.14), channel_id=1, source_target_pairs={{0,4},{1,5},{2,6},{3,7},{4,8},{5,9},{6,10},{7,11},{8,12},{9,13},{1... | collective-permute-start | bytes 589832 | tf_op jit(solution)/shard_map/ppermute | solution.py:487
  2.8 12.6 %collective-permute-start = (bf16[128,768]{1,0:T(8,128)(2,1)}, bf16[128,768]{1,0:T(8,128)(2,1)S(1)}, u32[]{:S(2)}, u32[]{:S(2)}) collective-permute-start(bf16[128,768]{1,0:T(8,128)(2,1)} %bitcast.9), channel_id=1, source_target_pairs={{0,1},{1,0},{2,3},{3,2},{4,5},{5,4},{6,7},{7,6},{8,9},{9,8},{10,11... | collective-permute-start | bytes 589832 | tf_op jit(solution)/shard_map/ppermute | solution.py:460
  3.8 11.7 %collective-permute-start.1 = (bf16[128,768]{1,0:T(8,128)(2,1)}, bf16[128,768]{1,0:T(8,128)(2,1)S(1)}, u32[]{:S(2)}, u32[]{:S(2)}) collective-permute-start(bf16[128,768]{1,0:T(8,128)(2,1)} %bitcast.10), channel_id=1, source_target_pairs={{1,2},{3,4},{5,6},{7,8},{9,10},{11,12},{13,14},{2,1},{4,3},{6,5},{... | collective-permute-start | bytes 589832 | tf_op jit(solution)/shard_map/ppermute | solution.py:461
  6.8 8.6 %collective-permute-start.3 = (bf16[128,768]{1,0:T(8,128)(2,1)}, bf16[128,768]{1,0:T(8,128)(2,1)S(1)}, u32[]{:S(2)}, u32[]{:S(2)}) collective-permute-start(bf16[128,768]{1,0:T(8,128)(2,1)} %bitcast.15), channel_id=1, source_target_pairs={{0,12},{1,13},{2,14},{3,15},{4,0},{5,1},{6,2},{7,3},{8,4},{9,5},{1... | collective-permute-start | bytes 589832 | tf_op jit(solution)/shard_map/ppermute | solution.py:487
  9.7 9.9 %collective-permute-start.4 = (bf16[128,768]{1,0:T(8,128)(2,1)S(1)}, bf16[128,768]{1,0:T(8,128)(2,1)S(1)}, u32[]{:S(2)}, u32[]{:S(2)}) collective-permute-start(bf16[128,768]{1,0:T(8,128)(2,1)S(1)} %collective-permute-done.2.refs_6_.rest_1_), channel_id=1, source_target_pairs={{0,4},{1,5},{2,6},{3,7},{4,8},{5,9},{6,10},{7,11},{8,12},{9,13},{1... | collective-permute-start | bytes 589832 | tf_op jit(solution)/shard_map/ppermute | solution.py:487
  9.7 1.2 %copy-start = (f32[343,768]{1,0:T(8,128)S(1)}, f32[343,768]{1,0:T(8,128)}, u32[]{:S(2)}) copy-start(f32[343,768]{1,0:T(8,128)} %refs_4_.1) | copy-start | bytes 3161092
  10.9 0.9 %copy-start.2 = (bf16[4,4,8,768]{3,2,1,0:T(8,128)(2,1)S(1)}, bf16[4,4,8,768]{3,2,1,0:T(8,128)(2,1)}, u32[]{:S(2)}) copy-start(bf16[4,4,8,768]{3,2,1,0:T(8,128)(2,1)} %param.8) | copy-start | bytes 589828
  11.8 0.7 copy-start.13
  12.5 0.7 copy-start.15
  15.4 7.5 %copy-start.3 = (bf16[4,4,8,768]{3,2,1,0:T(8,128)(2,1)S(1)}, bf16[4,4,8,768]{3,2,1,0:T(8,128)(2,1)}, u32[]{:S(2)}) copy-start(bf16[4,4,8,768]{3,2,1,0:T(8,128)(2,1)} %param.8) | copy-start | bytes 589828
  15.4 7.5 %copy-start.6 = (bf16[4,4,8,768]{3,2,1,0:T(8,128)(2,1)S(1)}, bf16[4,4,8,768]{3,2,1,0:T(8,128)(2,1)}, u32[]{:S(2)}) copy-start(bf16[4,4,8,768]{3,2,1,0:T(8,128)(2,1)} %param.15) | copy-start | bytes 589828
  15.4 7.5 %copy-start.12 = (f32[768]{0:T(1024)S(1)}, f32[768]{0:T(1024)}, u32[]{:S(2)}) copy-start(f32[768]{0:T(1024)} %refs_3_.3) | copy-start | bytes 9220
  15.4 7.5 %copy-start.14 = (f32[768]{0:T(1024)S(1)}, f32[768]{0:T(1024)}, u32[]{:S(2)}) copy-start(f32[768]{0:T(1024)} %norm_gain.1) | copy-start | bytes 9220
  19.6 17.1 %collective-permute-start.5 = (bf16[128,768]{1,0:T(8,128)(2,1)S(1)}, bf16[128,768]{1,0:T(8,128)(2,1)S(1)}, u32[]{:S(2)}, u32[]{:S(2)}) collective-permute-start(bf16[128,768]{1,0:T(8,128)(2,1)S(1)} %get-tuple-element.44.normed.rest_0_), channel_id=1, source_target_pairs={{0,4},{1,5},{2,6},{3,7},{4,8},{5,9},{6,10},{7,11},{8,12},{9,13},{1... | collective-permute-start | bytes 589832 | tf_op jit(solution)/shard_map/ppermute | solution.py:487
  19.6 17.1 %collective-permute-start.6 = (bf16[128,768]{1,0:T(8,128)(2,1)S(1)}, bf16[128,768]{1,0:T(8,128)(2,1)S(1)}, u32[]{:S(2)}, u32[]{:S(2)}) collective-permute-start(bf16[128,768]{1,0:T(8,128)(2,1)S(1)} %get-tuple-element.44.normed.rest_0_), channel_id=1, source_target_pairs={{0,12},{1,13},{2,14},{3,15},{4,0},{5,1},{6,2},{7,3},{8,4},{9,5},{1... | collective-permute-start | bytes 589832 | tf_op jit(solution)/shard_map/ppermute | solution.py:487
  31.1 15.3 %copy-start.4 = (bf16[128,768]{1,0:T(8,128)(2,1)}, bf16[128,768]{1,0:T(8,128)(2,1)S(1)}, u32[]{:S(2)}) copy-start(bf16[128,768]{1,0:T(8,128)(2,1)S(1)} %get-tuple-element.48.grads.refs_2_) | copy-start | bytes 589828
  31.1 12.0 %collective-permute-start.8 = (bf16[128,768]{1,0:T(8,128)(2,1)S(1)}, bf16[128,768]{1,0:T(8,128)(2,1)S(1)}, u32[]{:S(2)}, u32[]{:S(2)}) collective-permute-start(bf16[128,768]{1,0:T(8,128)(2,1)S(1)} %get-tuple-element.48.grads.refs_2_), channel_id=1, source_target_pairs={{0,1},{1,0},{2,3},{3,2},{4,5},{5,4},{6,7},{7,6},{8,9},{9,8},{10,11... | collective-permute-start | bytes 589832 | tf_op jit(solution)/shard_map/ppermute | solution.py:460
  34.8 9.0 %collective-permute-start.9 = (bf16[128,768]{1,0:T(8,128)(2,1)S(1)}, bf16[128,768]{1,0:T(8,128)(2,1)S(1)}, u32[]{:S(2)}, u32[]{:S(2)}) collective-permute-start(bf16[128,768]{1,0:T(8,128)(2,1)S(1)} %get-tuple-element.48.grads.refs_2_), channel_id=1, source_target_pairs={{1,2},{3,4},{5,6},{7,8},{9,10},{11,12},{13,14},{2,1},{4,3},{6,5},{... | collective-permute-start | bytes 589832 | tf_op jit(solution)/shard_map/ppermute | solution.py:461
  36.7 8.1 %collective-permute-start.7 = (bf16[128,768]{1,0:T(8,128)(2,1)S(1)}, bf16[128,768]{1,0:T(8,128)(2,1)S(1)}, u32[]{:S(2)}, u32[]{:S(2)}) collective-permute-start(bf16[128,768]{1,0:T(8,128)(2,1)S(1)} %collective-permute-done.5.rest_1_), channel_id=1, source_target_pairs={{0,4},{1,5},{2,6},{3,7},{4,8},{5,9},{6,10},{7,11},{8,12},{9,13},{1... | collective-permute-start | bytes 589832 | tf_op jit(solution)/shard_map/ppermute | solution.py:487
  43.1 0.7 copy-start.8
  43.7 0.7 copy-start.10
  44.8 1.6 %collective-permute-start.10 = (bf16[384,384]{1,0:T(8,128)(2,1)S(1)}, bf16[384,384]{1,0:T(8,128)(2,1)S(1)}, u32[]{:S(2)}, u32[]{:S(2)}) collective-permute-start(bf16[384,384]{1,0:T(8,128)(2,1)S(1)} %get-tuple-element.56), channel_id=1, source_target_pairs={{0,1},{1,0},{2,3},{3,2},{4,5},{5,4},{6,7},{7,6},{8,9},{9,8},{10,11... | collective-permute-start | bytes 884744 | tf_op jit(solution)/shard_map/ppermute | solution.py:642
  45.0 8.3 %collective-permute-start.12 = (bf16[4,128,768]{2,1,0:T(8,128)(2,1)S(1)}, bf16[4,128,768]{2,1,0:T(8,128)(2,1)S(1)}, u32[]{:S(2)}, u32[]{:S(2)}) collective-permute-start(bf16[4,128,768]{2,1,0:T(8,128)(2,1)S(1)} %get-tuple-element.60.refs_5_), channel_id=1, source_target_pairs={{0,1},{1,0},{2,3},{3,2},{4,5},{5,4},{6,7},{7,6},{8,9},{9,8},{10,11... | collective-permute-start | bytes 2359304 | tf_op jit(solution)/shard_map/ppermute | solution.py:665
  47.2 6.1 %collective-permute-start.11 = (bf16[4,128,768]{2,1,0:T(8,128)(2,1)S(1)}, bf16[4,128,768]{2,1,0:T(8,128)(2,1)S(1)}, u32[]{:S(2)}, u32[]{:S(2)}) collective-permute-start(bf16[4,128,768]{2,1,0:T(8,128)(2,1)S(1)} %get-tuple-element.59.refs_4_), channel_id=1, source_target_pairs={{0,1},{1,0},{2,3},{3,2},{4,5},{5,4},{6,7},{7,6},{8,9},{9,8},{10,11... | collective-permute-start | bytes 2359304 | tf_op jit(solution)/shard_map/ppermute | solution.py:664
  47.4 16.1 %all-to-all-start = ((bf16[8,48,384]{2,1,0:T(8,128)(2,1)}), bf16[8,48,384]{2,1,0:T(8,128)(2,1)S(1)}, u32[]{:S(2)}, u32[]{:S(2)}) async-start(bf16[8,48,384]{2,1,0:T(8,128)(2,1)} %bitcast.8), calls=%async_computation | async-start | bytes 589824 | tf_op jit(solution)/shard_map/all_to_all | solution.py:701
  53.3 5.9 %copy-start.1 = (f32[343,768]{1,0:T(8,128)S(1)}, f32[343,768]{1,0:T(8,128)}, u32[]{:S(2)}) copy-start(f32[343,768]{1,0:T(8,128)} %refs_4_.1) | copy-start | bytes 3161092
  53.3 5.9 %copy-start.5 = (bf16[128,768]{1,0:T(8,128)(2,1)S(1)}, bf16[128,768]{1,0:T(8,128)(2,1)}, u32[]{:S(2)}) copy-start(bf16[128,768]{1,0:T(8,128)(2,1)} %copy-done.4) | copy-start | bytes 589828
  53.3 5.9 %copy-start.7 = (bf16[4,4,8,768]{3,2,1,0:T(8,128)(2,1)S(1)}, bf16[4,4,8,768]{3,2,1,0:T(8,128)(2,1)}, u32[]{:S(2)}) copy-start(bf16[4,4,8,768]{3,2,1,0:T(8,128)(2,1)} %param.15) | copy-start | bytes 589828
  53.3 5.9 %copy-start.9 = (bf16[128,768]{1,0:T(8,128)(2,1)S(1)}, bf16[128,768]{1,0:T(8,128)(2,1)}, u32[]{:S(2)}) copy-start(bf16[128,768]{1,0:T(8,128)(2,1)} %copy-done.8) | copy-start | bytes 589828
  53.3 5.9 %copy-start.11 = (bf16[128,768]{1,0:T(8,128)(2,1)S(1)}, bf16[128,768]{1,0:T(8,128)(2,1)}, u32[]{:S(2)}) copy-start(bf16[128,768]{1,0:T(8,128)(2,1)} %copy-done.10) | copy-start | bytes 589828
  57.7 16.7 %collective-permute-start.13 = (bf16[2,192,768]{2,1,0:T(8,128)(2,1)}, bf16[2,192,768]{2,1,0:T(8,128)(2,1)}, u32[]{:S(2)}, u32[]{:S(2)}) collective-permute-start(bf16[2,192,768]{2,1,0:T(8,128)(2,1)} %weight_grads_far_side.1.refs_6_), channel_id=1, source_target_pairs={{0,2},{1,3},{2,0},{3,1},{4,6},{5,7},{6,4},{7,5},{8,10},{9,11},{10,... | collective-permute-start | bytes 1769480 | tf_op jit(solution)/shard_map/ppermute | solution.py:700
  64.2 14.8 %all-to-all-start.1 = ((bf16[8,48,384]{2,1,0:T(8,128)(2,1)}), bf16[8,48,384]{2,1,0:T(8,128)(2,1)S(1)}, u32[]{:S(2)}, u32[]{:S(2)}) async-start(bf16[8,48,384]{2,1,0:T(8,128)(2,1)} %kernel_grad_sum.1.refs_9_), calls=%async_computation.1 | async-start | bytes 589824 | tf_op jit(solution)/shard_map/all_to_all | solution.py:747
  79.0 3.6 %collective-permute-start.14 = (bf16[8,48,384]{2,1,0:T(8,128)(2,1)S(1)}, bf16[8,48,384]{2,1,0:T(8,128)(2,1)S(1)}, u32[]{:S(2)}, u32[]{:S(2)}) collective-permute-start(bf16[8,48,384]{2,1,0:T(8,128)(2,1)S(1)} %all-to-all-done.1.own), channel_id=1, source_target_pairs={{0,1},{1,0},{2,3},{3,2},{4,5},{5,4},{6,7},{7,6},{8,9},{9,8},{10,11... | collective-permute-start | bytes 884744 | tf_op jit(solution)/shard_map/ppermute | solution.py:754

commit v23 on v22

--- a/solution.py
+++ b/solution.py
@@ -636,13 +636,14 @@
         name="kernel_grad_terms",
     )(jnp.stack([core, 1 - core]), inner, own, outer, conv_grad, small)
 
-    half_sent, norm_line[2], grad_inner, grad_outer = lax.optimization_barrier(
-        (half_sent, norm_line[2], grad_inner, grad_outer)
+    corners = [part[: 2 * SUB, :LANES] for part in (grad_inner, grad_outer)]
+    half_sent, norm_line[2], *corners = lax.optimization_barrier(
+        (half_sent, norm_line[2], *corners)
     )
     half_got = lax.ppermute(half_sent, "row", other_core)
     sums, gathered = pl.pallas_call(
-        chip_sum_kernel,
-        in_specs=[whole_block(padded, wide)] * 2 + [whole] * line,
+        follow(chip_sum_kernel, 0, 2 + line, 2),
+        in_specs=[whole_block(padded, wide)] * 2 + [whole] * line + [IN_PLACE] * 2,
         out_specs=[whole_block(padded, wide), whole_block(line, rows, channels)],
         out_shape=[
             jax.ShapeDtypeStruct((padded, wide), BF16),
@@ -652,7 +653,7 @@
         compiler_params=params(),
         cost_estimate=NO_COST,
         name="kernel_grad_chip_sum",
-    )(half_kept, half_got, *norm_line)
+    )(half_kept, half_got, *norm_line, *corners)
 
     share = units // count
     tokens = line * rows

time: 84.5 us -> 85.6 us (1.013)
  waiting for transfers between devices: 10.8 us -> 15.6 us
  starting transfers between devices: 31.7 us -> 29.2 us
  local copies, waits for them, and re-layouts: 4.93 us -> 3.59 us
    ppermute x2, waiting for transfers between devices: 0.01 us -> 5.18 us  [rims(): lax.ppermute(cells, 'row', between + [(j, i) for i, j in between])]
    all_to_all x1, starting transfers between devices: 5.81 us -> 3.42 us  [on_device(): lax.all_to_all(sums.reshape(half, piece, wide), 'row', split_axis=0, conc...]
    unnamed x32, local copies, waits for them, and re-layouts: 4.93 us -> 3.58 us
  transfers between devices with their start and end apart: 17 -> 17, of which waited for: 6 -> 6; matrix products, arithmetic and copies ran while one was open for 0% -> 0% of each run, Pallas kernels for 41% -> 40%
where the time goes in v23:
time: 85.6 us; the launch traced here: 84.7 us
  Pallas kernels  35.2 us (41%)
  starting transfers between devices  29.2 us (34%)
  waiting for transfers between devices  15.6 us (18%)
  local copies, waits for them, and re-layouts  3.59 us (4%)
  between operations  0.9 us (1%)
    pallas_call x2, Pallas kernels, side_terms(): pl.pallas_call(follow(kernel, 1, 7 + len(more), 1), grid_spec=pltpu.Prefe...  9.03 us
    pallas_call x1, Pallas kernels, on_device(): pl.pallas_call(mlp_kernel, grid=(units // block,), in_specs=[whole, pl.Bl...  8.2 us
    ppermute x6, starting transfers between devices, along_line(): lax.ppermute(cells, 'row', [(i, (i + quad * steps) % count) for i in rang...  7.52 us
    pallas_call x1, Pallas kernels, on_device(): pl.pallas_call(functools.partial(kernel_grad_kernel, planes, height), gri...  6.18 us
    ppermute x1, waiting for transfers between devices, on_device(): got = lax.ppermute(sent, 'row', other_side)  5.87 us
    ppermute x2, waiting for transfers between devices, rims(): lax.ppermute(cells, 'row', between + [(j, i) for i, j in between])  5.18 us
    ppermute x2, starting transfers between devices, rims(): lax.ppermute(cells, 'row', between + [(j, i) for i, j in between])  4.93 us
    ppermute x2, starting transfers between devices, rims(): lax.ppermute(cells, 'row', [(i, i ^ 1) for i in range(count)])  4.65 us
  transfers between devices with their start and end apart: 17, of which 6 were waited for; matrix products, arithmetic and copies ran while one was open for 0% of the time, Pallas kernels for 40%

profile of v23, /device:TPU:1, one launch (start us, length us, event | category | flops | bytes accessed | tf_op | source)
XLA Modules:
  0.0 84.7 jit_solution(13260371711186303396)
XLA Ops:
  0.6 2.2 %collective-permute-start.2 = (bf16[128,768]{1,0:T(8,128)(2,1)}, bf16[128,768]{1,0:T(8,128)(2,1)S(1)}, u32[]{:S(2)}, u32[]{:S(2)}) collective-permute-start(bf16[128,768]{1,0:T(8,128)(2,1)} %bitcast.14), channel_id=1, source_target_pairs={{0,4},{1,5},{2,6},{3,7},{4,8},{5,9},{6,10},{7,11},{8,12},{9,13},{1... | collective-permute-start | bytes 589832 | tf_op jit(solution)/shard_map/ppermute | solution.py:487
  2.8 1.0 %collective-permute-start = (bf16[128,768]{1,0:T(8,128)(2,1)}, bf16[128,768]{1,0:T(8,128)(2,1)S(1)}, u32[]{:S(2)}, u32[]{:S(2)}) collective-permute-start(bf16[128,768]{1,0:T(8,128)(2,1)} %bitcast.9), channel_id=1, source_target_pairs={{0,1},{1,0},{2,3},{3,2},{4,5},{5,4},{6,7},{7,6},{8,9},{9,8},{10,11... | collective-permute-start | bytes 589832 | tf_op jit(solution)/shard_map/ppermute | solution.py:460
  3.8 3.0 %collective-permute-start.1 = (bf16[128,768]{1,0:T(8,128)(2,1)}, bf16[128,768]{1,0:T(8,128)(2,1)S(1)}, u32[]{:S(2)}, u32[]{:S(2)}) collective-permute-start(bf16[128,768]{1,0:T(8,128)(2,1)} %bitcast.10), channel_id=1, source_target_pairs={{1,2},{3,4},{5,6},{7,8},{9,10},{11,12},{13,14},{2,1},{4,3},{6,5},{... | collective-permute-start | bytes 589832 | tf_op jit(solution)/shard_map/ppermute | solution.py:461
  6.8 2.0 %collective-permute-start.3 = (bf16[128,768]{1,0:T(8,128)(2,1)}, bf16[128,768]{1,0:T(8,128)(2,1)S(1)}, u32[]{:S(2)}, u32[]{:S(2)}) collective-permute-start(bf16[128,768]{1,0:T(8,128)(2,1)} %bitcast.15), channel_id=1, source_target_pairs={{0,12},{1,13},{2,14},{3,15},{4,0},{5,1},{6,2},{7,3},{8,4},{9,5},{1... | collective-permute-start | bytes 589832 | tf_op jit(solution)/shard_map/ppermute | solution.py:487
  8.8 0.9 %collective-permute-done.2.refs_6_.rest_1_ = bf16[128,768]{1,0:T(8,128)(2,1)S(1)} collective-permute-done((bf16[128,768]{1,0:T(8,128)(2,1)}, bf16[128,768]{1,0:T(8,128)(2,1)S(1)}, u32[]{:S(2)}, u32[]{:S(2)}) %collective-permute-start.2) | collective-permute-done | bytes 196640 | tf_op jit(solution)/shard_map/ppermute | solution.py:487
  9.7 0.0 collective-permute-start.4
  9.7 1.2 %copy-done = f32[343,768]{1,0:T(8,128)S(1)} copy-done((f32[343,768]{1,0:T(8,128)S(1)}, f32[343,768]{1,0:T(8,128)}, u32[]{:S(2)}) %copy-start) | copy-done | bytes 1053720
  10.9 0.9 %copy-done.2 = bf16[4,4,8,768]{3,2,1,0:T(8,128)(2,1)S(1)} copy-done((bf16[4,4,8,768]{3,2,1,0:T(8,128)(2,1)S(1)}, bf16[4,4,8,768]{3,2,1,0:T(8,128)(2,1)}, u32[]{:S(2)}) %copy-start.2) | copy-done | bytes 196632
  11.8 0.7 copy-done.13
  12.5 0.7 copy-done.15
  13.2 2.2 %own_conv.1 = (f32[128,768]{1,0:T(8,128)S(1)}, f32[6,9,7,8,128]{4,3,2,1,0:T(8,128)S(1)}, f32[8,768]{1,0:T(8,128)S(1)}) custom-call(bf16[128,768]{1,0:T(8,128)(2,1)S(1)} %bitcast.11, f32[343,768]{1,0:T(8,128)S(1)} %copy-done, f32[768]{0:T(1024)S(1)} %copy-done.13, f32[768]{0:T(1024)S(1)} %copy-done.15), custom_call_target="tpu_custom_call" | custom-call | tf_op jit(solution)/shard_map/own_conv/pallas_call | solution.py:497
  15.4 0.0 copy-start.3
  15.4 0.0 copy-start.6
  15.4 0.0 copy-start.12
  15.4 0.0 copy-start.14
  15.4 0.0 collective-permute-done.1.refs_2_.outer
  15.4 0.0 collective-permute-done.3.refs_7_.rest_3_
  15.5 2.7 %rim_conv.1 = (bf16[128,768]{1,0:T(8,128)(2,1)S(1)}, f32[128,768]{1,0:T(8,128)S(1)}) custom-call(s32[1]{0:T(128)} %bitcast.refs_0_.core, bf16[128,768]{1,0:T(8,128)(2,1)S(1)} %collective-permute-done.refs_1_.inner, bf16[128,768]{1,0:T(8,128)(2,1)S(1)} %collective-permute-done.1.refs_2_.outer, f32[6,9,7,8,128]{4,3,2,1,0:T(8,128)S(1)} %get-tuple-element.40.refs_3_, ...), custom_call_target="tpu_custom_call" | custom-call | tf_op jit(solution)/shard_map/rim_conv/pallas_call | solution.py:515
  18.2 1.4 %collective-permute-done.4.rest_2_ = bf16[128,768]{1,0:T(8,128)(2,1)S(1)} collective-permute-done((bf16[128,768]{1,0:T(8,128)(2,1)S(1)}, bf16[128,768]{1,0:T(8,128)(2,1)S(1)}, u32[]{:S(2)}, u32[]{:S(2)}) %collective-permute-start.4) | collective-permute-done | bytes 196640 | tf_op jit(solution)/shard_map/ppermute | solution.py:487
  19.6 0.0 collective-permute-start.7
  19.6 3.3 %collective-permute-start.8 = (bf16[128,768]{1,0:T(8,128)(2,1)S(1)}, bf16[128,768]{1,0:T(8,128)(2,1)S(1)}, u32[]{:S(2)}, u32[]{:S(2)}) collective-permute-start(bf16[128,768]{1,0:T(8,128)(2,1)S(1)} %get-tuple-element.44.normed.refs_2_), channel_id=1, source_target_pairs={{0,12},{1,13},{2,14},{3,15},{4,0},{5,1},{6,2},{7,3},{8,4},{9,5},{1... | collective-permute-start | bytes 589832 | tf_op jit(solution)/shard_map/ppermute | solution.py:487
  22.9 8.2 %mlp_both_ways.1 = (bf16[128,768]{1,0:T(8,128)(2,1)}, bf16[128,768]{1,0:T(8,128)(2,1)S(1)}, f32[8,768]{1,0:T(8,128)S(1)}, bf16[4,128,768]{2,1,0:T(8,128)(2,1)S(1)}) custom-call(bf16[128,768]{1,0:T(8,128)(2,1)S(1)} %get-tuple-element.44.normed.refs_2_, bf16[3072,768]{1,0:T(8,128)(2,1)} %refs_1_.3, bf16[3072,768]{1,0:T(8,128)(2,1)} %refs_2_.3, ...), custom_call_target="tpu_custom_call" | custom-call | tf_op jit(solution)/shard_map/mlp_both_ways/pallas_call | solution.py:560
  31.1 3.7 %collective-permute-start.5 = (bf16[128,768]{1,0:T(8,128)(2,1)S(1)}, bf16[128,768]{1,0:T(8,128)(2,1)S(1)}, u32[]{:S(2)}, u32[]{:S(2)}) collective-permute-start(bf16[128,768]{1,0:T(8,128)(2,1)S(1)} %get-tuple-element.48.grads.refs_2_), channel_id=1, source_target_pairs={{0,1},{1,0},{2,3},{3,2},{4,5},{5,4},{6,7},{7,6},{8,9},{9,8},{10,11... | collective-permute-start | bytes 589832 | tf_op jit(solution)/shard_map/ppermute | solution.py:460
  34.8 1.9 %collective-permute-start.6 = (bf16[128,768]{1,0:T(8,128)(2,1)S(1)}, bf16[128,768]{1,0:T(8,128)(2,1)S(1)}, u32[]{:S(2)}, u32[]{:S(2)}) collective-permute-start(bf16[128,768]{1,0:T(8,128)(2,1)S(1)} %get-tuple-element.48.grads.refs_2_), channel_id=1, source_target_pairs={{1,2},{3,4},{5,6},{7,8},{9,10},{11,12},{13,14},{2,1},{4,3},{6,5},{... | collective-permute-start | bytes 589832 | tf_op jit(solution)/shard_map/ppermute | solution.py:461
  36.7 0.0 collective-permute-done.8.refs_5_
  36.7 0.1 collective-permute-start.9
  36.8 0.1 pad_add_fusion.1.which
  36.9 5.2 %collective-permute-done.6.refs_3_ = bf16[128,768]{1,0:T(8,128)(2,1)S(1)} collective-permute-done((bf16[128,768]{1,0:T(8,128)(2,1)S(1)}, bf16[128,768]{1,0:T(8,128)(2,1)S(1)}, u32[]{:S(2)}, u32[]{:S(2)}) %collective-permute-start.6) | collective-permute-done | bytes 196640 | tf_op jit(solution)/shard_map/ppermute | solution.py:461
  42.1 6.2 %kernel_grad_terms.1 = (bf16[384,384]{1,0:T(8,128)(2,1)S(1)}, bf16[384,384]{1,0:T(8,128)(2,1)S(1)}) custom-call(s32[2]{0:T(128)S(1)} %pad_add_fusion.1.which, bf16[128,768]{1,0:T(8,128)(2,1)S(1)} %collective-permute-done.refs_1_.inner, bf16[128,768]{1,0:T(8,128)(2,1)S(1)} %bitcast.13, bf16[128,768]{1,0:T(8,128)(2,1)S(1)} %collective-permute-done.1.refs_2_.outer, ...), custom_call_target="tpu_custom_call" | custom-call | tf_op jit(solution)/shard_map/kernel_grad_terms/pallas_call | solution.py:616
  48.2 0.1 collective-permute-start.10
  48.3 0.5 collective-permute-start.12
  48.8 1.1 %collective-permute-done.10.refs_1_ = bf16[384,384]{1,0:T(8,128)(2,1)S(1)} collective-permute-done((bf16[384,384]{1,0:T(8,128)(2,1)S(1)}, bf16[384,384]{1,0:T(8,128)(2,1)S(1)}, u32[]{:S(2)}, u32[]{:S(2)}) %collective-permute-start.10) | collective-permute-done | bytes 294944 | tf_op jit(solution)/shard_map/ppermute | solution.py:643
  49.9 0.8 kernel_grad_chip_sum.1
  50.7 0.1 collective-permute-start.11
  50.9 3.4 %all-to-all-start = ((bf16[8,48,384]{2,1,0:T(8,128)(2,1)}), bf16[8,48,384]{2,1,0:T(8,128)(2,1)S(1)}, u32[]{:S(2)}, u32[]{:S(2)}) async-start(bf16[8,48,384]{2,1,0:T(8,128)(2,1)} %bitcast.8), calls=%async_computation | async-start | bytes 589824 | tf_op jit(solution)/shard_map/all_to_all | solution.py:702
  54.3 0.1 pad_add_fusion.refs_0_
  54.4 0.0 collective-permute-done.12.refs_7_
  54.5 4.4 %weight_grads_far_side.1.refs_6_ = bf16[2,192,768]{2,1,0:T(8,128)(2,1)} custom-call(s32[2]{0:T(128)S(1)} %pad_add_fusion.refs_0_, bf16[3072,768]{1,0:T(8,128)(2,1)} %refs_1_.3, bf16[3072,768]{1,0:T(8,128)(2,1)} %refs_2_.3, f32[768]{0:T(1024)S(1)} %copy-done.12, bf16[4,128,768]{2,1,0:T(8,128)(2,1)S(1)} %get-tuple-element.59.refs_4_, ...), custom_call_target="tpu_custom_call" | custom-call | tf_op jit(solution)/shard_map/weight_grads_far_side/pallas_call | solution.py:670
  58.8 1.3 %collective-permute-start.13 = (bf16[2,192,768]{2,1,0:T(8,128)(2,1)}, bf16[2,192,768]{2,1,0:T(8,128)(2,1)}, u32[]{:S(2)}, u32[]{:S(2)}) collective-permute-start(bf16[2,192,768]{2,1,0:T(8,128)(2,1)} %weight_grads_far_side.1.refs_6_), channel_id=1, source_target_pairs={{0,2},{1,3},{2,0},{3,1},{4,6},{5,7},{6,4},{7,5},{8,10},{9,11},{10,... | collective-permute-start | bytes 1769480 | tf_op jit(solution)/shard_map/ppermute | solution.py:701
  60.2 4.3 %input_grad_conv.1 = (bf16[128,768]{1,0:T(8,128)(2,1)}, f32[8,128]{1,0:T(8,128)S(1)}) custom-call(s32[1]{0:T(128)} %bitcast.refs_0_.core, bf16[128,768]{1,0:T(8,128)(2,1)S(1)} %copy-done.9, bf16[128,768]{1,0:T(8,128)(2,1)S(1)} %copy-done.5, bf16[128,768]{1,0:T(8,128)(2,1)S(1)} %copy-done.11, f32[343,768]{1,0:T(8,128)S(1)} %copy-done.1, ...), custom_call_target="tpu_custom_call" | custom-call | tf_op jit(solution)/shard_map/input_grad_conv/pallas_call | solution.py:710
  64.5 0.8 kernel_grad_sum.1.refs_9_
  65.3 4.3 %all-to-all-start.1 = ((bf16[8,48,384]{2,1,0:T(8,128)(2,1)}), bf16[8,48,384]{2,1,0:T(8,128)(2,1)S(1)}, u32[]{:S(2)}, u32[]{:S(2)}) async-start(bf16[8,48,384]{2,1,0:T(8,128)(2,1)} %kernel_grad_sum.1.refs_9_), calls=%async_computation.1 | async-start | bytes 589824 | tf_op jit(solution)/shard_map/all_to_all | solution.py:748
  69.5 5.9 %collective-permute-done.13.refs_8_ = bf16[2,192,768]{2,1,0:T(8,128)(2,1)} collective-permute-done((bf16[2,192,768]{2,1,0:T(8,128)(2,1)}, bf16[2,192,768]{2,1,0:T(8,128)(2,1)}, u32[]{:S(2)}, u32[]{:S(2)}) %collective-permute-start.13) | collective-permute-done | bytes 589856 | tf_op jit(solution)/shard_map/ppermute | solution.py:701
  75.4 4.7 %weight_grads_near_side.1 = (f32[192,768]{1,0:T(8,128)}, f32[192,768]{1,0:T(8,128)}) custom-call(s32[2]{0:T(128)S(1)} %pad_add_fusion.refs_0_, bf16[3072,768]{1,0:T(8,128)(2,1)} %refs_1_.3, bf16[3072,768]{1,0:T(8,128)(2,1)} %refs_2_.3, f32[768]{0:T(1024)S(1)} %copy-done.12, bf16[4,128,768]{2,1,0:T(8,128)(2,1)S(1)} %get-tuple-element.59.refs_4_, ...), custom_call_target="tpu_custom_call" | custom-call | tf_op jit(solution)/shard_map/weight_grads_near_side/pallas_call | solution.py:670
  80.1 0.0 all-to-all-done.1.own
  80.1 2.4 %collective-permute-start.14 = (bf16[8,48,384]{2,1,0:T(8,128)(2,1)S(1)}, bf16[8,48,384]{2,1,0:T(8,128)(2,1)S(1)}, u32[]{:S(2)}, u32[]{:S(2)}) collective-permute-start(bf16[8,48,384]{2,1,0:T(8,128)(2,1)S(1)} %all-to-all-done.1.own), channel_id=1, source_target_pairs={{0,1},{1,0},{2,3},{3,2},{4,5},{5,4},{6,7},{7,6},{8,9},{9,8},{10,11... | collective-permute-start | bytes 884744 | tf_op jit(solution)/shard_map/ppermute | solution.py:755
  82.5 1.2 %collective-permute-done.14.other = bf16[8,48,384]{2,1,0:T(8,128)(2,1)S(1)} collective-permute-done((bf16[8,48,384]{2,1,0:T(8,128)(2,1)S(1)}, bf16[8,48,384]{2,1,0:T(8,128)(2,1)S(1)}, u32[]{:S(2)}, u32[]{:S(2)}) %collective-permute-start.14) | collective-permute-done | bytes 294944 | tf_op jit(solution)/shard_map/ppermute | solution.py:755
  83.7 1.1 %kernel_grad_unpack.1 = (f32[343,768]{1,0:T(8,128)}, f32[768]{0:T(1024)}, f32[768]{0:T(1024)}, f32[768]{0:T(1024)}) custom-call(s32[1]{0:T(128)} %bitcast.refs_0_.core, bf16[8,48,384]{2,1,0:T(8,128)(2,1)S(1)} %all-to-all-done.1.own, bf16[8,48,384]{2,1,0:T(8,128)(2,1)S(1)} %collective-permute-done.14.other), custom_call_target="tpu_custom_call" | custom-call | tf_op jit(solution)/shard_map/kernel_grad_unpack/pallas_call | solution.py:756
  (32 shorter events, 0.1 us)
Async XLA Ops:
  0.6 9.0 %collective-permute-start.2 = (bf16[128,768]{1,0:T(8,128)(2,1)}, bf16[128,768]{1,0:T(8,128)(2,1)S(1)}, u32[]{:S(2)}, u32[]{:S(2)}) collective-permute-start(bf16[128,768]{1,0:T(8,128)(2,1)} %bitcast.14), channel_id=1, source_target_pairs={{0,4},{1,5},{2,6},{3,7},{4,8},{5,9},{6,10},{7,11},{8,12},{9,13},{1... | collective-permute-start | bytes 589832 | tf_op jit(solution)/shard_map/ppermute | solution.py:487
  2.8 12.6 %collective-permute-start = (bf16[128,768]{1,0:T(8,128)(2,1)}, bf16[128,768]{1,0:T(8,128)(2,1)S(1)}, u32[]{:S(2)}, u32[]{:S(2)}) collective-permute-start(bf16[128,768]{1,0:T(8,128)(2,1)} %bitcast.9), channel_id=1, source_target_pairs={{0,1},{1,0},{2,3},{3,2},{4,5},{5,4},{6,7},{7,6},{8,9},{9,8},{10,11... | collective-permute-start | bytes 589832 | tf_op jit(solution)/shard_map/ppermute | solution.py:460
  3.8 11.7 %collective-permute-start.1 = (bf16[128,768]{1,0:T(8,128)(2,1)}, bf16[128,768]{1,0:T(8,128)(2,1)S(1)}, u32[]{:S(2)}, u32[]{:S(2)}) collective-permute-start(bf16[128,768]{1,0:T(8,128)(2,1)} %bitcast.10), channel_id=1, source_target_pairs={{1,2},{3,4},{5,6},{7,8},{9,10},{11,12},{13,14},{2,1},{4,3},{6,5},{... | collective-permute-start | bytes 589832 | tf_op jit(solution)/shard_map/ppermute | solution.py:461
  6.8 8.6 %collective-permute-start.3 = (bf16[128,768]{1,0:T(8,128)(2,1)}, bf16[128,768]{1,0:T(8,128)(2,1)S(1)}, u32[]{:S(2)}, u32[]{:S(2)}) collective-permute-start(bf16[128,768]{1,0:T(8,128)(2,1)} %bitcast.15), channel_id=1, source_target_pairs={{0,12},{1,13},{2,14},{3,15},{4,0},{5,1},{6,2},{7,3},{8,4},{9,5},{1... | collective-permute-start | bytes 589832 | tf_op jit(solution)/shard_map/ppermute | solution.py:487
  9.7 9.9 %collective-permute-start.4 = (bf16[128,768]{1,0:T(8,128)(2,1)S(1)}, bf16[128,768]{1,0:T(8,128)(2,1)S(1)}, u32[]{:S(2)}, u32[]{:S(2)}) collective-permute-start(bf16[128,768]{1,0:T(8,128)(2,1)S(1)} %collective-permute-done.2.refs_6_.rest_1_), channel_id=1, source_target_pairs={{0,4},{1,5},{2,6},{3,7},{4,8},{5,9},{6,10},{7,11},{8,12},{9,13},{1... | collective-permute-start | bytes 589832 | tf_op jit(solution)/shard_map/ppermute | solution.py:487
  9.7 1.2 %copy-start = (f32[343,768]{1,0:T(8,128)S(1)}, f32[343,768]{1,0:T(8,128)}, u32[]{:S(2)}) copy-start(f32[343,768]{1,0:T(8,128)} %refs_4_.1) | copy-start | bytes 3161092
  10.9 0.9 %copy-start.2 = (bf16[4,4,8,768]{3,2,1,0:T(8,128)(2,1)S(1)}, bf16[4,4,8,768]{3,2,1,0:T(8,128)(2,1)}, u32[]{:S(2)}) copy-start(bf16[4,4,8,768]{3,2,1,0:T(8,128)(2,1)} %param.8) | copy-start | bytes 589828
  11.8 0.7 copy-start.13
  12.5 0.7 copy-start.15
  15.4 7.5 %copy-start.3 = (bf16[4,4,8,768]{3,2,1,0:T(8,128)(2,1)S(1)}, bf16[4,4,8,768]{3,2,1,0:T(8,128)(2,1)}, u32[]{:S(2)}) copy-start(bf16[4,4,8,768]{3,2,1,0:T(8,128)(2,1)} %param.8) | copy-start | bytes 589828
  15.4 7.5 %copy-start.6 = (bf16[4,4,8,768]{3,2,1,0:T(8,128)(2,1)S(1)}, bf16[4,4,8,768]{3,2,1,0:T(8,128)(2,1)}, u32[]{:S(2)}) copy-start(bf16[4,4,8,768]{3,2,1,0:T(8,128)(2,1)} %param.15) | copy-start | bytes 589828
  15.4 7.5 %copy-start.12 = (f32[768]{0:T(1024)S(1)}, f32[768]{0:T(1024)}, u32[]{:S(2)}) copy-start(f32[768]{0:T(1024)} %refs_3_.3) | copy-start | bytes 9220
  15.4 7.5 %copy-start.14 = (f32[768]{0:T(1024)S(1)}, f32[768]{0:T(1024)}, u32[]{:S(2)}) copy-start(f32[768]{0:T(1024)} %norm_gain.1) | copy-start | bytes 9220
  19.6 17.1 %collective-permute-start.7 = (bf16[128,768]{1,0:T(8,128)(2,1)S(1)}, bf16[128,768]{1,0:T(8,128)(2,1)S(1)}, u32[]{:S(2)}, u32[]{:S(2)}) collective-permute-start(bf16[128,768]{1,0:T(8,128)(2,1)S(1)} %get-tuple-element.44.normed.refs_2_), channel_id=1, source_target_pairs={{0,4},{1,5},{2,6},{3,7},{4,8},{5,9},{6,10},{7,11},{8,12},{9,13},{1... | collective-permute-start | bytes 589832 | tf_op jit(solution)/shard_map/ppermute | solution.py:487
  19.6 17.1 %collective-permute-start.8 = (bf16[128,768]{1,0:T(8,128)(2,1)S(1)}, bf16[128,768]{1,0:T(8,128)(2,1)S(1)}, u32[]{:S(2)}, u32[]{:S(2)}) collective-permute-start(bf16[128,768]{1,0:T(8,128)(2,1)S(1)} %get-tuple-element.44.normed.refs_2_), channel_id=1, source_target_pairs={{0,12},{1,13},{2,14},{3,15},{4,0},{5,1},{6,2},{7,3},{8,4},{9,5},{1... | collective-permute-start | bytes 589832 | tf_op jit(solution)/shard_map/ppermute | solution.py:487
  31.1 18.8 %copy-start.4 = (bf16[128,768]{1,0:T(8,128)(2,1)}, bf16[128,768]{1,0:T(8,128)(2,1)S(1)}, u32[]{:S(2)}) copy-start(bf16[128,768]{1,0:T(8,128)(2,1)S(1)} %get-tuple-element.48.grads.refs_2_) | copy-start | bytes 589828
  31.1 5.8 %collective-permute-start.5 = (bf16[128,768]{1,0:T(8,128)(2,1)S(1)}, bf16[128,768]{1,0:T(8,128)(2,1)S(1)}, u32[]{:S(2)}, u32[]{:S(2)}) collective-permute-start(bf16[128,768]{1,0:T(8,128)(2,1)S(1)} %get-tuple-element.48.grads.refs_2_), channel_id=1, source_target_pairs={{0,1},{1,0},{2,3},{3,2},{4,5},{5,4},{6,7},{7,6},{8,9},{9,8},{10,11... | collective-permute-start | bytes 589832 | tf_op jit(solution)/shard_map/ppermute | solution.py:460
  34.8 7.3 %collective-permute-start.6 = (bf16[128,768]{1,0:T(8,128)(2,1)S(1)}, bf16[128,768]{1,0:T(8,128)(2,1)S(1)}, u32[]{:S(2)}, u32[]{:S(2)}) collective-permute-start(bf16[128,768]{1,0:T(8,128)(2,1)S(1)} %get-tuple-element.48.grads.refs_2_), channel_id=1, source_target_pairs={{1,2},{3,4},{5,6},{7,8},{9,10},{11,12},{13,14},{2,1},{4,3},{6,5},{... | collective-permute-start | bytes 589832 | tf_op jit(solution)/shard_map/ppermute | solution.py:461
  36.7 11.5 %collective-permute-start.9 = (bf16[128,768]{1,0:T(8,128)(2,1)S(1)}, bf16[128,768]{1,0:T(8,128)(2,1)S(1)}, u32[]{:S(2)}, u32[]{:S(2)}) collective-permute-start(bf16[128,768]{1,0:T(8,128)(2,1)S(1)} %collective-permute-done.7.refs_3_), channel_id=1, source_target_pairs={{0,4},{1,5},{2,6},{3,7},{4,8},{5,9},{6,10},{7,11},{8,12},{9,13},{1... | collective-permute-start | bytes 589832 | tf_op jit(solution)/shard_map/ppermute | solution.py:487
  36.9 11.5 %copy-start.8 = (bf16[128,768]{1,0:T(8,128)(2,1)}, bf16[128,768]{1,0:T(8,128)(2,1)S(1)}, u32[]{:S(2)}) copy-start(bf16[128,768]{1,0:T(8,128)(2,1)S(1)} %collective-permute-done.5.refs_1_) | copy-start | bytes 589828
  42.0 7.9 %copy-start.10 = (bf16[128,768]{1,0:T(8,128)(2,1)}, bf16[128,768]{1,0:T(8,128)(2,1)S(1)}, u32[]{:S(2)}) copy-start(bf16[128,768]{1,0:T(8,128)(2,1)S(1)} %collective-permute-done.6.refs_3_) | copy-start | bytes 589828
  48.2 1.6 %collective-permute-start.10 = (bf16[384,384]{1,0:T(8,128)(2,1)S(1)}, bf16[384,384]{1,0:T(8,128)(2,1)S(1)}, u32[]{:S(2)}, u32[]{:S(2)}) collective-permute-start(bf16[384,384]{1,0:T(8,128)(2,1)S(1)} %get-tuple-element.54), channel_id=1, source_target_pairs={{0,1},{1,0},{2,3},{3,2},{4,5},{5,4},{6,7},{7,6},{8,9},{9,8},{10,11... | collective-permute-start | bytes 884744 | tf_op jit(solution)/shard_map/ppermute | solution.py:643
  48.3 6.1 %collective-permute-start.12 = (bf16[4,128,768]{2,1,0:T(8,128)(2,1)S(1)}, bf16[4,128,768]{2,1,0:T(8,128)(2,1)S(1)}, u32[]{:S(2)}, u32[]{:S(2)}) collective-permute-start(bf16[4,128,768]{2,1,0:T(8,128)(2,1)S(1)} %get-tuple-element.60.refs_5_), channel_id=1, source_target_pairs={{0,1},{1,0},{2,3},{3,2},{4,5},{5,4},{6,7},{7,6},{8,9},{9,8},{10,11... | collective-permute-start | bytes 2359304 | tf_op jit(solution)/shard_map/ppermute | solution.py:666
  50.7 3.7 %collective-permute-start.11 = (bf16[4,128,768]{2,1,0:T(8,128)(2,1)S(1)}, bf16[4,128,768]{2,1,0:T(8,128)(2,1)S(1)}, u32[]{:S(2)}, u32[]{:S(2)}) collective-permute-start(bf16[4,128,768]{2,1,0:T(8,128)(2,1)S(1)} %get-tuple-element.59.refs_4_), channel_id=1, source_target_pairs={{0,1},{1,0},{2,3},{3,2},{4,5},{5,4},{6,7},{7,6},{8,9},{9,8},{10,11... | collective-permute-start | bytes 2359304 | tf_op jit(solution)/shard_map/ppermute | solution.py:665
  50.9 13.6 %all-to-all-start = ((bf16[8,48,384]{2,1,0:T(8,128)(2,1)}), bf16[8,48,384]{2,1,0:T(8,128)(2,1)S(1)}, u32[]{:S(2)}, u32[]{:S(2)}) async-start(bf16[8,48,384]{2,1,0:T(8,128)(2,1)} %bitcast.8), calls=%async_computation | async-start | bytes 589824 | tf_op jit(solution)/shard_map/all_to_all | solution.py:702
  54.4 5.7 %copy-start.1 = (f32[343,768]{1,0:T(8,128)S(1)}, f32[343,768]{1,0:T(8,128)}, u32[]{:S(2)}) copy-start(f32[343,768]{1,0:T(8,128)} %refs_4_.1) | copy-start | bytes 3161092
  54.4 5.7 %copy-start.5 = (bf16[128,768]{1,0:T(8,128)(2,1)S(1)}, bf16[128,768]{1,0:T(8,128)(2,1)}, u32[]{:S(2)}) copy-start(bf16[128,768]{1,0:T(8,128)(2,1)} %copy-done.4) | copy-start | bytes 589828
  54.4 5.7 %copy-start.7 = (bf16[4,4,8,768]{3,2,1,0:T(8,128)(2,1)S(1)}, bf16[4,4,8,768]{3,2,1,0:T(8,128)(2,1)}, u32[]{:S(2)}) copy-start(bf16[4,4,8,768]{3,2,1,0:T(8,128)(2,1)} %param.15) | copy-start | bytes 589828
  54.4 5.7 %copy-start.9 = (bf16[128,768]{1,0:T(8,128)(2,1)S(1)}, bf16[128,768]{1,0:T(8,128)(2,1)}, u32[]{:S(2)}) copy-start(bf16[128,768]{1,0:T(8,128)(2,1)} %copy-done.8) | copy-start | bytes 589828
  54.4 5.7 %copy-start.11 = (bf16[128,768]{1,0:T(8,128)(2,1)S(1)}, bf16[128,768]{1,0:T(8,128)(2,1)}, u32[]{:S(2)}) copy-start(bf16[128,768]{1,0:T(8,128)(2,1)} %copy-done.10) | copy-start | bytes 589828
  58.8 16.6 %collective-permute-start.13 = (bf16[2,192,768]{2,1,0:T(8,128)(2,1)}, bf16[2,192,768]{2,1,0:T(8,128)(2,1)}, u32[]{:S(2)}, u32[]{:S(2)}) collective-permute-start(bf16[2,192,768]{2,1,0:T(8,128)(2,1)} %weight_grads_far_side.1.refs_6_), channel_id=1, source_target_pairs={{0,2},{1,3},{2,0},{3,1},{4,6},{5,7},{6,4},{7,5},{8,10},{9,11},{10,... | collective-permute-start | bytes 1769480 | tf_op jit(solution)/shard_map/ppermute | solution.py:701
  65.3 14.8 %all-to-all-start.1 = ((bf16[8,48,384]{2,1,0:T(8,128)(2,1)}), bf16[8,48,384]{2,1,0:T(8,128)(2,1)S(1)}, u32[]{:S(2)}, u32[]{:S(2)}) async-start(bf16[8,48,384]{2,1,0:T(8,128)(2,1)} %kernel_grad_sum.1.refs_9_), calls=%async_computation.1 | async-start | bytes 589824 | tf_op jit(solution)/shard_map/all_to_all | solution.py:748
  80.1 3.6 %collective-permute-start.14 = (bf16[8,48,384]{2,1,0:T(8,128)(2,1)S(1)}, bf16[8,48,384]{2,1,0:T(8,128)(2,1)S(1)}, u32[]{:S(2)}, u32[]{:S(2)}) collective-permute-start(bf16[8,48,384]{2,1,0:T(8,128)(2,1)S(1)} %all-to-all-done.1.own), channel_id=1, source_target_pairs={{0,1},{1,0},{2,3},{3,2},{4,5},{5,4},{6,7},{7,6},{8,9},{9,8},{10,11... | collective-permute-start | bytes 884744 | tf_op jit(solution)/shard_map/ppermute | solution.py:755
